TPU v7x, 32 devices: a whole 2x2x4 slice. The times are simulated.
32 devices in a mesh: groups: 2 (over x), gx: 8 (over z, y), gy: 2 (over core).
Axes of the slice: x: 2, y: 2, z: 4, core: 2. Of those that a mesh axis runs over, the one named last changes fastest.
Arguments:
- activations: bfloat16 [128, 18432], P(('groups', 'gx'), 'gy'), parts along dimension 0, may hold values from -300 to 300
- norm_gain: bfloat16 [18432], P('gy'), may hold values from 0.099609375 to 1.8984375
- query_weight: bfloat16 [12288, 18432], P('gx', 'gy'), may hold values from -0.046875 to 0.046875
- keyval_weight: bfloat16 [512, 18432], P('gx', 'gy'), may hold values from -0.046875 to 0.046875
- output_weight: bfloat16 [12288, 18432], P('gy', 'gx'), may hold values from -0.3125 to 0.3125
- cache_keys: bfloat16 [128, 2048, 256], P(('groups', 'gx', 'gy')), parts along dimension 0, may hold values from -1000 to 1000
- cache_values: bfloat16 [128, 2048, 256], P(('groups', 'gx', 'gy')), parts along dimension 0, may hold values from -6 to 6
- cache_lengths: int32 [128], P(('groups', 'gx', 'gy')), parts along dimension 0, may hold values from 2 to 2048, as said below
Outputs:
- attention_out: bfloat16 [128, 18432], P(('groups', 'gy'), 'gx'), parts along dimension 0
There are 2 independent parts, one for each index of `groups`. A program takes and returns all parts, laid end to end along the dimension named above; an argument that names none is the same for every part. Nothing has to cross between parts.
Inputs may be any that keep to these rules, and one draw needn't show every extreme that they name: `cache_lengths`: the largest of a part's values is exactly 2048.
All inputs are finite; a program needn't handle non-finite values.
Results may differ from a plain program's by a relative error of at most 0.007.
The roundings to bfloat16 on the way count: a program that leaves them out, or rounds other values in their place, can miss the bound.
Values may be sent and summed in bfloat16 or wider, within the bound.
No kernel may reach another device: no remote copies, remote signals or barrier semaphores. Data moves between devices by JAX's collectives and lax.ppermute only.
A program may use at most 192 MiB of HBM per device.

v0:
```python
import math

import jax
import jax.numpy as jnp
from jax import lax
from jax.sharding import PartitionSpec as P

D = 18432
HEADS = 48
DH = 256


epsilon = 1e-06
contract = (((1,), (1,)), ((), ()))


def rotate(vectors, places):
    half_width = vectors.shape[-1] // 2
    indices = jnp.arange(half_width, dtype=jnp.float32)
    frequency = jnp.exp(-math.log(10000.0) * indices / half_width)
    angles = places * frequency
    cosine = jnp.cos(angles)
    sine = jnp.sin(angles)
    first_half = vectors[..., :half_width]
    second_half = vectors[..., half_width:]
    return jnp.concatenate(
        [first_half * cosine - second_half * sine, second_half * cosine + first_half * sine],
        axis=-1,
    )


def on_device(
    activations,
    norm_gain,
    query_weight,
    keyval_weight,
    output_weight,
    cache_keys,
    cache_values,
    cache_lengths,
):
    inputs = activations.astype(jnp.float32)
    row_sums, square_sums = lax.psum(
        (jnp.sum(inputs, axis=1), jnp.sum(inputs * inputs, axis=1)), "gy"
    )
    row_mean = row_sums[:, None] / D
    row_square = square_sums[:, None] / D
    variance = row_square - row_mean * row_mean
    normed = (
        (inputs - row_mean) * lax.rsqrt(variance + epsilon) * norm_gain.astype(jnp.float32)
    ).astype(jnp.bfloat16)
    shard_rows = lax.all_gather(normed, "gx", axis=0, tiled=True)
    query_part = lax.dot_general(
        shard_rows, query_weight, contract, preferred_element_type=jnp.float32
    )
    keyval_part = lax.dot_general(
        shard_rows, keyval_weight, contract, preferred_element_type=jnp.float32
    )
    partial_sums = jnp.concatenate([query_part, keyval_part], axis=1)
    wide_count = lax.axis_size("gx")
    pair_count = lax.axis_size("gy")
    local_rows = cache_lengths.shape[0]
    stripe = partial_sums.shape[1]
    arrived = lax.all_to_all(partial_sums, ("gx", "gy"), split_axis=0, concat_axis=1, tiled=True)
    gathered = jnp.sum(arrived.reshape(local_rows, wide_count, pair_count, stripe), axis=2).astype(
        jnp.bfloat16
    )
    query_cols = query_weight.shape[0]
    queries = gathered[:, :, :query_cols].reshape(local_rows, HEADS, DH)
    keyvals = gathered[:, :, query_cols:].reshape(local_rows, 2 * DH)
    places = cache_lengths.astype(jnp.float32)
    queries = rotate(queries.astype(jnp.float32), places[:, None, None]).astype(jnp.bfloat16)
    new_keys = rotate(keyvals[:, :DH].astype(jnp.float32), places[:, None]).astype(jnp.bfloat16)
    new_values = keyvals[:, DH:].astype(jnp.float32)
    score_scale = 1.0 / math.sqrt(DH)
    scores = (
        jnp.einsum("rhd,rtd->rht", queries, cache_keys, preferred_element_type=jnp.float32)
        * score_scale
    )
    visible = jnp.arange(cache_keys.shape[1])[None, :] < cache_lengths[:, None]
    scores = jnp.where(visible[:, None, :], scores, -1e30)
    own_score = (
        jnp.einsum("rhd,rd->rh", queries, new_keys, preferred_element_type=jnp.float32)
        * score_scale
    )
    highest = jnp.maximum(jnp.max(scores, axis=2), own_score)
    weights = jnp.exp(scores - highest[:, :, None])
    own_weight = jnp.exp(own_score - highest)
    totals = jnp.sum(weights, axis=2) + own_weight
    blended = jnp.einsum(
        "rht,rtd->rhd",
        weights.astype(jnp.bfloat16),
        cache_values,
        preferred_element_type=jnp.float32,
    )
    blended = blended + own_weight[:, :, None] * new_values[:, None, :]
    attended = (blended / totals[:, :, None]).astype(jnp.bfloat16).reshape(local_rows, HEADS * DH)
    swapped = lax.all_to_all(attended, "gy", split_axis=1, concat_axis=0, tiled=True)
    partial_out = jnp.dot(
        lax.all_gather(swapped, "gx", axis=0, tiled=True),
        output_weight,
        preferred_element_type=jnp.float32,
    )
    return lax.psum_scatter(partial_out, "gy", scatter_dimension=0, tiled=True).astype(jnp.bfloat16)


def solution(mesh):
    return jax.shard_map(
        on_device,
        mesh=mesh,
        in_specs=(
            P(("groups", "gx"), "gy"),
            P("gy"),
            P("gx", "gy"),
            P("gx", "gy"),
            P("gy", "gx"),
            P(("groups", "gx", "gy"), None, None),
            P(("groups", "gx", "gy"), None, None),
            P(("groups", "gx", "gy")),
        ),
        out_specs=P(("groups", "gy"), "gx"),
        check_vma=False,
    )
```

profile of v0, /device:TPU:0, one launch (start us, length us, event | category | flops | bytes accessed | tf_op | source)
XLA Modules:
  0.0 159.2 jit_solution(10203138880374009090)
XLA Ops:
  6.5 0.0 copy-start
  6.5 0.0 all-gather.2.cloned.1.call-start
  6.5 1.2 convert_reduce_fusion
  7.8 0.7 convert_element_type.39
  8.5 2.6 %all-reduce = (f32[8]{0:T(128)S(1)}, f32[8]{0:T(128)S(1)}) all-reduce(f32[8]{0:T(128)S(1)} %get-tuple-element.6, f32[8]{0:T(128)S(1)} %get-tuple-element.5), channel_id=1, replica_groups=mesh['groups'=2,'gx'=8,'gy'=2] {'gy'}, use_global_device_ids=true, to_apply=%region_3.0 | all-reduce | flops 16 | bytes 128 | tf_op jit(solution)/shard_map/psum | solution.py:43
  11.1 1.7 %fusion.9 = bf16[8,9216]{1,0:T(8,128)(2,1)} fusion(bf16[8,9216]{1,0:T(8,128)(2,1)} %param.8, f32[9216]{0:T(1024)S(1)} %convert_element_type.39, f32[8]{0:T(128)S(1)} %get-tuple-element.20, f32[8]{0:T(128)S(1)} %get-tuple-element.19), kind=kLoop, calls=%fused_computation.16 | loop fusion | flops 368640 | bytes 331840 | tf_op jit(solution)/shard_map/convert_element_type | solution.py:51
  12.8 0.0 all-gather.2.cloned.1.call-update
  12.8 43.8 %all-gather.2.cloned.1.call-done = bf16[64,9216]{1,0:T(8,128)(2,1)} async-done(((bf16[8,9216]{1,0:T(8,128)(2,1)}), bf16[64,9216]{1,0:T(8,128)(2,1)}) %all-gather.2.cloned.1.call-update) | async-done | bytes 1179664 | tf_op jit(solution)/shard_map/all_gather | solution.py:52
  56.6 0.0 copy-done
  56.6 0.0 copy-start.2
  56.6 1.8 %fusion.18 = f32[64,64]{1,0:T(8,128)S(1)} fusion(bf16[64,9216]{1,0:T(8,128)(2,1)} %all-gather.2.cloned.1.call-done, bf16[64,9216]{1,0:T(8,128)(2,1)S(1)} %copy-done), kind=kOutput, calls=%fused_computation.43 | convolution fusion | flops 75497472 | bytes 2375680 | tf_op jit(solution)/shard_map/dot_general | solution.py:56
  58.4 0.0 copy-done.2
  58.4 13.8 %fusion.17 = f32[64,1536]{1,0:T(8,128)S(1)} fusion(bf16[64,9216]{1,0:T(8,128)(2,1)S(1)} %copy-done.2, bf16[1536,9216]{1,0:T(8,128)(2,1)} %param.10), kind=kOutput, calls=%fused_computation.42 | convolution fusion | flops 1811939328 | bytes 29884416 | tf_op jit(solution)/shard_map/dot_general | solution.py:53
  72.3 0.0 copy-start.4
  72.3 0.9 all_to_all.26
  73.2 3.6 %all-to-all-start = ((f32[16,4,1600]{2,1,0:T(4,128)}), f32[16,4,1600]{2,1,0:T(4,128)S(1)}, u32[]{:S(2)}, u32[]{:S(2)}) async-start(f32[16,4,1600]{2,1,0:T(4,128)} %all_to_all.26), calls=%async_computation | async-start | bytes 851968 | tf_op jit(solution)/shard_map/all_to_all | solution.py:64
  76.8 0.0 reduce-scatter.2.cloned.1.call-start
  76.8 0.0 copy-done.4
  76.8 0.1 iota_compare_fusion
  76.9 12.5 %all-to-all-done = f32[16,4,1600]{2,1,0:T(4,128)S(1)} async-done(((f32[16,4,1600]{2,1,0:T(4,128)}), f32[16,4,1600]{2,1,0:T(4,128)S(1)}, u32[]{:S(2)}, u32[]{:S(2)}) %all-to-all-start) | async-done | bytes 409632 | tf_op jit(solution)/shard_map/all_to_all | solution.py:64
  89.4 0.1 bitcast_reduce_fusion
  89.6 0.1 reshape.114
  89.7 0.1 subtract_convert_fusion.1
  89.9 0.1 fusion.11
  90.0 0.0 copy-start.3
  90.0 3.8 %fusion.16 = (f32[4,48]{1,0:T(4,128)S(1)}, f32[4,48,2048]{2,1,0:T(8,128)S(1)}) fusion(bf16[4,2048,256]{2,1,0:T(8,128)(2,1)} %param.13, bf16[4,48,128]{2,1,0:T(8,128)(2,1)S(1)} %get-tuple-element.12, bf16[4,48,128]{2,1,0:T(8,128)(2,1)S(1)} %get-tuple-element.11, pred[4,2048]{1,0:T(4,128)(4,1)S(1)} %iota_compare_fusion), kind=kOutput, calls=%fused_computation.41 | convolution fusion | flops 202702656 | bytes 5874432 | tf_op jit(solution)/shard_map/rhd,rtd->rht/dot_general | solution.py:77
  93.8 0.4 fusion.1
  94.2 0.0 copy-done.3
  94.2 0.9 fusion.4
  95.2 0.1 copy.16
  95.2 3.8 %all_to_all.35 = bf16[4,2,6144]{2,0,1:T(4,128)(2,1)S(1)} all-to-all(bf16[4,2,6144]{2,0,1:T(4,128)(2,1)S(1)} %copy.16), channel_id=1, replica_groups=mesh['groups'=2,'gx'=8,'gy'=2] {'gy'}, dimensions={1} | all-to-all | bytes 196608 | tf_op jit(solution)/shard_map/all_to_all | solution.py:98
  99.0 32.2 %all_gather.7 = bf16[64,6144]{1,0:T(8,128)(2,1)S(1)} all-gather(bf16[8,6144]{1,0:T(8,128)(2,1)S(1)} %all_to_all.32), channel_id=1, replica_groups=mesh['groups'=2,'gx'=8,'gy'=2] {'gx'}, dimensions={0}, use_global_device_ids=true | all-gather | bytes 884736 | tf_op jit(solution)/shard_map/all_gather | solution.py:100
  131.2 0.0 copy-start.1
  131.2 12.5 %fusion.19 = f32[64,2304]{1,0:T(8,128)} fusion(bf16[64,6144]{1,0:T(8,128)(2,1)S(1)} %all_gather.7, bf16[6144,2304]{1,0:T(8,128)(2,1)} %param.12), kind=kOutput, calls=%fused_computation.44 | convolution fusion | flops 1811939328 | bytes 29687808 | tf_op jit(solution)/shard_map/dot_general | solution.py:99
  143.7 0.0 reduce-scatter.2.cloned.1.call-update
  143.7 7.0 %reduce-scatter.2.cloned.1.call-done = f32[32,2304]{1,0:T(8,128)} async-done(((f32[64,2304]{1,0:T(8,128)}), f32[32,2304]{1,0:T(8,128)}) %reduce-scatter.2.cloned.1.call-update) | async-done | bytes 294928 | tf_op jit(solution)/shard_map/reduce_scatter | solution.py:104
  150.8 1.6 %convert_element_type.49 = bf16[32,2304]{1,0:T(8,128)(2,1)} convert(f32[32,2304]{1,0:T(8,128)} %reduce-scatter.2.cloned.1.call-done) | non-fusion elementwise | flops 73728 | bytes 442368 | tf_op jit(solution)/shard_map/convert_element_type | solution.py:104
  152.4 0.0 copy-done.1
  (15 shorter events, 0.3 us)
Async XLA Ops:
  6.5 50.0 %copy-start = (bf16[64,9216]{1,0:T(8,128)(2,1)S(1)}, bf16[64,9216]{1,0:T(8,128)(2,1)}, u32[]{:S(2)}) copy-start(bf16[64,9216]{1,0:T(8,128)(2,1)} %param.11) | copy-start | bytes 3538948
  6.5 50.0 %all-gather.2.cloned.1.call-start = ((), (), s32[]{:S(2)}) async-start(), calls=%async_computation.3 | async-start | bytes 1327104 | tf_op jit(solution)/shard_map/all_gather | solution.py:52
  56.6 1.8 %copy-start.2 = (bf16[64,9216]{1,0:T(8,128)(2,1)S(1)}, bf16[64,9216]{1,0:T(8,128)(2,1)}, u32[]{:S(2)}) copy-start(bf16[64,9216]{1,0:T(8,128)(2,1)} %all-gather.2.cloned.1.call-done) | copy-start | bytes 3538948
  72.3 4.6 %copy-start.4 = (s32[4]{0:T(128)S(1)}, s32[4]{0:T(128)}, u32[]{:S(2)}) copy-start(s32[4]{0:T(128)} %param.15) | copy-start | bytes 52
  73.2 16.2 %all-to-all-start = ((f32[16,4,1600]{2,1,0:T(4,128)}), f32[16,4,1600]{2,1,0:T(4,128)S(1)}, u32[]{:S(2)}, u32[]{:S(2)}) async-start(f32[16,4,1600]{2,1,0:T(4,128)} %all_to_all.26), calls=%async_computation | async-start | bytes 851968 | tf_op jit(solution)/shard_map/all_to_all | solution.py:64
  76.8 74.0 %reduce-scatter.2.cloned.1.call-start = ((), (), s32[]{:S(2)}) async-start(), calls=%async_computation.4 | async-start | bytes 884736 | tf_op jit(solution)/shard_map/reduce_scatter | solution.py:104
  90.0 4.2 %copy-start.3 = (bf16[4,2048,256]{2,1,0:T(8,128)(2,1)S(1)}, bf16[4,2048,256]{2,1,0:T(8,128)(2,1)}, u32[]{:S(2)}) copy-start(bf16[4,2048,256]{2,1,0:T(8,128)(2,1)} %param.14) | copy-start | bytes 12582916
  131.2 21.2 %copy-start.1 = (bf16[64,9216]{1,0:T(8,128)(2,1)S(1)}, bf16[64,9216]{1,0:T(8,128)(2,1)}, u32[]{:S(2)}) copy-start(bf16[64,9216]{1,0:T(8,128)(2,1)} %param.11) | copy-start | bytes 3538948
Sparse Core Ops, SparseCore 0:
  12.9 43.6 all-gather.1
  143.9 6.8 reduce-scatter.1
where the time goes:
time: 160 us; the launch traced here: 159 us
  waiting for transfers between devices  63.4 us (40%)
  blocking collectives  38.5 us (24%)
  matrix products  33 us (21%)
  between operations  13.6 us (8%)
  other arithmetic  6.07 us (4%)
  starting transfers between devices  3.6 us (2%)
    all_gather x1, waiting for transfers between devices, on_device(): shard_rows = lax.all_gather(normed, 'gx', axis=0, tiled=True)  43.8 us
    all_gather x1, blocking collectives, on_device(): lax.all_gather(swapped, 'gx', axis=0, tiled=True)  32.2 us
    dot_general x1, matrix products, on_device(): lax.dot_general(shard_rows, query_weight, contract, preferred_element_typ...  13.8 us
    all_to_all x1, waiting for transfers between devices, on_device(): lax.all_to_all(partial_sums, ('gx', 'gy'), split_axis=0, concat_axis=1, t...  12.5 us
    dot_general x1, matrix products, on_device(): jnp.dot(lax.all_gather(swapped, 'gx', axis=0, tiled=True), output_weight,...  12.5 us
    reduce_scatter x1, waiting for transfers between devices, on_device(): lax.psum_scatter(partial_out, 'gy', scatter_dimension=0, tiled=True)  7.02 us
    dot_general x1, matrix products, on_device(): jnp.einsum('rhd,rtd->rht', queries, cache_keys, preferred_element_type=jn...  3.8 us
    all_to_all x1, blocking collectives, on_device(): lax.all_to_all(attended, 'gy', split_axis=1, concat_axis=0, tiled=True)  3.79 us
  transfers between devices with their start and end apart: 3, of which 3 were waited for; matrix products, arithmetic and copies ran while one was open for 0% of the time, Pallas kernels for 0%

commit v1 on v0

--- a/solution.py
+++ b/solution.py
@@ -29,6 +29,51 @@
     )
 
 
+def ring_order(n):
+    return list(range(0, n, 2)) + list(range(n - 1, 0, -2))
+
+
+def swap_pair(x):
+    return lax.ppermute(x, "gy", [(0, 1), (1, 0)])
+
+
+def ring_gather(shard, n):
+    order = ring_order(n)
+    onward = [(order[p], order[(p + 1) % n]) for p in range(n)]
+    back = [(order[p], order[(p - 1) % n]) for p in range(n)]
+    place = jnp.array([order.index(i) for i in range(n)], jnp.int32)[lax.axis_index("gx")]
+    owner = jnp.array(order, jnp.int32)
+    rows, cols = shard.shape
+    half = cols // 2
+    pieces = [(0, shard)]
+    left = right = shard
+    for step in range(1, n // 2):
+        left = lax.ppermute(left, "gx", onward)
+        right = lax.ppermute(right, "gx", back)
+        pieces += [(-step, left), (step, right)]
+    far_left = lax.ppermute(left[:, :half], "gx", onward)
+    far_right = lax.ppermute(right[:, half:], "gx", back)
+    pieces.append((n // 2, jnp.concatenate([far_left, far_right], axis=1)))
+    whole = jnp.zeros((n * rows, cols), shard.dtype)
+    for offset, piece in pieces:
+        source = owner[(place + offset) % n]
+        whole = lax.dynamic_update_slice(whole, piece, (source * rows, 0))
+    return whole
+
+
+def spread_rows(stats, n):
+    if n > 8:
+        return lax.all_gather(stats, "gx", axis=0, tiled=True)
+    me = lax.axis_index("gx")
+    rows = stats.shape[0]
+    whole = jnp.zeros((n * rows,) + stats.shape[1:], stats.dtype)
+    whole = lax.dynamic_update_slice(whole, stats, (me * rows, 0))
+    for shift in range(1, n):
+        got = lax.ppermute(stats, "gx", [(i, (i + shift) % n) for i in range(n)])
+        whole = lax.dynamic_update_slice(whole, got, (((me - shift) % n) * rows, 0))
+    return whole
+
+
 def on_device(
     activations,
     norm_gain,
@@ -39,17 +84,19 @@
     cache_values,
     cache_lengths,
 ):
+    n = lax.axis_size("gx")
+    side = lax.axis_index("gy")
+    everyone = ring_gather(activations, n).astype(jnp.float32)
     inputs = activations.astype(jnp.float32)
-    row_sums, square_sums = lax.psum(
-        (jnp.sum(inputs, axis=1), jnp.sum(inputs * inputs, axis=1)), "gy"
-    )
-    row_mean = row_sums[:, None] / D
-    row_square = square_sums[:, None] / D
+    sums = jnp.stack([jnp.sum(inputs, axis=1), jnp.sum(inputs * inputs, axis=1)], axis=1)
+    sums = sums + swap_pair(sums)
+    sums = spread_rows(sums, n)
+    row_mean = sums[:, :1] / D
+    row_square = sums[:, 1:] / D
     variance = row_square - row_mean * row_mean
-    normed = (
-        (inputs - row_mean) * lax.rsqrt(variance + epsilon) * norm_gain.astype(jnp.float32)
+    shard_rows = (
+        (everyone - row_mean) * lax.rsqrt(variance + epsilon) * norm_gain.astype(jnp.float32)
     ).astype(jnp.bfloat16)
-    shard_rows = lax.all_gather(normed, "gx", axis=0, tiled=True)
     query_part = lax.dot_general(
         shard_rows, query_weight, contract, preferred_element_type=jnp.float32
     )
@@ -57,14 +104,14 @@
         shard_rows, keyval_weight, contract, preferred_element_type=jnp.float32
     )
     partial_sums = jnp.concatenate([query_part, keyval_part], axis=1)
-    wide_count = lax.axis_size("gx")
-    pair_count = lax.axis_size("gy")
     local_rows = cache_lengths.shape[0]
     stripe = partial_sums.shape[1]
-    arrived = lax.all_to_all(partial_sums, ("gx", "gy"), split_axis=0, concat_axis=1, tiled=True)
-    gathered = jnp.sum(arrived.reshape(local_rows, wide_count, pair_count, stripe), axis=2).astype(
-        jnp.bfloat16
-    )
+    by_side = partial_sums.reshape(n, 2, local_rows, stripe)
+    keep = lax.dynamic_index_in_dim(by_side, side, axis=1, keepdims=False)
+    give = lax.dynamic_index_in_dim(by_side, 1 - side, axis=1, keepdims=False)
+    projected = (keep + swap_pair(give)).astype(jnp.bfloat16)
+    gathered = lax.all_to_all(projected, "gx", split_axis=0, concat_axis=0, tiled=True)
+    gathered = jnp.swapaxes(gathered, 0, 1)
     query_cols = query_weight.shape[0]
     queries = gathered[:, :, :query_cols].reshape(local_rows, HEADS, DH)
     keyvals = gathered[:, :, query_cols:].reshape(local_rows, 2 * DH)
@@ -94,14 +141,22 @@
         preferred_element_type=jnp.float32,
     )
     blended = blended + own_weight[:, :, None] * new_values[:, None, :]
-    attended = (blended / totals[:, :, None]).astype(jnp.bfloat16).reshape(local_rows, HEADS * DH)
-    swapped = lax.all_to_all(attended, "gy", split_axis=1, concat_axis=0, tiled=True)
+    attended = (blended / totals[:, :, None]).astype(jnp.bfloat16).reshape(local_rows, 2, -1)
+    mine = lax.dynamic_index_in_dim(attended, side, axis=1, keepdims=False)
+    other = lax.dynamic_index_in_dim(attended, 1 - side, axis=1, keepdims=False)
+    other = swap_pair(other)
+    first = jnp.where(side == 0, mine, other)
+    second = jnp.where(side == 0, other, mine)
+    swapped = jnp.concatenate([first, second], axis=0)
     partial_out = jnp.dot(
-        lax.all_gather(swapped, "gx", axis=0, tiled=True),
+        ring_gather(swapped, n),
         output_weight,
         preferred_element_type=jnp.float32,
     )
-    return lax.psum_scatter(partial_out, "gy", scatter_dimension=0, tiled=True).astype(jnp.bfloat16)
+    by_side = partial_out.reshape(2, -1, partial_out.shape[1])
+    keep = lax.dynamic_index_in_dim(by_side, side, axis=0, keepdims=False)
+    give = lax.dynamic_index_in_dim(by_side, 1 - side, axis=0, keepdims=False)
+    return (keep + swap_pair(give)).astype(jnp.bfloat16)
 
 
 def solution(mesh):

time: 160 us -> 123 us (0.77)
  blocking collectives: 38.5 us -> 0 us
  starting transfers between devices: 3.6 us -> 35.2 us
  waiting for transfers between devices: 63.4 us -> 34.6 us
  local copies, waits for them, and re-layouts: 1.16 us -> 5.99 us
  other arithmetic: 6.07 us -> 3.51 us
  matrix products: 33 us -> 31.1 us
    all_gather x1 -> x0, waiting for transfers between devices: 43.8 us -> none  [on_device(): shard_rows = lax.all_gather(normed, 'gx', axis=0, tiled=True)]
    all_gather x1 -> x0, blocking collectives: 32.2 us -> none  [on_device(): lax.all_gather(swapped, 'gx', axis=0, tiled=True)]
    ppermute x0 -> x27, starting transfers between devices: none -> 30 us  [the longest x7 12.7 us: spread_rows(): got = lax.ppermute(stats, 'gx', [(i, (i + shift) % n) for i in range(n)])]
    ppermute x0 -> x27, waiting for transfers between devices: none -> 27.5 us  [the longest x6 15.6 us: ring_gather(): left = lax.ppermute(left, 'gx', onward)]
    reduce_scatter x1 -> x0, waiting for transfers between devices: 7.02 us -> none  [on_device(): lax.psum_scatter(partial_out, 'gy', scatter_dimension=0, tiled=True)]
    all_to_all x1, waiting for transfers between devices: 12.5 us -> 7.06 us  [on_device(): lax.all_to_all(projected, 'gx', split_axis=0, concat_axis=0, tiled=True)]
    all_to_all x1 -> x0, blocking collectives: 3.79 us -> none  [on_device(): lax.all_to_all(attended, 'gy', split_axis=1, concat_axis=0, tiled=True)]
    dynamic_slice x0 -> x4, local copies, waits for them, and re-layouts: none -> 3.12 us  [the longest x1 1.62 us: ring_gather(): source = owner[(place + offset) % n]]
  transfers between devices with their start and end apart: 3 -> 28, of which waited for: 3 -> 19; matrix products, arithmetic and copies ran while one was open for 0% -> 5% of each run, Pallas kernels for 0% -> 0%
where the time goes in v1:
time: 123 us
  starting transfers between devices  35.2 us (29%)
  waiting for transfers between devices  34.6 us (28%)
  matrix products  31.1 us (25%)
  between operations  12.3 us (10%)
  local copies, waits for them, and re-layouts  5.99 us (5%)
  other arithmetic  3.51 us (3%)
    ppermute x6, waiting for transfers between devices, ring_gather(): left = lax.ppermute(left, 'gx', onward)  15.6 us
    dot_general x1, matrix products, on_device(): lax.dot_general(shard_rows, query_weight, contract, preferred_element_typ...  13.9 us
    ppermute x7, starting transfers between devices, spread_rows(): got = lax.ppermute(stats, 'gx', [(i, (i + shift) % n) for i in range(n)])  12.7 us
    dot_general x1, matrix products, on_device(): jnp.dot(ring_gather(swapped, n), output_weight, preferred_element_type=jn...  11.8 us
    ppermute x6, starting transfers between devices, ring_gather(): right = lax.ppermute(right, 'gx', back)  8.22 us
    all_to_all x1, waiting for transfers between devices, on_device(): lax.all_to_all(projected, 'gx', split_axis=0, concat_axis=0, tiled=True)  7.06 us
    all_to_all x1, starting transfers between devices, on_device(): lax.all_to_all(projected, 'gx', split_axis=0, concat_axis=0, tiled=True)  5.17 us
    ppermute x6, starting transfers between devices, ring_gather(): left = lax.ppermute(left, 'gx', onward)  5.04 us
  transfers between devices with their start and end apart: 28, of which 19 were waited for; matrix products, arithmetic and copies ran while one was open for 5% of the time, Pallas kernels for 0%

profile of v1, /device:TPU:0, one launch (start us, length us, event | category | flops | bytes accessed | tf_op | source)
XLA Modules:
  0.0 122.7 jit_solution(2140894996606995322)
XLA Ops:
  0.0 3.0 %collective-permute-start = (bf16[8,9216]{1,0:T(8,128)(2,1)}, bf16[8,9216]{1,0:T(8,128)(2,1)S(1)}, u32[]{:S(2)}, u32[]{:S(2)}) collective-permute-start(bf16[8,9216]{1,0:T(8,128)(2,1)} %param.12), channel_id=1, source_target_pairs={{0,4},{4,8},{8,12},{12,14},{14,10},{10,6},{6,2},{2,0},{1,5},{5,9},... | collective-permute-start | bytes 442376 | tf_op jit(solution)/shard_map/ppermute | solution.py:51
  3.0 1.2 convert_reduce_fusion
  4.3 1.2 %dynamic_slice.75 = s32[1]{0:T(128)} dynamic-slice(s32[8]{0:T(128)} %constant.205.clone, s32[]{:T(128)S(6)} %select_n.249), dynamic_slice_sizes={1} | dynamic-slice | bytes 12 | tf_op jit(solution)/shard_map/dynamic_slice | solution.py:44
  12.2 1.6 %fusion.20 = (s32[1]{0:T(128)}, s32[1]{0:T(128)}, s32[1]{0:T(128)}, s32[1]{0:T(128)}, s32[1]{0:T(128)}, /*index=5*/s32[1]{0:T(128)}, s32[1]{0:T(128)}, s32[1]{0:T(128)}) fusion(s32[8]{0:T(128)} %constant.206.clone, s32[]{:T(128)S(6)} %select_n.272, s32[]{:T(128)S(6)} %select_n.266, s32[]{:T(128)S(6)} %select_n.263, s32[]{:T(128)S(6)} %select_n.260, ...), kind=kLoop, calls=%fused_computation.74 | loop fusion | bytes 96 | tf_op jit(solution)/shard_map/dynamic_slice | solution.py:59
  19.0 0.7 convert_element_type.43
  20.0 2.0 %collective-permute-start.9 = (f32[8,2]{0,1:T(2,128)S(1)}, f32[8,2]{0,1:T(2,128)S(1)}, u32[]{:S(2)}, u32[]{:S(2)}) collective-permute-start(f32[8,2]{0,1:T(2,128)S(1)} %fusion.16), channel_id=1, source_target_pairs={{0,2},{2,4},{4,6},{6,8},{8,10},{10,12},{12,14},{14,0},{1,3},{3,5},... | collective-permute-start | bytes 200 | tf_op jit(solution)/shard_map/ppermute | solution.py:72
  22.0 1.6 %collective-permute-start.10 = (f32[8,2]{0,1:T(2,128)S(1)}, f32[8,2]{0,1:T(2,128)S(1)}, u32[]{:S(2)}, u32[]{:S(2)}) collective-permute-start(f32[8,2]{0,1:T(2,128)S(1)} %fusion.16), channel_id=1, source_target_pairs={{0,4},{2,6},{4,8},{6,10},{8,12},{10,14},{12,0},{14,2},{1,5},{3,7},... | collective-permute-start | bytes 200 | tf_op jit(solution)/shard_map/ppermute | solution.py:72
  23.5 2.5 %collective-permute-start.11 = (f32[8,2]{0,1:T(2,128)S(1)}, f32[8,2]{0,1:T(2,128)S(1)}, u32[]{:S(2)}, u32[]{:S(2)}) collective-permute-start(f32[8,2]{0,1:T(2,128)S(1)} %fusion.16), channel_id=1, source_target_pairs={{0,6},{2,8},{4,10},{6,12},{8,14},{10,0},{12,2},{14,4},{1,7},{3,9},... | collective-permute-start | bytes 200 | tf_op jit(solution)/shard_map/ppermute | solution.py:72
  26.2 0.4 collective-permute-done.9
  26.6 1.0 collective-permute-start.12
  27.8 2.7 %collective-permute-start.13 = (f32[8,2]{0,1:T(2,128)S(1)}, f32[8,2]{0,1:T(2,128)S(1)}, u32[]{:S(2)}, u32[]{:S(2)}) collective-permute-start(f32[8,2]{0,1:T(2,128)S(1)} %fusion.16), channel_id=1, source_target_pairs={{0,10},{2,12},{4,14},{6,0},{8,2},{10,4},{12,6},{14,8},{1,11},{3,13... | collective-permute-start | bytes 200 | tf_op jit(solution)/shard_map/ppermute | solution.py:72
  30.7 1.4 %collective-permute-start.14 = (f32[8,2]{0,1:T(2,128)S(1)}, f32[8,2]{0,1:T(2,128)S(1)}, u32[]{:S(2)}, u32[]{:S(2)}) collective-permute-start(f32[8,2]{0,1:T(2,128)S(1)} %fusion.16), channel_id=1, source_target_pairs={{0,12},{2,14},{4,0},{6,2},{8,4},{10,6},{12,8},{14,10},{1,13},{3,15... | collective-permute-start | bytes 200 | tf_op jit(solution)/shard_map/ppermute | solution.py:72
  32.3 1.5 %collective-permute-start.15 = (f32[8,2]{0,1:T(2,128)S(1)}, f32[8,2]{0,1:T(2,128)S(1)}, u32[]{:S(2)}, u32[]{:S(2)}) collective-permute-start(f32[8,2]{0,1:T(2,128)S(1)} %fusion.16), channel_id=1, source_target_pairs={{0,14},{2,0},{4,2},{6,4},{8,6},{10,8},{12,10},{14,12},{1,15},{3,1}... | collective-permute-start | bytes 200 | tf_op jit(solution)/shard_map/ppermute | solution.py:72
  34.5 1.4 %collective-permute-done.15 = f32[8,2]{0,1:T(2,128)S(1)} collective-permute-done((f32[8,2]{0,1:T(2,128)S(1)}, f32[8,2]{0,1:T(2,128)S(1)}, u32[]{:S(2)}, u32[]{:S(2)}) %collective-permute-start.15) | collective-permute-done | bytes 96 | tf_op jit(solution)/shard_map/ppermute | solution.py:72
  36.1 0.7 collective-permute-start.2
  36.8 1.3 %collective-permute-start.3 = (bf16[8,9216]{1,0:T(8,128)(2,1)S(1)}, bf16[8,9216]{1,0:T(8,128)(2,1)S(1)}, u32[]{:S(2)}, u32[]{:S(2)}) collective-permute-start(bf16[8,9216]{1,0:T(8,128)(2,1)S(1)} %collective-permute-done.1), channel_id=1, source_target_pairs={{0,2},{4,0},{8,4},{12,8},{14,12},{10,14},{6,10},{2,6},{1,3},{5,1},... | collective-permute-start | bytes 442376 | tf_op jit(solution)/shard_map/ppermute | solution.py:52
  38.2 4.0 %collective-permute-done.2 = bf16[8,9216]{1,0:T(8,128)(2,1)S(1)} collective-permute-done((bf16[8,9216]{1,0:T(8,128)(2,1)S(1)}, bf16[8,9216]{1,0:T(8,128)(2,1)S(1)}, u32[]{:S(2)}, u32[]{:S(2)}) %collective-permute-start.2) | collective-permute-done | bytes 147488 | tf_op jit(solution)/shard_map/ppermute | solution.py:51
  42.2 0.7 collective-permute-start.4
  42.9 0.3 collective-permute-done.3
  43.2 1.3 %collective-permute-start.5 = (bf16[8,9216]{1,0:T(8,128)(2,1)S(1)}, bf16[8,9216]{1,0:T(8,128)(2,1)S(1)}, u32[]{:S(2)}, u32[]{:S(2)}) collective-permute-start(bf16[8,9216]{1,0:T(8,128)(2,1)S(1)} %collective-permute-done.3), channel_id=1, source_target_pairs={{0,2},{4,0},{8,4},{12,8},{14,12},{10,14},{6,10},{2,6},{1,3},{5,1},... | collective-permute-start | bytes 442376 | tf_op jit(solution)/shard_map/ppermute | solution.py:52
  44.6 3.4 %collective-permute-done.4 = bf16[8,9216]{1,0:T(8,128)(2,1)S(1)} collective-permute-done((bf16[8,9216]{1,0:T(8,128)(2,1)S(1)}, bf16[8,9216]{1,0:T(8,128)(2,1)S(1)}, u32[]{:S(2)}, u32[]{:S(2)}) %collective-permute-start.4) | collective-permute-done | bytes 147488 | tf_op jit(solution)/shard_map/ppermute | solution.py:51
  48.0 0.4 collective-permute-start.6
  48.4 1.7 %collective-permute-start.7 = (bf16[8,4608]{1,0:T(8,128)(2,1)S(1)}, bf16[8,4608]{1,0:T(8,128)(2,1)S(1)}, u32[]{:S(2)}, u32[]{:S(2)}) collective-permute-start(bf16[8,4608]{1,0:T(8,128)(2,1)S(1)} %slice.57), channel_id=1, source_target_pairs={{0,2},{4,0},{8,4},{12,8},{14,12},{10,14},{6,10},{2,6},{1,3},{5,1},... | collective-permute-start | bytes 221192 | tf_op jit(solution)/shard_map/ppermute | solution.py:55
  50.1 2.2 %collective-permute-done.6 = bf16[8,4608]{1,0:T(8,128)(2,1)S(1)} collective-permute-done((bf16[8,4608]{1,0:T(8,128)(2,1)S(1)}, bf16[8,4608]{1,0:T(8,128)(2,1)S(1)}, u32[]{:S(2)}, u32[]{:S(2)}) %collective-permute-start.6) | collective-permute-done | bytes 73760 | tf_op jit(solution)/shard_map/ppermute | solution.py:54
  52.3 0.5 collective-permute-done.7
  52.8 13.9 %fusion.18 = f32[64,1536]{1,0:T(8,128)S(1)} fusion(bf16[1536,9216]{1,0:T(8,128)(2,1)} %param.14, bf16[64,9216]{1,0:T(8,128)(2,1)S(1)} %maximum_dynamic-update-slice_fusion, f32[9216]{0:T(1024)S(1)} %convert_element_type.43, f32[64]{0:T(128)S(1)} %get-tuple-element.26, f32[64]{0:T(128)S(1)} %get-tuple-element.25), kind=kOutput, calls=%fused_computation.72 | convolution fusion | flops 1814888448 | bytes 29921792 | tf_op jit(solution)/shard_map/dot_general | solution.py:100
  66.7 0.6 fusion.17
  67.7 1.5 %collective-permute-done.16 = f32[8,4,1600]{2,0,1:T(8,128)S(1)} collective-permute-done((f32[8,4,1600]{2,0,1:T(8,128)S(1)}, f32[8,4,1600]{2,0,1:T(8,128)S(1)}, u32[]{:S(2)}, u32[]{:S(2)}) %collective-permute-start.16) | collective-permute-done | bytes 204832 | tf_op jit(solution)/shard_map/ppermute | solution.py:37
  69.1 0.7 copy.32
  69.8 5.2 %all-to-all-start = ((bf16[8,4,1600]{2,1,0:T(4,128)(2,1)}), bf16[8,4,1600]{2,1,0:T(4,128)(2,1)S(1)}, u32[]{:S(2)}, u32[]{:S(2)}) async-start(bf16[8,4,1600]{2,1,0:T(4,128)(2,1)} %copy.32), calls=%async_computation | async-start | bytes 212992 | tf_op jit(solution)/shard_map/all_to_all | solution.py:113
  75.1 7.1 %all-to-all-done = bf16[8,4,1600]{2,1,0:T(4,128)(2,1)S(1)} async-done(((bf16[8,4,1600]{2,1,0:T(4,128)(2,1)}), bf16[8,4,1600]{2,1,0:T(4,128)(2,1)S(1)}, u32[]{:S(2)}, u32[]{:S(2)}) %all-to-all-start) | async-done | bytes 102432 | tf_op jit(solution)/shard_map/all_to_all | solution.py:113
  82.7 3.8 %fusion.21 = (f32[4,48]{1,0:T(4,128)S(1)}, f32[4,48,2048]{2,1,0:T(8,128)S(1)}) fusion(bf16[4,2048,256]{2,1,0:T(8,128)(2,1)} %param.17, bf16[4,48,128]{2,1,0:T(8,128)(2,1)S(1)} %get-tuple-element.12, bf16[4,48,128]{2,1,0:T(8,128)(2,1)S(1)} %get-tuple-element.11, pred[4,2048]{1,0:T(4,128)(4,1)S(1)} %iota_compare_fusion), kind=kOutput, calls=%fused_computation.75 | convolution fusion | flops 202702656 | bytes 5874432 | tf_op jit(solution)/shard_map/rhd,rtd->rht/dot_general | solution.py:124
  86.5 0.4 fusion.1
  86.9 0.9 fusion.4
  88.1 1.2 collective-permute-done.17
  89.6 2.0 %collective-permute-start.19 = (bf16[8,6144]{1,0:T(8,128)(2,1)S(1)}, bf16[8,6144]{1,0:T(8,128)(2,1)S(1)}, u32[]{:S(2)}, u32[]{:S(2)}) collective-permute-start(bf16[8,6144]{1,0:T(8,128)(2,1)S(1)} %get-tuple-element.15), channel_id=1, source_target_pairs={{0,2},{4,0},{8,4},{12,8},{14,12},{10,14},{6,10},{2,6},{1,3},{5,1},... | collective-permute-start | bytes 294920 | tf_op jit(solution)/shard_map/ppermute | solution.py:52
  91.6 2.8 %collective-permute-done.18 = bf16[8,6144]{1,0:T(8,128)(2,1)S(1)} collective-permute-done((bf16[8,6144]{1,0:T(8,128)(2,1)S(1)}, bf16[8,6144]{1,0:T(8,128)(2,1)S(1)}, u32[]{:S(2)}, u32[]{:S(2)}) %collective-permute-start.18) | collective-permute-done | bytes 98336 | tf_op jit(solution)/shard_map/ppermute | solution.py:51
  94.8 1.8 %collective-permute-start.21 = (bf16[8,6144]{1,0:T(8,128)(2,1)S(1)}, bf16[8,6144]{1,0:T(8,128)(2,1)S(1)}, u32[]{:S(2)}, u32[]{:S(2)}) collective-permute-start(bf16[8,6144]{1,0:T(8,128)(2,1)S(1)} %collective-permute-done.19), channel_id=1, source_target_pairs={{0,2},{4,0},{8,4},{12,8},{14,12},{10,14},{6,10},{2,6},{1,3},{5,1},... | collective-permute-start | bytes 294920 | tf_op jit(solution)/shard_map/ppermute | solution.py:52
  96.6 2.5 %collective-permute-done.20 = bf16[8,6144]{1,0:T(8,128)(2,1)S(1)} collective-permute-done((bf16[8,6144]{1,0:T(8,128)(2,1)S(1)}, bf16[8,6144]{1,0:T(8,128)(2,1)S(1)}, u32[]{:S(2)}, u32[]{:S(2)}) %collective-permute-start.20) | collective-permute-done | bytes 98336 | tf_op jit(solution)/shard_map/ppermute | solution.py:51
  99.4 1.7 %collective-permute-start.23 = (bf16[8,6144]{1,0:T(8,128)(2,1)S(1)}, bf16[8,6144]{1,0:T(8,128)(2,1)S(1)}, u32[]{:S(2)}, u32[]{:S(2)}) collective-permute-start(bf16[8,6144]{1,0:T(8,128)(2,1)S(1)} %collective-permute-done.21), channel_id=1, source_target_pairs={{0,2},{4,0},{8,4},{12,8},{14,12},{10,14},{6,10},{2,6},{1,3},{5,1},... | collective-permute-start | bytes 294920 | tf_op jit(solution)/shard_map/ppermute | solution.py:52
  101.2 2.9 %collective-permute-done.22 = bf16[8,6144]{1,0:T(8,128)(2,1)S(1)} collective-permute-done((bf16[8,6144]{1,0:T(8,128)(2,1)S(1)}, bf16[8,6144]{1,0:T(8,128)(2,1)S(1)}, u32[]{:S(2)}, u32[]{:S(2)}) %collective-permute-start.22) | collective-permute-done | bytes 98336 | tf_op jit(solution)/shard_map/ppermute | solution.py:51
  104.1 0.3 collective-permute-done.23
  104.4 1.8 %collective-permute-start.25 = (bf16[8,3072]{1,0:T(8,128)(2,1)S(1)}, bf16[8,3072]{1,0:T(8,128)(2,1)S(1)}, u32[]{:S(2)}, u32[]{:S(2)}) collective-permute-start(bf16[8,3072]{1,0:T(8,128)(2,1)S(1)} %slice.67), channel_id=1, source_target_pairs={{0,2},{4,0},{8,4},{12,8},{14,12},{10,14},{6,10},{2,6},{1,3},{5,1},... | collective-permute-start | bytes 147464 | tf_op jit(solution)/shard_map/ppermute | solution.py:55
  106.2 2.0 %collective-permute-done.24 = bf16[8,3072]{1,0:T(8,128)(2,1)S(1)} collective-permute-done((bf16[8,3072]{1,0:T(8,128)(2,1)S(1)}, bf16[8,3072]{1,0:T(8,128)(2,1)S(1)}, u32[]{:S(2)}, u32[]{:S(2)}) %collective-permute-start.24) | collective-permute-done | bytes 49184 | tf_op jit(solution)/shard_map/ppermute | solution.py:54
  108.2 0.3 collective-permute-done.25
  108.6 11.8 %fusion.22 = f32[64,2304]{1,0:T(8,128)S(1)} fusion(bf16[64,6144]{1,0:T(8,128)(2,1)S(1)} %maximum_dynamic-update-slice_fusion.1, bf16[6144,2304]{1,0:T(8,128)(2,1)} %param.16), kind=kOutput, calls=%fused_computation.76 | convolution fusion | flops 1811939328 | bytes 29687808 | tf_op jit(solution)/shard_map/dot_general | solution.py:151
  120.4 1.6 %collective-permute-done.26 = f32[32,2304]{1,0:T(8,128)S(1)} collective-permute-done((f32[32,2304]{1,0:T(8,128)S(1)}, f32[32,2304]{1,0:T(8,128)S(1)}, u32[]{:S(2)}, u32[]{:S(2)}) %collective-permute-start.26) | collective-permute-done | bytes 294944 | tf_op jit(solution)/shard_map/ppermute | solution.py:37
  122.0 0.7 fusion.8
  (89 shorter events, 4.2 us)
Async XLA Ops:
  0.0 66.7 %copy-start = (bf16[64,9216]{1,0:T(8,128)(2,1)S(1)}, bf16[64,9216]{1,0:T(8,128)(2,1)}, u32[]{:S(2)}) copy-start(bf16[64,9216]{1,0:T(8,128)(2,1)} %param.15) | copy-start | bytes 3538948
  0.0 19.8 %copy-start.3 = (bf16[8,9216]{1,0:T(8,128)(2,1)S(1)}, bf16[8,9216]{1,0:T(8,128)(2,1)}, u32[]{:S(2)}) copy-start(bf16[8,9216]{1,0:T(8,128)(2,1)} %param.12) | copy-start | bytes 442372
  0.0 36.1 %collective-permute-start = (bf16[8,9216]{1,0:T(8,128)(2,1)}, bf16[8,9216]{1,0:T(8,128)(2,1)S(1)}, u32[]{:S(2)}, u32[]{:S(2)}) collective-permute-start(bf16[8,9216]{1,0:T(8,128)(2,1)} %param.12), channel_id=1, source_target_pairs={{0,4},{4,8},{8,12},{12,14},{14,10},{10,6},{6,2},{2,0},{1,5},{5,9},... | collective-permute-start | bytes 442376 | tf_op jit(solution)/shard_map/ppermute | solution.py:51
  3.0 33.8 %collective-permute-start.1 = (bf16[8,9216]{1,0:T(8,128)(2,1)}, bf16[8,9216]{1,0:T(8,128)(2,1)S(1)}, u32[]{:S(2)}, u32[]{:S(2)}) collective-permute-start(bf16[8,9216]{1,0:T(8,128)(2,1)} %param.12), channel_id=1, source_target_pairs={{0,2},{4,0},{8,4},{12,8},{14,12},{10,14},{6,10},{2,6},{1,3},{5,1},... | collective-permute-start | bytes 442376 | tf_op jit(solution)/shard_map/ppermute | solution.py:52
  4.2 15.7 %collective-permute-start.8 = (f32[8,2]{0,1:T(2,128)S(1)}, f32[8,2]{0,1:T(2,128)S(1)}, u32[]{:S(2)}, u32[]{:S(2)}) collective-permute-start(f32[8,2]{0,1:T(2,128)S(1)} %pad_maximum_fusion.5), channel_id=1, source_target_pairs={{0,1},{1,0},{2,3},{3,2},{4,5},{5,4},{6,7},{7,6},{8,9},{9,8},{10,11... | collective-permute-start | bytes 200 | tf_op jit(solution)/shard_map/ppermute | solution.py:37
  20.0 6.6 %collective-permute-start.9 = (f32[8,2]{0,1:T(2,128)S(1)}, f32[8,2]{0,1:T(2,128)S(1)}, u32[]{:S(2)}, u32[]{:S(2)}) collective-permute-start(f32[8,2]{0,1:T(2,128)S(1)} %fusion.16), channel_id=1, source_target_pairs={{0,2},{2,4},{4,6},{6,8},{8,10},{10,12},{12,14},{14,0},{1,3},{3,5},... | collective-permute-start | bytes 200 | tf_op jit(solution)/shard_map/ppermute | solution.py:72
  22.0 5.8 %collective-permute-start.10 = (f32[8,2]{0,1:T(2,128)S(1)}, f32[8,2]{0,1:T(2,128)S(1)}, u32[]{:S(2)}, u32[]{:S(2)}) collective-permute-start(f32[8,2]{0,1:T(2,128)S(1)} %fusion.16), channel_id=1, source_target_pairs={{0,4},{2,6},{4,8},{6,10},{8,12},{10,14},{12,0},{14,2},{1,5},{3,7},... | collective-permute-start | bytes 200 | tf_op jit(solution)/shard_map/ppermute | solution.py:72
  23.5 7.1 %collective-permute-start.11 = (f32[8,2]{0,1:T(2,128)S(1)}, f32[8,2]{0,1:T(2,128)S(1)}, u32[]{:S(2)}, u32[]{:S(2)}) collective-permute-start(f32[8,2]{0,1:T(2,128)S(1)} %fusion.16), channel_id=1, source_target_pairs={{0,6},{2,8},{4,10},{6,12},{8,14},{10,0},{12,2},{14,4},{1,7},{3,9},... | collective-permute-start | bytes 200 | tf_op jit(solution)/shard_map/ppermute | solution.py:72
  26.6 5.7 %collective-permute-start.12 = (f32[8,2]{0,1:T(2,128)S(1)}, f32[8,2]{0,1:T(2,128)S(1)}, u32[]{:S(2)}, u32[]{:S(2)}) collective-permute-start(f32[8,2]{0,1:T(2,128)S(1)} %fusion.16), channel_id=1, source_target_pairs={{0,8},{2,10},{4,12},{6,14},{8,0},{10,2},{12,4},{14,6},{1,9},{3,11}... | collective-permute-start | bytes 200 | tf_op jit(solution)/shard_map/ppermute | solution.py:72
  27.8 6.1 %collective-permute-start.13 = (f32[8,2]{0,1:T(2,128)S(1)}, f32[8,2]{0,1:T(2,128)S(1)}, u32[]{:S(2)}, u32[]{:S(2)}) collective-permute-start(f32[8,2]{0,1:T(2,128)S(1)} %fusion.16), channel_id=1, source_target_pairs={{0,10},{2,12},{4,14},{6,0},{8,2},{10,4},{12,6},{14,8},{1,11},{3,13... | collective-permute-start | bytes 200 | tf_op jit(solution)/shard_map/ppermute | solution.py:72
  30.7 3.6 %collective-permute-start.14 = (f32[8,2]{0,1:T(2,128)S(1)}, f32[8,2]{0,1:T(2,128)S(1)}, u32[]{:S(2)}, u32[]{:S(2)}) collective-permute-start(f32[8,2]{0,1:T(2,128)S(1)} %fusion.16), channel_id=1, source_target_pairs={{0,12},{2,14},{4,0},{6,2},{8,4},{10,6},{12,8},{14,10},{1,13},{3,15... | collective-permute-start | bytes 200 | tf_op jit(solution)/shard_map/ppermute | solution.py:72
  32.3 3.6 %collective-permute-start.15 = (f32[8,2]{0,1:T(2,128)S(1)}, f32[8,2]{0,1:T(2,128)S(1)}, u32[]{:S(2)}, u32[]{:S(2)}) collective-permute-start(f32[8,2]{0,1:T(2,128)S(1)} %fusion.16), channel_id=1, source_target_pairs={{0,14},{2,0},{4,2},{6,4},{8,6},{10,8},{12,10},{14,12},{1,15},{3,1}... | collective-permute-start | bytes 200 | tf_op jit(solution)/shard_map/ppermute | solution.py:72
  36.1 6.1 %collective-permute-start.2 = (bf16[8,9216]{1,0:T(8,128)(2,1)S(1)}, bf16[8,9216]{1,0:T(8,128)(2,1)S(1)}, u32[]{:S(2)}, u32[]{:S(2)}) collective-permute-start(bf16[8,9216]{1,0:T(8,128)(2,1)S(1)} %collective-permute-done), channel_id=1, source_target_pairs={{0,4},{4,8},{8,12},{12,14},{14,10},{10,6},{6,2},{2,0},{1,5},{5,9},... | collective-permute-start | bytes 442376 | tf_op jit(solution)/shard_map/ppermute | solution.py:51
  36.8 6.4 %collective-permute-start.3 = (bf16[8,9216]{1,0:T(8,128)(2,1)S(1)}, bf16[8,9216]{1,0:T(8,128)(2,1)S(1)}, u32[]{:S(2)}, u32[]{:S(2)}) collective-permute-start(bf16[8,9216]{1,0:T(8,128)(2,1)S(1)} %collective-permute-done.1), channel_id=1, source_target_pairs={{0,2},{4,0},{8,4},{12,8},{14,12},{10,14},{6,10},{2,6},{1,3},{5,1},... | collective-permute-start | bytes 442376 | tf_op jit(solution)/shard_map/ppermute | solution.py:52
  42.2 5.7 %collective-permute-start.4 = (bf16[8,9216]{1,0:T(8,128)(2,1)S(1)}, bf16[8,9216]{1,0:T(8,128)(2,1)S(1)}, u32[]{:S(2)}, u32[]{:S(2)}) collective-permute-start(bf16[8,9216]{1,0:T(8,128)(2,1)S(1)} %collective-permute-done.2), channel_id=1, source_target_pairs={{0,4},{4,8},{8,12},{12,14},{14,10},{10,6},{6,2},{2,0},{1,5},{5,9},... | collective-permute-start | bytes 442376 | tf_op jit(solution)/shard_map/ppermute | solution.py:51
  43.2 5.1 %collective-permute-start.5 = (bf16[8,9216]{1,0:T(8,128)(2,1)S(1)}, bf16[8,9216]{1,0:T(8,128)(2,1)S(1)}, u32[]{:S(2)}, u32[]{:S(2)}) collective-permute-start(bf16[8,9216]{1,0:T(8,128)(2,1)S(1)} %collective-permute-done.3), channel_id=1, source_target_pairs={{0,2},{4,0},{8,4},{12,8},{14,12},{10,14},{6,10},{2,6},{1,3},{5,1},... | collective-permute-start | bytes 442376 | tf_op jit(solution)/shard_map/ppermute | solution.py:52
  48.0 4.4 %collective-permute-start.6 = (bf16[8,4608]{1,0:T(8,128)(2,1)S(1)}, bf16[8,4608]{1,0:T(8,128)(2,1)S(1)}, u32[]{:S(2)}, u32[]{:S(2)}) collective-permute-start(bf16[8,4608]{1,0:T(8,128)(2,1)S(1)} %slice.56), channel_id=1, source_target_pairs={{0,4},{4,8},{8,12},{12,14},{14,10},{10,6},{6,2},{2,0},{1,5},{5,9},... | collective-permute-start | bytes 221192 | tf_op jit(solution)/shard_map/ppermute | solution.py:54
  48.4 4.4 %collective-permute-start.7 = (bf16[8,4608]{1,0:T(8,128)(2,1)S(1)}, bf16[8,4608]{1,0:T(8,128)(2,1)S(1)}, u32[]{:S(2)}, u32[]{:S(2)}) collective-permute-start(bf16[8,4608]{1,0:T(8,128)(2,1)S(1)} %slice.57), channel_id=1, source_target_pairs={{0,2},{4,0},{8,4},{12,8},{14,12},{10,14},{6,10},{2,6},{1,3},{5,1},... | collective-permute-start | bytes 221192 | tf_op jit(solution)/shard_map/ppermute | solution.py:55
  67.4 7.6 %copy-start.4 = (s32[4]{0:T(128)S(1)}, s32[4]{0:T(128)}, u32[]{:S(2)}) copy-start(s32[4]{0:T(128)} %param.19) | copy-start | bytes 52
  67.6 1.5 %collective-permute-start.16 = (f32[8,4,1600]{2,0,1:T(8,128)S(1)}, f32[8,4,1600]{2,0,1:T(8,128)S(1)}, u32[]{:S(2)}, u32[]{:S(2)}) collective-permute-start(f32[8,4,1600]{2,0,1:T(8,128)S(1)} %bitcast.57), channel_id=1, source_target_pairs={{0,1},{1,0},{2,3},{3,2},{4,5},{5,4},{6,7},{7,6},{8,9},{9,8},{10,11... | collective-permute-start | bytes 614408 | tf_op jit(solution)/shard_map/ppermute | solution.py:37
  69.8 12.3 %all-to-all-start = ((bf16[8,4,1600]{2,1,0:T(4,128)(2,1)}), bf16[8,4,1600]{2,1,0:T(4,128)(2,1)S(1)}, u32[]{:S(2)}, u32[]{:S(2)}) async-start(bf16[8,4,1600]{2,1,0:T(4,128)(2,1)} %copy.32), calls=%async_computation | async-start | bytes 212992 | tf_op jit(solution)/shard_map/all_to_all | solution.py:113
  82.7 4.2 %copy-start.2 = (bf16[4,2048,256]{2,1,0:T(8,128)(2,1)S(1)}, bf16[4,2048,256]{2,1,0:T(8,128)(2,1)}, u32[]{:S(2)}) copy-start(bf16[4,2048,256]{2,1,0:T(8,128)(2,1)} %param.18) | copy-start | bytes 12582916
  88.1 1.3 %collective-permute-start.17 = (bf16[4,6144]{1,0:T(4,128)(2,1)S(1)}, bf16[4,6144]{1,0:T(4,128)(2,1)S(1)}, u32[]{:S(2)}, u32[]{:S(2)}) collective-permute-start(bf16[4,6144]{1,0:T(4,128)(2,1)S(1)} %bitcast.58), channel_id=1, source_target_pairs={{0,1},{1,0},{2,3},{3,2},{4,5},{5,4},{6,7},{7,6},{8,9},{9,8},{10,11... | collective-permute-start | bytes 147464 | tf_op jit(solution)/shard_map/ppermute | solution.py:37
  89.5 4.9 %collective-permute-start.18 = (bf16[8,6144]{1,0:T(8,128)(2,1)S(1)}, bf16[8,6144]{1,0:T(8,128)(2,1)S(1)}, u32[]{:S(2)}, u32[]{:S(2)}) collective-permute-start(bf16[8,6144]{1,0:T(8,128)(2,1)S(1)} %get-tuple-element.15), channel_id=1, source_target_pairs={{0,4},{4,8},{8,12},{12,14},{14,10},{10,6},{6,2},{2,0},{1,5},{5,9},... | collective-permute-start | bytes 294920 | tf_op jit(solution)/shard_map/ppermute | solution.py:51
  89.6 5.2 %collective-permute-start.19 = (bf16[8,6144]{1,0:T(8,128)(2,1)S(1)}, bf16[8,6144]{1,0:T(8,128)(2,1)S(1)}, u32[]{:S(2)}, u32[]{:S(2)}) collective-permute-start(bf16[8,6144]{1,0:T(8,128)(2,1)S(1)} %get-tuple-element.15), channel_id=1, source_target_pairs={{0,2},{4,0},{8,4},{12,8},{14,12},{10,14},{6,10},{2,6},{1,3},{5,1},... | collective-permute-start | bytes 294920 | tf_op jit(solution)/shard_map/ppermute | solution.py:52
  94.5 4.6 %collective-permute-start.20 = (bf16[8,6144]{1,0:T(8,128)(2,1)S(1)}, bf16[8,6144]{1,0:T(8,128)(2,1)S(1)}, u32[]{:S(2)}, u32[]{:S(2)}) collective-permute-start(bf16[8,6144]{1,0:T(8,128)(2,1)S(1)} %collective-permute-done.18), channel_id=1, source_target_pairs={{0,4},{4,8},{8,12},{12,14},{14,10},{10,6},{6,2},{2,0},{1,5},{5,9},... | collective-permute-start | bytes 294920 | tf_op jit(solution)/shard_map/ppermute | solution.py:51
  94.8 4.7 %collective-permute-start.21 = (bf16[8,6144]{1,0:T(8,128)(2,1)S(1)}, bf16[8,6144]{1,0:T(8,128)(2,1)S(1)}, u32[]{:S(2)}, u32[]{:S(2)}) collective-permute-start(bf16[8,6144]{1,0:T(8,128)(2,1)S(1)} %collective-permute-done.19), channel_id=1, source_target_pairs={{0,2},{4,0},{8,4},{12,8},{14,12},{10,14},{6,10},{2,6},{1,3},{5,1},... | collective-permute-start | bytes 294920 | tf_op jit(solution)/shard_map/ppermute | solution.py:52
  99.1 5.0 %collective-permute-start.22 = (bf16[8,6144]{1,0:T(8,128)(2,1)S(1)}, bf16[8,6144]{1,0:T(8,128)(2,1)S(1)}, u32[]{:S(2)}, u32[]{:S(2)}) collective-permute-start(bf16[8,6144]{1,0:T(8,128)(2,1)S(1)} %collective-permute-done.20), channel_id=1, source_target_pairs={{0,4},{4,8},{8,12},{12,14},{14,10},{10,6},{6,2},{2,0},{1,5},{5,9},... | collective-permute-start | bytes 294920 | tf_op jit(solution)/shard_map/ppermute | solution.py:51
  99.4 5.0 %collective-permute-start.23 = (bf16[8,6144]{1,0:T(8,128)(2,1)S(1)}, bf16[8,6144]{1,0:T(8,128)(2,1)S(1)}, u32[]{:S(2)}, u32[]{:S(2)}) collective-permute-start(bf16[8,6144]{1,0:T(8,128)(2,1)S(1)} %collective-permute-done.21), channel_id=1, source_target_pairs={{0,2},{4,0},{8,4},{12,8},{14,12},{10,14},{6,10},{2,6},{1,3},{5,1},... | collective-permute-start | bytes 294920 | tf_op jit(solution)/shard_map/ppermute | solution.py:52
  104.1 4.1 %collective-permute-start.24 = (bf16[8,3072]{1,0:T(8,128)(2,1)S(1)}, bf16[8,3072]{1,0:T(8,128)(2,1)S(1)}, u32[]{:S(2)}, u32[]{:S(2)}) collective-permute-start(bf16[8,3072]{1,0:T(8,128)(2,1)S(1)} %slice.66), channel_id=1, source_target_pairs={{0,4},{4,8},{8,12},{12,14},{14,10},{10,6},{6,2},{2,0},{1,5},{5,9},... | collective-permute-start | bytes 147464 | tf_op jit(solution)/shard_map/ppermute | solution.py:54
  104.4 4.1 %collective-permute-start.25 = (bf16[8,3072]{1,0:T(8,128)(2,1)S(1)}, bf16[8,3072]{1,0:T(8,128)(2,1)S(1)}, u32[]{:S(2)}, u32[]{:S(2)}) collective-permute-start(bf16[8,3072]{1,0:T(8,128)(2,1)S(1)} %slice.67), channel_id=1, source_target_pairs={{0,2},{4,0},{8,4},{12,8},{14,12},{10,14},{6,10},{2,6},{1,3},{5,1},... | collective-permute-start | bytes 147464 | tf_op jit(solution)/shard_map/ppermute | solution.py:55
  108.5 14.2 %copy-start.1 = (bf16[64,9216]{1,0:T(8,128)(2,1)S(1)}, bf16[64,9216]{1,0:T(8,128)(2,1)}, u32[]{:S(2)}) copy-start(bf16[64,9216]{1,0:T(8,128)(2,1)} %param.15) | copy-start | bytes 3538948
  120.4 1.6 %collective-permute-start.26 = (f32[32,2304]{1,0:T(8,128)S(1)}, f32[32,2304]{1,0:T(8,128)S(1)}, u32[]{:S(2)}, u32[]{:S(2)}) collective-permute-start(f32[32,2304]{1,0:T(8,128)S(1)} %dynamic-slice_bitcast_fusion), channel_id=1, source_target_pairs={{0,1},{1,0},{2,3},{3,2},{4,5},{5,4},{6,7},{7,6},{8,9},{9,8},{10,11... | collective-permute-start | bytes 884744 | tf_op jit(solution)/shard_map/ppermute | solution.py:37

commit v2 on v0

v2 whole, which is shorter than its diff:
```python
import math

import jax
import jax.numpy as jnp
from jax import lax
from jax.experimental import pallas as pl
from jax.experimental.pallas import tpu as pltpu
from jax.sharding import PartitionSpec as P

D = 18432
HEADS = 48
DH = 256


epsilon = 1e-06
contract = (((1,), (1,)), ((), ()))
MIB = 1 << 20
ANY = pl.BlockSpec(memory_space=pl.ANY)
IN_VMEM = pl.BlockSpec(memory_space=pltpu.VMEM)
IN_SMEM = pl.BlockSpec(memory_space=pltpu.SMEM)


def rotate(vectors, places):
    half_width = vectors.shape[-1] // 2
    indices = jnp.arange(half_width, dtype=jnp.float32)
    frequency = jnp.exp(-math.log(10000.0) * indices / half_width)
    angles = places * frequency
    cosine = jnp.cos(angles)
    sine = jnp.sin(angles)
    first_half = vectors[..., :half_width]
    second_half = vectors[..., half_width:]
    return jnp.concatenate(
        [first_half * cosine - second_half * sine, second_half * cosine + first_half * sine],
        axis=-1,
    )


def ring_order(n):
    return list(range(0, n, 2)) + list(range(n - 1, 0, -2))


def swap_pair(x):
    return lax.ppermute(x, "gy", [(0, 1), (1, 0)])


class Ring:
    def __init__(self, n):
        self.n = n
        order = ring_order(n)
        self.onward = [(order[p], order[(p + 1) % n]) for p in range(n)]
        self.back = [(order[p], order[(p - 1) % n]) for p in range(n)]
        self.across = [(order[p], order[(p + n // 2) % n]) for p in range(n)]
        self.offsets = [0]
        for step in range(1, n // 2):
            self.offsets += [-step, step]
        self.offsets.append(n // 2)

    def owners(self):
        n = self.n
        me = lax.axis_index("gx")
        place = jnp.where(me % 2 == 0, me // 2, n - 1 - me // 2)
        at = (place + jnp.array(self.offsets, jnp.int32) + n) % n
        owner = jnp.where(at < n // 2, 2 * at, 2 * (n - 1 - at) + 1)
        return jnp.concatenate([owner, lax.axis_index("gy")[None]]).astype(jnp.int32)

    def step(self, left, right):
        return lax.ppermute(left, "gx", self.onward), lax.ppermute(right, "gx", self.back)


def load_kernel(count, *refs):
    sources, targets, sems = refs[:count], refs[-count - 1 : -1], refs[-1]
    copies = [
        pltpu.make_async_copy(source, target, sems.at[i])
        for i, (source, target) in enumerate(zip(sources, targets))
    ]
    for copy in copies:
        copy.start()
    for copy in copies:
        copy.wait()


def load(arrays, after=()):
    return pl.pallas_call(
        lambda *refs: load_kernel(len(arrays), *refs),
        out_shape=[pltpu.VMEM(a.shape, a.dtype) for a in arrays],
        in_specs=[ANY] * (len(arrays) + len(after)),
        out_specs=[IN_VMEM] * len(arrays),
        scratch_shapes=[pltpu.SemaphoreType.DMA((len(arrays),))],
        compiler_params=pltpu.CompilerParams(vmem_limit_bytes=4 * MIB),
        name="load",
    )(*arrays, *after)


def load_rows_kernel(start, size, *refs):
    source, target, sem = refs[0], refs[-2], refs[-1]
    copy = pltpu.make_async_copy(source.at[pl.ds(start, size)], target, sem)
    copy.start()
    copy.wait()


def load_rows(array, start, size, after=()):
    return pl.pallas_call(
        lambda *refs: load_rows_kernel(start, size, *refs),
        out_shape=pltpu.VMEM((size,) + array.shape[1:], array.dtype),
        in_specs=[ANY] * (1 + len(after)),
        out_specs=IN_VMEM,
        scratch_shapes=[pltpu.SemaphoreType.DMA],
        compiler_params=pltpu.CompilerParams(vmem_limit_bytes=4 * MIB),
        name="load_rows",
    )(array, *after)


def sums_kernel(*refs):
    out = refs[-1]
    rows = refs[0].shape[0]
    lane = lax.broadcasted_iota(jnp.int32, (rows, 128), 1)
    for i, ref in enumerate(refs[:-1]):
        x = ref[...].astype(jnp.float32)
        total = jnp.sum(x, axis=1, keepdims=True)
        square = jnp.sum(x * x, axis=1, keepdims=True)
        both = jnp.where(lane == 0, total, jnp.where(lane == 1, square, 0.0))
        out[i * rows : (i + 1) * rows, :] = both


def row_sums(shards):
    rows = shards[0].shape[0]
    return pl.pallas_call(
        sums_kernel,
        out_shape=jax.ShapeDtypeStruct((len(shards) * rows, 128), jnp.float32),
        in_specs=[IN_VMEM] * len(shards),
        out_specs=IN_VMEM,
        compiler_params=pltpu.CompilerParams(vmem_limit_bytes=16 * MIB),
        name="row_sums",
    )(*shards)


def project_kernel(n, parts, *refs):
    owners, sums_a, sums_b, gain = refs[:4]
    near = refs[4 : 4 + n - 1]
    far = refs[4 + n - 1 : 4 + n + 1]
    weights = refs[4 + n + 1 : 4 + n + 1 + parts]
    keep, give, normed, total = refs[4 + n + 1 + parts :]
    rows = near[0].shape[0]
    half = far[0].shape[1]
    sums = sums_a[...] + sums_b[...]
    row_mean = sums[:, :1] / D
    row_square = sums[:, 1:2] / D
    scale = lax.rsqrt(row_square - row_mean * row_mean + epsilon)
    for part in range(2):
        cols = slice(part * half, (part + 1) * half)
        for i in range(n):
            at = slice(i * rows, (i + 1) * rows)
            x = near[i][:, cols] if i < n - 1 else far[part][...]
            x = (x.astype(jnp.float32) - row_mean[at]) * scale[at] * gain[:, cols]
            normed[at, cols] = x
        x = normed[:, cols].astype(jnp.bfloat16)
        start = 0
        for weight in weights:
            width = weight.shape[0]
            term = lax.dot_general(
                x, weight[:, cols], contract, preferred_element_type=jnp.float32
            )
            if part == 0:
                total[:, start : start + width] = term
            else:
                total[:, start : start + width] += term
            start += width
    side = owners[n]
    local = rows // 2
    for i in range(n):
        block = total[i * rows : (i + 1) * rows, :]
        low, high = block[:local], block[local:]
        keep[owners[i]] = jnp.where(side == 0, low, high)
        give[owners[i]] = jnp.where(side == 0, high, low)


def project(n, owners, sums, gain, near, far, weights):
    rows, width = near[0].shape
    stripe = sum(w.shape[0] for w in weights)
    shape = jax.ShapeDtypeStruct((n, rows // 2, stripe), jnp.float32)
    return pl.pallas_call(
        lambda *refs: project_kernel(n, len(weights), *refs),
        out_shape=[shape, shape],
        in_specs=[IN_SMEM] + [IN_VMEM] * (3 + n + 1 + len(weights)),
        out_specs=[IN_VMEM, IN_VMEM],
        scratch_shapes=[
            pltpu.VMEM((n * rows, width), jnp.float32),
            pltpu.VMEM((n * rows, stripe), jnp.float32),
        ],
        compiler_params=pltpu.CompilerParams(vmem_limit_bytes=(24 if n <= 8 else 48) * MIB),
        name="project",
    )(owners, *sums, gain, *near, *far, *weights)


def output_kernel(n, parts, *refs):
    owners = refs[0]
    near = refs[1:n]
    far = refs[n : n + 2]
    weights = refs[n + 2 : n + 2 + parts]
    keep, give, total, placed = refs[n + 2 + parts :]
    rows = near[0].shape[0]
    half = far[0].shape[1]
    depth = weights[0].shape[0]
    for part, weight in enumerate(weights):
        start = part * depth
        cols = slice(start, start + depth)
        pieces = [ref[:, cols] for ref in near]
        for i, ref in enumerate(far):
            low, high = max(start, i * half), min(start + depth, (i + 1) * half)
            if low < high:
                last = ref[:, low - i * half : high - i * half]
                pieces.append(last)
        if len(pieces) > n:
            pieces[n - 1 :] = [jnp.concatenate(pieces[n - 1 :], axis=1)]
        x = jnp.concatenate([p.astype(jnp.float32) for p in pieces], axis=0)
        term = jnp.dot(
            x.astype(jnp.bfloat16), weight[...], preferred_element_type=jnp.float32
        )
        if part == 0:
            total[...] = term
        else:
            total[...] += term
    for i in range(n):
        placed[owners[i]] = total[i * rows : (i + 1) * rows, :]
    side = owners[n]
    keep[...] = placed[pl.ds(side * (n // 2), n // 2)]
    give[...] = placed[pl.ds((1 - side) * (n // 2), n // 2)]


def output_project(n, owners, near, far, weights):
    rows = near[0].shape[0]
    cols = weights[0].shape[1]
    shape = jax.ShapeDtypeStruct((n // 2, rows, cols), jnp.float32)
    return pl.pallas_call(
        lambda *refs: output_kernel(n, len(weights), *refs),
        out_shape=[shape, shape],
        in_specs=[IN_SMEM] + [IN_VMEM] * (n + 1 + len(weights)),
        out_specs=[IN_VMEM, IN_VMEM],
        scratch_shapes=[
            pltpu.VMEM((n * rows, cols), jnp.float32),
            pltpu.VMEM((n, rows, cols), jnp.float32),
        ],
        compiler_params=pltpu.CompilerParams(vmem_limit_bytes=(24 if n <= 8 else 48) * MIB),
        name="output_project",
    )(owners, *near, *far, *weights)


def on_device(
    activations,
    norm_gain,
    query_weight,
    keyval_weight,
    output_weight,
    cache_keys,
    cache_values,
    cache_lengths,
):
    n = lax.axis_size("gx")
    ring = Ring(n)
    owners = ring.owners()
    query_cols = query_weight.shape[0]
    pieces = 3 if query_cols % (3 * 256) == 0 else 1
    piece = query_cols // pieces
    weights = []

    left = right = activations
    near = [activations]
    own_sums = row_sums([activations])
    far_sums = lax.ppermute(own_sums, "gx", ring.across)
    sums = [own_sums]
    for step in range(1, n // 2):
        if step <= pieces:
            after = [] if step == 1 else [left, right]
            weights.append(load_rows(query_weight, (step - 1) * piece, piece, after))
        left, right = ring.step(left, right)
        near += [left, right]
        sums.append(row_sums([left, right]))
    weights += load([keyval_weight], [left, right])
    half = activations.shape[1] // 2
    far = ring.step(left[:, :half], right[:, half:])
    sums = jnp.concatenate(sums + [far_sums], axis=0)
    sums = (sums, swap_pair(sums))
    gain = norm_gain.astype(jnp.float32)[None, :]
    keep, give = project(n, owners, sums, gain, near, far, weights)
    projected = (keep + swap_pair(give)).astype(jnp.bfloat16)
    local_rows = cache_lengths.shape[0]
    gathered = lax.all_to_all(projected, "gx", split_axis=0, concat_axis=0, tiled=True)
    gathered = jnp.swapaxes(gathered, 0, 1)
    queries = gathered[:, :, :query_cols].reshape(local_rows, HEADS, DH)
    keyvals = gathered[:, :, query_cols:].reshape(local_rows, 2 * DH)
    places = cache_lengths.astype(jnp.float32)
    queries = rotate(queries.astype(jnp.float32), places[:, None, None]).astype(jnp.bfloat16)
    new_keys = rotate(keyvals[:, :DH].astype(jnp.float32), places[:, None]).astype(jnp.bfloat16)
    new_values = keyvals[:, DH:].astype(jnp.float32)
    score_scale = 1.0 / math.sqrt(DH)
    scores = (
        jnp.einsum("rhd,rtd->rht", queries, cache_keys, preferred_element_type=jnp.float32)
        * score_scale
    )
    visible = jnp.arange(cache_keys.shape[1])[None, :] < cache_lengths[:, None]
    scores = jnp.where(visible[:, None, :], scores, -1e30)
    own_score = (
        jnp.einsum("rhd,rd->rh", queries, new_keys, preferred_element_type=jnp.float32)
        * score_scale
    )
    highest = jnp.maximum(jnp.max(scores, axis=2), own_score)
    weights = jnp.exp(scores - highest[:, :, None])
    own_weight = jnp.exp(own_score - highest)
    totals = jnp.sum(weights, axis=2) + own_weight
    blended = jnp.einsum(
        "rht,rtd->rhd",
        weights.astype(jnp.bfloat16),
        cache_values,
        preferred_element_type=jnp.float32,
    )
    blended = blended + own_weight[:, :, None] * new_values[:, None, :]
    attended = (blended / totals[:, :, None]).astype(jnp.bfloat16).reshape(local_rows, 2, -1)
    side = owners[n]
    mine = lax.dynamic_index_in_dim(attended, side, axis=1, keepdims=False)
    other = lax.dynamic_index_in_dim(attended, 1 - side, axis=1, keepdims=False)
    other = swap_pair(other)
    first = jnp.where(side == 0, mine, other)
    second = jnp.where(side == 0, other, mine)
    swapped = jnp.concatenate([first, second], axis=0)

    depth = output_weight.shape[0] // 4
    out_weights = [load_rows(output_weight, 0, depth, [projected])]
    left = right = swapped
    near = [swapped]
    for step in range(1, n // 2):
        if step <= 3:
            out_weights.append(load_rows(output_weight, step * depth, depth, [left, right]))
        left, right = ring.step(left, right)
        near += [left, right]
    half = swapped.shape[1] // 2
    far = ring.step(left[:, :half], right[:, half:])
    keep, give = output_project(n, owners, near, far, out_weights)
    out = (keep + swap_pair(give)).astype(jnp.bfloat16)
    return out.reshape(-1, out.shape[-1])


def solution(mesh):
    return jax.shard_map(
        on_device,
        mesh=mesh,
        in_specs=(
            P(("groups", "gx"), "gy"),
            P("gy"),
            P("gx", "gy"),
            P("gx", "gy"),
            P("gy", "gx"),
            P(("groups", "gx", "gy"), None, None),
            P(("groups", "gx", "gy"), None, None),
            P(("groups", "gx", "gy")),
        ),
        out_specs=P(("groups", "gy"), "gx"),
        check_vma=False,
    )
```

time: 160 us -> 129 us (0.81)
  local copies, waits for them, and re-layouts: 1.16 us -> 48.5 us
  blocking collectives: 38.5 us -> 0 us
  waiting for transfers between devices: 63.4 us -> 24.9 us
  matrix products: 33 us -> 4.83 us
  starting transfers between devices: 3.6 us -> 27.4 us
  Pallas kernels: 0 us -> 19.6 us
  between operations: 13.6 us -> 0.37 us
  other arithmetic: 6.07 us -> 2.91 us
    unnamed x10 -> x35, local copies, waits for them, and re-layouts: 0.02 us -> 48 us
    all_gather x1 -> x0, waiting for transfers between devices: 43.8 us -> none  [on_device(): shard_rows = lax.all_gather(normed, 'gx', axis=0, tiled=True)]
    all_gather x1 -> x0, blocking collectives: 32.2 us -> none  [on_device(): lax.all_gather(swapped, 'gx', axis=0, tiled=True)]
    dot_general x3 -> x0, matrix products: 28.2 us -> none  [the longest x1 13.8 us: on_device(): lax.dot_general(shard_rows, query_weight, contract, preferred_element_typ...]
    ppermute x0 -> x21, starting transfers between devices: none -> 22.9 us  [the longest x8 12.5 us: step(): lax.ppermute(right, 'gx', self.back)]
    pallas_call x0 -> x14, Pallas kernels: none -> 19.6 us  [the longest x1 9.29 us: project(): pl.pallas_call(lambda *refs: project_kernel(n, len(weights), *refs), out_...]
    ppermute x0 -> x21, waiting for transfers between devices: none -> 17.8 us  [the longest x8 13.6 us: step(): lax.ppermute(left, 'gx', self.onward)]
    reduce_scatter x1 -> x0, waiting for transfers between devices: 7.02 us -> none  [on_device(): lax.psum_scatter(partial_out, 'gy', scatter_dimension=0, tiled=True)]
  transfers between devices with their start and end apart: 3 -> 22, of which waited for: 3 -> 10; matrix products, arithmetic and copies ran while one was open for 0% -> 1% of each run, Pallas kernels for 0% -> 4%
where the time goes in v2:
time: 129 us; the launch traced here: 128 us
  local copies, waits for them, and re-layouts  48.5 us (38%)
  starting transfers between devices  27.4 us (21%)
  waiting for transfers between devices  24.9 us (19%)
  Pallas kernels  19.6 us (15%)
  matrix products  4.83 us (4%)
  other arithmetic  2.91 us (2%)
    unnamed x35, local copies, waits for them, and re-layouts  48 us
    ppermute x8, waiting for transfers between devices, step(): lax.ppermute(left, 'gx', self.onward)  13.6 us
    ppermute x8, starting transfers between devices, step(): lax.ppermute(right, 'gx', self.back)  12.5 us
    pallas_call x1, Pallas kernels, project(): pl.pallas_call(lambda *refs: project_kernel(n, len(weights), *refs), out_...  9.29 us
    all_to_all x1, waiting for transfers between devices, on_device(): lax.all_to_all(projected, 'gx', split_axis=0, concat_axis=0, tiled=True)  7.06 us
    pallas_call x1, Pallas kernels, output_project(): pl.pallas_call(lambda *refs: output_kernel(n, len(weights), *refs), out_s...  5.59 us
    ppermute x8, starting transfers between devices, step(): lax.ppermute(left, 'gx', self.onward)  5 us
    ppermute x1, starting transfers between devices, on_device(): far_sums = lax.ppermute(own_sums, 'gx', ring.across)  4.97 us
  transfers between devices with their start and end apart: 22, of which 10 were waited for; matrix products, arithmetic and copies ran while one was open for 1% of the time, Pallas kernels for 4%

profile of v2, /device:TPU:0, one launch (start us, length us, event | category | flops | bytes accessed | tf_op | source)
XLA Modules:
  0.0 128.5 jit_solution(8955503051993690200)
XLA Ops:
  0.0 3.0 %collective-permute-start = (bf16[8,9216]{1,0:T(8,128)(2,1)}, bf16[8,9216]{1,0:T(8,128)(2,1)S(1)}, u32[]{:S(2)}, u32[]{:S(2)}) collective-permute-start(bf16[8,9216]{1,0:T(8,128)(2,1)} %refs_4_.1), channel_id=1, source_target_pairs={{0,4},{4,8},{8,12},{12,14},{14,10},{10,6},{6,2},{2,0},{1,5},{5,9},... | collective-permute-start | bytes 442376 | tf_op jit(solution)/shard_map/ppermute | solution.py:67
  3.0 1.0 copy-done.10
  4.2 5.0 %collective-permute-start.6 = (f32[8,128]{1,0:T(8,128)S(1)}, f32[8,128]{1,0:T(8,128)S(1)}, u32[]{:S(2)}, u32[]{:S(2)}) collective-permute-start(f32[8,128]{1,0:T(8,128)S(1)} %row_sums.4), channel_id=1, source_target_pairs={{0,14},{4,10},{8,6},{12,2},{14,0},{10,4},{6,8},{2,12},{1,15},{5,11... | collective-permute-start | bytes 12296 | tf_op jit(solution)/shard_map/ppermute | solution.py:269
  9.1 2.0 %collective-permute-start.3 = (bf16[8,9216]{1,0:T(8,128)(2,1)S(1)}, bf16[8,9216]{1,0:T(8,128)(2,1)S(1)}, u32[]{:S(2)}, u32[]{:S(2)}) collective-permute-start(bf16[8,9216]{1,0:T(8,128)(2,1)S(1)} %collective-permute-done.1.refs_1_.refs_2_.refs_6_), channel_id=1, source_target_pairs={{0,2},{4,0},{8,4},{12,8},{14,12},{10,14},{6,10},{2,6},{1,3},{5,1},... | collective-permute-start | bytes 442376 | tf_op jit(solution)/shard_map/ppermute | solution.py:67
  11.2 0.7 compare_select_fusion.2
  12.0 2.3 %collective-permute-done.2.refs_0_.refs_1_.refs_7_ = bf16[8,9216]{1,0:T(8,128)(2,1)S(1)} collective-permute-done((bf16[8,9216]{1,0:T(8,128)(2,1)S(1)}, bf16[8,9216]{1,0:T(8,128)(2,1)S(1)}, u32[]{:S(2)}, u32[]{:S(2)}) %collective-permute-start.2) | collective-permute-done | bytes 147488 | tf_op jit(solution)/shard_map/ppermute | solution.py:67
  14.3 2.0 %collective-permute-start.5 = (bf16[8,9216]{1,0:T(8,128)(2,1)S(1)}, bf16[8,9216]{1,0:T(8,128)(2,1)S(1)}, u32[]{:S(2)}, u32[]{:S(2)}) collective-permute-start(bf16[8,9216]{1,0:T(8,128)(2,1)S(1)} %collective-permute-done.3.refs_1_.refs_2_.refs_8_), channel_id=1, source_target_pairs={{0,2},{4,0},{8,4},{12,8},{14,12},{10,14},{6,10},{2,6},{1,3},{5,1},... | collective-permute-start | bytes 442376 | tf_op jit(solution)/shard_map/ppermute | solution.py:67
  16.5 2.9 %collective-permute-done.4.refs_0_.refs_1_.refs_9_ = bf16[8,9216]{1,0:T(8,128)(2,1)S(1)} collective-permute-done((bf16[8,9216]{1,0:T(8,128)(2,1)S(1)}, bf16[8,9216]{1,0:T(8,128)(2,1)S(1)}, u32[]{:S(2)}, u32[]{:S(2)}) %collective-permute-start.4) | collective-permute-done | bytes 147488 | tf_op jit(solution)/shard_map/ppermute | solution.py:67
  19.8 1.3 %collective-permute-start.8 = (bf16[8,4608]{1,0:T(8,128)(2,1)S(1)}, bf16[8,4608]{1,0:T(8,128)(2,1)S(1)}, u32[]{:S(2)}, u32[]{:S(2)}) collective-permute-start(bf16[8,4608]{1,0:T(8,128)(2,1)S(1)} %slice.48), channel_id=1, source_target_pairs={{0,4},{4,8},{8,12},{12,14},{14,10},{10,6},{6,2},{2,0},{1,5},{5,9},... | collective-permute-start | bytes 221192 | tf_op jit(solution)/shard_map/ppermute | solution.py:67
  21.1 0.8 collective-permute-start.9
  21.9 9.1 %copy-done.1 = bf16[1536,9216]{1,0:T(8,128)(2,1)S(1)} copy-done((bf16[1536,9216]{1,0:T(8,128)(2,1)S(1)}, bf16[1536,9216]{1,0:T(8,128)(2,1)}, u32[]{:S(2)}) %copy-start.1) | copy-done | bytes 28311576
  31.0 0.6 load_rows.7.refs_13_
  31.7 9.1 %copy-done.2 = bf16[1536,9216]{1,0:T(8,128)(2,1)S(1)} copy-done((bf16[1536,9216]{1,0:T(8,128)(2,1)S(1)}, bf16[1536,9216]{1,0:T(8,128)(2,1)}, u32[]{:S(2)}) %copy-start.2) | copy-done | bytes 28311576
  40.8 0.6 load_rows.8.refs_14_
  41.4 3.6 %copy-done.3 = bf16[512,9216]{1,0:T(8,128)(2,1)} copy-done((bf16[512,9216]{1,0:T(8,128)(2,1)}, bf16[512,9216]{1,0:T(8,128)(2,1)S(1)}, u32[]{:S(2)}) %copy-start.3) | copy-done | bytes 9437208
  45.1 0.6 load_rows.9.refs_15_
  45.7 0.6 copy-done.9
  46.6 3.7 %copy-done.4 = bf16[512,9216]{1,0:T(8,128)(2,1)S(1)} copy-done((bf16[512,9216]{1,0:T(8,128)(2,1)S(1)}, bf16[512,9216]{1,0:T(8,128)(2,1)}, u32[]{:S(2)}) %copy-start.4) | copy-done | bytes 9437208
  50.3 9.3 %project.1 = (f32[8,4,1600]{2,1,0:T(4,128)S(1)}, f32[8,4,1600]{2,1,0:T(4,128)S(1)}) custom-call(s32[9]{0:T(128)S(1)} %pad_add_fusion.refs_0_, f32[64,128]{1,0:T(8,128)S(1)} %constant_dynamic-update-slice_fusion.refs_1_, f32[64,128]{1,0:T(8,128)S(1)} %collective-permute-done.7.refs_2_, f32[1,9216]{1,0:T(1,128)S(1)} %bitcast.20, ...), custom_call_target="tpu_custom_call" | custom-call | tf_op jit(solution)/shard_map/project/pallas_call | solution.py:181
  59.8 1.3 %collective-permute-done.10 = f32[8,4,1600]{2,1,0:T(4,128)S(1)} collective-permute-done((f32[8,4,1600]{2,1,0:T(4,128)S(1)}, f32[8,4,1600]{2,1,0:T(4,128)S(1)}, u32[]{:S(2)}, u32[]{:S(2)}) %collective-permute-start.10) | collective-permute-done | bytes 204832 | tf_op jit(solution)/shard_map/ppermute | solution.py:43
  61.1 0.7 add_convert_fusion.1.refs_1_
  61.8 4.5 %all-to-all-start = ((bf16[8,4,1600]{2,1,0:T(4,128)(2,1)}), bf16[8,4,1600]{2,1,0:T(4,128)(2,1)S(1)}, u32[]{:S(2)}, u32[]{:S(2)}) async-start(bf16[8,4,1600]{2,1,0:T(4,128)(2,1)} %add_convert_fusion.1.refs_1_), calls=%async_computation | async-start | bytes 212992 | tf_op jit(solution)/shard_map/all_to_all | solution.py:287
  66.4 7.1 %all-to-all-done = bf16[8,4,1600]{2,1,0:T(4,128)(2,1)S(1)} async-done(((bf16[8,4,1600]{2,1,0:T(4,128)(2,1)}), bf16[8,4,1600]{2,1,0:T(4,128)(2,1)S(1)}, u32[]{:S(2)}, u32[]{:S(2)}) %all-to-all-start) | async-done | bytes 102432 | tf_op jit(solution)/shard_map/all_to_all | solution.py:287
  74.0 3.8 %fusion.14 = (f32[4,48]{1,0:T(4,128)S(1)}, f32[4,48,2048]{2,1,0:T(8,128)S(1)}) fusion(bf16[4,2048,256]{2,1,0:T(8,128)(2,1)} %param.14, bf16[4,48,128]{2,1,0:T(8,128)(2,1)S(1)} %get-tuple-element.16, bf16[4,48,128]{2,1,0:T(8,128)(2,1)S(1)} %get-tuple-element.15, pred[4,2048]{1,0:T(4,128)(4,1)S(1)} %iota_compare_fusion), kind=kOutput, calls=%fused_computation.50 | convolution fusion | flops 202702656 | bytes 5874432 | tf_op jit(solution)/shard_map/rhd,rtd->rht/dot_general | solution.py:297
  77.9 0.4 fusion.1
  78.3 0.9 fusion.4
  79.5 1.2 collective-permute-done.11
  80.9 2.0 %collective-permute-start.13 = (bf16[8,6144]{1,0:T(8,128)(2,1)S(1)}, bf16[8,6144]{1,0:T(8,128)(2,1)S(1)}, u32[]{:S(2)}, u32[]{:S(2)}) collective-permute-start(bf16[8,6144]{1,0:T(8,128)(2,1)S(1)} %pad_maximum_fusion.1.refs_1_.refs_2_), channel_id=1, source_target_pairs={{0,2},{4,0},{8,4},{12,8},{14,12},{10,14},{6,10},{2,6},{1,3},{5,1},... | collective-permute-start | bytes 294920 | tf_op jit(solution)/shard_map/ppermute | solution.py:67
  83.0 2.8 %collective-permute-done.12.refs_1_.refs_2_ = bf16[8,6144]{1,0:T(8,128)(2,1)S(1)} collective-permute-done((bf16[8,6144]{1,0:T(8,128)(2,1)S(1)}, bf16[8,6144]{1,0:T(8,128)(2,1)S(1)}, u32[]{:S(2)}, u32[]{:S(2)}) %collective-permute-start.12) | collective-permute-done | bytes 98336 | tf_op jit(solution)/shard_map/ppermute | solution.py:67
  85.8 0.3 collective-permute-start.14
  86.1 1.7 %collective-permute-start.15 = (bf16[8,6144]{1,0:T(8,128)(2,1)S(1)}, bf16[8,6144]{1,0:T(8,128)(2,1)S(1)}, u32[]{:S(2)}, u32[]{:S(2)}) collective-permute-start(bf16[8,6144]{1,0:T(8,128)(2,1)S(1)} %collective-permute-done.13.refs_2_.refs_3_), channel_id=1, source_target_pairs={{0,2},{4,0},{8,4},{12,8},{14,12},{10,14},{6,10},{2,6},{1,3},{5,1},... | collective-permute-start | bytes 294920 | tf_op jit(solution)/shard_map/ppermute | solution.py:67
  87.8 2.6 %collective-permute-done.14.refs_1_.refs_4_ = bf16[8,6144]{1,0:T(8,128)(2,1)S(1)} collective-permute-done((bf16[8,6144]{1,0:T(8,128)(2,1)S(1)}, bf16[8,6144]{1,0:T(8,128)(2,1)S(1)}, u32[]{:S(2)}, u32[]{:S(2)}) %collective-permute-start.14) | collective-permute-done | bytes 98336 | tf_op jit(solution)/shard_map/ppermute | solution.py:67
  90.4 0.3 collective-permute-start.16
  90.7 1.7 %collective-permute-start.17 = (bf16[8,6144]{1,0:T(8,128)(2,1)S(1)}, bf16[8,6144]{1,0:T(8,128)(2,1)S(1)}, u32[]{:S(2)}, u32[]{:S(2)}) collective-permute-start(bf16[8,6144]{1,0:T(8,128)(2,1)S(1)} %collective-permute-done.15.refs_2_.refs_5_), channel_id=1, source_target_pairs={{0,2},{4,0},{8,4},{12,8},{14,12},{10,14},{6,10},{2,6},{1,3},{5,1},... | collective-permute-start | bytes 294920 | tf_op jit(solution)/shard_map/ppermute | solution.py:67
  92.4 3.0 %collective-permute-done.16.refs_6_ = bf16[8,6144]{1,0:T(8,128)(2,1)S(1)} collective-permute-done((bf16[8,6144]{1,0:T(8,128)(2,1)S(1)}, bf16[8,6144]{1,0:T(8,128)(2,1)S(1)}, u32[]{:S(2)}, u32[]{:S(2)}) %collective-permute-start.16) | collective-permute-done | bytes 98336 | tf_op jit(solution)/shard_map/ppermute | solution.py:67
  95.5 2.2 %collective-permute-start.19 = (bf16[8,3072]{1,0:T(8,128)(2,1)S(1)}, bf16[8,3072]{1,0:T(8,128)(2,1)S(1)}, u32[]{:S(2)}, u32[]{:S(2)}) collective-permute-start(bf16[8,3072]{1,0:T(8,128)(2,1)S(1)} %slice.59), channel_id=1, source_target_pairs={{0,2},{4,0},{8,4},{12,8},{14,12},{10,14},{6,10},{2,6},{1,3},{5,1},... | collective-permute-start | bytes 147464 | tf_op jit(solution)/shard_map/ppermute | solution.py:67
  97.7 9.1 %copy-done = bf16[6144,2304]{1,0:T(8,128)(2,1)S(1)} copy-done((bf16[6144,2304]{1,0:T(8,128)(2,1)S(1)}, bf16[6144,2304]{1,0:T(8,128)(2,1)}, u32[]{:S(2)}) %copy-start) | copy-done | bytes 28311576
  106.8 0.5 load_rows.10.refs_10_
  107.2 0.5 load_rows.11.refs_11_
  107.7 2.8 %copy-done.5 = bf16[1536,2304]{1,0:T(8,128)(2,1)} copy-done((bf16[1536,2304]{1,0:T(8,128)(2,1)}, bf16[1536,2304]{1,0:T(8,128)(2,1)S(1)}, u32[]{:S(2)}) %copy-start.5) | copy-done | bytes 7077912
  110.6 0.5 load_rows.12.refs_12_
  111.1 2.9 %copy-done.7 = bf16[1536,2304]{1,0:T(8,128)(2,1)} copy-done((bf16[1536,2304]{1,0:T(8,128)(2,1)}, bf16[1536,2304]{1,0:T(8,128)(2,1)S(1)}, u32[]{:S(2)}) %copy-start.7) | copy-done | bytes 7077912
  114.0 0.5 load_rows.13.refs_13_
  114.5 3.0 %copy-done.6 = bf16[1536,2304]{1,0:T(8,128)(2,1)S(1)} copy-done((bf16[1536,2304]{1,0:T(8,128)(2,1)S(1)}, bf16[1536,2304]{1,0:T(8,128)(2,1)}, u32[]{:S(2)}) %copy-start.6) | copy-done | bytes 7077912
  117.5 3.0 %copy-done.8 = bf16[1536,2304]{1,0:T(8,128)(2,1)S(1)} copy-done((bf16[1536,2304]{1,0:T(8,128)(2,1)S(1)}, bf16[1536,2304]{1,0:T(8,128)(2,1)}, u32[]{:S(2)}) %copy-start.8) | copy-done | bytes 7077912
  120.5 5.6 %output_project.1 = (f32[4,8,2304]{2,1,0:T(8,128)S(1)}, f32[4,8,2304]{2,1,0:T(8,128)S(1)}) custom-call(s32[9]{0:T(128)S(1)} %pad_add_fusion.refs_0_, bf16[8,6144]{1,0:T(8,128)(2,1)S(1)} %pad_maximum_fusion.1.refs_1_.refs_2_, bf16[8,6144]{1,0:T(8,128)(2,1)S(1)} %collective-permute-done.12.refs_1_.refs_2_, ...), custom_call_target="tpu_custom_call" | custom-call | tf_op jit(solution)/shard_map/output_project/pallas_call | solution.py:234
  126.2 1.6 %collective-permute-done.20 = f32[4,8,2304]{2,1,0:T(8,128)S(1)} collective-permute-done((f32[4,8,2304]{2,1,0:T(8,128)S(1)}, f32[4,8,2304]{2,1,0:T(8,128)S(1)}, u32[]{:S(2)}, u32[]{:S(2)}) %collective-permute-start.20) | collective-permute-done | bytes 294944 | tf_op jit(solution)/shard_map/ppermute | solution.py:43
  127.8 0.7 fusion.7
  (78 shorter events, 2.8 us)
Async XLA Ops:
  0.0 9.1 %collective-permute-start = (bf16[8,9216]{1,0:T(8,128)(2,1)}, bf16[8,9216]{1,0:T(8,128)(2,1)S(1)}, u32[]{:S(2)}, u32[]{:S(2)}) collective-permute-start(bf16[8,9216]{1,0:T(8,128)(2,1)} %refs_4_.1), channel_id=1, source_target_pairs={{0,4},{4,8},{8,12},{12,14},{14,10},{10,6},{6,2},{2,0},{1,5},{5,9},... | collective-permute-start | bytes 442376 | tf_op jit(solution)/shard_map/ppermute | solution.py:67
  3.0 6.1 %collective-permute-start.1 = (bf16[8,9216]{1,0:T(8,128)(2,1)}, bf16[8,9216]{1,0:T(8,128)(2,1)S(1)}, u32[]{:S(2)}, u32[]{:S(2)}) collective-permute-start(bf16[8,9216]{1,0:T(8,128)(2,1)} %refs_4_.1), channel_id=1, source_target_pairs={{0,2},{4,0},{8,4},{12,8},{14,12},{10,14},{6,10},{2,6},{1,3},{5,1},... | collective-permute-start | bytes 442376 | tf_op jit(solution)/shard_map/ppermute | solution.py:67
  3.0 1.0 copy-start.10
  4.2 15.5 %collective-permute-start.6 = (f32[8,128]{1,0:T(8,128)S(1)}, f32[8,128]{1,0:T(8,128)S(1)}, u32[]{:S(2)}, u32[]{:S(2)}) collective-permute-start(f32[8,128]{1,0:T(8,128)S(1)} %row_sums.4), channel_id=1, source_target_pairs={{0,14},{4,10},{8,6},{12,2},{14,0},{10,4},{6,8},{2,12},{1,15},{5,11... | collective-permute-start | bytes 12296 | tf_op jit(solution)/shard_map/ppermute | solution.py:269
  9.1 5.1 %collective-permute-start.2 = (bf16[8,9216]{1,0:T(8,128)(2,1)S(1)}, bf16[8,9216]{1,0:T(8,128)(2,1)S(1)}, u32[]{:S(2)}, u32[]{:S(2)}) collective-permute-start(bf16[8,9216]{1,0:T(8,128)(2,1)S(1)} %collective-permute-done.refs_0_.refs_1_.refs_5_), channel_id=1, source_target_pairs={{0,4},{4,8},{8,12},{12,14},{14,10},{10,6},{6,2},{2,0},{1,5},{5,9},... | collective-permute-start | bytes 442376 | tf_op jit(solution)/shard_map/ppermute | solution.py:67
  9.1 5.2 %collective-permute-start.3 = (bf16[8,9216]{1,0:T(8,128)(2,1)S(1)}, bf16[8,9216]{1,0:T(8,128)(2,1)S(1)}, u32[]{:S(2)}, u32[]{:S(2)}) collective-permute-start(bf16[8,9216]{1,0:T(8,128)(2,1)S(1)} %collective-permute-done.1.refs_1_.refs_2_.refs_6_), channel_id=1, source_target_pairs={{0,2},{4,0},{8,4},{12,8},{14,12},{10,14},{6,10},{2,6},{1,3},{5,1},... | collective-permute-start | bytes 442376 | tf_op jit(solution)/shard_map/ppermute | solution.py:67
  14.3 5.1 %collective-permute-start.4 = (bf16[8,9216]{1,0:T(8,128)(2,1)S(1)}, bf16[8,9216]{1,0:T(8,128)(2,1)S(1)}, u32[]{:S(2)}, u32[]{:S(2)}) collective-permute-start(bf16[8,9216]{1,0:T(8,128)(2,1)S(1)} %collective-permute-done.2.refs_0_.refs_1_.refs_7_), channel_id=1, source_target_pairs={{0,4},{4,8},{8,12},{12,14},{14,10},{10,6},{6,2},{2,0},{1,5},{5,9},... | collective-permute-start | bytes 442376 | tf_op jit(solution)/shard_map/ppermute | solution.py:67
  14.3 5.1 %collective-permute-start.5 = (bf16[8,9216]{1,0:T(8,128)(2,1)S(1)}, bf16[8,9216]{1,0:T(8,128)(2,1)S(1)}, u32[]{:S(2)}, u32[]{:S(2)}) collective-permute-start(bf16[8,9216]{1,0:T(8,128)(2,1)S(1)} %collective-permute-done.3.refs_1_.refs_2_.refs_8_), channel_id=1, source_target_pairs={{0,2},{4,0},{8,4},{12,8},{14,12},{10,14},{6,10},{2,6},{1,3},{5,1},... | collective-permute-start | bytes 442376 | tf_op jit(solution)/shard_map/ppermute | solution.py:67
  19.7 26.9 %collective-permute-start.7 = (f32[64,128]{1,0:T(8,128)S(1)}, f32[64,128]{1,0:T(8,128)S(1)}, u32[]{:S(2)}, u32[]{:S(2)}) collective-permute-start(f32[64,128]{1,0:T(8,128)S(1)} %constant_dynamic-update-slice_fusion.refs_1_), channel_id=1, source_target_pairs={{0,1},{1,0},{2,3},{3,2},{4,5},{5,4},{6,7},{7,6},{8,9},{9,8},{10,11... | collective-permute-start | bytes 98312 | tf_op jit(solution)/shard_map/ppermute | solution.py:43
  19.8 26.8 %collective-permute-start.8 = (bf16[8,4608]{1,0:T(8,128)(2,1)S(1)}, bf16[8,4608]{1,0:T(8,128)(2,1)S(1)}, u32[]{:S(2)}, u32[]{:S(2)}) collective-permute-start(bf16[8,4608]{1,0:T(8,128)(2,1)S(1)} %slice.48), channel_id=1, source_target_pairs={{0,4},{4,8},{8,12},{12,14},{14,10},{10,6},{6,2},{2,0},{1,5},{5,9},... | collective-permute-start | bytes 221192 | tf_op jit(solution)/shard_map/ppermute | solution.py:67
  21.1 25.5 %collective-permute-start.9 = (bf16[8,4608]{1,0:T(8,128)(2,1)S(1)}, bf16[8,4608]{1,0:T(8,128)(2,1)S(1)}, u32[]{:S(2)}, u32[]{:S(2)}) collective-permute-start(bf16[8,4608]{1,0:T(8,128)(2,1)S(1)} %slice.49), channel_id=1, source_target_pairs={{0,2},{4,0},{8,4},{12,8},{14,12},{10,14},{6,10},{2,6},{1,3},{5,1},... | collective-permute-start | bytes 221192 | tf_op jit(solution)/shard_map/ppermute | solution.py:67
  21.9 9.1 %copy-start.1 = (bf16[1536,9216]{1,0:T(8,128)(2,1)S(1)}, bf16[1536,9216]{1,0:T(8,128)(2,1)}, u32[]{:S(2)}) copy-start(bf16[1536,9216]{1,0:T(8,128)(2,1)} %refs_0_.12) | copy-start | bytes 84934656
  31.0 0.7 copy-start.13
  31.7 9.1 %copy-start.2 = (bf16[1536,9216]{1,0:T(8,128)(2,1)S(1)}, bf16[1536,9216]{1,0:T(8,128)(2,1)}, u32[]{:S(2)}) copy-start(bf16[1536,9216]{1,0:T(8,128)(2,1)} %refs_0_.12) | copy-start | bytes 84934656
  41.4 3.6 %copy-start.3 = (bf16[512,9216]{1,0:T(8,128)(2,1)}, bf16[512,9216]{1,0:T(8,128)(2,1)S(1)}, u32[]{:S(2)}) copy-start(bf16[512,9216]{1,0:T(8,128)(2,1)S(1)} %load_rows.8.refs_14_) | copy-start | bytes 28311556
  45.1 1.3 copy-start.9
  45.1 1.6 %copy-start.11 = (bf16[8,9216]{1,0:T(8,128)(2,1)S(1)}, bf16[8,9216]{1,0:T(8,128)(2,1)}, u32[]{:S(2)}) copy-start(bf16[8,9216]{1,0:T(8,128)(2,1)} %refs_4_.1) | copy-start | bytes 442372
  46.6 3.7 %copy-start.4 = (bf16[512,9216]{1,0:T(8,128)(2,1)S(1)}, bf16[512,9216]{1,0:T(8,128)(2,1)}, u32[]{:S(2)}) copy-start(bf16[512,9216]{1,0:T(8,128)(2,1)} %copy-done.3) | copy-start | bytes 28311556
  50.3 16.0 %copy-start.14 = (s32[4]{0:T(128)S(1)}, s32[4]{0:T(128)}, u32[]{:S(2)}) copy-start(s32[4]{0:T(128)} %param.16) | copy-start | bytes 52
  59.6 1.5 %collective-permute-start.10 = (f32[8,4,1600]{2,1,0:T(4,128)S(1)}, f32[8,4,1600]{2,1,0:T(4,128)S(1)}, u32[]{:S(2)}, u32[]{:S(2)}) collective-permute-start(f32[8,4,1600]{2,1,0:T(4,128)S(1)} %get-tuple-element.10), channel_id=1, source_target_pairs={{0,1},{1,0},{2,3},{3,2},{4,5},{5,4},{6,7},{7,6},{8,9},{9,8},{10,11... | collective-permute-start | bytes 614408 | tf_op jit(solution)/shard_map/ppermute | solution.py:43
  61.8 11.6 %all-to-all-start = ((bf16[8,4,1600]{2,1,0:T(4,128)(2,1)}), bf16[8,4,1600]{2,1,0:T(4,128)(2,1)S(1)}, u32[]{:S(2)}, u32[]{:S(2)}) async-start(bf16[8,4,1600]{2,1,0:T(4,128)(2,1)} %add_convert_fusion.1.refs_1_), calls=%async_computation | async-start | bytes 212992 | tf_op jit(solution)/shard_map/all_to_all | solution.py:287
  73.7 4.5 %copy-start.12 = (bf16[4,2048,256]{2,1,0:T(8,128)(2,1)S(1)}, bf16[4,2048,256]{2,1,0:T(8,128)(2,1)}, u32[]{:S(2)}) copy-start(bf16[4,2048,256]{2,1,0:T(8,128)(2,1)} %param.15) | copy-start | bytes 12582916
  79.5 1.3 %collective-permute-start.11 = (bf16[4,6144]{1,0:T(4,128)(2,1)S(1)}, bf16[4,6144]{1,0:T(4,128)(2,1)S(1)}, u32[]{:S(2)}, u32[]{:S(2)}) collective-permute-start(bf16[4,6144]{1,0:T(4,128)(2,1)S(1)} %bitcast.23), channel_id=1, source_target_pairs={{0,1},{1,0},{2,3},{3,2},{4,5},{5,4},{6,7},{7,6},{8,9},{9,8},{10,11... | collective-permute-start | bytes 147464 | tf_op jit(solution)/shard_map/ppermute | solution.py:43
  80.9 4.9 %collective-permute-start.12 = (bf16[8,6144]{1,0:T(8,128)(2,1)S(1)}, bf16[8,6144]{1,0:T(8,128)(2,1)S(1)}, u32[]{:S(2)}, u32[]{:S(2)}) collective-permute-start(bf16[8,6144]{1,0:T(8,128)(2,1)S(1)} %pad_maximum_fusion.1.refs_1_.refs_2_), channel_id=1, source_target_pairs={{0,4},{4,8},{8,12},{12,14},{14,10},{10,6},{6,2},{2,0},{1,5},{5,9},... | collective-permute-start | bytes 294920 | tf_op jit(solution)/shard_map/ppermute | solution.py:67
  80.9 5.1 %collective-permute-start.13 = (bf16[8,6144]{1,0:T(8,128)(2,1)S(1)}, bf16[8,6144]{1,0:T(8,128)(2,1)S(1)}, u32[]{:S(2)}, u32[]{:S(2)}) collective-permute-start(bf16[8,6144]{1,0:T(8,128)(2,1)S(1)} %pad_maximum_fusion.1.refs_1_.refs_2_), channel_id=1, source_target_pairs={{0,2},{4,0},{8,4},{12,8},{14,12},{10,14},{6,10},{2,6},{1,3},{5,1},... | collective-permute-start | bytes 294920 | tf_op jit(solution)/shard_map/ppermute | solution.py:67
  85.8 4.6 %collective-permute-start.14 = (bf16[8,6144]{1,0:T(8,128)(2,1)S(1)}, bf16[8,6144]{1,0:T(8,128)(2,1)S(1)}, u32[]{:S(2)}, u32[]{:S(2)}) collective-permute-start(bf16[8,6144]{1,0:T(8,128)(2,1)S(1)} %collective-permute-done.12.refs_1_.refs_2_), channel_id=1, source_target_pairs={{0,4},{4,8},{8,12},{12,14},{14,10},{10,6},{6,2},{2,0},{1,5},{5,9},... | collective-permute-start | bytes 294920 | tf_op jit(solution)/shard_map/ppermute | solution.py:67
  86.1 4.6 %collective-permute-start.15 = (bf16[8,6144]{1,0:T(8,128)(2,1)S(1)}, bf16[8,6144]{1,0:T(8,128)(2,1)S(1)}, u32[]{:S(2)}, u32[]{:S(2)}) collective-permute-start(bf16[8,6144]{1,0:T(8,128)(2,1)S(1)} %collective-permute-done.13.refs_2_.refs_3_), channel_id=1, source_target_pairs={{0,2},{4,0},{8,4},{12,8},{14,12},{10,14},{6,10},{2,6},{1,3},{5,1},... | collective-permute-start | bytes 294920 | tf_op jit(solution)/shard_map/ppermute | solution.py:67
  90.4 5.0 %collective-permute-start.16 = (bf16[8,6144]{1,0:T(8,128)(2,1)S(1)}, bf16[8,6144]{1,0:T(8,128)(2,1)S(1)}, u32[]{:S(2)}, u32[]{:S(2)}) collective-permute-start(bf16[8,6144]{1,0:T(8,128)(2,1)S(1)} %collective-permute-done.14.refs_1_.refs_4_), channel_id=1, source_target_pairs={{0,4},{4,8},{8,12},{12,14},{14,10},{10,6},{6,2},{2,0},{1,5},{5,9},... | collective-permute-start | bytes 294920 | tf_op jit(solution)/shard_map/ppermute | solution.py:67
  90.7 4.8 %collective-permute-start.17 = (bf16[8,6144]{1,0:T(8,128)(2,1)S(1)}, bf16[8,6144]{1,0:T(8,128)(2,1)S(1)}, u32[]{:S(2)}, u32[]{:S(2)}) collective-permute-start(bf16[8,6144]{1,0:T(8,128)(2,1)S(1)} %collective-permute-done.15.refs_2_.refs_5_), channel_id=1, source_target_pairs={{0,2},{4,0},{8,4},{12,8},{14,12},{10,14},{6,10},{2,6},{1,3},{5,1},... | collective-permute-start | bytes 294920 | tf_op jit(solution)/shard_map/ppermute | solution.py:67
  95.4 19.1 %collective-permute-start.18 = (bf16[8,3072]{1,0:T(8,128)(2,1)S(1)}, bf16[8,3072]{1,0:T(8,128)(2,1)S(1)}, u32[]{:S(2)}, u32[]{:S(2)}) collective-permute-start(bf16[8,3072]{1,0:T(8,128)(2,1)S(1)} %slice.58), channel_id=1, source_target_pairs={{0,4},{4,8},{8,12},{12,14},{14,10},{10,6},{6,2},{2,0},{1,5},{5,9},... | collective-permute-start | bytes 147464 | tf_op jit(solution)/shard_map/ppermute | solution.py:67
  95.5 19.0 %collective-permute-start.19 = (bf16[8,3072]{1,0:T(8,128)(2,1)S(1)}, bf16[8,3072]{1,0:T(8,128)(2,1)S(1)}, u32[]{:S(2)}, u32[]{:S(2)}) collective-permute-start(bf16[8,3072]{1,0:T(8,128)(2,1)S(1)} %slice.59), channel_id=1, source_target_pairs={{0,2},{4,0},{8,4},{12,8},{14,12},{10,14},{6,10},{2,6},{1,3},{5,1},... | collective-permute-start | bytes 147464 | tf_op jit(solution)/shard_map/ppermute | solution.py:67
  97.7 9.1 %copy-start = (bf16[6144,2304]{1,0:T(8,128)(2,1)S(1)}, bf16[6144,2304]{1,0:T(8,128)(2,1)}, u32[]{:S(2)}) copy-start(bf16[6144,2304]{1,0:T(8,128)(2,1)} %refs_0_.17) | copy-start | bytes 84934656
  107.7 2.9 %copy-start.5 = (bf16[1536,2304]{1,0:T(8,128)(2,1)}, bf16[1536,2304]{1,0:T(8,128)(2,1)S(1)}, u32[]{:S(2)}) copy-start(bf16[1536,2304]{1,0:T(8,128)(2,1)S(1)} %load_rows.11.refs_11_) | copy-start | bytes 21233668
  111.1 2.9 %copy-start.7 = (bf16[1536,2304]{1,0:T(8,128)(2,1)}, bf16[1536,2304]{1,0:T(8,128)(2,1)S(1)}, u32[]{:S(2)}) copy-start(bf16[1536,2304]{1,0:T(8,128)(2,1)S(1)} %load_rows.12.refs_12_) | copy-start | bytes 21233668
  114.5 3.0 %copy-start.6 = (bf16[1536,2304]{1,0:T(8,128)(2,1)S(1)}, bf16[1536,2304]{1,0:T(8,128)(2,1)}, u32[]{:S(2)}) copy-start(bf16[1536,2304]{1,0:T(8,128)(2,1)} %copy-done.5) | copy-start | bytes 21233668
  117.5 3.0 %copy-start.8 = (bf16[1536,2304]{1,0:T(8,128)(2,1)S(1)}, bf16[1536,2304]{1,0:T(8,128)(2,1)}, u32[]{:S(2)}) copy-start(bf16[1536,2304]{1,0:T(8,128)(2,1)} %copy-done.7) | copy-start | bytes 21233668
  126.1 1.6 %collective-permute-start.20 = (f32[4,8,2304]{2,1,0:T(8,128)S(1)}, f32[4,8,2304]{2,1,0:T(8,128)S(1)}, u32[]{:S(2)}, u32[]{:S(2)}) collective-permute-start(f32[4,8,2304]{2,1,0:T(8,128)S(1)} %get-tuple-element.12), channel_id=1, source_target_pairs={{0,1},{1,0},{2,3},{3,2},{4,5},{5,4},{6,7},{7,6},{8,9},{9,8},{10,11... | collective-permute-start | bytes 884744 | tf_op jit(solution)/shard_map/ppermute | solution.py:43

commit v3 on v2

--- a/solution.py
+++ b/solution.py
@@ -16,6 +16,7 @@
 contract = (((1,), (1,)), ((), ()))
 MIB = 1 << 20
 ANY = pl.BlockSpec(memory_space=pl.ANY)
+IN_HBM = pl.BlockSpec(memory_space=pltpu.HBM)
 IN_VMEM = pl.BlockSpec(memory_space=pltpu.VMEM)
 IN_SMEM = pl.BlockSpec(memory_space=pltpu.SMEM)
 
@@ -67,47 +68,32 @@
         return lax.ppermute(left, "gx", self.onward), lax.ppermute(right, "gx", self.back)
 
 
-def load_kernel(count, *refs):
-    sources, targets, sems = refs[:count], refs[-count - 1 : -1], refs[-1]
-    copies = [
-        pltpu.make_async_copy(source, target, sems.at[i])
-        for i, (source, target) in enumerate(zip(sources, targets))
-    ]
-    for copy in copies:
-        copy.start()
-    for copy in copies:
-        copy.wait()
-
-
-def load(arrays, after=()):
-    return pl.pallas_call(
-        lambda *refs: load_kernel(len(arrays), *refs),
-        out_shape=[pltpu.VMEM(a.shape, a.dtype) for a in arrays],
-        in_specs=[ANY] * (len(arrays) + len(after)),
-        out_specs=[IN_VMEM] * len(arrays),
-        scratch_shapes=[pltpu.SemaphoreType.DMA((len(arrays),))],
-        compiler_params=pltpu.CompilerParams(vmem_limit_bytes=4 * MIB),
-        name="load",
-    )(*arrays, *after)
-
-
-def load_rows_kernel(start, size, *refs):
+def load_kernel(start, *refs):
     source, target, sem = refs[0], refs[-2], refs[-1]
-    copy = pltpu.make_async_copy(source.at[pl.ds(start, size)], target, sem)
+    copy = pltpu.make_async_copy(source.at[pl.ds(start, target.shape[0])], target, sem)
     copy.start()
     copy.wait()
 
 
-def load_rows(array, start, size, after=()):
+def load(array, start, size, after=()):
     return pl.pallas_call(
-        lambda *refs: load_rows_kernel(start, size, *refs),
+        lambda *refs: load_kernel(start, *refs),
         out_shape=pltpu.VMEM((size,) + array.shape[1:], array.dtype),
-        in_specs=[ANY] * (1 + len(after)),
+        in_specs=[IN_HBM] + [ANY] * len(after),
         out_specs=IN_VMEM,
         scratch_shapes=[pltpu.SemaphoreType.DMA],
-        compiler_params=pltpu.CompilerParams(vmem_limit_bytes=4 * MIB),
-        name="load_rows",
-    )(array, *after)
+        compiler_params=pltpu.CompilerParams(vmem_limit_bytes=MIB),
+        name="load",
+    )(pltpu.with_memory_space_constraint(array, pltpu.HBM), *after)
+
+
+def in_vmem(array):
+    return pltpu.with_memory_space_constraint(array, pltpu.VMEM)
+
+
+def before(done, *rest):
+    held = lax.optimization_barrier((done,) + rest)
+    return held[0], held[1:]
 
 
 def sums_kernel(*refs):
@@ -187,9 +173,9 @@
             pltpu.VMEM((n * rows, width), jnp.float32),
             pltpu.VMEM((n * rows, stripe), jnp.float32),
         ],
-        compiler_params=pltpu.CompilerParams(vmem_limit_bytes=(24 if n <= 8 else 48) * MIB),
+        compiler_params=pltpu.CompilerParams(vmem_limit_bytes=(10 if n <= 8 else 48) * MIB),
         name="project",
-    )(owners, *sums, gain, *near, *far, *weights)
+    )(owners, *sums, gain, *near, *far, *[in_vmem(w) for w in weights])
 
 
 def output_kernel(n, parts, *refs):
@@ -240,9 +226,9 @@
             pltpu.VMEM((n * rows, cols), jnp.float32),
             pltpu.VMEM((n, rows, cols), jnp.float32),
         ],
-        compiler_params=pltpu.CompilerParams(vmem_limit_bytes=(24 if n <= 8 else 48) * MIB),
+        compiler_params=pltpu.CompilerParams(vmem_limit_bytes=(10 if n <= 8 else 48) * MIB),
         name="output_project",
-    )(owners, *near, *far, *weights)
+    )(owners, *near, *far, *[in_vmem(w) for w in weights])
 
 
 def on_device(
@@ -269,13 +255,15 @@
     far_sums = lax.ppermute(own_sums, "gx", ring.across)
     sums = [own_sums]
     for step in range(1, n // 2):
-        if step <= pieces:
-            after = [] if step == 1 else [left, right]
-            weights.append(load_rows(query_weight, (step - 1) * piece, piece, after))
+        after = [] if step == 1 else [left, right]
         left, right = ring.step(left, right)
         near += [left, right]
+        if step <= pieces:
+            loaded = load(query_weight, (step - 1) * piece, piece, after)
+            loaded, (left, right) = before(loaded, left, right)
+            weights.append(loaded)
         sums.append(row_sums([left, right]))
-    weights += load([keyval_weight], [left, right])
+    weights.append(load(keyval_weight, 0, keyval_weight.shape[0], [left, right]))
     half = activations.shape[1] // 2
     far = ring.step(left[:, :half], right[:, half:])
     sums = jnp.concatenate(sums + [far_sums], axis=0)
@@ -284,7 +272,10 @@
     keep, give = project(n, owners, sums, gain, near, far, weights)
     projected = (keep + swap_pair(give)).astype(jnp.bfloat16)
     local_rows = cache_lengths.shape[0]
+    depth = output_weight.shape[0] // 4
+    out_weights = [load(output_weight, 0, depth, [projected])]
     gathered = lax.all_to_all(projected, "gx", split_axis=0, concat_axis=0, tiled=True)
+    out_weights[0], (gathered,) = before(out_weights[0], gathered)
     gathered = jnp.swapaxes(gathered, 0, 1)
     queries = gathered[:, :, :query_cols].reshape(local_rows, HEADS, DH)
     keyvals = gathered[:, :, query_cols:].reshape(local_rows, 2 * DH)
@@ -323,15 +314,16 @@
     second = jnp.where(side == 0, other, mine)
     swapped = jnp.concatenate([first, second], axis=0)
 
-    depth = output_weight.shape[0] // 4
-    out_weights = [load_rows(output_weight, 0, depth, [projected])]
     left = right = swapped
     near = [swapped]
     for step in range(1, n // 2):
-        if step <= 3:
-            out_weights.append(load_rows(output_weight, step * depth, depth, [left, right]))
+        after = [left, right]
         left, right = ring.step(left, right)
         near += [left, right]
+        if step <= 3:
+            loaded = load(output_weight, step * depth, depth, after)
+            loaded, (left, right) = before(loaded, left, right)
+            out_weights.append(loaded)
     half = swapped.shape[1] // 2
     far = ring.step(left[:, :half], right[:, half:])
     keep, give = output_project(n, owners, near, far, out_weights)

time: 129 us -> 95.5 us (0.74)
  local copies, waits for them, and re-layouts: 48.5 us -> 8.04 us
  Pallas kernels: 19.6 us -> 40.3 us
  waiting for transfers between devices: 24.9 us -> 12.5 us
    unnamed x35 -> x31, local copies, waits for them, and re-layouts: 48 us -> 7.56 us
    pallas_call x8, Pallas kernels: 4.08 us -> 24.7 us  [load(): pl.pallas_call(lambda *refs: load_kernel(start, *refs), out_shape=pltpu.V...]
    ppermute x8, waiting for transfers between devices: 13.6 us -> 3.28 us  [step(): lax.ppermute(left, 'gx', self.onward)]
    all_to_all x1, waiting for transfers between devices: 7.06 us -> 1.18 us  [on_device(): lax.all_to_all(projected, 'gx', split_axis=0, concat_axis=0, tiled=True)]
    ppermute x8, starting transfers between devices: 12.5 us -> 8.81 us  [step(): lax.ppermute(right, 'gx', self.back)]
    ppermute x8, waiting for transfers between devices: 0.1 us -> 3.76 us  [step(): lax.ppermute(right, 'gx', self.back)]
    ppermute x8, starting transfers between devices: 5 us -> 8.54 us  [step(): lax.ppermute(left, 'gx', self.onward)]
  transfers between devices with their start and end apart: 22 -> 22, of which waited for: 10 -> 10; matrix products, arithmetic and copies ran while one was open for 1% -> 0% of each run, Pallas kernels for 4% -> 27%
where the time goes in v3:
time: 95.5 us; the launch traced here: 95.1 us
  Pallas kernels  40.3 us (42%)
  starting transfers between devices  26.8 us (28%)
  waiting for transfers between devices  12.5 us (13%)
  local copies, waits for them, and re-layouts  8.04 us (8%)
  matrix products  4.85 us (5%)
  other arithmetic  2.26 us (2%)
    pallas_call x8, Pallas kernels, load(): pl.pallas_call(lambda *refs: load_kernel(start, *refs), out_shape=pltpu.V...  24.7 us
    pallas_call x1, Pallas kernels, project(): pl.pallas_call(lambda *refs: project_kernel(n, len(weights), *refs), out_...  9.31 us
    ppermute x8, starting transfers between devices, step(): lax.ppermute(right, 'gx', self.back)  8.81 us
    ppermute x8, starting transfers between devices, step(): lax.ppermute(left, 'gx', self.onward)  8.54 us
    unnamed x31, local copies, waits for them, and re-layouts  7.56 us
    pallas_call x1, Pallas kernels, output_project(): pl.pallas_call(lambda *refs: output_kernel(n, len(weights), *refs), out_s...  5.6 us
    ppermute x1, starting transfers between devices, on_device(): far_sums = lax.ppermute(own_sums, 'gx', ring.across)  4.97 us
    ppermute x4, waiting for transfers between devices, swap_pair(): return lax.ppermute(x, 'gy', [(0, 1), (1, 0)])  4.24 us
  transfers between devices with their start and end apart: 22, of which 10 were waited for; matrix products, arithmetic and copies ran while one was open for 0% of the time, Pallas kernels for 27%

profile of v3, /device:TPU:0, one launch (start us, length us, event | category | flops | bytes accessed | tf_op | source)
XLA Modules:
  0.0 95.1 jit_solution(7659765116732862376)
XLA Ops:
  0.0 3.0 %collective-permute-start = (bf16[8,9216]{1,0:T(8,128)(2,1)}, bf16[8,9216]{1,0:T(8,128)(2,1)S(1)}, u32[]{:S(2)}, u32[]{:S(2)}) collective-permute-start(bf16[8,9216]{1,0:T(8,128)(2,1)} %refs_4_.1), channel_id=1, source_target_pairs={{0,4},{4,8},{8,12},{12,14},{14,10},{10,6},{6,2},{2,0},{1,5},{5,9},... | collective-permute-start | bytes 442376 | tf_op jit(solution)/shard_map/ppermute | solution.py:68
  3.0 1.0 %copy-done.2 = bf16[8,9216]{1,0:T(8,128)(2,1)S(1)} copy-done((bf16[8,9216]{1,0:T(8,128)(2,1)S(1)}, bf16[8,9216]{1,0:T(8,128)(2,1)}, u32[]{:S(2)}) %copy-start.2) | copy-done | bytes 147480
  4.0 0.2 row_sums.4
  4.2 5.0 %collective-permute-start.6 = (f32[8,128]{1,0:T(8,128)S(1)}, f32[8,128]{1,0:T(8,128)S(1)}, u32[]{:S(2)}, u32[]{:S(2)}) collective-permute-start(f32[8,128]{1,0:T(8,128)S(1)} %row_sums.4), channel_id=1, source_target_pairs={{0,14},{4,10},{8,6},{12,2},{14,0},{10,4},{6,8},{2,12},{1,15},{5,11... | collective-permute-start | bytes 12296 | tf_op jit(solution)/shard_map/ppermute | solution.py:255
  9.1 3.7 %load.8.refs_13_ = bf16[512,9216]{1,0:T(8,128)(2,1)S(1)} custom-call(bf16[1536,9216]{1,0:T(8,128)(2,1)} %refs_0_.12), custom_call_target="tpu_custom_call" | custom-call | tf_op jit(solution)/shard_map/load/pallas_call | solution.py:79
  12.9 3.6 %copy-done = bf16[512,9216]{1,0:T(8,128)(2,1)} copy-done((bf16[512,9216]{1,0:T(8,128)(2,1)}, bf16[512,9216]{1,0:T(8,128)(2,1)S(1)}, u32[]{:S(2)}) %copy-start) | copy-done | bytes 9437208
  16.5 2.0 %collective-permute-start.3 = (bf16[8,9216]{1,0:T(8,128)(2,1)S(1)}, bf16[8,9216]{1,0:T(8,128)(2,1)S(1)}, u32[]{:S(2)}, u32[]{:S(2)}) collective-permute-start(bf16[8,9216]{1,0:T(8,128)(2,1)S(1)} %collective-permute-done.1.refs_1_.refs_2_.refs_6_), channel_id=1, source_target_pairs={{0,2},{4,0},{8,4},{12,8},{14,12},{10,14},{6,10},{2,6},{1,3},{5,1},... | collective-permute-start | bytes 442376 | tf_op jit(solution)/shard_map/ppermute | solution.py:68
  18.6 3.7 %load.9.refs_14_ = bf16[512,9216]{1,0:T(8,128)(2,1)S(1)} custom-call(bf16[1536,9216]{1,0:T(8,128)(2,1)} %refs_0_.12, bf16[8,9216]{1,0:T(8,128)(2,1)S(1)} %collective-permute-done.refs_0_.refs_1_.refs_5_, bf16[8,9216]{1,0:T(8,128)(2,1)S(1)} %collective-permute-done.1.refs_1_.refs_2_.refs_6_), custom_call_target="tpu_custom_call" | custom-call | tf_op jit(solution)/shard_map/load/pallas_call | solution.py:79
  22.3 0.2 row_sums.5
  22.5 2.0 %collective-permute-start.5 = (bf16[8,9216]{1,0:T(8,128)(2,1)S(1)}, bf16[8,9216]{1,0:T(8,128)(2,1)S(1)}, u32[]{:S(2)}, u32[]{:S(2)}) collective-permute-start(bf16[8,9216]{1,0:T(8,128)(2,1)S(1)} %collective-permute-done.3.refs_1_.refs_2_.refs_8_), channel_id=1, source_target_pairs={{0,2},{4,0},{8,4},{12,8},{14,12},{10,14},{6,10},{2,6},{1,3},{5,1},... | collective-permute-start | bytes 442376 | tf_op jit(solution)/shard_map/ppermute | solution.py:68
  24.5 3.8 %load.10.refs_15_ = bf16[512,9216]{1,0:T(8,128)(2,1)S(1)} custom-call(bf16[1536,9216]{1,0:T(8,128)(2,1)} %refs_0_.12, bf16[8,9216]{1,0:T(8,128)(2,1)S(1)} %collective-permute-done.2.refs_0_.refs_1_.refs_7_, bf16[8,9216]{1,0:T(8,128)(2,1)S(1)} %collective-permute-done.3.refs_1_.refs_2_.refs_8_), custom_call_target="tpu_custom_call" | custom-call | tf_op jit(solution)/shard_map/load/pallas_call | solution.py:79
  28.4 0.2 row_sums.6
  28.6 0.2 row_sums.7
  29.0 2.0 %collective-permute-start.9 = (bf16[8,4608]{1,0:T(8,128)(2,1)S(1)}, bf16[8,4608]{1,0:T(8,128)(2,1)S(1)}, u32[]{:S(2)}, u32[]{:S(2)}) collective-permute-start(bf16[8,4608]{1,0:T(8,128)(2,1)S(1)} %slice.37), channel_id=1, source_target_pairs={{0,2},{4,0},{8,4},{12,8},{14,12},{10,14},{6,10},{2,6},{1,3},{5,1},... | collective-permute-start | bytes 221192 | tf_op jit(solution)/shard_map/ppermute | solution.py:68
  31.0 1.3 %load.11.refs_16_ = bf16[64,9216]{1,0:T(8,128)(2,1)S(1)} custom-call(bf16[64,9216]{1,0:T(8,128)(2,1)} %refs_0_.13, bf16[8,9216]{1,0:T(8,128)(2,1)S(1)} %collective-permute-done.4.refs_0_.refs_1_.refs_9_, bf16[8,9216]{1,0:T(8,128)(2,1)S(1)} %collective-permute-done.5.refs_1_.refs_2_.refs_10_), custom_call_target="tpu_custom_call" | custom-call | tf_op jit(solution)/shard_map/load/pallas_call | solution.py:79
  32.3 1.2 %collective-permute-done.8.refs_11_ = bf16[8,4608]{1,0:T(8,128)(2,1)S(1)} collective-permute-done((bf16[8,4608]{1,0:T(8,128)(2,1)S(1)}, bf16[8,4608]{1,0:T(8,128)(2,1)S(1)}, u32[]{:S(2)}, u32[]{:S(2)}) %collective-permute-start.8) | collective-permute-done | bytes 73760 | tf_op jit(solution)/shard_map/ppermute | solution.py:68
  33.6 9.3 %project.1 = (f32[8,4,1600]{2,1,0:T(4,128)S(1)}, f32[8,4,1600]{2,1,0:T(4,128)S(1)}) custom-call(s32[9]{0:T(128)S(1)} %pad_add_fusion.refs_0_, f32[64,128]{1,0:T(8,128)S(1)} %constant_dynamic-update-slice_fusion.refs_1_, f32[64,128]{1,0:T(8,128)S(1)} %collective-permute-done.7.refs_2_, f32[1,9216]{1,0:T(1,128)S(1)} %bitcast.24, ...), custom_call_target="tpu_custom_call" | custom-call | tf_op jit(solution)/shard_map/project/pallas_call | solution.py:167
  43.0 1.5 %collective-permute-done.10 = f32[8,4,1600]{2,1,0:T(4,128)S(1)} collective-permute-done((f32[8,4,1600]{2,1,0:T(4,128)S(1)}, f32[8,4,1600]{2,1,0:T(4,128)S(1)}, u32[]{:S(2)}, u32[]{:S(2)}) %collective-permute-start.10) | collective-permute-done | bytes 204832 | tf_op jit(solution)/shard_map/ppermute | solution.py:44
  44.5 0.7 add_convert_fusion.1.refs_1_
  45.2 4.2 %all-to-all-start = ((bf16[8,4,1600]{2,1,0:T(4,128)(2,1)}), bf16[8,4,1600]{2,1,0:T(4,128)(2,1)S(1)}, u32[]{:S(2)}, u32[]{:S(2)}) async-start(bf16[8,4,1600]{2,1,0:T(4,128)(2,1)} %add_convert_fusion.1.refs_1_), calls=%async_computation | async-start | bytes 212992 | tf_op jit(solution)/shard_map/all_to_all | solution.py:277
  49.4 3.0 %load.12.refs_10_ = bf16[1536,2304]{1,0:T(8,128)(2,1)S(1)} custom-call(bf16[6144,2304]{1,0:T(8,128)(2,1)} %refs_0_.17, bf16[8,4,1600]{2,1,0:T(4,128)(2,1)} %add_convert_fusion.1.refs_1_), custom_call_target="tpu_custom_call" | custom-call | tf_op jit(solution)/shard_map/load/pallas_call | solution.py:79
  52.5 2.8 %copy-done.1 = bf16[1536,2304]{1,0:T(8,128)(2,1)} copy-done((bf16[1536,2304]{1,0:T(8,128)(2,1)}, bf16[1536,2304]{1,0:T(8,128)(2,1)S(1)}, u32[]{:S(2)}) %copy-start.1) | copy-done | bytes 7077912
  55.3 1.2 %all-to-all-done = bf16[8,4,1600]{2,1,0:T(4,128)(2,1)S(1)} async-done(((bf16[8,4,1600]{2,1,0:T(4,128)(2,1)}), bf16[8,4,1600]{2,1,0:T(4,128)(2,1)S(1)}, u32[]{:S(2)}, u32[]{:S(2)}) %all-to-all-start) | async-done | bytes 102432 | tf_op jit(solution)/shard_map/all_to_all | solution.py:277
  56.9 0.1 fusion.8
  57.0 3.8 %fusion.14 = (f32[4,48]{1,0:T(4,128)S(1)}, f32[4,48,2048]{2,1,0:T(8,128)S(1)}) fusion(bf16[4,2048,256]{2,1,0:T(8,128)(2,1)} %param.14, bf16[4,48,128]{2,1,0:T(8,128)(2,1)S(1)} %get-tuple-element.56, bf16[4,48,128]{2,1,0:T(8,128)(2,1)S(1)} %get-tuple-element.55, pred[4,2048]{1,0:T(4,128)(4,1)S(1)} %iota_compare_fusion), kind=kOutput, calls=%fused_computation.50 | convolution fusion | flops 202702656 | bytes 5874432 | tf_op jit(solution)/shard_map/rhd,rtd->rht/dot_general | solution.py:288
  60.9 0.4 fusion.1
  61.3 0.9 fusion.4
  62.2 0.2 constant_dynamic-slice_fusion.1
  62.6 1.2 %collective-permute-done.11 = bf16[4,6144]{1,0:T(4,128)(2,1)S(1)} collective-permute-done((bf16[4,6144]{1,0:T(4,128)(2,1)S(1)}, bf16[4,6144]{1,0:T(4,128)(2,1)S(1)}, u32[]{:S(2)}, u32[]{:S(2)}) %collective-permute-start.11) | collective-permute-done | bytes 49184 | tf_op jit(solution)/shard_map/ppermute | solution.py:44
  63.9 0.9 collective-permute-start.12
  64.8 1.2 %collective-permute-start.13 = (bf16[8,6144]{1,0:T(8,128)(2,1)S(1)}, bf16[8,6144]{1,0:T(8,128)(2,1)S(1)}, u32[]{:S(2)}, u32[]{:S(2)}) collective-permute-start(bf16[8,6144]{1,0:T(8,128)(2,1)S(1)} %pad_maximum_fusion.1.refs_1_.refs_2_), channel_id=1, source_target_pairs={{0,2},{4,0},{8,4},{12,8},{14,12},{10,14},{6,10},{2,6},{1,3},{5,1},... | collective-permute-start | bytes 294920 | tf_op jit(solution)/shard_map/ppermute | solution.py:68
  66.0 3.0 %load.13.refs_11_ = bf16[1536,2304]{1,0:T(8,128)(2,1)S(1)} custom-call(bf16[6144,2304]{1,0:T(8,128)(2,1)} %refs_0_.17, bf16[8,6144]{1,0:T(8,128)(2,1)S(1)} %pad_maximum_fusion.1.refs_1_.refs_2_, bf16[8,6144]{1,0:T(8,128)(2,1)S(1)} %pad_maximum_fusion.1.refs_1_.refs_2_), custom_call_target="tpu_custom_call" | custom-call | tf_op jit(solution)/shard_map/load/pallas_call | solution.py:79
  69.0 0.4 collective-permute-done.13.refs_2_.refs_3_
  69.4 1.5 %collective-permute-start.14 = (bf16[8,6144]{1,0:T(8,128)(2,1)S(1)}, bf16[8,6144]{1,0:T(8,128)(2,1)S(1)}, u32[]{:S(2)}, u32[]{:S(2)}) collective-permute-start(bf16[8,6144]{1,0:T(8,128)(2,1)S(1)} %collective-permute-done.12.refs_1_.refs_2_), channel_id=1, source_target_pairs={{0,4},{4,8},{8,12},{12,14},{14,10},{10,6},{6,2},{2,0},{1,5},{5,9},... | collective-permute-start | bytes 294920 | tf_op jit(solution)/shard_map/ppermute | solution.py:68
  70.9 0.6 collective-permute-start.15
  71.5 3.2 %load.14.refs_12_ = bf16[1536,2304]{1,0:T(8,128)(2,1)S(1)} custom-call(bf16[6144,2304]{1,0:T(8,128)(2,1)} %refs_0_.17, bf16[8,6144]{1,0:T(8,128)(2,1)S(1)} %collective-permute-done.12.refs_1_.refs_2_, bf16[8,6144]{1,0:T(8,128)(2,1)S(1)} %collective-permute-done.13.refs_2_.refs_3_), custom_call_target="tpu_custom_call" | custom-call | tf_op jit(solution)/shard_map/load/pallas_call | solution.py:79
  74.6 0.9 collective-permute-done.15.refs_2_.refs_5_
  75.5 1.5 %collective-permute-start.16 = (bf16[8,6144]{1,0:T(8,128)(2,1)S(1)}, bf16[8,6144]{1,0:T(8,128)(2,1)S(1)}, u32[]{:S(2)}, u32[]{:S(2)}) collective-permute-start(bf16[8,6144]{1,0:T(8,128)(2,1)S(1)} %collective-permute-done.14.refs_1_.refs_4_), channel_id=1, source_target_pairs={{0,4},{4,8},{8,12},{12,14},{14,10},{10,6},{6,2},{2,0},{1,5},{5,9},... | collective-permute-start | bytes 294920 | tf_op jit(solution)/shard_map/ppermute | solution.py:68
  77.0 0.6 collective-permute-start.17
  77.5 3.0 %load.15.refs_13_ = bf16[1536,2304]{1,0:T(8,128)(2,1)S(1)} custom-call(bf16[6144,2304]{1,0:T(8,128)(2,1)} %refs_0_.17, bf16[8,6144]{1,0:T(8,128)(2,1)S(1)} %collective-permute-done.14.refs_1_.refs_4_, bf16[8,6144]{1,0:T(8,128)(2,1)S(1)} %collective-permute-done.15.refs_2_.refs_5_), custom_call_target="tpu_custom_call" | custom-call | tf_op jit(solution)/shard_map/load/pallas_call | solution.py:79
  80.6 1.0 %collective-permute-done.17.refs_7_ = bf16[8,6144]{1,0:T(8,128)(2,1)S(1)} collective-permute-done((bf16[8,6144]{1,0:T(8,128)(2,1)S(1)}, bf16[8,6144]{1,0:T(8,128)(2,1)S(1)}, u32[]{:S(2)}, u32[]{:S(2)}) %collective-permute-start.17) | collective-permute-done | bytes 98336 | tf_op jit(solution)/shard_map/ppermute | solution.py:68
  81.6 1.5 %collective-permute-start.18 = (bf16[8,3072]{1,0:T(8,128)(2,1)S(1)}, bf16[8,3072]{1,0:T(8,128)(2,1)S(1)}, u32[]{:S(2)}, u32[]{:S(2)}) collective-permute-start(bf16[8,3072]{1,0:T(8,128)(2,1)S(1)} %slice.46), channel_id=1, source_target_pairs={{0,4},{4,8},{8,12},{12,14},{14,10},{10,6},{6,2},{2,0},{1,5},{5,9},... | collective-permute-start | bytes 147464 | tf_op jit(solution)/shard_map/ppermute | solution.py:68
  83.1 0.6 collective-permute-start.19
  83.6 2.1 %collective-permute-done.18.refs_8_ = bf16[8,3072]{1,0:T(8,128)(2,1)S(1)} collective-permute-done((bf16[8,3072]{1,0:T(8,128)(2,1)S(1)}, bf16[8,3072]{1,0:T(8,128)(2,1)S(1)}, u32[]{:S(2)}, u32[]{:S(2)}) %collective-permute-start.18) | collective-permute-done | bytes 49184 | tf_op jit(solution)/shard_map/ppermute | solution.py:68
  85.7 1.5 %collective-permute-done.19.refs_9_ = bf16[8,3072]{1,0:T(8,128)(2,1)S(1)} collective-permute-done((bf16[8,3072]{1,0:T(8,128)(2,1)S(1)}, bf16[8,3072]{1,0:T(8,128)(2,1)S(1)}, u32[]{:S(2)}, u32[]{:S(2)}) %collective-permute-start.19) | collective-permute-done | bytes 49184 | tf_op jit(solution)/shard_map/ppermute | solution.py:68
  87.2 5.6 %output_project.1 = (f32[4,8,2304]{2,1,0:T(8,128)S(1)}, f32[4,8,2304]{2,1,0:T(8,128)S(1)}) custom-call(s32[9]{0:T(128)S(1)} %pad_add_fusion.refs_0_, bf16[8,6144]{1,0:T(8,128)(2,1)S(1)} %pad_maximum_fusion.1.refs_1_.refs_2_, bf16[8,6144]{1,0:T(8,128)(2,1)S(1)} %collective-permute-done.12.refs_1_.refs_2_, ...), custom_call_target="tpu_custom_call" | custom-call | tf_op jit(solution)/shard_map/output_project/pallas_call | solution.py:220
  92.8 1.6 %collective-permute-done.20 = f32[4,8,2304]{2,1,0:T(8,128)S(1)} collective-permute-done((f32[4,8,2304]{2,1,0:T(8,128)S(1)}, f32[4,8,2304]{2,1,0:T(8,128)S(1)}, u32[]{:S(2)}, u32[]{:S(2)}) %collective-permute-start.20) | collective-permute-done | bytes 294944 | tf_op jit(solution)/shard_map/ppermute | solution.py:44
  94.4 0.7 fusion.7
  (76 shorter events, 1.4 us)
Async XLA Ops:
  0.0 16.5 %collective-permute-start = (bf16[8,9216]{1,0:T(8,128)(2,1)}, bf16[8,9216]{1,0:T(8,128)(2,1)S(1)}, u32[]{:S(2)}, u32[]{:S(2)}) collective-permute-start(bf16[8,9216]{1,0:T(8,128)(2,1)} %refs_4_.1), channel_id=1, source_target_pairs={{0,4},{4,8},{8,12},{12,14},{14,10},{10,6},{6,2},{2,0},{1,5},{5,9},... | collective-permute-start | bytes 442376 | tf_op jit(solution)/shard_map/ppermute | solution.py:68
  3.0 13.5 %collective-permute-start.1 = (bf16[8,9216]{1,0:T(8,128)(2,1)}, bf16[8,9216]{1,0:T(8,128)(2,1)S(1)}, u32[]{:S(2)}, u32[]{:S(2)}) collective-permute-start(bf16[8,9216]{1,0:T(8,128)(2,1)} %refs_4_.1), channel_id=1, source_target_pairs={{0,2},{4,0},{8,4},{12,8},{14,12},{10,14},{6,10},{2,6},{1,3},{5,1},... | collective-permute-start | bytes 442376 | tf_op jit(solution)/shard_map/ppermute | solution.py:68
  3.0 1.0 %copy-start.2 = (bf16[8,9216]{1,0:T(8,128)(2,1)S(1)}, bf16[8,9216]{1,0:T(8,128)(2,1)}, u32[]{:S(2)}) copy-start(bf16[8,9216]{1,0:T(8,128)(2,1)} %refs_4_.1) | copy-start | bytes 442372
  4.2 24.6 %collective-permute-start.6 = (f32[8,128]{1,0:T(8,128)S(1)}, f32[8,128]{1,0:T(8,128)S(1)}, u32[]{:S(2)}, u32[]{:S(2)}) collective-permute-start(f32[8,128]{1,0:T(8,128)S(1)} %row_sums.4), channel_id=1, source_target_pairs={{0,14},{4,10},{8,6},{12,2},{14,0},{10,4},{6,8},{2,12},{1,15},{5,11... | collective-permute-start | bytes 12296 | tf_op jit(solution)/shard_map/ppermute | solution.py:255
  9.1 9.4 %copy-start.7 = (s32[8]{0:T(128)S(1)}, s32[8]{0:T(128)}, u32[]{:S(2)}) copy-start(s32[8]{0:T(128)} %constant.82.clone) | copy-start | bytes 100
  12.8 3.6 %copy-start = (bf16[512,9216]{1,0:T(8,128)(2,1)}, bf16[512,9216]{1,0:T(8,128)(2,1)S(1)}, u32[]{:S(2)}) copy-start(bf16[512,9216]{1,0:T(8,128)(2,1)S(1)} %load.8.refs_13_) | copy-start | bytes 28311556
  16.5 5.9 %collective-permute-start.2 = (bf16[8,9216]{1,0:T(8,128)(2,1)S(1)}, bf16[8,9216]{1,0:T(8,128)(2,1)S(1)}, u32[]{:S(2)}, u32[]{:S(2)}) collective-permute-start(bf16[8,9216]{1,0:T(8,128)(2,1)S(1)} %collective-permute-done.refs_0_.refs_1_.refs_5_), channel_id=1, source_target_pairs={{0,4},{4,8},{8,12},{12,14},{14,10},{10,6},{6,2},{2,0},{1,5},{5,9},... | collective-permute-start | bytes 442376 | tf_op jit(solution)/shard_map/ppermute | solution.py:68
  16.5 5.9 %collective-permute-start.3 = (bf16[8,9216]{1,0:T(8,128)(2,1)S(1)}, bf16[8,9216]{1,0:T(8,128)(2,1)S(1)}, u32[]{:S(2)}, u32[]{:S(2)}) collective-permute-start(bf16[8,9216]{1,0:T(8,128)(2,1)S(1)} %collective-permute-done.1.refs_1_.refs_2_.refs_6_), channel_id=1, source_target_pairs={{0,2},{4,0},{8,4},{12,8},{14,12},{10,14},{6,10},{2,6},{1,3},{5,1},... | collective-permute-start | bytes 442376 | tf_op jit(solution)/shard_map/ppermute | solution.py:68
  22.4 6.1 %collective-permute-start.4 = (bf16[8,9216]{1,0:T(8,128)(2,1)S(1)}, bf16[8,9216]{1,0:T(8,128)(2,1)S(1)}, u32[]{:S(2)}, u32[]{:S(2)}) collective-permute-start(bf16[8,9216]{1,0:T(8,128)(2,1)S(1)} %collective-permute-done.2.refs_0_.refs_1_.refs_7_), channel_id=1, source_target_pairs={{0,4},{4,8},{8,12},{12,14},{14,10},{10,6},{6,2},{2,0},{1,5},{5,9},... | collective-permute-start | bytes 442376 | tf_op jit(solution)/shard_map/ppermute | solution.py:68
  22.5 6.0 %collective-permute-start.5 = (bf16[8,9216]{1,0:T(8,128)(2,1)S(1)}, bf16[8,9216]{1,0:T(8,128)(2,1)S(1)}, u32[]{:S(2)}, u32[]{:S(2)}) collective-permute-start(bf16[8,9216]{1,0:T(8,128)(2,1)S(1)} %collective-permute-done.3.refs_1_.refs_2_.refs_8_), channel_id=1, source_target_pairs={{0,2},{4,0},{8,4},{12,8},{14,12},{10,14},{6,10},{2,6},{1,3},{5,1},... | collective-permute-start | bytes 442376 | tf_op jit(solution)/shard_map/ppermute | solution.py:68
  24.5 9.1 %slice-start = ((s8[9437184]{0:T(1024)(128)(4,1)}), s8[4194304]{0:T(1024)(128)(4,1)S(1)}, s32[]{:S(2)}) async-start(s8[9437184]{0:T(1024)(128)(4,1)} %bitcast.20), calls=%async_computation.1 | async-start | bytes 8388608
  24.5 6.5 %copy-start.5 = (bf16[9216]{0:T(1024)(128)(2,1)S(1)}, bf16[9216]{0:T(1024)(128)(2,1)}, u32[]{:S(2)}) copy-start(bf16[9216]{0:T(1024)(128)(2,1)} %param.10) | copy-start | bytes 55300
  24.5 9.1 %slice-start.1 = ((s8[9437184]{0:T(1024)(128)(4,1)}), s8[4194304]{0:T(1024)(128)(4,1)S(1)}, s32[]{:S(2)}) async-start(s8[9437184]{0:T(1024)(128)(4,1)} %bitcast.20), calls=%async_computation.2 | async-start | bytes 8388608
  24.5 9.1 %slice-start.2 = ((s8[9437184]{0:T(1024)(128)(4,1)}), s8[1048576]{0:T(1024)(128)(4,1)S(1)}, s32[]{:S(2)}) async-start(s8[9437184]{0:T(1024)(128)(4,1)} %bitcast.20), calls=%async_computation.3 | async-start | bytes 2097152
  24.5 9.1 %copy-start.3 = (bf16[8,9216]{1,0:T(8,128)(2,1)S(1)}, bf16[8,9216]{1,0:T(8,128)(2,1)}, u32[]{:S(2)}) copy-start(bf16[8,9216]{1,0:T(8,128)(2,1)} %refs_4_.1) | copy-start | bytes 442372
  28.8 3.5 %collective-permute-start.7 = (f32[64,128]{1,0:T(8,128)S(1)}, f32[64,128]{1,0:T(8,128)S(1)}, u32[]{:S(2)}, u32[]{:S(2)}) collective-permute-start(f32[64,128]{1,0:T(8,128)S(1)} %constant_dynamic-update-slice_fusion.refs_1_), channel_id=1, source_target_pairs={{0,1},{1,0},{2,3},{3,2},{4,5},{5,4},{6,7},{7,6},{8,9},{9,8},{10,11... | collective-permute-start | bytes 98312 | tf_op jit(solution)/shard_map/ppermute | solution.py:44
  28.9 4.7 %collective-permute-start.8 = (bf16[8,4608]{1,0:T(8,128)(2,1)S(1)}, bf16[8,4608]{1,0:T(8,128)(2,1)S(1)}, u32[]{:S(2)}, u32[]{:S(2)}) collective-permute-start(bf16[8,4608]{1,0:T(8,128)(2,1)S(1)} %slice.36), channel_id=1, source_target_pairs={{0,4},{4,8},{8,12},{12,14},{14,10},{10,6},{6,2},{2,0},{1,5},{5,9},... | collective-permute-start | bytes 221192 | tf_op jit(solution)/shard_map/ppermute | solution.py:68
  29.0 4.6 %collective-permute-start.9 = (bf16[8,4608]{1,0:T(8,128)(2,1)S(1)}, bf16[8,4608]{1,0:T(8,128)(2,1)S(1)}, u32[]{:S(2)}, u32[]{:S(2)}) collective-permute-start(bf16[8,4608]{1,0:T(8,128)(2,1)S(1)} %slice.37), channel_id=1, source_target_pairs={{0,2},{4,0},{8,4},{12,8},{14,12},{10,14},{6,10},{2,6},{1,3},{5,1},... | collective-permute-start | bytes 221192 | tf_op jit(solution)/shard_map/ppermute | solution.py:68
  33.6 15.7 %copy-start.6 = (s32[4]{0:T(128)S(1)}, s32[4]{0:T(128)}, u32[]{:S(2)}) copy-start(s32[4]{0:T(128)} %param.16) | copy-start | bytes 52
  42.9 1.5 %collective-permute-start.10 = (f32[8,4,1600]{2,1,0:T(4,128)S(1)}, f32[8,4,1600]{2,1,0:T(4,128)S(1)}, u32[]{:S(2)}, u32[]{:S(2)}) collective-permute-start(f32[8,4,1600]{2,1,0:T(4,128)S(1)} %get-tuple-element.39), channel_id=1, source_target_pairs={{0,1},{1,0},{2,3},{3,2},{4,5},{5,4},{6,7},{7,6},{8,9},{9,8},{10,11... | collective-permute-start | bytes 614408 | tf_op jit(solution)/shard_map/ppermute | solution.py:44
  45.2 11.3 %all-to-all-start = ((bf16[8,4,1600]{2,1,0:T(4,128)(2,1)}), bf16[8,4,1600]{2,1,0:T(4,128)(2,1)S(1)}, u32[]{:S(2)}, u32[]{:S(2)}) async-start(bf16[8,4,1600]{2,1,0:T(4,128)(2,1)} %add_convert_fusion.1.refs_1_), calls=%async_computation | async-start | bytes 212992 | tf_op jit(solution)/shard_map/all_to_all | solution.py:277
  52.5 2.9 %copy-start.1 = (bf16[1536,2304]{1,0:T(8,128)(2,1)}, bf16[1536,2304]{1,0:T(8,128)(2,1)S(1)}, u32[]{:S(2)}) copy-start(bf16[1536,2304]{1,0:T(8,128)(2,1)S(1)} %load.12.refs_10_) | copy-start | bytes 21233668
  56.7 4.5 %copy-start.4 = (bf16[4,2048,256]{2,1,0:T(8,128)(2,1)S(1)}, bf16[4,2048,256]{2,1,0:T(8,128)(2,1)}, u32[]{:S(2)}) copy-start(bf16[4,2048,256]{2,1,0:T(8,128)(2,1)} %param.15) | copy-start | bytes 12582916
  62.5 1.3 %collective-permute-start.11 = (bf16[4,6144]{1,0:T(4,128)(2,1)S(1)}, bf16[4,6144]{1,0:T(4,128)(2,1)S(1)}, u32[]{:S(2)}, u32[]{:S(2)}) collective-permute-start(bf16[4,6144]{1,0:T(4,128)(2,1)S(1)} %bitcast.27), channel_id=1, source_target_pairs={{0,1},{1,0},{2,3},{3,2},{4,5},{5,4},{6,7},{7,6},{8,9},{9,8},{10,11... | collective-permute-start | bytes 147464 | tf_op jit(solution)/shard_map/ppermute | solution.py:44
  63.9 5.1 %collective-permute-start.12 = (bf16[8,6144]{1,0:T(8,128)(2,1)S(1)}, bf16[8,6144]{1,0:T(8,128)(2,1)S(1)}, u32[]{:S(2)}, u32[]{:S(2)}) collective-permute-start(bf16[8,6144]{1,0:T(8,128)(2,1)S(1)} %pad_maximum_fusion.1.refs_1_.refs_2_), channel_id=1, source_target_pairs={{0,4},{4,8},{8,12},{12,14},{14,10},{10,6},{6,2},{2,0},{1,5},{5,9},... | collective-permute-start | bytes 294920 | tf_op jit(solution)/shard_map/ppermute | solution.py:68
  64.8 4.6 %collective-permute-start.13 = (bf16[8,6144]{1,0:T(8,128)(2,1)S(1)}, bf16[8,6144]{1,0:T(8,128)(2,1)S(1)}, u32[]{:S(2)}, u32[]{:S(2)}) collective-permute-start(bf16[8,6144]{1,0:T(8,128)(2,1)S(1)} %pad_maximum_fusion.1.refs_1_.refs_2_), channel_id=1, source_target_pairs={{0,2},{4,0},{8,4},{12,8},{14,12},{10,14},{6,10},{2,6},{1,3},{5,1},... | collective-permute-start | bytes 294920 | tf_op jit(solution)/shard_map/ppermute | solution.py:68
  69.4 5.2 %collective-permute-start.14 = (bf16[8,6144]{1,0:T(8,128)(2,1)S(1)}, bf16[8,6144]{1,0:T(8,128)(2,1)S(1)}, u32[]{:S(2)}, u32[]{:S(2)}) collective-permute-start(bf16[8,6144]{1,0:T(8,128)(2,1)S(1)} %collective-permute-done.12.refs_1_.refs_2_), channel_id=1, source_target_pairs={{0,4},{4,8},{8,12},{12,14},{14,10},{10,6},{6,2},{2,0},{1,5},{5,9},... | collective-permute-start | bytes 294920 | tf_op jit(solution)/shard_map/ppermute | solution.py:68
  70.9 4.6 %collective-permute-start.15 = (bf16[8,6144]{1,0:T(8,128)(2,1)S(1)}, bf16[8,6144]{1,0:T(8,128)(2,1)S(1)}, u32[]{:S(2)}, u32[]{:S(2)}) collective-permute-start(bf16[8,6144]{1,0:T(8,128)(2,1)S(1)} %collective-permute-done.13.refs_2_.refs_3_), channel_id=1, source_target_pairs={{0,2},{4,0},{8,4},{12,8},{14,12},{10,14},{6,10},{2,6},{1,3},{5,1},... | collective-permute-start | bytes 294920 | tf_op jit(solution)/shard_map/ppermute | solution.py:68
  71.4 15.7 %slice-start.3 = ((s8[7077888]{0:T(1024)(128)(4,1)}), s8[4194304]{0:T(1024)(128)(4,1)S(1)}, s32[]{:S(2)}) async-start(s8[7077888]{0:T(1024)(128)(4,1)} %bitcast.22), calls=%async_computation.4 | async-start | bytes 8388608
  74.6 12.5 %slice-start.4 = ((s8[7077888]{0:T(1024)(128)(4,1)}), s8[2883584]{0:T(1024)(128)(4,1)S(1)}, s32[]{:S(2)}) async-start(s8[7077888]{0:T(1024)(128)(4,1)} %bitcast.22), calls=%async_computation.5 | async-start | bytes 5767168
  75.5 5.1 %collective-permute-start.16 = (bf16[8,6144]{1,0:T(8,128)(2,1)S(1)}, bf16[8,6144]{1,0:T(8,128)(2,1)S(1)}, u32[]{:S(2)}, u32[]{:S(2)}) collective-permute-start(bf16[8,6144]{1,0:T(8,128)(2,1)S(1)} %collective-permute-done.14.refs_1_.refs_4_), channel_id=1, source_target_pairs={{0,4},{4,8},{8,12},{12,14},{14,10},{10,6},{6,2},{2,0},{1,5},{5,9},... | collective-permute-start | bytes 294920 | tf_op jit(solution)/shard_map/ppermute | solution.py:68
  77.0 4.6 %collective-permute-start.17 = (bf16[8,6144]{1,0:T(8,128)(2,1)S(1)}, bf16[8,6144]{1,0:T(8,128)(2,1)S(1)}, u32[]{:S(2)}, u32[]{:S(2)}) collective-permute-start(bf16[8,6144]{1,0:T(8,128)(2,1)S(1)} %collective-permute-done.15.refs_2_.refs_5_), channel_id=1, source_target_pairs={{0,2},{4,0},{8,4},{12,8},{14,12},{10,14},{6,10},{2,6},{1,3},{5,1},... | collective-permute-start | bytes 294920 | tf_op jit(solution)/shard_map/ppermute | solution.py:68
  81.6 4.1 %collective-permute-start.18 = (bf16[8,3072]{1,0:T(8,128)(2,1)S(1)}, bf16[8,3072]{1,0:T(8,128)(2,1)S(1)}, u32[]{:S(2)}, u32[]{:S(2)}) collective-permute-start(bf16[8,3072]{1,0:T(8,128)(2,1)S(1)} %slice.46), channel_id=1, source_target_pairs={{0,4},{4,8},{8,12},{12,14},{14,10},{10,6},{6,2},{2,0},{1,5},{5,9},... | collective-permute-start | bytes 147464 | tf_op jit(solution)/shard_map/ppermute | solution.py:68
  83.1 4.1 %collective-permute-start.19 = (bf16[8,3072]{1,0:T(8,128)(2,1)S(1)}, bf16[8,3072]{1,0:T(8,128)(2,1)S(1)}, u32[]{:S(2)}, u32[]{:S(2)}) collective-permute-start(bf16[8,3072]{1,0:T(8,128)(2,1)S(1)} %slice.47), channel_id=1, source_target_pairs={{0,2},{4,0},{8,4},{12,8},{14,12},{10,14},{6,10},{2,6},{1,3},{5,1},... | collective-permute-start | bytes 147464 | tf_op jit(solution)/shard_map/ppermute | solution.py:68
  92.8 1.6 %collective-permute-start.20 = (f32[4,8,2304]{2,1,0:T(8,128)S(1)}, f32[4,8,2304]{2,1,0:T(8,128)S(1)}, u32[]{:S(2)}, u32[]{:S(2)}) collective-permute-start(f32[4,8,2304]{2,1,0:T(8,128)S(1)} %get-tuple-element.52), channel_id=1, source_target_pairs={{0,1},{1,0},{2,3},{3,2},{4,5},{5,4},{6,7},{7,6},{8,9},{9,8},{10,11... | collective-permute-start | bytes 884744 | tf_op jit(solution)/shard_map/ppermute | solution.py:44

commit v4 on v3

v4 whole, which is shorter than its diff:
```python
import math

import jax
import jax.numpy as jnp
from jax import lax
from jax.experimental import pallas as pl
from jax.experimental.pallas import tpu as pltpu
from jax.sharding import PartitionSpec as P

D = 18432
HEADS = 48
DH = 256


epsilon = 1e-06
contract = (((1,), (1,)), ((), ()))
MIB = 1 << 20
ANY = pl.BlockSpec(memory_space=pl.ANY)
IN_HBM = pl.BlockSpec(memory_space=pltpu.HBM)
IN_VMEM = pl.BlockSpec(memory_space=pltpu.VMEM)
IN_SMEM = pl.BlockSpec(memory_space=pltpu.SMEM)


def rotate(vectors, places):
    half_width = vectors.shape[-1] // 2
    indices = jnp.arange(half_width, dtype=jnp.float32)
    frequency = jnp.exp(-math.log(10000.0) * indices / half_width)
    angles = places * frequency
    cosine = jnp.cos(angles)
    sine = jnp.sin(angles)
    first_half = vectors[..., :half_width]
    second_half = vectors[..., half_width:]
    return jnp.concatenate(
        [first_half * cosine - second_half * sine, second_half * cosine + first_half * sine],
        axis=-1,
    )


def ring_order(n):
    return list(range(0, n, 2)) + list(range(n - 1, 0, -2))


def swap_pair(x):
    return lax.ppermute(x, "gy", [(0, 1), (1, 0)])


class Ring:
    def __init__(self, n):
        self.n = n
        order = ring_order(n)
        self.onward = [(order[p], order[(p + 1) % n]) for p in range(n)]
        self.back = [(order[p], order[(p - 1) % n]) for p in range(n)]
        self.across = [(order[p], order[(p + n // 2) % n]) for p in range(n)]
        self.offsets = [0]
        for step in range(1, n // 2):
            self.offsets += [-step, step]
        self.offsets.append(n // 2)

    def owners(self):
        n = self.n
        me = lax.axis_index("gx")
        place = jnp.where(me % 2 == 0, me // 2, n - 1 - me // 2)
        at = (place + jnp.array(self.offsets, jnp.int32) + n) % n
        owner = jnp.where(at < n // 2, 2 * at, 2 * (n - 1 - at) + 1)
        return jnp.concatenate([owner, lax.axis_index("gy")[None]]).astype(jnp.int32)

    def step(self, left, right):
        return lax.ppermute(left, "gx", self.onward), lax.ppermute(right, "gx", self.back)


def start_copies(source, target, sems, count):
    rows = source.shape[0]
    size = -(-rows // (16 * count)) * 16
    copies = []
    for i, first in enumerate(range(0, rows, size)):
        at = pl.ds(first, min(size, rows - first))
        copy = pltpu.make_async_copy(source.at[at], target.at[at], sems.at[i])
        copy.start()
        copies.append(copy)
    return copies


def load_kernel(jobs, *refs):
    sources, buffer, sems = refs[: len(jobs)], refs[-2], refs[-1]
    copies = []
    for i, (source, (first, size, at)) in enumerate(zip(sources, jobs)):
        part = source.at[pl.ds(first, size)]
        copies += start_copies(part, buffer.at[pl.ds(at, size)], sems.at[i], 4)
    for copy in copies:
        copy.wait()


def load(buffer, jobs, after=()):
    new = isinstance(buffer, tuple)
    shape = buffer if new else buffer.shape
    arrays = [in_hbm(job[0]) for job in jobs]
    held = [] if new else [in_vmem(buffer)]
    return pl.pallas_call(
        lambda *refs: load_kernel([job[1:] for job in jobs], *refs),
        out_shape=pltpu.VMEM(shape, jnp.bfloat16),
        in_specs=[IN_HBM] * len(jobs) + [IN_VMEM] * len(held) + [ANY] * len(after),
        out_specs=IN_VMEM,
        input_output_aliases={} if new else {len(jobs): 0},
        scratch_shapes=[pltpu.SemaphoreType.DMA((len(jobs), 4))],
        compiler_params=pltpu.CompilerParams(vmem_limit_bytes=MIB),
        name="load",
    )(*arrays, *held, *after)


def in_hbm(array):
    return pltpu.with_memory_space_constraint(array, pltpu.HBM)


def in_vmem(array):
    return pltpu.with_memory_space_constraint(array, pltpu.VMEM)


def before(done, *rest):
    held = lax.optimization_barrier((done,) + rest)
    return held[0], held[1:]


def sums_kernel(*refs):
    out = refs[-1]
    rows = refs[0].shape[0]
    lane = lax.broadcasted_iota(jnp.int32, (rows, 128), 1)
    for i, ref in enumerate(refs[:-1]):
        x = ref[...].astype(jnp.float32)
        total = jnp.sum(x, axis=1, keepdims=True)
        square = jnp.sum(x * x, axis=1, keepdims=True)
        both = jnp.where(lane == 0, total, jnp.where(lane == 1, square, 0.0))
        out[i * rows : (i + 1) * rows, :] = both


def row_sums(shards):
    rows = shards[0].shape[0]
    return pl.pallas_call(
        sums_kernel,
        out_shape=jax.ShapeDtypeStruct((len(shards) * rows, 128), jnp.float32),
        in_specs=[IN_VMEM] * len(shards),
        out_specs=IN_VMEM,
        compiler_params=pltpu.CompilerParams(vmem_limit_bytes=16 * MIB),
        name="row_sums",
    )(*shards)


def project_kernel(n, turned, *refs):
    owners, sums_a, sums_b, gain = refs[:4]
    near = refs[4 : 4 + n - 1]
    far = refs[4 + n - 1 : 4 + n + 1]
    early, query_weight, keyval_weight, keep, give = refs[4 + n + 1 : 4 + n + 6]
    normed, late, keyval, total, sems = refs[4 + n + 6 :]
    at = pl.ds(early.shape[0], late.shape[0])
    copies = start_copies(query_weight.at[at], late, sems.at[0], 4)
    copies += start_copies(keyval_weight, keyval, sems.at[1], 1)
    rows = near[0].shape[0]
    half = far[0].shape[1]
    sums = sums_a[...] + sums_b[...]
    row_mean = sums[:, :1] / D
    row_square = sums[:, 1:2] / D
    scale = lax.rsqrt(row_square - row_mean * row_mean + epsilon)
    blocks = []

    def multiply(weight, part, start):
        cols = slice(part * half, (part + 1) * half)
        pair = (weight[:, cols], blocks[part])
        pair = pair if turned else pair[::-1]
        term = lax.dot_general(*pair, contract, preferred_element_type=jnp.float32)
        stripe = slice(start, start + weight.shape[0])
        where = (stripe, slice(None)) if turned else (slice(None), stripe)
        if part == 0:
            total[where] = term
        else:
            total[where] += term

    for part in range(2):
        cols = slice(part * half, (part + 1) * half)
        for i in range(n):
            at = slice(i * rows, (i + 1) * rows)
            x = near[i][:, cols] if i < n - 1 else far[part][...]
            x = (x.astype(jnp.float32) - row_mean[at]) * scale[at] * gain[:, cols]
            normed[at, cols] = x
        blocks.append(normed[:, cols].astype(jnp.bfloat16))
        multiply(early, part, 0)
    for copy in copies:
        copy.wait()
    for part in range(2):
        multiply(late, part, early.shape[0])
        multiply(keyval, part, early.shape[0] + late.shape[0])
    side = owners[n]
    local = rows // 2
    width = 128 if turned else total.shape[1]
    height = total.shape[0] if turned else total.shape[1]
    for start in range(0, height, width):
        size = min(width, height - start)
        cols = slice(start, start + size)
        stripe = total[cols, :].T if turned else total[...]
        for i in range(n):
            block = stripe[i * rows : (i + 1) * rows]
            low, high = block[:local], block[local:]
            keep[owners[i], :, cols] = jnp.where(side == 0, low, high)
            give[owners[i], :, cols] = jnp.where(side == 0, high, low)


def project(n, owners, sums, gain, near, far, early, query_weight, keyval_weight):
    rows, width = near[0].shape
    late = (query_weight.shape[0] - early.shape[0], width)
    stripe = query_weight.shape[0] + keyval_weight.shape[0]
    shape = jax.ShapeDtypeStruct((n, rows // 2, stripe), jnp.float32)
    turned = n <= 8
    sums_shape = (stripe, n * rows) if turned else (n * rows, stripe)
    return pl.pallas_call(
        lambda *refs: project_kernel(n, turned, *refs),
        out_shape=[shape, shape],
        in_specs=[IN_SMEM] + [IN_VMEM] * (3 + n + 2) + [IN_HBM] * 2,
        out_specs=[IN_VMEM] * 2,
        scratch_shapes=[
            pltpu.VMEM((n * rows, width), jnp.float32),
            pltpu.VMEM(late, jnp.bfloat16),
            pltpu.VMEM(keyval_weight.shape, jnp.bfloat16),
            pltpu.VMEM(sums_shape, jnp.float32),
            pltpu.SemaphoreType.DMA((2, 4)),
        ],
        compiler_params=pltpu.CompilerParams(vmem_limit_bytes=(18 if n <= 8 else 44) * MIB),
        name="project",
    )(owners, *sums, gain, *near, *far, in_vmem(early), in_hbm(query_weight), in_hbm(keyval_weight))


def attend_kernel(scalars, queries, new_keys, new_values, cache_keys, cache_values, mine, other, keys, values, sems):
    rows, heads, _ = queries.shape
    side = scalars[rows]
    score_scale = 1.0 / math.sqrt(DH)
    copies = []
    for r in range(rows):
        for i, (source, target) in enumerate([(cache_keys, keys), (cache_values, values)]):
            copies.append(pltpu.make_async_copy(source.at[r], target.at[r], sems.at[i, r]))
            copies[-1].start()
    for r in range(rows):
        q = queries[r]
        copies[2 * r].wait()
        scores = lax.dot_general(q, keys[r], contract, preferred_element_type=jnp.float32)
        scores = scores * score_scale
        place = lax.broadcasted_iota(jnp.int32, scores.shape, 1)
        scores = jnp.where(place < scalars[r], scores, -1e30)
        new_key = new_keys[r : r + 1, :].astype(jnp.float32)
        own_score = jnp.sum(q.astype(jnp.float32) * new_key, axis=1, keepdims=True) * score_scale
        highest = jnp.maximum(jnp.max(scores, axis=1, keepdims=True), own_score)
        weights = jnp.exp(scores - highest)
        own_weight = jnp.exp(own_score - highest)
        totals = jnp.sum(weights, axis=1, keepdims=True) + own_weight
        copies[2 * r + 1].wait()
        blended = jnp.dot(
            weights.astype(jnp.bfloat16), values[r], preferred_element_type=jnp.float32
        )
        blended = (blended + own_weight * new_values[r : r + 1, :]) / totals
        low, high = blended[: heads // 2], blended[heads // 2 :]
        mine[r] = jnp.where(side == 0, low, high).astype(jnp.bfloat16)
        other[r] = jnp.where(side == 0, high, low).astype(jnp.bfloat16)


def attend(scalars, queries, new_keys, new_values, keys, values):
    rows, heads, _ = queries.shape
    shape = jax.ShapeDtypeStruct((rows, heads // 2, DH), jnp.bfloat16)
    return pl.pallas_call(
        attend_kernel,
        out_shape=[shape, shape],
        in_specs=[IN_SMEM] + [IN_VMEM] * 3 + [IN_HBM] * 2,
        out_specs=[IN_VMEM] * 2,
        scratch_shapes=[
            pltpu.VMEM(keys.shape, jnp.bfloat16),
            pltpu.VMEM(values.shape, jnp.bfloat16),
            pltpu.SemaphoreType.DMA((2, rows)),
        ],
        compiler_params=pltpu.CompilerParams(vmem_limit_bytes=14 * MIB),
        name="attend",
    )(scalars, queries, new_keys, new_values, in_hbm(keys), in_hbm(values))


def output_kernel(n, *refs):
    owners = refs[0]
    near = refs[1:n]
    far = refs[n : n + 2]
    early, weight, keep, give, late, total, placed, sems = refs[n + 2 :]
    first = early.shape[0]
    copies = start_copies(weight.at[pl.ds(first, late.shape[0])], late, sems, 4)
    rows = near[0].shape[0]
    half = far[0].shape[1]
    x = [ref[...].astype(jnp.float32) for ref in near]
    x.append(jnp.concatenate([ref[...].astype(jnp.float32) for ref in far], axis=1))
    x = jnp.concatenate(x, axis=0).astype(jnp.bfloat16)
    total[...] = jnp.dot(x[:, :first], early[...], preferred_element_type=jnp.float32)
    for copy in copies:
        copy.wait()
    total[...] += jnp.dot(x[:, first:], late[...], preferred_element_type=jnp.float32)
    for i in range(n):
        placed[owners[i]] = total[i * rows : (i + 1) * rows, :]
    side = owners[n]
    keep[...] = placed[pl.ds(side * (n // 2), n // 2)]
    give[...] = placed[pl.ds((1 - side) * (n // 2), n // 2)]


def output_project(n, owners, near, far, early, weight):
    rows = near[0].shape[0]
    depth, cols = weight.shape
    shape = jax.ShapeDtypeStruct((n // 2, rows, cols), jnp.float32)
    return pl.pallas_call(
        lambda *refs: output_kernel(n, *refs),
        out_shape=[shape, shape],
        in_specs=[IN_SMEM] + [IN_VMEM] * (n + 2) + [IN_HBM],
        out_specs=[IN_VMEM] * 2,
        scratch_shapes=[
            pltpu.VMEM((depth - early.shape[0], cols), jnp.bfloat16),
            pltpu.VMEM((n * rows, cols), jnp.float32),
            pltpu.VMEM((n, rows, cols), jnp.float32),
            pltpu.SemaphoreType.DMA((4,)),
        ],
        compiler_params=pltpu.CompilerParams(vmem_limit_bytes=(18 if n <= 8 else 44) * MIB),
        name="output_project",
    )(owners, *near, *far, in_vmem(early), in_hbm(weight))


def on_device(
    activations,
    norm_gain,
    query_weight,
    keyval_weight,
    output_weight,
    cache_keys,
    cache_values,
    cache_lengths,
):
    n = lax.axis_size("gx")
    ring = Ring(n)
    owners = ring.owners()
    query_cols, width = query_weight.shape
    piece = query_cols // 64 * 16
    weight = (3 * piece, width)

    left = right = activations
    near = [activations]
    own_sums = row_sums([activations])
    far_sums = lax.ppermute(own_sums, "gx", ring.across)
    sums = [own_sums]
    for step in range(1, n // 2):
        after = [] if step == 1 else [left, right]
        left, right = ring.step(left, right)
        near += [left, right]
        if step <= 3:
            start = (step - 1) * piece
            weight = load(weight, [(query_weight, start, piece, start)], after)
            weight, (left, right) = before(weight, left, right)
        sums.append(row_sums([left, right]))
    half = activations.shape[1] // 2
    far = ring.step(left[:, :half], right[:, half:])
    sums = jnp.concatenate(sums + [far_sums], axis=0)
    sums = (sums, swap_pair(sums))
    gain = norm_gain.astype(jnp.float32)[None, :]
    keep, give = project(
        n, owners, sums, gain, near, far, weight, query_weight, keyval_weight
    )
    projected = (keep + swap_pair(give)).astype(jnp.bfloat16)
    local_rows = cache_lengths.shape[0]
    depth, out_cols = output_weight.shape
    early = depth // 48 * 32
    out_weight = load((early, out_cols), [(output_weight, 0, early, 0)], [projected])
    gathered = lax.all_to_all(projected, "gx", split_axis=0, concat_axis=0, tiled=True)
    out_weight, (gathered,) = before(out_weight, gathered)
    gathered = jnp.swapaxes(gathered, 0, 1)
    queries = gathered[:, :, :query_cols].reshape(local_rows, HEADS, DH)
    keyvals = gathered[:, :, query_cols:].reshape(local_rows, 2 * DH)
    places = cache_lengths.astype(jnp.float32)
    queries = rotate(queries.astype(jnp.float32), places[:, None, None]).astype(jnp.bfloat16)
    new_keys = rotate(keyvals[:, :DH].astype(jnp.float32), places[:, None]).astype(jnp.bfloat16)
    new_values = keyvals[:, DH:].astype(jnp.float32)
    side = lax.axis_index("gy")
    scalars = jnp.concatenate([cache_lengths, side[None].astype(jnp.int32)])
    mine, other = attend(
        scalars, queries, new_keys, new_values, cache_keys, cache_values
    )
    mine = mine.reshape(local_rows, -1)
    other = swap_pair(other.reshape(local_rows, -1))
    first = jnp.where(side == 0, mine, other)
    second = jnp.where(side == 0, other, mine)
    swapped = jnp.concatenate([first, second], axis=0)

    left = right = swapped
    near = [swapped]
    for step in range(1, n // 2):
        left, right = ring.step(left, right)
        near += [left, right]
    half = swapped.shape[1] // 2
    far = ring.step(left[:, :half], right[:, half:])
    keep, give = output_project(n, owners, near, far, out_weight, output_weight)
    out = (keep + swap_pair(give)).astype(jnp.bfloat16)
    return out.reshape(-1, out.shape[-1])


def solution(mesh):
    return jax.shard_map(
        on_device,
        mesh=mesh,
        in_specs=(
            P(("groups", "gx"), "gy"),
            P("gy"),
            P("gx", "gy"),
            P("gx", "gy"),
            P("gy", "gx"),
            P(("groups", "gx", "gy"), None, None),
            P(("groups", "gx", "gy"), None, None),
            P(("groups", "gx", "gy")),
        ),
        out_specs=P(("groups", "gy"), "gx"),
        check_vma=False,
    )
```

time: 95.5 us -> 144 us (1.51)
  local copies, waits for them, and re-layouts: 8.04 us -> 56.4 us
  waiting for transfers between devices: 12.5 us -> 18.8 us
  matrix products: 4.85 us -> 0 us
    unnamed x31 -> x32, local copies, waits for them, and re-layouts: 7.56 us -> 56.2 us
    ppermute x8, waiting for transfers between devices: 3.28 us -> 12.7 us  [step(): lax.ppermute(left, 'gx', self.onward)]
    dot_general x3 -> x0, matrix products: 4.85 us -> none  [the longest x1 3.83 us: on_device(): jnp.einsum('rhd,rtd->rht', queries, cache_keys, preferred_element_type=jn...]
    ppermute x8, starting transfers between devices: 8.54 us -> 10.5 us  [step(): lax.ppermute(left, 'gx', self.onward)]
    ppermute x8, starting transfers between devices: 8.81 us -> 6.9 us  [step(): lax.ppermute(right, 'gx', self.back)]
    ppermute x8, waiting for transfers between devices: 3.76 us -> 2.06 us  [step(): lax.ppermute(right, 'gx', self.back)]
    pallas_call x10 -> x7, Pallas kernels: 39.6 us -> 39.6 us  [the longest x4 15.9 us: load(): pl.pallas_call(lambda *refs: load_kernel([job[1:] for job in jobs], *refs...]
  transfers between devices with their start and end apart: 22 -> 22, of which waited for: 10 -> 9; matrix products, arithmetic and copies ran while one was open for 0% -> 0% of each run, Pallas kernels for 27% -> 11%
where the time goes in v4:
time: 144 us
  local copies, waits for them, and re-layouts  56.4 us (39%)
  Pallas kernels  40.3 us (28%)
  starting transfers between devices  26.3 us (18%)
  waiting for transfers between devices  18.8 us (13%)
  other arithmetic  1.86 us (1%)
    unnamed x32, local copies, waits for them, and re-layouts  56.2 us
    pallas_call x4, Pallas kernels, load(): pl.pallas_call(lambda *refs: load_kernel([job[1:] for job in jobs], *refs...  15.9 us
    ppermute x8, waiting for transfers between devices, step(): lax.ppermute(left, 'gx', self.onward)  12.7 us
    pallas_call x1, Pallas kernels, project(): pl.pallas_call(lambda *refs: project_kernel(n, turned, *refs), out_shape=...  11 us
    ppermute x8, starting transfers between devices, step(): lax.ppermute(left, 'gx', self.onward)  10.5 us
    ppermute x8, starting transfers between devices, step(): lax.ppermute(right, 'gx', self.back)  6.9 us
    pallas_call x1, Pallas kernels, attend(): pl.pallas_call(attend_kernel, out_shape=[shape, shape], in_specs=[IN_SMEM...  6.47 us
    pallas_call x1, Pallas kernels, output_project(): pl.pallas_call(lambda *refs: output_kernel(n, *refs), out_shape=[shape, s...  6.27 us
  transfers between devices with their start and end apart: 22, of which 9 were waited for; matrix products, arithmetic and copies ran while one was open for 0% of the time, Pallas kernels for 11%

profile of v4, /device:TPU:0, one launch (start us, length us, event | category | flops | bytes accessed | tf_op | source)
XLA Modules:
  0.0 143.9 jit_solution(12155161646980231076)
XLA Ops:
  0.0 3.0 %collective-permute-start = (bf16[8,9216]{1,0:T(8,128)(2,1)}, bf16[8,9216]{1,0:T(8,128)(2,1)S(1)}, u32[]{:S(2)}, u32[]{:S(2)}) collective-permute-start(bf16[8,9216]{1,0:T(8,128)(2,1)} %refs_4_.1), channel_id=1, source_target_pairs={{0,4},{4,8},{8,12},{12,14},{14,10},{10,6},{6,2},{2,0},{1,5},{5,9},... | collective-permute-start | bytes 442376 | tf_op jit(solution)/shard_map/ppermute | solution.py:68
  3.0 1.0 copy-done.8
  4.0 0.2 row_sums.4
  4.2 5.0 %collective-permute-start.6 = (f32[8,128]{1,0:T(8,128)S(1)}, f32[8,128]{1,0:T(8,128)S(1)}, u32[]{:S(2)}, u32[]{:S(2)}) collective-permute-start(f32[8,128]{1,0:T(8,128)S(1)} %row_sums.4), channel_id=1, source_target_pairs={{0,14},{4,10},{8,6},{12,2},{14,0},{10,4},{6,8},{2,12},{1,15},{5,11... | collective-permute-start | bytes 12296 | tf_op jit(solution)/shard_map/ppermute | solution.py:342
  9.1 3.1 %load.4.refs_1_ = bf16[1152,9216]{1,0:T(8,128)(2,1)S(1)} custom-call(bf16[1536,9216]{1,0:T(8,128)(2,1)} %refs_14_.1), custom_call_target="tpu_custom_call" | custom-call | tf_op jit(solution)/shard_map/load/pallas_call | solution.py:98
  12.3 7.1 %copy-done = bf16[1152,9216]{1,0:T(8,128)(2,1)} copy-done((bf16[1152,9216]{1,0:T(8,128)(2,1)}, bf16[1152,9216]{1,0:T(8,128)(2,1)S(1)}, u32[]{:S(2)}) %copy-start) | copy-done | bytes 21233688
  19.3 2.0 %collective-permute-start.3 = (bf16[8,9216]{1,0:T(8,128)(2,1)S(1)}, bf16[8,9216]{1,0:T(8,128)(2,1)S(1)}, u32[]{:S(2)}, u32[]{:S(2)}) collective-permute-start(bf16[8,9216]{1,0:T(8,128)(2,1)S(1)} %collective-permute-done.1.refs_1_.refs_3_.refs_6_), channel_id=1, source_target_pairs={{0,2},{4,0},{8,4},{12,8},{14,12},{10,14},{6,10},{2,6},{1,3},{5,1},... | collective-permute-start | bytes 442376 | tf_op jit(solution)/shard_map/ppermute | solution.py:68
  21.4 0.2 row_sums.5
  21.6 7.0 %copy-done.1 = bf16[1152,9216]{1,0:T(8,128)(2,1)S(1)} copy-done((bf16[1152,9216]{1,0:T(8,128)(2,1)S(1)}, bf16[1152,9216]{1,0:T(8,128)(2,1)}, u32[]{:S(2)}) %copy-start.1) | copy-done | bytes 21233688
  28.6 3.1 %load.5.refs_1_ = bf16[1152,9216]{1,0:T(8,128)(2,1)S(1)} custom-call(bf16[1536,9216]{1,0:T(8,128)(2,1)} %refs_14_.1, bf16[1152,9216]{1,0:T(8,128)(2,1)S(1)} %copy-done.1, bf16[8,9216]{1,0:T(8,128)(2,1)S(1)} %collective-permute-done.refs_0_.refs_2_.refs_5_, ...), custom_call_target="tpu_custom_call", output_to_operand_aliasing={{}: (1, {})} | custom-call | tf_op jit(solution)/shard_map/load/pallas_call | solution.py:98
  31.7 7.1 %copy-done.2 = bf16[1152,9216]{1,0:T(8,128)(2,1)} copy-done((bf16[1152,9216]{1,0:T(8,128)(2,1)}, bf16[1152,9216]{1,0:T(8,128)(2,1)S(1)}, u32[]{:S(2)}) %copy-start.2) | copy-done | bytes 21233688
  38.9 2.0 %collective-permute-start.5 = (bf16[8,9216]{1,0:T(8,128)(2,1)S(1)}, bf16[8,9216]{1,0:T(8,128)(2,1)S(1)}, u32[]{:S(2)}, u32[]{:S(2)}) collective-permute-start(bf16[8,9216]{1,0:T(8,128)(2,1)S(1)} %collective-permute-done.3.refs_1_.refs_3_.refs_8_), channel_id=1, source_target_pairs={{0,2},{4,0},{8,4},{12,8},{14,12},{10,14},{6,10},{2,6},{1,3},{5,1},... | collective-permute-start | bytes 442376 | tf_op jit(solution)/shard_map/ppermute | solution.py:68
  40.8 0.2 row_sums.6
  41.0 7.0 %copy-done.3 = bf16[1152,9216]{1,0:T(8,128)(2,1)S(1)} copy-done((bf16[1152,9216]{1,0:T(8,128)(2,1)S(1)}, bf16[1152,9216]{1,0:T(8,128)(2,1)}, u32[]{:S(2)}) %copy-start.3) | copy-done | bytes 21233688
  48.1 3.1 %load.6.refs_13_ = bf16[1152,9216]{1,0:T(8,128)(2,1)S(1)} custom-call(bf16[1536,9216]{1,0:T(8,128)(2,1)} %refs_14_.1, bf16[1152,9216]{1,0:T(8,128)(2,1)S(1)} %copy-done.3, bf16[8,9216]{1,0:T(8,128)(2,1)S(1)} %collective-permute-done.2.refs_0_.refs_2_.refs_7_, ...), custom_call_target="tpu_custom_call", output_to_operand_aliasing={{}: (1, {})} | custom-call | tf_op jit(solution)/shard_map/load/pallas_call | solution.py:98
  51.2 7.1 %copy-done.4 = bf16[1152,9216]{1,0:T(8,128)(2,1)} copy-done((bf16[1152,9216]{1,0:T(8,128)(2,1)}, bf16[1152,9216]{1,0:T(8,128)(2,1)S(1)}, u32[]{:S(2)}) %copy-start.4) | copy-done | bytes 21233688
  58.3 0.2 row_sums.7
  58.6 0.1 collective-permute-start.8
  58.7 2.0 %collective-permute-start.9 = (bf16[8,4608]{1,0:T(8,128)(2,1)S(1)}, bf16[8,4608]{1,0:T(8,128)(2,1)S(1)}, u32[]{:S(2)}, u32[]{:S(2)}) collective-permute-start(bf16[8,4608]{1,0:T(8,128)(2,1)S(1)} %slice.37), channel_id=1, source_target_pairs={{0,2},{4,0},{8,4},{12,8},{14,12},{10,14},{6,10},{2,6},{1,3},{5,1},... | collective-permute-start | bytes 221192 | tf_op jit(solution)/shard_map/ppermute | solution.py:68
  60.8 2.5 %collective-permute-done.8.refs_11_ = bf16[8,4608]{1,0:T(8,128)(2,1)S(1)} collective-permute-done((bf16[8,4608]{1,0:T(8,128)(2,1)S(1)}, bf16[8,4608]{1,0:T(8,128)(2,1)S(1)}, u32[]{:S(2)}, u32[]{:S(2)}) %collective-permute-start.8) | collective-permute-done | bytes 73760 | tf_op jit(solution)/shard_map/ppermute | solution.py:68
  63.3 7.0 %copy-done.5 = bf16[1152,9216]{1,0:T(8,128)(2,1)S(1)} copy-done((bf16[1152,9216]{1,0:T(8,128)(2,1)S(1)}, bf16[1152,9216]{1,0:T(8,128)(2,1)}, u32[]{:S(2)}) %copy-start.5) | copy-done | bytes 21233688
  70.3 11.0 %project.1 = (f32[8,4,1600]{2,1,0:T(4,128)S(1)}, f32[8,4,1600]{2,1,0:T(4,128)S(1)}) custom-call(s32[9]{0:T(128)S(1)} %pad_add_fusion.refs_0_, f32[64,128]{1,0:T(8,128)S(1)} %constant_dynamic-update-slice_fusion.refs_1_, f32[64,128]{1,0:T(8,128)S(1)} %collective-permute-done.7.refs_2_, f32[1,9216]{1,0:T(1,128)S(1)} %bitcast.9, bf16[8,9216]{1,0:T(8,128)(2,1)S(1)} %copy-done.9, ...), custom_call_target="tpu_custom_call" | custom-call | tf_op jit(solution)/shard_map/project/pallas_call | solution.py:212
  81.4 1.4 collective-permute-done.10
  82.8 0.7 add_convert_fusion.1.refs_1_
  83.5 3.5 %all-to-all-start = ((bf16[8,4,1600]{2,1,0:T(4,128)(2,1)}), bf16[8,4,1600]{2,1,0:T(4,128)(2,1)S(1)}, u32[]{:S(2)}, u32[]{:S(2)}) async-start(bf16[8,4,1600]{2,1,0:T(4,128)(2,1)} %add_convert_fusion.1.refs_1_), calls=%async_computation | async-start | bytes 212992 | tf_op jit(solution)/shard_map/all_to_all | solution.py:366
  87.2 6.5 %load.7.refs_10_ = bf16[4096,2304]{1,0:T(8,128)(2,1)S(1)} custom-call(bf16[6144,2304]{1,0:T(8,128)(2,1)} %refs_11_.1, bf16[8,4,1600]{2,1,0:T(4,128)(2,1)} %add_convert_fusion.1.refs_1_), custom_call_target="tpu_custom_call" | custom-call | tf_op jit(solution)/shard_map/load/pallas_call | solution.py:98
  93.7 6.4 %copy-done.6 = bf16[4096,2304]{1,0:T(8,128)(2,1)} copy-done((bf16[4096,2304]{1,0:T(8,128)(2,1)}, bf16[4096,2304]{1,0:T(8,128)(2,1)S(1)}, u32[]{:S(2)}) %copy-start.6) | copy-done | bytes 18874392
  100.4 0.1 subtract_convert_fusion.1
  100.6 6.5 %attend.1 = (bf16[4,24,256]{2,1,0:T(8,128)(2,1)S(1)}, bf16[4,24,256]{2,1,0:T(8,128)(2,1)S(1)}) custom-call(s32[5]{0:T(128)S(1)} %pad_add_fusion.1.scalars, bf16[4,48,256]{2,1,0:T(8,128)(2,1)S(1)} %pad_maximum_fusion.queries, bf16[4,256]{1,0:T(4,128)(2,1)S(1)} %pad_maximum_fusion.2.new_keys, f32[4,256]{1,0:T(4,128)S(1)} %get-tuple-element.45.new_values, ...), custom_call_target="tpu_custom_call" | custom-call | tf_op jit(solution)/shard_map/attend/pallas_call | solution.py:264
  107.1 0.2 collective-permute-start.11
  107.3 1.1 collective-permute-done.11
  108.5 1.8 %collective-permute-start.12 = (bf16[8,6144]{1,0:T(8,128)(2,1)S(1)}, bf16[8,6144]{1,0:T(8,128)(2,1)S(1)}, u32[]{:S(2)}, u32[]{:S(2)}) collective-permute-start(bf16[8,6144]{1,0:T(8,128)(2,1)S(1)} %pad_maximum_fusion.1.refs_1_), channel_id=1, source_target_pairs={{0,4},{4,8},{8,12},{12,14},{14,10},{10,6},{6,2},{2,0},{1,5},{5,9},... | collective-permute-start | bytes 294920 | tf_op jit(solution)/shard_map/ppermute | solution.py:68
  110.3 0.3 collective-permute-start.13
  110.6 2.8 %collective-permute-done.12.refs_2_ = bf16[8,6144]{1,0:T(8,128)(2,1)S(1)} collective-permute-done((bf16[8,6144]{1,0:T(8,128)(2,1)S(1)}, bf16[8,6144]{1,0:T(8,128)(2,1)S(1)}, u32[]{:S(2)}, u32[]{:S(2)}) %collective-permute-start.12) | collective-permute-done | bytes 98336 | tf_op jit(solution)/shard_map/ppermute | solution.py:68
  113.4 1.7 %collective-permute-start.14 = (bf16[8,6144]{1,0:T(8,128)(2,1)S(1)}, bf16[8,6144]{1,0:T(8,128)(2,1)S(1)}, u32[]{:S(2)}, u32[]{:S(2)}) collective-permute-start(bf16[8,6144]{1,0:T(8,128)(2,1)S(1)} %collective-permute-done.12.refs_2_), channel_id=1, source_target_pairs={{0,4},{4,8},{8,12},{12,14},{14,10},{10,6},{6,2},{2,0},{1,5},{5,9},... | collective-permute-start | bytes 294920 | tf_op jit(solution)/shard_map/ppermute | solution.py:68
  115.2 0.3 collective-permute-start.15
  115.4 2.6 %collective-permute-done.14.refs_4_ = bf16[8,6144]{1,0:T(8,128)(2,1)S(1)} collective-permute-done((bf16[8,6144]{1,0:T(8,128)(2,1)S(1)}, bf16[8,6144]{1,0:T(8,128)(2,1)S(1)}, u32[]{:S(2)}, u32[]{:S(2)}) %collective-permute-start.14) | collective-permute-done | bytes 98336 | tf_op jit(solution)/shard_map/ppermute | solution.py:68
  118.0 1.7 %collective-permute-start.16 = (bf16[8,6144]{1,0:T(8,128)(2,1)S(1)}, bf16[8,6144]{1,0:T(8,128)(2,1)S(1)}, u32[]{:S(2)}, u32[]{:S(2)}) collective-permute-start(bf16[8,6144]{1,0:T(8,128)(2,1)S(1)} %collective-permute-done.14.refs_4_), channel_id=1, source_target_pairs={{0,4},{4,8},{8,12},{12,14},{14,10},{10,6},{6,2},{2,0},{1,5},{5,9},... | collective-permute-start | bytes 294920 | tf_op jit(solution)/shard_map/ppermute | solution.py:68
  119.8 0.3 collective-permute-start.17
  120.1 2.8 %collective-permute-done.16.refs_6_ = bf16[8,6144]{1,0:T(8,128)(2,1)S(1)} collective-permute-done((bf16[8,6144]{1,0:T(8,128)(2,1)S(1)}, bf16[8,6144]{1,0:T(8,128)(2,1)S(1)}, u32[]{:S(2)}, u32[]{:S(2)}) %collective-permute-start.16) | collective-permute-done | bytes 98336 | tf_op jit(solution)/shard_map/ppermute | solution.py:68
  122.8 2.0 %collective-permute-start.18 = (bf16[8,3072]{1,0:T(8,128)(2,1)S(1)}, bf16[8,3072]{1,0:T(8,128)(2,1)S(1)}, u32[]{:S(2)}, u32[]{:S(2)}) collective-permute-start(bf16[8,3072]{1,0:T(8,128)(2,1)S(1)} %slice.56), channel_id=1, source_target_pairs={{0,4},{4,8},{8,12},{12,14},{14,10},{10,6},{6,2},{2,0},{1,5},{5,9},... | collective-permute-start | bytes 147464 | tf_op jit(solution)/shard_map/ppermute | solution.py:68
  124.8 0.1 collective-permute-start.19
  124.9 2.0 %collective-permute-done.18.refs_8_ = bf16[8,3072]{1,0:T(8,128)(2,1)S(1)} collective-permute-done((bf16[8,3072]{1,0:T(8,128)(2,1)S(1)}, bf16[8,3072]{1,0:T(8,128)(2,1)S(1)}, u32[]{:S(2)}, u32[]{:S(2)}) %collective-permute-start.18) | collective-permute-done | bytes 49184 | tf_op jit(solution)/shard_map/ppermute | solution.py:68
  126.9 2.0 %collective-permute-done.19.refs_9_ = bf16[8,3072]{1,0:T(8,128)(2,1)S(1)} collective-permute-done((bf16[8,3072]{1,0:T(8,128)(2,1)S(1)}, bf16[8,3072]{1,0:T(8,128)(2,1)S(1)}, u32[]{:S(2)}, u32[]{:S(2)}) %collective-permute-start.19) | collective-permute-done | bytes 49184 | tf_op jit(solution)/shard_map/ppermute | solution.py:68
  128.9 6.4 %copy-done.7 = bf16[4096,2304]{1,0:T(8,128)(2,1)S(1)} copy-done((bf16[4096,2304]{1,0:T(8,128)(2,1)S(1)}, bf16[4096,2304]{1,0:T(8,128)(2,1)}, u32[]{:S(2)}) %copy-start.7) | copy-done | bytes 18874392
  135.3 6.3 %output_project.1 = (f32[4,8,2304]{2,1,0:T(8,128)S(1)}, f32[4,8,2304]{2,1,0:T(8,128)S(1)}) custom-call(s32[9]{0:T(128)S(1)} %pad_add_fusion.refs_0_, bf16[8,6144]{1,0:T(8,128)(2,1)S(1)} %pad_maximum_fusion.1.refs_1_, bf16[8,6144]{1,0:T(8,128)(2,1)S(1)} %collective-permute-done.12.refs_2_, bf16[8,6144]{1,0:T(8,128)(2,1)S(1)} %collective-permute-done.13.refs_3_, ...), custom_call_target="tpu_custom_call" | custom-call | tf_op jit(solution)/shard_map/output_project/pallas_call | solution.py:306
  141.7 1.6 %collective-permute-done.20 = f32[4,8,2304]{2,1,0:T(8,128)S(1)} collective-permute-done((f32[4,8,2304]{2,1,0:T(8,128)S(1)}, f32[4,8,2304]{2,1,0:T(8,128)S(1)}, u32[]{:S(2)}, u32[]{:S(2)}) %collective-permute-start.20) | collective-permute-done | bytes 294944 | tf_op jit(solution)/shard_map/ppermute | solution.py:44
  143.2 0.7 fusion
  (65 shorter events, 1.0 us)
Async XLA Ops:
  0.0 19.3 %collective-permute-start = (bf16[8,9216]{1,0:T(8,128)(2,1)}, bf16[8,9216]{1,0:T(8,128)(2,1)S(1)}, u32[]{:S(2)}, u32[]{:S(2)}) collective-permute-start(bf16[8,9216]{1,0:T(8,128)(2,1)} %refs_4_.1), channel_id=1, source_target_pairs={{0,4},{4,8},{8,12},{12,14},{14,10},{10,6},{6,2},{2,0},{1,5},{5,9},... | collective-permute-start | bytes 442376 | tf_op jit(solution)/shard_map/ppermute | solution.py:68
  3.0 16.3 %collective-permute-start.1 = (bf16[8,9216]{1,0:T(8,128)(2,1)}, bf16[8,9216]{1,0:T(8,128)(2,1)S(1)}, u32[]{:S(2)}, u32[]{:S(2)}) collective-permute-start(bf16[8,9216]{1,0:T(8,128)(2,1)} %refs_4_.1), channel_id=1, source_target_pairs={{0,2},{4,0},{8,4},{12,8},{14,12},{10,14},{6,10},{2,6},{1,3},{5,1},... | collective-permute-start | bytes 442376 | tf_op jit(solution)/shard_map/ppermute | solution.py:68
  3.0 1.0 copy-start.8
  4.2 54.3 %collective-permute-start.6 = (f32[8,128]{1,0:T(8,128)S(1)}, f32[8,128]{1,0:T(8,128)S(1)}, u32[]{:S(2)}, u32[]{:S(2)}) collective-permute-start(f32[8,128]{1,0:T(8,128)S(1)} %row_sums.4), channel_id=1, source_target_pairs={{0,14},{4,10},{8,6},{12,2},{14,0},{10,4},{6,8},{2,12},{1,15},{5,11... | collective-permute-start | bytes 12296 | tf_op jit(solution)/shard_map/ppermute | solution.py:342
  9.1 12.2 %copy-start.12 = (s32[8]{0:T(128)S(1)}, s32[8]{0:T(128)}, u32[]{:S(2)}) copy-start(s32[8]{0:T(128)} %constant.64.clone) | copy-start | bytes 100
  12.3 7.1 %copy-start = (bf16[1152,9216]{1,0:T(8,128)(2,1)}, bf16[1152,9216]{1,0:T(8,128)(2,1)S(1)}, u32[]{:S(2)}) copy-start(bf16[1152,9216]{1,0:T(8,128)(2,1)S(1)} %load.4.refs_1_) | copy-start | bytes 63700996
  19.3 19.5 %collective-permute-start.2 = (bf16[8,9216]{1,0:T(8,128)(2,1)S(1)}, bf16[8,9216]{1,0:T(8,128)(2,1)S(1)}, u32[]{:S(2)}, u32[]{:S(2)}) collective-permute-start(bf16[8,9216]{1,0:T(8,128)(2,1)S(1)} %collective-permute-done.refs_0_.refs_2_.refs_5_), channel_id=1, source_target_pairs={{0,4},{4,8},{8,12},{12,14},{14,10},{10,6},{6,2},{2,0},{1,5},{5,9},... | collective-permute-start | bytes 442376 | tf_op jit(solution)/shard_map/ppermute | solution.py:68
  19.3 19.5 %collective-permute-start.3 = (bf16[8,9216]{1,0:T(8,128)(2,1)S(1)}, bf16[8,9216]{1,0:T(8,128)(2,1)S(1)}, u32[]{:S(2)}, u32[]{:S(2)}) collective-permute-start(bf16[8,9216]{1,0:T(8,128)(2,1)S(1)} %collective-permute-done.1.refs_1_.refs_3_.refs_6_), channel_id=1, source_target_pairs={{0,2},{4,0},{8,4},{12,8},{14,12},{10,14},{6,10},{2,6},{1,3},{5,1},... | collective-permute-start | bytes 442376 | tf_op jit(solution)/shard_map/ppermute | solution.py:68
  21.6 7.0 %copy-start.1 = (bf16[1152,9216]{1,0:T(8,128)(2,1)S(1)}, bf16[1152,9216]{1,0:T(8,128)(2,1)}, u32[]{:S(2)}) copy-start(bf16[1152,9216]{1,0:T(8,128)(2,1)} %copy-done) | copy-start | bytes 63700996
  31.7 7.1 %copy-start.2 = (bf16[1152,9216]{1,0:T(8,128)(2,1)}, bf16[1152,9216]{1,0:T(8,128)(2,1)S(1)}, u32[]{:S(2)}) copy-start(bf16[1152,9216]{1,0:T(8,128)(2,1)S(1)} %load.5.refs_1_) | copy-start | bytes 63700996
  38.8 19.5 %collective-permute-start.4 = (bf16[8,9216]{1,0:T(8,128)(2,1)S(1)}, bf16[8,9216]{1,0:T(8,128)(2,1)S(1)}, u32[]{:S(2)}, u32[]{:S(2)}) collective-permute-start(bf16[8,9216]{1,0:T(8,128)(2,1)S(1)} %collective-permute-done.2.refs_0_.refs_2_.refs_7_), channel_id=1, source_target_pairs={{0,4},{4,8},{8,12},{12,14},{14,10},{10,6},{6,2},{2,0},{1,5},{5,9},... | collective-permute-start | bytes 442376 | tf_op jit(solution)/shard_map/ppermute | solution.py:68
  38.9 19.4 %collective-permute-start.5 = (bf16[8,9216]{1,0:T(8,128)(2,1)S(1)}, bf16[8,9216]{1,0:T(8,128)(2,1)S(1)}, u32[]{:S(2)}, u32[]{:S(2)}) collective-permute-start(bf16[8,9216]{1,0:T(8,128)(2,1)S(1)} %collective-permute-done.3.refs_1_.refs_3_.refs_8_), channel_id=1, source_target_pairs={{0,2},{4,0},{8,4},{12,8},{14,12},{10,14},{6,10},{2,6},{1,3},{5,1},... | collective-permute-start | bytes 442376 | tf_op jit(solution)/shard_map/ppermute | solution.py:68
  41.0 7.0 %copy-start.3 = (bf16[1152,9216]{1,0:T(8,128)(2,1)S(1)}, bf16[1152,9216]{1,0:T(8,128)(2,1)}, u32[]{:S(2)}) copy-start(bf16[1152,9216]{1,0:T(8,128)(2,1)} %copy-done.2) | copy-start | bytes 63700996
  48.1 12.7 %copy-start.10 = (bf16[9216]{0:T(1024)(128)(2,1)S(1)}, bf16[9216]{0:T(1024)(128)(2,1)}, u32[]{:S(2)}) copy-start(bf16[9216]{0:T(1024)(128)(2,1)} %param.10) | copy-start | bytes 55300
  48.1 15.2 %copy-start.9 = (bf16[8,9216]{1,0:T(8,128)(2,1)S(1)}, bf16[8,9216]{1,0:T(8,128)(2,1)}, u32[]{:S(2)}) copy-start(bf16[8,9216]{1,0:T(8,128)(2,1)} %refs_4_.1) | copy-start | bytes 442372
  51.2 7.1 %copy-start.4 = (bf16[1152,9216]{1,0:T(8,128)(2,1)}, bf16[1152,9216]{1,0:T(8,128)(2,1)S(1)}, u32[]{:S(2)}) copy-start(bf16[1152,9216]{1,0:T(8,128)(2,1)S(1)} %load.6.refs_13_) | copy-start | bytes 63700996
  58.5 2.2 %collective-permute-start.7 = (f32[64,128]{1,0:T(8,128)S(1)}, f32[64,128]{1,0:T(8,128)S(1)}, u32[]{:S(2)}, u32[]{:S(2)}) collective-permute-start(f32[64,128]{1,0:T(8,128)S(1)} %constant_dynamic-update-slice_fusion.refs_1_), channel_id=1, source_target_pairs={{0,1},{1,0},{2,3},{3,2},{4,5},{5,4},{6,7},{7,6},{8,9},{9,8},{10,11... | collective-permute-start | bytes 98312 | tf_op jit(solution)/shard_map/ppermute | solution.py:44
  58.6 4.7 %collective-permute-start.8 = (bf16[8,4608]{1,0:T(8,128)(2,1)S(1)}, bf16[8,4608]{1,0:T(8,128)(2,1)S(1)}, u32[]{:S(2)}, u32[]{:S(2)}) collective-permute-start(bf16[8,4608]{1,0:T(8,128)(2,1)S(1)} %slice.36), channel_id=1, source_target_pairs={{0,4},{4,8},{8,12},{12,14},{14,10},{10,6},{6,2},{2,0},{1,5},{5,9},... | collective-permute-start | bytes 221192 | tf_op jit(solution)/shard_map/ppermute | solution.py:68
  58.7 4.6 %collective-permute-start.9 = (bf16[8,4608]{1,0:T(8,128)(2,1)S(1)}, bf16[8,4608]{1,0:T(8,128)(2,1)S(1)}, u32[]{:S(2)}, u32[]{:S(2)}) collective-permute-start(bf16[8,4608]{1,0:T(8,128)(2,1)S(1)} %slice.37), channel_id=1, source_target_pairs={{0,2},{4,0},{8,4},{12,8},{14,12},{10,14},{6,10},{2,6},{1,3},{5,1},... | collective-permute-start | bytes 221192 | tf_op jit(solution)/shard_map/ppermute | solution.py:68
  63.3 7.0 %copy-start.5 = (bf16[1152,9216]{1,0:T(8,128)(2,1)S(1)}, bf16[1152,9216]{1,0:T(8,128)(2,1)}, u32[]{:S(2)}) copy-start(bf16[1152,9216]{1,0:T(8,128)(2,1)} %copy-done.4) | copy-start | bytes 63700996
  70.3 11.1 %copy-start.11 = (s32[4]{0:T(128)S(1)}, s32[4]{0:T(128)}, u32[]{:S(2)}) copy-start(s32[4]{0:T(128)} %param.16) | copy-start | bytes 52
  81.3 1.5 %collective-permute-start.10 = (f32[8,4,1600]{2,1,0:T(4,128)S(1)}, f32[8,4,1600]{2,1,0:T(4,128)S(1)}, u32[]{:S(2)}, u32[]{:S(2)}) collective-permute-start(f32[8,4,1600]{2,1,0:T(4,128)S(1)} %get-tuple-element.32), channel_id=1, source_target_pairs={{0,1},{1,0},{2,3},{3,2},{4,5},{5,4},{6,7},{7,6},{8,9},{9,8},{10,11... | collective-permute-start | bytes 614408 | tf_op jit(solution)/shard_map/ppermute | solution.py:44
  83.5 16.6 %all-to-all-start = ((bf16[8,4,1600]{2,1,0:T(4,128)(2,1)}), bf16[8,4,1600]{2,1,0:T(4,128)(2,1)S(1)}, u32[]{:S(2)}, u32[]{:S(2)}) async-start(bf16[8,4,1600]{2,1,0:T(4,128)(2,1)} %add_convert_fusion.1.refs_1_), calls=%async_computation | async-start | bytes 212992 | tf_op jit(solution)/shard_map/all_to_all | solution.py:366
  93.7 6.4 %copy-start.6 = (bf16[4096,2304]{1,0:T(8,128)(2,1)}, bf16[4096,2304]{1,0:T(8,128)(2,1)S(1)}, u32[]{:S(2)}) copy-start(bf16[4096,2304]{1,0:T(8,128)(2,1)S(1)} %load.7.refs_10_) | copy-start | bytes 56623108
  107.1 1.3 collective-permute-start.11
  108.5 4.9 %collective-permute-start.12 = (bf16[8,6144]{1,0:T(8,128)(2,1)S(1)}, bf16[8,6144]{1,0:T(8,128)(2,1)S(1)}, u32[]{:S(2)}, u32[]{:S(2)}) collective-permute-start(bf16[8,6144]{1,0:T(8,128)(2,1)S(1)} %pad_maximum_fusion.1.refs_1_), channel_id=1, source_target_pairs={{0,4},{4,8},{8,12},{12,14},{14,10},{10,6},{6,2},{2,0},{1,5},{5,9},... | collective-permute-start | bytes 294920 | tf_op jit(solution)/shard_map/ppermute | solution.py:68
  110.3 4.9 %collective-permute-start.13 = (bf16[8,6144]{1,0:T(8,128)(2,1)S(1)}, bf16[8,6144]{1,0:T(8,128)(2,1)S(1)}, u32[]{:S(2)}, u32[]{:S(2)}) collective-permute-start(bf16[8,6144]{1,0:T(8,128)(2,1)S(1)} %pad_maximum_fusion.1.refs_1_), channel_id=1, source_target_pairs={{0,2},{4,0},{8,4},{12,8},{14,12},{10,14},{6,10},{2,6},{1,3},{5,1},... | collective-permute-start | bytes 294920 | tf_op jit(solution)/shard_map/ppermute | solution.py:68
  113.4 4.6 %collective-permute-start.14 = (bf16[8,6144]{1,0:T(8,128)(2,1)S(1)}, bf16[8,6144]{1,0:T(8,128)(2,1)S(1)}, u32[]{:S(2)}, u32[]{:S(2)}) collective-permute-start(bf16[8,6144]{1,0:T(8,128)(2,1)S(1)} %collective-permute-done.12.refs_2_), channel_id=1, source_target_pairs={{0,4},{4,8},{8,12},{12,14},{14,10},{10,6},{6,2},{2,0},{1,5},{5,9},... | collective-permute-start | bytes 294920 | tf_op jit(solution)/shard_map/ppermute | solution.py:68
  115.2 4.6 %collective-permute-start.15 = (bf16[8,6144]{1,0:T(8,128)(2,1)S(1)}, bf16[8,6144]{1,0:T(8,128)(2,1)S(1)}, u32[]{:S(2)}, u32[]{:S(2)}) collective-permute-start(bf16[8,6144]{1,0:T(8,128)(2,1)S(1)} %collective-permute-done.13.refs_3_), channel_id=1, source_target_pairs={{0,2},{4,0},{8,4},{12,8},{14,12},{10,14},{6,10},{2,6},{1,3},{5,1},... | collective-permute-start | bytes 294920 | tf_op jit(solution)/shard_map/ppermute | solution.py:68
  118.0 4.8 %collective-permute-start.16 = (bf16[8,6144]{1,0:T(8,128)(2,1)S(1)}, bf16[8,6144]{1,0:T(8,128)(2,1)S(1)}, u32[]{:S(2)}, u32[]{:S(2)}) collective-permute-start(bf16[8,6144]{1,0:T(8,128)(2,1)S(1)} %collective-permute-done.14.refs_4_), channel_id=1, source_target_pairs={{0,4},{4,8},{8,12},{12,14},{14,10},{10,6},{6,2},{2,0},{1,5},{5,9},... | collective-permute-start | bytes 294920 | tf_op jit(solution)/shard_map/ppermute | solution.py:68
  119.8 5.0 %collective-permute-start.17 = (bf16[8,6144]{1,0:T(8,128)(2,1)S(1)}, bf16[8,6144]{1,0:T(8,128)(2,1)S(1)}, u32[]{:S(2)}, u32[]{:S(2)}) collective-permute-start(bf16[8,6144]{1,0:T(8,128)(2,1)S(1)} %collective-permute-done.15.refs_5_), channel_id=1, source_target_pairs={{0,2},{4,0},{8,4},{12,8},{14,12},{10,14},{6,10},{2,6},{1,3},{5,1},... | collective-permute-start | bytes 294920 | tf_op jit(solution)/shard_map/ppermute | solution.py:68
  122.8 4.1 %collective-permute-start.18 = (bf16[8,3072]{1,0:T(8,128)(2,1)S(1)}, bf16[8,3072]{1,0:T(8,128)(2,1)S(1)}, u32[]{:S(2)}, u32[]{:S(2)}) collective-permute-start(bf16[8,3072]{1,0:T(8,128)(2,1)S(1)} %slice.56), channel_id=1, source_target_pairs={{0,4},{4,8},{8,12},{12,14},{14,10},{10,6},{6,2},{2,0},{1,5},{5,9},... | collective-permute-start | bytes 147464 | tf_op jit(solution)/shard_map/ppermute | solution.py:68
  124.8 4.1 %collective-permute-start.19 = (bf16[8,3072]{1,0:T(8,128)(2,1)S(1)}, bf16[8,3072]{1,0:T(8,128)(2,1)S(1)}, u32[]{:S(2)}, u32[]{:S(2)}) collective-permute-start(bf16[8,3072]{1,0:T(8,128)(2,1)S(1)} %slice.57), channel_id=1, source_target_pairs={{0,2},{4,0},{8,4},{12,8},{14,12},{10,14},{6,10},{2,6},{1,3},{5,1},... | collective-permute-start | bytes 147464 | tf_op jit(solution)/shard_map/ppermute | solution.py:68
  128.9 6.4 %copy-start.7 = (bf16[4096,2304]{1,0:T(8,128)(2,1)S(1)}, bf16[4096,2304]{1,0:T(8,128)(2,1)}, u32[]{:S(2)}) copy-start(bf16[4096,2304]{1,0:T(8,128)(2,1)} %copy-done.6) | copy-start | bytes 56623108
  141.6 1.6 %collective-permute-start.20 = (f32[4,8,2304]{2,1,0:T(8,128)S(1)}, f32[4,8,2304]{2,1,0:T(8,128)S(1)}, u32[]{:S(2)}, u32[]{:S(2)}) collective-permute-start(f32[4,8,2304]{2,1,0:T(8,128)S(1)} %get-tuple-element.38), channel_id=1, source_target_pairs={{0,1},{1,0},{2,3},{3,2},{4,5},{5,4},{6,7},{7,6},{8,9},{9,8},{10,11... | collective-permute-start | bytes 884744 | tf_op jit(solution)/shard_map/ppermute | solution.py:44

commit v5 on v4

v5 whole, which is shorter than its diff:
```python
import math

import jax
import jax.numpy as jnp
from jax import lax
from jax.experimental import pallas as pl
from jax.experimental.pallas import tpu as pltpu
from jax.sharding import PartitionSpec as P

D = 18432
HEADS = 48
DH = 256


epsilon = 1e-06
contract = (((1,), (1,)), ((), ()))
MIB = 1 << 20
ANY = pl.BlockSpec(memory_space=pl.ANY)
IN_HBM = pl.BlockSpec(memory_space=pltpu.HBM)
IN_VMEM = pl.BlockSpec(memory_space=pltpu.VMEM)
IN_SMEM = pl.BlockSpec(memory_space=pltpu.SMEM)


def rotate(vectors, places):
    half_width = vectors.shape[-1] // 2
    indices = jnp.arange(half_width, dtype=jnp.float32)
    frequency = jnp.exp(-math.log(10000.0) * indices / half_width)
    angles = places * frequency
    cosine = jnp.cos(angles)
    sine = jnp.sin(angles)
    first_half = vectors[..., :half_width]
    second_half = vectors[..., half_width:]
    return jnp.concatenate(
        [first_half * cosine - second_half * sine, second_half * cosine + first_half * sine],
        axis=-1,
    )


def ring_order(n):
    return list(range(0, n, 2)) + list(range(n - 1, 0, -2))


def swap_pair(x):
    return lax.ppermute(x, "gy", [(0, 1), (1, 0)])


class Ring:
    def __init__(self, n):
        self.n = n
        order = ring_order(n)
        self.onward = [(order[p], order[(p + 1) % n]) for p in range(n)]
        self.back = [(order[p], order[(p - 1) % n]) for p in range(n)]
        self.across = [(order[p], order[(p + n // 2) % n]) for p in range(n)]
        self.offsets = [0]
        for step in range(1, n // 2):
            self.offsets += [-step, step]
        self.offsets.append(n // 2)

    def owners(self):
        n = self.n
        me = lax.axis_index("gx")
        place = jnp.where(me % 2 == 0, me // 2, n - 1 - me // 2)
        at = (place + jnp.array(self.offsets, jnp.int32) + n) % n
        owner = jnp.where(at < n // 2, 2 * at, 2 * (n - 1 - at) + 1)
        return jnp.concatenate([owner, lax.axis_index("gy")[None]]).astype(jnp.int32)

    def step(self, left, right):
        return lax.ppermute(left, "gx", self.onward), lax.ppermute(right, "gx", self.back)


def start_copies(source, target, sems, count):
    rows = source.shape[0]
    size = -(-rows // (16 * count)) * 16
    copies = []
    for i, first in enumerate(range(0, rows, size)):
        at = pl.ds(first, min(size, rows - first))
        copy = pltpu.make_async_copy(source.at[at], target.at[at], sems.at[i])
        copy.start()
        copies.append(copy)
    return copies


def load_kernel(jobs, *refs):
    sources, targets, sems = refs[: len(jobs)], refs[-1 - len(jobs) : -1], refs[-1]
    copies = []
    for i, (first, size) in enumerate(jobs):
        part = sources[i].at[pl.ds(first, size)]
        if len(part.shape) == 3:
            for row in range(size):
                copies.append(pltpu.make_async_copy(part.at[row], targets[i].at[row], sems.at[i, row]))
                copies[-1].start()
        else:
            copies += start_copies(part, targets[i], sems.at[i], 4)
    for copy in copies:
        copy.wait()


def load(jobs, after=()):
    return pl.pallas_call(
        lambda *refs: load_kernel([job[1:] for job in jobs], *refs),
        out_shape=[pltpu.VMEM((size,) + array.shape[1:], array.dtype) for array, _, size in jobs],
        in_specs=[IN_HBM] * len(jobs) + [ANY] * len(after),
        out_specs=[IN_VMEM] * len(jobs),
        scratch_shapes=[pltpu.SemaphoreType.DMA((len(jobs), 4))],
        compiler_params=pltpu.CompilerParams(vmem_limit_bytes=MIB),
        name="load",
    )(*[in_hbm(job[0]) for job in jobs], *after)


def in_hbm(array):
    return pltpu.with_memory_space_constraint(array, pltpu.HBM)


def in_vmem(array):
    return pltpu.with_memory_space_constraint(array, pltpu.VMEM)


def before(done, *rest):
    held = lax.optimization_barrier((done,) + rest)
    return held[0], held[1:]


def sums_kernel(ready, count, *refs):
    out = refs[-1]
    start = 0
    for ref in refs[:ready]:
        out[start : start + ref.shape[0], :] = ref[...]
        start += ref.shape[0]
    rows = refs[ready].shape[0]
    lane = lax.broadcasted_iota(jnp.int32, (rows, 128), 1)
    for ref in refs[ready : ready + count]:
        x = ref[...].astype(jnp.float32)
        total = jnp.sum(x, axis=1, keepdims=True)
        square = jnp.sum(x * x, axis=1, keepdims=True)
        both = jnp.where(lane == 0, total, jnp.where(lane == 1, square, 0.0))
        out[start : start + rows, :] = both
        start += rows


def row_sums(shards, ready=(), after=()):
    rows = shards[0].shape[0] * len(shards) + sum(r.shape[0] for r in ready)
    return pl.pallas_call(
        lambda *refs: sums_kernel(len(ready), len(shards), *refs),
        out_shape=jax.ShapeDtypeStruct((rows, 128), jnp.float32),
        in_specs=[IN_VMEM] * (len(ready) + len(shards)) + [ANY] * len(after),
        out_specs=IN_VMEM,
        compiler_params=pltpu.CompilerParams(vmem_limit_bytes=8 * MIB),
        name="row_sums",
    )(*ready, *shards, *after)


def project_kernel(n, parts, *refs):
    owners, sums_a, sums_b, gain = refs[:4]
    near = refs[4 : 4 + n - 1]
    far = refs[4 + n - 1 : 4 + n + 1]
    early = refs[4 + n + 1 : 4 + n + 1 + parts]
    query_weight, keyval_weight, keep, give = refs[4 + n + 1 + parts : 4 + n + 5 + parts]
    normed, late, keyval, total, sems = refs[4 + n + 5 + parts :]
    at = pl.ds(sum(w.shape[0] for w in early), late.shape[0])
    copies = start_copies(query_weight.at[at], late, sems.at[0], 4)
    copies += start_copies(keyval_weight, keyval, sems.at[1], 1)
    rows = near[0].shape[0]
    half = far[0].shape[1]
    sums = sums_a[...] + sums_b[...]
    row_mean = sums[:, :1] / D
    row_square = sums[:, 1:2] / D
    scale = lax.rsqrt(row_square - row_mean * row_mean + epsilon)
    blocks = []

    def multiply(weights, part, start):
        cols = slice(part * half, (part + 1) * half)
        for weight in weights:
            term = lax.dot_general(
                blocks[part], weight[:, cols], contract, preferred_element_type=jnp.float32
            )
            stripe = slice(start, start + weight.shape[0])
            if part == 0:
                total[:, stripe] = term
            else:
                total[:, stripe] += term
            start = stripe.stop
        return start

    for part in range(2):
        cols = slice(part * half, (part + 1) * half)
        for i in range(n):
            at = slice(i * rows, (i + 1) * rows)
            x = near[i][:, cols] if i < n - 1 else far[part][...]
            x = (x.astype(jnp.float32) - row_mean[at]) * scale[at] * gain[:, cols]
            normed[at, cols] = x
        blocks.append(normed[:, cols].astype(jnp.bfloat16))
        done = multiply(early, part, 0)
    for copy in copies:
        copy.wait()
    for part in range(2):
        multiply([late, keyval], part, done)
    side = owners[n]
    local = rows // 2
    for i in range(n):
        block = total[i * rows : (i + 1) * rows, :]
        low, high = block[:local], block[local:]
        keep[owners[i]] = jnp.where(side == 0, low, high)
        give[owners[i]] = jnp.where(side == 0, high, low)


def project(n, owners, sums, gain, near, far, early, query_weight, keyval_weight):
    rows, width = near[0].shape
    late = (query_weight.shape[0] - sum(w.shape[0] for w in early), width)
    stripe = query_weight.shape[0] + keyval_weight.shape[0]
    shape = jax.ShapeDtypeStruct((n, rows // 2, stripe), jnp.float32)
    return pl.pallas_call(
        lambda *refs: project_kernel(n, len(early), *refs),
        out_shape=[shape, shape],
        in_specs=[IN_SMEM] + [IN_VMEM] * (3 + n + 1 + len(early)) + [IN_HBM] * 2,
        out_specs=[IN_VMEM] * 2,
        scratch_shapes=[
            pltpu.VMEM((n * rows, width), jnp.float32),
            pltpu.VMEM(late, jnp.bfloat16),
            pltpu.VMEM(keyval_weight.shape, jnp.bfloat16),
            pltpu.VMEM((n * rows, stripe), jnp.float32),
            pltpu.SemaphoreType.DMA((2, 4)),
        ],
        compiler_params=pltpu.CompilerParams(vmem_limit_bytes=(20 if n <= 8 else 44) * MIB),
        name="project",
    )(
        owners,
        *sums,
        gain,
        *near,
        *far,
        *[in_vmem(w) for w in early],
        in_hbm(query_weight),
        in_hbm(keyval_weight),
    )


def attend_kernel(scalars, queries, new_keys, new_values, keys, values, mine, other):
    rows, heads, _ = queries.shape
    side = scalars[rows]
    score_scale = 1.0 / math.sqrt(DH)
    for r in range(rows):
        q = queries[r]
        scores = lax.dot_general(q, keys[r], contract, preferred_element_type=jnp.float32)
        scores = scores * score_scale
        place = lax.broadcasted_iota(jnp.int32, scores.shape, 1)
        scores = jnp.where(place < scalars[r], scores, -1e30)
        new_key = new_keys[r : r + 1, :].astype(jnp.float32)
        own_score = jnp.sum(q.astype(jnp.float32) * new_key, axis=1, keepdims=True) * score_scale
        highest = jnp.maximum(jnp.max(scores, axis=1, keepdims=True), own_score)
        weights = jnp.exp(scores - highest)
        own_weight = jnp.exp(own_score - highest)
        totals = jnp.sum(weights, axis=1, keepdims=True) + own_weight
        blended = jnp.dot(
            weights.astype(jnp.bfloat16), values[r], preferred_element_type=jnp.float32
        )
        blended = (blended + own_weight * new_values[r : r + 1, :]) / totals
        low, high = blended[: heads // 2], blended[heads // 2 :]
        mine[r] = jnp.where(side == 0, low, high).astype(jnp.bfloat16)
        other[r] = jnp.where(side == 0, high, low).astype(jnp.bfloat16)


def attend(scalars, queries, new_keys, new_values, keys, values):
    rows, heads, _ = queries.shape
    shape = jax.ShapeDtypeStruct((rows, heads // 2, DH), jnp.bfloat16)
    return pl.pallas_call(
        attend_kernel,
        out_shape=[shape, shape],
        in_specs=[IN_SMEM] + [IN_VMEM] * 5,
        out_specs=[IN_VMEM] * 2,
        compiler_params=pltpu.CompilerParams(vmem_limit_bytes=6 * MIB),
        name="attend",
    )(scalars, queries, new_keys, new_values, in_vmem(keys), in_vmem(values))


def output_kernel(n, parts, *refs):
    owners = refs[0]
    near = refs[1:n]
    far = refs[n : n + 2]
    early = refs[n + 2 : n + 2 + parts]
    weight, keep, give, late, total, placed, sems = refs[n + 2 + parts :]
    first = sum(w.shape[0] for w in early)
    copies = start_copies(weight.at[pl.ds(first, late.shape[0])], late, sems, 4)
    rows = near[0].shape[0]
    x = [ref[...].astype(jnp.float32) for ref in near]
    x.append(jnp.concatenate([ref[...].astype(jnp.float32) for ref in far], axis=1))
    x = jnp.concatenate(x, axis=0).astype(jnp.bfloat16)
    start = 0
    for ref in early:
        stop = start + ref.shape[0]
        term = jnp.dot(x[:, start:stop], ref[...], preferred_element_type=jnp.float32)
        if start == 0:
            total[...] = term
        else:
            total[...] += term
        start = stop
    for copy in copies:
        copy.wait()
    total[...] += jnp.dot(x[:, first:], late[...], preferred_element_type=jnp.float32)
    for i in range(n):
        placed[owners[i]] = total[i * rows : (i + 1) * rows, :]
    side = owners[n]
    keep[...] = placed[pl.ds(side * (n // 2), n // 2)]
    give[...] = placed[pl.ds((1 - side) * (n // 2), n // 2)]


def output_project(n, owners, near, far, early, weight):
    rows = near[0].shape[0]
    depth, cols = weight.shape
    late = (depth - sum(w.shape[0] for w in early), cols)
    shape = jax.ShapeDtypeStruct((n // 2, rows, cols), jnp.float32)
    return pl.pallas_call(
        lambda *refs: output_kernel(n, len(early), *refs),
        out_shape=[shape, shape],
        in_specs=[IN_SMEM] + [IN_VMEM] * (n + 1 + len(early)) + [IN_HBM],
        out_specs=[IN_VMEM] * 2,
        scratch_shapes=[
            pltpu.VMEM(late, jnp.bfloat16),
            pltpu.VMEM((n * rows, cols), jnp.float32),
            pltpu.VMEM((n, rows, cols), jnp.float32),
            pltpu.SemaphoreType.DMA((4,)),
        ],
        compiler_params=pltpu.CompilerParams(vmem_limit_bytes=(18 if n <= 8 else 44) * MIB),
        name="output_project",
    )(owners, *near, *far, *[in_vmem(w) for w in early], in_hbm(weight))


def on_device(
    activations,
    norm_gain,
    query_weight,
    keyval_weight,
    output_weight,
    cache_keys,
    cache_values,
    cache_lengths,
):
    n = lax.axis_size("gx")
    ring = Ring(n)
    owners = ring.owners()
    query_cols = query_weight.shape[0]
    unit = query_cols // 96 * 16
    early = []

    left = right = activations
    near = [activations]
    for step in range(1, n // 2):
        after = near[1:][-2:]
        arrived = near[-2:] if step > 1 else None
        left, right = ring.step(left, right)
        near += [left, right]
        if step == 2:
            sums = row_sums([activations, *arrived])
            far_sums = lax.ppermute(sums[: activations.shape[0]], "gx", ring.across)
        elif step > 2:
            sums = row_sums(arrived, [sums])
        if step <= 3:
            first, size = [(0, 2), (2, 1), (3, 1)][step - 1]
            loaded = load([(query_weight, first * unit, size * unit)], after)
            loaded, (left, right) = before(loaded[0], left, right)
            near[-2:] = [left, right]
            early.append(loaded)
    half = activations.shape[1] // 2
    cut, (cut_right, left, right) = before(left[:, :half], right[:, half:], left, right)
    far = ring.step(cut, cut_right)
    sums = row_sums([left, right], [sums])
    sums = jnp.concatenate([sums, far_sums], axis=0)
    sums = (sums, swap_pair(sums))
    gain = norm_gain.astype(jnp.float32)[None, :]
    keep, give = project(
        n, owners, sums, gain, near, far, early, query_weight, keyval_weight
    )
    projected = (keep + swap_pair(give)).astype(jnp.bfloat16)
    local_rows = cache_lengths.shape[0]
    unit = output_weight.shape[0] // 96 * 16
    keys, values, loaded = load(
        [
            (cache_keys, 0, local_rows),
            (cache_values, 0, local_rows),
            (output_weight, 0, unit),
        ],
        [projected],
    )
    early = [loaded]
    gathered = lax.all_to_all(projected, "gx", split_axis=0, concat_axis=0, tiled=True)
    keys, (gathered,) = before(keys, gathered)
    gathered = jnp.swapaxes(gathered, 0, 1)
    queries = gathered[:, :, :query_cols].reshape(local_rows, HEADS, DH)
    keyvals = gathered[:, :, query_cols:].reshape(local_rows, 2 * DH)
    places = cache_lengths.astype(jnp.float32)
    queries = rotate(queries.astype(jnp.float32), places[:, None, None]).astype(jnp.bfloat16)
    new_keys = rotate(keyvals[:, :DH].astype(jnp.float32), places[:, None]).astype(jnp.bfloat16)
    new_values = keyvals[:, DH:].astype(jnp.float32)
    side = lax.axis_index("gy")
    scalars = jnp.concatenate([cache_lengths, side[None].astype(jnp.int32)])
    mine, other = attend(
        scalars, queries, new_keys, new_values, keys, values
    )
    mine = mine.reshape(local_rows, -1)
    other = swap_pair(other.reshape(local_rows, -1))
    first = jnp.where(side == 0, mine, other)
    second = jnp.where(side == 0, other, mine)
    swapped = jnp.concatenate([first, second], axis=0)

    left = right = swapped
    near = [swapped]
    for step in range(1, n // 2):
        after = near[-2:]
        left, right = ring.step(left, right)
        near += [left, right]
        if step <= 3:
            loaded = load([(output_weight, step * unit, unit)], after)
            loaded, (left, right) = before(loaded[0], left, right)
            near[-2:] = [left, right]
            early.append(loaded)
    half = swapped.shape[1] // 2
    far = ring.step(left[:, :half], right[:, half:])
    keep, give = output_project(n, owners, near, far, early, output_weight)
    out = (keep + swap_pair(give)).astype(jnp.bfloat16)
    return out.reshape(-1, out.shape[-1])


def solution(mesh):
    return jax.shard_map(
        on_device,
        mesh=mesh,
        in_specs=(
            P(("groups", "gx"), "gy"),
            P("gy"),
            P("gx", "gy"),
            P("gx", "gy"),
            P("gy", "gx"),
            P(("groups", "gx", "gy"), None, None),
            P(("groups", "gx", "gy"), None, None),
            P(("groups", "gx", "gy")),
        ),
        out_specs=P(("groups", "gy"), "gx"),
        check_vma=False,
    )
```

time: 144 us -> 108 us (0.75)
  local copies, waits for them, and re-layouts: 56.4 us -> 16.9 us
  Pallas kernels: 40.3 us -> 45 us
  waiting for transfers between devices: 18.8 us -> 16.7 us
    unnamed x32 -> x36, local copies, waits for them, and re-layouts: 56.2 us -> 16.6 us
    ppermute x8, waiting for transfers between devices: 12.7 us -> 6.04 us  [step(): lax.ppermute(left, 'gx', self.onward)]
    pallas_call x4 -> x7, Pallas kernels: 15.9 us -> 20.8 us  [load(): pl.pallas_call(lambda *refs: load_kernel([job[1:] for job in jobs], *refs...]
    ppermute x8, waiting for transfers between devices: 2.06 us -> 6.49 us  [step(): lax.ppermute(right, 'gx', self.back)]
    pallas_call x1, Pallas kernels: 6.47 us -> 3.35 us  [attend(): pl.pallas_call(attend_kernel, out_shape=[shape, shape], in_specs=[IN_SMEM...]
    pallas_call x6 -> x5, Pallas kernels: 17.9 us -> 20.8 us  [the longest x1 12.2 us: project(): pl.pallas_call(lambda *refs: project_kernel(n, len(early), *refs), out_sh...]
    ppermute x8, starting transfers between devices: 10.5 us -> 12.1 us  [step(): lax.ppermute(left, 'gx', self.onward)]
    ppermute x8, starting transfers between devices: 6.9 us -> 5.29 us  [step(): lax.ppermute(right, 'gx', self.back)]
  transfers between devices with their start and end apart: 22 -> 22, of which waited for: 9 -> 14; matrix products, arithmetic and copies ran while one was open for 0% -> 0% of each run, Pallas kernels for 11% -> 20%
where the time goes in v5:
time: 108 us
  Pallas kernels  45 us (42%)
  starting transfers between devices  26.9 us (25%)
  local copies, waits for them, and re-layouts  16.9 us (16%)
  waiting for transfers between devices  16.7 us (15%)
  other arithmetic  1.87 us (2%)
    pallas_call x7, Pallas kernels, load(): pl.pallas_call(lambda *refs: load_kernel([job[1:] for job in jobs], *refs...  20.8 us
    unnamed x36, local copies, waits for them, and re-layouts  16.6 us
    pallas_call x1, Pallas kernels, project(): pl.pallas_call(lambda *refs: project_kernel(n, len(early), *refs), out_sh...  12.2 us
    ppermute x8, starting transfers between devices, step(): lax.ppermute(left, 'gx', self.onward)  12.1 us
    pallas_call x1, Pallas kernels, output_project(): pl.pallas_call(lambda *refs: output_kernel(n, len(early), *refs), out_sha...  8 us
    ppermute x8, waiting for transfers between devices, step(): lax.ppermute(right, 'gx', self.back)  6.49 us
    ppermute x8, waiting for transfers between devices, step(): lax.ppermute(left, 'gx', self.onward)  6.04 us
    ppermute x8, starting transfers between devices, step(): lax.ppermute(right, 'gx', self.back)  5.29 us
  transfers between devices with their start and end apart: 22, of which 14 were waited for; matrix products, arithmetic and copies ran while one was open for 0% of the time, Pallas kernels for 20%

profile of v5, /device:TPU:0, one launch (start us, length us, event | category | flops | bytes accessed | tf_op | source)
XLA Modules:
  0.0 107.7 jit_solution(45254115742818912)
XLA Ops:
  0.0 3.0 %collective-permute-start = (bf16[8,9216]{1,0:T(8,128)(2,1)}, bf16[8,9216]{1,0:T(8,128)(2,1)S(1)}, u32[]{:S(2)}, u32[]{:S(2)}) collective-permute-start(bf16[8,9216]{1,0:T(8,128)(2,1)} %refs_4_.1), channel_id=1, source_target_pairs={{0,4},{4,8},{8,12},{12,14},{14,10},{10,6},{6,2},{2,0},{1,5},{5,9},... | collective-permute-start | bytes 442376 | tf_op jit(solution)/shard_map/ppermute | solution.py:68
  3.0 3.8 %load.7.refs_13_ = bf16[512,9216]{1,0:T(8,128)(2,1)S(1)} custom-call(bf16[1536,9216]{1,0:T(8,128)(2,1)} %refs_16_.1), custom_call_target="tpu_custom_call" | custom-call | tf_op jit(solution)/shard_map/load/pallas_call | solution.py:99
  6.8 3.6 %copy-done = bf16[512,9216]{1,0:T(8,128)(2,1)} copy-done((bf16[512,9216]{1,0:T(8,128)(2,1)}, bf16[512,9216]{1,0:T(8,128)(2,1)S(1)}, u32[]{:S(2)}) %copy-start) | copy-done | bytes 9437208
  10.5 2.0 %collective-permute-start.2 = (bf16[8,9216]{1,0:T(8,128)(2,1)S(1)}, bf16[8,9216]{1,0:T(8,128)(2,1)S(1)}, u32[]{:S(2)}, u32[]{:S(2)}) collective-permute-start(bf16[8,9216]{1,0:T(8,128)(2,1)S(1)} %collective-permute-done.refs_1_.refs_5_), channel_id=1, source_target_pairs={{0,4},{4,8},{8,12},{12,14},{14,10},{10,6},{6,2},{2,0},{1,5},{5,9},... | collective-permute-start | bytes 442376 | tf_op jit(solution)/shard_map/ppermute | solution.py:68
  12.5 2.4 %load.8.refs_14_ = bf16[256,9216]{1,0:T(8,128)(2,1)S(1)} custom-call(bf16[1536,9216]{1,0:T(8,128)(2,1)} %refs_16_.1, bf16[8,9216]{1,0:T(8,128)(2,1)S(1)} %collective-permute-done.refs_1_.refs_5_, bf16[8,9216]{1,0:T(8,128)(2,1)S(1)} %collective-permute-done.1.refs_2_.refs_6_), custom_call_target="tpu_custom_call" | custom-call | tf_op jit(solution)/shard_map/load/pallas_call | solution.py:99
  15.0 2.2 %copy-done.1 = bf16[256,9216]{1,0:T(8,128)(2,1)} copy-done((bf16[256,9216]{1,0:T(8,128)(2,1)}, bf16[256,9216]{1,0:T(8,128)(2,1)S(1)}, u32[]{:S(2)}) %copy-start.1) | copy-done | bytes 4718616
  17.2 0.2 row_sums.3.refs_0_
  17.4 5.0 %collective-permute-start.6 = (f32[8,128]{1,0:T(8,128)S(1)}, f32[8,128]{1,0:T(8,128)S(1)}, u32[]{:S(2)}, u32[]{:S(2)}) collective-permute-start(f32[8,128]{1,0:T(8,128)S(1)} %slice.52), channel_id=1, source_target_pairs={{0,14},{4,10},{8,6},{12,2},{14,0},{10,4},{6,8},{2,12},{1,15},{5,11... | collective-permute-start | bytes 12296 | tf_op jit(solution)/shard_map/ppermute | solution.py:353
  22.4 2.0 %collective-permute-start.5 = (bf16[8,9216]{1,0:T(8,128)(2,1)S(1)}, bf16[8,9216]{1,0:T(8,128)(2,1)S(1)}, u32[]{:S(2)}, u32[]{:S(2)}) collective-permute-start(bf16[8,9216]{1,0:T(8,128)(2,1)S(1)} %collective-permute-done.3.refs_2_.refs_8_), channel_id=1, source_target_pairs={{0,2},{4,0},{8,4},{12,8},{14,12},{10,14},{6,10},{2,6},{1,3},{5,1},... | collective-permute-start | bytes 442376 | tf_op jit(solution)/shard_map/ppermute | solution.py:68
  24.5 2.5 %load.9.refs_15_ = bf16[256,9216]{1,0:T(8,128)(2,1)S(1)} custom-call(bf16[1536,9216]{1,0:T(8,128)(2,1)} %refs_16_.1, bf16[8,9216]{1,0:T(8,128)(2,1)S(1)} %collective-permute-done.2.refs_1_.refs_7_, bf16[8,9216]{1,0:T(8,128)(2,1)S(1)} %collective-permute-done.3.refs_2_.refs_8_), custom_call_target="tpu_custom_call" | custom-call | tf_op jit(solution)/shard_map/load/pallas_call | solution.py:99
  27.1 0.2 row_sums.4.refs_0_
  27.2 0.3 collective-permute-done.4.refs_1_.refs_9_
  27.7 0.2 row_sums.5
  28.0 2.0 %collective-permute-start.9 = (bf16[8,4608]{1,0:T(8,128)(2,1)S(1)}, bf16[8,4608]{1,0:T(8,128)(2,1)S(1)}, u32[]{:S(2)}, u32[]{:S(2)}) collective-permute-start(bf16[8,4608]{1,0:T(8,128)(2,1)S(1)} %slice.40), channel_id=1, source_target_pairs={{0,2},{4,0},{8,4},{12,8},{14,12},{10,14},{6,10},{2,6},{1,3},{5,1},... | collective-permute-start | bytes 221192 | tf_op jit(solution)/shard_map/ppermute | solution.py:68
  30.1 2.7 %collective-permute-done.8.refs_11_ = bf16[8,4608]{1,0:T(8,128)(2,1)S(1)} collective-permute-done((bf16[8,4608]{1,0:T(8,128)(2,1)S(1)}, bf16[8,4608]{1,0:T(8,128)(2,1)S(1)}, u32[]{:S(2)}, u32[]{:S(2)}) %collective-permute-start.8) | collective-permute-done | bytes 73760 | tf_op jit(solution)/shard_map/ppermute | solution.py:68
  32.9 12.2 %project.1 = (f32[8,4,1600]{2,1,0:T(4,128)S(1)}, f32[8,4,1600]{2,1,0:T(4,128)S(1)}) custom-call(s32[9]{0:T(128)S(1)} %pad_add_fusion.refs_0_, f32[64,128]{1,0:T(8,128)S(1)} %pad_maximum_fusion.2.refs_1_, f32[64,128]{1,0:T(8,128)S(1)} %collective-permute-done.7.refs_2_, f32[1,9216]{1,0:T(1,128)S(1)} %bitcast.13, bf16[8,9216]{1,0:T(8,128)(2,1)S(1)} %copy-done.8, ...), custom_call_target="tpu_custom_call" | custom-call | tf_op jit(solution)/shard_map/project/pallas_call | solution.py:211
  45.2 1.4 %collective-permute-done.10 = f32[8,4,1600]{2,1,0:T(4,128)S(1)} collective-permute-done((f32[8,4,1600]{2,1,0:T(4,128)S(1)}, f32[8,4,1600]{2,1,0:T(4,128)S(1)}, u32[]{:S(2)}, u32[]{:S(2)}) %collective-permute-start.10) | collective-permute-done | bytes 204832 | tf_op jit(solution)/shard_map/ppermute | solution.py:44
  46.6 0.7 add_convert_fusion.1.refs_3_
  47.3 4.2 %all-to-all-start = ((bf16[8,4,1600]{2,1,0:T(4,128)(2,1)}), bf16[8,4,1600]{2,1,0:T(4,128)(2,1)S(1)}, u32[]{:S(2)}, u32[]{:S(2)}) async-start(bf16[8,4,1600]{2,1,0:T(4,128)(2,1)} %add_convert_fusion.1.refs_3_), calls=%async_computation | async-start | bytes 212992 | tf_op jit(solution)/shard_map/all_to_all | solution.py:384
  51.6 4.9 %load.10 = (bf16[4,2048,256]{2,1,0:T(8,128)(2,1)S(1)}, bf16[4,2048,256]{2,1,0:T(8,128)(2,1)S(1)}, bf16[1024,2304]{1,0:T(8,128)(2,1)S(1)}) custom-call(bf16[4,2048,256]{2,1,0:T(8,128)(2,1)} %refs_0_.12, bf16[4,2048,256]{2,1,0:T(8,128)(2,1)} %refs_1_.1, bf16[6144,2304]{1,0:T(8,128)(2,1)} %refs_14_.1, bf16[8,4,1600]{2,1,0:T(4,128)(2,1)} %add_convert_fusion.1.refs_3_), custom_call_target="tpu_custom_call" | custom-call | tf_op jit(solution)/shard_map/load/pallas_call | solution.py:99
  56.5 2.2 %copy-done.3 = bf16[1024,2304]{1,0:T(8,128)(2,1)} copy-done((bf16[1024,2304]{1,0:T(8,128)(2,1)}, bf16[1024,2304]{1,0:T(8,128)(2,1)S(1)}, u32[]{:S(2)}) %copy-start.3) | copy-done | bytes 4718616
  58.6 2.0 %copy-done.4 = bf16[4,2048,256]{2,1,0:T(8,128)(2,1)} copy-done((bf16[4,2048,256]{2,1,0:T(8,128)(2,1)}, bf16[4,2048,256]{2,1,0:T(8,128)(2,1)S(1)}, u32[]{:S(2)}) %copy-start.4) | copy-done | bytes 4194328
  60.7 2.1 %copy-done.6 = bf16[4,2048,256]{2,1,0:T(8,128)(2,1)} copy-done((bf16[4,2048,256]{2,1,0:T(8,128)(2,1)}, bf16[4,2048,256]{2,1,0:T(8,128)(2,1)S(1)}, u32[]{:S(2)}) %copy-start.6) | copy-done | bytes 4194328
  62.8 0.1 reshape.80
  63.0 0.1 subtract_convert_fusion.1
  63.2 2.2 %copy-done.5 = bf16[4,2048,256]{2,1,0:T(8,128)(2,1)S(1)} copy-done((bf16[4,2048,256]{2,1,0:T(8,128)(2,1)S(1)}, bf16[4,2048,256]{2,1,0:T(8,128)(2,1)}, u32[]{:S(2)}) %copy-start.5) | copy-done | bytes 4194328
  65.4 2.2 %copy-done.7 = bf16[4,2048,256]{2,1,0:T(8,128)(2,1)S(1)} copy-done((bf16[4,2048,256]{2,1,0:T(8,128)(2,1)S(1)}, bf16[4,2048,256]{2,1,0:T(8,128)(2,1)}, u32[]{:S(2)}) %copy-start.7) | copy-done | bytes 4194328
  67.6 3.3 %attend.1 = (bf16[4,24,256]{2,1,0:T(8,128)(2,1)S(1)}, bf16[4,24,256]{2,1,0:T(8,128)(2,1)S(1)}) custom-call(s32[5]{0:T(128)S(1)} %pad_add_fusion.1.scalars, bf16[4,48,256]{2,1,0:T(8,128)(2,1)S(1)} %pad_maximum_fusion.queries, bf16[4,256]{1,0:T(4,128)(2,1)S(1)} %pad_maximum_fusion.3.new_keys, f32[4,256]{1,0:T(4,128)S(1)} %get-tuple-element.77.new_values, ...), custom_call_target="tpu_custom_call" | custom-call | tf_op jit(solution)/shard_map/attend/pallas_call | solution.py:265
  71.1 1.2 %collective-permute-done.11 = bf16[4,6144]{1,0:T(4,128)(2,1)S(1)} collective-permute-done((bf16[4,6144]{1,0:T(4,128)(2,1)S(1)}, bf16[4,6144]{1,0:T(4,128)(2,1)S(1)}, u32[]{:S(2)}, u32[]{:S(2)}) %collective-permute-start.11) | collective-permute-done | bytes 49184 | tf_op jit(solution)/shard_map/ppermute | solution.py:44
  72.4 2.1 %collective-permute-start.12 = (bf16[8,6144]{1,0:T(8,128)(2,1)S(1)}, bf16[8,6144]{1,0:T(8,128)(2,1)S(1)}, u32[]{:S(2)}, u32[]{:S(2)}) collective-permute-start(bf16[8,6144]{1,0:T(8,128)(2,1)S(1)} %pad_maximum_fusion.1.refs_1_), channel_id=1, source_target_pairs={{0,4},{4,8},{8,12},{12,14},{14,10},{10,6},{6,2},{2,0},{1,5},{5,9},... | collective-permute-start | bytes 294920 | tf_op jit(solution)/shard_map/ppermute | solution.py:68
  74.5 2.4 %load.11.refs_11_ = bf16[1024,2304]{1,0:T(8,128)(2,1)S(1)} custom-call(bf16[6144,2304]{1,0:T(8,128)(2,1)} %refs_14_.1, bf16[8,6144]{1,0:T(8,128)(2,1)S(1)} %pad_maximum_fusion.1.refs_1_), custom_call_target="tpu_custom_call" | custom-call | tf_op jit(solution)/shard_map/load/pallas_call | solution.py:99
  76.9 0.7 collective-permute-done.12.refs_1_.refs_2_
  77.6 1.5 %collective-permute-done.13.refs_2_.refs_3_ = bf16[8,6144]{1,0:T(8,128)(2,1)S(1)} collective-permute-done((bf16[8,6144]{1,0:T(8,128)(2,1)S(1)}, bf16[8,6144]{1,0:T(8,128)(2,1)S(1)}, u32[]{:S(2)}, u32[]{:S(2)}) %collective-permute-start.13) | collective-permute-done | bytes 98336 | tf_op jit(solution)/shard_map/ppermute | solution.py:68
  79.1 1.5 %collective-permute-start.14 = (bf16[8,6144]{1,0:T(8,128)(2,1)S(1)}, bf16[8,6144]{1,0:T(8,128)(2,1)S(1)}, u32[]{:S(2)}, u32[]{:S(2)}) collective-permute-start(bf16[8,6144]{1,0:T(8,128)(2,1)S(1)} %collective-permute-done.12.refs_1_.refs_2_), channel_id=1, source_target_pairs={{0,4},{4,8},{8,12},{12,14},{14,10},{10,6},{6,2},{2,0},{1,5},{5,9},... | collective-permute-start | bytes 294920 | tf_op jit(solution)/shard_map/ppermute | solution.py:68
  80.5 0.6 collective-permute-start.15
  81.1 2.5 %load.12.refs_12_ = bf16[1024,2304]{1,0:T(8,128)(2,1)S(1)} custom-call(bf16[6144,2304]{1,0:T(8,128)(2,1)} %refs_14_.1, bf16[8,6144]{1,0:T(8,128)(2,1)S(1)} %collective-permute-done.12.refs_1_.refs_2_, bf16[8,6144]{1,0:T(8,128)(2,1)S(1)} %collective-permute-done.13.refs_2_.refs_3_), custom_call_target="tpu_custom_call" | custom-call | tf_op jit(solution)/shard_map/load/pallas_call | solution.py:99
  83.7 1.5 %collective-permute-done.15.refs_2_.refs_5_ = bf16[8,6144]{1,0:T(8,128)(2,1)S(1)} collective-permute-done((bf16[8,6144]{1,0:T(8,128)(2,1)S(1)}, bf16[8,6144]{1,0:T(8,128)(2,1)S(1)}, u32[]{:S(2)}, u32[]{:S(2)}) %collective-permute-start.15) | collective-permute-done | bytes 98336 | tf_op jit(solution)/shard_map/ppermute | solution.py:68
  85.2 1.5 %collective-permute-start.16 = (bf16[8,6144]{1,0:T(8,128)(2,1)S(1)}, bf16[8,6144]{1,0:T(8,128)(2,1)S(1)}, u32[]{:S(2)}, u32[]{:S(2)}) collective-permute-start(bf16[8,6144]{1,0:T(8,128)(2,1)S(1)} %collective-permute-done.14.refs_1_.refs_4_), channel_id=1, source_target_pairs={{0,4},{4,8},{8,12},{12,14},{14,10},{10,6},{6,2},{2,0},{1,5},{5,9},... | collective-permute-start | bytes 294920 | tf_op jit(solution)/shard_map/ppermute | solution.py:68
  86.6 0.6 collective-permute-start.17
  87.2 2.4 %load.13.refs_13_ = bf16[1024,2304]{1,0:T(8,128)(2,1)S(1)} custom-call(bf16[6144,2304]{1,0:T(8,128)(2,1)} %refs_14_.1, bf16[8,6144]{1,0:T(8,128)(2,1)S(1)} %collective-permute-done.14.refs_1_.refs_4_, bf16[8,6144]{1,0:T(8,128)(2,1)S(1)} %collective-permute-done.15.refs_2_.refs_5_), custom_call_target="tpu_custom_call" | custom-call | tf_op jit(solution)/shard_map/load/pallas_call | solution.py:99
  89.6 0.2 collective-permute-done.16.refs_6_
  89.8 1.5 %collective-permute-done.17.refs_7_ = bf16[8,6144]{1,0:T(8,128)(2,1)S(1)} collective-permute-done((bf16[8,6144]{1,0:T(8,128)(2,1)S(1)}, bf16[8,6144]{1,0:T(8,128)(2,1)S(1)}, u32[]{:S(2)}, u32[]{:S(2)}) %collective-permute-start.17) | collective-permute-done | bytes 98336 | tf_op jit(solution)/shard_map/ppermute | solution.py:68
  91.3 2.0 %collective-permute-start.18 = (bf16[8,3072]{1,0:T(8,128)(2,1)S(1)}, bf16[8,3072]{1,0:T(8,128)(2,1)S(1)}, u32[]{:S(2)}, u32[]{:S(2)}) collective-permute-start(bf16[8,3072]{1,0:T(8,128)(2,1)S(1)} %slice.50), channel_id=1, source_target_pairs={{0,4},{4,8},{8,12},{12,14},{14,10},{10,6},{6,2},{2,0},{1,5},{5,9},... | collective-permute-start | bytes 147464 | tf_op jit(solution)/shard_map/ppermute | solution.py:68
  93.3 2.1 %collective-permute-done.18.refs_8_ = bf16[8,3072]{1,0:T(8,128)(2,1)S(1)} collective-permute-done((bf16[8,3072]{1,0:T(8,128)(2,1)S(1)}, bf16[8,3072]{1,0:T(8,128)(2,1)S(1)}, u32[]{:S(2)}, u32[]{:S(2)}) %collective-permute-start.18) | collective-permute-done | bytes 49184 | tf_op jit(solution)/shard_map/ppermute | solution.py:68
  95.3 2.0 %collective-permute-done.19.refs_9_ = bf16[8,3072]{1,0:T(8,128)(2,1)S(1)} collective-permute-done((bf16[8,3072]{1,0:T(8,128)(2,1)S(1)}, bf16[8,3072]{1,0:T(8,128)(2,1)S(1)}, u32[]{:S(2)}, u32[]{:S(2)}) %collective-permute-start.19) | collective-permute-done | bytes 49184 | tf_op jit(solution)/shard_map/ppermute | solution.py:68
  97.3 8.0 %output_project.1 = (f32[4,8,2304]{2,1,0:T(8,128)S(1)}, f32[4,8,2304]{2,1,0:T(8,128)S(1)}) custom-call(s32[9]{0:T(128)S(1)} %pad_add_fusion.refs_0_, bf16[8,6144]{1,0:T(8,128)(2,1)S(1)} %pad_maximum_fusion.1.refs_1_, bf16[8,6144]{1,0:T(8,128)(2,1)S(1)} %collective-permute-done.12.refs_1_.refs_2_, ...), custom_call_target="tpu_custom_call" | custom-call | tf_op jit(solution)/shard_map/output_project/pallas_call | solution.py:311
  105.4 1.6 %collective-permute-done.20 = f32[4,8,2304]{2,1,0:T(8,128)S(1)} collective-permute-done((f32[4,8,2304]{2,1,0:T(8,128)S(1)}, f32[4,8,2304]{2,1,0:T(8,128)S(1)}, u32[]{:S(2)}, u32[]{:S(2)}) %collective-permute-start.20) | collective-permute-done | bytes 294944 | tf_op jit(solution)/shard_map/ppermute | solution.py:44
  107.0 0.7 fusion
  (74 shorter events, 1.2 us)
Async XLA Ops:
  0.0 10.5 %collective-permute-start = (bf16[8,9216]{1,0:T(8,128)(2,1)}, bf16[8,9216]{1,0:T(8,128)(2,1)S(1)}, u32[]{:S(2)}, u32[]{:S(2)}) collective-permute-start(bf16[8,9216]{1,0:T(8,128)(2,1)} %refs_4_.1), channel_id=1, source_target_pairs={{0,4},{4,8},{8,12},{12,14},{14,10},{10,6},{6,2},{2,0},{1,5},{5,9},... | collective-permute-start | bytes 442376 | tf_op jit(solution)/shard_map/ppermute | solution.py:68
  3.0 7.5 %collective-permute-start.1 = (bf16[8,9216]{1,0:T(8,128)(2,1)}, bf16[8,9216]{1,0:T(8,128)(2,1)S(1)}, u32[]{:S(2)}, u32[]{:S(2)}) collective-permute-start(bf16[8,9216]{1,0:T(8,128)(2,1)} %refs_4_.1), channel_id=1, source_target_pairs={{0,2},{4,0},{8,4},{12,8},{14,12},{10,14},{6,10},{2,6},{1,3},{5,1},... | collective-permute-start | bytes 442376 | tf_op jit(solution)/shard_map/ppermute | solution.py:68
  6.8 3.7 %copy-start = (bf16[512,9216]{1,0:T(8,128)(2,1)}, bf16[512,9216]{1,0:T(8,128)(2,1)S(1)}, u32[]{:S(2)}) copy-start(bf16[512,9216]{1,0:T(8,128)(2,1)S(1)} %load.7.refs_13_) | copy-start | bytes 28311556
  10.5 11.9 %collective-permute-start.2 = (bf16[8,9216]{1,0:T(8,128)(2,1)S(1)}, bf16[8,9216]{1,0:T(8,128)(2,1)S(1)}, u32[]{:S(2)}, u32[]{:S(2)}) collective-permute-start(bf16[8,9216]{1,0:T(8,128)(2,1)S(1)} %collective-permute-done.refs_1_.refs_5_), channel_id=1, source_target_pairs={{0,4},{4,8},{8,12},{12,14},{14,10},{10,6},{6,2},{2,0},{1,5},{5,9},... | collective-permute-start | bytes 442376 | tf_op jit(solution)/shard_map/ppermute | solution.py:68
  12.5 9.9 %collective-permute-start.3 = (bf16[8,9216]{1,0:T(8,128)(2,1)S(1)}, bf16[8,9216]{1,0:T(8,128)(2,1)S(1)}, u32[]{:S(2)}, u32[]{:S(2)}) collective-permute-start(bf16[8,9216]{1,0:T(8,128)(2,1)S(1)} %collective-permute-done.1.refs_2_.refs_6_), channel_id=1, source_target_pairs={{0,2},{4,0},{8,4},{12,8},{14,12},{10,14},{6,10},{2,6},{1,3},{5,1},... | collective-permute-start | bytes 442376 | tf_op jit(solution)/shard_map/ppermute | solution.py:68
  12.5 4.7 %copy-start.8 = (bf16[8,9216]{1,0:T(8,128)(2,1)S(1)}, bf16[8,9216]{1,0:T(8,128)(2,1)}, u32[]{:S(2)}) copy-start(bf16[8,9216]{1,0:T(8,128)(2,1)} %refs_4_.1) | copy-start | bytes 442372
  12.5 11.9 %copy-start.11 = (s32[8]{0:T(128)S(1)}, s32[8]{0:T(128)}, u32[]{:S(2)}) copy-start(s32[8]{0:T(128)} %constant.64.clone) | copy-start | bytes 100
  14.9 2.2 %copy-start.1 = (bf16[256,9216]{1,0:T(8,128)(2,1)}, bf16[256,9216]{1,0:T(8,128)(2,1)S(1)}, u32[]{:S(2)}) copy-start(bf16[256,9216]{1,0:T(8,128)(2,1)S(1)} %load.8.refs_14_) | copy-start | bytes 14155780
  17.4 10.4 %collective-permute-start.6 = (f32[8,128]{1,0:T(8,128)S(1)}, f32[8,128]{1,0:T(8,128)S(1)}, u32[]{:S(2)}, u32[]{:S(2)}) collective-permute-start(f32[8,128]{1,0:T(8,128)S(1)} %slice.52), channel_id=1, source_target_pairs={{0,14},{4,10},{8,6},{12,2},{14,0},{10,4},{6,8},{2,12},{1,15},{5,11... | collective-permute-start | bytes 12296 | tf_op jit(solution)/shard_map/ppermute | solution.py:353
  22.4 5.1 %collective-permute-start.4 = (bf16[8,9216]{1,0:T(8,128)(2,1)S(1)}, bf16[8,9216]{1,0:T(8,128)(2,1)S(1)}, u32[]{:S(2)}, u32[]{:S(2)}) collective-permute-start(bf16[8,9216]{1,0:T(8,128)(2,1)S(1)} %collective-permute-done.2.refs_1_.refs_7_), channel_id=1, source_target_pairs={{0,4},{4,8},{8,12},{12,14},{14,10},{10,6},{6,2},{2,0},{1,5},{5,9},... | collective-permute-start | bytes 442376 | tf_op jit(solution)/shard_map/ppermute | solution.py:68
  22.4 5.2 %collective-permute-start.5 = (bf16[8,9216]{1,0:T(8,128)(2,1)S(1)}, bf16[8,9216]{1,0:T(8,128)(2,1)S(1)}, u32[]{:S(2)}, u32[]{:S(2)}) collective-permute-start(bf16[8,9216]{1,0:T(8,128)(2,1)S(1)} %collective-permute-done.3.refs_2_.refs_8_), channel_id=1, source_target_pairs={{0,2},{4,0},{8,4},{12,8},{14,12},{10,14},{6,10},{2,6},{1,3},{5,1},... | collective-permute-start | bytes 442376 | tf_op jit(solution)/shard_map/ppermute | solution.py:68
  24.5 8.3 %slice-start = ((s8[9437184]{0:T(1024)(128)(4,1)}), s8[1048576]{0:T(1024)(128)(4,1)S(1)}, s32[]{:S(2)}) async-start(s8[9437184]{0:T(1024)(128)(4,1)} %bitcast.9), calls=%async_computation.1 | async-start | bytes 2097152
  24.5 5.6 %copy-start.9 = (bf16[9216]{0:T(1024)(128)(2,1)S(1)}, bf16[9216]{0:T(1024)(128)(2,1)}, u32[]{:S(2)}) copy-start(bf16[9216]{0:T(1024)(128)(2,1)} %param.10) | copy-start | bytes 55300
  24.5 8.3 %slice-start.1 = ((s8[9437184]{0:T(1024)(128)(4,1)}), s8[4194304]{0:T(1024)(128)(4,1)S(1)}, s32[]{:S(2)}) async-start(s8[9437184]{0:T(1024)(128)(4,1)} %bitcast.9), calls=%async_computation.2 | async-start | bytes 8388608
  24.5 8.3 %slice-start.2 = ((s8[9437184]{0:T(1024)(128)(4,1)}), s8[4194304]{0:T(1024)(128)(4,1)S(1)}, s32[]{:S(2)}) async-start(s8[9437184]{0:T(1024)(128)(4,1)} %bitcast.9), calls=%async_computation.3 | async-start | bytes 8388608
  24.5 8.3 %copy-start.2 = (bf16[256,9216]{1,0:T(8,128)(2,1)S(1)}, bf16[256,9216]{1,0:T(8,128)(2,1)}, u32[]{:S(2)}) copy-start(bf16[256,9216]{1,0:T(8,128)(2,1)} %copy-done.1) | copy-start | bytes 14155780
  27.8 2.3 %collective-permute-start.7 = (f32[64,128]{1,0:T(8,128)S(1)}, f32[64,128]{1,0:T(8,128)S(1)}, u32[]{:S(2)}, u32[]{:S(2)}) collective-permute-start(f32[64,128]{1,0:T(8,128)S(1)} %pad_maximum_fusion.2.refs_1_), channel_id=1, source_target_pairs={{0,1},{1,0},{2,3},{3,2},{4,5},{5,4},{6,7},{7,6},{8,9},{9,8},{10,11... | collective-permute-start | bytes 98312 | tf_op jit(solution)/shard_map/ppermute | solution.py:44
  27.9 4.9 %collective-permute-start.8 = (bf16[8,4608]{1,0:T(8,128)(2,1)S(1)}, bf16[8,4608]{1,0:T(8,128)(2,1)S(1)}, u32[]{:S(2)}, u32[]{:S(2)}) collective-permute-start(bf16[8,4608]{1,0:T(8,128)(2,1)S(1)} %slice.39), channel_id=1, source_target_pairs={{0,4},{4,8},{8,12},{12,14},{14,10},{10,6},{6,2},{2,0},{1,5},{5,9},... | collective-permute-start | bytes 221192 | tf_op jit(solution)/shard_map/ppermute | solution.py:68
  28.0 4.8 %collective-permute-start.9 = (bf16[8,4608]{1,0:T(8,128)(2,1)S(1)}, bf16[8,4608]{1,0:T(8,128)(2,1)S(1)}, u32[]{:S(2)}, u32[]{:S(2)}) collective-permute-start(bf16[8,4608]{1,0:T(8,128)(2,1)S(1)} %slice.40), channel_id=1, source_target_pairs={{0,2},{4,0},{8,4},{12,8},{14,12},{10,14},{6,10},{2,6},{1,3},{5,1},... | collective-permute-start | bytes 221192 | tf_op jit(solution)/shard_map/ppermute | solution.py:68
  32.8 12.3 %copy-start.10 = (s32[4]{0:T(128)S(1)}, s32[4]{0:T(128)}, u32[]{:S(2)}) copy-start(s32[4]{0:T(128)} %param.16) | copy-start | bytes 52
  45.1 1.5 %collective-permute-start.10 = (f32[8,4,1600]{2,1,0:T(4,128)S(1)}, f32[8,4,1600]{2,1,0:T(4,128)S(1)}, u32[]{:S(2)}, u32[]{:S(2)}) collective-permute-start(f32[8,4,1600]{2,1,0:T(4,128)S(1)} %get-tuple-element.52), channel_id=1, source_target_pairs={{0,1},{1,0},{2,3},{3,2},{4,5},{5,4},{6,7},{7,6},{8,9},{9,8},{10,11... | collective-permute-start | bytes 614408 | tf_op jit(solution)/shard_map/ppermute | solution.py:44
  47.3 15.5 %all-to-all-start = ((bf16[8,4,1600]{2,1,0:T(4,128)(2,1)}), bf16[8,4,1600]{2,1,0:T(4,128)(2,1)S(1)}, u32[]{:S(2)}, u32[]{:S(2)}) async-start(bf16[8,4,1600]{2,1,0:T(4,128)(2,1)} %add_convert_fusion.1.refs_3_), calls=%async_computation | async-start | bytes 212992 | tf_op jit(solution)/shard_map/all_to_all | solution.py:384
  56.5 2.2 %copy-start.3 = (bf16[1024,2304]{1,0:T(8,128)(2,1)}, bf16[1024,2304]{1,0:T(8,128)(2,1)S(1)}, u32[]{:S(2)}) copy-start(bf16[1024,2304]{1,0:T(8,128)(2,1)S(1)} %get-tuple-element.65.refs_10_) | copy-start | bytes 14155780
  58.6 2.0 %copy-start.4 = (bf16[4,2048,256]{2,1,0:T(8,128)(2,1)}, bf16[4,2048,256]{2,1,0:T(8,128)(2,1)S(1)}, u32[]{:S(2)}) copy-start(bf16[4,2048,256]{2,1,0:T(8,128)(2,1)S(1)} %get-tuple-element.55.keys) | copy-start | bytes 12582916
  60.7 2.1 %copy-start.6 = (bf16[4,2048,256]{2,1,0:T(8,128)(2,1)}, bf16[4,2048,256]{2,1,0:T(8,128)(2,1)S(1)}, u32[]{:S(2)}) copy-start(bf16[4,2048,256]{2,1,0:T(8,128)(2,1)S(1)} %get-tuple-element.56.values) | copy-start | bytes 12582916
  63.2 2.2 %copy-start.5 = (bf16[4,2048,256]{2,1,0:T(8,128)(2,1)S(1)}, bf16[4,2048,256]{2,1,0:T(8,128)(2,1)}, u32[]{:S(2)}) copy-start(bf16[4,2048,256]{2,1,0:T(8,128)(2,1)} %copy-done.4) | copy-start | bytes 12582916
  65.4 2.2 %copy-start.7 = (bf16[4,2048,256]{2,1,0:T(8,128)(2,1)S(1)}, bf16[4,2048,256]{2,1,0:T(8,128)(2,1)}, u32[]{:S(2)}) copy-start(bf16[4,2048,256]{2,1,0:T(8,128)(2,1)} %copy-done.6) | copy-start | bytes 12582916
  71.0 1.3 %collective-permute-start.11 = (bf16[4,6144]{1,0:T(4,128)(2,1)S(1)}, bf16[4,6144]{1,0:T(4,128)(2,1)S(1)}, u32[]{:S(2)}, u32[]{:S(2)}) collective-permute-start(bf16[4,6144]{1,0:T(4,128)(2,1)S(1)} %bitcast.19), channel_id=1, source_target_pairs={{0,1},{1,0},{2,3},{3,2},{4,5},{5,4},{6,7},{7,6},{8,9},{9,8},{10,11... | collective-permute-start | bytes 147464 | tf_op jit(solution)/shard_map/ppermute | solution.py:44
  72.4 5.2 %collective-permute-start.12 = (bf16[8,6144]{1,0:T(8,128)(2,1)S(1)}, bf16[8,6144]{1,0:T(8,128)(2,1)S(1)}, u32[]{:S(2)}, u32[]{:S(2)}) collective-permute-start(bf16[8,6144]{1,0:T(8,128)(2,1)S(1)} %pad_maximum_fusion.1.refs_1_), channel_id=1, source_target_pairs={{0,4},{4,8},{8,12},{12,14},{14,10},{10,6},{6,2},{2,0},{1,5},{5,9},... | collective-permute-start | bytes 294920 | tf_op jit(solution)/shard_map/ppermute | solution.py:68
  74.5 4.6 %collective-permute-start.13 = (bf16[8,6144]{1,0:T(8,128)(2,1)S(1)}, bf16[8,6144]{1,0:T(8,128)(2,1)S(1)}, u32[]{:S(2)}, u32[]{:S(2)}) collective-permute-start(bf16[8,6144]{1,0:T(8,128)(2,1)S(1)} %pad_maximum_fusion.1.refs_1_), channel_id=1, source_target_pairs={{0,2},{4,0},{8,4},{12,8},{14,12},{10,14},{6,10},{2,6},{1,3},{5,1},... | collective-permute-start | bytes 294920 | tf_op jit(solution)/shard_map/ppermute | solution.py:68
  79.1 4.6 %collective-permute-start.14 = (bf16[8,6144]{1,0:T(8,128)(2,1)S(1)}, bf16[8,6144]{1,0:T(8,128)(2,1)S(1)}, u32[]{:S(2)}, u32[]{:S(2)}) collective-permute-start(bf16[8,6144]{1,0:T(8,128)(2,1)S(1)} %collective-permute-done.12.refs_1_.refs_2_), channel_id=1, source_target_pairs={{0,4},{4,8},{8,12},{12,14},{14,10},{10,6},{6,2},{2,0},{1,5},{5,9},... | collective-permute-start | bytes 294920 | tf_op jit(solution)/shard_map/ppermute | solution.py:68
  80.5 4.6 %collective-permute-start.15 = (bf16[8,6144]{1,0:T(8,128)(2,1)S(1)}, bf16[8,6144]{1,0:T(8,128)(2,1)S(1)}, u32[]{:S(2)}, u32[]{:S(2)}) collective-permute-start(bf16[8,6144]{1,0:T(8,128)(2,1)S(1)} %collective-permute-done.13.refs_2_.refs_3_), channel_id=1, source_target_pairs={{0,2},{4,0},{8,4},{12,8},{14,12},{10,14},{6,10},{2,6},{1,3},{5,1},... | collective-permute-start | bytes 294920 | tf_op jit(solution)/shard_map/ppermute | solution.py:68
  81.1 16.2 %slice-start.3 = ((s8[4718592]{0:T(1024)(128)(4,1)}), s8[4194304]{0:T(1024)(128)(4,1)S(1)}, s32[]{:S(2)}) async-start(s8[4718592]{0:T(1024)(128)(4,1)} %bitcast.11), calls=%async_computation.4 | async-start | bytes 8388608
  83.6 13.7 %slice-start.4 = ((s8[4718592]{0:T(1024)(128)(4,1)}), s8[524288]{0:T(1024)(128)(4,1)S(1)}, s32[]{:S(2)}) async-start(s8[4718592]{0:T(1024)(128)(4,1)} %bitcast.11), calls=%async_computation.5 | async-start | bytes 1048576
  85.2 4.6 %collective-permute-start.16 = (bf16[8,6144]{1,0:T(8,128)(2,1)S(1)}, bf16[8,6144]{1,0:T(8,128)(2,1)S(1)}, u32[]{:S(2)}, u32[]{:S(2)}) collective-permute-start(bf16[8,6144]{1,0:T(8,128)(2,1)S(1)} %collective-permute-done.14.refs_1_.refs_4_), channel_id=1, source_target_pairs={{0,4},{4,8},{8,12},{12,14},{14,10},{10,6},{6,2},{2,0},{1,5},{5,9},... | collective-permute-start | bytes 294920 | tf_op jit(solution)/shard_map/ppermute | solution.py:68
  86.6 4.6 %collective-permute-start.17 = (bf16[8,6144]{1,0:T(8,128)(2,1)S(1)}, bf16[8,6144]{1,0:T(8,128)(2,1)S(1)}, u32[]{:S(2)}, u32[]{:S(2)}) collective-permute-start(bf16[8,6144]{1,0:T(8,128)(2,1)S(1)} %collective-permute-done.15.refs_2_.refs_5_), channel_id=1, source_target_pairs={{0,2},{4,0},{8,4},{12,8},{14,12},{10,14},{6,10},{2,6},{1,3},{5,1},... | collective-permute-start | bytes 294920 | tf_op jit(solution)/shard_map/ppermute | solution.py:68
  91.3 4.1 %collective-permute-start.18 = (bf16[8,3072]{1,0:T(8,128)(2,1)S(1)}, bf16[8,3072]{1,0:T(8,128)(2,1)S(1)}, u32[]{:S(2)}, u32[]{:S(2)}) collective-permute-start(bf16[8,3072]{1,0:T(8,128)(2,1)S(1)} %slice.50), channel_id=1, source_target_pairs={{0,4},{4,8},{8,12},{12,14},{14,10},{10,6},{6,2},{2,0},{1,5},{5,9},... | collective-permute-start | bytes 147464 | tf_op jit(solution)/shard_map/ppermute | solution.py:68
  93.2 4.1 %collective-permute-start.19 = (bf16[8,3072]{1,0:T(8,128)(2,1)S(1)}, bf16[8,3072]{1,0:T(8,128)(2,1)S(1)}, u32[]{:S(2)}, u32[]{:S(2)}) collective-permute-start(bf16[8,3072]{1,0:T(8,128)(2,1)S(1)} %slice.51), channel_id=1, source_target_pairs={{0,2},{4,0},{8,4},{12,8},{14,12},{10,14},{6,10},{2,6},{1,3},{5,1},... | collective-permute-start | bytes 147464 | tf_op jit(solution)/shard_map/ppermute | solution.py:68
  105.4 1.6 %collective-permute-start.20 = (f32[4,8,2304]{2,1,0:T(8,128)S(1)}, f32[4,8,2304]{2,1,0:T(8,128)S(1)}, u32[]{:S(2)}, u32[]{:S(2)}) collective-permute-start(f32[4,8,2304]{2,1,0:T(8,128)S(1)} %get-tuple-element.70), channel_id=1, source_target_pairs={{0,1},{1,0},{2,3},{3,2},{4,5},{5,4},{6,7},{7,6},{8,9},{9,8},{10,11... | collective-permute-start | bytes 884744 | tf_op jit(solution)/shard_map/ppermute | solution.py:44

commit v6 on v0

--- a/solution.py
+++ b/solution.py
@@ -3,6 +3,8 @@
 import jax
 import jax.numpy as jnp
 from jax import lax
+from jax.experimental import pallas as pl
+from jax.experimental.pallas import tpu as pltpu
 from jax.sharding import PartitionSpec as P
 
 D = 18432
@@ -12,6 +14,11 @@
 
 epsilon = 1e-06
 contract = (((1,), (1,)), ((), ()))
+MIB = 1 << 20
+ANY = pl.BlockSpec(memory_space=pl.ANY)
+IN_HBM = pl.BlockSpec(memory_space=pltpu.HBM)
+IN_VMEM = pl.BlockSpec(memory_space=pltpu.VMEM)
+IN_SMEM = pl.BlockSpec(memory_space=pltpu.SMEM)
 
 
 def rotate(vectors, places):
@@ -29,7 +36,320 @@
     )
 
 
-def on_device(
+def ring_order(n):
+    return list(range(0, n, 2)) + list(range(n - 1, 0, -2))
+
+
+def swap_pair(x):
+    return lax.ppermute(x, "gy", [(0, 1), (1, 0)])
+
+
+class Ring:
+    def __init__(self, n):
+        order = ring_order(n)
+        self.onward = [(order[p], order[(p + 1) % n]) for p in range(n)]
+        self.back = [(order[p], order[(p - 1) % n]) for p in range(n)]
+        self.across = [(order[p], order[(p + n // 2) % n]) for p in range(n)]
+
+    def step(self, left, right):
+        return lax.ppermute(left, "gx", self.onward), lax.ppermute(right, "gx", self.back)
+
+
+def owners(n):
+    offsets = [0]
+    for step in range(1, n // 2):
+        offsets += [-step, step]
+    offsets.append(n // 2)
+    me = lax.axis_index("gx")
+    half = lax.div(me, 2)
+    place = jnp.where(lax.rem(me, 2) == 0, half, n - 1 - half)
+    result = []
+    for offset in offsets:
+        at = lax.rem(place + (offset + n), n)
+        result.append(jnp.where(at < n // 2, 2 * at, 2 * (n - 1 - at) + 1))
+    return result
+
+
+def start_copies(source, target, sems, count):
+    rows = source.shape[0]
+    size = -(-rows // (16 * count)) * 16
+    copies = []
+    for i, first in enumerate(range(0, rows, size)):
+        at = pl.ds(first, min(size, rows - first))
+        copy = pltpu.make_async_copy(source.at[at], target.at[at], sems.at[i])
+        copy.start()
+        copies.append(copy)
+    return copies
+
+
+def load_kernel(jobs, *refs):
+    sources, target, sems = refs[: len(jobs)], refs[-2], refs[-1]
+    copies = []
+    for i, (first, size, at) in enumerate(jobs):
+        if at is None:
+            at = target.shape[0] - 2 * size
+            odd = lax.rem(lax.axis_index("gx"), 2)
+            unused = pl.ds(pl.multiple_of(at + (1 - odd) * size, size), size)
+            at = pl.multiple_of(at + odd * size, size)
+            target[unused, :] = jnp.zeros((size, target.shape[1]), target.dtype)
+        part = sources[i].at[pl.ds(first, size)]
+        copies += start_copies(part, target.at[pl.ds(at, size)], sems.at[i], 4)
+    for copy in copies:
+        copy.wait()
+
+
+def load(rows, jobs, after=()):
+    array = jobs[0][0]
+    return pl.pallas_call(
+        lambda *refs: load_kernel([job[1:] for job in jobs], *refs),
+        out_shape=pltpu.VMEM((rows, array.shape[1]), array.dtype),
+        in_specs=[IN_HBM] * len(jobs) + [ANY] * len(after),
+        out_specs=IN_VMEM,
+        scratch_shapes=[pltpu.SemaphoreType.DMA((len(jobs), 4))],
+        compiler_params=pltpu.CompilerParams(vmem_limit_bytes=MIB),
+        name="load",
+    )(*[in_hbm(job[0]) for job in jobs], *after)
+
+
+def load_caches_kernel(*refs):
+    sources, targets, sems = refs[:2], refs[-3:-1], refs[-1]
+    copies = []
+    for i, (source, target) in enumerate(zip(sources, targets)):
+        for row in range(source.shape[0]):
+            copies.append(pltpu.make_async_copy(source.at[row], target.at[row], sems.at[i, row]))
+            copies[-1].start()
+    for copy in copies:
+        copy.wait()
+
+
+def load_caches(keys, values, after):
+    return pl.pallas_call(
+        load_caches_kernel,
+        out_shape=[pltpu.VMEM(a.shape, a.dtype) for a in (keys, values)],
+        in_specs=[IN_HBM] * 2 + [ANY] * len(after),
+        out_specs=[IN_VMEM] * 2,
+        scratch_shapes=[pltpu.SemaphoreType.DMA((2, keys.shape[0]))],
+        compiler_params=pltpu.CompilerParams(vmem_limit_bytes=MIB),
+        name="load_caches",
+    )(in_hbm(keys), in_hbm(values), *after)
+
+
+def in_hbm(array):
+    return pltpu.with_memory_space_constraint(array, pltpu.HBM)
+
+
+def in_vmem(array):
+    return pltpu.with_memory_space_constraint(array, pltpu.VMEM)
+
+
+def before(done, *rest):
+    held = lax.optimization_barrier((done,) + rest)
+    return held[0], held[1:]
+
+
+def sums_kernel(ready, count, *refs):
+    out = refs[-1]
+    start = 0
+    for ref in refs[:ready]:
+        out[start : start + ref.shape[0], :] = ref[...]
+        start += ref.shape[0]
+    rows = refs[ready].shape[0]
+    lane = lax.broadcasted_iota(jnp.int32, (rows, 128), 1)
+    for ref in refs[ready : ready + count]:
+        x = ref[...].astype(jnp.float32)
+        total = jnp.sum(x, axis=1, keepdims=True)
+        square = jnp.sum(x * x, axis=1, keepdims=True)
+        both = jnp.where(lane == 0, total, jnp.where(lane == 1, square, 0.0))
+        out[start : start + rows, :] = both
+        start += rows
+
+
+def row_sums(shards, ready=(), after=()):
+    rows = shards[0].shape[0] * len(shards) + sum(r.shape[0] for r in ready)
+    return pl.pallas_call(
+        lambda *refs: sums_kernel(len(ready), len(shards), *refs),
+        out_shape=jax.ShapeDtypeStruct((rows, 128), jnp.float32),
+        in_specs=[IN_VMEM] * (len(ready) + len(shards)) + [ANY] * len(after),
+        out_specs=IN_VMEM,
+        compiler_params=pltpu.CompilerParams(vmem_limit_bytes=8 * MIB),
+        name="row_sums",
+    )(*ready, *shards, *after)
+
+
+def project_kernel(n, *refs):
+    sums_a, sums_b, gain = refs[:3]
+    near = refs[3 : 3 + n - 1]
+    far = refs[3 + n - 1 : 3 + n + 1]
+    weights = refs[3 + n + 1 : -4]
+    keep, give, normed, total = refs[-4:]
+    rows = near[0].shape[0]
+    half = far[0].shape[1]
+    sums = sums_a[...] + sums_b[...]
+    row_mean = sums[:, :1] / D
+    row_square = sums[:, 1:2] / D
+    scale = lax.rsqrt(row_square - row_mean * row_mean + epsilon)
+    for part in range(2):
+        cols = slice(part * half, (part + 1) * half)
+        for i in range(n):
+            at = slice(i * rows, (i + 1) * rows)
+            x = near[i][:, cols] if i < n - 1 else far[part][...]
+            x = (x.astype(jnp.float32) - row_mean[at]) * scale[at] * gain[:, cols]
+            normed[at, cols] = x
+        x = normed[:, cols].astype(jnp.bfloat16)
+        start = 0
+        for weight in weights:
+            term = lax.dot_general(
+                x, weight[:, cols], contract, preferred_element_type=jnp.float32
+            )
+            stripe = slice(start, start + weight.shape[0])
+            if part == 0:
+                total[:, stripe] = term
+            else:
+                total[:, stripe] += term
+            start = stripe.stop
+    side = lax.axis_index("gy")
+    local = rows // 2
+    for i, owner in enumerate(owners(n)):
+        block = total[i * rows : (i + 1) * rows, :]
+        low, high = block[:local], block[local:]
+        keep[owner] = jnp.where(side == 0, low, high)
+        give[owner] = jnp.where(side == 0, high, low)
+
+
+def project(n, sums, gain, near, far, weights):
+    rows, width = near[0].shape
+    stripe = sum(w.shape[0] for w in weights)
+    shape = jax.ShapeDtypeStruct((n, rows // 2, stripe), jnp.float32)
+    return pl.pallas_call(
+        lambda *refs: project_kernel(n, *refs),
+        out_shape=[shape, shape],
+        in_specs=[IN_VMEM] * (3 + n + 1 + len(weights)),
+        out_specs=[IN_VMEM] * 2,
+        scratch_shapes=[
+            pltpu.VMEM((n * rows, width), jnp.float32),
+            pltpu.VMEM((n * rows, stripe), jnp.float32),
+        ],
+        compiler_params=pltpu.CompilerParams(vmem_limit_bytes=8 * MIB),
+        name="project",
+    )(*sums, gain, *near, *far, *[in_vmem(w) for w in weights])
+
+
+def attend_kernel(lengths, arrived, cosine, sine, keys, values, mine, other, spread, held):
+    n, rows, stripe = arrived.shape
+    query_cols = stripe - 128
+    side = lax.axis_index("gy")
+    score_scale = 1.0 / math.sqrt(DH)
+    for i in range(n):
+        block = arrived[i].astype(jnp.float32)
+        for r in range(rows):
+            spread[r, i : i + 1, :] = block[r : r + 1, :]
+    for r in range(rows):
+        given = spread[r]
+        cos, sin = cosine[r : r + 1, :], sine[r : r + 1, :]
+
+        def turn(a, b):
+            turned = jnp.concatenate([a * cos - b * sin, b * cos + a * sin], axis=1)
+            return turned.astype(jnp.bfloat16)
+
+        starts = range(0, query_cols, DH)
+        q = turn(
+            jnp.concatenate([given[:, c : c + DH // 2] for c in starts], axis=0),
+            jnp.concatenate([given[:, c + DH // 2 : c + DH] for c in starts], axis=0),
+        )
+        new = [
+            given[i : i + 1, query_cols:] + given[i + 1 : i + 2, query_cols:]
+            for i in range(0, n, 2)
+        ]
+        new_key = turn(new[0], new[1]).astype(jnp.float32)
+        new_value = jnp.concatenate(new[2:], axis=1)
+        scores = lax.dot_general(q, keys[r], contract, preferred_element_type=jnp.float32)
+        scores = scores * score_scale
+        place = lax.broadcasted_iota(jnp.int32, scores.shape, 1)
+        scores = jnp.where(place < lengths[r], scores, -1e30)
+        own_score = jnp.sum(q.astype(jnp.float32) * new_key, axis=1, keepdims=True) * score_scale
+        highest = jnp.maximum(jnp.max(scores, axis=1, keepdims=True), own_score)
+        weights = jnp.exp(scores - highest)
+        own_weight = jnp.exp(own_score - highest)
+        totals = jnp.sum(weights, axis=1, keepdims=True) + own_weight
+        blended = jnp.dot(
+            weights.astype(jnp.bfloat16), values[r], preferred_element_type=jnp.float32
+        )
+        blended = (blended + own_weight * new_value) / totals
+        for j in range(len(starts)):
+            block = blended[j * n : (j + 1) * n]
+            swapped = pltpu.roll(block, n // 2, 0)
+            parts = [jnp.where(side == 0, block, swapped), jnp.where(side == 0, swapped, block)]
+            for i in range(n // 2):
+                at = (i * len(starts) + j) * DH
+                for k, part in enumerate(parts):
+                    held[k, r : r + 1, at : at + DH] = part[i : i + 1]
+    mine[...] = held[0].astype(jnp.bfloat16)
+    other[...] = held[1].astype(jnp.bfloat16)
+
+
+def attend(lengths, arrived, cosine, sine, keys, values):
+    n, rows, stripe = arrived.shape
+    shape = jax.ShapeDtypeStruct((rows, HEADS * DH // 2), jnp.bfloat16)
+    return pl.pallas_call(
+        attend_kernel,
+        out_shape=[shape, shape],
+        in_specs=[IN_SMEM] + [IN_VMEM] * 5,
+        out_specs=[IN_VMEM] * 2,
+        scratch_shapes=[
+            pltpu.VMEM((rows, n, stripe), jnp.float32),
+            pltpu.VMEM((2, rows, HEADS * DH // 2), jnp.float32),
+        ],
+        compiler_params=pltpu.CompilerParams(vmem_limit_bytes=8 * MIB),
+        name="attend",
+    )(lengths, arrived, cosine, sine, in_vmem(keys), in_vmem(values))
+
+
+def output_kernel(n, *refs):
+    near = refs[: n - 1]
+    far = refs[n - 1 : n + 1]
+    weights = refs[n + 1 : -4]
+    keep, give, total, placed = refs[-4:]
+    rows = near[0].shape[0]
+    half = far[0].shape[1]
+    depth = weights[0].shape[0]
+    for part, weight in enumerate(weights):
+        start = part * depth
+        cols = slice(start, start + depth)
+        last = slice(start % half, start % half + depth)
+        x = [ref[:, cols] for ref in near] + [far[start // half][:, last]]
+        x = jnp.concatenate([piece.astype(jnp.float32) for piece in x], axis=0)
+        term = jnp.dot(x.astype(jnp.bfloat16), weight[...], preferred_element_type=jnp.float32)
+        if part == 0:
+            total[...] = term
+        else:
+            total[...] += term
+    side = lax.axis_index("gy")
+    for i, owner in enumerate(owners(n)):
+        block = total[i * rows : (i + 1) * rows, :]
+        placed[owner] = jnp.where(side == 0, block, pltpu.roll(block, rows // 2, 0))
+    keep[...] = placed[pl.ds(side * (n // 2), n // 2)]
+    give[...] = placed[pl.ds((1 - side) * (n // 2), n // 2)]
+
+
+def output_project(n, near, far, weights):
+    rows = near[0].shape[0]
+    cols = weights[0].shape[1]
+    shape = jax.ShapeDtypeStruct((n // 2, rows, cols), jnp.float32)
+    return pl.pallas_call(
+        lambda *refs: output_kernel(n, *refs),
+        out_shape=[shape, shape],
+        in_specs=[IN_VMEM] * (n + 1 + len(weights)),
+        out_specs=[IN_VMEM] * 2,
+        scratch_shapes=[
+            pltpu.VMEM((n * rows, cols), jnp.float32),
+            pltpu.VMEM((n, rows, cols), jnp.float32),
+        ],
+        compiler_params=pltpu.CompilerParams(vmem_limit_bytes=8 * MIB),
+        name="output_project",
+    )(*near, *far, *[in_vmem(w) for w in weights])
+
+
+def on_any_grid(
     activations,
     norm_gain,
     query_weight,
@@ -104,9 +424,86 @@
     return lax.psum_scatter(partial_out, "gy", scatter_dimension=0, tiled=True).astype(jnp.bfloat16)
 
 
+def on_device(
+    activations,
+    norm_gain,
+    query_weight,
+    keyval_weight,
+    output_weight,
+    cache_keys,
+    cache_values,
+    cache_lengths,
+):
+    n = lax.axis_size("gx")
+    ring = Ring(n)
+    query_cols, width = query_weight.shape
+    new_cols = keyval_weight.shape[0]
+    piece = query_cols // 4
+    weights = []
+
+    indices = jnp.arange(DH // 2, dtype=jnp.float32)
+    frequency = jnp.exp(-math.log(10000.0) * indices / (DH // 2))
+    angles = cache_lengths.astype(jnp.float32)[:, None] * frequency
+    cosine, sine = jnp.cos(angles), jnp.sin(angles)
+
+    left = right = activations
+    near = [activations]
+    for step in range(1, n // 2):
+        arrived = near[1:][-2:]
+        left, right = ring.step(left, right)
+        if step == 2:
+            sums = row_sums([activations, *arrived])
+            far_sums = lax.ppermute(sums[: activations.shape[0]], "gx", ring.across)
+        elif step > 2:
+            sums = row_sums(arrived, [sums])
+        start = (step - 1) * piece
+        weight = load(piece, [(query_weight, start, piece, 0)], arrived)
+        weight, (left, right) = before(weight, left, right)
+        weights.append(weight)
+        near += [left, right]
+    half = width // 2
+    far = ring.step(left[:, :half], right[:, half:])
+    sums = row_sums([left, right], [sums])
+    jobs = [(query_weight, 3 * piece, piece, 0), (keyval_weight, 0, new_cols, None)]
+    weight = load(piece + 2 * new_cols, jobs, [sums])
+    sums = jnp.concatenate([sums, far_sums], axis=0)
+    other_sums = swap_pair(sums)
+    weight, (other_sums, *far) = before(weight, other_sums, *far)
+    weights.append(weight)
+    sums = (sums, other_sums)
+    gain = norm_gain.astype(jnp.float32)[None, :]
+    keep, give = project(n, sums, gain, near, far, weights)
+    projected = (keep + swap_pair(give)).astype(jnp.bfloat16)
+
+    piece = output_weight.shape[0] // 4
+    arrived = lax.all_to_all(projected, "gx", split_axis=0, concat_axis=0, tiled=True)
+    keys, values = load_caches(cache_keys, cache_values, [projected])
+    weight = load(piece, [(output_weight, 0, piece, 0)], [projected])
+    weight, (arrived,) = before(weight, arrived)
+    weights = [weight]
+    mine, other = attend(cache_lengths, arrived, cosine, sine, keys, values)
+    shard = jnp.concatenate([mine, swap_pair(other)], axis=0)
+
+    left = right = shard
+    near = [shard]
+    for step in range(1, n // 2):
+        arrived = near[-2:]
+        left, right = ring.step(left, right)
+        start = step * piece
+        weight = load(piece, [(output_weight, start, piece, 0)], arrived)
+        weight, (left, right) = before(weight, left, right)
+        weights.append(weight)
+        near += [left, right]
+    half = shard.shape[1] // 2
+    far = ring.step(left[:, :half], right[:, half:])
+    keep, give = output_project(n, near, far, weights)
+    out = (keep + swap_pair(give)).astype(jnp.bfloat16)
+    return out.reshape(-1, out.shape[-1])
+
+
 def solution(mesh):
     return jax.shard_map(
-        on_device,
+        on_device if mesh.shape["gx"] == 8 else on_any_grid,
         mesh=mesh,
         in_specs=(
             P(("groups", "gx"), "gy"),

time: 160 us -> 99.5 us (0.62)
  waiting for transfers between devices: 63.4 us -> 14.4 us
  Pallas kernels: 0 us -> 47.4 us
  blocking collectives: 38.5 us -> 0 us
  matrix products: 33 us -> 0 us
  starting transfers between devices: 3.6 us -> 24.1 us
  between operations: 13.6 us -> 0.27 us
  local copies, waits for them, and re-layouts: 1.16 us -> 11.3 us
  other arithmetic: 6.07 us -> 1.59 us
    pallas_call x0 -> x15, Pallas kernels: none -> 47.4 us  [the longest x8 25.3 us: load(): pl.pallas_call(lambda *refs: load_kernel([job[1:] for job in jobs], *refs...]
    all_gather x1 -> x0, waiting for transfers between devices: 43.8 us -> none  [on_device(): shard_rows = lax.all_gather(normed, 'gx', axis=0, tiled=True)]
    dot_general x6 -> x0, matrix products: 33 us -> none  [the longest x1 13.8 us: on_device(): lax.dot_general(shard_rows, query_weight, contract, preferred_element_typ...]
    all_gather x1 -> x0, blocking collectives: 32.2 us -> none  [on_device(): lax.all_gather(swapped, 'gx', axis=0, tiled=True)]
    ppermute x0 -> x21, starting transfers between devices: none -> 20.4 us  [the longest x8 13.1 us: step(): lax.ppermute(left, 'gx', self.onward)]
    ppermute x0 -> x21, waiting for transfers between devices: none -> 14.4 us  [the longest x8 7.7 us: step(): lax.ppermute(right, 'gx', self.back)]
    all_to_all x1, waiting for transfers between devices: 12.5 us -> 0.01 us  [on_device(): lax.all_to_all(projected, 'gx', split_axis=0, concat_axis=0, tiled=True)]
    unnamed x10 -> x20, local copies, waits for them, and re-layouts: 0.02 us -> 11.3 us
  transfers between devices with their start and end apart: 3 -> 22, of which waited for: 3 -> 11; matrix products, arithmetic and copies ran while one was open for 0% -> 0% of each run, Pallas kernels for 0% -> 30%
where the time goes in v6:
time: 99.5 us; the launch traced here: 99.2 us
  Pallas kernels  47.4 us (48%)
  starting transfers between devices  24.1 us (24%)
  waiting for transfers between devices  14.4 us (14%)
  local copies, waits for them, and re-layouts  11.3 us (11%)
  other arithmetic  1.59 us (2%)
    pallas_call x8, Pallas kernels, load(): pl.pallas_call(lambda *refs: load_kernel([job[1:] for job in jobs], *refs...  25.3 us
    ppermute x8, starting transfers between devices, step(): lax.ppermute(left, 'gx', self.onward)  13.1 us
    unnamed x20, local copies, waits for them, and re-layouts  11.3 us
    pallas_call x1, Pallas kernels, project(): pl.pallas_call(lambda *refs: project_kernel(n, *refs), out_shape=[shape,...  9.64 us
    ppermute x8, waiting for transfers between devices, step(): lax.ppermute(right, 'gx', self.back)  7.7 us
    pallas_call x1, Pallas kernels, output_project(): pl.pallas_call(lambda *refs: output_kernel(n, *refs), out_shape=[shape, s...  5.04 us
    ppermute x8, starting transfers between devices, step(): lax.ppermute(right, 'gx', self.back)  4.26 us
    ppermute x4, waiting for transfers between devices, swap_pair(): return lax.ppermute(x, 'gy', [(0, 1), (1, 0)])  3.8 us
  transfers between devices with their start and end apart: 22, of which 11 were waited for; matrix products, arithmetic and copies ran while one was open for 0% of the time, Pallas kernels for 30%

profile of v6, /device:TPU:0, one launch (start us, length us, event | category | flops | bytes accessed | tf_op | source)
XLA Modules:
  0.0 99.2 jit_solution(16392280880189729973)
XLA Ops:
  0.0 3.0 %collective-permute-start = (bf16[8,9216]{1,0:T(8,128)(2,1)}, bf16[8,9216]{1,0:T(8,128)(2,1)S(1)}, u32[]{:S(2)}, u32[]{:S(2)}) collective-permute-start(bf16[8,9216]{1,0:T(8,128)(2,1)} %refs_3_.1), channel_id=1, source_target_pairs={{0,4},{4,8},{8,12},{12,14},{14,10},{10,6},{6,2},{2,0},{1,5},{5,9},... | collective-permute-start | bytes 442376 | tf_op jit(solution)/shard_map/ppermute | solution.py:55
  3.0 3.1 %load.8.refs_12_ = bf16[384,9216]{1,0:T(8,128)(2,1)S(1)} custom-call(bf16[1536,9216]{1,0:T(8,128)(2,1)} %refs_0_.14), custom_call_target="tpu_custom_call" | custom-call | tf_op jit(solution)/shard_map/load/pallas_call | solution.py:103
  6.2 0.9 collective-permute-done.refs_1_.refs_4_
  7.0 1.5 %collective-permute-done.1.refs_2_.refs_5_ = bf16[8,9216]{1,0:T(8,128)(2,1)S(1)} collective-permute-done((bf16[8,9216]{1,0:T(8,128)(2,1)}, bf16[8,9216]{1,0:T(8,128)(2,1)S(1)}, u32[]{:S(2)}, u32[]{:S(2)}) %collective-permute-start.1) | collective-permute-done | bytes 147488 | tf_op jit(solution)/shard_map/ppermute | solution.py:55
  8.5 1.6 %collective-permute-start.2 = (bf16[8,9216]{1,0:T(8,128)(2,1)S(1)}, bf16[8,9216]{1,0:T(8,128)(2,1)S(1)}, u32[]{:S(2)}, u32[]{:S(2)}) collective-permute-start(bf16[8,9216]{1,0:T(8,128)(2,1)S(1)} %collective-permute-done.refs_1_.refs_4_), channel_id=1, source_target_pairs={{0,4},{4,8},{8,12},{12,14},{14,10},{10,6},{6,2},{2,0},{1,5},{5,9},... | collective-permute-start | bytes 442376 | tf_op jit(solution)/shard_map/ppermute | solution.py:55
  10.1 0.4 collective-permute-start.3
  10.6 3.1 %load.9.refs_13_ = bf16[384,9216]{1,0:T(8,128)(2,1)S(1)} custom-call(bf16[1536,9216]{1,0:T(8,128)(2,1)} %refs_0_.14, bf16[8,9216]{1,0:T(8,128)(2,1)S(1)} %collective-permute-done.refs_1_.refs_4_, bf16[8,9216]{1,0:T(8,128)(2,1)S(1)} %collective-permute-done.1.refs_2_.refs_5_), custom_call_target="tpu_custom_call" | custom-call | tf_op jit(solution)/shard_map/load/pallas_call | solution.py:103
  13.7 1.6 %collective-permute-done.3.refs_2_.refs_7_ = bf16[8,9216]{1,0:T(8,128)(2,1)S(1)} collective-permute-done((bf16[8,9216]{1,0:T(8,128)(2,1)S(1)}, bf16[8,9216]{1,0:T(8,128)(2,1)S(1)}, u32[]{:S(2)}, u32[]{:S(2)}) %collective-permute-start.3) | collective-permute-done | bytes 147488 | tf_op jit(solution)/shard_map/ppermute | solution.py:55
  15.3 1.6 %collective-permute-start.4 = (bf16[8,9216]{1,0:T(8,128)(2,1)S(1)}, bf16[8,9216]{1,0:T(8,128)(2,1)S(1)}, u32[]{:S(2)}, u32[]{:S(2)}) collective-permute-start(bf16[8,9216]{1,0:T(8,128)(2,1)S(1)} %collective-permute-done.2.refs_1_.refs_6_), channel_id=1, source_target_pairs={{0,4},{4,8},{8,12},{12,14},{14,10},{10,6},{6,2},{2,0},{1,5},{5,9},... | collective-permute-start | bytes 442376 | tf_op jit(solution)/shard_map/ppermute | solution.py:55
  16.8 0.4 collective-permute-start.5
  17.3 0.2 row_sums.3.refs_0_
  17.5 2.3 %collective-permute-start.6 = (f32[8,128]{1,0:T(8,128)S(1)}, f32[8,128]{1,0:T(8,128)S(1)}, u32[]{:S(2)}, u32[]{:S(2)}) collective-permute-start(f32[8,128]{1,0:T(8,128)S(1)} %slice.20), channel_id=1, source_target_pairs={{0,14},{4,10},{8,6},{12,2},{14,0},{10,4},{6,8},{2,12},{1,15},{5,11... | collective-permute-start | bytes 12296 | tf_op jit(solution)/shard_map/ppermute | solution.py:456
  19.8 3.1 %load.10.refs_14_ = bf16[384,9216]{1,0:T(8,128)(2,1)S(1)} custom-call(bf16[1536,9216]{1,0:T(8,128)(2,1)} %refs_0_.14, bf16[8,9216]{1,0:T(8,128)(2,1)S(1)} %collective-permute-done.2.refs_1_.refs_6_, bf16[8,9216]{1,0:T(8,128)(2,1)S(1)} %collective-permute-done.3.refs_2_.refs_7_), custom_call_target="tpu_custom_call" | custom-call | tf_op jit(solution)/shard_map/load/pallas_call | solution.py:103
  23.3 0.4 collective-permute-start.8
  23.8 1.6 %collective-permute-start.9 = (bf16[8,4608]{1,0:T(8,128)(2,1)S(1)}, bf16[8,4608]{1,0:T(8,128)(2,1)S(1)}, u32[]{:S(2)}, u32[]{:S(2)}) collective-permute-start(bf16[8,4608]{1,0:T(8,128)(2,1)S(1)} %slice.17), channel_id=1, source_target_pairs={{0,2},{4,0},{8,4},{12,8},{14,12},{10,14},{6,10},{2,6},{1,3},{5,1},... | collective-permute-start | bytes 221192 | tf_op jit(solution)/shard_map/ppermute | solution.py:55
  25.4 3.4 %load.11.refs_15_ = bf16[512,9216]{1,0:T(8,128)(2,1)S(1)} custom-call(bf16[1536,9216]{1,0:T(8,128)(2,1)} %refs_0_.14, bf16[64,9216]{1,0:T(8,128)(2,1)} %refs_1_.2, f32[56,128]{1,0:T(8,128)S(1)} %row_sums.5.refs_2_), custom_call_target="tpu_custom_call" | custom-call | tf_op jit(solution)/shard_map/load/pallas_call | solution.py:103
  28.9 9.6 %project.1 = (f32[8,4,1664]{2,1,0:T(4,128)S(1)}, f32[8,4,1664]{2,1,0:T(4,128)S(1)}) custom-call(f32[64,128]{1,0:T(8,128)S(1)} %pad_maximum_fusion.1.refs_0_, f32[64,128]{1,0:T(8,128)S(1)} %collective-permute-done.7.refs_1_, f32[1,9216]{1,0:T(1,128)S(1)} %bitcast.5, bf16[8,9216]{1,0:T(8,128)(2,1)S(1)} %copy-done.5, ...), custom_call_target="tpu_custom_call" | custom-call | tf_op jit(solution)/shard_map/project/pallas_call | solution.py:223
  38.5 0.6 collective-permute-start.10
  39.1 1.1 %collective-permute-done.10 = f32[8,4,1664]{2,1,0:T(4,128)S(1)} collective-permute-done((f32[8,4,1664]{2,1,0:T(4,128)S(1)}, f32[8,4,1664]{2,1,0:T(4,128)S(1)}, u32[]{:S(2)}, u32[]{:S(2)}) %collective-permute-start.10) | collective-permute-done | bytes 213024 | tf_op jit(solution)/shard_map/ppermute | solution.py:44
  40.1 0.7 add_convert_fusion.1.refs_1_.refs_2_
  40.8 3.7 %all-to-all-start = ((bf16[8,4,1664]{2,1,0:T(4,128)(2,1)}), bf16[8,4,1664]{2,1,0:T(4,128)(2,1)S(1)}, u32[]{:S(2)}, u32[]{:S(2)}) async-start(bf16[8,4,1664]{2,1,0:T(4,128)(2,1)} %add_convert_fusion.1.refs_1_.refs_2_), calls=%async_computation | async-start | bytes 212992 | tf_op jit(solution)/shard_map/all_to_all | solution.py:479
  44.7 3.1 %load.12.refs_9_ = bf16[1536,2304]{1,0:T(8,128)(2,1)S(1)} custom-call(bf16[6144,2304]{1,0:T(8,128)(2,1)} %refs_0_.19, bf16[8,4,1664]{2,1,0:T(4,128)(2,1)} %add_convert_fusion.1.refs_1_.refs_2_), custom_call_target="tpu_custom_call" | custom-call | tf_op jit(solution)/shard_map/load/pallas_call | solution.py:103
  47.8 2.9 %copy-done = bf16[1536,2304]{1,0:T(8,128)(2,1)} copy-done((bf16[1536,2304]{1,0:T(8,128)(2,1)}, bf16[1536,2304]{1,0:T(8,128)(2,1)S(1)}, u32[]{:S(2)}) %copy-start) | copy-done | bytes 7077912
  50.6 3.5 %load_caches.1 = (bf16[4,2048,256]{2,1,0:T(8,128)(2,1)S(1)}, bf16[4,2048,256]{2,1,0:T(8,128)(2,1)S(1)}) custom-call(bf16[4,2048,256]{2,1,0:T(8,128)(2,1)} %refs_0_.16, bf16[4,2048,256]{2,1,0:T(8,128)(2,1)} %refs_1_.3, bf16[8,4,1664]{2,1,0:T(4,128)(2,1)} %add_convert_fusion.1.refs_1_.refs_2_), custom_call_target="tpu_custom_call" | custom-call | tf_op jit(solution)/shard_map/load_caches/pallas_call | solution.py:126
  54.1 2.1 %copy-done.1 = bf16[4,2048,256]{2,1,0:T(8,128)(2,1)} copy-done((bf16[4,2048,256]{2,1,0:T(8,128)(2,1)}, bf16[4,2048,256]{2,1,0:T(8,128)(2,1)S(1)}, u32[]{:S(2)}) %copy-start.1) | copy-done | bytes 4194328
  56.2 2.0 %copy-done.3 = bf16[4,2048,256]{2,1,0:T(8,128)(2,1)} copy-done((bf16[4,2048,256]{2,1,0:T(8,128)(2,1)}, bf16[4,2048,256]{2,1,0:T(8,128)(2,1)S(1)}, u32[]{:S(2)}) %copy-start.3) | copy-done | bytes 4194328
  58.2 2.2 %copy-done.2 = bf16[4,2048,256]{2,1,0:T(8,128)(2,1)S(1)} copy-done((bf16[4,2048,256]{2,1,0:T(8,128)(2,1)S(1)}, bf16[4,2048,256]{2,1,0:T(8,128)(2,1)}, u32[]{:S(2)}) %copy-start.2) | copy-done | bytes 4194328
  60.4 2.2 %copy-done.4 = bf16[4,2048,256]{2,1,0:T(8,128)(2,1)S(1)} copy-done((bf16[4,2048,256]{2,1,0:T(8,128)(2,1)S(1)}, bf16[4,2048,256]{2,1,0:T(8,128)(2,1)}, u32[]{:S(2)}) %copy-start.4) | copy-done | bytes 4194328
  62.6 3.4 %attend.1 = (bf16[4,6144]{1,0:T(4,128)(2,1)S(1)}, bf16[4,6144]{1,0:T(4,128)(2,1)S(1)}) custom-call(s32[4]{0:T(128)S(1)} %copy-done.6, bf16[8,4,1664]{2,1,0:T(4,128)(2,1)S(1)} %all-to-all-done.arrived, f32[4,128]{1,0:T(4,128)S(1)} %get-tuple-element.70.cosine, f32[4,128]{1,0:T(4,128)S(1)} %get-tuple-element.69.sine, bf16[4,2048,256]{2,1,0:T(8,128)(2,1)S(1)} %copy-done.2, ...), custom_call_target="tpu_custom_call" | custom-call | tf_op jit(solution)/shard_map/attend/pallas_call | solution.py:293
  66.2 1.2 %collective-permute-done.11 = bf16[4,6144]{1,0:T(4,128)(2,1)S(1)} collective-permute-done((bf16[4,6144]{1,0:T(4,128)(2,1)S(1)}, bf16[4,6144]{1,0:T(4,128)(2,1)S(1)}, u32[]{:S(2)}, u32[]{:S(2)}) %collective-permute-start.11) | collective-permute-done | bytes 49184 | tf_op jit(solution)/shard_map/ppermute | solution.py:44
  67.4 2.1 %collective-permute-start.12 = (bf16[8,6144]{1,0:T(8,128)(2,1)S(1)}, bf16[8,6144]{1,0:T(8,128)(2,1)S(1)}, u32[]{:S(2)}, u32[]{:S(2)}) collective-permute-start(bf16[8,6144]{1,0:T(8,128)(2,1)S(1)} %pad_maximum_fusion.refs_1_.refs_0_), channel_id=1, source_target_pairs={{0,4},{4,8},{8,12},{12,14},{14,10},{10,6},{6,2},{2,0},{1,5},{5,9},... | collective-permute-start | bytes 294920 | tf_op jit(solution)/shard_map/ppermute | solution.py:55
  69.5 3.1 %load.13.refs_10_ = bf16[1536,2304]{1,0:T(8,128)(2,1)S(1)} custom-call(bf16[6144,2304]{1,0:T(8,128)(2,1)} %refs_0_.19, bf16[8,6144]{1,0:T(8,128)(2,1)S(1)} %pad_maximum_fusion.refs_1_.refs_0_), custom_call_target="tpu_custom_call" | custom-call | tf_op jit(solution)/shard_map/load/pallas_call | solution.py:103
  72.6 1.4 %collective-permute-done.13.refs_2_ = bf16[8,6144]{1,0:T(8,128)(2,1)S(1)} collective-permute-done((bf16[8,6144]{1,0:T(8,128)(2,1)S(1)}, bf16[8,6144]{1,0:T(8,128)(2,1)S(1)}, u32[]{:S(2)}, u32[]{:S(2)}) %collective-permute-start.13) | collective-permute-done | bytes 98336 | tf_op jit(solution)/shard_map/ppermute | solution.py:55
  74.1 1.5 %collective-permute-start.14 = (bf16[8,6144]{1,0:T(8,128)(2,1)S(1)}, bf16[8,6144]{1,0:T(8,128)(2,1)S(1)}, u32[]{:S(2)}, u32[]{:S(2)}) collective-permute-start(bf16[8,6144]{1,0:T(8,128)(2,1)S(1)} %collective-permute-done.12.refs_1_), channel_id=1, source_target_pairs={{0,4},{4,8},{8,12},{12,14},{14,10},{10,6},{6,2},{2,0},{1,5},{5,9},... | collective-permute-start | bytes 294920 | tf_op jit(solution)/shard_map/ppermute | solution.py:55
  75.5 0.6 collective-permute-start.15
  76.1 3.2 %load.14.refs_11_ = bf16[1536,2304]{1,0:T(8,128)(2,1)S(1)} custom-call(bf16[6144,2304]{1,0:T(8,128)(2,1)} %refs_0_.19, bf16[8,6144]{1,0:T(8,128)(2,1)S(1)} %collective-permute-done.12.refs_1_, bf16[8,6144]{1,0:T(8,128)(2,1)S(1)} %collective-permute-done.13.refs_2_), custom_call_target="tpu_custom_call" | custom-call | tf_op jit(solution)/shard_map/load/pallas_call | solution.py:103
  79.4 0.8 collective-permute-done.15.refs_2_.refs_4_
  80.2 1.5 %collective-permute-start.16 = (bf16[8,6144]{1,0:T(8,128)(2,1)S(1)}, bf16[8,6144]{1,0:T(8,128)(2,1)S(1)}, u32[]{:S(2)}, u32[]{:S(2)}) collective-permute-start(bf16[8,6144]{1,0:T(8,128)(2,1)S(1)} %collective-permute-done.14.refs_1_.refs_3_), channel_id=1, source_target_pairs={{0,4},{4,8},{8,12},{12,14},{14,10},{10,6},{6,2},{2,0},{1,5},{5,9},... | collective-permute-start | bytes 294920 | tf_op jit(solution)/shard_map/ppermute | solution.py:55
  81.6 0.6 collective-permute-start.17
  82.2 3.1 %load.15.refs_12_ = bf16[1536,2304]{1,0:T(8,128)(2,1)S(1)} custom-call(bf16[6144,2304]{1,0:T(8,128)(2,1)} %refs_0_.19, bf16[8,6144]{1,0:T(8,128)(2,1)S(1)} %collective-permute-done.14.refs_1_.refs_3_, bf16[8,6144]{1,0:T(8,128)(2,1)S(1)} %collective-permute-done.15.refs_2_.refs_4_), custom_call_target="tpu_custom_call" | custom-call | tf_op jit(solution)/shard_map/load/pallas_call | solution.py:103
  85.3 0.9 collective-permute-done.17.refs_6_
  86.2 1.5 %collective-permute-start.18 = (bf16[8,3072]{1,0:T(8,128)(2,1)S(1)}, bf16[8,3072]{1,0:T(8,128)(2,1)S(1)}, u32[]{:S(2)}, u32[]{:S(2)}) collective-permute-start(bf16[8,3072]{1,0:T(8,128)(2,1)S(1)} %slice.18), channel_id=1, source_target_pairs={{0,4},{4,8},{8,12},{12,14},{14,10},{10,6},{6,2},{2,0},{1,5},{5,9},... | collective-permute-start | bytes 147464 | tf_op jit(solution)/shard_map/ppermute | solution.py:55
  87.7 0.6 collective-permute-start.19
  88.3 2.1 %collective-permute-done.18.refs_7_ = bf16[8,3072]{1,0:T(8,128)(2,1)S(1)} collective-permute-done((bf16[8,3072]{1,0:T(8,128)(2,1)S(1)}, bf16[8,3072]{1,0:T(8,128)(2,1)S(1)}, u32[]{:S(2)}, u32[]{:S(2)}) %collective-permute-start.18) | collective-permute-done | bytes 49184 | tf_op jit(solution)/shard_map/ppermute | solution.py:55
  90.3 1.5 %collective-permute-done.19.refs_8_ = bf16[8,3072]{1,0:T(8,128)(2,1)S(1)} collective-permute-done((bf16[8,3072]{1,0:T(8,128)(2,1)S(1)}, bf16[8,3072]{1,0:T(8,128)(2,1)S(1)}, u32[]{:S(2)}, u32[]{:S(2)}) %collective-permute-start.19) | collective-permute-done | bytes 49184 | tf_op jit(solution)/shard_map/ppermute | solution.py:55
  91.8 5.0 %output_project.1 = (f32[4,8,2304]{2,1,0:T(8,128)S(1)}, f32[4,8,2304]{2,1,0:T(8,128)S(1)}) custom-call(bf16[8,6144]{1,0:T(8,128)(2,1)S(1)} %pad_maximum_fusion.refs_1_.refs_0_, bf16[8,6144]{1,0:T(8,128)(2,1)S(1)} %collective-permute-done.12.refs_1_, bf16[8,6144]{1,0:T(8,128)(2,1)S(1)} %collective-permute-done.13.refs_2_, ...), custom_call_target="tpu_custom_call" | custom-call | tf_op jit(solution)/shard_map/output_project/pallas_call | solution.py:338
  96.9 1.6 %collective-permute-done.20 = f32[4,8,2304]{2,1,0:T(8,128)S(1)} collective-permute-done((f32[4,8,2304]{2,1,0:T(8,128)S(1)}, f32[4,8,2304]{2,1,0:T(8,128)S(1)}, u32[]{:S(2)}, u32[]{:S(2)}) %collective-permute-start.20) | collective-permute-done | bytes 294944 | tf_op jit(solution)/shard_map/ppermute | solution.py:44
  98.5 0.7 fusion
  (45 shorter events, 0.9 us)
Async XLA Ops:
  0.0 7.0 %collective-permute-start = (bf16[8,9216]{1,0:T(8,128)(2,1)}, bf16[8,9216]{1,0:T(8,128)(2,1)S(1)}, u32[]{:S(2)}, u32[]{:S(2)}) collective-permute-start(bf16[8,9216]{1,0:T(8,128)(2,1)} %refs_3_.1), channel_id=1, source_target_pairs={{0,4},{4,8},{8,12},{12,14},{14,10},{10,6},{6,2},{2,0},{1,5},{5,9},... | collective-permute-start | bytes 442376 | tf_op jit(solution)/shard_map/ppermute | solution.py:55
  3.0 5.5 %collective-permute-start.1 = (bf16[8,9216]{1,0:T(8,128)(2,1)}, bf16[8,9216]{1,0:T(8,128)(2,1)S(1)}, u32[]{:S(2)}, u32[]{:S(2)}) collective-permute-start(bf16[8,9216]{1,0:T(8,128)(2,1)} %refs_3_.1), channel_id=1, source_target_pairs={{0,2},{4,0},{8,4},{12,8},{14,12},{10,14},{6,10},{2,6},{1,3},{5,1},... | collective-permute-start | bytes 442376 | tf_op jit(solution)/shard_map/ppermute | solution.py:55
  6.1 11.2 %copy-start.5 = (bf16[8,9216]{1,0:T(8,128)(2,1)S(1)}, bf16[8,9216]{1,0:T(8,128)(2,1)}, u32[]{:S(2)}) copy-start(bf16[8,9216]{1,0:T(8,128)(2,1)} %refs_3_.1) | copy-start | bytes 442372
  8.5 5.1 %collective-permute-start.2 = (bf16[8,9216]{1,0:T(8,128)(2,1)S(1)}, bf16[8,9216]{1,0:T(8,128)(2,1)S(1)}, u32[]{:S(2)}, u32[]{:S(2)}) collective-permute-start(bf16[8,9216]{1,0:T(8,128)(2,1)S(1)} %collective-permute-done.refs_1_.refs_4_), channel_id=1, source_target_pairs={{0,4},{4,8},{8,12},{12,14},{14,10},{10,6},{6,2},{2,0},{1,5},{5,9},... | collective-permute-start | bytes 442376 | tf_op jit(solution)/shard_map/ppermute | solution.py:55
  10.1 5.1 %collective-permute-start.3 = (bf16[8,9216]{1,0:T(8,128)(2,1)S(1)}, bf16[8,9216]{1,0:T(8,128)(2,1)S(1)}, u32[]{:S(2)}, u32[]{:S(2)}) collective-permute-start(bf16[8,9216]{1,0:T(8,128)(2,1)S(1)} %collective-permute-done.1.refs_2_.refs_5_), channel_id=1, source_target_pairs={{0,2},{4,0},{8,4},{12,8},{14,12},{10,14},{6,10},{2,6},{1,3},{5,1},... | collective-permute-start | bytes 442376 | tf_op jit(solution)/shard_map/ppermute | solution.py:55
  15.3 7.9 %collective-permute-start.4 = (bf16[8,9216]{1,0:T(8,128)(2,1)S(1)}, bf16[8,9216]{1,0:T(8,128)(2,1)S(1)}, u32[]{:S(2)}, u32[]{:S(2)}) collective-permute-start(bf16[8,9216]{1,0:T(8,128)(2,1)S(1)} %collective-permute-done.2.refs_1_.refs_6_), channel_id=1, source_target_pairs={{0,4},{4,8},{8,12},{12,14},{14,10},{10,6},{6,2},{2,0},{1,5},{5,9},... | collective-permute-start | bytes 442376 | tf_op jit(solution)/shard_map/ppermute | solution.py:55
  16.8 6.3 %collective-permute-start.5 = (bf16[8,9216]{1,0:T(8,128)(2,1)S(1)}, bf16[8,9216]{1,0:T(8,128)(2,1)S(1)}, u32[]{:S(2)}, u32[]{:S(2)}) collective-permute-start(bf16[8,9216]{1,0:T(8,128)(2,1)S(1)} %collective-permute-done.3.refs_2_.refs_7_), channel_id=1, source_target_pairs={{0,2},{4,0},{8,4},{12,8},{14,12},{10,14},{6,10},{2,6},{1,3},{5,1},... | collective-permute-start | bytes 442376 | tf_op jit(solution)/shard_map/ppermute | solution.py:55
  17.5 7.9 %copy-start.7 = (bf16[9216]{0:T(1024)(128)(2,1)S(1)}, bf16[9216]{0:T(1024)(128)(2,1)}, u32[]{:S(2)}) copy-start(bf16[9216]{0:T(1024)(128)(2,1)} %param.9) | copy-start | bytes 55300
  17.5 7.9 %collective-permute-start.6 = (f32[8,128]{1,0:T(8,128)S(1)}, f32[8,128]{1,0:T(8,128)S(1)}, u32[]{:S(2)}, u32[]{:S(2)}) collective-permute-start(f32[8,128]{1,0:T(8,128)S(1)} %slice.20), channel_id=1, source_target_pairs={{0,14},{4,10},{8,6},{12,2},{14,0},{10,4},{6,8},{2,12},{1,15},{5,11... | collective-permute-start | bytes 12296 | tf_op jit(solution)/shard_map/ppermute | solution.py:456
  23.3 5.5 %collective-permute-start.8 = (bf16[8,4608]{1,0:T(8,128)(2,1)S(1)}, bf16[8,4608]{1,0:T(8,128)(2,1)S(1)}, u32[]{:S(2)}, u32[]{:S(2)}) collective-permute-start(bf16[8,4608]{1,0:T(8,128)(2,1)S(1)} %slice.16), channel_id=1, source_target_pairs={{0,4},{4,8},{8,12},{12,14},{14,10},{10,6},{6,2},{2,0},{1,5},{5,9},... | collective-permute-start | bytes 221192 | tf_op jit(solution)/shard_map/ppermute | solution.py:55
  23.8 5.1 %collective-permute-start.9 = (bf16[8,4608]{1,0:T(8,128)(2,1)S(1)}, bf16[8,4608]{1,0:T(8,128)(2,1)S(1)}, u32[]{:S(2)}, u32[]{:S(2)}) collective-permute-start(bf16[8,4608]{1,0:T(8,128)(2,1)S(1)} %slice.17), channel_id=1, source_target_pairs={{0,2},{4,0},{8,4},{12,8},{14,12},{10,14},{6,10},{2,6},{1,3},{5,1},... | collective-permute-start | bytes 221192 | tf_op jit(solution)/shard_map/ppermute | solution.py:55
  25.4 3.4 %collective-permute-start.7 = (f32[64,128]{1,0:T(8,128)S(1)}, f32[64,128]{1,0:T(8,128)S(1)}, u32[]{:S(2)}, u32[]{:S(2)}) collective-permute-start(f32[64,128]{1,0:T(8,128)S(1)} %pad_maximum_fusion.1.refs_0_), channel_id=1, source_target_pairs={{0,1},{1,0},{2,3},{3,2},{4,5},{5,4},{6,7},{7,6},{8,9},{9,8},{10,11... | collective-permute-start | bytes 98312 | tf_op jit(solution)/shard_map/ppermute | solution.py:44
  28.8 10.2 %copy-start.6 = (s32[4]{0:T(128)S(1)}, s32[4]{0:T(128)}, u32[]{:S(2)}) copy-start(s32[4]{0:T(128)} %lengths.1) | copy-start | bytes 52
  38.5 1.6 %collective-permute-start.10 = (f32[8,4,1664]{2,1,0:T(4,128)S(1)}, f32[8,4,1664]{2,1,0:T(4,128)S(1)}, u32[]{:S(2)}, u32[]{:S(2)}) collective-permute-start(f32[8,4,1664]{2,1,0:T(4,128)S(1)} %get-tuple-element.51), channel_id=1, source_target_pairs={{0,1},{1,0},{2,3},{3,2},{4,5},{5,4},{6,7},{7,6},{8,9},{9,8},{10,11... | collective-permute-start | bytes 638984 | tf_op jit(solution)/shard_map/ppermute | solution.py:44
  40.8 17.4 %all-to-all-start = ((bf16[8,4,1664]{2,1,0:T(4,128)(2,1)}), bf16[8,4,1664]{2,1,0:T(4,128)(2,1)S(1)}, u32[]{:S(2)}, u32[]{:S(2)}) async-start(bf16[8,4,1664]{2,1,0:T(4,128)(2,1)} %add_convert_fusion.1.refs_1_.refs_2_), calls=%async_computation | async-start | bytes 212992 | tf_op jit(solution)/shard_map/all_to_all | solution.py:479
  47.8 2.9 %copy-start = (bf16[1536,2304]{1,0:T(8,128)(2,1)}, bf16[1536,2304]{1,0:T(8,128)(2,1)S(1)}, u32[]{:S(2)}) copy-start(bf16[1536,2304]{1,0:T(8,128)(2,1)S(1)} %load.12.refs_9_) | copy-start | bytes 21233668
  54.1 2.1 %copy-start.1 = (bf16[4,2048,256]{2,1,0:T(8,128)(2,1)}, bf16[4,2048,256]{2,1,0:T(8,128)(2,1)S(1)}, u32[]{:S(2)}) copy-start(bf16[4,2048,256]{2,1,0:T(8,128)(2,1)S(1)} %get-tuple-element.53.keys) | copy-start | bytes 12582916
  56.2 2.0 %copy-start.3 = (bf16[4,2048,256]{2,1,0:T(8,128)(2,1)}, bf16[4,2048,256]{2,1,0:T(8,128)(2,1)S(1)}, u32[]{:S(2)}) copy-start(bf16[4,2048,256]{2,1,0:T(8,128)(2,1)S(1)} %get-tuple-element.54.values) | copy-start | bytes 12582916
  58.2 2.2 %copy-start.2 = (bf16[4,2048,256]{2,1,0:T(8,128)(2,1)S(1)}, bf16[4,2048,256]{2,1,0:T(8,128)(2,1)}, u32[]{:S(2)}) copy-start(bf16[4,2048,256]{2,1,0:T(8,128)(2,1)} %copy-done.1) | copy-start | bytes 12582916
  60.4 2.2 %copy-start.4 = (bf16[4,2048,256]{2,1,0:T(8,128)(2,1)S(1)}, bf16[4,2048,256]{2,1,0:T(8,128)(2,1)}, u32[]{:S(2)}) copy-start(bf16[4,2048,256]{2,1,0:T(8,128)(2,1)} %copy-done.3) | copy-start | bytes 12582916
  66.0 1.3 %collective-permute-start.11 = (bf16[4,6144]{1,0:T(4,128)(2,1)S(1)}, bf16[4,6144]{1,0:T(4,128)(2,1)S(1)}, u32[]{:S(2)}, u32[]{:S(2)}) collective-permute-start(bf16[4,6144]{1,0:T(4,128)(2,1)S(1)} %get-tuple-element.56), channel_id=1, source_target_pairs={{0,1},{1,0},{2,3},{3,2},{4,5},{5,4},{6,7},{7,6},{8,9},{9,8},{10,11... | collective-permute-start | bytes 147464 | tf_op jit(solution)/shard_map/ppermute | solution.py:44
  67.4 5.3 %collective-permute-start.12 = (bf16[8,6144]{1,0:T(8,128)(2,1)S(1)}, bf16[8,6144]{1,0:T(8,128)(2,1)S(1)}, u32[]{:S(2)}, u32[]{:S(2)}) collective-permute-start(bf16[8,6144]{1,0:T(8,128)(2,1)S(1)} %pad_maximum_fusion.refs_1_.refs_0_), channel_id=1, source_target_pairs={{0,4},{4,8},{8,12},{12,14},{14,10},{10,6},{6,2},{2,0},{1,5},{5,9},... | collective-permute-start | bytes 294920 | tf_op jit(solution)/shard_map/ppermute | solution.py:55
  69.5 4.6 %collective-permute-start.13 = (bf16[8,6144]{1,0:T(8,128)(2,1)S(1)}, bf16[8,6144]{1,0:T(8,128)(2,1)S(1)}, u32[]{:S(2)}, u32[]{:S(2)}) collective-permute-start(bf16[8,6144]{1,0:T(8,128)(2,1)S(1)} %pad_maximum_fusion.refs_1_.refs_0_), channel_id=1, source_target_pairs={{0,2},{4,0},{8,4},{12,8},{14,12},{10,14},{6,10},{2,6},{1,3},{5,1},... | collective-permute-start | bytes 294920 | tf_op jit(solution)/shard_map/ppermute | solution.py:55
  74.1 5.3 %collective-permute-start.14 = (bf16[8,6144]{1,0:T(8,128)(2,1)S(1)}, bf16[8,6144]{1,0:T(8,128)(2,1)S(1)}, u32[]{:S(2)}, u32[]{:S(2)}) collective-permute-start(bf16[8,6144]{1,0:T(8,128)(2,1)S(1)} %collective-permute-done.12.refs_1_), channel_id=1, source_target_pairs={{0,4},{4,8},{8,12},{12,14},{14,10},{10,6},{6,2},{2,0},{1,5},{5,9},... | collective-permute-start | bytes 294920 | tf_op jit(solution)/shard_map/ppermute | solution.py:55
  75.5 4.6 %collective-permute-start.15 = (bf16[8,6144]{1,0:T(8,128)(2,1)S(1)}, bf16[8,6144]{1,0:T(8,128)(2,1)S(1)}, u32[]{:S(2)}, u32[]{:S(2)}) collective-permute-start(bf16[8,6144]{1,0:T(8,128)(2,1)S(1)} %collective-permute-done.13.refs_2_), channel_id=1, source_target_pairs={{0,2},{4,0},{8,4},{12,8},{14,12},{10,14},{6,10},{2,6},{1,3},{5,1},... | collective-permute-start | bytes 294920 | tf_op jit(solution)/shard_map/ppermute | solution.py:55
  76.1 15.7 %slice-start = ((s8[7077888]{0:T(1024)(128)(4,1)}), s8[4194304]{0:T(1024)(128)(4,1)S(1)}, s32[]{:S(2)}) async-start(s8[7077888]{0:T(1024)(128)(4,1)} %bitcast.3), calls=%async_computation.1 | async-start | bytes 8388608
  79.4 12.4 %slice-start.1 = ((s8[7077888]{0:T(1024)(128)(4,1)}), s8[2883584]{0:T(1024)(128)(4,1)S(1)}, s32[]{:S(2)}) async-start(s8[7077888]{0:T(1024)(128)(4,1)} %bitcast.3), calls=%async_computation.2 | async-start | bytes 5767168
  80.2 5.1 %collective-permute-start.16 = (bf16[8,6144]{1,0:T(8,128)(2,1)S(1)}, bf16[8,6144]{1,0:T(8,128)(2,1)S(1)}, u32[]{:S(2)}, u32[]{:S(2)}) collective-permute-start(bf16[8,6144]{1,0:T(8,128)(2,1)S(1)} %collective-permute-done.14.refs_1_.refs_3_), channel_id=1, source_target_pairs={{0,4},{4,8},{8,12},{12,14},{14,10},{10,6},{6,2},{2,0},{1,5},{5,9},... | collective-permute-start | bytes 294920 | tf_op jit(solution)/shard_map/ppermute | solution.py:55
  81.6 4.6 %collective-permute-start.17 = (bf16[8,6144]{1,0:T(8,128)(2,1)S(1)}, bf16[8,6144]{1,0:T(8,128)(2,1)S(1)}, u32[]{:S(2)}, u32[]{:S(2)}) collective-permute-start(bf16[8,6144]{1,0:T(8,128)(2,1)S(1)} %collective-permute-done.15.refs_2_.refs_4_), channel_id=1, source_target_pairs={{0,2},{4,0},{8,4},{12,8},{14,12},{10,14},{6,10},{2,6},{1,3},{5,1},... | collective-permute-start | bytes 294920 | tf_op jit(solution)/shard_map/ppermute | solution.py:55
  86.2 4.1 %collective-permute-start.18 = (bf16[8,3072]{1,0:T(8,128)(2,1)S(1)}, bf16[8,3072]{1,0:T(8,128)(2,1)S(1)}, u32[]{:S(2)}, u32[]{:S(2)}) collective-permute-start(bf16[8,3072]{1,0:T(8,128)(2,1)S(1)} %slice.18), channel_id=1, source_target_pairs={{0,4},{4,8},{8,12},{12,14},{14,10},{10,6},{6,2},{2,0},{1,5},{5,9},... | collective-permute-start | bytes 147464 | tf_op jit(solution)/shard_map/ppermute | solution.py:55
  87.7 4.1 %collective-permute-start.19 = (bf16[8,3072]{1,0:T(8,128)(2,1)S(1)}, bf16[8,3072]{1,0:T(8,128)(2,1)S(1)}, u32[]{:S(2)}, u32[]{:S(2)}) collective-permute-start(bf16[8,3072]{1,0:T(8,128)(2,1)S(1)} %slice.19), channel_id=1, source_target_pairs={{0,2},{4,0},{8,4},{12,8},{14,12},{10,14},{6,10},{2,6},{1,3},{5,1},... | collective-permute-start | bytes 147464 | tf_op jit(solution)/shard_map/ppermute | solution.py:55
  96.9 1.6 %collective-permute-start.20 = (f32[4,8,2304]{2,1,0:T(8,128)S(1)}, f32[4,8,2304]{2,1,0:T(8,128)S(1)}, u32[]{:S(2)}, u32[]{:S(2)}) collective-permute-start(f32[4,8,2304]{2,1,0:T(8,128)S(1)} %get-tuple-element.68), channel_id=1, source_target_pairs={{0,1},{1,0},{2,3},{3,2},{4,5},{5,4},{6,7},{7,6},{8,9},{9,8},{10,11... | collective-permute-start | bytes 884744 | tf_op jit(solution)/shard_map/ppermute | solution.py:44

commit v7 on v6

--- a/solution.py
+++ b/solution.py
@@ -234,15 +234,37 @@
     )(*sums, gain, *near, *far, *[in_vmem(w) for w in weights])
 
 
-def attend_kernel(lengths, arrived, cosine, sine, keys, values, mine, other, spread, held):
-    n, rows, stripe = arrived.shape
+def split_kernel(keep, got, *outs):
+    me = lax.axis_index("gx")
+    for d, out in enumerate(outs):
+        at = jnp.bitwise_xor(me, d)
+        out[...] = (keep[at] + got[at]).astype(jnp.bfloat16)
+
+
+def split(keep, got):
+    n = keep.shape[0]
+    return pl.pallas_call(
+        split_kernel,
+        out_shape=[jax.ShapeDtypeStruct(keep.shape[1:], jnp.bfloat16)] * n,
+        in_specs=[IN_VMEM] * 2,
+        out_specs=[IN_VMEM] * n,
+        compiler_params=pltpu.CompilerParams(vmem_limit_bytes=8 * MIB),
+        name="split",
+    )(keep, got)
+
+
+def attend_kernel(n, lengths, *refs):
+    arrived = refs[:n]
+    cosine, sine, keys, values, mine, other, spread, held = refs[n:]
+    rows, stripe = arrived[0].shape
+    me = lax.axis_index("gx")
     query_cols = stripe - 128
     side = lax.axis_index("gy")
     score_scale = 1.0 / math.sqrt(DH)
-    for i in range(n):
-        block = arrived[i].astype(jnp.float32)
+    for d in range(n):
+        block = arrived[d][...].astype(jnp.float32)
         for r in range(rows):
-            spread[r, i : i + 1, :] = block[r : r + 1, :]
+            spread[r, pl.ds(jnp.bitwise_xor(me, d), 1), :] = block[r : r + 1, :]
     for r in range(rows):
         given = spread[r]
         cos, sin = cosine[r : r + 1, :], sine[r : r + 1, :]
@@ -288,12 +310,13 @@
 
 
 def attend(lengths, arrived, cosine, sine, keys, values):
-    n, rows, stripe = arrived.shape
+    n = len(arrived)
+    rows, stripe = arrived[0].shape
     shape = jax.ShapeDtypeStruct((rows, HEADS * DH // 2), jnp.bfloat16)
     return pl.pallas_call(
-        attend_kernel,
+        lambda *refs: attend_kernel(n, *refs),
         out_shape=[shape, shape],
-        in_specs=[IN_SMEM] + [IN_VMEM] * 5,
+        in_specs=[IN_SMEM] + [IN_VMEM] * (n + 4),
         out_specs=[IN_VMEM] * 2,
         scratch_shapes=[
             pltpu.VMEM((rows, n, stripe), jnp.float32),
@@ -301,7 +324,7 @@
         ],
         compiler_params=pltpu.CompilerParams(vmem_limit_bytes=8 * MIB),
         name="attend",
-    )(lengths, arrived, cosine, sine, in_vmem(keys), in_vmem(values))
+    )(lengths, *arrived, cosine, sine, in_vmem(keys), in_vmem(values))
 
 
 def output_kernel(n, *refs):
@@ -311,18 +334,18 @@
     keep, give, total, placed = refs[-4:]
     rows = near[0].shape[0]
     half = far[0].shape[1]
-    depth = weights[0].shape[0]
-    for part, weight in enumerate(weights):
-        start = part * depth
-        cols = slice(start, start + depth)
-        last = slice(start % half, start % half + depth)
+    start = 0
+    for weight in weights:
+        cols = slice(start, start + weight.shape[0])
+        last = slice(start % half, start % half + weight.shape[0])
         x = [ref[:, cols] for ref in near] + [far[start // half][:, last]]
         x = jnp.concatenate([piece.astype(jnp.float32) for piece in x], axis=0)
         term = jnp.dot(x.astype(jnp.bfloat16), weight[...], preferred_element_type=jnp.float32)
-        if part == 0:
+        if start == 0:
             total[...] = term
         else:
             total[...] += term
+        start = cols.stop
     side = lax.axis_index("gy")
     for i, owner in enumerate(owners(n)):
         block = total[i * rows : (i + 1) * rows, :]
@@ -451,14 +474,17 @@
     for step in range(1, n // 2):
         arrived = near[1:][-2:]
         left, right = ring.step(left, right)
-        if step == 2:
-            sums = row_sums([activations, *arrived])
-            far_sums = lax.ppermute(sums[: activations.shape[0]], "gx", ring.across)
-        elif step > 2:
+        if step > 1:
             sums = row_sums(arrived, [sums])
         start = (step - 1) * piece
         weight = load(piece, [(query_weight, start, piece, 0)], arrived)
-        weight, (left, right) = before(weight, left, right)
+        if step == 1:
+            weight, (own,) = before(weight, activations)
+            sums = row_sums([own])
+            far_sums = lax.ppermute(sums, "gx", ring.across)
+            weight, (left, right, sums) = before(weight, left, right, sums)
+        else:
+            weight, (left, right) = before(weight, left, right)
         weights.append(weight)
         near += [left, right]
     half = width // 2
@@ -473,13 +499,16 @@
     sums = (sums, other_sums)
     gain = norm_gain.astype(jnp.float32)[None, :]
     keep, give = project(n, sums, gain, near, far, weights)
-    projected = (keep + swap_pair(give)).astype(jnp.bfloat16)
-
-    piece = output_weight.shape[0] // 4
-    arrived = lax.all_to_all(projected, "gx", split_axis=0, concat_axis=0, tiled=True)
-    keys, values = load_caches(cache_keys, cache_values, [projected])
-    weight = load(piece, [(output_weight, 0, piece, 0)], [projected])
-    weight, (arrived,) = before(weight, arrived)
+    blocks = split(keep, swap_pair(give))
+    arrived = [blocks[0]]
+    for d in range(1, n):
+        arrived.append(lax.ppermute(blocks[d], "gx", [(i, i ^ d) for i in range(n)]))
+    keys, values = load_caches(cache_keys, cache_values, [blocks[1]])
+    unit = output_weight.shape[0] // 12
+    sizes = [3 * unit, 3 * unit, 2 * unit, 2 * unit, 2 * unit]
+    weight = load(sizes[0], [(output_weight, 0, sizes[0], 0)], [blocks[1]])
+    keys, arrived = before(keys, *arrived)
+    weight, arrived = before(weight, *arrived)
     weights = [weight]
     mine, other = attend(cache_lengths, arrived, cosine, sine, keys, values)
     shard = jnp.concatenate([mine, swap_pair(other)], axis=0)
@@ -489,13 +518,15 @@
     for step in range(1, n // 2):
         arrived = near[-2:]
         left, right = ring.step(left, right)
-        start = step * piece
-        weight = load(piece, [(output_weight, start, piece, 0)], arrived)
+        weight = load(sizes[step], [(output_weight, sum(sizes[:step]), sizes[step], 0)], arrived)
         weight, (left, right) = before(weight, left, right)
         weights.append(weight)
         near += [left, right]
     half = shard.shape[1] // 2
     far = ring.step(left[:, :half], right[:, half:])
+    weight = load(sizes[-1], [(output_weight, sum(sizes[:-1]), sizes[-1], 0)], [left, right])
+    weight, far = before(weight, *far)
+    weights.append(weight)
     keep, give = output_project(n, near, far, weights)
     out = (keep + swap_pair(give)).astype(jnp.bfloat16)
     return out.reshape(-1, out.shape[-1])

time: 99.5 us -> 93.1 us (0.936)
  local copies, waits for them, and re-layouts: 11.3 us -> 0.03 us
  starting transfers between devices: 24.1 us -> 31.6 us
  waiting for transfers between devices: 14.4 us -> 11.7 us
  Pallas kernels: 47.4 us -> 48.4 us
    unnamed x20 -> x6, local copies, waits for them, and re-layouts: 11.3 us -> 0.01 us
    ppermute x1 -> x8, starting transfers between devices: 2.33 us -> 13.6 us  [the longest x7 11.3 us: on_device(): lax.ppermute(blocks[d], 'gx', [(i, i ^ d) for i in range(n)])]
    all_to_all x1 -> x0, starting transfers between devices: 3.7 us -> none  [on_device(): lax.all_to_all(projected, 'gx', split_axis=0, concat_axis=0, tiled=True)]
    ppermute x8, starting transfers between devices: 13.1 us -> 10.7 us  [step(): lax.ppermute(left, 'gx', self.onward)]
    ppermute x8, starting transfers between devices: 4.26 us -> 6.56 us  [step(): lax.ppermute(right, 'gx', self.back)]
    ppermute x8, waiting for transfers between devices: 2.94 us -> 1.23 us  [step(): lax.ppermute(left, 'gx', self.onward)]
    ppermute x8, waiting for transfers between devices: 7.7 us -> 6.59 us  [step(): lax.ppermute(right, 'gx', self.back)]
    pallas_call x8 -> x9, Pallas kernels: 25.3 us -> 26 us  [load(): pl.pallas_call(lambda *refs: load_kernel([job[1:] for job in jobs], *refs...]
  transfers between devices with their start and end apart: 22 -> 28, of which waited for: 11 -> 11; matrix products, arithmetic and copies ran while one was open for 0% -> 0% of each run, Pallas kernels for 30% -> 33%
where the time goes in v7:
time: 93.1 us; the launch traced here: 92.9 us
  Pallas kernels  48.4 us (52%)
  starting transfers between devices  31.6 us (34%)
  waiting for transfers between devices  11.7 us (13%)
    pallas_call x9, Pallas kernels, load(): pl.pallas_call(lambda *refs: load_kernel([job[1:] for job in jobs], *refs...  26 us
    ppermute x7, starting transfers between devices, on_device(): lax.ppermute(blocks[d], 'gx', [(i, i ^ d) for i in range(n)])  11.3 us
    ppermute x8, starting transfers between devices, step(): lax.ppermute(left, 'gx', self.onward)  10.7 us
    pallas_call x1, Pallas kernels, project(): pl.pallas_call(lambda *refs: project_kernel(n, *refs), out_shape=[shape,...  9.64 us
    ppermute x8, waiting for transfers between devices, step(): lax.ppermute(right, 'gx', self.back)  6.59 us
    ppermute x8, starting transfers between devices, step(): lax.ppermute(right, 'gx', self.back)  6.56 us
    pallas_call x1, Pallas kernels, output_project(): pl.pallas_call(lambda *refs: output_kernel(n, *refs), out_shape=[shape, s...  5.04 us
    ppermute x4, waiting for transfers between devices, swap_pair(): return lax.ppermute(x, 'gy', [(0, 1), (1, 0)])  3.88 us
  transfers between devices with their start and end apart: 28, of which 11 were waited for; matrix products, arithmetic and copies ran while one was open for 0% of the time, Pallas kernels for 33%

profile of v7, /device:TPU:0, one launch (start us, length us, event | category | flops | bytes accessed | tf_op | source)
XLA Modules:
  0.0 92.9 jit_solution(462891431409782188)
XLA Ops:
  0.0 3.0 %collective-permute-start = (bf16[8,9216]{1,0:T(8,128)(2,1)}, bf16[8,9216]{1,0:T(8,128)(2,1)S(1)}, u32[]{:S(2)}, u32[]{:S(2)}) collective-permute-start(bf16[8,9216]{1,0:T(8,128)(2,1)} %refs_3_.1), channel_id=1, source_target_pairs={{0,4},{4,8},{8,12},{12,14},{14,10},{10,6},{6,2},{2,0},{1,5},{5,9},... | collective-permute-start | bytes 442376 | tf_op jit(solution)/shard_map/ppermute | solution.py:55
  3.0 3.1 %load.9.refs_12_ = bf16[384,9216]{1,0:T(8,128)(2,1)S(1)} custom-call(bf16[1536,9216]{1,0:T(8,128)(2,1)} %refs_0_.15), custom_call_target="tpu_custom_call" | custom-call | tf_op jit(solution)/shard_map/load/pallas_call | solution.py:103
  6.3 0.8 collective-permute-done.refs_1_.refs_4_
  7.1 1.4 %collective-permute-done.1.refs_2_.refs_5_ = bf16[8,9216]{1,0:T(8,128)(2,1)S(1)} collective-permute-done((bf16[8,9216]{1,0:T(8,128)(2,1)}, bf16[8,9216]{1,0:T(8,128)(2,1)S(1)}, u32[]{:S(2)}, u32[]{:S(2)}) %collective-permute-start.1) | collective-permute-done | bytes 147488 | tf_op jit(solution)/shard_map/ppermute | solution.py:55
  8.5 1.6 %collective-permute-start.2 = (bf16[8,9216]{1,0:T(8,128)(2,1)S(1)}, bf16[8,9216]{1,0:T(8,128)(2,1)S(1)}, u32[]{:S(2)}, u32[]{:S(2)}) collective-permute-start(bf16[8,9216]{1,0:T(8,128)(2,1)S(1)} %collective-permute-done.refs_1_.refs_4_), channel_id=1, source_target_pairs={{0,4},{4,8},{8,12},{12,14},{14,10},{10,6},{6,2},{2,0},{1,5},{5,9},... | collective-permute-start | bytes 442376 | tf_op jit(solution)/shard_map/ppermute | solution.py:55
  10.1 0.4 collective-permute-start.3
  10.6 3.1 %load.10.refs_13_ = bf16[384,9216]{1,0:T(8,128)(2,1)S(1)} custom-call(bf16[1536,9216]{1,0:T(8,128)(2,1)} %refs_0_.15, bf16[8,9216]{1,0:T(8,128)(2,1)S(1)} %collective-permute-done.refs_1_.refs_4_, bf16[8,9216]{1,0:T(8,128)(2,1)S(1)} %collective-permute-done.1.refs_2_.refs_5_), custom_call_target="tpu_custom_call" | custom-call | tf_op jit(solution)/shard_map/load/pallas_call | solution.py:103
  13.7 1.6 %collective-permute-done.3.refs_2_.refs_7_ = bf16[8,9216]{1,0:T(8,128)(2,1)S(1)} collective-permute-done((bf16[8,9216]{1,0:T(8,128)(2,1)S(1)}, bf16[8,9216]{1,0:T(8,128)(2,1)S(1)}, u32[]{:S(2)}, u32[]{:S(2)}) %collective-permute-start.3) | collective-permute-done | bytes 147488 | tf_op jit(solution)/shard_map/ppermute | solution.py:55
  15.3 1.6 %collective-permute-start.4 = (bf16[8,9216]{1,0:T(8,128)(2,1)S(1)}, bf16[8,9216]{1,0:T(8,128)(2,1)S(1)}, u32[]{:S(2)}, u32[]{:S(2)}) collective-permute-start(bf16[8,9216]{1,0:T(8,128)(2,1)S(1)} %collective-permute-done.2.refs_1_.refs_6_), channel_id=1, source_target_pairs={{0,4},{4,8},{8,12},{12,14},{14,10},{10,6},{6,2},{2,0},{1,5},{5,9},... | collective-permute-start | bytes 442376 | tf_op jit(solution)/shard_map/ppermute | solution.py:55
  16.8 0.4 collective-permute-start.5
  17.3 2.3 %collective-permute-start.6 = (f32[8,128]{1,0:T(8,128)S(1)}, f32[8,128]{1,0:T(8,128)S(1)}, u32[]{:S(2)}, u32[]{:S(2)}) collective-permute-start(f32[8,128]{1,0:T(8,128)S(1)} %row_sums.4.refs_0_), channel_id=1, source_target_pairs={{0,14},{4,10},{8,6},{12,2},{14,0},{10,4},{6,8},{2,12},{1,15},{5,11... | collective-permute-start | bytes 12296 | tf_op jit(solution)/shard_map/ppermute | solution.py:484
  19.8 3.1 %load.11.refs_14_ = bf16[384,9216]{1,0:T(8,128)(2,1)S(1)} custom-call(bf16[1536,9216]{1,0:T(8,128)(2,1)} %refs_0_.15, bf16[8,9216]{1,0:T(8,128)(2,1)S(1)} %collective-permute-done.2.refs_1_.refs_6_, bf16[8,9216]{1,0:T(8,128)(2,1)S(1)} %collective-permute-done.3.refs_2_.refs_7_), custom_call_target="tpu_custom_call" | custom-call | tf_op jit(solution)/shard_map/load/pallas_call | solution.py:103
  23.3 0.6 collective-permute-start.8
  23.8 1.5 %collective-permute-start.9 = (bf16[8,4608]{1,0:T(8,128)(2,1)S(1)}, bf16[8,4608]{1,0:T(8,128)(2,1)S(1)}, u32[]{:S(2)}, u32[]{:S(2)}) collective-permute-start(bf16[8,4608]{1,0:T(8,128)(2,1)S(1)} %slice.13), channel_id=1, source_target_pairs={{0,2},{4,0},{8,4},{12,8},{14,12},{10,14},{6,10},{2,6},{1,3},{5,1},... | collective-permute-start | bytes 221192 | tf_op jit(solution)/shard_map/ppermute | solution.py:55
  25.3 3.4 %load.12.refs_15_ = bf16[512,9216]{1,0:T(8,128)(2,1)S(1)} custom-call(bf16[1536,9216]{1,0:T(8,128)(2,1)} %refs_0_.15, bf16[64,9216]{1,0:T(8,128)(2,1)} %refs_1_.2, f32[56,128]{1,0:T(8,128)S(1)} %row_sums.7.refs_2_), custom_call_target="tpu_custom_call" | custom-call | tf_op jit(solution)/shard_map/load/pallas_call | solution.py:103
  28.8 9.6 %project.1 = (f32[8,4,1664]{2,1,0:T(4,128)S(1)}, f32[8,4,1664]{2,1,0:T(4,128)S(1)}) custom-call(f32[64,128]{1,0:T(8,128)S(1)} %pad_maximum_fusion.1.refs_0_, f32[64,128]{1,0:T(8,128)S(1)} %collective-permute-done.7.refs_1_, f32[1,9216]{1,0:T(1,128)S(1)} %bitcast.3, bf16[8,9216]{1,0:T(8,128)(2,1)S(1)} %copy-done, ...), custom_call_target="tpu_custom_call" | custom-call | tf_op jit(solution)/shard_map/project/pallas_call | solution.py:223
  38.4 0.6 collective-permute-start.10
  39.0 1.1 %collective-permute-done.10.got = f32[8,4,1664]{2,1,0:T(4,128)S(1)} collective-permute-done((f32[8,4,1664]{2,1,0:T(4,128)S(1)}, f32[8,4,1664]{2,1,0:T(4,128)S(1)}, u32[]{:S(2)}, u32[]{:S(2)}) %collective-permute-start.10) | collective-permute-done | bytes 213024 | tf_op jit(solution)/shard_map/ppermute | solution.py:44
  40.1 1.7 %collective-permute-start.11 = (bf16[4,1664]{1,0:T(4,128)(2,1)S(1)}, bf16[4,1664]{1,0:T(4,128)(2,1)S(1)}, u32[]{:S(2)}, u32[]{:S(2)}) collective-permute-start(bf16[4,1664]{1,0:T(4,128)(2,1)S(1)} %get-tuple-element.85.refs_1_.refs_2_), channel_id=1, source_target_pairs={{0,2},{2,0},{4,6},{6,4},{8,10},{10,8},{12,14},{14,12},{1,3},{3,1},... | collective-permute-start | bytes 39944 | tf_op jit(solution)/shard_map/ppermute | solution.py:505
  41.8 0.7 collective-permute-start.12
  42.5 1.2 %collective-permute-start.13 = (bf16[4,1664]{1,0:T(4,128)(2,1)S(1)}, bf16[4,1664]{1,0:T(4,128)(2,1)S(1)}, u32[]{:S(2)}, u32[]{:S(2)}) collective-permute-start(bf16[4,1664]{1,0:T(4,128)(2,1)S(1)} %get-tuple-element.89), channel_id=1, source_target_pairs={{0,6},{2,4},{4,2},{6,0},{8,14},{10,12},{12,10},{14,8},{1,7},{3,5},... | collective-permute-start | bytes 39944 | tf_op jit(solution)/shard_map/ppermute | solution.py:505
  43.8 0.7 collective-permute-start.14
  44.5 3.3 %collective-permute-start.15 = (bf16[4,1664]{1,0:T(4,128)(2,1)S(1)}, bf16[4,1664]{1,0:T(4,128)(2,1)S(1)}, u32[]{:S(2)}, u32[]{:S(2)}) collective-permute-start(bf16[4,1664]{1,0:T(4,128)(2,1)S(1)} %get-tuple-element.91), channel_id=1, source_target_pairs={{0,10},{2,8},{4,14},{6,12},{8,2},{10,0},{12,6},{14,4},{1,11},{3,9}... | collective-permute-start | bytes 39944 | tf_op jit(solution)/shard_map/ppermute | solution.py:505
  47.7 1.4 %collective-permute-start.16 = (bf16[4,1664]{1,0:T(4,128)(2,1)S(1)}, bf16[4,1664]{1,0:T(4,128)(2,1)S(1)}, u32[]{:S(2)}, u32[]{:S(2)}) collective-permute-start(bf16[4,1664]{1,0:T(4,128)(2,1)S(1)} %get-tuple-element.92), channel_id=1, source_target_pairs={{0,12},{2,14},{4,8},{6,10},{8,4},{10,6},{12,0},{14,2},{1,13},{3,15... | collective-permute-start | bytes 39944 | tf_op jit(solution)/shard_map/ppermute | solution.py:505
  49.1 2.3 %collective-permute-start.17 = (bf16[4,1664]{1,0:T(4,128)(2,1)S(1)}, bf16[4,1664]{1,0:T(4,128)(2,1)S(1)}, u32[]{:S(2)}, u32[]{:S(2)}) collective-permute-start(bf16[4,1664]{1,0:T(4,128)(2,1)S(1)} %get-tuple-element.93), channel_id=1, source_target_pairs={{0,14},{2,12},{4,10},{6,8},{8,6},{10,4},{12,2},{14,0},{1,15},{3,13... | collective-permute-start | bytes 39944 | tf_op jit(solution)/shard_map/ppermute | solution.py:505
  51.5 3.1 %load.13.refs_9_ = bf16[1536,2304]{1,0:T(8,128)(2,1)S(1)} custom-call(bf16[6144,2304]{1,0:T(8,128)(2,1)} %refs_0_.22, bf16[4,1664]{1,0:T(4,128)(2,1)S(1)} %get-tuple-element.85.refs_1_.refs_2_), custom_call_target="tpu_custom_call" | custom-call | tf_op jit(solution)/shard_map/load/pallas_call | solution.py:103
  54.7 3.5 %load_caches.1 = (bf16[4,2048,256]{2,1,0:T(8,128)(2,1)S(1)}, bf16[4,2048,256]{2,1,0:T(8,128)(2,1)S(1)}) custom-call(bf16[4,2048,256]{2,1,0:T(8,128)(2,1)} %refs_0_.17, bf16[4,2048,256]{2,1,0:T(8,128)(2,1)} %refs_1_.3, bf16[4,1664]{1,0:T(4,128)(2,1)S(1)} %get-tuple-element.85.refs_1_.refs_2_), custom_call_target="tpu_custom_call" | custom-call | tf_op jit(solution)/shard_map/load_caches/pallas_call | solution.py:126
  58.2 3.5 %attend.1 = (bf16[4,6144]{1,0:T(4,128)(2,1)S(1)}, bf16[4,6144]{1,0:T(4,128)(2,1)S(1)}) custom-call(s32[4]{0:T(128)S(1)} %copy-done.1, bf16[4,1664]{1,0:T(4,128)(2,1)S(1)} %get-tuple-element.102.refs_1_, bf16[4,1664]{1,0:T(4,128)(2,1)S(1)} %collective-permute-done.11.refs_2_, bf16[4,1664]{1,0:T(4,128)(2,1)S(1)} %collective-permute-done.12.refs_3_, ...), custom_call_target="tpu_custom_call" | custom-call | tf_op jit(solution)/shard_map/attend/pallas_call | solution.py:316
  61.8 1.2 %collective-permute-done.18 = bf16[4,6144]{1,0:T(4,128)(2,1)S(1)} collective-permute-done((bf16[4,6144]{1,0:T(4,128)(2,1)S(1)}, bf16[4,6144]{1,0:T(4,128)(2,1)S(1)}, u32[]{:S(2)}, u32[]{:S(2)}) %collective-permute-start.18) | collective-permute-done | bytes 49184 | tf_op jit(solution)/shard_map/ppermute | solution.py:44
  63.1 2.0 %collective-permute-start.20 = (bf16[8,6144]{1,0:T(8,128)(2,1)S(1)}, bf16[8,6144]{1,0:T(8,128)(2,1)S(1)}, u32[]{:S(2)}, u32[]{:S(2)}) collective-permute-start(bf16[8,6144]{1,0:T(8,128)(2,1)S(1)} %pad_maximum_fusion.refs_1_.refs_0_), channel_id=1, source_target_pairs={{0,2},{4,0},{8,4},{12,8},{14,12},{10,14},{6,10},{2,6},{1,3},{5,1},... | collective-permute-start | bytes 294920 | tf_op jit(solution)/shard_map/ppermute | solution.py:55
  65.1 3.1 %load.14.refs_10_ = bf16[1536,2304]{1,0:T(8,128)(2,1)S(1)} custom-call(bf16[6144,2304]{1,0:T(8,128)(2,1)} %refs_0_.22, bf16[8,6144]{1,0:T(8,128)(2,1)S(1)} %pad_maximum_fusion.refs_1_.refs_0_), custom_call_target="tpu_custom_call" | custom-call | tf_op jit(solution)/shard_map/load/pallas_call | solution.py:103
  68.2 0.5 collective-permute-start.21
  68.8 1.6 %collective-permute-start.22 = (bf16[8,6144]{1,0:T(8,128)(2,1)S(1)}, bf16[8,6144]{1,0:T(8,128)(2,1)S(1)}, u32[]{:S(2)}, u32[]{:S(2)}) collective-permute-start(bf16[8,6144]{1,0:T(8,128)(2,1)S(1)} %collective-permute-done.20.refs_2_), channel_id=1, source_target_pairs={{0,2},{4,0},{8,4},{12,8},{14,12},{10,14},{6,10},{2,6},{1,3},{5,1},... | collective-permute-start | bytes 294920 | tf_op jit(solution)/shard_map/ppermute | solution.py:55
  70.3 2.4 %load.15.refs_11_ = bf16[1024,2304]{1,0:T(8,128)(2,1)S(1)} custom-call(bf16[6144,2304]{1,0:T(8,128)(2,1)} %refs_0_.22, bf16[8,6144]{1,0:T(8,128)(2,1)S(1)} %collective-permute-done.19.refs_1_, bf16[8,6144]{1,0:T(8,128)(2,1)S(1)} %collective-permute-done.20.refs_2_), custom_call_target="tpu_custom_call" | custom-call | tf_op jit(solution)/shard_map/load/pallas_call | solution.py:103
  72.7 0.2 collective-permute-done.21.refs_1_.refs_3_
  72.9 0.5 collective-permute-done.22.refs_2_.refs_4_
  73.4 1.8 %collective-permute-start.23 = (bf16[8,6144]{1,0:T(8,128)(2,1)S(1)}, bf16[8,6144]{1,0:T(8,128)(2,1)S(1)}, u32[]{:S(2)}, u32[]{:S(2)}) collective-permute-start(bf16[8,6144]{1,0:T(8,128)(2,1)S(1)} %collective-permute-done.21.refs_1_.refs_3_), channel_id=1, source_target_pairs={{0,4},{4,8},{8,12},{12,14},{14,10},{10,6},{6,2},{2,0},{1,5},{5,9},... | collective-permute-start | bytes 294920 | tf_op jit(solution)/shard_map/ppermute | solution.py:55
  75.2 0.2 collective-permute-start.24
  75.4 2.4 %load.16.refs_12_ = bf16[1024,2304]{1,0:T(8,128)(2,1)S(1)} custom-call(bf16[6144,2304]{1,0:T(8,128)(2,1)} %refs_0_.22, bf16[8,6144]{1,0:T(8,128)(2,1)S(1)} %collective-permute-done.21.refs_1_.refs_3_, bf16[8,6144]{1,0:T(8,128)(2,1)S(1)} %collective-permute-done.22.refs_2_.refs_4_), custom_call_target="tpu_custom_call" | custom-call | tf_op jit(solution)/shard_map/load/pallas_call | solution.py:103
  77.8 0.2 collective-permute-done.23.refs_1_.refs_5_
  78.0 1.8 %collective-permute-done.24.refs_2_.refs_6_ = bf16[8,6144]{1,0:T(8,128)(2,1)S(1)} collective-permute-done((bf16[8,6144]{1,0:T(8,128)(2,1)S(1)}, bf16[8,6144]{1,0:T(8,128)(2,1)S(1)}, u32[]{:S(2)}, u32[]{:S(2)}) %collective-permute-start.24) | collective-permute-done | bytes 98336 | tf_op jit(solution)/shard_map/ppermute | solution.py:55
  79.8 1.7 %collective-permute-start.25 = (bf16[8,3072]{1,0:T(8,128)(2,1)S(1)}, bf16[8,3072]{1,0:T(8,128)(2,1)S(1)}, u32[]{:S(2)}, u32[]{:S(2)}) collective-permute-start(bf16[8,3072]{1,0:T(8,128)(2,1)S(1)} %slice.14), channel_id=1, source_target_pairs={{0,4},{4,8},{8,12},{12,14},{14,10},{10,6},{6,2},{2,0},{1,5},{5,9},... | collective-permute-start | bytes 147464 | tf_op jit(solution)/shard_map/ppermute | solution.py:55
  81.4 0.4 collective-permute-start.26
  81.8 2.4 %load.17.refs_13_ = bf16[1024,2304]{1,0:T(8,128)(2,1)S(1)} custom-call(bf16[6144,2304]{1,0:T(8,128)(2,1)} %refs_0_.22, bf16[8,6144]{1,0:T(8,128)(2,1)S(1)} %collective-permute-done.23.refs_1_.refs_5_, bf16[8,6144]{1,0:T(8,128)(2,1)S(1)} %collective-permute-done.24.refs_2_.refs_6_), custom_call_target="tpu_custom_call" | custom-call | tf_op jit(solution)/shard_map/load/pallas_call | solution.py:103
  84.2 1.3 %collective-permute-done.26.refs_8_ = bf16[8,3072]{1,0:T(8,128)(2,1)S(1)} collective-permute-done((bf16[8,3072]{1,0:T(8,128)(2,1)S(1)}, bf16[8,3072]{1,0:T(8,128)(2,1)S(1)}, u32[]{:S(2)}, u32[]{:S(2)}) %collective-permute-start.26) | collective-permute-done | bytes 49184 | tf_op jit(solution)/shard_map/ppermute | solution.py:55
  85.5 5.0 %output_project.1 = (f32[4,8,2304]{2,1,0:T(8,128)S(1)}, f32[4,8,2304]{2,1,0:T(8,128)S(1)}) custom-call(bf16[8,6144]{1,0:T(8,128)(2,1)S(1)} %pad_maximum_fusion.refs_1_.refs_0_, bf16[8,6144]{1,0:T(8,128)(2,1)S(1)} %collective-permute-done.19.refs_1_, bf16[8,6144]{1,0:T(8,128)(2,1)S(1)} %collective-permute-done.20.refs_2_, ...), custom_call_target="tpu_custom_call" | custom-call | tf_op jit(solution)/shard_map/output_project/pallas_call | solution.py:361
  90.7 1.6 %collective-permute-done.27 = f32[4,8,2304]{2,1,0:T(8,128)S(1)} collective-permute-done((f32[4,8,2304]{2,1,0:T(8,128)S(1)}, f32[4,8,2304]{2,1,0:T(8,128)S(1)}, u32[]{:S(2)}, u32[]{:S(2)}) %collective-permute-start.27) | collective-permute-done | bytes 294944 | tf_op jit(solution)/shard_map/ppermute | solution.py:44
  92.2 0.7 fusion
  (43 shorter events, 1.2 us)
Async XLA Ops:
  0.0 6.1 %copy-start = (bf16[8,9216]{1,0:T(8,128)(2,1)S(1)}, bf16[8,9216]{1,0:T(8,128)(2,1)}, u32[]{:S(2)}) copy-start(bf16[8,9216]{1,0:T(8,128)(2,1)} %refs_3_.1) | copy-start | bytes 442372
  0.0 7.1 %collective-permute-start = (bf16[8,9216]{1,0:T(8,128)(2,1)}, bf16[8,9216]{1,0:T(8,128)(2,1)S(1)}, u32[]{:S(2)}, u32[]{:S(2)}) collective-permute-start(bf16[8,9216]{1,0:T(8,128)(2,1)} %refs_3_.1), channel_id=1, source_target_pairs={{0,4},{4,8},{8,12},{12,14},{14,10},{10,6},{6,2},{2,0},{1,5},{5,9},... | collective-permute-start | bytes 442376 | tf_op jit(solution)/shard_map/ppermute | solution.py:55
  3.0 5.5 %collective-permute-start.1 = (bf16[8,9216]{1,0:T(8,128)(2,1)}, bf16[8,9216]{1,0:T(8,128)(2,1)S(1)}, u32[]{:S(2)}, u32[]{:S(2)}) collective-permute-start(bf16[8,9216]{1,0:T(8,128)(2,1)} %refs_3_.1), channel_id=1, source_target_pairs={{0,2},{4,0},{8,4},{12,8},{14,12},{10,14},{6,10},{2,6},{1,3},{5,1},... | collective-permute-start | bytes 442376 | tf_op jit(solution)/shard_map/ppermute | solution.py:55
  8.5 5.1 %collective-permute-start.2 = (bf16[8,9216]{1,0:T(8,128)(2,1)S(1)}, bf16[8,9216]{1,0:T(8,128)(2,1)S(1)}, u32[]{:S(2)}, u32[]{:S(2)}) collective-permute-start(bf16[8,9216]{1,0:T(8,128)(2,1)S(1)} %collective-permute-done.refs_1_.refs_4_), channel_id=1, source_target_pairs={{0,4},{4,8},{8,12},{12,14},{14,10},{10,6},{6,2},{2,0},{1,5},{5,9},... | collective-permute-start | bytes 442376 | tf_op jit(solution)/shard_map/ppermute | solution.py:55
  10.1 5.1 %collective-permute-start.3 = (bf16[8,9216]{1,0:T(8,128)(2,1)S(1)}, bf16[8,9216]{1,0:T(8,128)(2,1)S(1)}, u32[]{:S(2)}, u32[]{:S(2)}) collective-permute-start(bf16[8,9216]{1,0:T(8,128)(2,1)S(1)} %collective-permute-done.1.refs_2_.refs_5_), channel_id=1, source_target_pairs={{0,2},{4,0},{8,4},{12,8},{14,12},{10,14},{6,10},{2,6},{1,3},{5,1},... | collective-permute-start | bytes 442376 | tf_op jit(solution)/shard_map/ppermute | solution.py:55
  15.3 7.8 %collective-permute-start.4 = (bf16[8,9216]{1,0:T(8,128)(2,1)S(1)}, bf16[8,9216]{1,0:T(8,128)(2,1)S(1)}, u32[]{:S(2)}, u32[]{:S(2)}) collective-permute-start(bf16[8,9216]{1,0:T(8,128)(2,1)S(1)} %collective-permute-done.2.refs_1_.refs_6_), channel_id=1, source_target_pairs={{0,4},{4,8},{8,12},{12,14},{14,10},{10,6},{6,2},{2,0},{1,5},{5,9},... | collective-permute-start | bytes 442376 | tf_op jit(solution)/shard_map/ppermute | solution.py:55
  16.8 6.2 %collective-permute-start.5 = (bf16[8,9216]{1,0:T(8,128)(2,1)S(1)}, bf16[8,9216]{1,0:T(8,128)(2,1)S(1)}, u32[]{:S(2)}, u32[]{:S(2)}) collective-permute-start(bf16[8,9216]{1,0:T(8,128)(2,1)S(1)} %collective-permute-done.3.refs_2_.refs_7_), channel_id=1, source_target_pairs={{0,2},{4,0},{8,4},{12,8},{14,12},{10,14},{6,10},{2,6},{1,3},{5,1},... | collective-permute-start | bytes 442376 | tf_op jit(solution)/shard_map/ppermute | solution.py:55
  17.3 8.0 %collective-permute-start.6 = (f32[8,128]{1,0:T(8,128)S(1)}, f32[8,128]{1,0:T(8,128)S(1)}, u32[]{:S(2)}, u32[]{:S(2)}) collective-permute-start(f32[8,128]{1,0:T(8,128)S(1)} %row_sums.4.refs_0_), channel_id=1, source_target_pairs={{0,14},{4,10},{8,6},{12,2},{14,0},{10,4},{6,8},{2,12},{1,15},{5,11... | collective-permute-start | bytes 12296 | tf_op jit(solution)/shard_map/ppermute | solution.py:484
  19.8 5.6 %copy-start.2 = (bf16[9216]{0:T(1024)(128)(2,1)S(1)}, bf16[9216]{0:T(1024)(128)(2,1)}, u32[]{:S(2)}) copy-start(bf16[9216]{0:T(1024)(128)(2,1)} %param.9) | copy-start | bytes 55300
  23.3 5.5 %collective-permute-start.8 = (bf16[8,4608]{1,0:T(8,128)(2,1)S(1)}, bf16[8,4608]{1,0:T(8,128)(2,1)S(1)}, u32[]{:S(2)}, u32[]{:S(2)}) collective-permute-start(bf16[8,4608]{1,0:T(8,128)(2,1)S(1)} %slice.12), channel_id=1, source_target_pairs={{0,4},{4,8},{8,12},{12,14},{14,10},{10,6},{6,2},{2,0},{1,5},{5,9},... | collective-permute-start | bytes 221192 | tf_op jit(solution)/shard_map/ppermute | solution.py:55
  23.8 4.9 %collective-permute-start.9 = (bf16[8,4608]{1,0:T(8,128)(2,1)S(1)}, bf16[8,4608]{1,0:T(8,128)(2,1)S(1)}, u32[]{:S(2)}, u32[]{:S(2)}) collective-permute-start(bf16[8,4608]{1,0:T(8,128)(2,1)S(1)} %slice.13), channel_id=1, source_target_pairs={{0,2},{4,0},{8,4},{12,8},{14,12},{10,14},{6,10},{2,6},{1,3},{5,1},... | collective-permute-start | bytes 221192 | tf_op jit(solution)/shard_map/ppermute | solution.py:55
  25.3 3.4 %collective-permute-start.7 = (f32[64,128]{1,0:T(8,128)S(1)}, f32[64,128]{1,0:T(8,128)S(1)}, u32[]{:S(2)}, u32[]{:S(2)}) collective-permute-start(f32[64,128]{1,0:T(8,128)S(1)} %pad_maximum_fusion.1.refs_0_), channel_id=1, source_target_pairs={{0,1},{1,0},{2,3},{3,2},{4,5},{5,4},{6,7},{7,6},{8,9},{9,8},{10,11... | collective-permute-start | bytes 98312 | tf_op jit(solution)/shard_map/ppermute | solution.py:44
  28.8 13.8 %copy-start.1 = (s32[4]{0:T(128)S(1)}, s32[4]{0:T(128)}, u32[]{:S(2)}) copy-start(s32[4]{0:T(128)} %refs_0_.18) | copy-start | bytes 52
  38.4 1.6 %collective-permute-start.10 = (f32[8,4,1664]{2,1,0:T(4,128)S(1)}, f32[8,4,1664]{2,1,0:T(4,128)S(1)}, u32[]{:S(2)}, u32[]{:S(2)}) collective-permute-start(f32[8,4,1664]{2,1,0:T(4,128)S(1)} %get-tuple-element.84), channel_id=1, source_target_pairs={{0,1},{1,0},{2,3},{3,2},{4,5},{5,4},{6,7},{7,6},{8,9},{9,8},{10,11... | collective-permute-start | bytes 638984 | tf_op jit(solution)/shard_map/ppermute | solution.py:44
  40.1 7.6 %collective-permute-start.11 = (bf16[4,1664]{1,0:T(4,128)(2,1)S(1)}, bf16[4,1664]{1,0:T(4,128)(2,1)S(1)}, u32[]{:S(2)}, u32[]{:S(2)}) collective-permute-start(bf16[4,1664]{1,0:T(4,128)(2,1)S(1)} %get-tuple-element.85.refs_1_.refs_2_), channel_id=1, source_target_pairs={{0,2},{2,0},{4,6},{6,4},{8,10},{10,8},{12,14},{14,12},{1,3},{3,1},... | collective-permute-start | bytes 39944 | tf_op jit(solution)/shard_map/ppermute | solution.py:505
  41.8 7.3 %collective-permute-start.12 = (bf16[4,1664]{1,0:T(4,128)(2,1)S(1)}, bf16[4,1664]{1,0:T(4,128)(2,1)S(1)}, u32[]{:S(2)}, u32[]{:S(2)}) collective-permute-start(bf16[4,1664]{1,0:T(4,128)(2,1)S(1)} %get-tuple-element.88), channel_id=1, source_target_pairs={{0,4},{2,6},{4,0},{6,2},{8,12},{10,14},{12,8},{14,10},{1,5},{3,7},... | collective-permute-start | bytes 39944 | tf_op jit(solution)/shard_map/ppermute | solution.py:505
  42.5 15.6 %collective-permute-start.13 = (bf16[4,1664]{1,0:T(4,128)(2,1)S(1)}, bf16[4,1664]{1,0:T(4,128)(2,1)S(1)}, u32[]{:S(2)}, u32[]{:S(2)}) collective-permute-start(bf16[4,1664]{1,0:T(4,128)(2,1)S(1)} %get-tuple-element.89), channel_id=1, source_target_pairs={{0,6},{2,4},{4,2},{6,0},{8,14},{10,12},{12,10},{14,8},{1,7},{3,5},... | collective-permute-start | bytes 39944 | tf_op jit(solution)/shard_map/ppermute | solution.py:505
  43.8 14.4 %collective-permute-start.14 = (bf16[4,1664]{1,0:T(4,128)(2,1)S(1)}, bf16[4,1664]{1,0:T(4,128)(2,1)S(1)}, u32[]{:S(2)}, u32[]{:S(2)}) collective-permute-start(bf16[4,1664]{1,0:T(4,128)(2,1)S(1)} %get-tuple-element.90), channel_id=1, source_target_pairs={{0,8},{2,10},{4,12},{6,14},{8,0},{10,2},{12,4},{14,6},{1,9},{3,11}... | collective-permute-start | bytes 39944 | tf_op jit(solution)/shard_map/ppermute | solution.py:505
  44.5 13.7 %collective-permute-start.15 = (bf16[4,1664]{1,0:T(4,128)(2,1)S(1)}, bf16[4,1664]{1,0:T(4,128)(2,1)S(1)}, u32[]{:S(2)}, u32[]{:S(2)}) collective-permute-start(bf16[4,1664]{1,0:T(4,128)(2,1)S(1)} %get-tuple-element.91), channel_id=1, source_target_pairs={{0,10},{2,8},{4,14},{6,12},{8,2},{10,0},{12,6},{14,4},{1,11},{3,9}... | collective-permute-start | bytes 39944 | tf_op jit(solution)/shard_map/ppermute | solution.py:505
  47.7 10.5 %collective-permute-start.16 = (bf16[4,1664]{1,0:T(4,128)(2,1)S(1)}, bf16[4,1664]{1,0:T(4,128)(2,1)S(1)}, u32[]{:S(2)}, u32[]{:S(2)}) collective-permute-start(bf16[4,1664]{1,0:T(4,128)(2,1)S(1)} %get-tuple-element.92), channel_id=1, source_target_pairs={{0,12},{2,14},{4,8},{6,10},{8,4},{10,6},{12,0},{14,2},{1,13},{3,15... | collective-permute-start | bytes 39944 | tf_op jit(solution)/shard_map/ppermute | solution.py:505
  49.1 9.1 %collective-permute-start.17 = (bf16[4,1664]{1,0:T(4,128)(2,1)S(1)}, bf16[4,1664]{1,0:T(4,128)(2,1)S(1)}, u32[]{:S(2)}, u32[]{:S(2)}) collective-permute-start(bf16[4,1664]{1,0:T(4,128)(2,1)S(1)} %get-tuple-element.93), channel_id=1, source_target_pairs={{0,14},{2,12},{4,10},{6,8},{8,6},{10,4},{12,2},{14,0},{1,15},{3,13... | collective-permute-start | bytes 39944 | tf_op jit(solution)/shard_map/ppermute | solution.py:505
  61.7 1.3 %collective-permute-start.18 = (bf16[4,6144]{1,0:T(4,128)(2,1)S(1)}, bf16[4,6144]{1,0:T(4,128)(2,1)S(1)}, u32[]{:S(2)}, u32[]{:S(2)}) collective-permute-start(bf16[4,6144]{1,0:T(4,128)(2,1)S(1)} %get-tuple-element.113), channel_id=1, source_target_pairs={{0,1},{1,0},{2,3},{3,2},{4,5},{5,4},{6,7},{7,6},{8,9},{9,8},{10,11... | collective-permute-start | bytes 147464 | tf_op jit(solution)/shard_map/ppermute | solution.py:44
  63.0 5.2 %collective-permute-start.19 = (bf16[8,6144]{1,0:T(8,128)(2,1)S(1)}, bf16[8,6144]{1,0:T(8,128)(2,1)S(1)}, u32[]{:S(2)}, u32[]{:S(2)}) collective-permute-start(bf16[8,6144]{1,0:T(8,128)(2,1)S(1)} %pad_maximum_fusion.refs_1_.refs_0_), channel_id=1, source_target_pairs={{0,4},{4,8},{8,12},{12,14},{14,10},{10,6},{6,2},{2,0},{1,5},{5,9},... | collective-permute-start | bytes 294920 | tf_op jit(solution)/shard_map/ppermute | solution.py:55
  63.1 5.1 %collective-permute-start.20 = (bf16[8,6144]{1,0:T(8,128)(2,1)S(1)}, bf16[8,6144]{1,0:T(8,128)(2,1)S(1)}, u32[]{:S(2)}, u32[]{:S(2)}) collective-permute-start(bf16[8,6144]{1,0:T(8,128)(2,1)S(1)} %pad_maximum_fusion.refs_1_.refs_0_), channel_id=1, source_target_pairs={{0,2},{4,0},{8,4},{12,8},{14,12},{10,14},{6,10},{2,6},{1,3},{5,1},... | collective-permute-start | bytes 294920 | tf_op jit(solution)/shard_map/ppermute | solution.py:55
  68.2 4.7 %collective-permute-start.21 = (bf16[8,6144]{1,0:T(8,128)(2,1)S(1)}, bf16[8,6144]{1,0:T(8,128)(2,1)S(1)}, u32[]{:S(2)}, u32[]{:S(2)}) collective-permute-start(bf16[8,6144]{1,0:T(8,128)(2,1)S(1)} %collective-permute-done.19.refs_1_), channel_id=1, source_target_pairs={{0,4},{4,8},{8,12},{12,14},{14,10},{10,6},{6,2},{2,0},{1,5},{5,9},... | collective-permute-start | bytes 294920 | tf_op jit(solution)/shard_map/ppermute | solution.py:55
  68.8 4.6 %collective-permute-start.22 = (bf16[8,6144]{1,0:T(8,128)(2,1)S(1)}, bf16[8,6144]{1,0:T(8,128)(2,1)S(1)}, u32[]{:S(2)}, u32[]{:S(2)}) collective-permute-start(bf16[8,6144]{1,0:T(8,128)(2,1)S(1)} %collective-permute-done.20.refs_2_), channel_id=1, source_target_pairs={{0,2},{4,0},{8,4},{12,8},{14,12},{10,14},{6,10},{2,6},{1,3},{5,1},... | collective-permute-start | bytes 294920 | tf_op jit(solution)/shard_map/ppermute | solution.py:55
  73.4 4.6 %collective-permute-start.23 = (bf16[8,6144]{1,0:T(8,128)(2,1)S(1)}, bf16[8,6144]{1,0:T(8,128)(2,1)S(1)}, u32[]{:S(2)}, u32[]{:S(2)}) collective-permute-start(bf16[8,6144]{1,0:T(8,128)(2,1)S(1)} %collective-permute-done.21.refs_1_.refs_3_), channel_id=1, source_target_pairs={{0,4},{4,8},{8,12},{12,14},{14,10},{10,6},{6,2},{2,0},{1,5},{5,9},... | collective-permute-start | bytes 294920 | tf_op jit(solution)/shard_map/ppermute | solution.py:55
  75.2 4.6 %collective-permute-start.24 = (bf16[8,6144]{1,0:T(8,128)(2,1)S(1)}, bf16[8,6144]{1,0:T(8,128)(2,1)S(1)}, u32[]{:S(2)}, u32[]{:S(2)}) collective-permute-start(bf16[8,6144]{1,0:T(8,128)(2,1)S(1)} %collective-permute-done.22.refs_2_.refs_4_), channel_id=1, source_target_pairs={{0,2},{4,0},{8,4},{12,8},{14,12},{10,14},{6,10},{2,6},{1,3},{5,1},... | collective-permute-start | bytes 294920 | tf_op jit(solution)/shard_map/ppermute | solution.py:55
  79.8 4.4 %collective-permute-start.25 = (bf16[8,3072]{1,0:T(8,128)(2,1)S(1)}, bf16[8,3072]{1,0:T(8,128)(2,1)S(1)}, u32[]{:S(2)}, u32[]{:S(2)}) collective-permute-start(bf16[8,3072]{1,0:T(8,128)(2,1)S(1)} %slice.14), channel_id=1, source_target_pairs={{0,4},{4,8},{8,12},{12,14},{14,10},{10,6},{6,2},{2,0},{1,5},{5,9},... | collective-permute-start | bytes 147464 | tf_op jit(solution)/shard_map/ppermute | solution.py:55
  81.4 4.1 %collective-permute-start.26 = (bf16[8,3072]{1,0:T(8,128)(2,1)S(1)}, bf16[8,3072]{1,0:T(8,128)(2,1)S(1)}, u32[]{:S(2)}, u32[]{:S(2)}) collective-permute-start(bf16[8,3072]{1,0:T(8,128)(2,1)S(1)} %slice.15), channel_id=1, source_target_pairs={{0,2},{4,0},{8,4},{12,8},{14,12},{10,14},{6,10},{2,6},{1,3},{5,1},... | collective-permute-start | bytes 147464 | tf_op jit(solution)/shard_map/ppermute | solution.py:55
  90.6 1.6 %collective-permute-start.27 = (f32[4,8,2304]{2,1,0:T(8,128)S(1)}, f32[4,8,2304]{2,1,0:T(8,128)S(1)}, u32[]{:S(2)}, u32[]{:S(2)}) collective-permute-start(f32[4,8,2304]{2,1,0:T(8,128)S(1)} %get-tuple-element.128), channel_id=1, source_target_pairs={{0,1},{1,0},{2,3},{3,2},{4,5},{5,4},{6,7},{7,6},{8,9},{9,8},{10,11... | collective-permute-start | bytes 884744 | tf_op jit(solution)/shard_map/ppermute | solution.py:44

commit v8 on v7

--- a/solution.py
+++ b/solution.py
@@ -53,6 +53,10 @@
 
     def step(self, left, right):
         return lax.ppermute(left, "gx", self.onward), lax.ppermute(right, "gx", self.back)
+
+    def send_across(self, shard, part):
+        half = shard.shape[1] // 2
+        return lax.ppermute(shard[:, part * half : (part + 1) * half], "gx", self.across)
 
 
 def owners(n):
@@ -109,29 +113,6 @@
         compiler_params=pltpu.CompilerParams(vmem_limit_bytes=MIB),
         name="load",
     )(*[in_hbm(job[0]) for job in jobs], *after)
-
-
-def load_caches_kernel(*refs):
-    sources, targets, sems = refs[:2], refs[-3:-1], refs[-1]
-    copies = []
-    for i, (source, target) in enumerate(zip(sources, targets)):
-        for row in range(source.shape[0]):
-            copies.append(pltpu.make_async_copy(source.at[row], target.at[row], sems.at[i, row]))
-            copies[-1].start()
-    for copy in copies:
-        copy.wait()
-
-
-def load_caches(keys, values, after):
-    return pl.pallas_call(
-        load_caches_kernel,
-        out_shape=[pltpu.VMEM(a.shape, a.dtype) for a in (keys, values)],
-        in_specs=[IN_HBM] * 2 + [ANY] * len(after),
-        out_specs=[IN_VMEM] * 2,
-        scratch_shapes=[pltpu.SemaphoreType.DMA((2, keys.shape[0]))],
-        compiler_params=pltpu.CompilerParams(vmem_limit_bytes=MIB),
-        name="load_caches",
-    )(in_hbm(keys), in_hbm(values), *after)
 
 
 def in_hbm(array):
@@ -176,25 +157,28 @@
     )(*ready, *shards, *after)
 
 
-def project_kernel(n, *refs):
+def project_kernel(n, parts, *refs):
     sums_a, sums_b, gain = refs[:3]
-    near = refs[3 : 3 + n - 1]
-    far = refs[3 + n - 1 : 3 + n + 1]
-    weights = refs[3 + n + 1 : -4]
-    keep, give, normed, total = refs[-4:]
-    rows = near[0].shape[0]
-    half = far[0].shape[1]
+    shards = refs[3 : 3 + n]
+    weights = refs[3 + n : 3 + n + parts]
+    caches = refs[3 + n + parts : 5 + n + parts]
+    keep, give, *copied, normed, total, sems = refs[5 + n + parts :]
+    copies = []
+    for i, (source, target) in enumerate(zip(caches, copied)):
+        for row in range(source.shape[0]):
+            copies.append(pltpu.make_async_copy(source.at[row], target.at[row], sems.at[i, row]))
+            copies[-1].start()
+    rows, width = shards[0].shape
     sums = sums_a[...] + sums_b[...]
     row_mean = sums[:, :1] / D
     row_square = sums[:, 1:2] / D
     scale = lax.rsqrt(row_square - row_mean * row_mean + epsilon)
     for part in range(2):
-        cols = slice(part * half, (part + 1) * half)
-        for i in range(n):
+        cols = slice(part * width // 2, (part + 1) * width // 2)
+        for i, shard in enumerate(shards):
             at = slice(i * rows, (i + 1) * rows)
-            x = near[i][:, cols] if i < n - 1 else far[part][...]
-            x = (x.astype(jnp.float32) - row_mean[at]) * scale[at] * gain[:, cols]
-            normed[at, cols] = x
+            x = shard[:, cols].astype(jnp.float32)
+            normed[at, cols] = (x - row_mean[at]) * scale[at] * gain[:, cols]
         x = normed[:, cols].astype(jnp.bfloat16)
         start = 0
         for weight in weights:
@@ -214,55 +198,78 @@
         low, high = block[:local], block[local:]
         keep[owner] = jnp.where(side == 0, low, high)
         give[owner] = jnp.where(side == 0, high, low)
-
-
-def project(n, sums, gain, near, far, weights):
-    rows, width = near[0].shape
+    for copy in copies:
+        copy.wait()
+
+
+def project(sums, gain, shards, weights, caches):
+    n = len(shards)
+    rows, width = shards[0].shape
     stripe = sum(w.shape[0] for w in weights)
     shape = jax.ShapeDtypeStruct((n, rows // 2, stripe), jnp.float32)
     return pl.pallas_call(
-        lambda *refs: project_kernel(n, *refs),
-        out_shape=[shape, shape],
-        in_specs=[IN_VMEM] * (3 + n + 1 + len(weights)),
-        out_specs=[IN_VMEM] * 2,
+        lambda *refs: project_kernel(n, len(weights), *refs),
+        out_shape=[shape, shape] + [pltpu.VMEM(a.shape, a.dtype) for a in caches],
+        in_specs=[IN_VMEM] * (3 + n + len(weights)) + [IN_HBM] * 2,
+        out_specs=[IN_VMEM] * 4,
         scratch_shapes=[
             pltpu.VMEM((n * rows, width), jnp.float32),
             pltpu.VMEM((n * rows, stripe), jnp.float32),
+            pltpu.SemaphoreType.DMA((2, caches[0].shape[0])),
         ],
         compiler_params=pltpu.CompilerParams(vmem_limit_bytes=8 * MIB),
         name="project",
-    )(*sums, gain, *near, *far, *[in_vmem(w) for w in weights])
-
-
-def split_kernel(keep, got, *outs):
+    )(*sums, gain, *shards, *[in_vmem(w) for w in weights], *[in_hbm(a) for a in caches])
+
+
+def split_kernel(keep, got, here, there):
     me = lax.axis_index("gx")
-    for d, out in enumerate(outs):
+    for d in range(keep.shape[0]):
         at = jnp.bitwise_xor(me, d)
-        out[...] = (keep[at] + got[at]).astype(jnp.bfloat16)
+        out = there if d % 2 else here
+        out[d // 2] = (keep[at] + got[at]).astype(jnp.bfloat16)
 
 
 def split(keep, got):
-    n = keep.shape[0]
+    shape = jax.ShapeDtypeStruct((keep.shape[0] // 2,) + keep.shape[1:], jnp.bfloat16)
     return pl.pallas_call(
         split_kernel,
-        out_shape=[jax.ShapeDtypeStruct(keep.shape[1:], jnp.bfloat16)] * n,
+        out_shape=[shape] * 2,
         in_specs=[IN_VMEM] * 2,
-        out_specs=[IN_VMEM] * n,
+        out_specs=[IN_VMEM] * 2,
         compiler_params=pltpu.CompilerParams(vmem_limit_bytes=8 * MIB),
         name="split",
     )(keep, got)
 
 
+def pair_kernel(here, came, *outs):
+    for d, out in enumerate(outs):
+        out[0] = here[d]
+        out[1] = came[d]
+
+
+def pair(here, came):
+    shape = jax.ShapeDtypeStruct((2,) + here.shape[1:], here.dtype)
+    return pl.pallas_call(
+        pair_kernel,
+        out_shape=[shape] * here.shape[0],
+        in_specs=[IN_VMEM] * 2,
+        out_specs=[IN_VMEM] * here.shape[0],
+        compiler_params=pltpu.CompilerParams(vmem_limit_bytes=8 * MIB),
+        name="pair",
+    )(here, came)
+
+
 def attend_kernel(n, lengths, *refs):
-    arrived = refs[:n]
-    cosine, sine, keys, values, mine, other, spread, held = refs[n:]
-    rows, stripe = arrived[0].shape
+    arrived = refs[: n // 2]
+    cosine, sine, keys, values, mine, other, spread, held = refs[n // 2 :]
+    _, rows, stripe = arrived[0].shape
     me = lax.axis_index("gx")
     query_cols = stripe - 128
     side = lax.axis_index("gy")
     score_scale = 1.0 / math.sqrt(DH)
     for d in range(n):
-        block = arrived[d][...].astype(jnp.float32)
+        block = arrived[d // 2][d % 2].astype(jnp.float32)
         for r in range(rows):
             spread[r, pl.ds(jnp.bitwise_xor(me, d), 1), :] = block[r : r + 1, :]
     for r in range(rows):
@@ -310,13 +317,13 @@
 
 
 def attend(lengths, arrived, cosine, sine, keys, values):
-    n = len(arrived)
-    rows, stripe = arrived[0].shape
+    n = 2 * len(arrived)
+    _, rows, stripe = arrived[0].shape
     shape = jax.ShapeDtypeStruct((rows, HEADS * DH // 2), jnp.bfloat16)
     return pl.pallas_call(
         lambda *refs: attend_kernel(n, *refs),
         out_shape=[shape, shape],
-        in_specs=[IN_SMEM] + [IN_VMEM] * (n + 4),
+        in_specs=[IN_SMEM] + [IN_VMEM] * (n // 2 + 4),
         out_specs=[IN_VMEM] * 2,
         scratch_shapes=[
             pltpu.VMEM((rows, n, stripe), jnp.float32),
@@ -328,18 +335,14 @@
 
 
 def output_kernel(n, *refs):
-    near = refs[: n - 1]
-    far = refs[n - 1 : n + 1]
-    weights = refs[n + 1 : -4]
+    shards = refs[:n]
+    weights = refs[n:-4]
     keep, give, total, placed = refs[-4:]
-    rows = near[0].shape[0]
-    half = far[0].shape[1]
+    rows = shards[0].shape[0]
     start = 0
     for weight in weights:
         cols = slice(start, start + weight.shape[0])
-        last = slice(start % half, start % half + weight.shape[0])
-        x = [ref[:, cols] for ref in near] + [far[start // half][:, last]]
-        x = jnp.concatenate([piece.astype(jnp.float32) for piece in x], axis=0)
+        x = jnp.concatenate([ref[:, cols].astype(jnp.float32) for ref in shards], axis=0)
         term = jnp.dot(x.astype(jnp.bfloat16), weight[...], preferred_element_type=jnp.float32)
         if start == 0:
             total[...] = term
@@ -354,14 +357,15 @@
     give[...] = placed[pl.ds((1 - side) * (n // 2), n // 2)]
 
 
-def output_project(n, near, far, weights):
-    rows = near[0].shape[0]
+def output_project(shards, weights):
+    n = len(shards)
+    rows = shards[0].shape[0]
     cols = weights[0].shape[1]
     shape = jax.ShapeDtypeStruct((n // 2, rows, cols), jnp.float32)
     return pl.pallas_call(
         lambda *refs: output_kernel(n, *refs),
         out_shape=[shape, shape],
-        in_specs=[IN_VMEM] * (n + 1 + len(weights)),
+        in_specs=[IN_VMEM] * (n + len(weights)),
         out_specs=[IN_VMEM] * 2,
         scratch_shapes=[
             pltpu.VMEM((n * rows, cols), jnp.float32),
@@ -369,7 +373,7 @@
         ],
         compiler_params=pltpu.CompilerParams(vmem_limit_bytes=8 * MIB),
         name="output_project",
-    )(*near, *far, *[in_vmem(w) for w in weights])
+    )(*shards, *[in_vmem(w) for w in weights])
 
 
 def on_any_grid(
@@ -469,65 +473,66 @@
     angles = cache_lengths.astype(jnp.float32)[:, None] * frequency
     cosine, sine = jnp.cos(angles), jnp.sin(angles)
 
+    def piece_of(array, start, size, after):
+        return load(size, [(array, start, size, 0)], after)
+
     left = right = activations
-    near = [activations]
+    shards = [activations]
+    far = []
+    sums = ()
     for step in range(1, n // 2):
-        arrived = near[1:][-2:]
+        arrived = shards[-2:] if step > 1 else shards
         left, right = ring.step(left, right)
-        if step > 1:
-            sums = row_sums(arrived, [sums])
-        start = (step - 1) * piece
-        weight = load(piece, [(query_weight, start, piece, 0)], arrived)
-        if step == 1:
-            weight, (own,) = before(weight, activations)
-            sums = row_sums([own])
-            far_sums = lax.ppermute(sums, "gx", ring.across)
-            weight, (left, right, sums) = before(weight, left, right, sums)
-        else:
-            weight, (left, right) = before(weight, left, right)
+        weight = piece_of(query_weight, (step - 1) * piece, piece, arrived if step > 1 else [])
+        if step <= 2:
+            half = ring.send_across(activations, step - 1)
+            weight, (half,) = before(weight, half)
+            far.append(half)
+        weight, (left, right, *arrived) = before(weight, left, right, *arrived)
+        sums = (row_sums(arrived, sums),)
         weights.append(weight)
-        near += [left, right]
-    half = width // 2
-    far = ring.step(left[:, :half], right[:, half:])
-    sums = row_sums([left, right], [sums])
+        shards += [left, right]
+    shards.append(jnp.concatenate(far, axis=1))
+    sums = row_sums([left, right, shards[-1]], sums)
     jobs = [(query_weight, 3 * piece, piece, 0), (keyval_weight, 0, new_cols, None)]
     weight = load(piece + 2 * new_cols, jobs, [sums])
-    sums = jnp.concatenate([sums, far_sums], axis=0)
     other_sums = swap_pair(sums)
-    weight, (other_sums, *far) = before(weight, other_sums, *far)
+    weight, (other_sums,) = before(weight, other_sums)
     weights.append(weight)
-    sums = (sums, other_sums)
     gain = norm_gain.astype(jnp.float32)[None, :]
-    keep, give = project(n, sums, gain, near, far, weights)
-    blocks = split(keep, swap_pair(give))
+    keep, give, keys, values = project(
+        (sums, other_sums), gain, shards, weights, [cache_keys, cache_values]
+    )
+
+    here, there = split(keep, swap_pair(give))
+    came = lax.ppermute(there, "gx", [(i, i ^ 1) for i in range(n)])
+    blocks = pair(here, came)
     arrived = [blocks[0]]
-    for d in range(1, n):
-        arrived.append(lax.ppermute(blocks[d], "gx", [(i, i ^ d) for i in range(n)]))
-    keys, values = load_caches(cache_keys, cache_values, [blocks[1]])
-    unit = output_weight.shape[0] // 12
-    sizes = [3 * unit, 3 * unit, 2 * unit, 2 * unit, 2 * unit]
-    weight = load(sizes[0], [(output_weight, 0, sizes[0], 0)], [blocks[1]])
-    keys, arrived = before(keys, *arrived)
+    for d in range(1, n // 2):
+        arrived.append(lax.ppermute(blocks[d], "gx", [(i, i ^ (2 * d)) for i in range(n)]))
+    piece = output_weight.shape[0] // 4
+    weight = piece_of(output_weight, 0, piece, [blocks[1]])
     weight, arrived = before(weight, *arrived)
     weights = [weight]
     mine, other = attend(cache_lengths, arrived, cosine, sine, keys, values)
     shard = jnp.concatenate([mine, swap_pair(other)], axis=0)
 
     left = right = shard
-    near = [shard]
+    shards = [shard]
+    far = []
     for step in range(1, n // 2):
-        arrived = near[-2:]
+        arrived = shards[-2:]
         left, right = ring.step(left, right)
-        weight = load(sizes[step], [(output_weight, sum(sizes[:step]), sizes[step], 0)], arrived)
+        weight = piece_of(output_weight, step * piece, piece, arrived)
+        if step <= 2:
+            half = ring.send_across(shard, step - 1)
+            weight, (half,) = before(weight, half)
+            far.append(half)
         weight, (left, right) = before(weight, left, right)
         weights.append(weight)
-        near += [left, right]
-    half = shard.shape[1] // 2
-    far = ring.step(left[:, :half], right[:, half:])
-    weight = load(sizes[-1], [(output_weight, sum(sizes[:-1]), sizes[-1], 0)], [left, right])
-    weight, far = before(weight, *far)
-    weights.append(weight)
-    keep, give = output_project(n, near, far, weights)
+        shards += [left, right]
+    shards.append(jnp.concatenate(far, axis=1))
+    keep, give = output_project(shards, weights)
     out = (keep + swap_pair(give)).astype(jnp.bfloat16)
     return out.reshape(-1, out.shape[-1])
 

time: 93.1 us -> 91.7 us (0.985)
  waiting for transfers between devices: 11.7 us -> 16.5 us
  Pallas kernels: 48.4 us -> 44.8 us
  starting transfers between devices: 31.6 us -> 28 us
  local copies, waits for them, and re-layouts: 0.03 us -> 0.99 us
    ppermute x8, waiting for transfers between devices: 0.02 us -> 8.02 us  [the longest x1 4.1 us: on_device(): came = lax.ppermute(there, 'gx', [(i, i ^ 1) for i in range(n)])]
    ppermute x8 -> x6, starting transfers between devices: 10.7 us -> 7.42 us  [step(): lax.ppermute(left, 'gx', self.onward)]
    pallas_call x3, Pallas kernels: 13.2 us -> 10.4 us  [the longest x1 10.4 us: project(): pl.pallas_call(lambda *refs: project_kernel(n, len(weights), *refs), out_...]
    ppermute x8 -> x6, waiting for transfers between devices: 6.59 us -> 3.92 us  [step(): lax.ppermute(right, 'gx', self.back)]
    slice x4 -> x1, local copies, waits for them, and re-layouts: 0.02 us -> 0.96 us  [send_across(): shard[:, part * half:(part + 1) * half]]
    pallas_call x9 -> x8, Pallas kernels: 26 us -> 25.2 us  [load(): pl.pallas_call(lambda *refs: load_kernel([job[1:] for job in jobs], *refs...]
    ppermute x8 -> x6, starting transfers between devices: 6.56 us -> 6.31 us  [step(): lax.ppermute(right, 'gx', self.back)]
  transfers between devices with their start and end apart: 28 -> 24, of which waited for: 11 -> 10; matrix products, arithmetic and copies ran while one was open for 0% -> 1% of each run, Pallas kernels for 33% -> 28%
where the time goes in v8:
time: 91.7 us; the launch traced here: 91.6 us
  Pallas kernels  44.8 us (49%)
  starting transfers between devices  28 us (31%)
  waiting for transfers between devices  16.5 us (18%)
  local copies, waits for them, and re-layouts  0.99 us (1%)
  other arithmetic  0.95 us (1%)
    pallas_call x8, Pallas kernels, load(): pl.pallas_call(lambda *refs: load_kernel([job[1:] for job in jobs], *refs...  25.2 us
    pallas_call x1, Pallas kernels, project(): pl.pallas_call(lambda *refs: project_kernel(n, len(weights), *refs), out_...  10.4 us
    ppermute x4, starting transfers between devices, send_across(): lax.ppermute(shard[:, part * half:(part + 1) * half], 'gx', self.across)  9.05 us
    ppermute x6, starting transfers between devices, step(): lax.ppermute(left, 'gx', self.onward)  7.42 us
    ppermute x6, starting transfers between devices, step(): lax.ppermute(right, 'gx', self.back)  6.31 us
    pallas_call x1, Pallas kernels, output_project(): pl.pallas_call(lambda *refs: output_kernel(n, *refs), out_shape=[shape, s...  5.04 us
    ppermute x3, starting transfers between devices, on_device(): lax.ppermute(blocks[d], 'gx', [(i, i ^ 2 * d) for i in range(n)])  4.45 us
    ppermute x1, waiting for transfers between devices, on_device(): came = lax.ppermute(there, 'gx', [(i, i ^ 1) for i in range(n)])  4.1 us
  transfers between devices with their start and end apart: 24, of which 10 were waited for; matrix products, arithmetic and copies ran while one was open for 1% of the time, Pallas kernels for 28%

profile of v8, /device:TPU:0, one launch (start us, length us, event | category | flops | bytes accessed | tf_op | source)
XLA Modules:
  0.0 91.6 jit_solution(4314125745254134674)
XLA Ops:
  0.0 3.0 %collective-permute-start.1 = (bf16[8,9216]{1,0:T(8,128)(2,1)}, bf16[8,9216]{1,0:T(8,128)(2,1)S(1)}, u32[]{:S(2)}, u32[]{:S(2)}) collective-permute-start(bf16[8,9216]{1,0:T(8,128)(2,1)} %refs_3_.1), channel_id=1, source_target_pairs={{0,4},{4,8},{8,12},{12,14},{14,10},{10,6},{6,2},{2,0},{1,5},{5,9},... | collective-permute-start | bytes 442376 | tf_op jit(solution)/shard_map/ppermute | solution.py:55
  3.0 1.0 %fusion.3 = (bf16[8,4608]{1,0:T(8,128)(2,1)S(1)}, bf16[8,4608]{1,0:T(8,128)(2,1)S(1)}) fusion(bf16[8,9216]{1,0:T(8,128)(2,1)} %refs_3_.1), kind=kLoop, calls=%fused_computation.15 | loop fusion | bytes 294912 | tf_op jit(solution)/shard_map/slice | solution.py:59
  4.0 5.1 %collective-permute-start = (bf16[8,4608]{1,0:T(8,128)(2,1)S(1)}, bf16[8,4608]{1,0:T(8,128)(2,1)S(1)}, u32[]{:S(2)}, u32[]{:S(2)}) collective-permute-start(bf16[8,4608]{1,0:T(8,128)(2,1)S(1)} %get-tuple-element.110), channel_id=1, source_target_pairs={{0,14},{4,10},{8,6},{12,2},{14,0},{10,4},{6,8},{2,12},{1,15},{5,11... | collective-permute-start | bytes 221192 | tf_op jit(solution)/shard_map/ppermute | solution.py:59
  9.1 0.1 collective-permute-start.3
  9.1 3.1 %load.8.refs_11_ = bf16[384,9216]{1,0:T(8,128)(2,1)S(1)} custom-call(bf16[1536,9216]{1,0:T(8,128)(2,1)} %refs_0_.13), custom_call_target="tpu_custom_call" | custom-call | tf_op jit(solution)/shard_map/load/pallas_call | solution.py:107
  12.3 1.8 %collective-permute-start.4 = (bf16[8,9216]{1,0:T(8,128)(2,1)S(1)}, bf16[8,9216]{1,0:T(8,128)(2,1)S(1)}, u32[]{:S(2)}, u32[]{:S(2)}) collective-permute-start(bf16[8,9216]{1,0:T(8,128)(2,1)S(1)} %collective-permute-done.1.refs_1_.refs_4_), channel_id=1, source_target_pairs={{0,4},{4,8},{8,12},{12,14},{14,10},{10,6},{6,2},{2,0},{1,5},{5,9},... | collective-permute-start | bytes 442376 | tf_op jit(solution)/shard_map/ppermute | solution.py:55
  14.1 0.3 collective-permute-start.5
  14.4 3.1 %load.9.refs_12_ = bf16[384,9216]{1,0:T(8,128)(2,1)S(1)} custom-call(bf16[1536,9216]{1,0:T(8,128)(2,1)} %refs_0_.13, bf16[8,9216]{1,0:T(8,128)(2,1)S(1)} %collective-permute-done.1.refs_1_.refs_4_, bf16[8,9216]{1,0:T(8,128)(2,1)S(1)} %collective-permute-done.2.refs_2_.refs_5_), custom_call_target="tpu_custom_call" | custom-call | tf_op jit(solution)/shard_map/load/pallas_call | solution.py:107
  17.5 0.7 collective-permute-done.4.refs_1_.refs_6_
  18.2 2.3 %collective-permute-done.5.refs_2_.refs_7_ = bf16[8,9216]{1,0:T(8,128)(2,1)S(1)} collective-permute-done((bf16[8,9216]{1,0:T(8,128)(2,1)S(1)}, bf16[8,9216]{1,0:T(8,128)(2,1)S(1)}, u32[]{:S(2)}, u32[]{:S(2)}) %collective-permute-start.5) | collective-permute-done | bytes 147488 | tf_op jit(solution)/shard_map/ppermute | solution.py:55
  20.4 2.5 %collective-permute-start.6 = (bf16[8,9216]{1,0:T(8,128)(2,1)S(1)}, bf16[8,9216]{1,0:T(8,128)(2,1)S(1)}, u32[]{:S(2)}, u32[]{:S(2)}) collective-permute-start(bf16[8,9216]{1,0:T(8,128)(2,1)S(1)} %collective-permute-done.4.refs_1_.refs_6_), channel_id=1, source_target_pairs={{0,4},{4,8},{8,12},{12,14},{14,10},{10,6},{6,2},{2,0},{1,5},{5,9},... | collective-permute-start | bytes 442376 | tf_op jit(solution)/shard_map/ppermute | solution.py:55
  23.0 0.2 row_sums.4.refs_0_
  23.1 3.1 %load.10.refs_13_ = bf16[384,9216]{1,0:T(8,128)(2,1)S(1)} custom-call(bf16[1536,9216]{1,0:T(8,128)(2,1)} %refs_0_.13, bf16[8,9216]{1,0:T(8,128)(2,1)S(1)} %collective-permute-done.4.refs_1_.refs_6_, bf16[8,9216]{1,0:T(8,128)(2,1)S(1)} %collective-permute-done.5.refs_2_.refs_7_), custom_call_target="tpu_custom_call" | custom-call | tf_op jit(solution)/shard_map/load/pallas_call | solution.py:107
  26.3 0.2 row_sums.5.refs_0_
  26.4 1.7 %collective-permute-done.7.refs_2_.refs_9_ = bf16[8,9216]{1,0:T(8,128)(2,1)S(1)} collective-permute-done((bf16[8,9216]{1,0:T(8,128)(2,1)S(1)}, bf16[8,9216]{1,0:T(8,128)(2,1)S(1)}, u32[]{:S(2)}, u32[]{:S(2)}) %collective-permute-start.7) | collective-permute-done | bytes 147488 | tf_op jit(solution)/shard_map/ppermute | solution.py:55
  28.1 0.2 row_sums.6.refs_0_
  28.3 0.2 row_sums.7.refs_2_.refs_0_
  28.5 3.4 %load.11.refs_14_ = bf16[512,9216]{1,0:T(8,128)(2,1)S(1)} custom-call(bf16[1536,9216]{1,0:T(8,128)(2,1)} %refs_0_.13, bf16[64,9216]{1,0:T(8,128)(2,1)} %refs_1_.1, f32[64,128]{1,0:T(8,128)S(1)} %row_sums.7.refs_2_.refs_0_), custom_call_target="tpu_custom_call" | custom-call | tf_op jit(solution)/shard_map/load/pallas_call | solution.py:107
  31.9 10.4 %project.1 = (f32[8,4,1664]{2,1,0:T(4,128)S(1)}, f32[8,4,1664]{2,1,0:T(4,128)S(1)}, bf16[4,2048,256]{2,1,0:T(8,128)(2,1)S(1)}, bf16[4,2048,256]{2,1,0:T(8,128)(2,1)S(1)}) custom-call(f32[64,128]{1,0:T(8,128)S(1)} %row_sums.7.refs_2_.refs_0_, f32[64,128]{1,0:T(8,128)S(1)} %collective-permute-done.8.refs_1_, f32[1,9216]{1,0:T(1,128)S(1)} %bitcast.3, ...), custom_call_target="tpu_custom_call" | custom-call | tf_op jit(solution)/shard_map/project/pallas_call | solution.py:210
  42.3 0.5 collective-permute-start.9
  42.9 1.1 %collective-permute-done.9.got = f32[8,4,1664]{2,1,0:T(4,128)S(1)} collective-permute-done((f32[8,4,1664]{2,1,0:T(4,128)S(1)}, f32[8,4,1664]{2,1,0:T(4,128)S(1)}, u32[]{:S(2)}, u32[]{:S(2)}) %collective-permute-start.9) | collective-permute-done | bytes 213024 | tf_op jit(solution)/shard_map/ppermute | solution.py:44
  44.0 0.1 collective-permute-start.10
  44.1 4.1 %collective-permute-done.10.came = bf16[4,4,1664]{2,1,0:T(4,128)(2,1)S(1)} collective-permute-done((bf16[4,4,1664]{2,1,0:T(4,128)(2,1)S(1)}, bf16[4,4,1664]{2,1,0:T(4,128)(2,1)S(1)}, u32[]{:S(2)}, u32[]{:S(2)}) %collective-permute-start.10) | collective-permute-done | bytes 53280 | tf_op jit(solution)/shard_map/ppermute | solution.py:508
  48.3 0.4 collective-permute-start.11
  48.7 1.8 %collective-permute-start.12 = (bf16[2,4,1664]{2,1,0:T(4,128)(2,1)S(1)}, bf16[2,4,1664]{2,1,0:T(4,128)(2,1)S(1)}, u32[]{:S(2)}, u32[]{:S(2)}) collective-permute-start(bf16[2,4,1664]{2,1,0:T(4,128)(2,1)S(1)} %get-tuple-element.83), channel_id=1, source_target_pairs={{0,8},{2,10},{4,12},{6,14},{8,0},{10,2},{12,4},{14,6},{1,9},{3,11}... | collective-permute-start | bytes 79880 | tf_op jit(solution)/shard_map/ppermute | solution.py:512
  50.5 2.2 %collective-permute-start.13 = (bf16[2,4,1664]{2,1,0:T(4,128)(2,1)S(1)}, bf16[2,4,1664]{2,1,0:T(4,128)(2,1)S(1)}, u32[]{:S(2)}, u32[]{:S(2)}) collective-permute-start(bf16[2,4,1664]{2,1,0:T(4,128)(2,1)S(1)} %get-tuple-element.84), channel_id=1, source_target_pairs={{0,12},{2,14},{4,8},{6,10},{8,4},{10,6},{12,0},{14,2},{1,13},{3,15... | collective-permute-start | bytes 79880 | tf_op jit(solution)/shard_map/ppermute | solution.py:512
  52.7 0.1 multiply_sine_fusion
  52.8 3.1 %load.12.refs_8_ = bf16[1536,2304]{1,0:T(8,128)(2,1)S(1)} custom-call(bf16[6144,2304]{1,0:T(8,128)(2,1)} %refs_0_.18, bf16[2,4,1664]{2,1,0:T(4,128)(2,1)S(1)} %get-tuple-element.81.refs_1_), custom_call_target="tpu_custom_call" | custom-call | tf_op jit(solution)/shard_map/load/pallas_call | solution.py:107
  56.0 0.2 collective-permute-done.13.refs_4_
  56.1 3.5 %attend.1 = (bf16[4,6144]{1,0:T(4,128)(2,1)S(1)}, bf16[4,6144]{1,0:T(4,128)(2,1)S(1)}) custom-call(s32[4]{0:T(128)S(1)} %copy-done.1, bf16[2,4,1664]{2,1,0:T(4,128)(2,1)S(1)} %get-tuple-element.85.refs_1_, bf16[2,4,1664]{2,1,0:T(4,128)(2,1)S(1)} %collective-permute-done.11.refs_2_, bf16[2,4,1664]{2,1,0:T(4,128)(2,1)S(1)} %collective-permute-done.12.refs_3_, ...), custom_call_target="tpu_custom_call" | custom-call | tf_op jit(solution)/shard_map/attend/pallas_call | solution.py:323
  59.6 0.1 collective-permute-start.14
  59.7 1.2 %collective-permute-done.14 = bf16[4,6144]{1,0:T(4,128)(2,1)S(1)} collective-permute-done((bf16[4,6144]{1,0:T(4,128)(2,1)S(1)}, bf16[4,6144]{1,0:T(4,128)(2,1)S(1)}, u32[]{:S(2)}, u32[]{:S(2)}) %collective-permute-start.14) | collective-permute-done | bytes 49184 | tf_op jit(solution)/shard_map/ppermute | solution.py:44
  60.9 0.1 pad_maximum_fusion.refs_1_.refs_0_
  60.9 0.1 collective-permute-start.16
  61.0 2.0 %collective-permute-start.17 = (bf16[8,6144]{1,0:T(8,128)(2,1)S(1)}, bf16[8,6144]{1,0:T(8,128)(2,1)S(1)}, u32[]{:S(2)}, u32[]{:S(2)}) collective-permute-start(bf16[8,6144]{1,0:T(8,128)(2,1)S(1)} %pad_maximum_fusion.refs_1_.refs_0_), channel_id=1, source_target_pairs={{0,2},{4,0},{8,4},{12,8},{14,12},{10,14},{6,10},{2,6},{1,3},{5,1},... | collective-permute-start | bytes 294920 | tf_op jit(solution)/shard_map/ppermute | solution.py:55
  63.1 2.0 %collective-permute-start.15 = (bf16[8,3072]{1,0:T(8,128)(2,1)S(1)}, bf16[8,3072]{1,0:T(8,128)(2,1)S(1)}, u32[]{:S(2)}, u32[]{:S(2)}) collective-permute-start(bf16[8,3072]{1,0:T(8,128)(2,1)S(1)} %get-tuple-element.112), channel_id=1, source_target_pairs={{0,14},{4,10},{8,6},{12,2},{14,0},{10,4},{6,8},{2,12},{1,15},{5,11... | collective-permute-start | bytes 147464 | tf_op jit(solution)/shard_map/ppermute | solution.py:59
  65.1 3.1 %load.13.refs_9_ = bf16[1536,2304]{1,0:T(8,128)(2,1)S(1)} custom-call(bf16[6144,2304]{1,0:T(8,128)(2,1)} %refs_0_.18, bf16[8,6144]{1,0:T(8,128)(2,1)S(1)} %pad_maximum_fusion.refs_1_.refs_0_), custom_call_target="tpu_custom_call" | custom-call | tf_op jit(solution)/shard_map/load/pallas_call | solution.py:107
  68.2 1.8 %collective-permute-done.15 = bf16[8,3072]{1,0:T(8,128)(2,1)S(1)} collective-permute-done((bf16[8,3072]{1,0:T(8,128)(2,1)S(1)}, bf16[8,3072]{1,0:T(8,128)(2,1)S(1)}, u32[]{:S(2)}, u32[]{:S(2)}) %collective-permute-start.15) | collective-permute-done | bytes 49184 | tf_op jit(solution)/shard_map/ppermute | solution.py:59
  70.0 2.0 %collective-permute-start.20 = (bf16[8,6144]{1,0:T(8,128)(2,1)S(1)}, bf16[8,6144]{1,0:T(8,128)(2,1)S(1)}, u32[]{:S(2)}, u32[]{:S(2)}) collective-permute-start(bf16[8,6144]{1,0:T(8,128)(2,1)S(1)} %collective-permute-done.17.refs_2_), channel_id=1, source_target_pairs={{0,2},{4,0},{8,4},{12,8},{14,12},{10,14},{6,10},{2,6},{1,3},{5,1},... | collective-permute-start | bytes 294920 | tf_op jit(solution)/shard_map/ppermute | solution.py:55
  72.0 1.9 %collective-permute-start.18 = (bf16[8,3072]{1,0:T(8,128)(2,1)S(1)}, bf16[8,3072]{1,0:T(8,128)(2,1)S(1)}, u32[]{:S(2)}, u32[]{:S(2)}) collective-permute-start(bf16[8,3072]{1,0:T(8,128)(2,1)S(1)} %get-tuple-element.111), channel_id=1, source_target_pairs={{0,14},{4,10},{8,6},{12,2},{14,0},{10,4},{6,8},{2,12},{1,15},{5,11... | collective-permute-start | bytes 147464 | tf_op jit(solution)/shard_map/ppermute | solution.py:59
  73.9 3.1 %load.14.refs_10_ = bf16[1536,2304]{1,0:T(8,128)(2,1)S(1)} custom-call(bf16[6144,2304]{1,0:T(8,128)(2,1)} %refs_0_.18, bf16[8,6144]{1,0:T(8,128)(2,1)S(1)} %collective-permute-done.16.refs_1_, bf16[8,6144]{1,0:T(8,128)(2,1)S(1)} %collective-permute-done.17.refs_2_), custom_call_target="tpu_custom_call" | custom-call | tf_op jit(solution)/shard_map/load/pallas_call | solution.py:107
  77.0 2.0 %collective-permute-done.18 = bf16[8,3072]{1,0:T(8,128)(2,1)S(1)} collective-permute-done((bf16[8,3072]{1,0:T(8,128)(2,1)S(1)}, bf16[8,3072]{1,0:T(8,128)(2,1)S(1)}, u32[]{:S(2)}, u32[]{:S(2)}) %collective-permute-start.18) | collective-permute-done | bytes 49184 | tf_op jit(solution)/shard_map/ppermute | solution.py:59
  79.0 2.0 %collective-permute-start.22 = (bf16[8,6144]{1,0:T(8,128)(2,1)S(1)}, bf16[8,6144]{1,0:T(8,128)(2,1)S(1)}, u32[]{:S(2)}, u32[]{:S(2)}) collective-permute-start(bf16[8,6144]{1,0:T(8,128)(2,1)S(1)} %collective-permute-done.20.refs_2_.refs_4_), channel_id=1, source_target_pairs={{0,2},{4,0},{8,4},{12,8},{14,12},{10,14},{6,10},{2,6},{1,3},{5,1},... | collective-permute-start | bytes 294920 | tf_op jit(solution)/shard_map/ppermute | solution.py:55
  81.0 3.1 %load.15.refs_11_ = bf16[1536,2304]{1,0:T(8,128)(2,1)S(1)} custom-call(bf16[6144,2304]{1,0:T(8,128)(2,1)} %refs_0_.18, bf16[8,6144]{1,0:T(8,128)(2,1)S(1)} %collective-permute-done.19.refs_1_.refs_3_, bf16[8,6144]{1,0:T(8,128)(2,1)S(1)} %collective-permute-done.20.refs_2_.refs_4_), custom_call_target="tpu_custom_call" | custom-call | tf_op jit(solution)/shard_map/load/pallas_call | solution.py:107
  84.2 5.0 %output_project.1 = (f32[4,8,2304]{2,1,0:T(8,128)S(1)}, f32[4,8,2304]{2,1,0:T(8,128)S(1)}) custom-call(bf16[8,6144]{1,0:T(8,128)(2,1)S(1)} %pad_maximum_fusion.refs_1_.refs_0_, bf16[8,6144]{1,0:T(8,128)(2,1)S(1)} %collective-permute-done.16.refs_1_, bf16[8,6144]{1,0:T(8,128)(2,1)S(1)} %collective-permute-done.17.refs_2_, ...), custom_call_target="tpu_custom_call" | custom-call | tf_op jit(solution)/shard_map/output_project/pallas_call | solution.py:365
  89.2 0.1 collective-permute-start.23
  89.3 1.6 %collective-permute-done.23 = f32[4,8,2304]{2,1,0:T(8,128)S(1)} collective-permute-done((f32[4,8,2304]{2,1,0:T(8,128)S(1)}, f32[4,8,2304]{2,1,0:T(8,128)S(1)}, u32[]{:S(2)}, u32[]{:S(2)}) %collective-permute-start.23) | collective-permute-done | bytes 294944 | tf_op jit(solution)/shard_map/ppermute | solution.py:44
  90.9 0.7 fusion
  (34 shorter events, 0.2 us)
Async XLA Ops:
  0.0 12.3 %collective-permute-start.1 = (bf16[8,9216]{1,0:T(8,128)(2,1)}, bf16[8,9216]{1,0:T(8,128)(2,1)S(1)}, u32[]{:S(2)}, u32[]{:S(2)}) collective-permute-start(bf16[8,9216]{1,0:T(8,128)(2,1)} %refs_3_.1), channel_id=1, source_target_pairs={{0,4},{4,8},{8,12},{12,14},{14,10},{10,6},{6,2},{2,0},{1,5},{5,9},... | collective-permute-start | bytes 442376 | tf_op jit(solution)/shard_map/ppermute | solution.py:55
  3.0 9.3 %collective-permute-start.2 = (bf16[8,9216]{1,0:T(8,128)(2,1)}, bf16[8,9216]{1,0:T(8,128)(2,1)S(1)}, u32[]{:S(2)}, u32[]{:S(2)}) collective-permute-start(bf16[8,9216]{1,0:T(8,128)(2,1)} %refs_3_.1), channel_id=1, source_target_pairs={{0,2},{4,0},{8,4},{12,8},{14,12},{10,14},{6,10},{2,6},{1,3},{5,1},... | collective-permute-start | bytes 442376 | tf_op jit(solution)/shard_map/ppermute | solution.py:55
  4.0 8.3 %collective-permute-start = (bf16[8,4608]{1,0:T(8,128)(2,1)S(1)}, bf16[8,4608]{1,0:T(8,128)(2,1)S(1)}, u32[]{:S(2)}, u32[]{:S(2)}) collective-permute-start(bf16[8,4608]{1,0:T(8,128)(2,1)S(1)} %get-tuple-element.110), channel_id=1, source_target_pairs={{0,14},{4,10},{8,6},{12,2},{14,0},{10,4},{6,8},{2,12},{1,15},{5,11... | collective-permute-start | bytes 221192 | tf_op jit(solution)/shard_map/ppermute | solution.py:59
  9.1 8.5 %collective-permute-start.3 = (bf16[8,4608]{1,0:T(8,128)(2,1)S(1)}, bf16[8,4608]{1,0:T(8,128)(2,1)S(1)}, u32[]{:S(2)}, u32[]{:S(2)}) collective-permute-start(bf16[8,4608]{1,0:T(8,128)(2,1)S(1)} %get-tuple-element.109), channel_id=1, source_target_pairs={{0,14},{4,10},{8,6},{12,2},{14,0},{10,4},{6,8},{2,12},{1,15},{5,11... | collective-permute-start | bytes 221192 | tf_op jit(solution)/shard_map/ppermute | solution.py:59
  12.3 5.9 %collective-permute-start.4 = (bf16[8,9216]{1,0:T(8,128)(2,1)S(1)}, bf16[8,9216]{1,0:T(8,128)(2,1)S(1)}, u32[]{:S(2)}, u32[]{:S(2)}) collective-permute-start(bf16[8,9216]{1,0:T(8,128)(2,1)S(1)} %collective-permute-done.1.refs_1_.refs_4_), channel_id=1, source_target_pairs={{0,4},{4,8},{8,12},{12,14},{14,10},{10,6},{6,2},{2,0},{1,5},{5,9},... | collective-permute-start | bytes 442376 | tf_op jit(solution)/shard_map/ppermute | solution.py:55
  14.1 6.3 %collective-permute-start.5 = (bf16[8,9216]{1,0:T(8,128)(2,1)S(1)}, bf16[8,9216]{1,0:T(8,128)(2,1)S(1)}, u32[]{:S(2)}, u32[]{:S(2)}) collective-permute-start(bf16[8,9216]{1,0:T(8,128)(2,1)S(1)} %collective-permute-done.2.refs_2_.refs_5_), channel_id=1, source_target_pairs={{0,2},{4,0},{8,4},{12,8},{14,12},{10,14},{6,10},{2,6},{1,3},{5,1},... | collective-permute-start | bytes 442376 | tf_op jit(solution)/shard_map/ppermute | solution.py:55
  14.4 8.6 %copy-start = (bf16[8,9216]{1,0:T(8,128)(2,1)S(1)}, bf16[8,9216]{1,0:T(8,128)(2,1)}, u32[]{:S(2)}) copy-start(bf16[8,9216]{1,0:T(8,128)(2,1)} %refs_3_.1) | copy-start | bytes 442372
  20.4 6.0 %collective-permute-start.6 = (bf16[8,9216]{1,0:T(8,128)(2,1)S(1)}, bf16[8,9216]{1,0:T(8,128)(2,1)S(1)}, u32[]{:S(2)}, u32[]{:S(2)}) collective-permute-start(bf16[8,9216]{1,0:T(8,128)(2,1)S(1)} %collective-permute-done.4.refs_1_.refs_6_), channel_id=1, source_target_pairs={{0,4},{4,8},{8,12},{12,14},{14,10},{10,6},{6,2},{2,0},{1,5},{5,9},... | collective-permute-start | bytes 442376 | tf_op jit(solution)/shard_map/ppermute | solution.py:55
  23.0 5.1 %collective-permute-start.7 = (bf16[8,9216]{1,0:T(8,128)(2,1)S(1)}, bf16[8,9216]{1,0:T(8,128)(2,1)S(1)}, u32[]{:S(2)}, u32[]{:S(2)}) collective-permute-start(bf16[8,9216]{1,0:T(8,128)(2,1)S(1)} %collective-permute-done.5.refs_2_.refs_7_), channel_id=1, source_target_pairs={{0,2},{4,0},{8,4},{12,8},{14,12},{10,14},{6,10},{2,6},{1,3},{5,1},... | collective-permute-start | bytes 442376 | tf_op jit(solution)/shard_map/ppermute | solution.py:55
  23.1 5.4 %copy-start.2 = (bf16[9216]{0:T(1024)(128)(2,1)S(1)}, bf16[9216]{0:T(1024)(128)(2,1)}, u32[]{:S(2)}) copy-start(bf16[9216]{0:T(1024)(128)(2,1)} %param.9) | copy-start | bytes 55300
  28.5 3.4 %collective-permute-start.8 = (f32[64,128]{1,0:T(8,128)S(1)}, f32[64,128]{1,0:T(8,128)S(1)}, u32[]{:S(2)}, u32[]{:S(2)}) collective-permute-start(f32[64,128]{1,0:T(8,128)S(1)} %row_sums.7.refs_2_.refs_0_), channel_id=1, source_target_pairs={{0,1},{1,0},{2,3},{3,2},{4,5},{5,4},{6,7},{7,6},{8,9},{9,8},{10,11... | collective-permute-start | bytes 98312 | tf_op jit(solution)/shard_map/ppermute | solution.py:44
  31.9 12.2 %copy-start.1 = (s32[4]{0:T(128)S(1)}, s32[4]{0:T(128)}, u32[]{:S(2)}) copy-start(s32[4]{0:T(128)} %refs_0_.15) | copy-start | bytes 52
  42.3 1.6 %collective-permute-start.9 = (f32[8,4,1664]{2,1,0:T(4,128)S(1)}, f32[8,4,1664]{2,1,0:T(4,128)S(1)}, u32[]{:S(2)}, u32[]{:S(2)}) collective-permute-start(f32[8,4,1664]{2,1,0:T(4,128)S(1)} %get-tuple-element.78), channel_id=1, source_target_pairs={{0,1},{1,0},{2,3},{3,2},{4,5},{5,4},{6,7},{7,6},{8,9},{9,8},{10,11... | collective-permute-start | bytes 638984 | tf_op jit(solution)/shard_map/ppermute | solution.py:44
  44.0 4.2 %collective-permute-start.10 = (bf16[4,4,1664]{2,1,0:T(4,128)(2,1)S(1)}, bf16[4,4,1664]{2,1,0:T(4,128)(2,1)S(1)}, u32[]{:S(2)}, u32[]{:S(2)}) collective-permute-start(bf16[4,4,1664]{2,1,0:T(4,128)(2,1)S(1)} %get-tuple-element.80), channel_id=1, source_target_pairs={{0,2},{2,0},{4,6},{6,4},{8,10},{10,8},{12,14},{14,12},{1,3},{3,1},... | collective-permute-start | bytes 159752 | tf_op jit(solution)/shard_map/ppermute | solution.py:508
  48.3 7.7 %collective-permute-start.11 = (bf16[2,4,1664]{2,1,0:T(4,128)(2,1)S(1)}, bf16[2,4,1664]{2,1,0:T(4,128)(2,1)S(1)}, u32[]{:S(2)}, u32[]{:S(2)}) collective-permute-start(bf16[2,4,1664]{2,1,0:T(4,128)(2,1)S(1)} %get-tuple-element.81.refs_1_), channel_id=1, source_target_pairs={{0,4},{2,6},{4,0},{6,2},{8,12},{10,14},{12,8},{14,10},{1,5},{3,7},... | collective-permute-start | bytes 79880 | tf_op jit(solution)/shard_map/ppermute | solution.py:512
  48.7 7.3 %collective-permute-start.12 = (bf16[2,4,1664]{2,1,0:T(4,128)(2,1)S(1)}, bf16[2,4,1664]{2,1,0:T(4,128)(2,1)S(1)}, u32[]{:S(2)}, u32[]{:S(2)}) collective-permute-start(bf16[2,4,1664]{2,1,0:T(4,128)(2,1)S(1)} %get-tuple-element.83), channel_id=1, source_target_pairs={{0,8},{2,10},{4,12},{6,14},{8,0},{10,2},{12,4},{14,6},{1,9},{3,11}... | collective-permute-start | bytes 79880 | tf_op jit(solution)/shard_map/ppermute | solution.py:512
  50.5 5.6 %collective-permute-start.13 = (bf16[2,4,1664]{2,1,0:T(4,128)(2,1)S(1)}, bf16[2,4,1664]{2,1,0:T(4,128)(2,1)S(1)}, u32[]{:S(2)}, u32[]{:S(2)}) collective-permute-start(bf16[2,4,1664]{2,1,0:T(4,128)(2,1)S(1)} %get-tuple-element.84), channel_id=1, source_target_pairs={{0,12},{2,14},{4,8},{6,10},{8,4},{10,6},{12,0},{14,2},{1,13},{3,15... | collective-permute-start | bytes 79880 | tf_op jit(solution)/shard_map/ppermute | solution.py:512
  59.6 1.3 %collective-permute-start.14 = (bf16[4,6144]{1,0:T(4,128)(2,1)S(1)}, bf16[4,6144]{1,0:T(4,128)(2,1)S(1)}, u32[]{:S(2)}, u32[]{:S(2)}) collective-permute-start(bf16[4,6144]{1,0:T(4,128)(2,1)S(1)} %get-tuple-element.92), channel_id=1, source_target_pairs={{0,1},{1,0},{2,3},{3,2},{4,5},{5,4},{6,7},{7,6},{8,9},{9,8},{10,11... | collective-permute-start | bytes 147464 | tf_op jit(solution)/shard_map/ppermute | solution.py:44
  60.9 9.0 %collective-permute-start.16 = (bf16[8,6144]{1,0:T(8,128)(2,1)S(1)}, bf16[8,6144]{1,0:T(8,128)(2,1)S(1)}, u32[]{:S(2)}, u32[]{:S(2)}) collective-permute-start(bf16[8,6144]{1,0:T(8,128)(2,1)S(1)} %pad_maximum_fusion.refs_1_.refs_0_), channel_id=1, source_target_pairs={{0,4},{4,8},{8,12},{12,14},{14,10},{10,6},{6,2},{2,0},{1,5},{5,9},... | collective-permute-start | bytes 294920 | tf_op jit(solution)/shard_map/ppermute | solution.py:55
  61.0 8.9 %collective-permute-start.17 = (bf16[8,6144]{1,0:T(8,128)(2,1)S(1)}, bf16[8,6144]{1,0:T(8,128)(2,1)S(1)}, u32[]{:S(2)}, u32[]{:S(2)}) collective-permute-start(bf16[8,6144]{1,0:T(8,128)(2,1)S(1)} %pad_maximum_fusion.refs_1_.refs_0_), channel_id=1, source_target_pairs={{0,2},{4,0},{8,4},{12,8},{14,12},{10,14},{6,10},{2,6},{1,3},{5,1},... | collective-permute-start | bytes 294920 | tf_op jit(solution)/shard_map/ppermute | solution.py:55
  63.1 6.9 %collective-permute-start.15 = (bf16[8,3072]{1,0:T(8,128)(2,1)S(1)}, bf16[8,3072]{1,0:T(8,128)(2,1)S(1)}, u32[]{:S(2)}, u32[]{:S(2)}) collective-permute-start(bf16[8,3072]{1,0:T(8,128)(2,1)S(1)} %get-tuple-element.112), channel_id=1, source_target_pairs={{0,14},{4,10},{8,6},{12,2},{14,0},{10,4},{6,8},{2,12},{1,15},{5,11... | collective-permute-start | bytes 147464 | tf_op jit(solution)/shard_map/ppermute | solution.py:59
  69.9 9.1 %collective-permute-start.19 = (bf16[8,6144]{1,0:T(8,128)(2,1)S(1)}, bf16[8,6144]{1,0:T(8,128)(2,1)S(1)}, u32[]{:S(2)}, u32[]{:S(2)}) collective-permute-start(bf16[8,6144]{1,0:T(8,128)(2,1)S(1)} %collective-permute-done.16.refs_1_), channel_id=1, source_target_pairs={{0,4},{4,8},{8,12},{12,14},{14,10},{10,6},{6,2},{2,0},{1,5},{5,9},... | collective-permute-start | bytes 294920 | tf_op jit(solution)/shard_map/ppermute | solution.py:55
  70.0 9.0 %collective-permute-start.20 = (bf16[8,6144]{1,0:T(8,128)(2,1)S(1)}, bf16[8,6144]{1,0:T(8,128)(2,1)S(1)}, u32[]{:S(2)}, u32[]{:S(2)}) collective-permute-start(bf16[8,6144]{1,0:T(8,128)(2,1)S(1)} %collective-permute-done.17.refs_2_), channel_id=1, source_target_pairs={{0,2},{4,0},{8,4},{12,8},{14,12},{10,14},{6,10},{2,6},{1,3},{5,1},... | collective-permute-start | bytes 294920 | tf_op jit(solution)/shard_map/ppermute | solution.py:55
  72.0 7.0 %collective-permute-start.18 = (bf16[8,3072]{1,0:T(8,128)(2,1)S(1)}, bf16[8,3072]{1,0:T(8,128)(2,1)S(1)}, u32[]{:S(2)}, u32[]{:S(2)}) collective-permute-start(bf16[8,3072]{1,0:T(8,128)(2,1)S(1)} %get-tuple-element.111), channel_id=1, source_target_pairs={{0,14},{4,10},{8,6},{12,2},{14,0},{10,4},{6,8},{2,12},{1,15},{5,11... | collective-permute-start | bytes 147464 | tf_op jit(solution)/shard_map/ppermute | solution.py:59
  79.0 5.2 %collective-permute-start.21 = (bf16[8,6144]{1,0:T(8,128)(2,1)S(1)}, bf16[8,6144]{1,0:T(8,128)(2,1)S(1)}, u32[]{:S(2)}, u32[]{:S(2)}) collective-permute-start(bf16[8,6144]{1,0:T(8,128)(2,1)S(1)} %collective-permute-done.19.refs_1_.refs_3_), channel_id=1, source_target_pairs={{0,4},{4,8},{8,12},{12,14},{14,10},{10,6},{6,2},{2,0},{1,5},{5,9},... | collective-permute-start | bytes 294920 | tf_op jit(solution)/shard_map/ppermute | solution.py:55
  79.0 5.2 %collective-permute-start.22 = (bf16[8,6144]{1,0:T(8,128)(2,1)S(1)}, bf16[8,6144]{1,0:T(8,128)(2,1)S(1)}, u32[]{:S(2)}, u32[]{:S(2)}) collective-permute-start(bf16[8,6144]{1,0:T(8,128)(2,1)S(1)} %collective-permute-done.20.refs_2_.refs_4_), channel_id=1, source_target_pairs={{0,2},{4,0},{8,4},{12,8},{14,12},{10,14},{6,10},{2,6},{1,3},{5,1},... | collective-permute-start | bytes 294920 | tf_op jit(solution)/shard_map/ppermute | solution.py:55
  89.2 1.6 %collective-permute-start.23 = (f32[4,8,2304]{2,1,0:T(8,128)S(1)}, f32[4,8,2304]{2,1,0:T(8,128)S(1)}, u32[]{:S(2)}, u32[]{:S(2)}) collective-permute-start(f32[4,8,2304]{2,1,0:T(8,128)S(1)} %get-tuple-element.108), channel_id=1, source_target_pairs={{0,1},{1,0},{2,3},{3,2},{4,5},{5,4},{6,7},{7,6},{8,9},{9,8},{10,11... | collective-permute-start | bytes 884744 | tf_op jit(solution)/shard_map/ppermute | solution.py:44

commit v9 on v8

--- a/solution.py
+++ b/solution.py
@@ -53,10 +53,6 @@
 
     def step(self, left, right):
         return lax.ppermute(left, "gx", self.onward), lax.ppermute(right, "gx", self.back)
-
-    def send_across(self, shard, part):
-        half = shard.shape[1] // 2
-        return lax.ppermute(shard[:, part * half : (part + 1) * half], "gx", self.across)
 
 
 def owners(n):
@@ -113,6 +109,29 @@
         compiler_params=pltpu.CompilerParams(vmem_limit_bytes=MIB),
         name="load",
     )(*[in_hbm(job[0]) for job in jobs], *after)
+
+
+def load_caches_kernel(*refs):
+    sources, targets, sems = refs[:2], refs[-3:-1], refs[-1]
+    copies = []
+    for i, (source, target) in enumerate(zip(sources, targets)):
+        for row in range(source.shape[0]):
+            copies.append(pltpu.make_async_copy(source.at[row], target.at[row], sems.at[i, row]))
+            copies[-1].start()
+    for copy in copies:
+        copy.wait()
+
+
+def load_caches(keys, values, after):
+    return pl.pallas_call(
+        load_caches_kernel,
+        out_shape=[pltpu.VMEM(a.shape, a.dtype) for a in (keys, values)],
+        in_specs=[IN_HBM] * 2 + [ANY] * len(after),
+        out_specs=[IN_VMEM] * 2,
+        scratch_shapes=[pltpu.SemaphoreType.DMA((2, keys.shape[0]))],
+        compiler_params=pltpu.CompilerParams(vmem_limit_bytes=MIB),
+        name="load_caches",
+    )(in_hbm(keys), in_hbm(values), *after)
 
 
 def in_hbm(array):
@@ -159,15 +178,11 @@
 
 def project_kernel(n, parts, *refs):
     sums_a, sums_b, gain = refs[:3]
-    shards = refs[3 : 3 + n]
-    weights = refs[3 + n : 3 + n + parts]
-    caches = refs[3 + n + parts : 5 + n + parts]
-    keep, give, *copied, normed, total, sems = refs[5 + n + parts :]
-    copies = []
-    for i, (source, target) in enumerate(zip(caches, copied)):
-        for row in range(source.shape[0]):
-            copies.append(pltpu.make_async_copy(source.at[row], target.at[row], sems.at[i, row]))
-            copies[-1].start()
+    shards = refs[3 : 3 + n - 1]
+    far = refs[3 + n - 1 : 3 + n + 1]
+    weights = refs[4 + n : 4 + n + parts]
+    later, keep, give, early, normed, total, sems = refs[4 + n + parts :]
+    copies = start_copies(later.at[pl.ds(0, early.shape[0])], early, sems, 4)
     rows, width = shards[0].shape
     sums = sums_a[...] + sums_b[...]
     row_mean = sums[:, :1] / D
@@ -175,9 +190,10 @@
     scale = lax.rsqrt(row_square - row_mean * row_mean + epsilon)
     for part in range(2):
         cols = slice(part * width // 2, (part + 1) * width // 2)
-        for i, shard in enumerate(shards):
+        for i in range(n):
             at = slice(i * rows, (i + 1) * rows)
-            x = shard[:, cols].astype(jnp.float32)
+            x = shards[i][:, cols] if i < n - 1 else far[part][...]
+            x = x.astype(jnp.float32)
             normed[at, cols] = (x - row_mean[at]) * scale[at] * gain[:, cols]
         x = normed[:, cols].astype(jnp.bfloat16)
         start = 0
@@ -202,24 +218,31 @@
         copy.wait()
 
 
-def project(sums, gain, shards, weights, caches):
-    n = len(shards)
+def project(sums, gain, shards, far, weights, later, size):
+    n = len(shards) + 1
     rows, width = shards[0].shape
     stripe = sum(w.shape[0] for w in weights)
     shape = jax.ShapeDtypeStruct((n, rows // 2, stripe), jnp.float32)
     return pl.pallas_call(
         lambda *refs: project_kernel(n, len(weights), *refs),
-        out_shape=[shape, shape] + [pltpu.VMEM(a.shape, a.dtype) for a in caches],
-        in_specs=[IN_VMEM] * (3 + n + len(weights)) + [IN_HBM] * 2,
-        out_specs=[IN_VMEM] * 4,
+        out_shape=[shape, shape, pltpu.VMEM((size, later.shape[1]), later.dtype)],
+        in_specs=[IN_VMEM] * (4 + n + len(weights)) + [IN_HBM],
+        out_specs=[IN_VMEM] * 3,
         scratch_shapes=[
             pltpu.VMEM((n * rows, width), jnp.float32),
             pltpu.VMEM((n * rows, stripe), jnp.float32),
-            pltpu.SemaphoreType.DMA((2, caches[0].shape[0])),
+            pltpu.SemaphoreType.DMA((4,)),
         ],
-        compiler_params=pltpu.CompilerParams(vmem_limit_bytes=8 * MIB),
+        compiler_params=pltpu.CompilerParams(vmem_limit_bytes=6 * MIB),
         name="project",
-    )(*sums, gain, *shards, *[in_vmem(w) for w in weights], *[in_hbm(a) for a in caches])
+    )(
+        *sums,
+        gain,
+        *shards,
+        *far,
+        *[in_vmem(w) for w in weights],
+        in_hbm(later),
+    )
 
 
 def split_kernel(keep, got, here, there):
@@ -335,20 +358,32 @@
 
 
 def output_kernel(n, *refs):
-    shards = refs[:n]
-    weights = refs[n:-4]
+    shards = refs[: n - 1]
+    far = refs[n - 1 : n + 1]
+    weights = refs[n + 1 : -4]
     keep, give, total, placed = refs[-4:]
     rows = shards[0].shape[0]
-    start = 0
-    for weight in weights:
-        cols = slice(start, start + weight.shape[0])
-        x = jnp.concatenate([ref[:, cols].astype(jnp.float32) for ref in shards], axis=0)
-        term = jnp.dot(x.astype(jnp.bfloat16), weight[...], preferred_element_type=jnp.float32)
-        if start == 0:
-            total[...] = term
-        else:
-            total[...] += term
-        start = cols.stop
+    half = far[0].shape[1]
+    for part in range(2):
+        start = part * half
+        cols = slice(start, start + half)
+        x = [ref[:, cols] for ref in shards] + [far[part][...]]
+        x = jnp.concatenate([piece.astype(jnp.float32) for piece in x], axis=0)
+        x = x.astype(jnp.bfloat16)
+        first = 0
+        for weight in weights:
+            last = first + weight.shape[0]
+            if start <= first and last <= start + half:
+                term = jnp.dot(
+                    x[:, first - start : last - start],
+                    weight[...],
+                    preferred_element_type=jnp.float32,
+                )
+                if first == 0:
+                    total[...] = term
+                else:
+                    total[...] += term
+            first = last
     side = lax.axis_index("gy")
     for i, owner in enumerate(owners(n)):
         block = total[i * rows : (i + 1) * rows, :]
@@ -357,15 +392,15 @@
     give[...] = placed[pl.ds((1 - side) * (n // 2), n // 2)]
 
 
-def output_project(shards, weights):
-    n = len(shards)
+def output_project(shards, far, weights):
+    n = len(shards) + 1
     rows = shards[0].shape[0]
     cols = weights[0].shape[1]
     shape = jax.ShapeDtypeStruct((n // 2, rows, cols), jnp.float32)
     return pl.pallas_call(
         lambda *refs: output_kernel(n, *refs),
         out_shape=[shape, shape],
-        in_specs=[IN_VMEM] * (n + len(weights)),
+        in_specs=[IN_VMEM] * (n + 1 + len(weights)),
         out_specs=[IN_VMEM] * 2,
         scratch_shapes=[
             pltpu.VMEM((n * rows, cols), jnp.float32),
@@ -373,7 +408,7 @@
         ],
         compiler_params=pltpu.CompilerParams(vmem_limit_bytes=8 * MIB),
         name="output_project",
-    )(*shards, *[in_vmem(w) for w in weights])
+    )(*shards, *far, *[in_vmem(w) for w in weights])
 
 
 def on_any_grid(
@@ -478,61 +513,63 @@
 
     left = right = activations
     shards = [activations]
-    far = []
-    sums = ()
     for step in range(1, n // 2):
-        arrived = shards[-2:] if step > 1 else shards
+        arrived = shards[-2:] if step > 1 else []
         left, right = ring.step(left, right)
-        weight = piece_of(query_weight, (step - 1) * piece, piece, arrived if step > 1 else [])
-        if step <= 2:
-            half = ring.send_across(activations, step - 1)
-            weight, (half,) = before(weight, half)
-            far.append(half)
-        weight, (left, right, *arrived) = before(weight, left, right, *arrived)
-        sums = (row_sums(arrived, sums),)
+        if step > 1:
+            sums = row_sums(arrived, [sums])
+        weight = piece_of(query_weight, (step - 1) * piece, piece, arrived)
+        if step == 1:
+            weight, (own,) = before(weight, activations)
+            sums = row_sums([own])
+            far_sums = lax.ppermute(sums, "gx", ring.across)
+            weight, (left, right, sums) = before(weight, left, right, sums)
+        else:
+            weight, (left, right) = before(weight, left, right)
         weights.append(weight)
         shards += [left, right]
-    shards.append(jnp.concatenate(far, axis=1))
-    sums = row_sums([left, right, shards[-1]], sums)
+    cut, (cut_right, left, right) = before(
+        left[:, : width // 2], right[:, width // 2 :], left, right
+    )
+    far = ring.step(cut, cut_right)
+    sums = row_sums([left, right], [sums])
     jobs = [(query_weight, 3 * piece, piece, 0), (keyval_weight, 0, new_cols, None)]
     weight = load(piece + 2 * new_cols, jobs, [sums])
+    sums = jnp.concatenate([sums, far_sums], axis=0)
     other_sums = swap_pair(sums)
-    weight, (other_sums,) = before(weight, other_sums)
+    weight, (other_sums, *far) = before(weight, other_sums, *far)
     weights.append(weight)
     gain = norm_gain.astype(jnp.float32)[None, :]
-    keep, give, keys, values = project(
-        (sums, other_sums), gain, shards, weights, [cache_keys, cache_values]
-    )
+    piece = output_weight.shape[0] // 4
+    keep, give, weight = project(
+        (sums, other_sums), gain, shards, far, weights, output_weight, 2 * piece
+    )
+    weights = [weight]
 
     here, there = split(keep, swap_pair(give))
     came = lax.ppermute(there, "gx", [(i, i ^ 1) for i in range(n)])
+    keys, values = load_caches(cache_keys, cache_values, [there])
+    keys, (came,) = before(keys, came)
     blocks = pair(here, came)
     arrived = [blocks[0]]
     for d in range(1, n // 2):
         arrived.append(lax.ppermute(blocks[d], "gx", [(i, i ^ (2 * d)) for i in range(n)]))
-    piece = output_weight.shape[0] // 4
-    weight = piece_of(output_weight, 0, piece, [blocks[1]])
-    weight, arrived = before(weight, *arrived)
-    weights = [weight]
     mine, other = attend(cache_lengths, arrived, cosine, sine, keys, values)
     shard = jnp.concatenate([mine, swap_pair(other)], axis=0)
 
     left = right = shard
     shards = [shard]
-    far = []
     for step in range(1, n // 2):
         arrived = shards[-2:]
         left, right = ring.step(left, right)
-        weight = piece_of(output_weight, step * piece, piece, arrived)
         if step <= 2:
-            half = ring.send_across(shard, step - 1)
-            weight, (half,) = before(weight, half)
-            far.append(half)
-        weight, (left, right) = before(weight, left, right)
-        weights.append(weight)
+            weight = piece_of(output_weight, (1 + step) * piece, piece, arrived)
+            weight, (left, right) = before(weight, left, right)
+            weights.append(weight)
         shards += [left, right]
-    shards.append(jnp.concatenate(far, axis=1))
-    keep, give = output_project(shards, weights)
+    half = shard.shape[1] // 2
+    far = ring.step(left[:, :half], right[:, half:])
+    keep, give = output_project(shards, far, weights)
     out = (keep + swap_pair(give)).astype(jnp.bfloat16)
     return out.reshape(-1, out.shape[-1])
 

time: 91.7 us -> 89.9 us (0.980)
  waiting for transfers between devices: 16.5 us -> 18.2 us
  Pallas kernels: 44.8 us -> 43.4 us
  starting transfers between devices: 28 us -> 26.9 us
  local copies, waits for them, and re-layouts: 0.99 us -> 0.03 us
    ppermute x4 -> x1, starting transfers between devices: 9.05 us -> 2.3 us  [on_device(): far_sums = lax.ppermute(sums, 'gx', ring.across)]
    pallas_call x8 -> x6, Pallas kernels: 25.2 us -> 18.9 us  [load(): pl.pallas_call(lambda *refs: load_kernel([job[1:] for job in jobs], *refs...]
    ppermute x6 -> x8, starting transfers between devices: 7.42 us -> 12.2 us  [step(): lax.ppermute(left, 'gx', self.onward)]
    ppermute x6 -> x8, waiting for transfers between devices: 0.67 us -> 5.09 us  [step(): lax.ppermute(left, 'gx', self.onward)]
    ppermute x1, waiting for transfers between devices: 4.1 us -> 0.01 us  [on_device(): came = lax.ppermute(there, 'gx', [(i, i ^ 1) for i in range(n)])]
    ppermute x4 -> x1, waiting for transfers between devices: 3.75 us -> 0.01 us  [on_device(): far_sums = lax.ppermute(sums, 'gx', ring.across)]
    pallas_call x0 -> x1, Pallas kernels: none -> 3.48 us  [load_caches(): pl.pallas_call(load_caches_kernel, out_shape=[pltpu.VMEM(a.shape, a.dtype...]
    ppermute x3, waiting for transfers between devices: 0.17 us -> 3.12 us  [on_device(): lax.ppermute(blocks[d], 'gx', [(i, i ^ 2 * d) for i in range(n)])]
  transfers between devices with their start and end apart: 24 -> 25, of which waited for: 10 -> 12; matrix products, arithmetic and copies ran while one was open for 1% -> 0% of each run, Pallas kernels for 28% -> 26%
where the time goes in v9:
time: 89.9 us; the launch traced here: 89.7 us
  Pallas kernels  43.4 us (48%)
  starting transfers between devices  26.9 us (30%)
  waiting for transfers between devices  18.2 us (20%)
    pallas_call x6, Pallas kernels, load(): pl.pallas_call(lambda *refs: load_kernel([job[1:] for job in jobs], *refs...  18.9 us
    ppermute x8, starting transfers between devices, step(): lax.ppermute(left, 'gx', self.onward)  12.2 us
    pallas_call x1, Pallas kernels, project(): pl.pallas_call(lambda *refs: project_kernel(n, len(weights), *refs), out_...  11.7 us
    ppermute x8, waiting for transfers between devices, step(): lax.ppermute(right, 'gx', self.back)  6.12 us
    ppermute x8, starting transfers between devices, step(): lax.ppermute(right, 'gx', self.back)  5.57 us
    ppermute x8, waiting for transfers between devices, step(): lax.ppermute(left, 'gx', self.onward)  5.09 us
    pallas_call x1, Pallas kernels, output_project(): pl.pallas_call(lambda *refs: output_kernel(n, *refs), out_shape=[shape, s...  5.05 us
    ppermute x3, starting transfers between devices, on_device(): lax.ppermute(blocks[d], 'gx', [(i, i ^ 2 * d) for i in range(n)])  4.45 us
  transfers between devices with their start and end apart: 25, of which 12 were waited for; matrix products, arithmetic and copies ran while one was open for 0% of the time, Pallas kernels for 26%

profile of v9, /device:TPU:0, one launch (start us, length us, event | category | flops | bytes accessed | tf_op | source)
XLA Modules:
  0.0 89.7 jit_solution(7527877287478824479)
XLA Ops:
  0.0 3.0 %collective-permute-start = (bf16[8,9216]{1,0:T(8,128)(2,1)}, bf16[8,9216]{1,0:T(8,128)(2,1)S(1)}, u32[]{:S(2)}, u32[]{:S(2)}) collective-permute-start(bf16[8,9216]{1,0:T(8,128)(2,1)} %refs_3_.1), channel_id=1, source_target_pairs={{0,4},{4,8},{8,12},{12,14},{14,10},{10,6},{6,2},{2,0},{1,5},{5,9},... | collective-permute-start | bytes 442376 | tf_op jit(solution)/shard_map/ppermute | solution.py:55
  3.0 3.1 %load.6.refs_12_ = bf16[384,9216]{1,0:T(8,128)(2,1)S(1)} custom-call(bf16[1536,9216]{1,0:T(8,128)(2,1)} %refs_0_.12), custom_call_target="tpu_custom_call" | custom-call | tf_op jit(solution)/shard_map/load/pallas_call | solution.py:103
  6.2 0.2 row_sums.4.refs_0_
  6.3 0.8 collective-permute-done.refs_1_.refs_4_
  7.1 1.4 %collective-permute-done.1.refs_2_.refs_5_ = bf16[8,9216]{1,0:T(8,128)(2,1)S(1)} collective-permute-done((bf16[8,9216]{1,0:T(8,128)(2,1)}, bf16[8,9216]{1,0:T(8,128)(2,1)S(1)}, u32[]{:S(2)}, u32[]{:S(2)}) %collective-permute-start.1) | collective-permute-done | bytes 147488 | tf_op jit(solution)/shard_map/ppermute | solution.py:55
  8.5 1.6 %collective-permute-start.2 = (bf16[8,9216]{1,0:T(8,128)(2,1)S(1)}, bf16[8,9216]{1,0:T(8,128)(2,1)S(1)}, u32[]{:S(2)}, u32[]{:S(2)}) collective-permute-start(bf16[8,9216]{1,0:T(8,128)(2,1)S(1)} %collective-permute-done.refs_1_.refs_4_), channel_id=1, source_target_pairs={{0,4},{4,8},{8,12},{12,14},{14,10},{10,6},{6,2},{2,0},{1,5},{5,9},... | collective-permute-start | bytes 442376 | tf_op jit(solution)/shard_map/ppermute | solution.py:55
  10.1 0.4 collective-permute-start.3
  10.6 3.1 %load.7.refs_13_ = bf16[384,9216]{1,0:T(8,128)(2,1)S(1)} custom-call(bf16[1536,9216]{1,0:T(8,128)(2,1)} %refs_0_.12, bf16[8,9216]{1,0:T(8,128)(2,1)S(1)} %collective-permute-done.refs_1_.refs_4_, bf16[8,9216]{1,0:T(8,128)(2,1)S(1)} %collective-permute-done.1.refs_2_.refs_5_), custom_call_target="tpu_custom_call" | custom-call | tf_op jit(solution)/shard_map/load/pallas_call | solution.py:103
  13.7 1.6 %collective-permute-done.3.refs_2_.refs_7_ = bf16[8,9216]{1,0:T(8,128)(2,1)S(1)} collective-permute-done((bf16[8,9216]{1,0:T(8,128)(2,1)S(1)}, bf16[8,9216]{1,0:T(8,128)(2,1)S(1)}, u32[]{:S(2)}, u32[]{:S(2)}) %collective-permute-start.3) | collective-permute-done | bytes 147488 | tf_op jit(solution)/shard_map/ppermute | solution.py:55
  15.3 1.6 %collective-permute-start.4 = (bf16[8,9216]{1,0:T(8,128)(2,1)S(1)}, bf16[8,9216]{1,0:T(8,128)(2,1)S(1)}, u32[]{:S(2)}, u32[]{:S(2)}) collective-permute-start(bf16[8,9216]{1,0:T(8,128)(2,1)S(1)} %collective-permute-done.2.refs_1_.refs_6_), channel_id=1, source_target_pairs={{0,4},{4,8},{8,12},{12,14},{14,10},{10,6},{6,2},{2,0},{1,5},{5,9},... | collective-permute-start | bytes 442376 | tf_op jit(solution)/shard_map/ppermute | solution.py:55
  16.8 0.4 collective-permute-start.5
  17.3 2.3 %collective-permute-start.6 = (f32[8,128]{1,0:T(8,128)S(1)}, f32[8,128]{1,0:T(8,128)S(1)}, u32[]{:S(2)}, u32[]{:S(2)}) collective-permute-start(f32[8,128]{1,0:T(8,128)S(1)} %row_sums.4.refs_0_), channel_id=1, source_target_pairs={{0,14},{4,10},{8,6},{12,2},{14,0},{10,4},{6,8},{2,12},{1,15},{5,11... | collective-permute-start | bytes 12296 | tf_op jit(solution)/shard_map/ppermute | solution.py:525
  19.6 0.2 row_sums.5.refs_0_
  19.8 3.1 %load.8.refs_14_ = bf16[384,9216]{1,0:T(8,128)(2,1)S(1)} custom-call(bf16[1536,9216]{1,0:T(8,128)(2,1)} %refs_0_.12, bf16[8,9216]{1,0:T(8,128)(2,1)S(1)} %collective-permute-done.2.refs_1_.refs_6_, bf16[8,9216]{1,0:T(8,128)(2,1)S(1)} %collective-permute-done.3.refs_2_.refs_7_), custom_call_target="tpu_custom_call" | custom-call | tf_op jit(solution)/shard_map/load/pallas_call | solution.py:103
  22.9 0.2 row_sums.6.refs_0_
  23.1 0.8 collective-permute-start.8
  23.9 1.3 %collective-permute-start.9 = (bf16[8,4608]{1,0:T(8,128)(2,1)S(1)}, bf16[8,4608]{1,0:T(8,128)(2,1)S(1)}, u32[]{:S(2)}, u32[]{:S(2)}) collective-permute-start(bf16[8,4608]{1,0:T(8,128)(2,1)S(1)} %slice.13), channel_id=1, source_target_pairs={{0,2},{4,0},{8,4},{12,8},{14,12},{10,14},{6,10},{2,6},{1,3},{5,1},... | collective-permute-start | bytes 221192 | tf_op jit(solution)/shard_map/ppermute | solution.py:55
  25.2 0.2 row_sums.7.refs_2_
  25.5 3.4 %load.9.refs_15_ = bf16[512,9216]{1,0:T(8,128)(2,1)S(1)} custom-call(bf16[1536,9216]{1,0:T(8,128)(2,1)} %refs_0_.12, bf16[64,9216]{1,0:T(8,128)(2,1)} %refs_1_.2, f32[56,128]{1,0:T(8,128)S(1)} %row_sums.7.refs_2_), custom_call_target="tpu_custom_call" | custom-call | tf_op jit(solution)/shard_map/load/pallas_call | solution.py:103
  28.9 11.7 %project.1 = (f32[8,4,1664]{2,1,0:T(4,128)S(1)}, f32[8,4,1664]{2,1,0:T(4,128)S(1)}, bf16[3072,2304]{1,0:T(8,128)(2,1)S(1)}) custom-call(f32[64,128]{1,0:T(8,128)S(1)} %pad_maximum_fusion.1.refs_0_, f32[64,128]{1,0:T(8,128)S(1)} %collective-permute-done.7.refs_1_, f32[1,9216]{1,0:T(1,128)S(1)} %bitcast.3, bf16[8,9216]{1,0:T(8,128)(2,1)S(1)} %copy-done, ...), custom_call_target="tpu_custom_call" | custom-call | tf_op jit(solution)/shard_map/project/pallas_call | solution.py:226
  40.6 0.5 collective-permute-start.10
  41.1 1.1 %collective-permute-done.10.got = f32[8,4,1664]{2,1,0:T(4,128)S(1)} collective-permute-done((f32[8,4,1664]{2,1,0:T(4,128)S(1)}, f32[8,4,1664]{2,1,0:T(4,128)S(1)}, u32[]{:S(2)}, u32[]{:S(2)}) %collective-permute-start.10) | collective-permute-done | bytes 213024 | tf_op jit(solution)/shard_map/ppermute | solution.py:44
  42.3 1.7 %collective-permute-start.11 = (bf16[4,4,1664]{2,1,0:T(4,128)(2,1)S(1)}, bf16[4,4,1664]{2,1,0:T(4,128)(2,1)S(1)}, u32[]{:S(2)}, u32[]{:S(2)}) collective-permute-start(bf16[4,4,1664]{2,1,0:T(4,128)(2,1)S(1)} %get-tuple-element.71.refs_2_), channel_id=1, source_target_pairs={{0,2},{2,0},{4,6},{6,4},{8,10},{10,8},{12,14},{14,12},{1,3},{3,1},... | collective-permute-start | bytes 159752 | tf_op jit(solution)/shard_map/ppermute | solution.py:550
  44.0 3.5 %load_caches.1 = (bf16[4,2048,256]{2,1,0:T(8,128)(2,1)S(1)}, bf16[4,2048,256]{2,1,0:T(8,128)(2,1)S(1)}) custom-call(bf16[4,2048,256]{2,1,0:T(8,128)(2,1)} %refs_0_.13, bf16[4,2048,256]{2,1,0:T(8,128)(2,1)} %refs_1_.3, bf16[4,4,1664]{2,1,0:T(4,128)(2,1)S(1)} %get-tuple-element.71.refs_2_), custom_call_target="tpu_custom_call" | custom-call | tf_op jit(solution)/shard_map/load_caches/pallas_call | solution.py:126
  47.5 0.7 collective-permute-start.12
  48.2 1.3 %collective-permute-start.13 = (bf16[2,4,1664]{2,1,0:T(4,128)(2,1)S(1)}, bf16[2,4,1664]{2,1,0:T(4,128)(2,1)S(1)}, u32[]{:S(2)}, u32[]{:S(2)}) collective-permute-start(bf16[2,4,1664]{2,1,0:T(4,128)(2,1)S(1)} %get-tuple-element.76), channel_id=1, source_target_pairs={{0,8},{2,10},{4,12},{6,14},{8,0},{10,2},{12,4},{14,6},{1,9},{3,11}... | collective-permute-start | bytes 79880 | tf_op jit(solution)/shard_map/ppermute | solution.py:556
  49.5 2.4 %collective-permute-start.14 = (bf16[2,4,1664]{2,1,0:T(4,128)(2,1)S(1)}, bf16[2,4,1664]{2,1,0:T(4,128)(2,1)S(1)}, u32[]{:S(2)}, u32[]{:S(2)}) collective-permute-start(bf16[2,4,1664]{2,1,0:T(4,128)(2,1)S(1)} %get-tuple-element.77), channel_id=1, source_target_pairs={{0,12},{2,14},{4,8},{6,10},{8,4},{10,6},{12,0},{14,2},{1,13},{3,15... | collective-permute-start | bytes 79880 | tf_op jit(solution)/shard_map/ppermute | solution.py:556
  51.9 0.1 multiply_sine_fusion
  52.0 0.9 %collective-permute-done.13.refs_3_ = bf16[2,4,1664]{2,1,0:T(4,128)(2,1)S(1)} collective-permute-done((bf16[2,4,1664]{2,1,0:T(4,128)(2,1)S(1)}, bf16[2,4,1664]{2,1,0:T(4,128)(2,1)S(1)}, u32[]{:S(2)}, u32[]{:S(2)}) %collective-permute-start.13) | collective-permute-done | bytes 26656 | tf_op jit(solution)/shard_map/ppermute | solution.py:556
  53.0 2.2 %collective-permute-done.14.refs_4_ = bf16[2,4,1664]{2,1,0:T(4,128)(2,1)S(1)} collective-permute-done((bf16[2,4,1664]{2,1,0:T(4,128)(2,1)S(1)}, bf16[2,4,1664]{2,1,0:T(4,128)(2,1)S(1)}, u32[]{:S(2)}, u32[]{:S(2)}) %collective-permute-start.14) | collective-permute-done | bytes 26656 | tf_op jit(solution)/shard_map/ppermute | solution.py:556
  55.2 3.5 %attend.1 = (bf16[4,6144]{1,0:T(4,128)(2,1)S(1)}, bf16[4,6144]{1,0:T(4,128)(2,1)S(1)}) custom-call(s32[4]{0:T(128)S(1)} %copy-done.1, bf16[2,4,1664]{2,1,0:T(4,128)(2,1)S(1)} %get-tuple-element.74.refs_1_, bf16[2,4,1664]{2,1,0:T(4,128)(2,1)S(1)} %collective-permute-done.12.refs_2_, bf16[2,4,1664]{2,1,0:T(4,128)(2,1)S(1)} %collective-permute-done.13.refs_3_, ...), custom_call_target="tpu_custom_call" | custom-call | tf_op jit(solution)/shard_map/attend/pallas_call | solution.py:346
  58.7 1.2 %collective-permute-done.15 = bf16[4,6144]{1,0:T(4,128)(2,1)S(1)} collective-permute-done((bf16[4,6144]{1,0:T(4,128)(2,1)S(1)}, bf16[4,6144]{1,0:T(4,128)(2,1)S(1)}, u32[]{:S(2)}, u32[]{:S(2)}) %collective-permute-start.15) | collective-permute-done | bytes 49184 | tf_op jit(solution)/shard_map/ppermute | solution.py:44
  60.1 2.0 %collective-permute-start.17 = (bf16[8,6144]{1,0:T(8,128)(2,1)S(1)}, bf16[8,6144]{1,0:T(8,128)(2,1)S(1)}, u32[]{:S(2)}, u32[]{:S(2)}) collective-permute-start(bf16[8,6144]{1,0:T(8,128)(2,1)S(1)} %pad_maximum_fusion.refs_1_.refs_0_), channel_id=1, source_target_pairs={{0,2},{4,0},{8,4},{12,8},{14,12},{10,14},{6,10},{2,6},{1,3},{5,1},... | collective-permute-start | bytes 294920 | tf_op jit(solution)/shard_map/ppermute | solution.py:55
  62.1 3.1 %load.10.refs_10_ = bf16[1536,2304]{1,0:T(8,128)(2,1)S(1)} custom-call(bf16[6144,2304]{1,0:T(8,128)(2,1)} %refs_0_.16, bf16[8,6144]{1,0:T(8,128)(2,1)S(1)} %pad_maximum_fusion.refs_1_.refs_0_), custom_call_target="tpu_custom_call" | custom-call | tf_op jit(solution)/shard_map/load/pallas_call | solution.py:103
  65.2 1.2 %collective-permute-start.18 = (bf16[8,6144]{1,0:T(8,128)(2,1)S(1)}, bf16[8,6144]{1,0:T(8,128)(2,1)S(1)}, u32[]{:S(2)}, u32[]{:S(2)}) collective-permute-start(bf16[8,6144]{1,0:T(8,128)(2,1)S(1)} %collective-permute-done.16.refs_1_), channel_id=1, source_target_pairs={{0,4},{4,8},{8,12},{12,14},{14,10},{10,6},{6,2},{2,0},{1,5},{5,9},... | collective-permute-start | bytes 294920 | tf_op jit(solution)/shard_map/ppermute | solution.py:55
  66.4 0.9 collective-permute-start.19
  67.3 3.1 %load.11.refs_11_ = bf16[1536,2304]{1,0:T(8,128)(2,1)S(1)} custom-call(bf16[6144,2304]{1,0:T(8,128)(2,1)} %refs_0_.16, bf16[8,6144]{1,0:T(8,128)(2,1)S(1)} %collective-permute-done.16.refs_1_, bf16[8,6144]{1,0:T(8,128)(2,1)S(1)} %collective-permute-done.17.refs_2_), custom_call_target="tpu_custom_call" | custom-call | tf_op jit(solution)/shard_map/load/pallas_call | solution.py:103
  70.4 0.6 collective-permute-done.19.refs_4_
  71.0 1.8 %collective-permute-start.20 = (bf16[8,6144]{1,0:T(8,128)(2,1)S(1)}, bf16[8,6144]{1,0:T(8,128)(2,1)S(1)}, u32[]{:S(2)}, u32[]{:S(2)}) collective-permute-start(bf16[8,6144]{1,0:T(8,128)(2,1)S(1)} %collective-permute-done.18.refs_3_), channel_id=1, source_target_pairs={{0,4},{4,8},{8,12},{12,14},{14,10},{10,6},{6,2},{2,0},{1,5},{5,9},... | collective-permute-start | bytes 294920 | tf_op jit(solution)/shard_map/ppermute | solution.py:55
  72.8 0.2 collective-permute-start.21
  73.1 2.7 %collective-permute-done.20.refs_5_ = bf16[8,6144]{1,0:T(8,128)(2,1)S(1)} collective-permute-done((bf16[8,6144]{1,0:T(8,128)(2,1)S(1)}, bf16[8,6144]{1,0:T(8,128)(2,1)S(1)}, u32[]{:S(2)}, u32[]{:S(2)}) %collective-permute-start.20) | collective-permute-done | bytes 98336 | tf_op jit(solution)/shard_map/ppermute | solution.py:55
  75.8 2.2 %collective-permute-start.22 = (bf16[8,3072]{1,0:T(8,128)(2,1)S(1)}, bf16[8,3072]{1,0:T(8,128)(2,1)S(1)}, u32[]{:S(2)}, u32[]{:S(2)}) collective-permute-start(bf16[8,3072]{1,0:T(8,128)(2,1)S(1)} %slice.16), channel_id=1, source_target_pairs={{0,4},{4,8},{8,12},{12,14},{14,10},{10,6},{6,2},{2,0},{1,5},{5,9},... | collective-permute-start | bytes 147464 | tf_op jit(solution)/shard_map/ppermute | solution.py:55
  78.0 0.2 collective-permute-start.23
  78.2 1.6 %collective-permute-done.22.refs_7_ = bf16[8,3072]{1,0:T(8,128)(2,1)S(1)} collective-permute-done((bf16[8,3072]{1,0:T(8,128)(2,1)S(1)}, bf16[8,3072]{1,0:T(8,128)(2,1)S(1)}, u32[]{:S(2)}, u32[]{:S(2)}) %collective-permute-start.22) | collective-permute-done | bytes 49184 | tf_op jit(solution)/shard_map/ppermute | solution.py:55
  79.8 2.5 %collective-permute-done.23.refs_8_ = bf16[8,3072]{1,0:T(8,128)(2,1)S(1)} collective-permute-done((bf16[8,3072]{1,0:T(8,128)(2,1)S(1)}, bf16[8,3072]{1,0:T(8,128)(2,1)S(1)}, u32[]{:S(2)}, u32[]{:S(2)}) %collective-permute-start.23) | collective-permute-done | bytes 49184 | tf_op jit(solution)/shard_map/ppermute | solution.py:55
  82.3 5.1 %output_project.1 = (f32[4,8,2304]{2,1,0:T(8,128)S(1)}, f32[4,8,2304]{2,1,0:T(8,128)S(1)}) custom-call(bf16[8,6144]{1,0:T(8,128)(2,1)S(1)} %pad_maximum_fusion.refs_1_.refs_0_, bf16[8,6144]{1,0:T(8,128)(2,1)S(1)} %collective-permute-done.16.refs_1_, bf16[8,6144]{1,0:T(8,128)(2,1)S(1)} %collective-permute-done.17.refs_2_, ...), custom_call_target="tpu_custom_call" | custom-call | tf_op jit(solution)/shard_map/output_project/pallas_call | solution.py:400
  87.4 1.6 %collective-permute-done.24 = f32[4,8,2304]{2,1,0:T(8,128)S(1)} collective-permute-done((f32[4,8,2304]{2,1,0:T(8,128)S(1)}, f32[4,8,2304]{2,1,0:T(8,128)S(1)}, u32[]{:S(2)}, u32[]{:S(2)}) %collective-permute-start.24) | collective-permute-done | bytes 294944 | tf_op jit(solution)/shard_map/ppermute | solution.py:44
  89.0 0.7 fusion
  (35 shorter events, 0.5 us)
Async XLA Ops:
  0.0 6.1 %copy-start = (bf16[8,9216]{1,0:T(8,128)(2,1)S(1)}, bf16[8,9216]{1,0:T(8,128)(2,1)}, u32[]{:S(2)}) copy-start(bf16[8,9216]{1,0:T(8,128)(2,1)} %refs_3_.1) | copy-start | bytes 442372
  0.0 7.1 %collective-permute-start = (bf16[8,9216]{1,0:T(8,128)(2,1)}, bf16[8,9216]{1,0:T(8,128)(2,1)S(1)}, u32[]{:S(2)}, u32[]{:S(2)}) collective-permute-start(bf16[8,9216]{1,0:T(8,128)(2,1)} %refs_3_.1), channel_id=1, source_target_pairs={{0,4},{4,8},{8,12},{12,14},{14,10},{10,6},{6,2},{2,0},{1,5},{5,9},... | collective-permute-start | bytes 442376 | tf_op jit(solution)/shard_map/ppermute | solution.py:55
  3.0 5.5 %collective-permute-start.1 = (bf16[8,9216]{1,0:T(8,128)(2,1)}, bf16[8,9216]{1,0:T(8,128)(2,1)S(1)}, u32[]{:S(2)}, u32[]{:S(2)}) collective-permute-start(bf16[8,9216]{1,0:T(8,128)(2,1)} %refs_3_.1), channel_id=1, source_target_pairs={{0,2},{4,0},{8,4},{12,8},{14,12},{10,14},{6,10},{2,6},{1,3},{5,1},... | collective-permute-start | bytes 442376 | tf_op jit(solution)/shard_map/ppermute | solution.py:55
  8.5 5.1 %collective-permute-start.2 = (bf16[8,9216]{1,0:T(8,128)(2,1)S(1)}, bf16[8,9216]{1,0:T(8,128)(2,1)S(1)}, u32[]{:S(2)}, u32[]{:S(2)}) collective-permute-start(bf16[8,9216]{1,0:T(8,128)(2,1)S(1)} %collective-permute-done.refs_1_.refs_4_), channel_id=1, source_target_pairs={{0,4},{4,8},{8,12},{12,14},{14,10},{10,6},{6,2},{2,0},{1,5},{5,9},... | collective-permute-start | bytes 442376 | tf_op jit(solution)/shard_map/ppermute | solution.py:55
  10.1 5.1 %collective-permute-start.3 = (bf16[8,9216]{1,0:T(8,128)(2,1)S(1)}, bf16[8,9216]{1,0:T(8,128)(2,1)S(1)}, u32[]{:S(2)}, u32[]{:S(2)}) collective-permute-start(bf16[8,9216]{1,0:T(8,128)(2,1)S(1)} %collective-permute-done.1.refs_2_.refs_5_), channel_id=1, source_target_pairs={{0,2},{4,0},{8,4},{12,8},{14,12},{10,14},{6,10},{2,6},{1,3},{5,1},... | collective-permute-start | bytes 442376 | tf_op jit(solution)/shard_map/ppermute | solution.py:55
  15.3 7.8 %collective-permute-start.4 = (bf16[8,9216]{1,0:T(8,128)(2,1)S(1)}, bf16[8,9216]{1,0:T(8,128)(2,1)S(1)}, u32[]{:S(2)}, u32[]{:S(2)}) collective-permute-start(bf16[8,9216]{1,0:T(8,128)(2,1)S(1)} %collective-permute-done.2.refs_1_.refs_6_), channel_id=1, source_target_pairs={{0,4},{4,8},{8,12},{12,14},{14,10},{10,6},{6,2},{2,0},{1,5},{5,9},... | collective-permute-start | bytes 442376 | tf_op jit(solution)/shard_map/ppermute | solution.py:55
  16.8 6.2 %collective-permute-start.5 = (bf16[8,9216]{1,0:T(8,128)(2,1)S(1)}, bf16[8,9216]{1,0:T(8,128)(2,1)S(1)}, u32[]{:S(2)}, u32[]{:S(2)}) collective-permute-start(bf16[8,9216]{1,0:T(8,128)(2,1)S(1)} %collective-permute-done.3.refs_2_.refs_7_), channel_id=1, source_target_pairs={{0,2},{4,0},{8,4},{12,8},{14,12},{10,14},{6,10},{2,6},{1,3},{5,1},... | collective-permute-start | bytes 442376 | tf_op jit(solution)/shard_map/ppermute | solution.py:55
  17.3 8.1 %collective-permute-start.6 = (f32[8,128]{1,0:T(8,128)S(1)}, f32[8,128]{1,0:T(8,128)S(1)}, u32[]{:S(2)}, u32[]{:S(2)}) collective-permute-start(f32[8,128]{1,0:T(8,128)S(1)} %row_sums.4.refs_0_), channel_id=1, source_target_pairs={{0,14},{4,10},{8,6},{12,2},{14,0},{10,4},{6,8},{2,12},{1,15},{5,11... | collective-permute-start | bytes 12296 | tf_op jit(solution)/shard_map/ppermute | solution.py:525
  19.8 5.7 %copy-start.2 = (bf16[9216]{0:T(1024)(128)(2,1)S(1)}, bf16[9216]{0:T(1024)(128)(2,1)}, u32[]{:S(2)}) copy-start(bf16[9216]{0:T(1024)(128)(2,1)} %param.9) | copy-start | bytes 55300
  23.1 5.8 %collective-permute-start.8 = (bf16[8,4608]{1,0:T(8,128)(2,1)S(1)}, bf16[8,4608]{1,0:T(8,128)(2,1)S(1)}, u32[]{:S(2)}, u32[]{:S(2)}) collective-permute-start(bf16[8,4608]{1,0:T(8,128)(2,1)S(1)} %slice.12), channel_id=1, source_target_pairs={{0,4},{4,8},{8,12},{12,14},{14,10},{10,6},{6,2},{2,0},{1,5},{5,9},... | collective-permute-start | bytes 221192 | tf_op jit(solution)/shard_map/ppermute | solution.py:55
  23.9 5.0 %collective-permute-start.9 = (bf16[8,4608]{1,0:T(8,128)(2,1)S(1)}, bf16[8,4608]{1,0:T(8,128)(2,1)S(1)}, u32[]{:S(2)}, u32[]{:S(2)}) collective-permute-start(bf16[8,4608]{1,0:T(8,128)(2,1)S(1)} %slice.13), channel_id=1, source_target_pairs={{0,2},{4,0},{8,4},{12,8},{14,12},{10,14},{6,10},{2,6},{1,3},{5,1},... | collective-permute-start | bytes 221192 | tf_op jit(solution)/shard_map/ppermute | solution.py:55
  25.4 3.5 %collective-permute-start.7 = (f32[64,128]{1,0:T(8,128)S(1)}, f32[64,128]{1,0:T(8,128)S(1)}, u32[]{:S(2)}, u32[]{:S(2)}) collective-permute-start(f32[64,128]{1,0:T(8,128)S(1)} %pad_maximum_fusion.1.refs_0_), channel_id=1, source_target_pairs={{0,1},{1,0},{2,3},{3,2},{4,5},{5,4},{6,7},{7,6},{8,9},{9,8},{10,11... | collective-permute-start | bytes 98312 | tf_op jit(solution)/shard_map/ppermute | solution.py:44
  28.9 15.1 %copy-start.1 = (s32[4]{0:T(128)S(1)}, s32[4]{0:T(128)}, u32[]{:S(2)}) copy-start(s32[4]{0:T(128)} %refs_0_.14) | copy-start | bytes 52
  40.6 1.6 %collective-permute-start.10 = (f32[8,4,1664]{2,1,0:T(4,128)S(1)}, f32[8,4,1664]{2,1,0:T(4,128)S(1)}, u32[]{:S(2)}, u32[]{:S(2)}) collective-permute-start(f32[8,4,1664]{2,1,0:T(4,128)S(1)} %get-tuple-element.69), channel_id=1, source_target_pairs={{0,1},{1,0},{2,3},{3,2},{4,5},{5,4},{6,7},{7,6},{8,9},{9,8},{10,11... | collective-permute-start | bytes 638984 | tf_op jit(solution)/shard_map/ppermute | solution.py:44
  42.3 5.2 %collective-permute-start.11 = (bf16[4,4,1664]{2,1,0:T(4,128)(2,1)S(1)}, bf16[4,4,1664]{2,1,0:T(4,128)(2,1)S(1)}, u32[]{:S(2)}, u32[]{:S(2)}) collective-permute-start(bf16[4,4,1664]{2,1,0:T(4,128)(2,1)S(1)} %get-tuple-element.71.refs_2_), channel_id=1, source_target_pairs={{0,2},{2,0},{4,6},{6,4},{8,10},{10,8},{12,14},{14,12},{1,3},{3,1},... | collective-permute-start | bytes 159752 | tf_op jit(solution)/shard_map/ppermute | solution.py:550
  47.5 4.6 %collective-permute-start.12 = (bf16[2,4,1664]{2,1,0:T(4,128)(2,1)S(1)}, bf16[2,4,1664]{2,1,0:T(4,128)(2,1)S(1)}, u32[]{:S(2)}, u32[]{:S(2)}) collective-permute-start(bf16[2,4,1664]{2,1,0:T(4,128)(2,1)S(1)} %get-tuple-element.75), channel_id=1, source_target_pairs={{0,4},{2,6},{4,0},{6,2},{8,12},{10,14},{12,8},{14,10},{1,5},{3,7},... | collective-permute-start | bytes 79880 | tf_op jit(solution)/shard_map/ppermute | solution.py:556
  48.2 4.7 %collective-permute-start.13 = (bf16[2,4,1664]{2,1,0:T(4,128)(2,1)S(1)}, bf16[2,4,1664]{2,1,0:T(4,128)(2,1)S(1)}, u32[]{:S(2)}, u32[]{:S(2)}) collective-permute-start(bf16[2,4,1664]{2,1,0:T(4,128)(2,1)S(1)} %get-tuple-element.76), channel_id=1, source_target_pairs={{0,8},{2,10},{4,12},{6,14},{8,0},{10,2},{12,4},{14,6},{1,9},{3,11}... | collective-permute-start | bytes 79880 | tf_op jit(solution)/shard_map/ppermute | solution.py:556
  49.5 5.6 %collective-permute-start.14 = (bf16[2,4,1664]{2,1,0:T(4,128)(2,1)S(1)}, bf16[2,4,1664]{2,1,0:T(4,128)(2,1)S(1)}, u32[]{:S(2)}, u32[]{:S(2)}) collective-permute-start(bf16[2,4,1664]{2,1,0:T(4,128)(2,1)S(1)} %get-tuple-element.77), channel_id=1, source_target_pairs={{0,12},{2,14},{4,8},{6,10},{8,4},{10,6},{12,0},{14,2},{1,13},{3,15... | collective-permute-start | bytes 79880 | tf_op jit(solution)/shard_map/ppermute | solution.py:556
  58.6 1.3 %collective-permute-start.15 = (bf16[4,6144]{1,0:T(4,128)(2,1)S(1)}, bf16[4,6144]{1,0:T(4,128)(2,1)S(1)}, u32[]{:S(2)}, u32[]{:S(2)}) collective-permute-start(bf16[4,6144]{1,0:T(4,128)(2,1)S(1)} %get-tuple-element.81), channel_id=1, source_target_pairs={{0,1},{1,0},{2,3},{3,2},{4,5},{5,4},{6,7},{7,6},{8,9},{9,8},{10,11... | collective-permute-start | bytes 147464 | tf_op jit(solution)/shard_map/ppermute | solution.py:44
  60.0 5.2 %collective-permute-start.16 = (bf16[8,6144]{1,0:T(8,128)(2,1)S(1)}, bf16[8,6144]{1,0:T(8,128)(2,1)S(1)}, u32[]{:S(2)}, u32[]{:S(2)}) collective-permute-start(bf16[8,6144]{1,0:T(8,128)(2,1)S(1)} %pad_maximum_fusion.refs_1_.refs_0_), channel_id=1, source_target_pairs={{0,4},{4,8},{8,12},{12,14},{14,10},{10,6},{6,2},{2,0},{1,5},{5,9},... | collective-permute-start | bytes 294920 | tf_op jit(solution)/shard_map/ppermute | solution.py:55
  60.1 5.1 %collective-permute-start.17 = (bf16[8,6144]{1,0:T(8,128)(2,1)S(1)}, bf16[8,6144]{1,0:T(8,128)(2,1)S(1)}, u32[]{:S(2)}, u32[]{:S(2)}) collective-permute-start(bf16[8,6144]{1,0:T(8,128)(2,1)S(1)} %pad_maximum_fusion.refs_1_.refs_0_), channel_id=1, source_target_pairs={{0,2},{4,0},{8,4},{12,8},{14,12},{10,14},{6,10},{2,6},{1,3},{5,1},... | collective-permute-start | bytes 294920 | tf_op jit(solution)/shard_map/ppermute | solution.py:55
  65.2 5.2 %collective-permute-start.18 = (bf16[8,6144]{1,0:T(8,128)(2,1)S(1)}, bf16[8,6144]{1,0:T(8,128)(2,1)S(1)}, u32[]{:S(2)}, u32[]{:S(2)}) collective-permute-start(bf16[8,6144]{1,0:T(8,128)(2,1)S(1)} %collective-permute-done.16.refs_1_), channel_id=1, source_target_pairs={{0,4},{4,8},{8,12},{12,14},{14,10},{10,6},{6,2},{2,0},{1,5},{5,9},... | collective-permute-start | bytes 294920 | tf_op jit(solution)/shard_map/ppermute | solution.py:55
  66.4 4.6 %collective-permute-start.19 = (bf16[8,6144]{1,0:T(8,128)(2,1)S(1)}, bf16[8,6144]{1,0:T(8,128)(2,1)S(1)}, u32[]{:S(2)}, u32[]{:S(2)}) collective-permute-start(bf16[8,6144]{1,0:T(8,128)(2,1)S(1)} %collective-permute-done.17.refs_2_), channel_id=1, source_target_pairs={{0,2},{4,0},{8,4},{12,8},{14,12},{10,14},{6,10},{2,6},{1,3},{5,1},... | collective-permute-start | bytes 294920 | tf_op jit(solution)/shard_map/ppermute | solution.py:55
  71.0 4.7 %collective-permute-start.20 = (bf16[8,6144]{1,0:T(8,128)(2,1)S(1)}, bf16[8,6144]{1,0:T(8,128)(2,1)S(1)}, u32[]{:S(2)}, u32[]{:S(2)}) collective-permute-start(bf16[8,6144]{1,0:T(8,128)(2,1)S(1)} %collective-permute-done.18.refs_3_), channel_id=1, source_target_pairs={{0,4},{4,8},{8,12},{12,14},{14,10},{10,6},{6,2},{2,0},{1,5},{5,9},... | collective-permute-start | bytes 294920 | tf_op jit(solution)/shard_map/ppermute | solution.py:55
  72.8 5.2 %collective-permute-start.21 = (bf16[8,6144]{1,0:T(8,128)(2,1)S(1)}, bf16[8,6144]{1,0:T(8,128)(2,1)S(1)}, u32[]{:S(2)}, u32[]{:S(2)}) collective-permute-start(bf16[8,6144]{1,0:T(8,128)(2,1)S(1)} %collective-permute-done.19.refs_4_), channel_id=1, source_target_pairs={{0,2},{4,0},{8,4},{12,8},{14,12},{10,14},{6,10},{2,6},{1,3},{5,1},... | collective-permute-start | bytes 294920 | tf_op jit(solution)/shard_map/ppermute | solution.py:55
  75.8 4.1 %collective-permute-start.22 = (bf16[8,3072]{1,0:T(8,128)(2,1)S(1)}, bf16[8,3072]{1,0:T(8,128)(2,1)S(1)}, u32[]{:S(2)}, u32[]{:S(2)}) collective-permute-start(bf16[8,3072]{1,0:T(8,128)(2,1)S(1)} %slice.16), channel_id=1, source_target_pairs={{0,4},{4,8},{8,12},{12,14},{14,10},{10,6},{6,2},{2,0},{1,5},{5,9},... | collective-permute-start | bytes 147464 | tf_op jit(solution)/shard_map/ppermute | solution.py:55
  78.0 4.3 %collective-permute-start.23 = (bf16[8,3072]{1,0:T(8,128)(2,1)S(1)}, bf16[8,3072]{1,0:T(8,128)(2,1)S(1)}, u32[]{:S(2)}, u32[]{:S(2)}) collective-permute-start(bf16[8,3072]{1,0:T(8,128)(2,1)S(1)} %slice.17), channel_id=1, source_target_pairs={{0,2},{4,0},{8,4},{12,8},{14,12},{10,14},{6,10},{2,6},{1,3},{5,1},... | collective-permute-start | bytes 147464 | tf_op jit(solution)/shard_map/ppermute | solution.py:55
  87.4 1.6 %collective-permute-start.24 = (f32[4,8,2304]{2,1,0:T(8,128)S(1)}, f32[4,8,2304]{2,1,0:T(8,128)S(1)}, u32[]{:S(2)}, u32[]{:S(2)}) collective-permute-start(f32[4,8,2304]{2,1,0:T(8,128)S(1)} %get-tuple-element.90), channel_id=1, source_target_pairs={{0,1},{1,0},{2,3},{3,2},{4,5},{5,4},{6,7},{7,6},{8,9},{9,8},{10,11... | collective-permute-start | bytes 884744 | tf_op jit(solution)/shard_map/ppermute | solution.py:44

commit v10 on v9

--- a/solution.py
+++ b/solution.py
@@ -111,27 +111,26 @@
     )(*[in_hbm(job[0]) for job in jobs], *after)
 
 
-def load_caches_kernel(*refs):
-    sources, targets, sems = refs[:2], refs[-3:-1], refs[-1]
+def load_cache_kernel(source, *refs):
+    target, sems = refs[-2:]
     copies = []
-    for i, (source, target) in enumerate(zip(sources, targets)):
-        for row in range(source.shape[0]):
-            copies.append(pltpu.make_async_copy(source.at[row], target.at[row], sems.at[i, row]))
-            copies[-1].start()
+    for row in range(source.shape[0]):
+        copies.append(pltpu.make_async_copy(source.at[row], target.at[row], sems.at[row]))
+        copies[-1].start()
     for copy in copies:
         copy.wait()
 
 
-def load_caches(keys, values, after):
-    return pl.pallas_call(
-        load_caches_kernel,
-        out_shape=[pltpu.VMEM(a.shape, a.dtype) for a in (keys, values)],
-        in_specs=[IN_HBM] * 2 + [ANY] * len(after),
-        out_specs=[IN_VMEM] * 2,
-        scratch_shapes=[pltpu.SemaphoreType.DMA((2, keys.shape[0]))],
+def load_cache(cache, after):
+    return pl.pallas_call(
+        load_cache_kernel,
+        out_shape=pltpu.VMEM(cache.shape, cache.dtype),
+        in_specs=[IN_HBM] + [ANY] * len(after),
+        out_specs=IN_VMEM,
+        scratch_shapes=[pltpu.SemaphoreType.DMA((cache.shape[0],))],
         compiler_params=pltpu.CompilerParams(vmem_limit_bytes=MIB),
-        name="load_caches",
-    )(in_hbm(keys), in_hbm(values), *after)
+        name="load_cache",
+    )(in_hbm(cache), *after)
 
 
 def in_hbm(array):
@@ -153,27 +152,32 @@
     for ref in refs[:ready]:
         out[start : start + ref.shape[0], :] = ref[...]
         start += ref.shape[0]
-    rows = refs[ready].shape[0]
-    lane = lax.broadcasted_iota(jnp.int32, (rows, 128), 1)
-    for ref in refs[ready : ready + count]:
+
+    def both_sums(ref):
         x = ref[...].astype(jnp.float32)
         total = jnp.sum(x, axis=1, keepdims=True)
         square = jnp.sum(x * x, axis=1, keepdims=True)
-        both = jnp.where(lane == 0, total, jnp.where(lane == 1, square, 0.0))
-        out[start : start + rows, :] = both
-        start += rows
-
-
-def row_sums(shards, ready=(), after=()):
-    rows = shards[0].shape[0] * len(shards) + sum(r.shape[0] for r in ready)
+        lane = lax.broadcasted_iota(jnp.int32, (x.shape[0], 128), 1)
+        return jnp.where(lane == 0, total, jnp.where(lane == 1, square, 0.0))
+
+    for ref in refs[ready : ready + count]:
+        out[start : start + ref.shape[0], :] = both_sums(ref)
+        start += ref.shape[0]
+    halves = refs[ready + count : -1]
+    if halves:
+        out[start:, :] = both_sums(halves[0]) + both_sums(halves[1])
+
+
+def row_sums(shards, ready=(), halves=()):
+    rows = sum(a.shape[0] for a in (*ready, *shards, *halves[:1]))
     return pl.pallas_call(
         lambda *refs: sums_kernel(len(ready), len(shards), *refs),
         out_shape=jax.ShapeDtypeStruct((rows, 128), jnp.float32),
-        in_specs=[IN_VMEM] * (len(ready) + len(shards)) + [ANY] * len(after),
+        in_specs=[IN_VMEM] * (len(ready) + len(shards) + len(halves)),
         out_specs=IN_VMEM,
         compiler_params=pltpu.CompilerParams(vmem_limit_bytes=8 * MIB),
         name="row_sums",
-    )(*ready, *shards, *after)
+    )(*ready, *shards, *halves)
 
 
 def project_kernel(n, parts, *refs):
@@ -190,12 +194,13 @@
     scale = lax.rsqrt(row_square - row_mean * row_mean + epsilon)
     for part in range(2):
         cols = slice(part * width // 2, (part + 1) * width // 2)
-        for i in range(n):
-            at = slice(i * rows, (i + 1) * rows)
-            x = shards[i][:, cols] if i < n - 1 else far[part][...]
-            x = x.astype(jnp.float32)
-            normed[at, cols] = (x - row_mean[at]) * scale[at] * gain[:, cols]
-        x = normed[:, cols].astype(jnp.bfloat16)
+        for i in range(0, n, 2):
+            x = [ref[:, cols] if ref is not far[part] else ref[...] for ref in (*shards, far[part])]
+            x = jnp.concatenate([piece.astype(jnp.float32) for piece in x[i : i + 2]], axis=0)
+            at = slice(i * rows, (i + 2) * rows)
+            x = (x - row_mean[at]) * scale[at] * gain[:, cols]
+            normed[at, cols] = x.astype(jnp.bfloat16)
+        x = normed[:, cols]
         start = 0
         for weight in weights:
             term = lax.dot_general(
@@ -229,7 +234,7 @@
         in_specs=[IN_VMEM] * (4 + n + len(weights)) + [IN_HBM],
         out_specs=[IN_VMEM] * 3,
         scratch_shapes=[
-            pltpu.VMEM((n * rows, width), jnp.float32),
+            pltpu.VMEM((n * rows, width), jnp.bfloat16),
             pltpu.VMEM((n * rows, stripe), jnp.float32),
             pltpu.SemaphoreType.DMA((4,)),
         ],
@@ -265,34 +270,34 @@
     )(keep, got)
 
 
-def pair_kernel(here, came, *outs):
-    for d, out in enumerate(outs):
-        out[0] = here[d]
-        out[1] = came[d]
-
-
-def pair(here, came):
-    shape = jax.ShapeDtypeStruct((2,) + here.shape[1:], here.dtype)
-    return pl.pallas_call(
-        pair_kernel,
-        out_shape=[shape] * here.shape[0],
-        in_specs=[IN_VMEM] * 2,
-        out_specs=[IN_VMEM] * here.shape[0],
+def pack(picks, *sources):
+    def pack_kernel(*refs):
+        for k, (i, j) in enumerate(picks):
+            refs[-1][k] = refs[i][j]
+
+    return pl.pallas_call(
+        pack_kernel,
+        out_shape=jax.ShapeDtypeStruct((len(picks),) + sources[0].shape[1:], sources[0].dtype),
+        in_specs=[IN_VMEM] * len(sources),
+        out_specs=IN_VMEM,
         compiler_params=pltpu.CompilerParams(vmem_limit_bytes=8 * MIB),
-        name="pair",
-    )(here, came)
-
-
-def attend_kernel(n, lengths, *refs):
-    arrived = refs[: n // 2]
-    cosine, sine, keys, values, mine, other, spread, held = refs[n // 2 :]
-    _, rows, stripe = arrived[0].shape
+        name="pack",
+    )(*sources)
+
+
+ARRIVED = [(0, 0), (1, 0), (2, 0), (2, 1), (3, 0), (3, 1), (3, 2), (3, 3)]
+
+
+def attend_kernel(lengths, *refs):
+    arrived = refs[:4]
+    cosine, sine, keys, values, mine, other, spread, held = refs[4:]
+    n, rows, stripe = spread.shape[1], spread.shape[0], spread.shape[2]
     me = lax.axis_index("gx")
     query_cols = stripe - 128
     side = lax.axis_index("gy")
     score_scale = 1.0 / math.sqrt(DH)
-    for d in range(n):
-        block = arrived[d // 2][d % 2].astype(jnp.float32)
+    for d, (i, j) in enumerate(ARRIVED):
+        block = arrived[i][j].astype(jnp.float32)
         for r in range(rows):
             spread[r, pl.ds(jnp.bitwise_xor(me, d), 1), :] = block[r : r + 1, :]
     for r in range(rows):
@@ -340,13 +345,13 @@
 
 
 def attend(lengths, arrived, cosine, sine, keys, values):
-    n = 2 * len(arrived)
+    n = len(ARRIVED)
     _, rows, stripe = arrived[0].shape
     shape = jax.ShapeDtypeStruct((rows, HEADS * DH // 2), jnp.bfloat16)
     return pl.pallas_call(
-        lambda *refs: attend_kernel(n, *refs),
+        attend_kernel,
         out_shape=[shape, shape],
-        in_specs=[IN_SMEM] + [IN_VMEM] * (n // 2 + 4),
+        in_specs=[IN_SMEM] + [IN_VMEM] * 8,
         out_specs=[IN_VMEM] * 2,
         scratch_shapes=[
             pltpu.VMEM((rows, n, stripe), jnp.float32),
@@ -513,31 +518,23 @@
 
     left = right = activations
     shards = [activations]
+    sums = []
     for step in range(1, n // 2):
         arrived = shards[-2:] if step > 1 else []
         left, right = ring.step(left, right)
         if step > 1:
-            sums = row_sums(arrived, [sums])
+            sums = [row_sums([activations, *arrived] if step == 2 else arrived, sums)]
         weight = piece_of(query_weight, (step - 1) * piece, piece, arrived)
-        if step == 1:
-            weight, (own,) = before(weight, activations)
-            sums = row_sums([own])
-            far_sums = lax.ppermute(sums, "gx", ring.across)
-            weight, (left, right, sums) = before(weight, left, right, sums)
-        else:
-            weight, (left, right) = before(weight, left, right)
+        weight, (left, right, *sums) = before(weight, left, right, *sums)
         weights.append(weight)
         shards += [left, right]
-    cut, (cut_right, left, right) = before(
-        left[:, : width // 2], right[:, width // 2 :], left, right
-    )
-    far = ring.step(cut, cut_right)
-    sums = row_sums([left, right], [sums])
+    far = ring.step(left[:, : width // 2], right[:, width // 2 :])
+    sums = row_sums([left, right], sums)
     jobs = [(query_weight, 3 * piece, piece, 0), (keyval_weight, 0, new_cols, None)]
-    weight = load(piece + 2 * new_cols, jobs, [sums])
-    sums = jnp.concatenate([sums, far_sums], axis=0)
+    weight = load(piece + 2 * new_cols, jobs, [left, right])
+    weight, far = before(weight, *far)
+    sums = row_sums([], [sums], far)
     other_sums = swap_pair(sums)
-    weight, (other_sums, *far) = before(weight, other_sums, *far)
     weights.append(weight)
     gain = norm_gain.astype(jnp.float32)[None, :]
     piece = output_weight.shape[0] // 4
@@ -547,28 +544,39 @@
     weights = [weight]
 
     here, there = split(keep, swap_pair(give))
-    came = lax.ppermute(there, "gx", [(i, i ^ 1) for i in range(n)])
-    keys, values = load_caches(cache_keys, cache_values, [there])
-    keys, (came,) = before(keys, came)
-    blocks = pair(here, came)
-    arrived = [blocks[0]]
-    for d in range(1, n // 2):
-        arrived.append(lax.ppermute(blocks[d], "gx", [(i, i ^ (2 * d)) for i in range(n)]))
+    def exchange(blocks, bit):
+        return lax.ppermute(blocks, "gx", [(i, i ^ bit) for i in range(n)])
+
+    second = exchange(there, 1)
+    keys = load_cache(cache_keys, [there])
+    keys, (second,) = before(keys, second)
+    across = pack([(0, 1), (1, 1), (0, 3), (1, 3)], here, second)
+    third = exchange(across, 2)
+    values = load_cache(cache_values, [across])
+    values, (third,) = before(values, third)
+    across = pack([(0, 2), (1, 2), (2, 2), (2, 3)], here, second, third)
+    fourth = exchange(across, 4)
+    arrived = [here, second, third, fourth]
     mine, other = attend(cache_lengths, arrived, cosine, sine, keys, values)
     shard = jnp.concatenate([mine, swap_pair(other)], axis=0)
 
     left = right = shard
     shards = [shard]
+    done = 2 * piece
+    piece = piece // 2
+
     for step in range(1, n // 2):
         arrived = shards[-2:]
         left, right = ring.step(left, right)
-        if step <= 2:
-            weight = piece_of(output_weight, (1 + step) * piece, piece, arrived)
-            weight, (left, right) = before(weight, left, right)
-            weights.append(weight)
+        weight = piece_of(output_weight, done + (step - 1) * piece, piece, arrived)
+        weight, (left, right) = before(weight, left, right)
+        weights.append(weight)
         shards += [left, right]
     half = shard.shape[1] // 2
     far = ring.step(left[:, :half], right[:, half:])
+    weight = piece_of(output_weight, done + 3 * piece, piece, [left, right])
+    weight, far = before(weight, *far)
+    weights.append(weight)
     keep, give = output_project(shards, far, weights)
     out = (keep + swap_pair(give)).astype(jnp.bfloat16)
     return out.reshape(-1, out.shape[-1])

time: 89.9 us -> 89.4 us (level)
  starting transfers between devices: 26.9 us -> 19.9 us
  waiting for transfers between devices: 18.2 us -> 22.2 us
  Pallas kernels: 43.4 us -> 46.1 us
    ppermute x5 -> x3, starting transfers between devices: 8.41 us -> 2.12 us  [exchange(): return lax.ppermute(blocks, 'gx', [(i, i ^ bit) for i in range(n)])]
    ppermute x5 -> x3, waiting for transfers between devices: 3.12 us -> 6.69 us  [exchange(): return lax.ppermute(blocks, 'gx', [(i, i ^ bit) for i in range(n)])]
    ppermute x8, starting transfers between devices: 12.2 us -> 10.1 us  [step(): lax.ppermute(left, 'gx', self.onward)]
    pallas_call x6 -> x8, Pallas kernels: 18.9 us -> 20.7 us  [load(): pl.pallas_call(lambda *refs: load_kernel([job[1:] for job in jobs], *refs...]
    ppermute x8, waiting for transfers between devices: 5.09 us -> 3.39 us  [step(): lax.ppermute(left, 'gx', self.onward)]
    ppermute x8, starting transfers between devices: 5.57 us -> 7.26 us  [step(): lax.ppermute(right, 'gx', self.back)]
    ppermute x4, waiting for transfers between devices: 3.88 us -> 5.27 us  [swap_pair(): return lax.ppermute(x, 'gy', [(0, 1), (1, 0)])]
    pallas_call x3 -> x5, Pallas kernels: 6.97 us -> 7.91 us  [the longest x2 4.41 us: load_cache(): pl.pallas_call(load_cache_kernel, out_shape=pltpu.VMEM(cache.shape, cache...]
  transfers between devices with their start and end apart: 25 -> 23, of which waited for: 12 -> 19; matrix products, arithmetic and copies ran while one was open for 0% -> 0% of each run, Pallas kernels for 26% -> 29%
where the time goes in v10:
time: 89.4 us; the launch traced here: 89.2 us
  Pallas kernels  46.1 us (52%)
  waiting for transfers between devices  22.2 us (25%)
  starting transfers between devices  19.9 us (22%)
    pallas_call x8, Pallas kernels, load(): pl.pallas_call(lambda *refs: load_kernel([job[1:] for job in jobs], *refs...  20.7 us
    pallas_call x1, Pallas kernels, project(): pl.pallas_call(lambda *refs: project_kernel(n, len(weights), *refs), out_...  11.7 us
    ppermute x8, starting transfers between devices, step(): lax.ppermute(left, 'gx', self.onward)  10.1 us
    ppermute x8, starting transfers between devices, step(): lax.ppermute(right, 'gx', self.back)  7.26 us
    ppermute x8, waiting for transfers between devices, step(): lax.ppermute(right, 'gx', self.back)  6.82 us
    ppermute x3, waiting for transfers between devices, exchange(): return lax.ppermute(blocks, 'gx', [(i, i ^ bit) for i in range(n)])  6.69 us
    ppermute x4, waiting for transfers between devices, swap_pair(): return lax.ppermute(x, 'gy', [(0, 1), (1, 0)])  5.27 us
    pallas_call x1, Pallas kernels, output_project(): pl.pallas_call(lambda *refs: output_kernel(n, *refs), out_shape=[shape, s...  5.05 us
  transfers between devices with their start and end apart: 23, of which 19 were waited for; matrix products, arithmetic and copies ran while one was open for 0% of the time, Pallas kernels for 29%

profile of v10, /device:TPU:0, one launch (start us, length us, event | category | flops | bytes accessed | tf_op | source)
XLA Modules:
  0.0 89.2 jit_solution(15488214083894794138)
XLA Ops:
  0.0 3.0 %collective-permute-start = (bf16[8,9216]{1,0:T(8,128)(2,1)}, bf16[8,9216]{1,0:T(8,128)(2,1)S(1)}, u32[]{:S(2)}, u32[]{:S(2)}) collective-permute-start(bf16[8,9216]{1,0:T(8,128)(2,1)} %refs_3_.1), channel_id=1, source_target_pairs={{0,4},{4,8},{8,12},{12,14},{14,10},{10,6},{6,2},{2,0},{1,5},{5,9},... | collective-permute-start | bytes 442376 | tf_op jit(solution)/shard_map/ppermute | solution.py:55
  3.0 3.1 %load.8.refs_12_ = bf16[384,9216]{1,0:T(8,128)(2,1)S(1)} custom-call(bf16[1536,9216]{1,0:T(8,128)(2,1)} %refs_0_.13), custom_call_target="tpu_custom_call" | custom-call | tf_op jit(solution)/shard_map/load/pallas_call | solution.py:103
  6.1 1.0 %collective-permute-done.refs_1_.refs_4_ = bf16[8,9216]{1,0:T(8,128)(2,1)S(1)} collective-permute-done((bf16[8,9216]{1,0:T(8,128)(2,1)}, bf16[8,9216]{1,0:T(8,128)(2,1)S(1)}, u32[]{:S(2)}, u32[]{:S(2)}) %collective-permute-start) | collective-permute-done | bytes 147488 | tf_op jit(solution)/shard_map/ppermute | solution.py:55
  7.1 1.4 %collective-permute-done.1.refs_2_.refs_5_ = bf16[8,9216]{1,0:T(8,128)(2,1)S(1)} collective-permute-done((bf16[8,9216]{1,0:T(8,128)(2,1)}, bf16[8,9216]{1,0:T(8,128)(2,1)S(1)}, u32[]{:S(2)}, u32[]{:S(2)}) %collective-permute-start.1) | collective-permute-done | bytes 147488 | tf_op jit(solution)/shard_map/ppermute | solution.py:55
  8.5 1.6 %collective-permute-start.2 = (bf16[8,9216]{1,0:T(8,128)(2,1)S(1)}, bf16[8,9216]{1,0:T(8,128)(2,1)S(1)}, u32[]{:S(2)}, u32[]{:S(2)}) collective-permute-start(bf16[8,9216]{1,0:T(8,128)(2,1)S(1)} %collective-permute-done.refs_1_.refs_4_), channel_id=1, source_target_pairs={{0,4},{4,8},{8,12},{12,14},{14,10},{10,6},{6,2},{2,0},{1,5},{5,9},... | collective-permute-start | bytes 442376 | tf_op jit(solution)/shard_map/ppermute | solution.py:55
  10.1 0.4 collective-permute-start.3
  10.8 3.1 %load.9.refs_13_ = bf16[384,9216]{1,0:T(8,128)(2,1)S(1)} custom-call(bf16[1536,9216]{1,0:T(8,128)(2,1)} %refs_0_.13, bf16[8,9216]{1,0:T(8,128)(2,1)S(1)} %collective-permute-done.refs_1_.refs_4_, bf16[8,9216]{1,0:T(8,128)(2,1)S(1)} %collective-permute-done.1.refs_2_.refs_5_), custom_call_target="tpu_custom_call" | custom-call | tf_op jit(solution)/shard_map/load/pallas_call | solution.py:103
  13.9 1.3 %collective-permute-done.3.refs_2_.refs_7_ = bf16[8,9216]{1,0:T(8,128)(2,1)S(1)} collective-permute-done((bf16[8,9216]{1,0:T(8,128)(2,1)S(1)}, bf16[8,9216]{1,0:T(8,128)(2,1)S(1)}, u32[]{:S(2)}, u32[]{:S(2)}) %collective-permute-start.3) | collective-permute-done | bytes 147488 | tf_op jit(solution)/shard_map/ppermute | solution.py:55
  15.3 1.6 %collective-permute-start.4 = (bf16[8,9216]{1,0:T(8,128)(2,1)S(1)}, bf16[8,9216]{1,0:T(8,128)(2,1)S(1)}, u32[]{:S(2)}, u32[]{:S(2)}) collective-permute-start(bf16[8,9216]{1,0:T(8,128)(2,1)S(1)} %collective-permute-done.2.refs_1_.refs_6_), channel_id=1, source_target_pairs={{0,4},{4,8},{8,12},{12,14},{14,10},{10,6},{6,2},{2,0},{1,5},{5,9},... | collective-permute-start | bytes 442376 | tf_op jit(solution)/shard_map/ppermute | solution.py:55
  16.8 0.4 collective-permute-start.5
  17.3 3.1 %load.10.refs_14_ = bf16[384,9216]{1,0:T(8,128)(2,1)S(1)} custom-call(bf16[1536,9216]{1,0:T(8,128)(2,1)} %refs_0_.13, bf16[8,9216]{1,0:T(8,128)(2,1)S(1)} %collective-permute-done.2.refs_1_.refs_6_, bf16[8,9216]{1,0:T(8,128)(2,1)S(1)} %collective-permute-done.3.refs_2_.refs_7_), custom_call_target="tpu_custom_call" | custom-call | tf_op jit(solution)/shard_map/load/pallas_call | solution.py:103
  20.6 1.4 %collective-permute-done.5.refs_2_.refs_3_.refs_9_ = bf16[8,9216]{1,0:T(8,128)(2,1)S(1)} collective-permute-done((bf16[8,9216]{1,0:T(8,128)(2,1)S(1)}, bf16[8,9216]{1,0:T(8,128)(2,1)S(1)}, u32[]{:S(2)}, u32[]{:S(2)}) %collective-permute-start.5) | collective-permute-done | bytes 147488 | tf_op jit(solution)/shard_map/ppermute | solution.py:55
  22.0 1.9 %collective-permute-start.6 = (bf16[8,4608]{1,0:T(8,128)(2,1)S(1)}, bf16[8,4608]{1,0:T(8,128)(2,1)S(1)}, u32[]{:S(2)}, u32[]{:S(2)}) collective-permute-start(bf16[8,4608]{1,0:T(8,128)(2,1)S(1)} %slice.12), channel_id=1, source_target_pairs={{0,4},{4,8},{8,12},{12,14},{14,10},{10,6},{6,2},{2,0},{1,5},{5,9},... | collective-permute-start | bytes 221192 | tf_op jit(solution)/shard_map/ppermute | solution.py:55
  24.1 3.4 %load.11.refs_15_ = bf16[512,9216]{1,0:T(8,128)(2,1)S(1)} custom-call(bf16[1536,9216]{1,0:T(8,128)(2,1)} %refs_0_.13, bf16[64,9216]{1,0:T(8,128)(2,1)} %refs_1_.1, bf16[8,9216]{1,0:T(8,128)(2,1)S(1)} %collective-permute-done.4.refs_1_.refs_2_.refs_8_, bf16[8,9216]{1,0:T(8,128)(2,1)S(1)} %collective-permute-done.5.refs_2_.refs_3_.refs_9_), custom_call_target="tpu_custom_call" | custom-call | tf_op jit(solution)/shard_map/load/pallas_call | solution.py:103
  27.6 0.7 collective-permute-done.7.refs_2_.refs_11_
  28.5 1.2 %collective-permute-done.8.refs_1_ = f32[64,128]{1,0:T(8,128)S(1)} collective-permute-done((f32[64,128]{1,0:T(8,128)S(1)}, f32[64,128]{1,0:T(8,128)S(1)}, u32[]{:S(2)}, u32[]{:S(2)}) %collective-permute-start.8) | collective-permute-done | bytes 32800 | tf_op jit(solution)/shard_map/ppermute | solution.py:44
  29.7 11.7 %project.1 = (f32[8,4,1664]{2,1,0:T(4,128)S(1)}, f32[8,4,1664]{2,1,0:T(4,128)S(1)}, bf16[3072,2304]{1,0:T(8,128)(2,1)S(1)}) custom-call(f32[64,128]{1,0:T(8,128)S(1)} %row_sums.7.refs_0_, f32[64,128]{1,0:T(8,128)S(1)} %collective-permute-done.8.refs_1_, f32[1,9216]{1,0:T(1,128)S(1)} %bitcast.3, bf16[8,9216]{1,0:T(8,128)(2,1)S(1)} %copy-done, ...), custom_call_target="tpu_custom_call" | custom-call | tf_op jit(solution)/shard_map/project/pallas_call | solution.py:231
  41.4 0.2 collective-permute-start.9
  41.6 1.3 %collective-permute-done.9.got = f32[8,4,1664]{2,1,0:T(4,128)S(1)} collective-permute-done((f32[8,4,1664]{2,1,0:T(4,128)S(1)}, f32[8,4,1664]{2,1,0:T(4,128)S(1)}, u32[]{:S(2)}, u32[]{:S(2)}) %collective-permute-start.9) | collective-permute-done | bytes 213024 | tf_op jit(solution)/shard_map/ppermute | solution.py:44
  43.1 2.2 %load_cache.2.refs_6_ = bf16[4,2048,256]{2,1,0:T(8,128)(2,1)S(1)} custom-call(bf16[4,2048,256]{2,1,0:T(8,128)(2,1)} %source.2, bf16[4,4,1664]{2,1,0:T(4,128)(2,1)S(1)} %get-tuple-element.61.refs_0_), custom_call_target="tpu_custom_call" | custom-call | tf_op jit(solution)/shard_map/load_cache/pallas_call | solution.py:125
  45.3 1.8 %collective-permute-done.10.refs_1_ = bf16[4,4,1664]{2,1,0:T(4,128)(2,1)S(1)} collective-permute-done((bf16[4,4,1664]{2,1,0:T(4,128)(2,1)S(1)}, bf16[4,4,1664]{2,1,0:T(4,128)(2,1)S(1)}, u32[]{:S(2)}, u32[]{:S(2)}) %collective-permute-start.10) | collective-permute-done | bytes 53280 | tf_op jit(solution)/shard_map/ppermute | solution.py:548
  47.2 1.2 %collective-permute-start.11 = (bf16[4,4,1664]{2,1,0:T(4,128)(2,1)S(1)}, bf16[4,4,1664]{2,1,0:T(4,128)(2,1)S(1)}, u32[]{:S(2)}, u32[]{:S(2)}) collective-permute-start(bf16[4,4,1664]{2,1,0:T(4,128)(2,1)S(1)} %pack.2.refs_0_), channel_id=1, source_target_pairs={{0,4},{2,6},{4,0},{6,2},{8,12},{10,14},{12,8},{14,10},{1,5},{3,7},... | collective-permute-start | bytes 159752 | tf_op jit(solution)/shard_map/ppermute | solution.py:548
  48.4 2.2 %load_cache.3.refs_7_ = bf16[4,2048,256]{2,1,0:T(8,128)(2,1)S(1)} custom-call(bf16[4,2048,256]{2,1,0:T(8,128)(2,1)} %source.3, bf16[4,4,1664]{2,1,0:T(4,128)(2,1)S(1)} %pack.2.refs_0_), custom_call_target="tpu_custom_call" | custom-call | tf_op jit(solution)/shard_map/load_cache/pallas_call | solution.py:125
  50.7 0.7 collective-permute-done.11.refs_2_
  51.3 0.7 collective-permute-start.12
  52.1 4.2 %collective-permute-done.12.refs_3_ = bf16[4,4,1664]{2,1,0:T(4,128)(2,1)S(1)} collective-permute-done((bf16[4,4,1664]{2,1,0:T(4,128)(2,1)S(1)}, bf16[4,4,1664]{2,1,0:T(4,128)(2,1)S(1)}, u32[]{:S(2)}, u32[]{:S(2)}) %collective-permute-start.12) | collective-permute-done | bytes 53280 | tf_op jit(solution)/shard_map/ppermute | solution.py:548
  56.3 3.5 %attend.1 = (bf16[4,6144]{1,0:T(4,128)(2,1)S(1)}, bf16[4,6144]{1,0:T(4,128)(2,1)S(1)}) custom-call(s32[4]{0:T(128)S(1)} %copy-done.1, bf16[4,4,1664]{2,1,0:T(4,128)(2,1)S(1)} %get-tuple-element.60.refs_0_, bf16[4,4,1664]{2,1,0:T(4,128)(2,1)S(1)} %collective-permute-done.10.refs_1_, bf16[4,4,1664]{2,1,0:T(4,128)(2,1)S(1)} %collective-permute-done.11.refs_2_, ...), custom_call_target="tpu_custom_call" | custom-call | tf_op jit(solution)/shard_map/attend/pallas_call | solution.py:351
  59.9 1.2 %collective-permute-done.13 = bf16[4,6144]{1,0:T(4,128)(2,1)S(1)} collective-permute-done((bf16[4,6144]{1,0:T(4,128)(2,1)S(1)}, bf16[4,6144]{1,0:T(4,128)(2,1)S(1)}, u32[]{:S(2)}, u32[]{:S(2)}) %collective-permute-start.13) | collective-permute-done | bytes 49184 | tf_op jit(solution)/shard_map/ppermute | solution.py:44
  61.2 1.4 %collective-permute-start.14 = (bf16[8,6144]{1,0:T(8,128)(2,1)S(1)}, bf16[8,6144]{1,0:T(8,128)(2,1)S(1)}, u32[]{:S(2)}, u32[]{:S(2)}) collective-permute-start(bf16[8,6144]{1,0:T(8,128)(2,1)S(1)} %pad_maximum_fusion.refs_1_.refs_0_), channel_id=1, source_target_pairs={{0,4},{4,8},{8,12},{12,14},{14,10},{10,6},{6,2},{2,0},{1,5},{5,9},... | collective-permute-start | bytes 294920 | tf_op jit(solution)/shard_map/ppermute | solution.py:55
  62.6 0.7 collective-permute-start.15
  63.3 2.0 %load.12.refs_10_ = bf16[768,2304]{1,0:T(8,128)(2,1)S(1)} custom-call(bf16[6144,2304]{1,0:T(8,128)(2,1)} %refs_0_.17, bf16[8,6144]{1,0:T(8,128)(2,1)S(1)} %pad_maximum_fusion.refs_1_.refs_0_), custom_call_target="tpu_custom_call" | custom-call | tf_op jit(solution)/shard_map/load/pallas_call | solution.py:103
  65.3 0.8 collective-permute-done.14.refs_1_
  66.1 1.1 %collective-permute-done.15.refs_2_ = bf16[8,6144]{1,0:T(8,128)(2,1)S(1)} collective-permute-done((bf16[8,6144]{1,0:T(8,128)(2,1)S(1)}, bf16[8,6144]{1,0:T(8,128)(2,1)S(1)}, u32[]{:S(2)}, u32[]{:S(2)}) %collective-permute-start.15) | collective-permute-done | bytes 98336 | tf_op jit(solution)/shard_map/ppermute | solution.py:55
  67.2 0.3 collective-permute-start.16
  67.5 1.7 %collective-permute-start.17 = (bf16[8,6144]{1,0:T(8,128)(2,1)S(1)}, bf16[8,6144]{1,0:T(8,128)(2,1)S(1)}, u32[]{:S(2)}, u32[]{:S(2)}) collective-permute-start(bf16[8,6144]{1,0:T(8,128)(2,1)S(1)} %collective-permute-done.15.refs_2_), channel_id=1, source_target_pairs={{0,2},{4,0},{8,4},{12,8},{14,12},{10,14},{6,10},{2,6},{1,3},{5,1},... | collective-permute-start | bytes 294920 | tf_op jit(solution)/shard_map/ppermute | solution.py:55
  69.3 2.0 %load.13.refs_11_ = bf16[768,2304]{1,0:T(8,128)(2,1)S(1)} custom-call(bf16[6144,2304]{1,0:T(8,128)(2,1)} %refs_0_.17, bf16[8,6144]{1,0:T(8,128)(2,1)S(1)} %collective-permute-done.14.refs_1_, bf16[8,6144]{1,0:T(8,128)(2,1)S(1)} %collective-permute-done.15.refs_2_), custom_call_target="tpu_custom_call" | custom-call | tf_op jit(solution)/shard_map/load/pallas_call | solution.py:103
  71.3 0.6 collective-permute-done.16.refs_1_.refs_3_
  71.8 0.3 collective-permute-done.17.refs_2_.refs_4_
  72.2 0.3 collective-permute-start.18
  72.4 1.8 %collective-permute-start.19 = (bf16[8,6144]{1,0:T(8,128)(2,1)S(1)}, bf16[8,6144]{1,0:T(8,128)(2,1)S(1)}, u32[]{:S(2)}, u32[]{:S(2)}) collective-permute-start(bf16[8,6144]{1,0:T(8,128)(2,1)S(1)} %collective-permute-done.17.refs_2_.refs_4_), channel_id=1, source_target_pairs={{0,2},{4,0},{8,4},{12,8},{14,12},{10,14},{6,10},{2,6},{1,3},{5,1},... | collective-permute-start | bytes 294920 | tf_op jit(solution)/shard_map/ppermute | solution.py:55
  74.2 2.0 %load.14.refs_12_ = bf16[768,2304]{1,0:T(8,128)(2,1)S(1)} custom-call(bf16[6144,2304]{1,0:T(8,128)(2,1)} %refs_0_.17, bf16[8,6144]{1,0:T(8,128)(2,1)S(1)} %collective-permute-done.16.refs_1_.refs_3_, bf16[8,6144]{1,0:T(8,128)(2,1)S(1)} %collective-permute-done.17.refs_2_.refs_4_), custom_call_target="tpu_custom_call" | custom-call | tf_op jit(solution)/shard_map/load/pallas_call | solution.py:103
  76.2 1.0 %collective-permute-done.18.refs_1_.refs_5_ = bf16[8,6144]{1,0:T(8,128)(2,1)S(1)} collective-permute-done((bf16[8,6144]{1,0:T(8,128)(2,1)S(1)}, bf16[8,6144]{1,0:T(8,128)(2,1)S(1)}, u32[]{:S(2)}, u32[]{:S(2)}) %collective-permute-start.18) | collective-permute-done | bytes 98336 | tf_op jit(solution)/shard_map/ppermute | solution.py:55
  77.2 0.3 collective-permute-done.19.refs_2_.refs_6_
  77.5 2.1 %collective-permute-start.21 = (bf16[8,3072]{1,0:T(8,128)(2,1)S(1)}, bf16[8,3072]{1,0:T(8,128)(2,1)S(1)}, u32[]{:S(2)}, u32[]{:S(2)}) collective-permute-start(bf16[8,3072]{1,0:T(8,128)(2,1)S(1)} %slice.15), channel_id=1, source_target_pairs={{0,2},{4,0},{8,4},{12,8},{14,12},{10,14},{6,10},{2,6},{1,3},{5,1},... | collective-permute-start | bytes 147464 | tf_op jit(solution)/shard_map/ppermute | solution.py:55
  79.6 2.0 %load.15.refs_13_ = bf16[768,2304]{1,0:T(8,128)(2,1)S(1)} custom-call(bf16[6144,2304]{1,0:T(8,128)(2,1)} %refs_0_.17, bf16[8,6144]{1,0:T(8,128)(2,1)S(1)} %collective-permute-done.18.refs_1_.refs_5_, bf16[8,6144]{1,0:T(8,128)(2,1)S(1)} %collective-permute-done.19.refs_2_.refs_6_), custom_call_target="tpu_custom_call" | custom-call | tf_op jit(solution)/shard_map/load/pallas_call | solution.py:103
  81.8 5.1 %output_project.1 = (f32[4,8,2304]{2,1,0:T(8,128)S(1)}, f32[4,8,2304]{2,1,0:T(8,128)S(1)}) custom-call(bf16[8,6144]{1,0:T(8,128)(2,1)S(1)} %pad_maximum_fusion.refs_1_.refs_0_, bf16[8,6144]{1,0:T(8,128)(2,1)S(1)} %collective-permute-done.14.refs_1_, bf16[8,6144]{1,0:T(8,128)(2,1)S(1)} %collective-permute-done.15.refs_2_, ...), custom_call_target="tpu_custom_call" | custom-call | tf_op jit(solution)/shard_map/output_project/pallas_call | solution.py:405
  87.0 1.6 %collective-permute-done.22 = f32[4,8,2304]{2,1,0:T(8,128)S(1)} collective-permute-done((f32[4,8,2304]{2,1,0:T(8,128)S(1)}, f32[4,8,2304]{2,1,0:T(8,128)S(1)}, u32[]{:S(2)}, u32[]{:S(2)}) %collective-permute-start.22) | collective-permute-done | bytes 294944 | tf_op jit(solution)/shard_map/ppermute | solution.py:44
  88.5 0.7 fusion
  (34 shorter events, 1.7 us)
Async XLA Ops:
  0.0 10.6 %copy-start = (bf16[8,9216]{1,0:T(8,128)(2,1)S(1)}, bf16[8,9216]{1,0:T(8,128)(2,1)}, u32[]{:S(2)}) copy-start(bf16[8,9216]{1,0:T(8,128)(2,1)} %refs_3_.1) | copy-start | bytes 442372
  0.0 7.1 %collective-permute-start = (bf16[8,9216]{1,0:T(8,128)(2,1)}, bf16[8,9216]{1,0:T(8,128)(2,1)S(1)}, u32[]{:S(2)}, u32[]{:S(2)}) collective-permute-start(bf16[8,9216]{1,0:T(8,128)(2,1)} %refs_3_.1), channel_id=1, source_target_pairs={{0,4},{4,8},{8,12},{12,14},{14,10},{10,6},{6,2},{2,0},{1,5},{5,9},... | collective-permute-start | bytes 442376 | tf_op jit(solution)/shard_map/ppermute | solution.py:55
  3.0 5.5 %collective-permute-start.1 = (bf16[8,9216]{1,0:T(8,128)(2,1)}, bf16[8,9216]{1,0:T(8,128)(2,1)S(1)}, u32[]{:S(2)}, u32[]{:S(2)}) collective-permute-start(bf16[8,9216]{1,0:T(8,128)(2,1)} %refs_3_.1), channel_id=1, source_target_pairs={{0,2},{4,0},{8,4},{12,8},{14,12},{10,14},{6,10},{2,6},{1,3},{5,1},... | collective-permute-start | bytes 442376 | tf_op jit(solution)/shard_map/ppermute | solution.py:55
  8.5 5.4 %collective-permute-start.2 = (bf16[8,9216]{1,0:T(8,128)(2,1)S(1)}, bf16[8,9216]{1,0:T(8,128)(2,1)S(1)}, u32[]{:S(2)}, u32[]{:S(2)}) collective-permute-start(bf16[8,9216]{1,0:T(8,128)(2,1)S(1)} %collective-permute-done.refs_1_.refs_4_), channel_id=1, source_target_pairs={{0,4},{4,8},{8,12},{12,14},{14,10},{10,6},{6,2},{2,0},{1,5},{5,9},... | collective-permute-start | bytes 442376 | tf_op jit(solution)/shard_map/ppermute | solution.py:55
  10.1 5.1 %collective-permute-start.3 = (bf16[8,9216]{1,0:T(8,128)(2,1)S(1)}, bf16[8,9216]{1,0:T(8,128)(2,1)S(1)}, u32[]{:S(2)}, u32[]{:S(2)}) collective-permute-start(bf16[8,9216]{1,0:T(8,128)(2,1)S(1)} %collective-permute-done.1.refs_2_.refs_5_), channel_id=1, source_target_pairs={{0,2},{4,0},{8,4},{12,8},{14,12},{10,14},{6,10},{2,6},{1,3},{5,1},... | collective-permute-start | bytes 442376 | tf_op jit(solution)/shard_map/ppermute | solution.py:55
  15.3 5.3 %collective-permute-start.4 = (bf16[8,9216]{1,0:T(8,128)(2,1)S(1)}, bf16[8,9216]{1,0:T(8,128)(2,1)S(1)}, u32[]{:S(2)}, u32[]{:S(2)}) collective-permute-start(bf16[8,9216]{1,0:T(8,128)(2,1)S(1)} %collective-permute-done.2.refs_1_.refs_6_), channel_id=1, source_target_pairs={{0,4},{4,8},{8,12},{12,14},{14,10},{10,6},{6,2},{2,0},{1,5},{5,9},... | collective-permute-start | bytes 442376 | tf_op jit(solution)/shard_map/ppermute | solution.py:55
  16.8 5.1 %collective-permute-start.5 = (bf16[8,9216]{1,0:T(8,128)(2,1)S(1)}, bf16[8,9216]{1,0:T(8,128)(2,1)S(1)}, u32[]{:S(2)}, u32[]{:S(2)}) collective-permute-start(bf16[8,9216]{1,0:T(8,128)(2,1)S(1)} %collective-permute-done.3.refs_2_.refs_7_), channel_id=1, source_target_pairs={{0,2},{4,0},{8,4},{12,8},{14,12},{10,14},{6,10},{2,6},{1,3},{5,1},... | collective-permute-start | bytes 442376 | tf_op jit(solution)/shard_map/ppermute | solution.py:55
  22.0 5.7 %collective-permute-start.6 = (bf16[8,4608]{1,0:T(8,128)(2,1)S(1)}, bf16[8,4608]{1,0:T(8,128)(2,1)S(1)}, u32[]{:S(2)}, u32[]{:S(2)}) collective-permute-start(bf16[8,4608]{1,0:T(8,128)(2,1)S(1)} %slice.12), channel_id=1, source_target_pairs={{0,4},{4,8},{8,12},{12,14},{14,10},{10,6},{6,2},{2,0},{1,5},{5,9},... | collective-permute-start | bytes 221192 | tf_op jit(solution)/shard_map/ppermute | solution.py:55
  23.9 4.5 %copy-start.2 = (bf16[9216]{0:T(1024)(128)(2,1)S(1)}, bf16[9216]{0:T(1024)(128)(2,1)}, u32[]{:S(2)}) copy-start(bf16[9216]{0:T(1024)(128)(2,1)} %param.9) | copy-start | bytes 55300
  23.9 4.4 %collective-permute-start.7 = (bf16[8,4608]{1,0:T(8,128)(2,1)S(1)}, bf16[8,4608]{1,0:T(8,128)(2,1)S(1)}, u32[]{:S(2)}, u32[]{:S(2)}) collective-permute-start(bf16[8,4608]{1,0:T(8,128)(2,1)S(1)} %slice.13), channel_id=1, source_target_pairs={{0,2},{4,0},{8,4},{12,8},{14,12},{10,14},{6,10},{2,6},{1,3},{5,1},... | collective-permute-start | bytes 221192 | tf_op jit(solution)/shard_map/ppermute | solution.py:55
  28.5 1.2 %collective-permute-start.8 = (f32[64,128]{1,0:T(8,128)S(1)}, f32[64,128]{1,0:T(8,128)S(1)}, u32[]{:S(2)}, u32[]{:S(2)}) collective-permute-start(f32[64,128]{1,0:T(8,128)S(1)} %row_sums.7.refs_0_), channel_id=1, source_target_pairs={{0,1},{1,0},{2,3},{3,2},{4,5},{5,4},{6,7},{7,6},{8,9},{9,8},{10,11... | collective-permute-start | bytes 98312 | tf_op jit(solution)/shard_map/ppermute | solution.py:44
  41.4 1.5 %collective-permute-start.9 = (f32[8,4,1664]{2,1,0:T(4,128)S(1)}, f32[8,4,1664]{2,1,0:T(4,128)S(1)}, u32[]{:S(2)}, u32[]{:S(2)}) collective-permute-start(f32[8,4,1664]{2,1,0:T(4,128)S(1)} %get-tuple-element.59), channel_id=1, source_target_pairs={{0,1},{1,0},{2,3},{3,2},{4,5},{5,4},{6,7},{7,6},{8,9},{9,8},{10,11... | collective-permute-start | bytes 638984 | tf_op jit(solution)/shard_map/ppermute | solution.py:44
  43.0 5.5 %copy-start.1 = (s32[4]{0:T(128)S(1)}, s32[4]{0:T(128)}, u32[]{:S(2)}) copy-start(s32[4]{0:T(128)} %lengths.1) | copy-start | bytes 52
  43.0 4.2 %collective-permute-start.10 = (bf16[4,4,1664]{2,1,0:T(4,128)(2,1)S(1)}, bf16[4,4,1664]{2,1,0:T(4,128)(2,1)S(1)}, u32[]{:S(2)}, u32[]{:S(2)}) collective-permute-start(bf16[4,4,1664]{2,1,0:T(4,128)(2,1)S(1)} %get-tuple-element.61.refs_0_), channel_id=1, source_target_pairs={{0,2},{2,0},{4,6},{6,4},{8,10},{10,8},{12,14},{14,12},{1,3},{3,1},... | collective-permute-start | bytes 159752 | tf_op jit(solution)/shard_map/ppermute | solution.py:548
  47.2 4.1 %collective-permute-start.11 = (bf16[4,4,1664]{2,1,0:T(4,128)(2,1)S(1)}, bf16[4,4,1664]{2,1,0:T(4,128)(2,1)S(1)}, u32[]{:S(2)}, u32[]{:S(2)}) collective-permute-start(bf16[4,4,1664]{2,1,0:T(4,128)(2,1)S(1)} %pack.2.refs_0_), channel_id=1, source_target_pairs={{0,4},{2,6},{4,0},{6,2},{8,12},{10,14},{12,8},{14,10},{1,5},{3,7},... | collective-permute-start | bytes 159752 | tf_op jit(solution)/shard_map/ppermute | solution.py:548
  51.3 5.0 %collective-permute-start.12 = (bf16[4,4,1664]{2,1,0:T(4,128)(2,1)S(1)}, bf16[4,4,1664]{2,1,0:T(4,128)(2,1)S(1)}, u32[]{:S(2)}, u32[]{:S(2)}) collective-permute-start(bf16[4,4,1664]{2,1,0:T(4,128)(2,1)S(1)} %pack.3), channel_id=1, source_target_pairs={{0,8},{2,10},{4,12},{6,14},{8,0},{10,2},{12,4},{14,6},{1,9},{3,11}... | collective-permute-start | bytes 159752 | tf_op jit(solution)/shard_map/ppermute | solution.py:548
  59.8 1.3 %collective-permute-start.13 = (bf16[4,6144]{1,0:T(4,128)(2,1)S(1)}, bf16[4,6144]{1,0:T(4,128)(2,1)S(1)}, u32[]{:S(2)}, u32[]{:S(2)}) collective-permute-start(bf16[4,6144]{1,0:T(4,128)(2,1)S(1)} %get-tuple-element.67), channel_id=1, source_target_pairs={{0,1},{1,0},{2,3},{3,2},{4,5},{5,4},{6,7},{7,6},{8,9},{9,8},{10,11... | collective-permute-start | bytes 147464 | tf_op jit(solution)/shard_map/ppermute | solution.py:44
  61.2 4.9 %collective-permute-start.14 = (bf16[8,6144]{1,0:T(8,128)(2,1)S(1)}, bf16[8,6144]{1,0:T(8,128)(2,1)S(1)}, u32[]{:S(2)}, u32[]{:S(2)}) collective-permute-start(bf16[8,6144]{1,0:T(8,128)(2,1)S(1)} %pad_maximum_fusion.refs_1_.refs_0_), channel_id=1, source_target_pairs={{0,4},{4,8},{8,12},{12,14},{14,10},{10,6},{6,2},{2,0},{1,5},{5,9},... | collective-permute-start | bytes 294920 | tf_op jit(solution)/shard_map/ppermute | solution.py:55
  62.6 4.6 %collective-permute-start.15 = (bf16[8,6144]{1,0:T(8,128)(2,1)S(1)}, bf16[8,6144]{1,0:T(8,128)(2,1)S(1)}, u32[]{:S(2)}, u32[]{:S(2)}) collective-permute-start(bf16[8,6144]{1,0:T(8,128)(2,1)S(1)} %pad_maximum_fusion.refs_1_.refs_0_), channel_id=1, source_target_pairs={{0,2},{4,0},{8,4},{12,8},{14,12},{10,14},{6,10},{2,6},{1,3},{5,1},... | collective-permute-start | bytes 294920 | tf_op jit(solution)/shard_map/ppermute | solution.py:55
  67.2 4.6 %collective-permute-start.16 = (bf16[8,6144]{1,0:T(8,128)(2,1)S(1)}, bf16[8,6144]{1,0:T(8,128)(2,1)S(1)}, u32[]{:S(2)}, u32[]{:S(2)}) collective-permute-start(bf16[8,6144]{1,0:T(8,128)(2,1)S(1)} %collective-permute-done.14.refs_1_), channel_id=1, source_target_pairs={{0,4},{4,8},{8,12},{12,14},{14,10},{10,6},{6,2},{2,0},{1,5},{5,9},... | collective-permute-start | bytes 294920 | tf_op jit(solution)/shard_map/ppermute | solution.py:55
  67.5 4.6 %collective-permute-start.17 = (bf16[8,6144]{1,0:T(8,128)(2,1)S(1)}, bf16[8,6144]{1,0:T(8,128)(2,1)S(1)}, u32[]{:S(2)}, u32[]{:S(2)}) collective-permute-start(bf16[8,6144]{1,0:T(8,128)(2,1)S(1)} %collective-permute-done.15.refs_2_), channel_id=1, source_target_pairs={{0,2},{4,0},{8,4},{12,8},{14,12},{10,14},{6,10},{2,6},{1,3},{5,1},... | collective-permute-start | bytes 294920 | tf_op jit(solution)/shard_map/ppermute | solution.py:55
  72.2 5.0 %collective-permute-start.18 = (bf16[8,6144]{1,0:T(8,128)(2,1)S(1)}, bf16[8,6144]{1,0:T(8,128)(2,1)S(1)}, u32[]{:S(2)}, u32[]{:S(2)}) collective-permute-start(bf16[8,6144]{1,0:T(8,128)(2,1)S(1)} %collective-permute-done.16.refs_1_.refs_3_), channel_id=1, source_target_pairs={{0,4},{4,8},{8,12},{12,14},{14,10},{10,6},{6,2},{2,0},{1,5},{5,9},... | collective-permute-start | bytes 294920 | tf_op jit(solution)/shard_map/ppermute | solution.py:55
  72.4 5.1 %collective-permute-start.19 = (bf16[8,6144]{1,0:T(8,128)(2,1)S(1)}, bf16[8,6144]{1,0:T(8,128)(2,1)S(1)}, u32[]{:S(2)}, u32[]{:S(2)}) collective-permute-start(bf16[8,6144]{1,0:T(8,128)(2,1)S(1)} %collective-permute-done.17.refs_2_.refs_4_), channel_id=1, source_target_pairs={{0,2},{4,0},{8,4},{12,8},{14,12},{10,14},{6,10},{2,6},{1,3},{5,1},... | collective-permute-start | bytes 294920 | tf_op jit(solution)/shard_map/ppermute | solution.py:55
  77.5 4.1 %collective-permute-start.20 = (bf16[8,3072]{1,0:T(8,128)(2,1)S(1)}, bf16[8,3072]{1,0:T(8,128)(2,1)S(1)}, u32[]{:S(2)}, u32[]{:S(2)}) collective-permute-start(bf16[8,3072]{1,0:T(8,128)(2,1)S(1)} %slice.14), channel_id=1, source_target_pairs={{0,4},{4,8},{8,12},{12,14},{14,10},{10,6},{6,2},{2,0},{1,5},{5,9},... | collective-permute-start | bytes 147464 | tf_op jit(solution)/shard_map/ppermute | solution.py:55
  77.5 4.3 %collective-permute-start.21 = (bf16[8,3072]{1,0:T(8,128)(2,1)S(1)}, bf16[8,3072]{1,0:T(8,128)(2,1)S(1)}, u32[]{:S(2)}, u32[]{:S(2)}) collective-permute-start(bf16[8,3072]{1,0:T(8,128)(2,1)S(1)} %slice.15), channel_id=1, source_target_pairs={{0,2},{4,0},{8,4},{12,8},{14,12},{10,14},{6,10},{2,6},{1,3},{5,1},... | collective-permute-start | bytes 147464 | tf_op jit(solution)/shard_map/ppermute | solution.py:55
  86.9 1.6 %collective-permute-start.22 = (f32[4,8,2304]{2,1,0:T(8,128)S(1)}, f32[4,8,2304]{2,1,0:T(8,128)S(1)}, u32[]{:S(2)}, u32[]{:S(2)}) collective-permute-start(f32[4,8,2304]{2,1,0:T(8,128)S(1)} %get-tuple-element.82), channel_id=1, source_target_pairs={{0,1},{1,0},{2,3},{3,2},{4,5},{5,4},{6,7},{7,6},{8,9},{9,8},{10,11... | collective-permute-start | bytes 884744 | tf_op jit(solution)/shard_map/ppermute | solution.py:44

commit v11 on v10

--- a/solution.py
+++ b/solution.py
@@ -250,21 +250,20 @@
     )
 
 
-def split_kernel(keep, got, here, there):
+def split_kernel(keep, got, *outs):
     me = lax.axis_index("gx")
     for d in range(keep.shape[0]):
         at = jnp.bitwise_xor(me, d)
-        out = there if d % 2 else here
-        out[d // 2] = (keep[at] + got[at]).astype(jnp.bfloat16)
+        outs[d % 4][d // 4] = (keep[at] + got[at]).astype(jnp.bfloat16)
 
 
 def split(keep, got):
-    shape = jax.ShapeDtypeStruct((keep.shape[0] // 2,) + keep.shape[1:], jnp.bfloat16)
+    shape = jax.ShapeDtypeStruct((2,) + keep.shape[1:], jnp.bfloat16)
     return pl.pallas_call(
         split_kernel,
-        out_shape=[shape] * 2,
+        out_shape=[shape] * 4,
         in_specs=[IN_VMEM] * 2,
-        out_specs=[IN_VMEM] * 2,
+        out_specs=[IN_VMEM] * 4,
         compiler_params=pltpu.CompilerParams(vmem_limit_bytes=8 * MIB),
         name="split",
     )(keep, got)
@@ -285,12 +284,12 @@
     )(*sources)
 
 
-ARRIVED = [(0, 0), (1, 0), (2, 0), (2, 1), (3, 0), (3, 1), (3, 2), (3, 3)]
+ARRIVED = [(0, 0), (1, 0), (2, 0), (3, 0), (4, 0), (4, 1), (4, 2), (4, 3)]
 
 
 def attend_kernel(lengths, *refs):
-    arrived = refs[:4]
-    cosine, sine, keys, values, mine, other, spread, held = refs[4:]
+    arrived = refs[:5]
+    cosine, sine, keys, values, mine, other, spread, held = refs[5:]
     n, rows, stripe = spread.shape[1], spread.shape[0], spread.shape[2]
     me = lax.axis_index("gx")
     query_cols = stripe - 128
@@ -351,7 +350,7 @@
     return pl.pallas_call(
         attend_kernel,
         out_shape=[shape, shape],
-        in_specs=[IN_SMEM] + [IN_VMEM] * 8,
+        in_specs=[IN_SMEM] + [IN_VMEM] * 9,
         out_specs=[IN_VMEM] * 2,
         scratch_shapes=[
             pltpu.VMEM((rows, n, stripe), jnp.float32),
@@ -543,20 +542,18 @@
     )
     weights = [weight]
 
-    here, there = split(keep, swap_pair(give))
-    def exchange(blocks, bit):
-        return lax.ppermute(blocks, "gx", [(i, i ^ bit) for i in range(n)])
-
-    second = exchange(there, 1)
-    keys = load_cache(cache_keys, [there])
-    keys, (second,) = before(keys, second)
-    across = pack([(0, 1), (1, 1), (0, 3), (1, 3)], here, second)
-    third = exchange(across, 2)
+    def exchange(blocks, d):
+        return lax.ppermute(blocks, "gx", [(i, i ^ d) for i in range(n)])
+
+    blocks = split(keep, swap_pair(give))
+    arrived = [blocks[0]] + [exchange(blocks[d], d) for d in range(1, 4)]
+    keys = load_cache(cache_keys, [blocks[1]])
+    keys, arrived = before(keys, *arrived)
+    across = pack([(0, 1), (1, 1), (2, 1), (3, 1)], *arrived)
+    last = exchange(across, 4)
     values = load_cache(cache_values, [across])
-    values, (third,) = before(values, third)
-    across = pack([(0, 2), (1, 2), (2, 2), (2, 3)], here, second, third)
-    fourth = exchange(across, 4)
-    arrived = [here, second, third, fourth]
+    values, (last,) = before(values, last)
+    arrived = [*arrived, last]
     mine, other = attend(cache_lengths, arrived, cosine, sine, keys, values)
     shard = jnp.concatenate([mine, swap_pair(other)], axis=0)
 

time: 89.4 us -> 89.6 us (level)
  starting transfers between devices: 19.9 us -> 22 us
  waiting for transfers between devices: 22.2 us -> 20.2 us
    ppermute x3 -> x4, waiting for transfers between devices: 6.69 us -> 3.13 us  [exchange(): return lax.ppermute(blocks, 'gx', [(i, i ^ d) for i in range(n)])]
    ppermute x8, starting transfers between devices: 10.1 us -> 12.7 us  [step(): lax.ppermute(left, 'gx', self.onward)]
    ppermute x8, starting transfers between devices: 7.26 us -> 4.93 us  [step(): lax.ppermute(right, 'gx', self.back)]
    ppermute x3 -> x4, starting transfers between devices: 2.12 us -> 4.03 us  [exchange(): return lax.ppermute(blocks, 'gx', [(i, i ^ d) for i in range(n)])]
    ppermute x8, waiting for transfers between devices: 6.82 us -> 8.69 us  [step(): lax.ppermute(right, 'gx', self.back)]
  transfers between devices with their start and end apart: 23 -> 24, of which waited for: 19 -> 18; matrix products, arithmetic and copies ran while one was open for 0% -> 0% of each run, Pallas kernels for 29% -> 29%
where the time goes in v11:
time: 89.6 us; the launch traced here: 89.4 us
  Pallas kernels  46 us (51%)
  starting transfers between devices  22 us (25%)
  waiting for transfers between devices  20.2 us (23%)
    pallas_call x8, Pallas kernels, load(): pl.pallas_call(lambda *refs: load_kernel([job[1:] for job in jobs], *refs...  20.7 us
    ppermute x8, starting transfers between devices, step(): lax.ppermute(left, 'gx', self.onward)  12.7 us
    pallas_call x1, Pallas kernels, project(): pl.pallas_call(lambda *refs: project_kernel(n, len(weights), *refs), out_...  11.7 us
    ppermute x8, waiting for transfers between devices, step(): lax.ppermute(right, 'gx', self.back)  8.69 us
    ppermute x4, waiting for transfers between devices, swap_pair(): return lax.ppermute(x, 'gy', [(0, 1), (1, 0)])  5.26 us
    pallas_call x1, Pallas kernels, output_project(): pl.pallas_call(lambda *refs: output_kernel(n, *refs), out_shape=[shape, s...  5.05 us
    ppermute x8, starting transfers between devices, step(): lax.ppermute(right, 'gx', self.back)  4.93 us
    pallas_call x2, Pallas kernels, load_cache(): pl.pallas_call(load_cache_kernel, out_shape=pltpu.VMEM(cache.shape, cache...  4.42 us
  transfers between devices with their start and end apart: 24, of which 18 were waited for; matrix products, arithmetic and copies ran while one was open for 0% of the time, Pallas kernels for 29%

profile of v11, /device:TPU:0, one launch (start us, length us, event | category | flops | bytes accessed | tf_op | source)
XLA Modules:
  0.0 89.4 jit_solution(12933909886538460814)
XLA Ops:
  0.0 3.0 %collective-permute-start = (bf16[8,9216]{1,0:T(8,128)(2,1)}, bf16[8,9216]{1,0:T(8,128)(2,1)S(1)}, u32[]{:S(2)}, u32[]{:S(2)}) collective-permute-start(bf16[8,9216]{1,0:T(8,128)(2,1)} %refs_3_.1), channel_id=1, source_target_pairs={{0,4},{4,8},{8,12},{12,14},{14,10},{10,6},{6,2},{2,0},{1,5},{5,9},... | collective-permute-start | bytes 442376 | tf_op jit(solution)/shard_map/ppermute | solution.py:55
  3.0 3.1 %load.8.refs_12_ = bf16[384,9216]{1,0:T(8,128)(2,1)S(1)} custom-call(bf16[1536,9216]{1,0:T(8,128)(2,1)} %refs_0_.13), custom_call_target="tpu_custom_call" | custom-call | tf_op jit(solution)/shard_map/load/pallas_call | solution.py:103
  6.1 1.0 %collective-permute-done.refs_1_.refs_4_ = bf16[8,9216]{1,0:T(8,128)(2,1)S(1)} collective-permute-done((bf16[8,9216]{1,0:T(8,128)(2,1)}, bf16[8,9216]{1,0:T(8,128)(2,1)S(1)}, u32[]{:S(2)}, u32[]{:S(2)}) %collective-permute-start) | collective-permute-done | bytes 147488 | tf_op jit(solution)/shard_map/ppermute | solution.py:55
  7.1 1.4 %collective-permute-done.1.refs_2_.refs_5_ = bf16[8,9216]{1,0:T(8,128)(2,1)S(1)} collective-permute-done((bf16[8,9216]{1,0:T(8,128)(2,1)}, bf16[8,9216]{1,0:T(8,128)(2,1)S(1)}, u32[]{:S(2)}, u32[]{:S(2)}) %collective-permute-start.1) | collective-permute-done | bytes 147488 | tf_op jit(solution)/shard_map/ppermute | solution.py:55
  8.5 1.6 %collective-permute-start.2 = (bf16[8,9216]{1,0:T(8,128)(2,1)S(1)}, bf16[8,9216]{1,0:T(8,128)(2,1)S(1)}, u32[]{:S(2)}, u32[]{:S(2)}) collective-permute-start(bf16[8,9216]{1,0:T(8,128)(2,1)S(1)} %collective-permute-done.refs_1_.refs_4_), channel_id=1, source_target_pairs={{0,4},{4,8},{8,12},{12,14},{14,10},{10,6},{6,2},{2,0},{1,5},{5,9},... | collective-permute-start | bytes 442376 | tf_op jit(solution)/shard_map/ppermute | solution.py:55
  10.1 0.4 collective-permute-start.3
  10.8 3.1 %load.9.refs_13_ = bf16[384,9216]{1,0:T(8,128)(2,1)S(1)} custom-call(bf16[1536,9216]{1,0:T(8,128)(2,1)} %refs_0_.13, bf16[8,9216]{1,0:T(8,128)(2,1)S(1)} %collective-permute-done.refs_1_.refs_4_, bf16[8,9216]{1,0:T(8,128)(2,1)S(1)} %collective-permute-done.1.refs_2_.refs_5_), custom_call_target="tpu_custom_call" | custom-call | tf_op jit(solution)/shard_map/load/pallas_call | solution.py:103
  13.9 1.3 %collective-permute-done.3.refs_2_.refs_7_ = bf16[8,9216]{1,0:T(8,128)(2,1)S(1)} collective-permute-done((bf16[8,9216]{1,0:T(8,128)(2,1)S(1)}, bf16[8,9216]{1,0:T(8,128)(2,1)S(1)}, u32[]{:S(2)}, u32[]{:S(2)}) %collective-permute-start.3) | collective-permute-done | bytes 147488 | tf_op jit(solution)/shard_map/ppermute | solution.py:55
  15.3 1.6 %collective-permute-start.4 = (bf16[8,9216]{1,0:T(8,128)(2,1)S(1)}, bf16[8,9216]{1,0:T(8,128)(2,1)S(1)}, u32[]{:S(2)}, u32[]{:S(2)}) collective-permute-start(bf16[8,9216]{1,0:T(8,128)(2,1)S(1)} %collective-permute-done.2.refs_1_.refs_6_), channel_id=1, source_target_pairs={{0,4},{4,8},{8,12},{12,14},{14,10},{10,6},{6,2},{2,0},{1,5},{5,9},... | collective-permute-start | bytes 442376 | tf_op jit(solution)/shard_map/ppermute | solution.py:55
  16.8 0.4 collective-permute-start.5
  17.3 3.1 %load.10.refs_14_ = bf16[384,9216]{1,0:T(8,128)(2,1)S(1)} custom-call(bf16[1536,9216]{1,0:T(8,128)(2,1)} %refs_0_.13, bf16[8,9216]{1,0:T(8,128)(2,1)S(1)} %collective-permute-done.2.refs_1_.refs_6_, bf16[8,9216]{1,0:T(8,128)(2,1)S(1)} %collective-permute-done.3.refs_2_.refs_7_), custom_call_target="tpu_custom_call" | custom-call | tf_op jit(solution)/shard_map/load/pallas_call | solution.py:103
  20.6 1.4 %collective-permute-done.5.refs_2_.refs_3_.refs_9_ = bf16[8,9216]{1,0:T(8,128)(2,1)S(1)} collective-permute-done((bf16[8,9216]{1,0:T(8,128)(2,1)S(1)}, bf16[8,9216]{1,0:T(8,128)(2,1)S(1)}, u32[]{:S(2)}, u32[]{:S(2)}) %collective-permute-start.5) | collective-permute-done | bytes 147488 | tf_op jit(solution)/shard_map/ppermute | solution.py:55
  22.0 1.9 %collective-permute-start.6 = (bf16[8,4608]{1,0:T(8,128)(2,1)S(1)}, bf16[8,4608]{1,0:T(8,128)(2,1)S(1)}, u32[]{:S(2)}, u32[]{:S(2)}) collective-permute-start(bf16[8,4608]{1,0:T(8,128)(2,1)S(1)} %slice.12), channel_id=1, source_target_pairs={{0,4},{4,8},{8,12},{12,14},{14,10},{10,6},{6,2},{2,0},{1,5},{5,9},... | collective-permute-start | bytes 221192 | tf_op jit(solution)/shard_map/ppermute | solution.py:55
  24.1 3.4 %load.11.refs_15_ = bf16[512,9216]{1,0:T(8,128)(2,1)S(1)} custom-call(bf16[1536,9216]{1,0:T(8,128)(2,1)} %refs_0_.13, bf16[64,9216]{1,0:T(8,128)(2,1)} %refs_1_.1, bf16[8,9216]{1,0:T(8,128)(2,1)S(1)} %collective-permute-done.4.refs_1_.refs_2_.refs_8_, bf16[8,9216]{1,0:T(8,128)(2,1)S(1)} %collective-permute-done.5.refs_2_.refs_3_.refs_9_), custom_call_target="tpu_custom_call" | custom-call | tf_op jit(solution)/shard_map/load/pallas_call | solution.py:103
  27.6 0.7 collective-permute-done.7.refs_2_.refs_11_
  28.5 1.2 %collective-permute-done.8.refs_1_ = f32[64,128]{1,0:T(8,128)S(1)} collective-permute-done((f32[64,128]{1,0:T(8,128)S(1)}, f32[64,128]{1,0:T(8,128)S(1)}, u32[]{:S(2)}, u32[]{:S(2)}) %collective-permute-start.8) | collective-permute-done | bytes 32800 | tf_op jit(solution)/shard_map/ppermute | solution.py:44
  29.7 11.7 %project.1 = (f32[8,4,1664]{2,1,0:T(4,128)S(1)}, f32[8,4,1664]{2,1,0:T(4,128)S(1)}, bf16[3072,2304]{1,0:T(8,128)(2,1)S(1)}) custom-call(f32[64,128]{1,0:T(8,128)S(1)} %row_sums.7.refs_0_, f32[64,128]{1,0:T(8,128)S(1)} %collective-permute-done.8.refs_1_, f32[1,9216]{1,0:T(1,128)S(1)} %bitcast.3, bf16[8,9216]{1,0:T(8,128)(2,1)S(1)} %copy-done, ...), custom_call_target="tpu_custom_call" | custom-call | tf_op jit(solution)/shard_map/project/pallas_call | solution.py:231
  41.4 0.2 collective-permute-start.9
  41.6 1.3 %collective-permute-done.9.got = f32[8,4,1664]{2,1,0:T(4,128)S(1)} collective-permute-done((f32[8,4,1664]{2,1,0:T(4,128)S(1)}, f32[8,4,1664]{2,1,0:T(4,128)S(1)}, u32[]{:S(2)}, u32[]{:S(2)}) %collective-permute-start.9) | collective-permute-done | bytes 213024 | tf_op jit(solution)/shard_map/ppermute | solution.py:44
  43.1 1.2 %collective-permute-start.11 = (bf16[2,4,1664]{2,1,0:T(4,128)(2,1)S(1)}, bf16[2,4,1664]{2,1,0:T(4,128)(2,1)S(1)}, u32[]{:S(2)}, u32[]{:S(2)}) collective-permute-start(bf16[2,4,1664]{2,1,0:T(4,128)(2,1)S(1)} %get-tuple-element.67), channel_id=1, source_target_pairs={{0,4},{2,6},{4,0},{6,2},{8,12},{10,14},{12,8},{14,10},{1,5},{3,7},... | collective-permute-start | bytes 79880 | tf_op jit(solution)/shard_map/ppermute | solution.py:546
  44.3 2.2 %collective-permute-start.12 = (bf16[2,4,1664]{2,1,0:T(4,128)(2,1)S(1)}, bf16[2,4,1664]{2,1,0:T(4,128)(2,1)S(1)}, u32[]{:S(2)}, u32[]{:S(2)}) collective-permute-start(bf16[2,4,1664]{2,1,0:T(4,128)(2,1)S(1)} %get-tuple-element.68), channel_id=1, source_target_pairs={{0,6},{2,4},{4,2},{6,0},{8,14},{10,12},{12,10},{14,8},{1,7},{3,5},... | collective-permute-start | bytes 79880 | tf_op jit(solution)/shard_map/ppermute | solution.py:546
  46.5 2.2 %load_cache.2.refs_7_ = bf16[4,2048,256]{2,1,0:T(8,128)(2,1)S(1)} custom-call(bf16[4,2048,256]{2,1,0:T(8,128)(2,1)} %source.2, bf16[2,4,1664]{2,1,0:T(4,128)(2,1)S(1)} %get-tuple-element.65.refs_0_), custom_call_target="tpu_custom_call" | custom-call | tf_op jit(solution)/shard_map/load_cache/pallas_call | solution.py:125
  48.8 0.3 collective-permute-done.12.refs_3_
  49.1 0.5 collective-permute-start.13
  49.7 2.2 %load_cache.3.refs_8_ = bf16[4,2048,256]{2,1,0:T(8,128)(2,1)S(1)} custom-call(bf16[4,2048,256]{2,1,0:T(8,128)(2,1)} %source.3, bf16[4,4,1664]{2,1,0:T(4,128)(2,1)S(1)} %pack.1.refs_0_), custom_call_target="tpu_custom_call" | custom-call | tf_op jit(solution)/shard_map/load_cache/pallas_call | solution.py:125
  51.9 2.8 %collective-permute-done.13.refs_4_ = bf16[4,4,1664]{2,1,0:T(4,128)(2,1)S(1)} collective-permute-done((bf16[4,4,1664]{2,1,0:T(4,128)(2,1)S(1)}, bf16[4,4,1664]{2,1,0:T(4,128)(2,1)S(1)}, u32[]{:S(2)}, u32[]{:S(2)}) %collective-permute-start.13) | collective-permute-done | bytes 53280 | tf_op jit(solution)/shard_map/ppermute | solution.py:546
  54.7 3.4 %attend.1 = (bf16[4,6144]{1,0:T(4,128)(2,1)S(1)}, bf16[4,6144]{1,0:T(4,128)(2,1)S(1)}) custom-call(s32[4]{0:T(128)S(1)} %copy-done.1, bf16[2,4,1664]{2,1,0:T(4,128)(2,1)S(1)} %get-tuple-element.69.refs_0_, bf16[2,4,1664]{2,1,0:T(4,128)(2,1)S(1)} %collective-permute-done.10.refs_1_, bf16[2,4,1664]{2,1,0:T(4,128)(2,1)S(1)} %collective-permute-done.11.refs_2_, ...), custom_call_target="tpu_custom_call" | custom-call | tf_op jit(solution)/shard_map/attend/pallas_call | solution.py:350
  58.2 1.2 %collective-permute-done.14 = bf16[4,6144]{1,0:T(4,128)(2,1)S(1)} collective-permute-done((bf16[4,6144]{1,0:T(4,128)(2,1)S(1)}, bf16[4,6144]{1,0:T(4,128)(2,1)S(1)}, u32[]{:S(2)}, u32[]{:S(2)}) %collective-permute-start.14) | collective-permute-done | bytes 49184 | tf_op jit(solution)/shard_map/ppermute | solution.py:44
  59.5 0.6 collective-permute-start.15
  60.1 1.5 %collective-permute-start.16 = (bf16[8,6144]{1,0:T(8,128)(2,1)S(1)}, bf16[8,6144]{1,0:T(8,128)(2,1)S(1)}, u32[]{:S(2)}, u32[]{:S(2)}) collective-permute-start(bf16[8,6144]{1,0:T(8,128)(2,1)S(1)} %pad_maximum_fusion.refs_1_.refs_0_), channel_id=1, source_target_pairs={{0,2},{4,0},{8,4},{12,8},{14,12},{10,14},{6,10},{2,6},{1,3},{5,1},... | collective-permute-start | bytes 294920 | tf_op jit(solution)/shard_map/ppermute | solution.py:55
  61.6 2.0 %load.12.refs_10_ = bf16[768,2304]{1,0:T(8,128)(2,1)S(1)} custom-call(bf16[6144,2304]{1,0:T(8,128)(2,1)} %refs_0_.17, bf16[8,6144]{1,0:T(8,128)(2,1)S(1)} %pad_maximum_fusion.refs_1_.refs_0_), custom_call_target="tpu_custom_call" | custom-call | tf_op jit(solution)/shard_map/load/pallas_call | solution.py:103
  63.6 1.0 %collective-permute-done.15.refs_1_ = bf16[8,6144]{1,0:T(8,128)(2,1)S(1)} collective-permute-done((bf16[8,6144]{1,0:T(8,128)(2,1)S(1)}, bf16[8,6144]{1,0:T(8,128)(2,1)S(1)}, u32[]{:S(2)}, u32[]{:S(2)}) %collective-permute-start.15) | collective-permute-done | bytes 98336 | tf_op jit(solution)/shard_map/ppermute | solution.py:55
  64.7 0.3 collective-permute-start.17
  65.0 1.7 %collective-permute-start.18 = (bf16[8,6144]{1,0:T(8,128)(2,1)S(1)}, bf16[8,6144]{1,0:T(8,128)(2,1)S(1)}, u32[]{:S(2)}, u32[]{:S(2)}) collective-permute-start(bf16[8,6144]{1,0:T(8,128)(2,1)S(1)} %collective-permute-done.16.refs_2_), channel_id=1, source_target_pairs={{0,2},{4,0},{8,4},{12,8},{14,12},{10,14},{6,10},{2,6},{1,3},{5,1},... | collective-permute-start | bytes 294920 | tf_op jit(solution)/shard_map/ppermute | solution.py:55
  66.7 2.0 %load.13.refs_11_ = bf16[768,2304]{1,0:T(8,128)(2,1)S(1)} custom-call(bf16[6144,2304]{1,0:T(8,128)(2,1)} %refs_0_.17, bf16[8,6144]{1,0:T(8,128)(2,1)S(1)} %collective-permute-done.15.refs_1_, bf16[8,6144]{1,0:T(8,128)(2,1)S(1)} %collective-permute-done.16.refs_2_), custom_call_target="tpu_custom_call" | custom-call | tf_op jit(solution)/shard_map/load/pallas_call | solution.py:103
  68.7 0.6 collective-permute-done.17.refs_1_.refs_3_
  69.3 0.3 collective-permute-done.18.refs_2_.refs_4_
  69.6 1.4 %collective-permute-start.19 = (bf16[8,6144]{1,0:T(8,128)(2,1)S(1)}, bf16[8,6144]{1,0:T(8,128)(2,1)S(1)}, u32[]{:S(2)}, u32[]{:S(2)}) collective-permute-start(bf16[8,6144]{1,0:T(8,128)(2,1)S(1)} %collective-permute-done.17.refs_1_.refs_3_), channel_id=1, source_target_pairs={{0,4},{4,8},{8,12},{12,14},{14,10},{10,6},{6,2},{2,0},{1,5},{5,9},... | collective-permute-start | bytes 294920 | tf_op jit(solution)/shard_map/ppermute | solution.py:55
  71.0 0.7 collective-permute-start.20
  71.7 2.0 %load.14.refs_12_ = bf16[768,2304]{1,0:T(8,128)(2,1)S(1)} custom-call(bf16[6144,2304]{1,0:T(8,128)(2,1)} %refs_0_.17, bf16[8,6144]{1,0:T(8,128)(2,1)S(1)} %collective-permute-done.17.refs_1_.refs_3_, bf16[8,6144]{1,0:T(8,128)(2,1)S(1)} %collective-permute-done.18.refs_2_.refs_4_), custom_call_target="tpu_custom_call" | custom-call | tf_op jit(solution)/shard_map/load/pallas_call | solution.py:103
  73.7 0.6 collective-permute-done.19.refs_1_.refs_5_
  74.2 1.4 %collective-permute-done.20.refs_2_.refs_6_ = bf16[8,6144]{1,0:T(8,128)(2,1)S(1)} collective-permute-done((bf16[8,6144]{1,0:T(8,128)(2,1)S(1)}, bf16[8,6144]{1,0:T(8,128)(2,1)S(1)}, u32[]{:S(2)}, u32[]{:S(2)}) %collective-permute-start.20) | collective-permute-done | bytes 98336 | tf_op jit(solution)/shard_map/ppermute | solution.py:55
  75.6 2.3 %collective-permute-start.21 = (bf16[8,3072]{1,0:T(8,128)(2,1)S(1)}, bf16[8,3072]{1,0:T(8,128)(2,1)S(1)}, u32[]{:S(2)}, u32[]{:S(2)}) collective-permute-start(bf16[8,3072]{1,0:T(8,128)(2,1)S(1)} %slice.14), channel_id=1, source_target_pairs={{0,4},{4,8},{8,12},{12,14},{14,10},{10,6},{6,2},{2,0},{1,5},{5,9},... | collective-permute-start | bytes 147464 | tf_op jit(solution)/shard_map/ppermute | solution.py:55
  77.9 2.0 %load.15.refs_13_ = bf16[768,2304]{1,0:T(8,128)(2,1)S(1)} custom-call(bf16[6144,2304]{1,0:T(8,128)(2,1)} %refs_0_.17, bf16[8,6144]{1,0:T(8,128)(2,1)S(1)} %collective-permute-done.19.refs_1_.refs_5_, bf16[8,6144]{1,0:T(8,128)(2,1)S(1)} %collective-permute-done.20.refs_2_.refs_6_), custom_call_target="tpu_custom_call" | custom-call | tf_op jit(solution)/shard_map/load/pallas_call | solution.py:103
  79.9 2.1 %collective-permute-done.22.refs_8_ = bf16[8,3072]{1,0:T(8,128)(2,1)S(1)} collective-permute-done((bf16[8,3072]{1,0:T(8,128)(2,1)S(1)}, bf16[8,3072]{1,0:T(8,128)(2,1)S(1)}, u32[]{:S(2)}, u32[]{:S(2)}) %collective-permute-start.22) | collective-permute-done | bytes 49184 | tf_op jit(solution)/shard_map/ppermute | solution.py:55
  82.0 5.1 %output_project.1 = (f32[4,8,2304]{2,1,0:T(8,128)S(1)}, f32[4,8,2304]{2,1,0:T(8,128)S(1)}) custom-call(bf16[8,6144]{1,0:T(8,128)(2,1)S(1)} %pad_maximum_fusion.refs_1_.refs_0_, bf16[8,6144]{1,0:T(8,128)(2,1)S(1)} %collective-permute-done.15.refs_1_, bf16[8,6144]{1,0:T(8,128)(2,1)S(1)} %collective-permute-done.16.refs_2_, ...), custom_call_target="tpu_custom_call" | custom-call | tf_op jit(solution)/shard_map/output_project/pallas_call | solution.py:404
  87.1 1.6 %collective-permute-done.23 = f32[4,8,2304]{2,1,0:T(8,128)S(1)} collective-permute-done((f32[4,8,2304]{2,1,0:T(8,128)S(1)}, f32[4,8,2304]{2,1,0:T(8,128)S(1)}, u32[]{:S(2)}, u32[]{:S(2)}) %collective-permute-start.23) | collective-permute-done | bytes 294944 | tf_op jit(solution)/shard_map/ppermute | solution.py:44
  88.7 0.7 fusion
  (35 shorter events, 1.5 us)
Async XLA Ops:
  0.0 10.6 %copy-start = (bf16[8,9216]{1,0:T(8,128)(2,1)S(1)}, bf16[8,9216]{1,0:T(8,128)(2,1)}, u32[]{:S(2)}) copy-start(bf16[8,9216]{1,0:T(8,128)(2,1)} %refs_3_.1) | copy-start | bytes 442372
  0.0 7.1 %collective-permute-start = (bf16[8,9216]{1,0:T(8,128)(2,1)}, bf16[8,9216]{1,0:T(8,128)(2,1)S(1)}, u32[]{:S(2)}, u32[]{:S(2)}) collective-permute-start(bf16[8,9216]{1,0:T(8,128)(2,1)} %refs_3_.1), channel_id=1, source_target_pairs={{0,4},{4,8},{8,12},{12,14},{14,10},{10,6},{6,2},{2,0},{1,5},{5,9},... | collective-permute-start | bytes 442376 | tf_op jit(solution)/shard_map/ppermute | solution.py:55
  3.0 5.5 %collective-permute-start.1 = (bf16[8,9216]{1,0:T(8,128)(2,1)}, bf16[8,9216]{1,0:T(8,128)(2,1)S(1)}, u32[]{:S(2)}, u32[]{:S(2)}) collective-permute-start(bf16[8,9216]{1,0:T(8,128)(2,1)} %refs_3_.1), channel_id=1, source_target_pairs={{0,2},{4,0},{8,4},{12,8},{14,12},{10,14},{6,10},{2,6},{1,3},{5,1},... | collective-permute-start | bytes 442376 | tf_op jit(solution)/shard_map/ppermute | solution.py:55
  8.5 5.4 %collective-permute-start.2 = (bf16[8,9216]{1,0:T(8,128)(2,1)S(1)}, bf16[8,9216]{1,0:T(8,128)(2,1)S(1)}, u32[]{:S(2)}, u32[]{:S(2)}) collective-permute-start(bf16[8,9216]{1,0:T(8,128)(2,1)S(1)} %collective-permute-done.refs_1_.refs_4_), channel_id=1, source_target_pairs={{0,4},{4,8},{8,12},{12,14},{14,10},{10,6},{6,2},{2,0},{1,5},{5,9},... | collective-permute-start | bytes 442376 | tf_op jit(solution)/shard_map/ppermute | solution.py:55
  10.1 5.1 %collective-permute-start.3 = (bf16[8,9216]{1,0:T(8,128)(2,1)S(1)}, bf16[8,9216]{1,0:T(8,128)(2,1)S(1)}, u32[]{:S(2)}, u32[]{:S(2)}) collective-permute-start(bf16[8,9216]{1,0:T(8,128)(2,1)S(1)} %collective-permute-done.1.refs_2_.refs_5_), channel_id=1, source_target_pairs={{0,2},{4,0},{8,4},{12,8},{14,12},{10,14},{6,10},{2,6},{1,3},{5,1},... | collective-permute-start | bytes 442376 | tf_op jit(solution)/shard_map/ppermute | solution.py:55
  15.3 5.3 %collective-permute-start.4 = (bf16[8,9216]{1,0:T(8,128)(2,1)S(1)}, bf16[8,9216]{1,0:T(8,128)(2,1)S(1)}, u32[]{:S(2)}, u32[]{:S(2)}) collective-permute-start(bf16[8,9216]{1,0:T(8,128)(2,1)S(1)} %collective-permute-done.2.refs_1_.refs_6_), channel_id=1, source_target_pairs={{0,4},{4,8},{8,12},{12,14},{14,10},{10,6},{6,2},{2,0},{1,5},{5,9},... | collective-permute-start | bytes 442376 | tf_op jit(solution)/shard_map/ppermute | solution.py:55
  16.8 5.1 %collective-permute-start.5 = (bf16[8,9216]{1,0:T(8,128)(2,1)S(1)}, bf16[8,9216]{1,0:T(8,128)(2,1)S(1)}, u32[]{:S(2)}, u32[]{:S(2)}) collective-permute-start(bf16[8,9216]{1,0:T(8,128)(2,1)S(1)} %collective-permute-done.3.refs_2_.refs_7_), channel_id=1, source_target_pairs={{0,2},{4,0},{8,4},{12,8},{14,12},{10,14},{6,10},{2,6},{1,3},{5,1},... | collective-permute-start | bytes 442376 | tf_op jit(solution)/shard_map/ppermute | solution.py:55
  22.0 5.7 %collective-permute-start.6 = (bf16[8,4608]{1,0:T(8,128)(2,1)S(1)}, bf16[8,4608]{1,0:T(8,128)(2,1)S(1)}, u32[]{:S(2)}, u32[]{:S(2)}) collective-permute-start(bf16[8,4608]{1,0:T(8,128)(2,1)S(1)} %slice.12), channel_id=1, source_target_pairs={{0,4},{4,8},{8,12},{12,14},{14,10},{10,6},{6,2},{2,0},{1,5},{5,9},... | collective-permute-start | bytes 221192 | tf_op jit(solution)/shard_map/ppermute | solution.py:55
  23.9 4.5 %copy-start.2 = (bf16[9216]{0:T(1024)(128)(2,1)S(1)}, bf16[9216]{0:T(1024)(128)(2,1)}, u32[]{:S(2)}) copy-start(bf16[9216]{0:T(1024)(128)(2,1)} %param.9) | copy-start | bytes 55300
  23.9 4.4 %collective-permute-start.7 = (bf16[8,4608]{1,0:T(8,128)(2,1)S(1)}, bf16[8,4608]{1,0:T(8,128)(2,1)S(1)}, u32[]{:S(2)}, u32[]{:S(2)}) collective-permute-start(bf16[8,4608]{1,0:T(8,128)(2,1)S(1)} %slice.13), channel_id=1, source_target_pairs={{0,2},{4,0},{8,4},{12,8},{14,12},{10,14},{6,10},{2,6},{1,3},{5,1},... | collective-permute-start | bytes 221192 | tf_op jit(solution)/shard_map/ppermute | solution.py:55
  28.5 1.2 %collective-permute-start.8 = (f32[64,128]{1,0:T(8,128)S(1)}, f32[64,128]{1,0:T(8,128)S(1)}, u32[]{:S(2)}, u32[]{:S(2)}) collective-permute-start(f32[64,128]{1,0:T(8,128)S(1)} %row_sums.7.refs_0_), channel_id=1, source_target_pairs={{0,1},{1,0},{2,3},{3,2},{4,5},{5,4},{6,7},{7,6},{8,9},{9,8},{10,11... | collective-permute-start | bytes 98312 | tf_op jit(solution)/shard_map/ppermute | solution.py:44
  29.7 16.8 %copy-start.1 = (s32[4]{0:T(128)S(1)}, s32[4]{0:T(128)}, u32[]{:S(2)}) copy-start(s32[4]{0:T(128)} %lengths.1) | copy-start | bytes 52
  41.4 1.5 %collective-permute-start.9 = (f32[8,4,1664]{2,1,0:T(4,128)S(1)}, f32[8,4,1664]{2,1,0:T(4,128)S(1)}, u32[]{:S(2)}, u32[]{:S(2)}) collective-permute-start(f32[8,4,1664]{2,1,0:T(4,128)S(1)} %get-tuple-element.64), channel_id=1, source_target_pairs={{0,1},{1,0},{2,3},{3,2},{4,5},{5,4},{6,7},{7,6},{8,9},{9,8},{10,11... | collective-permute-start | bytes 638984 | tf_op jit(solution)/shard_map/ppermute | solution.py:44
  42.9 5.8 %collective-permute-start.10 = (bf16[2,4,1664]{2,1,0:T(4,128)(2,1)S(1)}, bf16[2,4,1664]{2,1,0:T(4,128)(2,1)S(1)}, u32[]{:S(2)}, u32[]{:S(2)}) collective-permute-start(bf16[2,4,1664]{2,1,0:T(4,128)(2,1)S(1)} %get-tuple-element.65.refs_0_), channel_id=1, source_target_pairs={{0,2},{2,0},{4,6},{6,4},{8,10},{10,8},{12,14},{14,12},{1,3},{3,1},... | collective-permute-start | bytes 79880 | tf_op jit(solution)/shard_map/ppermute | solution.py:546
  43.1 5.6 %collective-permute-start.11 = (bf16[2,4,1664]{2,1,0:T(4,128)(2,1)S(1)}, bf16[2,4,1664]{2,1,0:T(4,128)(2,1)S(1)}, u32[]{:S(2)}, u32[]{:S(2)}) collective-permute-start(bf16[2,4,1664]{2,1,0:T(4,128)(2,1)S(1)} %get-tuple-element.67), channel_id=1, source_target_pairs={{0,4},{2,6},{4,0},{6,2},{8,12},{10,14},{12,8},{14,10},{1,5},{3,7},... | collective-permute-start | bytes 79880 | tf_op jit(solution)/shard_map/ppermute | solution.py:546
  44.3 4.7 %collective-permute-start.12 = (bf16[2,4,1664]{2,1,0:T(4,128)(2,1)S(1)}, bf16[2,4,1664]{2,1,0:T(4,128)(2,1)S(1)}, u32[]{:S(2)}, u32[]{:S(2)}) collective-permute-start(bf16[2,4,1664]{2,1,0:T(4,128)(2,1)S(1)} %get-tuple-element.68), channel_id=1, source_target_pairs={{0,6},{2,4},{4,2},{6,0},{8,14},{10,12},{12,10},{14,8},{1,7},{3,5},... | collective-permute-start | bytes 79880 | tf_op jit(solution)/shard_map/ppermute | solution.py:546
  49.1 5.6 %collective-permute-start.13 = (bf16[4,4,1664]{2,1,0:T(4,128)(2,1)S(1)}, bf16[4,4,1664]{2,1,0:T(4,128)(2,1)S(1)}, u32[]{:S(2)}, u32[]{:S(2)}) collective-permute-start(bf16[4,4,1664]{2,1,0:T(4,128)(2,1)S(1)} %pack.1.refs_0_), channel_id=1, source_target_pairs={{0,8},{2,10},{4,12},{6,14},{8,0},{10,2},{12,4},{14,6},{1,9},{3,11}... | collective-permute-start | bytes 159752 | tf_op jit(solution)/shard_map/ppermute | solution.py:546
  58.1 1.3 %collective-permute-start.14 = (bf16[4,6144]{1,0:T(4,128)(2,1)S(1)}, bf16[4,6144]{1,0:T(4,128)(2,1)S(1)}, u32[]{:S(2)}, u32[]{:S(2)}) collective-permute-start(bf16[4,6144]{1,0:T(4,128)(2,1)S(1)} %get-tuple-element.77), channel_id=1, source_target_pairs={{0,1},{1,0},{2,3},{3,2},{4,5},{5,4},{6,7},{7,6},{8,9},{9,8},{10,11... | collective-permute-start | bytes 147464 | tf_op jit(solution)/shard_map/ppermute | solution.py:44
  59.5 5.1 %collective-permute-start.15 = (bf16[8,6144]{1,0:T(8,128)(2,1)S(1)}, bf16[8,6144]{1,0:T(8,128)(2,1)S(1)}, u32[]{:S(2)}, u32[]{:S(2)}) collective-permute-start(bf16[8,6144]{1,0:T(8,128)(2,1)S(1)} %pad_maximum_fusion.refs_1_.refs_0_), channel_id=1, source_target_pairs={{0,4},{4,8},{8,12},{12,14},{14,10},{10,6},{6,2},{2,0},{1,5},{5,9},... | collective-permute-start | bytes 294920 | tf_op jit(solution)/shard_map/ppermute | solution.py:55
  60.1 4.6 %collective-permute-start.16 = (bf16[8,6144]{1,0:T(8,128)(2,1)S(1)}, bf16[8,6144]{1,0:T(8,128)(2,1)S(1)}, u32[]{:S(2)}, u32[]{:S(2)}) collective-permute-start(bf16[8,6144]{1,0:T(8,128)(2,1)S(1)} %pad_maximum_fusion.refs_1_.refs_0_), channel_id=1, source_target_pairs={{0,2},{4,0},{8,4},{12,8},{14,12},{10,14},{6,10},{2,6},{1,3},{5,1},... | collective-permute-start | bytes 294920 | tf_op jit(solution)/shard_map/ppermute | solution.py:55
  64.7 4.6 %collective-permute-start.17 = (bf16[8,6144]{1,0:T(8,128)(2,1)S(1)}, bf16[8,6144]{1,0:T(8,128)(2,1)S(1)}, u32[]{:S(2)}, u32[]{:S(2)}) collective-permute-start(bf16[8,6144]{1,0:T(8,128)(2,1)S(1)} %collective-permute-done.15.refs_1_), channel_id=1, source_target_pairs={{0,4},{4,8},{8,12},{12,14},{14,10},{10,6},{6,2},{2,0},{1,5},{5,9},... | collective-permute-start | bytes 294920 | tf_op jit(solution)/shard_map/ppermute | solution.py:55
  65.0 4.6 %collective-permute-start.18 = (bf16[8,6144]{1,0:T(8,128)(2,1)S(1)}, bf16[8,6144]{1,0:T(8,128)(2,1)S(1)}, u32[]{:S(2)}, u32[]{:S(2)}) collective-permute-start(bf16[8,6144]{1,0:T(8,128)(2,1)S(1)} %collective-permute-done.16.refs_2_), channel_id=1, source_target_pairs={{0,2},{4,0},{8,4},{12,8},{14,12},{10,14},{6,10},{2,6},{1,3},{5,1},... | collective-permute-start | bytes 294920 | tf_op jit(solution)/shard_map/ppermute | solution.py:55
  69.6 4.6 %collective-permute-start.19 = (bf16[8,6144]{1,0:T(8,128)(2,1)S(1)}, bf16[8,6144]{1,0:T(8,128)(2,1)S(1)}, u32[]{:S(2)}, u32[]{:S(2)}) collective-permute-start(bf16[8,6144]{1,0:T(8,128)(2,1)S(1)} %collective-permute-done.17.refs_1_.refs_3_), channel_id=1, source_target_pairs={{0,4},{4,8},{8,12},{12,14},{14,10},{10,6},{6,2},{2,0},{1,5},{5,9},... | collective-permute-start | bytes 294920 | tf_op jit(solution)/shard_map/ppermute | solution.py:55
  71.0 4.6 %collective-permute-start.20 = (bf16[8,6144]{1,0:T(8,128)(2,1)S(1)}, bf16[8,6144]{1,0:T(8,128)(2,1)S(1)}, u32[]{:S(2)}, u32[]{:S(2)}) collective-permute-start(bf16[8,6144]{1,0:T(8,128)(2,1)S(1)} %collective-permute-done.18.refs_2_.refs_4_), channel_id=1, source_target_pairs={{0,2},{4,0},{8,4},{12,8},{14,12},{10,14},{6,10},{2,6},{1,3},{5,1},... | collective-permute-start | bytes 294920 | tf_op jit(solution)/shard_map/ppermute | solution.py:55
  75.6 4.3 %collective-permute-start.21 = (bf16[8,3072]{1,0:T(8,128)(2,1)S(1)}, bf16[8,3072]{1,0:T(8,128)(2,1)S(1)}, u32[]{:S(2)}, u32[]{:S(2)}) collective-permute-start(bf16[8,3072]{1,0:T(8,128)(2,1)S(1)} %slice.14), channel_id=1, source_target_pairs={{0,4},{4,8},{8,12},{12,14},{14,10},{10,6},{6,2},{2,0},{1,5},{5,9},... | collective-permute-start | bytes 147464 | tf_op jit(solution)/shard_map/ppermute | solution.py:55
  77.9 4.1 %collective-permute-start.22 = (bf16[8,3072]{1,0:T(8,128)(2,1)S(1)}, bf16[8,3072]{1,0:T(8,128)(2,1)S(1)}, u32[]{:S(2)}, u32[]{:S(2)}) collective-permute-start(bf16[8,3072]{1,0:T(8,128)(2,1)S(1)} %slice.15), channel_id=1, source_target_pairs={{0,2},{4,0},{8,4},{12,8},{14,12},{10,14},{6,10},{2,6},{1,3},{5,1},... | collective-permute-start | bytes 147464 | tf_op jit(solution)/shard_map/ppermute | solution.py:55
  87.1 1.6 %collective-permute-start.23 = (f32[4,8,2304]{2,1,0:T(8,128)S(1)}, f32[4,8,2304]{2,1,0:T(8,128)S(1)}, u32[]{:S(2)}, u32[]{:S(2)}) collective-permute-start(f32[4,8,2304]{2,1,0:T(8,128)S(1)} %get-tuple-element.92), channel_id=1, source_target_pairs={{0,1},{1,0},{2,3},{3,2},{4,5},{5,4},{6,7},{7,6},{8,9},{9,8},{10,11... | collective-permute-start | bytes 884744 | tf_op jit(solution)/shard_map/ppermute | solution.py:44

commit v12 on v11

--- a/solution.py
+++ b/solution.py
@@ -82,33 +82,23 @@
     return copies
 
 
-def load_kernel(jobs, *refs):
-    sources, target, sems = refs[: len(jobs)], refs[-2], refs[-1]
-    copies = []
-    for i, (first, size, at) in enumerate(jobs):
-        if at is None:
-            at = target.shape[0] - 2 * size
-            odd = lax.rem(lax.axis_index("gx"), 2)
-            unused = pl.ds(pl.multiple_of(at + (1 - odd) * size, size), size)
-            at = pl.multiple_of(at + odd * size, size)
-            target[unused, :] = jnp.zeros((size, target.shape[1]), target.dtype)
-        part = sources[i].at[pl.ds(first, size)]
-        copies += start_copies(part, target.at[pl.ds(at, size)], sems.at[i], 4)
-    for copy in copies:
+def load_kernel(start, source, *refs):
+    target, sems = refs[-2:]
+    part = source.at[pl.ds(start, target.shape[0])]
+    for copy in start_copies(part, target, sems, 4):
         copy.wait()
 
 
-def load(rows, jobs, after=()):
-    array = jobs[0][0]
-    return pl.pallas_call(
-        lambda *refs: load_kernel([job[1:] for job in jobs], *refs),
-        out_shape=pltpu.VMEM((rows, array.shape[1]), array.dtype),
-        in_specs=[IN_HBM] * len(jobs) + [ANY] * len(after),
+def load(array, start, size, after):
+    return pl.pallas_call(
+        lambda *refs: load_kernel(start, *refs),
+        out_shape=pltpu.VMEM((size, array.shape[1]), array.dtype),
+        in_specs=[IN_HBM] + [ANY] * len(after),
         out_specs=IN_VMEM,
-        scratch_shapes=[pltpu.SemaphoreType.DMA((len(jobs), 4))],
+        scratch_shapes=[pltpu.SemaphoreType.DMA((4,))],
         compiler_params=pltpu.CompilerParams(vmem_limit_bytes=MIB),
         name="load",
-    )(*[in_hbm(job[0]) for job in jobs], *after)
+    )(in_hbm(array), *after)
 
 
 def load_cache_kernel(source, *refs):
@@ -184,14 +174,35 @@
     sums_a, sums_b, gain = refs[:3]
     shards = refs[3 : 3 + n - 1]
     far = refs[3 + n - 1 : 3 + n + 1]
-    weights = refs[4 + n : 4 + n + parts]
-    later, keep, give, early, normed, total, sems = refs[4 + n + parts :]
-    copies = start_copies(later.at[pl.ds(0, early.shape[0])], early, sems, 4)
+    early = refs[4 + n : 4 + n + parts]
+    query_weight, keyval_weight, keep, give, late, normed, total, sems = refs[4 + n + parts :]
+    first = sum(w.shape[0] for w in early)
+    rest = query_weight.shape[0] - first
+    size = keyval_weight.shape[0]
+    odd = lax.rem(lax.axis_index("gx"), 2)
+    at = pl.multiple_of(rest + odd * size, size)
+    copies = start_copies(query_weight.at[pl.ds(first, rest)], late.at[pl.ds(0, rest)], sems.at[0], 4)
+    copies += start_copies(keyval_weight, late.at[pl.ds(at, size)], sems.at[1], 1)
+    unused = pl.ds(pl.multiple_of(rest + (1 - odd) * size, size), size)
+    late[unused, :] = jnp.zeros((size, late.shape[1]), late.dtype)
     rows, width = shards[0].shape
     sums = sums_a[...] + sums_b[...]
     row_mean = sums[:, :1] / D
     row_square = sums[:, 1:2] / D
     scale = lax.rsqrt(row_square - row_mean * row_mean + epsilon)
+
+    def multiply(weight, part, start):
+        cols = slice(part * width // 2, (part + 1) * width // 2)
+        term = lax.dot_general(
+            normed[:, cols], weight[:, cols], contract, preferred_element_type=jnp.float32
+        )
+        stripe = slice(start, start + weight.shape[0])
+        if part == 0:
+            total[:, stripe] = term
+        else:
+            total[:, stripe] += term
+        return stripe.stop
+
     for part in range(2):
         cols = slice(part * width // 2, (part + 1) * width // 2)
         for i in range(0, n, 2):
@@ -200,18 +211,13 @@
             at = slice(i * rows, (i + 2) * rows)
             x = (x - row_mean[at]) * scale[at] * gain[:, cols]
             normed[at, cols] = x.astype(jnp.bfloat16)
-        x = normed[:, cols]
         start = 0
-        for weight in weights:
-            term = lax.dot_general(
-                x, weight[:, cols], contract, preferred_element_type=jnp.float32
-            )
-            stripe = slice(start, start + weight.shape[0])
-            if part == 0:
-                total[:, stripe] = term
-            else:
-                total[:, stripe] += term
-            start = stripe.stop
+        for weight in early:
+            start = multiply(weight, part, start)
+    for copy in copies:
+        copy.wait()
+    for part in range(2):
+        multiply(late, part, first)
     side = lax.axis_index("gy")
     local = rows // 2
     for i, owner in enumerate(owners(n)):
@@ -219,34 +225,35 @@
         low, high = block[:local], block[local:]
         keep[owner] = jnp.where(side == 0, low, high)
         give[owner] = jnp.where(side == 0, high, low)
-    for copy in copies:
-        copy.wait()
-
-
-def project(sums, gain, shards, far, weights, later, size):
+
+
+def project(sums, gain, shards, far, early, query_weight, keyval_weight):
     n = len(shards) + 1
     rows, width = shards[0].shape
-    stripe = sum(w.shape[0] for w in weights)
+    stripe = query_weight.shape[0] + 2 * keyval_weight.shape[0]
+    late = stripe - sum(w.shape[0] for w in early)
     shape = jax.ShapeDtypeStruct((n, rows // 2, stripe), jnp.float32)
     return pl.pallas_call(
-        lambda *refs: project_kernel(n, len(weights), *refs),
-        out_shape=[shape, shape, pltpu.VMEM((size, later.shape[1]), later.dtype)],
-        in_specs=[IN_VMEM] * (4 + n + len(weights)) + [IN_HBM],
-        out_specs=[IN_VMEM] * 3,
+        lambda *refs: project_kernel(n, len(early), *refs),
+        out_shape=[shape, shape],
+        in_specs=[IN_VMEM] * (4 + n + len(early)) + [IN_HBM] * 2,
+        out_specs=[IN_VMEM] * 2,
         scratch_shapes=[
+            pltpu.VMEM((late, width), jnp.bfloat16),
             pltpu.VMEM((n * rows, width), jnp.bfloat16),
             pltpu.VMEM((n * rows, stripe), jnp.float32),
-            pltpu.SemaphoreType.DMA((4,)),
+            pltpu.SemaphoreType.DMA((2, 4)),
         ],
-        compiler_params=pltpu.CompilerParams(vmem_limit_bytes=6 * MIB),
+        compiler_params=pltpu.CompilerParams(vmem_limit_bytes=20 * MIB),
         name="project",
     )(
         *sums,
         gain,
         *shards,
         *far,
-        *[in_vmem(w) for w in weights],
-        in_hbm(later),
+        *[in_vmem(w) for w in early],
+        in_hbm(query_weight),
+        in_hbm(keyval_weight),
     )
 
 
@@ -287,9 +294,10 @@
 ARRIVED = [(0, 0), (1, 0), (2, 0), (3, 0), (4, 0), (4, 1), (4, 2), (4, 3)]
 
 
-def attend_kernel(lengths, *refs):
+def attend_kernel(first, lengths, *refs):
     arrived = refs[:5]
-    cosine, sine, keys, values, mine, other, spread, held = refs[5:]
+    cosine, sine, keys, values, later, mine, other, copied, spread, held, sems = refs[5:]
+    copies = start_copies(later.at[pl.ds(first, copied.shape[0])], copied, sems, 4)
     n, rows, stripe = spread.shape[1], spread.shape[0], spread.shape[2]
     me = lax.axis_index("gx")
     query_cols = stripe - 128
@@ -341,24 +349,27 @@
                     held[k, r : r + 1, at : at + DH] = part[i : i + 1]
     mine[...] = held[0].astype(jnp.bfloat16)
     other[...] = held[1].astype(jnp.bfloat16)
-
-
-def attend(lengths, arrived, cosine, sine, keys, values):
+    for copy in copies:
+        copy.wait()
+
+
+def attend(lengths, arrived, cosine, sine, keys, values, later, first, size):
     n = len(ARRIVED)
     _, rows, stripe = arrived[0].shape
     shape = jax.ShapeDtypeStruct((rows, HEADS * DH // 2), jnp.bfloat16)
     return pl.pallas_call(
-        attend_kernel,
-        out_shape=[shape, shape],
-        in_specs=[IN_SMEM] + [IN_VMEM] * 9,
-        out_specs=[IN_VMEM] * 2,
+        lambda *refs: attend_kernel(first, *refs),
+        out_shape=[shape, shape, pltpu.VMEM((size, later.shape[1]), later.dtype)],
+        in_specs=[IN_SMEM] + [IN_VMEM] * 9 + [IN_HBM],
+        out_specs=[IN_VMEM] * 3,
         scratch_shapes=[
             pltpu.VMEM((rows, n, stripe), jnp.float32),
             pltpu.VMEM((2, rows, HEADS * DH // 2), jnp.float32),
+            pltpu.SemaphoreType.DMA((4,)),
         ],
         compiler_params=pltpu.CompilerParams(vmem_limit_bytes=8 * MIB),
         name="attend",
-    )(lengths, *arrived, cosine, sine, in_vmem(keys), in_vmem(values))
+    )(lengths, *arrived, cosine, sine, in_vmem(keys), in_vmem(values), in_hbm(later))
 
 
 def output_kernel(n, *refs):
@@ -377,13 +388,14 @@
         first = 0
         for weight in weights:
             last = first + weight.shape[0]
-            if start <= first and last <= start + half:
+            low, high = max(first, start), min(last, start + half)
+            if low < high:
                 term = jnp.dot(
-                    x[:, first - start : last - start],
-                    weight[...],
+                    x[:, low - start : high - start],
+                    weight[low - first : high - first, :],
                     preferred_element_type=jnp.float32,
                 )
-                if first == 0:
+                if low == 0:
                     total[...] = term
                 else:
                     total[...] += term
@@ -503,17 +515,13 @@
     n = lax.axis_size("gx")
     ring = Ring(n)
     query_cols, width = query_weight.shape
-    new_cols = keyval_weight.shape[0]
-    piece = query_cols // 4
+    piece = query_cols // 6
     weights = []
 
     indices = jnp.arange(DH // 2, dtype=jnp.float32)
     frequency = jnp.exp(-math.log(10000.0) * indices / (DH // 2))
     angles = cache_lengths.astype(jnp.float32)[:, None] * frequency
     cosine, sine = jnp.cos(angles), jnp.sin(angles)
-
-    def piece_of(array, start, size, after):
-        return load(size, [(array, start, size, 0)], after)
 
     left = right = activations
     shards = [activations]
@@ -523,24 +531,21 @@
         left, right = ring.step(left, right)
         if step > 1:
             sums = [row_sums([activations, *arrived] if step == 2 else arrived, sums)]
-        weight = piece_of(query_weight, (step - 1) * piece, piece, arrived)
+        weight = load(query_weight, (step - 1) * piece, piece, arrived)
         weight, (left, right, *sums) = before(weight, left, right, *sums)
         weights.append(weight)
         shards += [left, right]
     far = ring.step(left[:, : width // 2], right[:, width // 2 :])
     sums = row_sums([left, right], sums)
-    jobs = [(query_weight, 3 * piece, piece, 0), (keyval_weight, 0, new_cols, None)]
-    weight = load(piece + 2 * new_cols, jobs, [left, right])
+    weight = load(query_weight, 3 * piece, piece, [left, right])
     weight, far = before(weight, *far)
     sums = row_sums([], [sums], far)
     other_sums = swap_pair(sums)
     weights.append(weight)
     gain = norm_gain.astype(jnp.float32)[None, :]
-    piece = output_weight.shape[0] // 4
-    keep, give, weight = project(
-        (sums, other_sums), gain, shards, far, weights, output_weight, 2 * piece
-    )
-    weights = [weight]
+    keep, give = project(
+        (sums, other_sums), gain, shards, far, weights, query_weight, keyval_weight
+    )
 
     def exchange(blocks, d):
         return lax.ppermute(blocks, "gx", [(i, i ^ d) for i in range(n)])
@@ -552,26 +557,31 @@
     across = pack([(0, 1), (1, 1), (2, 1), (3, 1)], *arrived)
     last = exchange(across, 4)
     values = load_cache(cache_values, [across])
+    unit = output_weight.shape[0] // 48
+    sizes = [8 * unit, 12 * unit] + [7 * unit] * 4
+    starts = [sum(sizes[:i]) for i in range(len(sizes))]
+    weight = load(output_weight, starts[0], sizes[0], [across])
     values, (last,) = before(values, last)
+    weight, (last,) = before(weight, last)
     arrived = [*arrived, last]
-    mine, other = attend(cache_lengths, arrived, cosine, sine, keys, values)
+    mine, other, copied = attend(
+        cache_lengths, arrived, cosine, sine, keys, values, output_weight, starts[1], sizes[1]
+    )
+    weights = [weight, copied]
     shard = jnp.concatenate([mine, swap_pair(other)], axis=0)
 
     left = right = shard
     shards = [shard]
-    done = 2 * piece
-    piece = piece // 2
-
     for step in range(1, n // 2):
         arrived = shards[-2:]
         left, right = ring.step(left, right)
-        weight = piece_of(output_weight, done + (step - 1) * piece, piece, arrived)
+        weight = load(output_weight, starts[1 + step], sizes[1 + step], arrived)
         weight, (left, right) = before(weight, left, right)
         weights.append(weight)
         shards += [left, right]
     half = shard.shape[1] // 2
     far = ring.step(left[:, :half], right[:, half:])
-    weight = piece_of(output_weight, done + 3 * piece, piece, [left, right])
+    weight = load(output_weight, starts[-1], sizes[-1], [left, right])
     weight, far = before(weight, *far)
     weights.append(weight)
     keep, give = output_project(shards, far, weights)

time: 89.6 us -> 93.1 us (1.039)
  Pallas kernels: 46 us -> 48.7 us
  starting transfers between devices: 22 us -> 23.9 us
  waiting for transfers between devices: 20.2 us -> 19.2 us
    ppermute x8, starting transfers between devices: 12.7 us -> 8.82 us  [step(): lax.ppermute(left, 'gx', self.onward)]
    ppermute x8, starting transfers between devices: 4.93 us -> 8.59 us  [step(): lax.ppermute(right, 'gx', self.back)]
    pallas_call x10 -> x11, Pallas kernels: 35.8 us -> 38.6 us  [the longest x9 20.6 us: load(): pl.pallas_call(lambda *refs: load_kernel(start, *refs), out_shape=pltpu.V...]
    ppermute x4, starting transfers between devices: 4.03 us -> 6.14 us  [exchange(): return lax.ppermute(blocks, 'gx', [(i, i ^ d) for i in range(n)])]
    ppermute x4, waiting for transfers between devices: 3.13 us -> 1.21 us  [exchange(): return lax.ppermute(blocks, 'gx', [(i, i ^ d) for i in range(n)])]
    ppermute x8, waiting for transfers between devices: 3.16 us -> 4.57 us  [step(): lax.ppermute(left, 'gx', self.onward)]
  transfers between devices with their start and end apart: 24 -> 24, of which waited for: 18 -> 20; matrix products, arithmetic and copies ran while one was open for 0% -> 0% of each run, Pallas kernels for 29% -> 28%
where the time goes in v12:
time: 93.1 us; the launch traced here: 92.9 us
  Pallas kernels  48.7 us (52%)
  starting transfers between devices  23.9 us (26%)
  waiting for transfers between devices  19.2 us (21%)
    pallas_call x9, Pallas kernels, load(): pl.pallas_call(lambda *refs: load_kernel(start, *refs), out_shape=pltpu.V...  20.6 us
    pallas_call x1, Pallas kernels, project(): pl.pallas_call(lambda *refs: project_kernel(n, len(early), *refs), out_sh...  12 us
    ppermute x8, starting transfers between devices, step(): lax.ppermute(left, 'gx', self.onward)  8.82 us
    ppermute x8, starting transfers between devices, step(): lax.ppermute(right, 'gx', self.back)  8.59 us
    ppermute x8, waiting for transfers between devices, step(): lax.ppermute(right, 'gx', self.back)  8.14 us
    ppermute x4, starting transfers between devices, exchange(): return lax.ppermute(blocks, 'gx', [(i, i ^ d) for i in range(n)])  6.14 us
    pallas_call x1, Pallas kernels, attend(): pl.pallas_call(lambda *refs: attend_kernel(first, *refs), out_shape=[shap...  5.99 us
    ppermute x4, waiting for transfers between devices, swap_pair(): return lax.ppermute(x, 'gy', [(0, 1), (1, 0)])  5.27 us
  transfers between devices with their start and end apart: 24, of which 20 were waited for; matrix products, arithmetic and copies ran while one was open for 0% of the time, Pallas kernels for 28%

profile of v12, /device:TPU:0, one launch (start us, length us, event | category | flops | bytes accessed | tf_op | source)
XLA Modules:
  0.0 92.9 jit_solution(18306643255808642704)
XLA Ops:
  0.0 3.0 %collective-permute-start.1 = (bf16[8,9216]{1,0:T(8,128)(2,1)}, bf16[8,9216]{1,0:T(8,128)(2,1)S(1)}, u32[]{:S(2)}, u32[]{:S(2)}) collective-permute-start(bf16[8,9216]{1,0:T(8,128)(2,1)} %refs_3_.1), channel_id=1, source_target_pairs={{0,2},{4,0},{8,4},{12,8},{14,12},{10,14},{6,10},{2,6},{1,3},{5,1},... | collective-permute-start | bytes 442376 | tf_op jit(solution)/shard_map/ppermute | solution.py:55
  3.1 2.4 %load.9.refs_12_ = bf16[256,9216]{1,0:T(8,128)(2,1)S(1)} custom-call(bf16[1536,9216]{1,0:T(8,128)(2,1)} %refs_16_.1), custom_call_target="tpu_custom_call" | custom-call | tf_op jit(solution)/shard_map/load/pallas_call | solution.py:93
  5.5 1.7 %collective-permute-done.1.refs_2_.refs_5_ = bf16[8,9216]{1,0:T(8,128)(2,1)S(1)} collective-permute-done((bf16[8,9216]{1,0:T(8,128)(2,1)}, bf16[8,9216]{1,0:T(8,128)(2,1)S(1)}, u32[]{:S(2)}, u32[]{:S(2)}) %collective-permute-start.1) | collective-permute-done | bytes 147488 | tf_op jit(solution)/shard_map/ppermute | solution.py:55
  7.2 1.3 %collective-permute-done.refs_1_.refs_4_ = bf16[8,9216]{1,0:T(8,128)(2,1)S(1)} collective-permute-done((bf16[8,9216]{1,0:T(8,128)(2,1)}, bf16[8,9216]{1,0:T(8,128)(2,1)S(1)}, u32[]{:S(2)}, u32[]{:S(2)}) %collective-permute-start) | collective-permute-done | bytes 147488 | tf_op jit(solution)/shard_map/ppermute | solution.py:55
  8.9 1.6 %collective-permute-start.3 = (bf16[8,9216]{1,0:T(8,128)(2,1)S(1)}, bf16[8,9216]{1,0:T(8,128)(2,1)S(1)}, u32[]{:S(2)}, u32[]{:S(2)}) collective-permute-start(bf16[8,9216]{1,0:T(8,128)(2,1)S(1)} %collective-permute-done.1.refs_2_.refs_5_), channel_id=1, source_target_pairs={{0,2},{4,0},{8,4},{12,8},{14,12},{10,14},{6,10},{2,6},{1,3},{5,1},... | collective-permute-start | bytes 442376 | tf_op jit(solution)/shard_map/ppermute | solution.py:55
  10.7 2.4 %load.10.refs_13_ = bf16[256,9216]{1,0:T(8,128)(2,1)S(1)} custom-call(bf16[1536,9216]{1,0:T(8,128)(2,1)} %refs_16_.1, bf16[8,9216]{1,0:T(8,128)(2,1)S(1)} %collective-permute-done.refs_1_.refs_4_, bf16[8,9216]{1,0:T(8,128)(2,1)S(1)} %collective-permute-done.1.refs_2_.refs_5_), custom_call_target="tpu_custom_call" | custom-call | tf_op jit(solution)/shard_map/load/pallas_call | solution.py:93
  13.1 0.5 collective-permute-done.2.refs_1_.refs_6_
  14.0 1.7 %collective-permute-start.4 = (bf16[8,9216]{1,0:T(8,128)(2,1)S(1)}, bf16[8,9216]{1,0:T(8,128)(2,1)S(1)}, u32[]{:S(2)}, u32[]{:S(2)}) collective-permute-start(bf16[8,9216]{1,0:T(8,128)(2,1)S(1)} %collective-permute-done.2.refs_1_.refs_6_), channel_id=1, source_target_pairs={{0,4},{4,8},{8,12},{12,14},{14,10},{10,6},{6,2},{2,0},{1,5},{5,9},... | collective-permute-start | bytes 442376 | tf_op jit(solution)/shard_map/ppermute | solution.py:55
  16.0 2.4 %load.11.refs_14_ = bf16[256,9216]{1,0:T(8,128)(2,1)S(1)} custom-call(bf16[1536,9216]{1,0:T(8,128)(2,1)} %refs_16_.1, bf16[8,9216]{1,0:T(8,128)(2,1)S(1)} %collective-permute-done.2.refs_1_.refs_6_, bf16[8,9216]{1,0:T(8,128)(2,1)S(1)} %collective-permute-done.3.refs_2_.refs_7_), custom_call_target="tpu_custom_call" | custom-call | tf_op jit(solution)/shard_map/load/pallas_call | solution.py:93
  18.6 0.6 collective-permute-done.4.refs_1_.refs_8_
  19.2 2.5 %collective-permute-done.5.refs_2_.refs_9_ = bf16[8,9216]{1,0:T(8,128)(2,1)S(1)} collective-permute-done((bf16[8,9216]{1,0:T(8,128)(2,1)S(1)}, bf16[8,9216]{1,0:T(8,128)(2,1)S(1)}, u32[]{:S(2)}, u32[]{:S(2)}) %collective-permute-start.5) | collective-permute-done | bytes 147488 | tf_op jit(solution)/shard_map/ppermute | solution.py:55
  22.1 1.7 %collective-permute-start.6 = (bf16[8,4608]{1,0:T(8,128)(2,1)S(1)}, bf16[8,4608]{1,0:T(8,128)(2,1)S(1)}, u32[]{:S(2)}, u32[]{:S(2)}) collective-permute-start(bf16[8,4608]{1,0:T(8,128)(2,1)S(1)} %slice.12), channel_id=1, source_target_pairs={{0,4},{4,8},{8,12},{12,14},{14,10},{10,6},{6,2},{2,0},{1,5},{5,9},... | collective-permute-start | bytes 221192 | tf_op jit(solution)/shard_map/ppermute | solution.py:55
  23.8 2.4 %load.12.refs_15_ = bf16[256,9216]{1,0:T(8,128)(2,1)S(1)} custom-call(bf16[1536,9216]{1,0:T(8,128)(2,1)} %refs_16_.1, bf16[8,9216]{1,0:T(8,128)(2,1)S(1)} %collective-permute-done.4.refs_1_.refs_8_, bf16[8,9216]{1,0:T(8,128)(2,1)S(1)} %collective-permute-done.5.refs_2_.refs_9_), custom_call_target="tpu_custom_call" | custom-call | tf_op jit(solution)/shard_map/load/pallas_call | solution.py:93
  26.6 1.2 %collective-permute-done.8.refs_1_ = f32[64,128]{1,0:T(8,128)S(1)} collective-permute-done((f32[64,128]{1,0:T(8,128)S(1)}, f32[64,128]{1,0:T(8,128)S(1)}, u32[]{:S(2)}, u32[]{:S(2)}) %collective-permute-start.8) | collective-permute-done | bytes 32800 | tf_op jit(solution)/shard_map/ppermute | solution.py:44
  27.8 12.0 %project.1 = (f32[8,4,1664]{2,1,0:T(4,128)S(1)}, f32[8,4,1664]{2,1,0:T(4,128)S(1)}) custom-call(f32[64,128]{1,0:T(8,128)S(1)} %row_sums.7.refs_0_, f32[64,128]{1,0:T(8,128)S(1)} %collective-permute-done.8.refs_1_, f32[1,9216]{1,0:T(1,128)S(1)} %bitcast.3, bf16[8,9216]{1,0:T(8,128)(2,1)S(1)} %copy-done, ...), custom_call_target="tpu_custom_call" | custom-call | tf_op jit(solution)/shard_map/project/pallas_call | solution.py:236
  40.0 1.3 %collective-permute-done.9.got = f32[8,4,1664]{2,1,0:T(4,128)S(1)} collective-permute-done((f32[8,4,1664]{2,1,0:T(4,128)S(1)}, f32[8,4,1664]{2,1,0:T(4,128)S(1)}, u32[]{:S(2)}, u32[]{:S(2)}) %collective-permute-start.9) | collective-permute-done | bytes 213024 | tf_op jit(solution)/shard_map/ppermute | solution.py:44
  41.3 1.8 %collective-permute-start.11 = (bf16[2,4,1664]{2,1,0:T(4,128)(2,1)S(1)}, bf16[2,4,1664]{2,1,0:T(4,128)(2,1)S(1)}, u32[]{:S(2)}, u32[]{:S(2)}) collective-permute-start(bf16[2,4,1664]{2,1,0:T(4,128)(2,1)S(1)} %get-tuple-element.69), channel_id=1, source_target_pairs={{0,4},{2,6},{4,0},{6,2},{8,12},{10,14},{12,8},{14,10},{1,5},{3,7},... | collective-permute-start | bytes 79880 | tf_op jit(solution)/shard_map/ppermute | solution.py:551
  43.1 1.4 %collective-permute-start.12 = (bf16[2,4,1664]{2,1,0:T(4,128)(2,1)S(1)}, bf16[2,4,1664]{2,1,0:T(4,128)(2,1)S(1)}, u32[]{:S(2)}, u32[]{:S(2)}) collective-permute-start(bf16[2,4,1664]{2,1,0:T(4,128)(2,1)S(1)} %get-tuple-element.70), channel_id=1, source_target_pairs={{0,6},{2,4},{4,2},{6,0},{8,14},{10,12},{12,10},{14,8},{1,7},{3,5},... | collective-permute-start | bytes 79880 | tf_op jit(solution)/shard_map/ppermute | solution.py:551
  44.9 2.2 %load_cache.2.refs_8_ = bf16[4,2048,256]{2,1,0:T(8,128)(2,1)S(1)} custom-call(bf16[4,2048,256]{2,1,0:T(8,128)(2,1)} %source.2, bf16[2,4,1664]{2,1,0:T(4,128)(2,1)S(1)} %get-tuple-element.67.refs_0_), custom_call_target="tpu_custom_call" | custom-call | tf_op jit(solution)/shard_map/load_cache/pallas_call | solution.py:115
  47.1 0.7 collective-permute-done.12.refs_3_.refs_4_
  47.8 0.5 collective-permute-done.10.refs_1_.refs_2_
  48.3 2.6 %collective-permute-start.13 = (bf16[4,4,1664]{2,1,0:T(4,128)(2,1)S(1)}, bf16[4,4,1664]{2,1,0:T(4,128)(2,1)S(1)}, u32[]{:S(2)}, u32[]{:S(2)}) collective-permute-start(bf16[4,4,1664]{2,1,0:T(4,128)(2,1)S(1)} %pack.1.refs_1_.refs_0_), channel_id=1, source_target_pairs={{0,8},{2,10},{4,12},{6,14},{8,0},{10,2},{12,4},{14,6},{1,9},{3,11}... | collective-permute-start | bytes 159752 | tf_op jit(solution)/shard_map/ppermute | solution.py:551
  51.0 2.2 %load_cache.3.refs_9_ = bf16[4,2048,256]{2,1,0:T(8,128)(2,1)S(1)} custom-call(bf16[4,2048,256]{2,1,0:T(8,128)(2,1)} %source.3, bf16[4,4,1664]{2,1,0:T(4,128)(2,1)S(1)} %pack.1.refs_1_.refs_0_), custom_call_target="tpu_custom_call" | custom-call | tf_op jit(solution)/shard_map/load_cache/pallas_call | solution.py:115
  53.3 2.4 %load.13.refs_9_ = bf16[1024,2304]{1,0:T(8,128)(2,1)S(1)} custom-call(bf16[6144,2304]{1,0:T(8,128)(2,1)} %refs_0_.21, bf16[4,4,1664]{2,1,0:T(4,128)(2,1)S(1)} %pack.1.refs_1_.refs_0_), custom_call_target="tpu_custom_call" | custom-call | tf_op jit(solution)/shard_map/load/pallas_call | solution.py:93
  55.6 6.0 %attend.1 = (bf16[4,6144]{1,0:T(4,128)(2,1)S(1)}, bf16[4,6144]{1,0:T(4,128)(2,1)S(1)}, bf16[1536,2304]{1,0:T(8,128)(2,1)S(1)}) custom-call(s32[4]{0:T(128)S(1)} %copy-done.1, bf16[2,4,1664]{2,1,0:T(4,128)(2,1)S(1)} %get-tuple-element.71.refs_0_.refs_1_, bf16[2,4,1664]{2,1,0:T(4,128)(2,1)S(1)} %collective-permute-done.10.refs_1_.refs_2_, ...), custom_call_target="tpu_custom_call" | custom-call | tf_op jit(solution)/shard_map/attend/pallas_call | solution.py:360
  61.7 1.2 %collective-permute-done.14 = bf16[4,6144]{1,0:T(4,128)(2,1)S(1)} collective-permute-done((bf16[4,6144]{1,0:T(4,128)(2,1)S(1)}, bf16[4,6144]{1,0:T(4,128)(2,1)S(1)}, u32[]{:S(2)}, u32[]{:S(2)}) %collective-permute-start.14) | collective-permute-done | bytes 49184 | tf_op jit(solution)/shard_map/ppermute | solution.py:44
  63.0 1.1 %collective-permute-start.16 = (bf16[8,6144]{1,0:T(8,128)(2,1)S(1)}, bf16[8,6144]{1,0:T(8,128)(2,1)S(1)}, u32[]{:S(2)}, u32[]{:S(2)}) collective-permute-start(bf16[8,6144]{1,0:T(8,128)(2,1)S(1)} %pad_maximum_fusion.refs_1_.refs_0_), channel_id=1, source_target_pairs={{0,2},{4,0},{8,4},{12,8},{14,12},{10,14},{6,10},{2,6},{1,3},{5,1},... | collective-permute-start | bytes 294920 | tf_op jit(solution)/shard_map/ppermute | solution.py:55
  64.1 0.9 %collective-permute-start.15 = (bf16[8,6144]{1,0:T(8,128)(2,1)S(1)}, bf16[8,6144]{1,0:T(8,128)(2,1)S(1)}, u32[]{:S(2)}, u32[]{:S(2)}) collective-permute-start(bf16[8,6144]{1,0:T(8,128)(2,1)S(1)} %pad_maximum_fusion.refs_1_.refs_0_), channel_id=1, source_target_pairs={{0,4},{4,8},{8,12},{12,14},{14,10},{10,6},{6,2},{2,0},{1,5},{5,9},... | collective-permute-start | bytes 294920 | tf_op jit(solution)/shard_map/ppermute | solution.py:55
  65.1 2.2 %load.14.refs_11_ = bf16[896,2304]{1,0:T(8,128)(2,1)S(1)} custom-call(bf16[6144,2304]{1,0:T(8,128)(2,1)} %refs_0_.21, bf16[8,6144]{1,0:T(8,128)(2,1)S(1)} %pad_maximum_fusion.refs_1_.refs_0_), custom_call_target="tpu_custom_call" | custom-call | tf_op jit(solution)/shard_map/load/pallas_call | solution.py:93
  67.3 0.6 collective-permute-done.16.refs_2_
  67.9 0.8 collective-permute-done.15.refs_1_
  68.8 0.9 %collective-permute-start.17 = (bf16[8,6144]{1,0:T(8,128)(2,1)S(1)}, bf16[8,6144]{1,0:T(8,128)(2,1)S(1)}, u32[]{:S(2)}, u32[]{:S(2)}) collective-permute-start(bf16[8,6144]{1,0:T(8,128)(2,1)S(1)} %collective-permute-done.15.refs_1_), channel_id=1, source_target_pairs={{0,4},{4,8},{8,12},{12,14},{14,10},{10,6},{6,2},{2,0},{1,5},{5,9},... | collective-permute-start | bytes 294920 | tf_op jit(solution)/shard_map/ppermute | solution.py:55
  69.7 1.1 %collective-permute-start.18 = (bf16[8,6144]{1,0:T(8,128)(2,1)S(1)}, bf16[8,6144]{1,0:T(8,128)(2,1)S(1)}, u32[]{:S(2)}, u32[]{:S(2)}) collective-permute-start(bf16[8,6144]{1,0:T(8,128)(2,1)S(1)} %collective-permute-done.16.refs_2_), channel_id=1, source_target_pairs={{0,2},{4,0},{8,4},{12,8},{14,12},{10,14},{6,10},{2,6},{1,3},{5,1},... | collective-permute-start | bytes 294920 | tf_op jit(solution)/shard_map/ppermute | solution.py:55
  70.8 2.2 %load.15.refs_12_ = bf16[896,2304]{1,0:T(8,128)(2,1)S(1)} custom-call(bf16[6144,2304]{1,0:T(8,128)(2,1)} %refs_0_.21, bf16[8,6144]{1,0:T(8,128)(2,1)S(1)} %collective-permute-done.15.refs_1_, bf16[8,6144]{1,0:T(8,128)(2,1)S(1)} %collective-permute-done.16.refs_2_), custom_call_target="tpu_custom_call" | custom-call | tf_op jit(solution)/shard_map/load/pallas_call | solution.py:93
  73.0 0.4 collective-permute-done.17.refs_1_.refs_3_
  73.4 0.9 %collective-permute-done.18.refs_2_.refs_4_ = bf16[8,6144]{1,0:T(8,128)(2,1)S(1)} collective-permute-done((bf16[8,6144]{1,0:T(8,128)(2,1)S(1)}, bf16[8,6144]{1,0:T(8,128)(2,1)S(1)}, u32[]{:S(2)}, u32[]{:S(2)}) %collective-permute-start.18) | collective-permute-done | bytes 98336 | tf_op jit(solution)/shard_map/ppermute | solution.py:55
  74.3 1.6 %collective-permute-start.19 = (bf16[8,6144]{1,0:T(8,128)(2,1)S(1)}, bf16[8,6144]{1,0:T(8,128)(2,1)S(1)}, u32[]{:S(2)}, u32[]{:S(2)}) collective-permute-start(bf16[8,6144]{1,0:T(8,128)(2,1)S(1)} %collective-permute-done.17.refs_1_.refs_3_), channel_id=1, source_target_pairs={{0,4},{4,8},{8,12},{12,14},{14,10},{10,6},{6,2},{2,0},{1,5},{5,9},... | collective-permute-start | bytes 294920 | tf_op jit(solution)/shard_map/ppermute | solution.py:55
  75.9 0.4 collective-permute-start.20
  76.3 2.2 %load.16.refs_13_ = bf16[896,2304]{1,0:T(8,128)(2,1)S(1)} custom-call(bf16[6144,2304]{1,0:T(8,128)(2,1)} %refs_0_.21, bf16[8,6144]{1,0:T(8,128)(2,1)S(1)} %collective-permute-done.17.refs_1_.refs_3_, bf16[8,6144]{1,0:T(8,128)(2,1)S(1)} %collective-permute-done.18.refs_2_.refs_4_), custom_call_target="tpu_custom_call" | custom-call | tf_op jit(solution)/shard_map/load/pallas_call | solution.py:93
  78.5 0.4 collective-permute-done.19.refs_1_.refs_5_
  78.9 2.0 %collective-permute-done.20.refs_2_.refs_6_ = bf16[8,6144]{1,0:T(8,128)(2,1)S(1)} collective-permute-done((bf16[8,6144]{1,0:T(8,128)(2,1)S(1)}, bf16[8,6144]{1,0:T(8,128)(2,1)S(1)}, u32[]{:S(2)}, u32[]{:S(2)}) %collective-permute-start.20) | collective-permute-done | bytes 98336 | tf_op jit(solution)/shard_map/ppermute | solution.py:55
  80.9 0.6 collective-permute-start.22
  81.5 1.5 %collective-permute-start.21 = (bf16[8,3072]{1,0:T(8,128)(2,1)S(1)}, bf16[8,3072]{1,0:T(8,128)(2,1)S(1)}, u32[]{:S(2)}, u32[]{:S(2)}) collective-permute-start(bf16[8,3072]{1,0:T(8,128)(2,1)S(1)} %slice.14), channel_id=1, source_target_pairs={{0,4},{4,8},{8,12},{12,14},{14,10},{10,6},{6,2},{2,0},{1,5},{5,9},... | collective-permute-start | bytes 147464 | tf_op jit(solution)/shard_map/ppermute | solution.py:55
  83.0 2.2 %load.17.refs_14_ = bf16[896,2304]{1,0:T(8,128)(2,1)S(1)} custom-call(bf16[6144,2304]{1,0:T(8,128)(2,1)} %refs_0_.21, bf16[8,6144]{1,0:T(8,128)(2,1)S(1)} %collective-permute-done.19.refs_1_.refs_5_, bf16[8,6144]{1,0:T(8,128)(2,1)S(1)} %collective-permute-done.20.refs_2_.refs_6_), custom_call_target="tpu_custom_call" | custom-call | tf_op jit(solution)/shard_map/load/pallas_call | solution.py:93
  85.2 0.4 collective-permute-done.21.refs_7_
  85.6 4.9 %output_project.1 = (f32[4,8,2304]{2,1,0:T(8,128)S(1)}, f32[4,8,2304]{2,1,0:T(8,128)S(1)}) custom-call(bf16[8,6144]{1,0:T(8,128)(2,1)S(1)} %pad_maximum_fusion.refs_1_.refs_0_, bf16[8,6144]{1,0:T(8,128)(2,1)S(1)} %collective-permute-done.15.refs_1_, bf16[8,6144]{1,0:T(8,128)(2,1)S(1)} %collective-permute-done.16.refs_2_, ...), custom_call_target="tpu_custom_call" | custom-call | tf_op jit(solution)/shard_map/output_project/pallas_call | solution.py:416
  90.7 1.6 %collective-permute-done.23 = f32[4,8,2304]{2,1,0:T(8,128)S(1)} collective-permute-done((f32[4,8,2304]{2,1,0:T(8,128)S(1)}, f32[4,8,2304]{2,1,0:T(8,128)S(1)}, u32[]{:S(2)}, u32[]{:S(2)}) %collective-permute-start.23) | collective-permute-done | bytes 294944 | tf_op jit(solution)/shard_map/ppermute | solution.py:44
  92.2 0.7 fusion
  (36 shorter events, 3.4 us)
Async XLA Ops:
  0.0 10.5 %copy-start = (bf16[8,9216]{1,0:T(8,128)(2,1)S(1)}, bf16[8,9216]{1,0:T(8,128)(2,1)}, u32[]{:S(2)}) copy-start(bf16[8,9216]{1,0:T(8,128)(2,1)} %refs_3_.1) | copy-start | bytes 442372
  0.0 7.2 %collective-permute-start.1 = (bf16[8,9216]{1,0:T(8,128)(2,1)}, bf16[8,9216]{1,0:T(8,128)(2,1)S(1)}, u32[]{:S(2)}, u32[]{:S(2)}) collective-permute-start(bf16[8,9216]{1,0:T(8,128)(2,1)} %refs_3_.1), channel_id=1, source_target_pairs={{0,2},{4,0},{8,4},{12,8},{14,12},{10,14},{6,10},{2,6},{1,3},{5,1},... | collective-permute-start | bytes 442376 | tf_op jit(solution)/shard_map/ppermute | solution.py:55
  3.0 5.5 %collective-permute-start = (bf16[8,9216]{1,0:T(8,128)(2,1)}, bf16[8,9216]{1,0:T(8,128)(2,1)S(1)}, u32[]{:S(2)}, u32[]{:S(2)}) collective-permute-start(bf16[8,9216]{1,0:T(8,128)(2,1)} %refs_3_.1), channel_id=1, source_target_pairs={{0,4},{4,8},{8,12},{12,14},{14,10},{10,6},{6,2},{2,0},{1,5},{5,9},... | collective-permute-start | bytes 442376 | tf_op jit(solution)/shard_map/ppermute | solution.py:55
  8.5 5.1 %collective-permute-start.2 = (bf16[8,9216]{1,0:T(8,128)(2,1)S(1)}, bf16[8,9216]{1,0:T(8,128)(2,1)S(1)}, u32[]{:S(2)}, u32[]{:S(2)}) collective-permute-start(bf16[8,9216]{1,0:T(8,128)(2,1)S(1)} %collective-permute-done.refs_1_.refs_4_), channel_id=1, source_target_pairs={{0,4},{4,8},{8,12},{12,14},{14,10},{10,6},{6,2},{2,0},{1,5},{5,9},... | collective-permute-start | bytes 442376 | tf_op jit(solution)/shard_map/ppermute | solution.py:55
  8.9 5.1 %collective-permute-start.3 = (bf16[8,9216]{1,0:T(8,128)(2,1)S(1)}, bf16[8,9216]{1,0:T(8,128)(2,1)S(1)}, u32[]{:S(2)}, u32[]{:S(2)}) collective-permute-start(bf16[8,9216]{1,0:T(8,128)(2,1)S(1)} %collective-permute-done.1.refs_2_.refs_5_), channel_id=1, source_target_pairs={{0,2},{4,0},{8,4},{12,8},{14,12},{10,14},{6,10},{2,6},{1,3},{5,1},... | collective-permute-start | bytes 442376 | tf_op jit(solution)/shard_map/ppermute | solution.py:55
  14.0 5.1 %collective-permute-start.4 = (bf16[8,9216]{1,0:T(8,128)(2,1)S(1)}, bf16[8,9216]{1,0:T(8,128)(2,1)S(1)}, u32[]{:S(2)}, u32[]{:S(2)}) collective-permute-start(bf16[8,9216]{1,0:T(8,128)(2,1)S(1)} %collective-permute-done.2.refs_1_.refs_6_), channel_id=1, source_target_pairs={{0,4},{4,8},{8,12},{12,14},{14,10},{10,6},{6,2},{2,0},{1,5},{5,9},... | collective-permute-start | bytes 442376 | tf_op jit(solution)/shard_map/ppermute | solution.py:55
  15.7 5.9 %collective-permute-start.5 = (bf16[8,9216]{1,0:T(8,128)(2,1)S(1)}, bf16[8,9216]{1,0:T(8,128)(2,1)S(1)}, u32[]{:S(2)}, u32[]{:S(2)}) collective-permute-start(bf16[8,9216]{1,0:T(8,128)(2,1)S(1)} %collective-permute-done.3.refs_2_.refs_7_), channel_id=1, source_target_pairs={{0,2},{4,0},{8,4},{12,8},{14,12},{10,14},{6,10},{2,6},{1,3},{5,1},... | collective-permute-start | bytes 442376 | tf_op jit(solution)/shard_map/ppermute | solution.py:55
  21.7 4.9 %copy-start.2 = (bf16[9216]{0:T(1024)(128)(2,1)S(1)}, bf16[9216]{0:T(1024)(128)(2,1)}, u32[]{:S(2)}) copy-start(bf16[9216]{0:T(1024)(128)(2,1)} %param.9) | copy-start | bytes 55300
  21.7 4.6 %collective-permute-start.7 = (bf16[8,4608]{1,0:T(8,128)(2,1)S(1)}, bf16[8,4608]{1,0:T(8,128)(2,1)S(1)}, u32[]{:S(2)}, u32[]{:S(2)}) collective-permute-start(bf16[8,4608]{1,0:T(8,128)(2,1)S(1)} %slice.13), channel_id=1, source_target_pairs={{0,2},{4,0},{8,4},{12,8},{14,12},{10,14},{6,10},{2,6},{1,3},{5,1},... | collective-permute-start | bytes 221192 | tf_op jit(solution)/shard_map/ppermute | solution.py:55
  22.1 4.4 %collective-permute-start.6 = (bf16[8,4608]{1,0:T(8,128)(2,1)S(1)}, bf16[8,4608]{1,0:T(8,128)(2,1)S(1)}, u32[]{:S(2)}, u32[]{:S(2)}) collective-permute-start(bf16[8,4608]{1,0:T(8,128)(2,1)S(1)} %slice.12), channel_id=1, source_target_pairs={{0,4},{4,8},{8,12},{12,14},{14,10},{10,6},{6,2},{2,0},{1,5},{5,9},... | collective-permute-start | bytes 221192 | tf_op jit(solution)/shard_map/ppermute | solution.py:55
  26.5 1.2 %collective-permute-start.8 = (f32[64,128]{1,0:T(8,128)S(1)}, f32[64,128]{1,0:T(8,128)S(1)}, u32[]{:S(2)}, u32[]{:S(2)}) collective-permute-start(f32[64,128]{1,0:T(8,128)S(1)} %row_sums.7.refs_0_), channel_id=1, source_target_pairs={{0,1},{1,0},{2,3},{3,2},{4,5},{5,4},{6,7},{7,6},{8,9},{9,8},{10,11... | collective-permute-start | bytes 98312 | tf_op jit(solution)/shard_map/ppermute | solution.py:44
  27.8 17.1 %copy-start.1 = (s32[4]{0:T(128)S(1)}, s32[4]{0:T(128)}, u32[]{:S(2)}) copy-start(s32[4]{0:T(128)} %refs_0_.17) | copy-start | bytes 52
  39.7 1.5 %collective-permute-start.9 = (f32[8,4,1664]{2,1,0:T(4,128)S(1)}, f32[8,4,1664]{2,1,0:T(4,128)S(1)}, u32[]{:S(2)}, u32[]{:S(2)}) collective-permute-start(f32[8,4,1664]{2,1,0:T(4,128)S(1)} %get-tuple-element.66), channel_id=1, source_target_pairs={{0,1},{1,0},{2,3},{3,2},{4,5},{5,4},{6,7},{7,6},{8,9},{9,8},{10,11... | collective-permute-start | bytes 638984 | tf_op jit(solution)/shard_map/ppermute | solution.py:44
  41.3 5.8 %collective-permute-start.11 = (bf16[2,4,1664]{2,1,0:T(4,128)(2,1)S(1)}, bf16[2,4,1664]{2,1,0:T(4,128)(2,1)S(1)}, u32[]{:S(2)}, u32[]{:S(2)}) collective-permute-start(bf16[2,4,1664]{2,1,0:T(4,128)(2,1)S(1)} %get-tuple-element.69), channel_id=1, source_target_pairs={{0,4},{2,6},{4,0},{6,2},{8,12},{10,14},{12,8},{14,10},{1,5},{3,7},... | collective-permute-start | bytes 79880 | tf_op jit(solution)/shard_map/ppermute | solution.py:551
  43.1 4.7 %collective-permute-start.12 = (bf16[2,4,1664]{2,1,0:T(4,128)(2,1)S(1)}, bf16[2,4,1664]{2,1,0:T(4,128)(2,1)S(1)}, u32[]{:S(2)}, u32[]{:S(2)}) collective-permute-start(bf16[2,4,1664]{2,1,0:T(4,128)(2,1)S(1)} %get-tuple-element.70), channel_id=1, source_target_pairs={{0,6},{2,4},{4,2},{6,0},{8,14},{10,12},{12,10},{14,8},{1,7},{3,5},... | collective-permute-start | bytes 79880 | tf_op jit(solution)/shard_map/ppermute | solution.py:551
  44.5 3.8 %collective-permute-start.10 = (bf16[2,4,1664]{2,1,0:T(4,128)(2,1)S(1)}, bf16[2,4,1664]{2,1,0:T(4,128)(2,1)S(1)}, u32[]{:S(2)}, u32[]{:S(2)}) collective-permute-start(bf16[2,4,1664]{2,1,0:T(4,128)(2,1)S(1)} %get-tuple-element.67.refs_0_), channel_id=1, source_target_pairs={{0,2},{2,0},{4,6},{6,4},{8,10},{10,8},{12,14},{14,12},{1,3},{3,1},... | collective-permute-start | bytes 79880 | tf_op jit(solution)/shard_map/ppermute | solution.py:551
  48.3 7.3 %collective-permute-start.13 = (bf16[4,4,1664]{2,1,0:T(4,128)(2,1)S(1)}, bf16[4,4,1664]{2,1,0:T(4,128)(2,1)S(1)}, u32[]{:S(2)}, u32[]{:S(2)}) collective-permute-start(bf16[4,4,1664]{2,1,0:T(4,128)(2,1)S(1)} %pack.1.refs_1_.refs_0_), channel_id=1, source_target_pairs={{0,8},{2,10},{4,12},{6,14},{8,0},{10,2},{12,4},{14,6},{1,9},{3,11}... | collective-permute-start | bytes 159752 | tf_op jit(solution)/shard_map/ppermute | solution.py:551
  61.6 1.3 %collective-permute-start.14 = (bf16[4,6144]{1,0:T(4,128)(2,1)S(1)}, bf16[4,6144]{1,0:T(4,128)(2,1)S(1)}, u32[]{:S(2)}, u32[]{:S(2)}) collective-permute-start(bf16[4,6144]{1,0:T(4,128)(2,1)S(1)} %get-tuple-element.80), channel_id=1, source_target_pairs={{0,1},{1,0},{2,3},{3,2},{4,5},{5,4},{6,7},{7,6},{8,9},{9,8},{10,11... | collective-permute-start | bytes 147464 | tf_op jit(solution)/shard_map/ppermute | solution.py:44
  63.0 4.9 %collective-permute-start.16 = (bf16[8,6144]{1,0:T(8,128)(2,1)S(1)}, bf16[8,6144]{1,0:T(8,128)(2,1)S(1)}, u32[]{:S(2)}, u32[]{:S(2)}) collective-permute-start(bf16[8,6144]{1,0:T(8,128)(2,1)S(1)} %pad_maximum_fusion.refs_1_.refs_0_), channel_id=1, source_target_pairs={{0,2},{4,0},{8,4},{12,8},{14,12},{10,14},{6,10},{2,6},{1,3},{5,1},... | collective-permute-start | bytes 294920 | tf_op jit(solution)/shard_map/ppermute | solution.py:55
  64.1 4.6 %collective-permute-start.15 = (bf16[8,6144]{1,0:T(8,128)(2,1)S(1)}, bf16[8,6144]{1,0:T(8,128)(2,1)S(1)}, u32[]{:S(2)}, u32[]{:S(2)}) collective-permute-start(bf16[8,6144]{1,0:T(8,128)(2,1)S(1)} %pad_maximum_fusion.refs_1_.refs_0_), channel_id=1, source_target_pairs={{0,4},{4,8},{8,12},{12,14},{14,10},{10,6},{6,2},{2,0},{1,5},{5,9},... | collective-permute-start | bytes 294920 | tf_op jit(solution)/shard_map/ppermute | solution.py:55
  68.8 4.6 %collective-permute-start.17 = (bf16[8,6144]{1,0:T(8,128)(2,1)S(1)}, bf16[8,6144]{1,0:T(8,128)(2,1)S(1)}, u32[]{:S(2)}, u32[]{:S(2)}) collective-permute-start(bf16[8,6144]{1,0:T(8,128)(2,1)S(1)} %collective-permute-done.15.refs_1_), channel_id=1, source_target_pairs={{0,4},{4,8},{8,12},{12,14},{14,10},{10,6},{6,2},{2,0},{1,5},{5,9},... | collective-permute-start | bytes 294920 | tf_op jit(solution)/shard_map/ppermute | solution.py:55
  69.7 4.6 %collective-permute-start.18 = (bf16[8,6144]{1,0:T(8,128)(2,1)S(1)}, bf16[8,6144]{1,0:T(8,128)(2,1)S(1)}, u32[]{:S(2)}, u32[]{:S(2)}) collective-permute-start(bf16[8,6144]{1,0:T(8,128)(2,1)S(1)} %collective-permute-done.16.refs_2_), channel_id=1, source_target_pairs={{0,2},{4,0},{8,4},{12,8},{14,12},{10,14},{6,10},{2,6},{1,3},{5,1},... | collective-permute-start | bytes 294920 | tf_op jit(solution)/shard_map/ppermute | solution.py:55
  74.3 4.6 %collective-permute-start.19 = (bf16[8,6144]{1,0:T(8,128)(2,1)S(1)}, bf16[8,6144]{1,0:T(8,128)(2,1)S(1)}, u32[]{:S(2)}, u32[]{:S(2)}) collective-permute-start(bf16[8,6144]{1,0:T(8,128)(2,1)S(1)} %collective-permute-done.17.refs_1_.refs_3_), channel_id=1, source_target_pairs={{0,4},{4,8},{8,12},{12,14},{14,10},{10,6},{6,2},{2,0},{1,5},{5,9},... | collective-permute-start | bytes 294920 | tf_op jit(solution)/shard_map/ppermute | solution.py:55
  75.9 5.0 %collective-permute-start.20 = (bf16[8,6144]{1,0:T(8,128)(2,1)S(1)}, bf16[8,6144]{1,0:T(8,128)(2,1)S(1)}, u32[]{:S(2)}, u32[]{:S(2)}) collective-permute-start(bf16[8,6144]{1,0:T(8,128)(2,1)S(1)} %collective-permute-done.18.refs_2_.refs_4_), channel_id=1, source_target_pairs={{0,2},{4,0},{8,4},{12,8},{14,12},{10,14},{6,10},{2,6},{1,3},{5,1},... | collective-permute-start | bytes 294920 | tf_op jit(solution)/shard_map/ppermute | solution.py:55
  80.9 4.3 %collective-permute-start.22 = (bf16[8,3072]{1,0:T(8,128)(2,1)S(1)}, bf16[8,3072]{1,0:T(8,128)(2,1)S(1)}, u32[]{:S(2)}, u32[]{:S(2)}) collective-permute-start(bf16[8,3072]{1,0:T(8,128)(2,1)S(1)} %slice.15), channel_id=1, source_target_pairs={{0,2},{4,0},{8,4},{12,8},{14,12},{10,14},{6,10},{2,6},{1,3},{5,1},... | collective-permute-start | bytes 147464 | tf_op jit(solution)/shard_map/ppermute | solution.py:55
  81.5 4.1 %collective-permute-start.21 = (bf16[8,3072]{1,0:T(8,128)(2,1)S(1)}, bf16[8,3072]{1,0:T(8,128)(2,1)S(1)}, u32[]{:S(2)}, u32[]{:S(2)}) collective-permute-start(bf16[8,3072]{1,0:T(8,128)(2,1)S(1)} %slice.14), channel_id=1, source_target_pairs={{0,4},{4,8},{8,12},{12,14},{14,10},{10,6},{6,2},{2,0},{1,5},{5,9},... | collective-permute-start | bytes 147464 | tf_op jit(solution)/shard_map/ppermute | solution.py:55
  90.6 1.6 %collective-permute-start.23 = (f32[4,8,2304]{2,1,0:T(8,128)S(1)}, f32[4,8,2304]{2,1,0:T(8,128)S(1)}, u32[]{:S(2)}, u32[]{:S(2)}) collective-permute-start(f32[4,8,2304]{2,1,0:T(8,128)S(1)} %get-tuple-element.96), channel_id=1, source_target_pairs={{0,1},{1,0},{2,3},{3,2},{4,5},{5,4},{6,7},{7,6},{8,9},{9,8},{10,11... | collective-permute-start | bytes 884744 | tf_op jit(solution)/shard_map/ppermute | solution.py:44

commit v13 on v11

--- a/solution.py
+++ b/solution.py
@@ -44,28 +44,27 @@
     return lax.ppermute(x, "gy", [(0, 1), (1, 0)])
 
 
-class Ring:
-    def __init__(self, n):
-        order = ring_order(n)
-        self.onward = [(order[p], order[(p + 1) % n]) for p in range(n)]
-        self.back = [(order[p], order[(p - 1) % n]) for p in range(n)]
-        self.across = [(order[p], order[(p + n // 2) % n]) for p in range(n)]
-
-    def step(self, left, right):
-        return lax.ppermute(left, "gx", self.onward), lax.ppermute(right, "gx", self.back)
+def ring_move(x):
+    n = lax.axis_size("gx")
+    order = ring_order(n)
+    onward = [(2 * order[p], 2 * order[(p + 1) % n]) for p in range(n)]
+    back = [(2 * order[p] + 1, 2 * order[(p - 1) % n] + 1) for p in range(n)]
+    return lax.ppermute(x, ("gx", "gy"), onward + back)
 
 
 def owners(n):
-    offsets = [0]
-    for step in range(1, n // 2):
-        offsets += [-step, step]
-    offsets.append(n // 2)
-    me = lax.axis_index("gx")
+    steps = n // 2 - 1
+    me, side = lax.axis_index("gx"), lax.axis_index("gy")
     half = lax.div(me, 2)
     place = jnp.where(lax.rem(me, 2) == 0, half, n - 1 - half)
+    ahead = 2 * side - 1
+    offsets = [0 * ahead]
+    offsets += [ahead * step for step in range(1, steps + 1)]
+    offsets += [-ahead * step for step in range(1, steps + 1)]
+    offsets.append(0 * ahead + n // 2)
     result = []
     for offset in offsets:
-        at = lax.rem(place + (offset + n), n)
+        at = lax.rem(place + offset + n, n)
         result.append(jnp.where(at < n // 2, 2 * at, 2 * (n - 1 - at) + 1))
     return result
 
@@ -146,57 +145,88 @@
     return held[0], held[1:]
 
 
-def sums_kernel(ready, count, *refs):
+def both_sums(x):
+    rows = x.shape[0] // 2
+    total = jnp.sum(x, axis=1, keepdims=True)
+    square = jnp.sum(x * x, axis=1, keepdims=True)
+    total = total[:rows] + total[rows:]
+    square = square[:rows] + square[rows:]
+    lane = lax.broadcasted_iota(jnp.int32, (rows, 128), 1)
+    return jnp.where(lane == 0, total, jnp.where(lane == 1, square, 0.0))
+
+
+def sums_kernel(shard, *refs):
     out = refs[-1]
     start = 0
-    for ref in refs[:ready]:
+    for ref in refs[:-1]:
         out[start : start + ref.shape[0], :] = ref[...]
         start += ref.shape[0]
-
-    def both_sums(ref):
-        x = ref[...].astype(jnp.float32)
-        total = jnp.sum(x, axis=1, keepdims=True)
-        square = jnp.sum(x * x, axis=1, keepdims=True)
-        lane = lax.broadcasted_iota(jnp.int32, (x.shape[0], 128), 1)
-        return jnp.where(lane == 0, total, jnp.where(lane == 1, square, 0.0))
-
-    for ref in refs[ready : ready + count]:
-        out[start : start + ref.shape[0], :] = both_sums(ref)
-        start += ref.shape[0]
-    halves = refs[ready + count : -1]
-    if halves:
-        out[start:, :] = both_sums(halves[0]) + both_sums(halves[1])
-
-
-def row_sums(shards, ready=(), halves=()):
-    rows = sum(a.shape[0] for a in (*ready, *shards, *halves[:1]))
-    return pl.pallas_call(
-        lambda *refs: sums_kernel(len(ready), len(shards), *refs),
+    out[start:, :] = both_sums(shard[...].astype(jnp.float32))
+
+
+def row_sums(shard, ready):
+    rows = shard.shape[0] // 2 + sum(a.shape[0] for a in ready)
+    return pl.pallas_call(
+        sums_kernel,
         out_shape=jax.ShapeDtypeStruct((rows, 128), jnp.float32),
-        in_specs=[IN_VMEM] * (len(ready) + len(shards) + len(halves)),
+        in_specs=[IN_VMEM] * (1 + len(ready)),
         out_specs=IN_VMEM,
         compiler_params=pltpu.CompilerParams(vmem_limit_bytes=8 * MIB),
         name="row_sums",
-    )(*ready, *shards, *halves)
+    )(shard, *ready)
+
+
+def last_kernel(shard, ready, payload, sums):
+    rows, width = shard.shape[0] // 2, shard.shape[1]
+    x = shard[...].astype(jnp.float32)
+    new = both_sums(x)
+    first = ready.shape[0]
+    sums[:first, :] = ready[...]
+    sums[first:, :] = new
+    payload[:, :width] = x[:rows].astype(jnp.bfloat16)
+    lane = lax.broadcasted_iota(jnp.int32, (rows, 128), 1)
+    value = jnp.where(lane < 3, new[:, :1], new[:, 1:2])
+    high = value.astype(jnp.bfloat16).astype(jnp.float32)
+    middle = (value - high).astype(jnp.bfloat16).astype(jnp.float32)
+    low = value - high - middle
+    part = jnp.where(lane % 3 == 0, high, jnp.where(lane % 3 == 1, middle, low))
+    payload[:, width:] = part.astype(jnp.bfloat16)
+
+
+def last_payload(shard, ready):
+    rows, width = shard.shape[0] // 2, shard.shape[1]
+    return pl.pallas_call(
+        last_kernel,
+        out_shape=[
+            jax.ShapeDtypeStruct((rows, width + 128), jnp.bfloat16),
+            jax.ShapeDtypeStruct((ready.shape[0] + rows, 128), jnp.float32),
+        ],
+        in_specs=[IN_VMEM] * 2,
+        out_specs=[IN_VMEM] * 2,
+        compiler_params=pltpu.CompilerParams(vmem_limit_bytes=8 * MIB),
+        name="last_payload",
+    )(shard, ready)
 
 
 def project_kernel(n, parts, *refs):
-    sums_a, sums_b, gain = refs[:3]
-    shards = refs[3 : 3 + n - 1]
-    far = refs[3 + n - 1 : 3 + n + 1]
-    weights = refs[4 + n : 4 + n + parts]
-    later, keep, give, early, normed, total, sems = refs[4 + n + parts :]
+    sums_here, sums_there, gain = refs[:3]
+    shards = refs[3 : 3 + n]
+    weights = refs[3 + n : 3 + n + parts]
+    later, keep, give, early, normed, total, sems = refs[3 + n + parts :]
     copies = start_copies(later.at[pl.ds(0, early.shape[0])], early, sems, 4)
     rows, width = shards[0].shape
-    sums = sums_a[...] + sums_b[...]
-    row_mean = sums[:, :1] / D
-    row_square = sums[:, 1:2] / D
+    beside = shards[-1][:, width:].astype(jnp.float32)
+    far_total = beside[:, 0:1] + beside[:, 1:2] + beside[:, 2:3]
+    far_square = beside[:, 3:4] + beside[:, 4:5] + beside[:, 5:6]
+    here, there = sums_here[...], sums_there[...]
+    row_mean = jnp.concatenate([here[:, :1], there[rows:, :1], far_total], axis=0) / D
+    row_square = jnp.concatenate([here[:, 1:2], there[rows:, 1:2], far_square], axis=0) / D
     scale = lax.rsqrt(row_square - row_mean * row_mean + epsilon)
     for part in range(2):
         cols = slice(part * width // 2, (part + 1) * width // 2)
         for i in range(0, n, 2):
-            x = [ref[:, cols] if ref is not far[part] else ref[...] for ref in (*shards, far[part])]
-            x = jnp.concatenate([piece.astype(jnp.float32) for piece in x[i : i + 2]], axis=0)
+            x = [ref[:, cols].astype(jnp.float32)[:rows] for ref in shards[i : i + 2]]
+            x = jnp.concatenate(x, axis=0)
             at = slice(i * rows, (i + 2) * rows)
             x = (x - row_mean[at]) * scale[at] * gain[:, cols]
             normed[at, cols] = x.astype(jnp.bfloat16)
@@ -223,15 +253,15 @@
         copy.wait()
 
 
-def project(sums, gain, shards, far, weights, later, size):
-    n = len(shards) + 1
+def project(sums, gain, shards, weights, later, size):
+    n = len(shards)
     rows, width = shards[0].shape
     stripe = sum(w.shape[0] for w in weights)
     shape = jax.ShapeDtypeStruct((n, rows // 2, stripe), jnp.float32)
     return pl.pallas_call(
         lambda *refs: project_kernel(n, len(weights), *refs),
         out_shape=[shape, shape, pltpu.VMEM((size, later.shape[1]), later.dtype)],
-        in_specs=[IN_VMEM] * (4 + n + len(weights)) + [IN_HBM],
+        in_specs=[IN_VMEM] * (3 + n + len(weights)) + [IN_HBM],
         out_specs=[IN_VMEM] * 3,
         scratch_shapes=[
             pltpu.VMEM((n * rows, width), jnp.bfloat16),
@@ -244,7 +274,6 @@
         *sums,
         gain,
         *shards,
-        *far,
         *[in_vmem(w) for w in weights],
         in_hbm(later),
     )
@@ -289,7 +318,7 @@
 
 def attend_kernel(lengths, *refs):
     arrived = refs[:5]
-    cosine, sine, keys, values, mine, other, spread, held = refs[5:]
+    cosine, sine, keys, values, out, spread, held = refs[5:]
     n, rows, stripe = spread.shape[1], spread.shape[0], spread.shape[2]
     me = lax.axis_index("gx")
     query_cols = stripe - 128
@@ -339,19 +368,18 @@
                 at = (i * len(starts) + j) * DH
                 for k, part in enumerate(parts):
                     held[k, r : r + 1, at : at + DH] = part[i : i + 1]
-    mine[...] = held[0].astype(jnp.bfloat16)
-    other[...] = held[1].astype(jnp.bfloat16)
+    out[...] = jnp.concatenate([held[1], held[0]], axis=0).astype(jnp.bfloat16)
 
 
 def attend(lengths, arrived, cosine, sine, keys, values):
     n = len(ARRIVED)
     _, rows, stripe = arrived[0].shape
-    shape = jax.ShapeDtypeStruct((rows, HEADS * DH // 2), jnp.bfloat16)
+    shape = jax.ShapeDtypeStruct((2 * rows, HEADS * DH // 2), jnp.bfloat16)
     return pl.pallas_call(
         attend_kernel,
-        out_shape=[shape, shape],
+        out_shape=shape,
         in_specs=[IN_SMEM] + [IN_VMEM] * 9,
-        out_specs=[IN_VMEM] * 2,
+        out_specs=IN_VMEM,
         scratch_shapes=[
             pltpu.VMEM((rows, n, stripe), jnp.float32),
             pltpu.VMEM((2, rows, HEADS * DH // 2), jnp.float32),
@@ -362,18 +390,16 @@
 
 
 def output_kernel(n, *refs):
-    shards = refs[: n - 1]
-    far = refs[n - 1 : n + 1]
-    weights = refs[n + 1 : -4]
+    shards = refs[:n]
+    weights = refs[n:-4]
     keep, give, total, placed = refs[-4:]
-    rows = shards[0].shape[0]
-    half = far[0].shape[1]
+    rows, width = shards[-1].shape
+    half = width // 2
     for part in range(2):
         start = part * half
         cols = slice(start, start + half)
-        x = [ref[:, cols] for ref in shards] + [far[part][...]]
-        x = jnp.concatenate([piece.astype(jnp.float32) for piece in x], axis=0)
-        x = x.astype(jnp.bfloat16)
+        x = [ref[:, cols].astype(jnp.float32)[:rows] for ref in shards]
+        x = jnp.concatenate(x, axis=0).astype(jnp.bfloat16)
         first = 0
         for weight in weights:
             last = first + weight.shape[0]
@@ -391,20 +417,21 @@
     side = lax.axis_index("gy")
     for i, owner in enumerate(owners(n)):
         block = total[i * rows : (i + 1) * rows, :]
-        placed[owner] = jnp.where(side == 0, block, pltpu.roll(block, rows // 2, 0))
+        sender = 1 - side if n // 2 <= i < n - 1 else side
+        placed[owner] = jnp.where(sender == 0, block, pltpu.roll(block, rows // 2, 0))
     keep[...] = placed[pl.ds(side * (n // 2), n // 2)]
     give[...] = placed[pl.ds((1 - side) * (n // 2), n // 2)]
 
 
-def output_project(shards, far, weights):
-    n = len(shards) + 1
-    rows = shards[0].shape[0]
+def output_project(shards, weights):
+    n = len(shards)
+    rows = shards[-1].shape[0]
     cols = weights[0].shape[1]
     shape = jax.ShapeDtypeStruct((n // 2, rows, cols), jnp.float32)
     return pl.pallas_call(
         lambda *refs: output_kernel(n, *refs),
         out_shape=[shape, shape],
-        in_specs=[IN_VMEM] * (n + 1 + len(weights)),
+        in_specs=[IN_VMEM] * (n + len(weights)),
         out_specs=[IN_VMEM] * 2,
         scratch_shapes=[
             pltpu.VMEM((n * rows, cols), jnp.float32),
@@ -412,7 +439,7 @@
         ],
         compiler_params=pltpu.CompilerParams(vmem_limit_bytes=8 * MIB),
         name="output_project",
-    )(*shards, *far, *[in_vmem(w) for w in weights])
+    )(*shards, *[in_vmem(w) for w in weights])
 
 
 def on_any_grid(
@@ -501,7 +528,6 @@
     cache_lengths,
 ):
     n = lax.axis_size("gx")
-    ring = Ring(n)
     query_cols, width = query_weight.shape
     new_cols = keyval_weight.shape[0]
     piece = query_cols // 4
@@ -515,30 +541,34 @@
     def piece_of(array, start, size, after):
         return load(size, [(array, start, size, 0)], after)
 
-    left = right = activations
-    shards = [activations]
-    sums = []
+    rows = activations.shape[0]
+    shard = jnp.concatenate([activations, swap_pair(activations)], axis=0)
+    came, swapped, sums = [], [], []
     for step in range(1, n // 2):
-        arrived = shards[-2:] if step > 1 else []
-        left, right = ring.step(left, right)
+        moved = ring_move(shard)
         if step > 1:
-            sums = [row_sums([activations, *arrived] if step == 2 else arrived, sums)]
-        weight = piece_of(query_weight, (step - 1) * piece, piece, arrived)
-        weight, (left, right, *sums) = before(weight, left, right, *sums)
+            swapped.append(swap_pair(shard[rows:]))
+        sums = [row_sums(shard, sums)]
+        weight = load(piece, [(query_weight, (step - 1) * piece, piece, 0)], [shard])
+        weight, (moved, *held) = before(weight, moved, *sums, *swapped)
+        sums, swapped = held[:1], held[1:]
         weights.append(weight)
-        shards += [left, right]
-    far = ring.step(left[:, : width // 2], right[:, width // 2 :])
-    sums = row_sums([left, right], sums)
+        came.append(moved)
+        shard = moved
+    payload, sums = last_payload(shard, sums[0])
+    far = ring_move(payload)
+    swapped.append(swap_pair(shard[rows:]))
+    other_sums = swap_pair(sums)
     jobs = [(query_weight, 3 * piece, piece, 0), (keyval_weight, 0, new_cols, None)]
-    weight = load(piece + 2 * new_cols, jobs, [left, right])
-    weight, far = before(weight, *far)
-    sums = row_sums([], [sums], far)
-    other_sums = swap_pair(sums)
+    weight = load(piece + 2 * new_cols, jobs, [payload])
+    weight, (far, other_sums, *swapped) = before(weight, far, other_sums, *swapped)
     weights.append(weight)
+    shards = [activations, *came, *swapped, far]
+    sums = (sums, other_sums)
     gain = norm_gain.astype(jnp.float32)[None, :]
     piece = output_weight.shape[0] // 4
     keep, give, weight = project(
-        (sums, other_sums), gain, shards, far, weights, output_weight, 2 * piece
+        sums, gain, shards, weights, output_weight, 2 * piece
     )
     weights = [weight]
 
@@ -554,27 +584,30 @@
     values = load_cache(cache_values, [across])
     values, (last,) = before(values, last)
     arrived = [*arrived, last]
-    mine, other = attend(cache_lengths, arrived, cosine, sine, keys, values)
-    shard = jnp.concatenate([mine, swap_pair(other)], axis=0)
-
-    left = right = shard
-    shards = [shard]
+    halves = attend(cache_lengths, arrived, cosine, sine, keys, values)
+    got = swap_pair(halves)
+    rows = halves.shape[0]
+    local = rows // 2
+    shard = jnp.concatenate([halves[local:], got[:local], halves[:local], got[local:]], axis=0)
+
     done = 2 * piece
     piece = piece // 2
-
+    shards, swapped = [shard], []
     for step in range(1, n // 2):
-        arrived = shards[-2:]
-        left, right = ring.step(left, right)
-        weight = piece_of(output_weight, done + (step - 1) * piece, piece, arrived)
-        weight, (left, right) = before(weight, left, right)
+        moved = ring_move(shard)
+        if step > 1:
+            swapped.append(swap_pair(shard[rows:]))
+        weight = load(piece, [(output_weight, done + (step - 1) * piece, piece, 0)], [shard])
+        weight, (moved, *swapped) = before(weight, moved, *swapped)
         weights.append(weight)
-        shards += [left, right]
-    half = shard.shape[1] // 2
-    far = ring.step(left[:, :half], right[:, half:])
-    weight = piece_of(output_weight, done + 3 * piece, piece, [left, right])
-    weight, far = before(weight, *far)
+        shards.append(moved)
+        shard = moved
+    far = ring_move(shard[:rows])
+    swapped.append(swap_pair(shard[rows:]))
+    weight = load(piece, [(output_weight, done + 3 * piece, piece, 0)], [shard])
+    weight, (far, *swapped) = before(weight, far, *swapped)
     weights.append(weight)
-    keep, give = output_project(shards, far, weights)
+    keep, give = output_project([*shards, *swapped, far], weights)
     out = (keep + swap_pair(give)).astype(jnp.bfloat16)
     return out.reshape(-1, out.shape[-1])
 

time: 89.6 us -> 89.3 us (level)
  starting transfers between devices: 22 us -> 18 us
  waiting for transfers between devices: 20.2 us -> 23.3 us
  local copies, waits for them, and re-layouts: 0.03 us -> 1.08 us
    ppermute x16 -> x8, starting transfers between devices: 17.6 us -> 10.2 us  [ring_move(): return lax.ppermute(x, ('gx', 'gy'), onward + back)]
    ppermute x16 -> x8, waiting for transfers between devices: 11.9 us -> 16.6 us  [ring_move(): return lax.ppermute(x, ('gx', 'gy'), onward + back)]
    ppermute x4, starting transfers between devices: 4.03 us -> 6.14 us  [exchange(): return lax.ppermute(blocks, 'gx', [(i, i ^ d) for i in range(n)])]
    ppermute x4 -> x11, starting transfers between devices: 0.37 us -> 1.59 us  [swap_pair(): return lax.ppermute(x, 'gy', [(0, 1), (1, 0)])]
    ppermute x4, waiting for transfers between devices: 3.13 us -> 2.18 us  [exchange(): return lax.ppermute(blocks, 'gx', [(i, i ^ d) for i in range(n)])]
    unnamed x6 -> x7, local copies, waits for them, and re-layouts: 0.01 us -> 0.94 us
    ppermute x4 -> x11, waiting for transfers between devices: 5.26 us -> 4.51 us  [swap_pair(): return lax.ppermute(x, 'gy', [(0, 1), (1, 0)])]
  transfers between devices with their start and end apart: 24 -> 23, of which waited for: 18 -> 13; matrix products, arithmetic and copies ran while one was open for 0% -> 1% of each run, Pallas kernels for 29% -> 29%
where the time goes in v13:
time: 89.3 us; the launch traced here: 89.1 us
  Pallas kernels  45.5 us (51%)
  waiting for transfers between devices  23.3 us (26%)
  starting transfers between devices  18 us (20%)
  local copies, waits for them, and re-layouts  1.08 us (1%)
  other arithmetic  0.95 us (1%)
    pallas_call x8, Pallas kernels, load(): pl.pallas_call(lambda *refs: load_kernel([job[1:] for job in jobs], *refs...  20.8 us
    ppermute x8, waiting for transfers between devices, ring_move(): return lax.ppermute(x, ('gx', 'gy'), onward + back)  16.6 us
    pallas_call x1, Pallas kernels, project(): pl.pallas_call(lambda *refs: project_kernel(n, len(weights), *refs), out_...  11.1 us
    ppermute x8, starting transfers between devices, ring_move(): return lax.ppermute(x, ('gx', 'gy'), onward + back)  10.2 us
    ppermute x4, starting transfers between devices, exchange(): return lax.ppermute(blocks, 'gx', [(i, i ^ d) for i in range(n)])  6.14 us
    pallas_call x1, Pallas kernels, output_project(): pl.pallas_call(lambda *refs: output_kernel(n, *refs), out_shape=[shape, s...  5.06 us
    ppermute x11, waiting for transfers between devices, swap_pair(): return lax.ppermute(x, 'gy', [(0, 1), (1, 0)])  4.51 us
    pallas_call x2, Pallas kernels, load_cache(): pl.pallas_call(load_cache_kernel, out_shape=pltpu.VMEM(cache.shape, cache...  4.42 us
  transfers between devices with their start and end apart: 23, of which 13 were waited for; matrix products, arithmetic and copies ran while one was open for 1% of the time, Pallas kernels for 29%

profile of v13, /device:TPU:0, one launch (start us, length us, event | category | flops | bytes accessed | tf_op | source)
XLA Modules:
  0.0 89.1 jit_solution(10110061054363036252)
XLA Ops:
  0.0 0.5 collective-permute-start
  0.5 0.9 %constant_dynamic-update-slice_fusion.1 = bf16[16,9216]{1,0:T(8,128)(2,1)S(1)} fusion(bf16[8,9216]{1,0:T(8,128)(2,1)} %refs_3_.1), kind=kLoop, calls=%fused_computation.4 | loop fusion | bytes 294912
  1.4 0.3 collective-permute-done
  1.7 3.0 %collective-permute-start.1 = (bf16[16,9216]{1,0:T(8,128)(2,1)S(1)}, bf16[16,9216]{1,0:T(8,128)(2,1)S(1)}, u32[]{:S(2)}, u32[]{:S(2)}) collective-permute-start(bf16[16,9216]{1,0:T(8,128)(2,1)S(1)} %constant_dynamic-update-slice_fusion.refs_1_.shard), channel_id=1, source_target_pairs={{0,4},{4,8},{8,12},{12,14},{14,10},{10,6},{6,2},{2,0},{1,3},{5,1},... | collective-permute-start | bytes 884744 | tf_op jit(solution)/shard_map/ppermute | solution.py:52
  4.7 0.2 row_sums.3.refs_0_
  4.8 3.1 %load.8.refs_11_ = bf16[384,9216]{1,0:T(8,128)(2,1)S(1)} custom-call(bf16[1536,9216]{1,0:T(8,128)(2,1)} %refs_0_.11, bf16[16,9216]{1,0:T(8,128)(2,1)S(1)} %constant_dynamic-update-slice_fusion.refs_1_.shard), custom_call_target="tpu_custom_call" | custom-call | tf_op jit(solution)/shard_map/load/pallas_call | solution.py:102
  8.0 1.3 %collective-permute-done.1.refs_1_.shard.refs_4_ = bf16[16,9216]{1,0:T(8,128)(2,1)S(1)} collective-permute-done((bf16[16,9216]{1,0:T(8,128)(2,1)S(1)}, bf16[16,9216]{1,0:T(8,128)(2,1)S(1)}, u32[]{:S(2)}, u32[]{:S(2)}) %collective-permute-start.1) | collective-permute-done | bytes 294944 | tf_op jit(solution)/shard_map/ppermute | solution.py:52
  9.3 2.1 %collective-permute-start.2 = (bf16[16,9216]{1,0:T(8,128)(2,1)S(1)}, bf16[16,9216]{1,0:T(8,128)(2,1)S(1)}, u32[]{:S(2)}, u32[]{:S(2)}) collective-permute-start(bf16[16,9216]{1,0:T(8,128)(2,1)S(1)} %collective-permute-done.1.refs_1_.shard.refs_4_), channel_id=1, source_target_pairs={{0,4},{4,8},{8,12},{12,14},{14,10},{10,6},{6,2},{2,0},{1,3},{5,1},... | collective-permute-start | bytes 884744 | tf_op jit(solution)/shard_map/ppermute | solution.py:52
  11.5 3.1 %load.9.refs_12_ = bf16[384,9216]{1,0:T(8,128)(2,1)S(1)} custom-call(bf16[1536,9216]{1,0:T(8,128)(2,1)} %refs_0_.11, bf16[16,9216]{1,0:T(8,128)(2,1)S(1)} %collective-permute-done.1.refs_1_.shard.refs_4_), custom_call_target="tpu_custom_call" | custom-call | tf_op jit(solution)/shard_map/load/pallas_call | solution.py:102
  14.6 0.2 row_sums.4.refs_0_
  14.8 1.3 %collective-permute-done.2.refs_1_.shard.refs_5_ = bf16[16,9216]{1,0:T(8,128)(2,1)S(1)} collective-permute-done((bf16[16,9216]{1,0:T(8,128)(2,1)S(1)}, bf16[16,9216]{1,0:T(8,128)(2,1)S(1)}, u32[]{:S(2)}, u32[]{:S(2)}) %collective-permute-start.2) | collective-permute-done | bytes 294944 | tf_op jit(solution)/shard_map/ppermute | solution.py:52
  16.0 2.1 %collective-permute-start.4 = (bf16[16,9216]{1,0:T(8,128)(2,1)S(1)}, bf16[16,9216]{1,0:T(8,128)(2,1)S(1)}, u32[]{:S(2)}, u32[]{:S(2)}) collective-permute-start(bf16[16,9216]{1,0:T(8,128)(2,1)S(1)} %collective-permute-done.2.refs_1_.shard.refs_5_), channel_id=1, source_target_pairs={{0,4},{4,8},{8,12},{12,14},{14,10},{10,6},{6,2},{2,0},{1,3},{5,1},... | collective-permute-start | bytes 884744 | tf_op jit(solution)/shard_map/ppermute | solution.py:52
  18.2 3.1 %load.10.refs_13_ = bf16[384,9216]{1,0:T(8,128)(2,1)S(1)} custom-call(bf16[1536,9216]{1,0:T(8,128)(2,1)} %refs_0_.11, bf16[16,9216]{1,0:T(8,128)(2,1)S(1)} %collective-permute-done.2.refs_1_.shard.refs_5_), custom_call_target="tpu_custom_call" | custom-call | tf_op jit(solution)/shard_map/load/pallas_call | solution.py:102
  21.3 0.2 row_sums.5.ready
  21.5 1.2 %collective-permute-done.4.shard.refs_6_ = bf16[16,9216]{1,0:T(8,128)(2,1)S(1)} collective-permute-done((bf16[16,9216]{1,0:T(8,128)(2,1)S(1)}, bf16[16,9216]{1,0:T(8,128)(2,1)S(1)}, u32[]{:S(2)}, u32[]{:S(2)}) %collective-permute-start.4) | collective-permute-done | bytes 294944 | tf_op jit(solution)/shard_map/ppermute | solution.py:52
  22.8 0.2 last_payload.1
  23.0 2.1 %collective-permute-start.6 = (bf16[8,9344]{1,0:T(8,128)(2,1)S(1)}, bf16[8,9344]{1,0:T(8,128)(2,1)S(1)}, u32[]{:S(2)}, u32[]{:S(2)}) collective-permute-start(bf16[8,9344]{1,0:T(8,128)(2,1)S(1)} %get-tuple-element.63.refs_2_), channel_id=1, source_target_pairs={{0,4},{4,8},{8,12},{12,14},{14,10},{10,6},{6,2},{2,0},{1,3},{5,1},... | collective-permute-start | bytes 448520 | tf_op jit(solution)/shard_map/ppermute | solution.py:52
  25.2 0.5 collective-permute-start.7
  25.7 3.4 %load.11.refs_14_ = bf16[512,9216]{1,0:T(8,128)(2,1)S(1)} custom-call(bf16[1536,9216]{1,0:T(8,128)(2,1)} %refs_0_.11, bf16[64,9216]{1,0:T(8,128)(2,1)} %refs_1_.1, bf16[8,9344]{1,0:T(8,128)(2,1)S(1)} %get-tuple-element.63.refs_2_), custom_call_target="tpu_custom_call" | custom-call | tf_op jit(solution)/shard_map/load/pallas_call | solution.py:102
  29.2 11.1 %project.1 = (f32[8,4,1664]{2,1,0:T(4,128)S(1)}, f32[8,4,1664]{2,1,0:T(4,128)S(1)}, bf16[3072,2304]{1,0:T(8,128)(2,1)S(1)}) custom-call(f32[32,128]{1,0:T(8,128)S(1)} %get-tuple-element.62.refs_0_, f32[32,128]{1,0:T(8,128)S(1)} %collective-permute-done.7.refs_1_, f32[1,9216]{1,0:T(1,128)S(1)} %bitcast.3, bf16[8,9216]{1,0:T(8,128)(2,1)S(1)} %copy-done, ...), custom_call_target="tpu_custom_call" | custom-call | tf_op jit(solution)/shard_map/project/pallas_call | solution.py:261
  40.3 0.1 collective-permute-start.9
  40.4 1.4 %collective-permute-done.9.got = f32[8,4,1664]{2,1,0:T(4,128)S(1)} collective-permute-done((f32[8,4,1664]{2,1,0:T(4,128)S(1)}, f32[8,4,1664]{2,1,0:T(4,128)S(1)}, u32[]{:S(2)}, u32[]{:S(2)}) %collective-permute-start.9) | collective-permute-done | bytes 213024 | tf_op jit(solution)/shard_map/ppermute | solution.py:44
  41.8 1.1 %collective-permute-start.10 = (bf16[2,4,1664]{2,1,0:T(4,128)(2,1)S(1)}, bf16[2,4,1664]{2,1,0:T(4,128)(2,1)S(1)}, u32[]{:S(2)}, u32[]{:S(2)}) collective-permute-start(bf16[2,4,1664]{2,1,0:T(4,128)(2,1)S(1)} %get-tuple-element.77.refs_0_), channel_id=1, source_target_pairs={{0,2},{2,0},{4,6},{6,4},{8,10},{10,8},{12,14},{14,12},{1,3},{3,1},... | collective-permute-start | bytes 79880 | tf_op jit(solution)/shard_map/ppermute | solution.py:576
  42.9 1.6 %collective-permute-start.11 = (bf16[2,4,1664]{2,1,0:T(4,128)(2,1)S(1)}, bf16[2,4,1664]{2,1,0:T(4,128)(2,1)S(1)}, u32[]{:S(2)}, u32[]{:S(2)}) collective-permute-start(bf16[2,4,1664]{2,1,0:T(4,128)(2,1)S(1)} %get-tuple-element.79), channel_id=1, source_target_pairs={{0,4},{2,6},{4,0},{6,2},{8,12},{10,14},{12,8},{14,10},{1,5},{3,7},... | collective-permute-start | bytes 79880 | tf_op jit(solution)/shard_map/ppermute | solution.py:576
  44.5 0.9 collective-permute-start.12
  45.4 2.2 %load_cache.2.refs_7_ = bf16[4,2048,256]{2,1,0:T(8,128)(2,1)S(1)} custom-call(bf16[4,2048,256]{2,1,0:T(8,128)(2,1)} %source.2, bf16[2,4,1664]{2,1,0:T(4,128)(2,1)S(1)} %get-tuple-element.77.refs_0_), custom_call_target="tpu_custom_call" | custom-call | tf_op jit(solution)/shard_map/load_cache/pallas_call | solution.py:124
  47.7 1.6 %collective-permute-done.12.refs_3_ = bf16[2,4,1664]{2,1,0:T(4,128)(2,1)S(1)} collective-permute-done((bf16[2,4,1664]{2,1,0:T(4,128)(2,1)S(1)}, bf16[2,4,1664]{2,1,0:T(4,128)(2,1)S(1)}, u32[]{:S(2)}, u32[]{:S(2)}) %collective-permute-start.12) | collective-permute-done | bytes 26656 | tf_op jit(solution)/shard_map/ppermute | solution.py:576
  49.3 2.6 %collective-permute-start.13 = (bf16[4,4,1664]{2,1,0:T(4,128)(2,1)S(1)}, bf16[4,4,1664]{2,1,0:T(4,128)(2,1)S(1)}, u32[]{:S(2)}, u32[]{:S(2)}) collective-permute-start(bf16[4,4,1664]{2,1,0:T(4,128)(2,1)S(1)} %pack.1.refs_0_), channel_id=1, source_target_pairs={{0,8},{2,10},{4,12},{6,14},{8,0},{10,2},{12,4},{14,6},{1,9},{3,11}... | collective-permute-start | bytes 159752 | tf_op jit(solution)/shard_map/ppermute | solution.py:576
  51.9 0.1 multiply_sine_fusion
  52.0 2.2 %load_cache.3.refs_8_ = bf16[4,2048,256]{2,1,0:T(8,128)(2,1)S(1)} custom-call(bf16[4,2048,256]{2,1,0:T(8,128)(2,1)} %source.3, bf16[4,4,1664]{2,1,0:T(4,128)(2,1)S(1)} %pack.1.refs_0_), custom_call_target="tpu_custom_call" | custom-call | tf_op jit(solution)/shard_map/load_cache/pallas_call | solution.py:124
  54.2 0.6 collective-permute-done.13.refs_4_
  54.8 3.4 %attend.1 = bf16[8,6144]{1,0:T(8,128)(2,1)S(1)} custom-call(s32[4]{0:T(128)S(1)} %copy-done.1, bf16[2,4,1664]{2,1,0:T(4,128)(2,1)S(1)} %get-tuple-element.81.refs_0_, bf16[2,4,1664]{2,1,0:T(4,128)(2,1)S(1)} %collective-permute-done.10.refs_1_, bf16[2,4,1664]{2,1,0:T(4,128)(2,1)S(1)} %collective-permute-done.11.refs_2_, ...), custom_call_target="tpu_custom_call" | custom-call | tf_op jit(solution)/shard_map/attend/pallas_call | solution.py:378
  58.3 1.2 %collective-permute-done.14 = bf16[8,6144]{1,0:T(8,128)(2,1)S(1)} collective-permute-done((bf16[8,6144]{1,0:T(8,128)(2,1)S(1)}, bf16[8,6144]{1,0:T(8,128)(2,1)S(1)}, u32[]{:S(2)}, u32[]{:S(2)}) %collective-permute-start.14) | collective-permute-done | bytes 98336 | tf_op jit(solution)/shard_map/ppermute | solution.py:44
  59.6 0.1 pad_maximum_fusion.refs_1_.refs_0_
  59.8 2.0 %load.12.refs_9_ = bf16[768,2304]{1,0:T(8,128)(2,1)S(1)} custom-call(bf16[6144,2304]{1,0:T(8,128)(2,1)} %refs_0_.15, bf16[16,6144]{1,0:T(8,128)(2,1)S(1)} %pad_maximum_fusion.refs_1_.refs_0_), custom_call_target="tpu_custom_call" | custom-call | tf_op jit(solution)/shard_map/load/pallas_call | solution.py:102
  61.8 3.6 %collective-permute-done.15.refs_1_ = bf16[16,6144]{1,0:T(8,128)(2,1)S(1)} collective-permute-done((bf16[16,6144]{1,0:T(8,128)(2,1)S(1)}, bf16[16,6144]{1,0:T(8,128)(2,1)S(1)}, u32[]{:S(2)}, u32[]{:S(2)}) %collective-permute-start.15) | collective-permute-done | bytes 196640 | tf_op jit(solution)/shard_map/ppermute | solution.py:52
  65.5 0.2 collective-permute-start.16
  65.8 2.0 %load.13.refs_10_ = bf16[768,2304]{1,0:T(8,128)(2,1)S(1)} custom-call(bf16[6144,2304]{1,0:T(8,128)(2,1)} %refs_0_.15, bf16[16,6144]{1,0:T(8,128)(2,1)S(1)} %collective-permute-done.15.refs_1_), custom_call_target="tpu_custom_call" | custom-call | tf_op jit(solution)/shard_map/load/pallas_call | solution.py:102
  67.8 3.3 %collective-permute-done.16.refs_1_.refs_2_ = bf16[16,6144]{1,0:T(8,128)(2,1)S(1)} collective-permute-done((bf16[16,6144]{1,0:T(8,128)(2,1)S(1)}, bf16[16,6144]{1,0:T(8,128)(2,1)S(1)}, u32[]{:S(2)}, u32[]{:S(2)}) %collective-permute-start.16) | collective-permute-done | bytes 196640 | tf_op jit(solution)/shard_map/ppermute | solution.py:52
  71.1 0.2 collective-permute-start.18
  71.4 2.0 %load.14.refs_11_ = bf16[768,2304]{1,0:T(8,128)(2,1)S(1)} custom-call(bf16[6144,2304]{1,0:T(8,128)(2,1)} %refs_0_.15, bf16[16,6144]{1,0:T(8,128)(2,1)S(1)} %collective-permute-done.16.refs_1_.refs_2_), custom_call_target="tpu_custom_call" | custom-call | tf_op jit(solution)/shard_map/load/pallas_call | solution.py:102
  73.5 3.3 %collective-permute-done.18.refs_1_.refs_3_ = bf16[16,6144]{1,0:T(8,128)(2,1)S(1)} collective-permute-done((bf16[16,6144]{1,0:T(8,128)(2,1)S(1)}, bf16[16,6144]{1,0:T(8,128)(2,1)S(1)}, u32[]{:S(2)}, u32[]{:S(2)}) %collective-permute-start.18) | collective-permute-done | bytes 196640 | tf_op jit(solution)/shard_map/ppermute | solution.py:52
  76.8 0.4 collective-permute-start.20
  77.3 2.0 %load.15.refs_12_ = bf16[768,2304]{1,0:T(8,128)(2,1)S(1)} custom-call(bf16[6144,2304]{1,0:T(8,128)(2,1)} %refs_0_.15, bf16[16,6144]{1,0:T(8,128)(2,1)S(1)} %collective-permute-done.18.refs_1_.refs_3_), custom_call_target="tpu_custom_call" | custom-call | tf_op jit(solution)/shard_map/load/pallas_call | solution.py:102
  79.3 2.4 %collective-permute-done.20.refs_7_ = bf16[8,6144]{1,0:T(8,128)(2,1)S(1)} collective-permute-done((bf16[8,6144]{1,0:T(8,128)(2,1)S(1)}, bf16[8,6144]{1,0:T(8,128)(2,1)S(1)}, u32[]{:S(2)}, u32[]{:S(2)}) %collective-permute-start.20) | collective-permute-done | bytes 98336 | tf_op jit(solution)/shard_map/ppermute | solution.py:52
  81.7 5.1 %output_project.1 = (f32[4,8,2304]{2,1,0:T(8,128)S(1)}, f32[4,8,2304]{2,1,0:T(8,128)S(1)}) custom-call(bf16[16,6144]{1,0:T(8,128)(2,1)S(1)} %pad_maximum_fusion.refs_1_.refs_0_, bf16[16,6144]{1,0:T(8,128)(2,1)S(1)} %collective-permute-done.15.refs_1_, bf16[16,6144]{1,0:T(8,128)(2,1)S(1)} %collective-permute-done.16.refs_1_.refs_2_, ...), custom_call_target="tpu_custom_call" | custom-call | tf_op jit(solution)/shard_map/output_project/pallas_call | solution.py:431
  86.8 1.6 %collective-permute-done.22 = f32[4,8,2304]{2,1,0:T(8,128)S(1)} collective-permute-done((f32[4,8,2304]{2,1,0:T(8,128)S(1)}, f32[4,8,2304]{2,1,0:T(8,128)S(1)}, u32[]{:S(2)}, u32[]{:S(2)}) %collective-permute-start.22) | collective-permute-done | bytes 294944 | tf_op jit(solution)/shard_map/ppermute | solution.py:44
  88.4 0.7 fusion
  (39 shorter events, 0.8 us)
Async XLA Ops:
  0.0 1.7 %collective-permute-start = (bf16[8,9216]{1,0:T(8,128)(2,1)}, bf16[8,9216]{1,0:T(8,128)(2,1)S(1)}, u32[]{:S(2)}, u32[]{:S(2)}) collective-permute-start(bf16[8,9216]{1,0:T(8,128)(2,1)} %refs_3_.1), channel_id=1, source_target_pairs={{0,1},{1,0},{2,3},{3,2},{4,5},{5,4},{6,7},{7,6},{8,9},{9,8},{10,11... | collective-permute-start | bytes 442376 | tf_op jit(solution)/shard_map/ppermute | solution.py:44
  1.7 7.6 %collective-permute-start.1 = (bf16[16,9216]{1,0:T(8,128)(2,1)S(1)}, bf16[16,9216]{1,0:T(8,128)(2,1)S(1)}, u32[]{:S(2)}, u32[]{:S(2)}) collective-permute-start(bf16[16,9216]{1,0:T(8,128)(2,1)S(1)} %constant_dynamic-update-slice_fusion.refs_1_.shard), channel_id=1, source_target_pairs={{0,4},{4,8},{8,12},{12,14},{14,10},{10,6},{6,2},{2,0},{1,3},{5,1},... | collective-permute-start | bytes 884744 | tf_op jit(solution)/shard_map/ppermute | solution.py:52
  9.3 6.7 %collective-permute-start.2 = (bf16[16,9216]{1,0:T(8,128)(2,1)S(1)}, bf16[16,9216]{1,0:T(8,128)(2,1)S(1)}, u32[]{:S(2)}, u32[]{:S(2)}) collective-permute-start(bf16[16,9216]{1,0:T(8,128)(2,1)S(1)} %collective-permute-done.1.refs_1_.shard.refs_4_), channel_id=1, source_target_pairs={{0,4},{4,8},{8,12},{12,14},{14,10},{10,6},{6,2},{2,0},{1,3},{5,1},... | collective-permute-start | bytes 884744 | tf_op jit(solution)/shard_map/ppermute | solution.py:52
  11.4 3.4 %collective-permute-start.3 = (bf16[8,9216]{1,0:T(8,128)(2,1)S(1)}, bf16[8,9216]{1,0:T(8,128)(2,1)S(1)}, u32[]{:S(2)}, u32[]{:S(2)}) collective-permute-start(bf16[8,9216]{1,0:T(8,128)(2,1)S(1)} %slice.33), channel_id=1, source_target_pairs={{0,1},{1,0},{2,3},{3,2},{4,5},{5,4},{6,7},{7,6},{8,9},{9,8},{10,11... | collective-permute-start | bytes 442376 | tf_op jit(solution)/shard_map/ppermute | solution.py:44
  16.0 6.7 %collective-permute-start.4 = (bf16[16,9216]{1,0:T(8,128)(2,1)S(1)}, bf16[16,9216]{1,0:T(8,128)(2,1)S(1)}, u32[]{:S(2)}, u32[]{:S(2)}) collective-permute-start(bf16[16,9216]{1,0:T(8,128)(2,1)S(1)} %collective-permute-done.2.refs_1_.shard.refs_5_), channel_id=1, source_target_pairs={{0,4},{4,8},{8,12},{12,14},{14,10},{10,6},{6,2},{2,0},{1,3},{5,1},... | collective-permute-start | bytes 884744 | tf_op jit(solution)/shard_map/ppermute | solution.py:52
  18.1 7.6 %copy-start.2 = (bf16[9216]{0:T(1024)(128)(2,1)S(1)}, bf16[9216]{0:T(1024)(128)(2,1)}, u32[]{:S(2)}) copy-start(bf16[9216]{0:T(1024)(128)(2,1)} %param.9) | copy-start | bytes 55300
  18.1 3.4 %collective-permute-start.5 = (bf16[8,9216]{1,0:T(8,128)(2,1)S(1)}, bf16[8,9216]{1,0:T(8,128)(2,1)S(1)}, u32[]{:S(2)}, u32[]{:S(2)}) collective-permute-start(bf16[8,9216]{1,0:T(8,128)(2,1)S(1)} %slice.34), channel_id=1, source_target_pairs={{0,1},{1,0},{2,3},{3,2},{4,5},{5,4},{6,7},{7,6},{8,9},{9,8},{10,11... | collective-permute-start | bytes 442376 | tf_op jit(solution)/shard_map/ppermute | solution.py:44
  23.0 6.2 %collective-permute-start.6 = (bf16[8,9344]{1,0:T(8,128)(2,1)S(1)}, bf16[8,9344]{1,0:T(8,128)(2,1)S(1)}, u32[]{:S(2)}, u32[]{:S(2)}) collective-permute-start(bf16[8,9344]{1,0:T(8,128)(2,1)S(1)} %get-tuple-element.63.refs_2_), channel_id=1, source_target_pairs={{0,4},{4,8},{8,12},{12,14},{14,10},{10,6},{6,2},{2,0},{1,3},{5,1},... | collective-permute-start | bytes 448520 | tf_op jit(solution)/shard_map/ppermute | solution.py:52
  25.1 4.0 %collective-permute-start.8 = (bf16[8,9216]{1,0:T(8,128)(2,1)S(1)}, bf16[8,9216]{1,0:T(8,128)(2,1)S(1)}, u32[]{:S(2)}, u32[]{:S(2)}) collective-permute-start(bf16[8,9216]{1,0:T(8,128)(2,1)S(1)} %slice.35), channel_id=1, source_target_pairs={{0,1},{1,0},{2,3},{3,2},{4,5},{5,4},{6,7},{7,6},{8,9},{9,8},{10,11... | collective-permute-start | bytes 442376 | tf_op jit(solution)/shard_map/ppermute | solution.py:44
  25.2 3.9 %collective-permute-start.7 = (f32[32,128]{1,0:T(8,128)S(1)}, f32[32,128]{1,0:T(8,128)S(1)}, u32[]{:S(2)}, u32[]{:S(2)}) collective-permute-start(f32[32,128]{1,0:T(8,128)S(1)} %get-tuple-element.62.refs_0_), channel_id=1, source_target_pairs={{0,1},{1,0},{2,3},{3,2},{4,5},{5,4},{6,7},{7,6},{8,9},{9,8},{10,11... | collective-permute-start | bytes 49160 | tf_op jit(solution)/shard_map/ppermute | solution.py:44
  25.7 3.5 %copy-start = (bf16[8,9216]{1,0:T(8,128)(2,1)S(1)}, bf16[8,9216]{1,0:T(8,128)(2,1)}, u32[]{:S(2)}) copy-start(bf16[8,9216]{1,0:T(8,128)(2,1)} %refs_3_.1) | copy-start | bytes 442372
  29.2 16.2 %copy-start.1 = (s32[4]{0:T(128)S(1)}, s32[4]{0:T(128)}, u32[]{:S(2)}) copy-start(s32[4]{0:T(128)} %lengths.1) | copy-start | bytes 52
  40.3 1.5 %collective-permute-start.9 = (f32[8,4,1664]{2,1,0:T(4,128)S(1)}, f32[8,4,1664]{2,1,0:T(4,128)S(1)}, u32[]{:S(2)}, u32[]{:S(2)}) collective-permute-start(f32[8,4,1664]{2,1,0:T(4,128)S(1)} %get-tuple-element.76), channel_id=1, source_target_pairs={{0,1},{1,0},{2,3},{3,2},{4,5},{5,4},{6,7},{7,6},{8,9},{9,8},{10,11... | collective-permute-start | bytes 638984 | tf_op jit(solution)/shard_map/ppermute | solution.py:44
  41.8 5.8 %collective-permute-start.10 = (bf16[2,4,1664]{2,1,0:T(4,128)(2,1)S(1)}, bf16[2,4,1664]{2,1,0:T(4,128)(2,1)S(1)}, u32[]{:S(2)}, u32[]{:S(2)}) collective-permute-start(bf16[2,4,1664]{2,1,0:T(4,128)(2,1)S(1)} %get-tuple-element.77.refs_0_), channel_id=1, source_target_pairs={{0,2},{2,0},{4,6},{6,4},{8,10},{10,8},{12,14},{14,12},{1,3},{3,1},... | collective-permute-start | bytes 79880 | tf_op jit(solution)/shard_map/ppermute | solution.py:576
  42.9 4.7 %collective-permute-start.11 = (bf16[2,4,1664]{2,1,0:T(4,128)(2,1)S(1)}, bf16[2,4,1664]{2,1,0:T(4,128)(2,1)S(1)}, u32[]{:S(2)}, u32[]{:S(2)}) collective-permute-start(bf16[2,4,1664]{2,1,0:T(4,128)(2,1)S(1)} %get-tuple-element.79), channel_id=1, source_target_pairs={{0,4},{2,6},{4,0},{6,2},{8,12},{10,14},{12,8},{14,10},{1,5},{3,7},... | collective-permute-start | bytes 79880 | tf_op jit(solution)/shard_map/ppermute | solution.py:576
  44.5 4.7 %collective-permute-start.12 = (bf16[2,4,1664]{2,1,0:T(4,128)(2,1)S(1)}, bf16[2,4,1664]{2,1,0:T(4,128)(2,1)S(1)}, u32[]{:S(2)}, u32[]{:S(2)}) collective-permute-start(bf16[2,4,1664]{2,1,0:T(4,128)(2,1)S(1)} %get-tuple-element.80), channel_id=1, source_target_pairs={{0,6},{2,4},{4,2},{6,0},{8,14},{10,12},{12,10},{14,8},{1,7},{3,5},... | collective-permute-start | bytes 79880 | tf_op jit(solution)/shard_map/ppermute | solution.py:576
  49.3 5.5 %collective-permute-start.13 = (bf16[4,4,1664]{2,1,0:T(4,128)(2,1)S(1)}, bf16[4,4,1664]{2,1,0:T(4,128)(2,1)S(1)}, u32[]{:S(2)}, u32[]{:S(2)}) collective-permute-start(bf16[4,4,1664]{2,1,0:T(4,128)(2,1)S(1)} %pack.1.refs_0_), channel_id=1, source_target_pairs={{0,8},{2,10},{4,12},{6,14},{8,0},{10,2},{12,4},{14,6},{1,9},{3,11}... | collective-permute-start | bytes 159752 | tf_op jit(solution)/shard_map/ppermute | solution.py:576
  58.2 1.4 %collective-permute-start.14 = (bf16[8,6144]{1,0:T(8,128)(2,1)S(1)}, bf16[8,6144]{1,0:T(8,128)(2,1)S(1)}, u32[]{:S(2)}, u32[]{:S(2)}) collective-permute-start(bf16[8,6144]{1,0:T(8,128)(2,1)S(1)} %attend.1), channel_id=1, source_target_pairs={{0,1},{1,0},{2,3},{3,2},{4,5},{5,4},{6,7},{7,6},{8,9},{9,8},{10,11... | collective-permute-start | bytes 294920 | tf_op jit(solution)/shard_map/ppermute | solution.py:44
  59.7 5.7 %collective-permute-start.15 = (bf16[16,6144]{1,0:T(8,128)(2,1)S(1)}, bf16[16,6144]{1,0:T(8,128)(2,1)S(1)}, u32[]{:S(2)}, u32[]{:S(2)}) collective-permute-start(bf16[16,6144]{1,0:T(8,128)(2,1)S(1)} %pad_maximum_fusion.refs_1_.refs_0_), channel_id=1, source_target_pairs={{0,4},{4,8},{8,12},{12,14},{14,10},{10,6},{6,2},{2,0},{1,3},{5,1},... | collective-permute-start | bytes 589832 | tf_op jit(solution)/shard_map/ppermute | solution.py:52
  65.5 5.7 %collective-permute-start.16 = (bf16[16,6144]{1,0:T(8,128)(2,1)S(1)}, bf16[16,6144]{1,0:T(8,128)(2,1)S(1)}, u32[]{:S(2)}, u32[]{:S(2)}) collective-permute-start(bf16[16,6144]{1,0:T(8,128)(2,1)S(1)} %collective-permute-done.15.refs_1_), channel_id=1, source_target_pairs={{0,4},{4,8},{8,12},{12,14},{14,10},{10,6},{6,2},{2,0},{1,3},{5,1},... | collective-permute-start | bytes 589832 | tf_op jit(solution)/shard_map/ppermute | solution.py:52
  65.7 2.1 %collective-permute-start.17 = (bf16[8,6144]{1,0:T(8,128)(2,1)S(1)}, bf16[8,6144]{1,0:T(8,128)(2,1)S(1)}, u32[]{:S(2)}, u32[]{:S(2)}) collective-permute-start(bf16[8,6144]{1,0:T(8,128)(2,1)S(1)} %slice.40), channel_id=1, source_target_pairs={{0,1},{1,0},{2,3},{3,2},{4,5},{5,4},{6,7},{7,6},{8,9},{9,8},{10,11... | collective-permute-start | bytes 294920 | tf_op jit(solution)/shard_map/ppermute | solution.py:44
  71.1 5.7 %collective-permute-start.18 = (bf16[16,6144]{1,0:T(8,128)(2,1)S(1)}, bf16[16,6144]{1,0:T(8,128)(2,1)S(1)}, u32[]{:S(2)}, u32[]{:S(2)}) collective-permute-start(bf16[16,6144]{1,0:T(8,128)(2,1)S(1)} %collective-permute-done.16.refs_1_.refs_2_), channel_id=1, source_target_pairs={{0,4},{4,8},{8,12},{12,14},{14,10},{10,6},{6,2},{2,0},{1,3},{5,1},... | collective-permute-start | bytes 589832 | tf_op jit(solution)/shard_map/ppermute | solution.py:52
  71.4 2.1 %collective-permute-start.19 = (bf16[8,6144]{1,0:T(8,128)(2,1)S(1)}, bf16[8,6144]{1,0:T(8,128)(2,1)S(1)}, u32[]{:S(2)}, u32[]{:S(2)}) collective-permute-start(bf16[8,6144]{1,0:T(8,128)(2,1)S(1)} %slice.41), channel_id=1, source_target_pairs={{0,1},{1,0},{2,3},{3,2},{4,5},{5,4},{6,7},{7,6},{8,9},{9,8},{10,11... | collective-permute-start | bytes 294920 | tf_op jit(solution)/shard_map/ppermute | solution.py:44
  76.8 4.8 %collective-permute-start.20 = (bf16[8,6144]{1,0:T(8,128)(2,1)S(1)}, bf16[8,6144]{1,0:T(8,128)(2,1)S(1)}, u32[]{:S(2)}, u32[]{:S(2)}) collective-permute-start(bf16[8,6144]{1,0:T(8,128)(2,1)S(1)} %get-tuple-element.106), channel_id=1, source_target_pairs={{0,4},{4,8},{8,12},{12,14},{14,10},{10,6},{6,2},{2,0},{1,3},{5,1},... | collective-permute-start | bytes 294920 | tf_op jit(solution)/shard_map/ppermute | solution.py:52
  77.3 4.4 %collective-permute-start.21 = (bf16[8,6144]{1,0:T(8,128)(2,1)S(1)}, bf16[8,6144]{1,0:T(8,128)(2,1)S(1)}, u32[]{:S(2)}, u32[]{:S(2)}) collective-permute-start(bf16[8,6144]{1,0:T(8,128)(2,1)S(1)} %get-tuple-element.105), channel_id=1, source_target_pairs={{0,1},{1,0},{2,3},{3,2},{4,5},{5,4},{6,7},{7,6},{8,9},{9,8},{10,11... | collective-permute-start | bytes 294920 | tf_op jit(solution)/shard_map/ppermute | solution.py:44
  86.7 1.6 %collective-permute-start.22 = (f32[4,8,2304]{2,1,0:T(8,128)S(1)}, f32[4,8,2304]{2,1,0:T(8,128)S(1)}, u32[]{:S(2)}, u32[]{:S(2)}) collective-permute-start(f32[4,8,2304]{2,1,0:T(8,128)S(1)} %get-tuple-element.104), channel_id=1, source_target_pairs={{0,1},{1,0},{2,3},{3,2},{4,5},{5,4},{6,7},{7,6},{8,9},{9,8},{10,11... | collective-permute-start | bytes 884744 | tf_op jit(solution)/shard_map/ppermute | solution.py:44

commit v14 on v11

--- a/solution.py
+++ b/solution.py
@@ -185,8 +185,7 @@
     shards = refs[3 : 3 + n - 1]
     far = refs[3 + n - 1 : 3 + n + 1]
     weights = refs[4 + n : 4 + n + parts]
-    later, keep, give, early, normed, total, sems = refs[4 + n + parts :]
-    copies = start_copies(later.at[pl.ds(0, early.shape[0])], early, sems, 4)
+    keep, give, normed, total = refs[4 + n + parts :]
     rows, width = shards[0].shape
     sums = sums_a[...] + sums_b[...]
     row_mean = sums[:, :1] / D
@@ -219,24 +218,21 @@
         low, high = block[:local], block[local:]
         keep[owner] = jnp.where(side == 0, low, high)
         give[owner] = jnp.where(side == 0, high, low)
-    for copy in copies:
-        copy.wait()
-
-
-def project(sums, gain, shards, far, weights, later, size):
+
+
+def project(sums, gain, shards, far, weights):
     n = len(shards) + 1
     rows, width = shards[0].shape
     stripe = sum(w.shape[0] for w in weights)
     shape = jax.ShapeDtypeStruct((n, rows // 2, stripe), jnp.float32)
     return pl.pallas_call(
         lambda *refs: project_kernel(n, len(weights), *refs),
-        out_shape=[shape, shape, pltpu.VMEM((size, later.shape[1]), later.dtype)],
-        in_specs=[IN_VMEM] * (4 + n + len(weights)) + [IN_HBM],
-        out_specs=[IN_VMEM] * 3,
+        out_shape=[shape, shape],
+        in_specs=[IN_VMEM] * (4 + n + len(weights)),
+        out_specs=[IN_VMEM] * 2,
         scratch_shapes=[
             pltpu.VMEM((n * rows, width), jnp.bfloat16),
             pltpu.VMEM((n * rows, stripe), jnp.float32),
-            pltpu.SemaphoreType.DMA((4,)),
         ],
         compiler_params=pltpu.CompilerParams(vmem_limit_bytes=6 * MIB),
         name="project",
@@ -246,7 +242,6 @@
         *shards,
         *far,
         *[in_vmem(w) for w in weights],
-        in_hbm(later),
     )
 
 
@@ -377,13 +372,14 @@
         first = 0
         for weight in weights:
             last = first + weight.shape[0]
-            if start <= first and last <= start + half:
+            low, high = max(first, start), min(last, start + half)
+            if low < high:
                 term = jnp.dot(
-                    x[:, first - start : last - start],
-                    weight[...],
+                    x[:, low - start : high - start],
+                    weight[low - first : high - first, :],
                     preferred_element_type=jnp.float32,
                 )
-                if first == 0:
+                if low == 0:
                     total[...] = term
                 else:
                     total[...] += term
@@ -536,11 +532,7 @@
     other_sums = swap_pair(sums)
     weights.append(weight)
     gain = norm_gain.astype(jnp.float32)[None, :]
-    piece = output_weight.shape[0] // 4
-    keep, give, weight = project(
-        (sums, other_sums), gain, shards, far, weights, output_weight, 2 * piece
-    )
-    weights = [weight]
+    keep, give = project((sums, other_sums), gain, shards, far, weights)
 
     def exchange(blocks, d):
         return lax.ppermute(blocks, "gx", [(i, i ^ d) for i in range(n)])
@@ -552,15 +544,18 @@
     across = pack([(0, 1), (1, 1), (2, 1), (3, 1)], *arrived)
     last = exchange(across, 4)
     values = load_cache(cache_values, [across])
+    done = output_weight.shape[0] // 6
+    weight = load(done, [(output_weight, 0, done, 0)], [across])
     values, (last,) = before(values, last)
+    weight, (last,) = before(weight, last)
+    weights = [weight]
     arrived = [*arrived, last]
     mine, other = attend(cache_lengths, arrived, cosine, sine, keys, values)
     shard = jnp.concatenate([mine, swap_pair(other)], axis=0)
 
     left = right = shard
     shards = [shard]
-    done = 2 * piece
-    piece = piece // 2
+    piece = (output_weight.shape[0] - done) // 4
 
     for step in range(1, n // 2):
         arrived = shards[-2:]

time: 89.6 us -> 88.4 us (0.987)
  waiting for transfers between devices: 20.2 us -> 16 us
  Pallas kernels: 46 us -> 49.3 us
    pallas_call x8 -> x9, Pallas kernels: 20.7 us -> 26 us  [load(): pl.pallas_call(lambda *refs: load_kernel([job[1:] for job in jobs], *refs...]
    ppermute x4, waiting for transfers between devices: 3.13 us -> 0.75 us  [exchange(): return lax.ppermute(blocks, 'gx', [(i, i ^ d) for i in range(n)])]
    pallas_call x1, Pallas kernels: 11.7 us -> 9.63 us  [project(): pl.pallas_call(lambda *refs: project_kernel(n, len(weights), *refs), out_...]
    ppermute x8, waiting for transfers between devices: 3.16 us -> 1.26 us  [step(): lax.ppermute(left, 'gx', self.onward)]
    ppermute x8, starting transfers between devices: 4.93 us -> 4.03 us  [step(): lax.ppermute(right, 'gx', self.back)]
  transfers between devices with their start and end apart: 24 -> 24, of which waited for: 18 -> 16; matrix products, arithmetic and copies ran while one was open for 0% -> 0% of each run, Pallas kernels for 29% -> 35%
where the time goes in v14:
time: 88.4 us; the launch traced here: 88.2 us
  Pallas kernels  49.3 us (56%)
  starting transfers between devices  21.7 us (25%)
  waiting for transfers between devices  16 us (18%)
    pallas_call x9, Pallas kernels, load(): pl.pallas_call(lambda *refs: load_kernel([job[1:] for job in jobs], *refs...  26 us
    ppermute x8, starting transfers between devices, step(): lax.ppermute(left, 'gx', self.onward)  13.3 us
    pallas_call x1, Pallas kernels, project(): pl.pallas_call(lambda *refs: project_kernel(n, len(weights), *refs), out_...  9.63 us
    ppermute x8, waiting for transfers between devices, step(): lax.ppermute(right, 'gx', self.back)  8.73 us
    ppermute x4, waiting for transfers between devices, swap_pair(): return lax.ppermute(x, 'gy', [(0, 1), (1, 0)])  5.26 us
    pallas_call x1, Pallas kernels, output_project(): pl.pallas_call(lambda *refs: output_kernel(n, *refs), out_shape=[shape, s...  5.05 us
    pallas_call x2, Pallas kernels, load_cache(): pl.pallas_call(load_cache_kernel, out_shape=pltpu.VMEM(cache.shape, cache...  4.42 us
    ppermute x8, starting transfers between devices, step(): lax.ppermute(right, 'gx', self.back)  4.03 us
  transfers between devices with their start and end apart: 24, of which 16 were waited for; matrix products, arithmetic and copies ran while one was open for 0% of the time, Pallas kernels for 35%

profile of v14, /device:TPU:0, one launch (start us, length us, event | category | flops | bytes accessed | tf_op | source)
XLA Modules:
  0.0 88.2 jit_solution(17382856101030034345)
XLA Ops:
  0.0 3.0 %collective-permute-start = (bf16[8,9216]{1,0:T(8,128)(2,1)}, bf16[8,9216]{1,0:T(8,128)(2,1)S(1)}, u32[]{:S(2)}, u32[]{:S(2)}) collective-permute-start(bf16[8,9216]{1,0:T(8,128)(2,1)} %refs_3_.1), channel_id=1, source_target_pairs={{0,4},{4,8},{8,12},{12,14},{14,10},{10,6},{6,2},{2,0},{1,5},{5,9},... | collective-permute-start | bytes 442376 | tf_op jit(solution)/shard_map/ppermute | solution.py:55
  3.0 3.1 %load.9.refs_12_ = bf16[384,9216]{1,0:T(8,128)(2,1)S(1)} custom-call(bf16[1536,9216]{1,0:T(8,128)(2,1)} %refs_0_.14), custom_call_target="tpu_custom_call" | custom-call | tf_op jit(solution)/shard_map/load/pallas_call | solution.py:103
  6.1 1.0 %collective-permute-done.refs_1_.refs_4_ = bf16[8,9216]{1,0:T(8,128)(2,1)S(1)} collective-permute-done((bf16[8,9216]{1,0:T(8,128)(2,1)}, bf16[8,9216]{1,0:T(8,128)(2,1)S(1)}, u32[]{:S(2)}, u32[]{:S(2)}) %collective-permute-start) | collective-permute-done | bytes 147488 | tf_op jit(solution)/shard_map/ppermute | solution.py:55
  7.1 1.4 %collective-permute-done.1.refs_2_.refs_5_ = bf16[8,9216]{1,0:T(8,128)(2,1)S(1)} collective-permute-done((bf16[8,9216]{1,0:T(8,128)(2,1)}, bf16[8,9216]{1,0:T(8,128)(2,1)S(1)}, u32[]{:S(2)}, u32[]{:S(2)}) %collective-permute-start.1) | collective-permute-done | bytes 147488 | tf_op jit(solution)/shard_map/ppermute | solution.py:55
  8.5 1.6 %collective-permute-start.2 = (bf16[8,9216]{1,0:T(8,128)(2,1)S(1)}, bf16[8,9216]{1,0:T(8,128)(2,1)S(1)}, u32[]{:S(2)}, u32[]{:S(2)}) collective-permute-start(bf16[8,9216]{1,0:T(8,128)(2,1)S(1)} %collective-permute-done.refs_1_.refs_4_), channel_id=1, source_target_pairs={{0,4},{4,8},{8,12},{12,14},{14,10},{10,6},{6,2},{2,0},{1,5},{5,9},... | collective-permute-start | bytes 442376 | tf_op jit(solution)/shard_map/ppermute | solution.py:55
  10.1 0.4 collective-permute-start.3
  10.8 3.1 %load.10.refs_13_ = bf16[384,9216]{1,0:T(8,128)(2,1)S(1)} custom-call(bf16[1536,9216]{1,0:T(8,128)(2,1)} %refs_0_.14, bf16[8,9216]{1,0:T(8,128)(2,1)S(1)} %collective-permute-done.refs_1_.refs_4_, bf16[8,9216]{1,0:T(8,128)(2,1)S(1)} %collective-permute-done.1.refs_2_.refs_5_), custom_call_target="tpu_custom_call" | custom-call | tf_op jit(solution)/shard_map/load/pallas_call | solution.py:103
  13.9 1.3 %collective-permute-done.3.refs_2_.refs_7_ = bf16[8,9216]{1,0:T(8,128)(2,1)S(1)} collective-permute-done((bf16[8,9216]{1,0:T(8,128)(2,1)S(1)}, bf16[8,9216]{1,0:T(8,128)(2,1)S(1)}, u32[]{:S(2)}, u32[]{:S(2)}) %collective-permute-start.3) | collective-permute-done | bytes 147488 | tf_op jit(solution)/shard_map/ppermute | solution.py:55
  15.3 1.6 %collective-permute-start.4 = (bf16[8,9216]{1,0:T(8,128)(2,1)S(1)}, bf16[8,9216]{1,0:T(8,128)(2,1)S(1)}, u32[]{:S(2)}, u32[]{:S(2)}) collective-permute-start(bf16[8,9216]{1,0:T(8,128)(2,1)S(1)} %collective-permute-done.2.refs_1_.refs_6_), channel_id=1, source_target_pairs={{0,4},{4,8},{8,12},{12,14},{14,10},{10,6},{6,2},{2,0},{1,5},{5,9},... | collective-permute-start | bytes 442376 | tf_op jit(solution)/shard_map/ppermute | solution.py:55
  16.8 0.4 collective-permute-start.5
  17.3 3.1 %load.11.refs_14_ = bf16[384,9216]{1,0:T(8,128)(2,1)S(1)} custom-call(bf16[1536,9216]{1,0:T(8,128)(2,1)} %refs_0_.14, bf16[8,9216]{1,0:T(8,128)(2,1)S(1)} %collective-permute-done.2.refs_1_.refs_6_, bf16[8,9216]{1,0:T(8,128)(2,1)S(1)} %collective-permute-done.3.refs_2_.refs_7_), custom_call_target="tpu_custom_call" | custom-call | tf_op jit(solution)/shard_map/load/pallas_call | solution.py:103
  20.6 1.4 %collective-permute-done.5.refs_2_.refs_3_.refs_9_ = bf16[8,9216]{1,0:T(8,128)(2,1)S(1)} collective-permute-done((bf16[8,9216]{1,0:T(8,128)(2,1)S(1)}, bf16[8,9216]{1,0:T(8,128)(2,1)S(1)}, u32[]{:S(2)}, u32[]{:S(2)}) %collective-permute-start.5) | collective-permute-done | bytes 147488 | tf_op jit(solution)/shard_map/ppermute | solution.py:55
  22.0 1.9 %collective-permute-start.6 = (bf16[8,4608]{1,0:T(8,128)(2,1)S(1)}, bf16[8,4608]{1,0:T(8,128)(2,1)S(1)}, u32[]{:S(2)}, u32[]{:S(2)}) collective-permute-start(bf16[8,4608]{1,0:T(8,128)(2,1)S(1)} %slice.12), channel_id=1, source_target_pairs={{0,4},{4,8},{8,12},{12,14},{14,10},{10,6},{6,2},{2,0},{1,5},{5,9},... | collective-permute-start | bytes 221192 | tf_op jit(solution)/shard_map/ppermute | solution.py:55
  24.1 3.4 %load.12.refs_15_ = bf16[512,9216]{1,0:T(8,128)(2,1)S(1)} custom-call(bf16[1536,9216]{1,0:T(8,128)(2,1)} %refs_0_.14, bf16[64,9216]{1,0:T(8,128)(2,1)} %refs_1_.1, bf16[8,9216]{1,0:T(8,128)(2,1)S(1)} %collective-permute-done.4.refs_1_.refs_2_.refs_8_, bf16[8,9216]{1,0:T(8,128)(2,1)S(1)} %collective-permute-done.5.refs_2_.refs_3_.refs_9_), custom_call_target="tpu_custom_call" | custom-call | tf_op jit(solution)/shard_map/load/pallas_call | solution.py:103
  27.6 0.7 collective-permute-done.7.refs_2_.refs_11_
  28.5 1.2 %collective-permute-done.8.refs_1_ = f32[64,128]{1,0:T(8,128)S(1)} collective-permute-done((f32[64,128]{1,0:T(8,128)S(1)}, f32[64,128]{1,0:T(8,128)S(1)}, u32[]{:S(2)}, u32[]{:S(2)}) %collective-permute-start.8) | collective-permute-done | bytes 32800 | tf_op jit(solution)/shard_map/ppermute | solution.py:44
  29.7 9.6 %project.1 = (f32[8,4,1664]{2,1,0:T(4,128)S(1)}, f32[8,4,1664]{2,1,0:T(4,128)S(1)}) custom-call(f32[64,128]{1,0:T(8,128)S(1)} %row_sums.7.refs_0_, f32[64,128]{1,0:T(8,128)S(1)} %collective-permute-done.8.refs_1_, f32[1,9216]{1,0:T(1,128)S(1)} %bitcast.3, bf16[8,9216]{1,0:T(8,128)(2,1)S(1)} %copy-done, ...), custom_call_target="tpu_custom_call" | custom-call | tf_op jit(solution)/shard_map/project/pallas_call | solution.py:228
  39.6 1.3 %collective-permute-done.9.got = f32[8,4,1664]{2,1,0:T(4,128)S(1)} collective-permute-done((f32[8,4,1664]{2,1,0:T(4,128)S(1)}, f32[8,4,1664]{2,1,0:T(4,128)S(1)}, u32[]{:S(2)}, u32[]{:S(2)}) %collective-permute-start.9) | collective-permute-done | bytes 213024 | tf_op jit(solution)/shard_map/ppermute | solution.py:44
  41.1 1.2 %collective-permute-start.11 = (bf16[2,4,1664]{2,1,0:T(4,128)(2,1)S(1)}, bf16[2,4,1664]{2,1,0:T(4,128)(2,1)S(1)}, u32[]{:S(2)}, u32[]{:S(2)}) collective-permute-start(bf16[2,4,1664]{2,1,0:T(4,128)(2,1)S(1)} %get-tuple-element.68), channel_id=1, source_target_pairs={{0,4},{2,6},{4,0},{6,2},{8,12},{10,14},{12,8},{14,10},{1,5},{3,7},... | collective-permute-start | bytes 79880 | tf_op jit(solution)/shard_map/ppermute | solution.py:538
  42.3 2.2 %collective-permute-start.12 = (bf16[2,4,1664]{2,1,0:T(4,128)(2,1)S(1)}, bf16[2,4,1664]{2,1,0:T(4,128)(2,1)S(1)}, u32[]{:S(2)}, u32[]{:S(2)}) collective-permute-start(bf16[2,4,1664]{2,1,0:T(4,128)(2,1)S(1)} %get-tuple-element.69), channel_id=1, source_target_pairs={{0,6},{2,4},{4,2},{6,0},{8,14},{10,12},{12,10},{14,8},{1,7},{3,5},... | collective-permute-start | bytes 79880 | tf_op jit(solution)/shard_map/ppermute | solution.py:538
  44.5 2.2 %load_cache.2.refs_7_ = bf16[4,2048,256]{2,1,0:T(8,128)(2,1)S(1)} custom-call(bf16[4,2048,256]{2,1,0:T(8,128)(2,1)} %source.2, bf16[2,4,1664]{2,1,0:T(4,128)(2,1)S(1)} %get-tuple-element.66.refs_0_), custom_call_target="tpu_custom_call" | custom-call | tf_op jit(solution)/shard_map/load_cache/pallas_call | solution.py:125
  46.7 0.3 collective-permute-done.12.refs_3_
  47.0 0.5 collective-permute-start.13
  47.6 2.2 %load_cache.3.refs_8_ = bf16[4,2048,256]{2,1,0:T(8,128)(2,1)S(1)} custom-call(bf16[4,2048,256]{2,1,0:T(8,128)(2,1)} %source.3, bf16[4,4,1664]{2,1,0:T(4,128)(2,1)S(1)} %pack.1.refs_1_.refs_0_), custom_call_target="tpu_custom_call" | custom-call | tf_op jit(solution)/shard_map/load_cache/pallas_call | solution.py:125
  49.9 2.4 %load.13.refs_9_ = bf16[1024,2304]{1,0:T(8,128)(2,1)S(1)} custom-call(bf16[6144,2304]{1,0:T(8,128)(2,1)} %refs_0_.19, bf16[4,4,1664]{2,1,0:T(4,128)(2,1)S(1)} %pack.1.refs_1_.refs_0_), custom_call_target="tpu_custom_call" | custom-call | tf_op jit(solution)/shard_map/load/pallas_call | solution.py:103
  52.2 0.4 collective-permute-done.13.refs_4_
  52.7 3.4 %attend.1 = (bf16[4,6144]{1,0:T(4,128)(2,1)S(1)}, bf16[4,6144]{1,0:T(4,128)(2,1)S(1)}) custom-call(s32[4]{0:T(128)S(1)} %copy-done.1, bf16[2,4,1664]{2,1,0:T(4,128)(2,1)S(1)} %get-tuple-element.70.refs_0_, bf16[2,4,1664]{2,1,0:T(4,128)(2,1)S(1)} %collective-permute-done.10.refs_1_, bf16[2,4,1664]{2,1,0:T(4,128)(2,1)S(1)} %collective-permute-done.11.refs_2_, ...), custom_call_target="tpu_custom_call" | custom-call | tf_op jit(solution)/shard_map/attend/pallas_call | solution.py:345
  56.2 1.2 %collective-permute-done.14 = bf16[4,6144]{1,0:T(4,128)(2,1)S(1)} collective-permute-done((bf16[4,6144]{1,0:T(4,128)(2,1)S(1)}, bf16[4,6144]{1,0:T(4,128)(2,1)S(1)}, u32[]{:S(2)}, u32[]{:S(2)}) %collective-permute-start.14) | collective-permute-done | bytes 49184 | tf_op jit(solution)/shard_map/ppermute | solution.py:44
  57.5 0.7 collective-permute-start.15
  58.1 1.4 %collective-permute-start.16 = (bf16[8,6144]{1,0:T(8,128)(2,1)S(1)}, bf16[8,6144]{1,0:T(8,128)(2,1)S(1)}, u32[]{:S(2)}, u32[]{:S(2)}) collective-permute-start(bf16[8,6144]{1,0:T(8,128)(2,1)S(1)} %pad_maximum_fusion.refs_1_.refs_0_), channel_id=1, source_target_pairs={{0,2},{4,0},{8,4},{12,8},{14,12},{10,14},{6,10},{2,6},{1,3},{5,1},... | collective-permute-start | bytes 294920 | tf_op jit(solution)/shard_map/ppermute | solution.py:55
  59.5 2.7 %load.14.refs_10_ = bf16[1280,2304]{1,0:T(8,128)(2,1)S(1)} custom-call(bf16[6144,2304]{1,0:T(8,128)(2,1)} %refs_0_.19, bf16[8,6144]{1,0:T(8,128)(2,1)S(1)} %pad_maximum_fusion.refs_1_.refs_0_), custom_call_target="tpu_custom_call" | custom-call | tf_op jit(solution)/shard_map/load/pallas_call | solution.py:103
  62.3 0.3 collective-permute-done.15.refs_1_
  62.6 0.4 collective-permute-done.16.refs_2_
  63.0 1.8 %collective-permute-start.17 = (bf16[8,6144]{1,0:T(8,128)(2,1)S(1)}, bf16[8,6144]{1,0:T(8,128)(2,1)S(1)}, u32[]{:S(2)}, u32[]{:S(2)}) collective-permute-start(bf16[8,6144]{1,0:T(8,128)(2,1)S(1)} %collective-permute-done.15.refs_1_), channel_id=1, source_target_pairs={{0,4},{4,8},{8,12},{12,14},{14,10},{10,6},{6,2},{2,0},{1,5},{5,9},... | collective-permute-start | bytes 294920 | tf_op jit(solution)/shard_map/ppermute | solution.py:55
  64.7 0.2 collective-permute-start.18
  65.0 2.7 %load.15.refs_11_ = bf16[1280,2304]{1,0:T(8,128)(2,1)S(1)} custom-call(bf16[6144,2304]{1,0:T(8,128)(2,1)} %refs_0_.19, bf16[8,6144]{1,0:T(8,128)(2,1)S(1)} %collective-permute-done.15.refs_1_, bf16[8,6144]{1,0:T(8,128)(2,1)S(1)} %collective-permute-done.16.refs_2_), custom_call_target="tpu_custom_call" | custom-call | tf_op jit(solution)/shard_map/load/pallas_call | solution.py:103
  67.7 1.6 %collective-permute-done.18.refs_2_.refs_4_ = bf16[8,6144]{1,0:T(8,128)(2,1)S(1)} collective-permute-done((bf16[8,6144]{1,0:T(8,128)(2,1)S(1)}, bf16[8,6144]{1,0:T(8,128)(2,1)S(1)}, u32[]{:S(2)}, u32[]{:S(2)}) %collective-permute-start.18) | collective-permute-done | bytes 98336 | tf_op jit(solution)/shard_map/ppermute | solution.py:55
  69.4 1.0 %collective-permute-start.19 = (bf16[8,6144]{1,0:T(8,128)(2,1)S(1)}, bf16[8,6144]{1,0:T(8,128)(2,1)S(1)}, u32[]{:S(2)}, u32[]{:S(2)}) collective-permute-start(bf16[8,6144]{1,0:T(8,128)(2,1)S(1)} %collective-permute-done.17.refs_1_.refs_3_), channel_id=1, source_target_pairs={{0,4},{4,8},{8,12},{12,14},{14,10},{10,6},{6,2},{2,0},{1,5},{5,9},... | collective-permute-start | bytes 294920 | tf_op jit(solution)/shard_map/ppermute | solution.py:55
  70.4 1.0 %collective-permute-start.20 = (bf16[8,6144]{1,0:T(8,128)(2,1)S(1)}, bf16[8,6144]{1,0:T(8,128)(2,1)S(1)}, u32[]{:S(2)}, u32[]{:S(2)}) collective-permute-start(bf16[8,6144]{1,0:T(8,128)(2,1)S(1)} %collective-permute-done.18.refs_2_.refs_4_), channel_id=1, source_target_pairs={{0,2},{4,0},{8,4},{12,8},{14,12},{10,14},{6,10},{2,6},{1,3},{5,1},... | collective-permute-start | bytes 294920 | tf_op jit(solution)/shard_map/ppermute | solution.py:55
  71.4 2.7 %load.16.refs_12_ = bf16[1280,2304]{1,0:T(8,128)(2,1)S(1)} custom-call(bf16[6144,2304]{1,0:T(8,128)(2,1)} %refs_0_.19, bf16[8,6144]{1,0:T(8,128)(2,1)S(1)} %collective-permute-done.17.refs_1_.refs_3_, bf16[8,6144]{1,0:T(8,128)(2,1)S(1)} %collective-permute-done.18.refs_2_.refs_4_), custom_call_target="tpu_custom_call" | custom-call | tf_op jit(solution)/shard_map/load/pallas_call | solution.py:103
  74.1 0.8 collective-permute-done.20.refs_2_.refs_6_
  75.0 1.7 %collective-permute-start.21 = (bf16[8,3072]{1,0:T(8,128)(2,1)S(1)}, bf16[8,3072]{1,0:T(8,128)(2,1)S(1)}, u32[]{:S(2)}, u32[]{:S(2)}) collective-permute-start(bf16[8,3072]{1,0:T(8,128)(2,1)S(1)} %slice.14), channel_id=1, source_target_pairs={{0,4},{4,8},{8,12},{12,14},{14,10},{10,6},{6,2},{2,0},{1,5},{5,9},... | collective-permute-start | bytes 147464 | tf_op jit(solution)/shard_map/ppermute | solution.py:55
  76.7 0.3 collective-permute-start.22
  77.0 2.7 %load.17.refs_13_ = bf16[1280,2304]{1,0:T(8,128)(2,1)S(1)} custom-call(bf16[6144,2304]{1,0:T(8,128)(2,1)} %refs_0_.19, bf16[8,6144]{1,0:T(8,128)(2,1)S(1)} %collective-permute-done.19.refs_1_.refs_5_, bf16[8,6144]{1,0:T(8,128)(2,1)S(1)} %collective-permute-done.20.refs_2_.refs_6_), custom_call_target="tpu_custom_call" | custom-call | tf_op jit(solution)/shard_map/load/pallas_call | solution.py:103
  79.8 1.0 %collective-permute-done.22.refs_8_ = bf16[8,3072]{1,0:T(8,128)(2,1)S(1)} collective-permute-done((bf16[8,3072]{1,0:T(8,128)(2,1)S(1)}, bf16[8,3072]{1,0:T(8,128)(2,1)S(1)}, u32[]{:S(2)}, u32[]{:S(2)}) %collective-permute-start.22) | collective-permute-done | bytes 49184 | tf_op jit(solution)/shard_map/ppermute | solution.py:55
  80.8 5.0 %output_project.1 = (f32[4,8,2304]{2,1,0:T(8,128)S(1)}, f32[4,8,2304]{2,1,0:T(8,128)S(1)}) custom-call(bf16[8,6144]{1,0:T(8,128)(2,1)S(1)} %pad_maximum_fusion.refs_1_.refs_0_, bf16[8,6144]{1,0:T(8,128)(2,1)S(1)} %collective-permute-done.15.refs_1_, bf16[8,6144]{1,0:T(8,128)(2,1)S(1)} %collective-permute-done.16.refs_2_, ...), custom_call_target="tpu_custom_call" | custom-call | tf_op jit(solution)/shard_map/output_project/pallas_call | solution.py:400
  85.9 1.6 %collective-permute-done.23 = f32[4,8,2304]{2,1,0:T(8,128)S(1)} collective-permute-done((f32[4,8,2304]{2,1,0:T(8,128)S(1)}, f32[4,8,2304]{2,1,0:T(8,128)S(1)}, u32[]{:S(2)}, u32[]{:S(2)}) %collective-permute-start.23) | collective-permute-done | bytes 294944 | tf_op jit(solution)/shard_map/ppermute | solution.py:44
  87.5 0.7 fusion
  (36 shorter events, 1.7 us)
Async XLA Ops:
  0.0 10.6 %copy-start = (bf16[8,9216]{1,0:T(8,128)(2,1)S(1)}, bf16[8,9216]{1,0:T(8,128)(2,1)}, u32[]{:S(2)}) copy-start(bf16[8,9216]{1,0:T(8,128)(2,1)} %refs_3_.1) | copy-start | bytes 442372
  0.0 7.1 %collective-permute-start = (bf16[8,9216]{1,0:T(8,128)(2,1)}, bf16[8,9216]{1,0:T(8,128)(2,1)S(1)}, u32[]{:S(2)}, u32[]{:S(2)}) collective-permute-start(bf16[8,9216]{1,0:T(8,128)(2,1)} %refs_3_.1), channel_id=1, source_target_pairs={{0,4},{4,8},{8,12},{12,14},{14,10},{10,6},{6,2},{2,0},{1,5},{5,9},... | collective-permute-start | bytes 442376 | tf_op jit(solution)/shard_map/ppermute | solution.py:55
  3.0 5.5 %collective-permute-start.1 = (bf16[8,9216]{1,0:T(8,128)(2,1)}, bf16[8,9216]{1,0:T(8,128)(2,1)S(1)}, u32[]{:S(2)}, u32[]{:S(2)}) collective-permute-start(bf16[8,9216]{1,0:T(8,128)(2,1)} %refs_3_.1), channel_id=1, source_target_pairs={{0,2},{4,0},{8,4},{12,8},{14,12},{10,14},{6,10},{2,6},{1,3},{5,1},... | collective-permute-start | bytes 442376 | tf_op jit(solution)/shard_map/ppermute | solution.py:55
  8.5 5.4 %collective-permute-start.2 = (bf16[8,9216]{1,0:T(8,128)(2,1)S(1)}, bf16[8,9216]{1,0:T(8,128)(2,1)S(1)}, u32[]{:S(2)}, u32[]{:S(2)}) collective-permute-start(bf16[8,9216]{1,0:T(8,128)(2,1)S(1)} %collective-permute-done.refs_1_.refs_4_), channel_id=1, source_target_pairs={{0,4},{4,8},{8,12},{12,14},{14,10},{10,6},{6,2},{2,0},{1,5},{5,9},... | collective-permute-start | bytes 442376 | tf_op jit(solution)/shard_map/ppermute | solution.py:55
  10.1 5.1 %collective-permute-start.3 = (bf16[8,9216]{1,0:T(8,128)(2,1)S(1)}, bf16[8,9216]{1,0:T(8,128)(2,1)S(1)}, u32[]{:S(2)}, u32[]{:S(2)}) collective-permute-start(bf16[8,9216]{1,0:T(8,128)(2,1)S(1)} %collective-permute-done.1.refs_2_.refs_5_), channel_id=1, source_target_pairs={{0,2},{4,0},{8,4},{12,8},{14,12},{10,14},{6,10},{2,6},{1,3},{5,1},... | collective-permute-start | bytes 442376 | tf_op jit(solution)/shard_map/ppermute | solution.py:55
  15.3 5.3 %collective-permute-start.4 = (bf16[8,9216]{1,0:T(8,128)(2,1)S(1)}, bf16[8,9216]{1,0:T(8,128)(2,1)S(1)}, u32[]{:S(2)}, u32[]{:S(2)}) collective-permute-start(bf16[8,9216]{1,0:T(8,128)(2,1)S(1)} %collective-permute-done.2.refs_1_.refs_6_), channel_id=1, source_target_pairs={{0,4},{4,8},{8,12},{12,14},{14,10},{10,6},{6,2},{2,0},{1,5},{5,9},... | collective-permute-start | bytes 442376 | tf_op jit(solution)/shard_map/ppermute | solution.py:55
  16.8 5.1 %collective-permute-start.5 = (bf16[8,9216]{1,0:T(8,128)(2,1)S(1)}, bf16[8,9216]{1,0:T(8,128)(2,1)S(1)}, u32[]{:S(2)}, u32[]{:S(2)}) collective-permute-start(bf16[8,9216]{1,0:T(8,128)(2,1)S(1)} %collective-permute-done.3.refs_2_.refs_7_), channel_id=1, source_target_pairs={{0,2},{4,0},{8,4},{12,8},{14,12},{10,14},{6,10},{2,6},{1,3},{5,1},... | collective-permute-start | bytes 442376 | tf_op jit(solution)/shard_map/ppermute | solution.py:55
  22.0 5.7 %collective-permute-start.6 = (bf16[8,4608]{1,0:T(8,128)(2,1)S(1)}, bf16[8,4608]{1,0:T(8,128)(2,1)S(1)}, u32[]{:S(2)}, u32[]{:S(2)}) collective-permute-start(bf16[8,4608]{1,0:T(8,128)(2,1)S(1)} %slice.12), channel_id=1, source_target_pairs={{0,4},{4,8},{8,12},{12,14},{14,10},{10,6},{6,2},{2,0},{1,5},{5,9},... | collective-permute-start | bytes 221192 | tf_op jit(solution)/shard_map/ppermute | solution.py:55
  23.9 4.5 %copy-start.2 = (bf16[9216]{0:T(1024)(128)(2,1)S(1)}, bf16[9216]{0:T(1024)(128)(2,1)}, u32[]{:S(2)}) copy-start(bf16[9216]{0:T(1024)(128)(2,1)} %param.9) | copy-start | bytes 55300
  23.9 4.4 %collective-permute-start.7 = (bf16[8,4608]{1,0:T(8,128)(2,1)S(1)}, bf16[8,4608]{1,0:T(8,128)(2,1)S(1)}, u32[]{:S(2)}, u32[]{:S(2)}) collective-permute-start(bf16[8,4608]{1,0:T(8,128)(2,1)S(1)} %slice.13), channel_id=1, source_target_pairs={{0,2},{4,0},{8,4},{12,8},{14,12},{10,14},{6,10},{2,6},{1,3},{5,1},... | collective-permute-start | bytes 221192 | tf_op jit(solution)/shard_map/ppermute | solution.py:55
  28.5 1.2 %collective-permute-start.8 = (f32[64,128]{1,0:T(8,128)S(1)}, f32[64,128]{1,0:T(8,128)S(1)}, u32[]{:S(2)}, u32[]{:S(2)}) collective-permute-start(f32[64,128]{1,0:T(8,128)S(1)} %row_sums.7.refs_0_), channel_id=1, source_target_pairs={{0,1},{1,0},{2,3},{3,2},{4,5},{5,4},{6,7},{7,6},{8,9},{9,8},{10,11... | collective-permute-start | bytes 98312 | tf_op jit(solution)/shard_map/ppermute | solution.py:44
  29.7 14.8 %copy-start.1 = (s32[4]{0:T(128)S(1)}, s32[4]{0:T(128)}, u32[]{:S(2)}) copy-start(s32[4]{0:T(128)} %lengths.1) | copy-start | bytes 52
  39.3 1.5 %collective-permute-start.9 = (f32[8,4,1664]{2,1,0:T(4,128)S(1)}, f32[8,4,1664]{2,1,0:T(4,128)S(1)}, u32[]{:S(2)}, u32[]{:S(2)}) collective-permute-start(f32[8,4,1664]{2,1,0:T(4,128)S(1)} %get-tuple-element.65), channel_id=1, source_target_pairs={{0,1},{1,0},{2,3},{3,2},{4,5},{5,4},{6,7},{7,6},{8,9},{9,8},{10,11... | collective-permute-start | bytes 638984 | tf_op jit(solution)/shard_map/ppermute | solution.py:44
  40.9 5.8 %collective-permute-start.10 = (bf16[2,4,1664]{2,1,0:T(4,128)(2,1)S(1)}, bf16[2,4,1664]{2,1,0:T(4,128)(2,1)S(1)}, u32[]{:S(2)}, u32[]{:S(2)}) collective-permute-start(bf16[2,4,1664]{2,1,0:T(4,128)(2,1)S(1)} %get-tuple-element.66.refs_0_), channel_id=1, source_target_pairs={{0,2},{2,0},{4,6},{6,4},{8,10},{10,8},{12,14},{14,12},{1,3},{3,1},... | collective-permute-start | bytes 79880 | tf_op jit(solution)/shard_map/ppermute | solution.py:538
  41.1 5.6 %collective-permute-start.11 = (bf16[2,4,1664]{2,1,0:T(4,128)(2,1)S(1)}, bf16[2,4,1664]{2,1,0:T(4,128)(2,1)S(1)}, u32[]{:S(2)}, u32[]{:S(2)}) collective-permute-start(bf16[2,4,1664]{2,1,0:T(4,128)(2,1)S(1)} %get-tuple-element.68), channel_id=1, source_target_pairs={{0,4},{2,6},{4,0},{6,2},{8,12},{10,14},{12,8},{14,10},{1,5},{3,7},... | collective-permute-start | bytes 79880 | tf_op jit(solution)/shard_map/ppermute | solution.py:538
  42.3 4.7 %collective-permute-start.12 = (bf16[2,4,1664]{2,1,0:T(4,128)(2,1)S(1)}, bf16[2,4,1664]{2,1,0:T(4,128)(2,1)S(1)}, u32[]{:S(2)}, u32[]{:S(2)}) collective-permute-start(bf16[2,4,1664]{2,1,0:T(4,128)(2,1)S(1)} %get-tuple-element.69), channel_id=1, source_target_pairs={{0,6},{2,4},{4,2},{6,0},{8,14},{10,12},{12,10},{14,8},{1,7},{3,5},... | collective-permute-start | bytes 79880 | tf_op jit(solution)/shard_map/ppermute | solution.py:538
  47.0 5.6 %collective-permute-start.13 = (bf16[4,4,1664]{2,1,0:T(4,128)(2,1)S(1)}, bf16[4,4,1664]{2,1,0:T(4,128)(2,1)S(1)}, u32[]{:S(2)}, u32[]{:S(2)}) collective-permute-start(bf16[4,4,1664]{2,1,0:T(4,128)(2,1)S(1)} %pack.1.refs_1_.refs_0_), channel_id=1, source_target_pairs={{0,8},{2,10},{4,12},{6,14},{8,0},{10,2},{12,4},{14,6},{1,9},{3,11}... | collective-permute-start | bytes 159752 | tf_op jit(solution)/shard_map/ppermute | solution.py:538
  56.1 1.3 %collective-permute-start.14 = (bf16[4,6144]{1,0:T(4,128)(2,1)S(1)}, bf16[4,6144]{1,0:T(4,128)(2,1)S(1)}, u32[]{:S(2)}, u32[]{:S(2)}) collective-permute-start(bf16[4,6144]{1,0:T(4,128)(2,1)S(1)} %get-tuple-element.79), channel_id=1, source_target_pairs={{0,1},{1,0},{2,3},{3,2},{4,5},{5,4},{6,7},{7,6},{8,9},{9,8},{10,11... | collective-permute-start | bytes 147464 | tf_op jit(solution)/shard_map/ppermute | solution.py:44
  57.5 5.1 %collective-permute-start.15 = (bf16[8,6144]{1,0:T(8,128)(2,1)S(1)}, bf16[8,6144]{1,0:T(8,128)(2,1)S(1)}, u32[]{:S(2)}, u32[]{:S(2)}) collective-permute-start(bf16[8,6144]{1,0:T(8,128)(2,1)S(1)} %pad_maximum_fusion.refs_1_.refs_0_), channel_id=1, source_target_pairs={{0,4},{4,8},{8,12},{12,14},{14,10},{10,6},{6,2},{2,0},{1,5},{5,9},... | collective-permute-start | bytes 294920 | tf_op jit(solution)/shard_map/ppermute | solution.py:55
  58.1 4.8 %collective-permute-start.16 = (bf16[8,6144]{1,0:T(8,128)(2,1)S(1)}, bf16[8,6144]{1,0:T(8,128)(2,1)S(1)}, u32[]{:S(2)}, u32[]{:S(2)}) collective-permute-start(bf16[8,6144]{1,0:T(8,128)(2,1)S(1)} %pad_maximum_fusion.refs_1_.refs_0_), channel_id=1, source_target_pairs={{0,2},{4,0},{8,4},{12,8},{14,12},{10,14},{6,10},{2,6},{1,3},{5,1},... | collective-permute-start | bytes 294920 | tf_op jit(solution)/shard_map/ppermute | solution.py:55
  63.0 4.8 %collective-permute-start.17 = (bf16[8,6144]{1,0:T(8,128)(2,1)S(1)}, bf16[8,6144]{1,0:T(8,128)(2,1)S(1)}, u32[]{:S(2)}, u32[]{:S(2)}) collective-permute-start(bf16[8,6144]{1,0:T(8,128)(2,1)S(1)} %collective-permute-done.15.refs_1_), channel_id=1, source_target_pairs={{0,4},{4,8},{8,12},{12,14},{14,10},{10,6},{6,2},{2,0},{1,5},{5,9},... | collective-permute-start | bytes 294920 | tf_op jit(solution)/shard_map/ppermute | solution.py:55
  64.7 4.6 %collective-permute-start.18 = (bf16[8,6144]{1,0:T(8,128)(2,1)S(1)}, bf16[8,6144]{1,0:T(8,128)(2,1)S(1)}, u32[]{:S(2)}, u32[]{:S(2)}) collective-permute-start(bf16[8,6144]{1,0:T(8,128)(2,1)S(1)} %collective-permute-done.16.refs_2_), channel_id=1, source_target_pairs={{0,2},{4,0},{8,4},{12,8},{14,12},{10,14},{6,10},{2,6},{1,3},{5,1},... | collective-permute-start | bytes 294920 | tf_op jit(solution)/shard_map/ppermute | solution.py:55
  69.4 4.8 %collective-permute-start.19 = (bf16[8,6144]{1,0:T(8,128)(2,1)S(1)}, bf16[8,6144]{1,0:T(8,128)(2,1)S(1)}, u32[]{:S(2)}, u32[]{:S(2)}) collective-permute-start(bf16[8,6144]{1,0:T(8,128)(2,1)S(1)} %collective-permute-done.17.refs_1_.refs_3_), channel_id=1, source_target_pairs={{0,4},{4,8},{8,12},{12,14},{14,10},{10,6},{6,2},{2,0},{1,5},{5,9},... | collective-permute-start | bytes 294920 | tf_op jit(solution)/shard_map/ppermute | solution.py:55
  70.4 4.6 %collective-permute-start.20 = (bf16[8,6144]{1,0:T(8,128)(2,1)S(1)}, bf16[8,6144]{1,0:T(8,128)(2,1)S(1)}, u32[]{:S(2)}, u32[]{:S(2)}) collective-permute-start(bf16[8,6144]{1,0:T(8,128)(2,1)S(1)} %collective-permute-done.18.refs_2_.refs_4_), channel_id=1, source_target_pairs={{0,2},{4,0},{8,4},{12,8},{14,12},{10,14},{6,10},{2,6},{1,3},{5,1},... | collective-permute-start | bytes 294920 | tf_op jit(solution)/shard_map/ppermute | solution.py:55
  75.0 4.8 %collective-permute-start.21 = (bf16[8,3072]{1,0:T(8,128)(2,1)S(1)}, bf16[8,3072]{1,0:T(8,128)(2,1)S(1)}, u32[]{:S(2)}, u32[]{:S(2)}) collective-permute-start(bf16[8,3072]{1,0:T(8,128)(2,1)S(1)} %slice.14), channel_id=1, source_target_pairs={{0,4},{4,8},{8,12},{12,14},{14,10},{10,6},{6,2},{2,0},{1,5},{5,9},... | collective-permute-start | bytes 147464 | tf_op jit(solution)/shard_map/ppermute | solution.py:55
  76.7 4.1 %collective-permute-start.22 = (bf16[8,3072]{1,0:T(8,128)(2,1)S(1)}, bf16[8,3072]{1,0:T(8,128)(2,1)S(1)}, u32[]{:S(2)}, u32[]{:S(2)}) collective-permute-start(bf16[8,3072]{1,0:T(8,128)(2,1)S(1)} %slice.15), channel_id=1, source_target_pairs={{0,2},{4,0},{8,4},{12,8},{14,12},{10,14},{6,10},{2,6},{1,3},{5,1},... | collective-permute-start | bytes 147464 | tf_op jit(solution)/shard_map/ppermute | solution.py:55
  85.9 1.6 %collective-permute-start.23 = (f32[4,8,2304]{2,1,0:T(8,128)S(1)}, f32[4,8,2304]{2,1,0:T(8,128)S(1)}, u32[]{:S(2)}, u32[]{:S(2)}) collective-permute-start(f32[4,8,2304]{2,1,0:T(8,128)S(1)} %get-tuple-element.94), channel_id=1, source_target_pairs={{0,1},{1,0},{2,3},{3,2},{4,5},{5,4},{6,7},{7,6},{8,9},{9,8},{10,11... | collective-permute-start | bytes 884744 | tf_op jit(solution)/shard_map/ppermute | solution.py:44

commit v15 on v11

--- a/solution.py
+++ b/solution.py
@@ -299,6 +299,8 @@
         block = arrived[i][j].astype(jnp.float32)
         for r in range(rows):
             spread[r, pl.ds(jnp.bitwise_xor(me, d), 1), :] = block[r : r + 1, :]
+    starts = range(0, query_cols, DH)
+    ready = []
     for r in range(rows):
         given = spread[r]
         cos, sin = cosine[r : r + 1, :], sine[r : r + 1, :]
@@ -307,11 +309,11 @@
             turned = jnp.concatenate([a * cos - b * sin, b * cos + a * sin], axis=1)
             return turned.astype(jnp.bfloat16)
 
-        starts = range(0, query_cols, DH)
         q = turn(
             jnp.concatenate([given[:, c : c + DH // 2] for c in starts], axis=0),
             jnp.concatenate([given[:, c + DH // 2 : c + DH] for c in starts], axis=0),
         )
+        q = (q.astype(jnp.float32) * score_scale).astype(jnp.bfloat16)
         new = [
             given[i : i + 1, query_cols:] + given[i + 1 : i + 2, query_cols:]
             for i in range(0, n, 2)
@@ -319,10 +321,11 @@
         new_key = turn(new[0], new[1]).astype(jnp.float32)
         new_value = jnp.concatenate(new[2:], axis=1)
         scores = lax.dot_general(q, keys[r], contract, preferred_element_type=jnp.float32)
-        scores = scores * score_scale
+        own_score = jnp.sum(q.astype(jnp.float32) * new_key, axis=1, keepdims=True)
+        ready.append((scores, own_score, new_value))
+    for r, (scores, own_score, new_value) in enumerate(ready):
         place = lax.broadcasted_iota(jnp.int32, scores.shape, 1)
         scores = jnp.where(place < lengths[r], scores, -1e30)
-        own_score = jnp.sum(q.astype(jnp.float32) * new_key, axis=1, keepdims=True) * score_scale
         highest = jnp.maximum(jnp.max(scores, axis=1, keepdims=True), own_score)
         weights = jnp.exp(scores - highest)
         own_weight = jnp.exp(own_score - highest)
@@ -377,13 +380,14 @@
         first = 0
         for weight in weights:
             last = first + weight.shape[0]
-            if start <= first and last <= start + half:
+            low, high = max(first, start), min(last, start + half)
+            if low < high:
                 term = jnp.dot(
-                    x[:, first - start : last - start],
-                    weight[...],
+                    x[:, low - start : high - start],
+                    weight[low - first : high - first, :],
                     preferred_element_type=jnp.float32,
                 )
-                if first == 0:
+                if low == 0:
                     total[...] = term
                 else:
                     total[...] += term
@@ -536,9 +540,9 @@
     other_sums = swap_pair(sums)
     weights.append(weight)
     gain = norm_gain.astype(jnp.float32)[None, :]
-    piece = output_weight.shape[0] // 4
+    unit = output_weight.shape[0] // 24
     keep, give, weight = project(
-        (sums, other_sums), gain, shards, far, weights, output_weight, 2 * piece
+        (sums, other_sums), gain, shards, far, weights, output_weight, 8 * unit
     )
     weights = [weight]
 
@@ -552,15 +556,17 @@
     across = pack([(0, 1), (1, 1), (2, 1), (3, 1)], *arrived)
     last = exchange(across, 4)
     values = load_cache(cache_values, [across])
+    weight = load(4 * unit, [(output_weight, 8 * unit, 4 * unit, 0)], [across])
     values, (last,) = before(values, last)
+    weight, (last,) = before(weight, last)
+    weights.append(weight)
     arrived = [*arrived, last]
     mine, other = attend(cache_lengths, arrived, cosine, sine, keys, values)
     shard = jnp.concatenate([mine, swap_pair(other)], axis=0)
 
     left = right = shard
     shards = [shard]
-    done = 2 * piece
-    piece = piece // 2
+    done, piece = 12 * unit, 3 * unit
 
     for step in range(1, n // 2):
         arrived = shards[-2:]

time: 89.6 us -> 89.2 us (level)
  Pallas kernels: 46 us -> 47.2 us
  waiting for transfers between devices: 20.2 us -> 19 us
    ppermute x4, waiting for transfers between devices: 3.13 us -> 0.75 us  [exchange(): return lax.ppermute(blocks, 'gx', [(i, i ^ d) for i in range(n)])]
    pallas_call x8 -> x9, Pallas kernels: 20.7 us -> 23.1 us  [load(): pl.pallas_call(lambda *refs: load_kernel([job[1:] for job in jobs], *refs...]
  transfers between devices with their start and end apart: 24 -> 24, of which waited for: 18 -> 19; matrix products, arithmetic and copies ran while one was open for 0% -> 0% of each run, Pallas kernels for 29% -> 32%
where the time goes in v15:
time: 89.2 us; the launch traced here: 89 us
  Pallas kernels  47.2 us (53%)
  starting transfers between devices  21.7 us (24%)
  waiting for transfers between devices  19 us (21%)
    pallas_call x9, Pallas kernels, load(): pl.pallas_call(lambda *refs: load_kernel([job[1:] for job in jobs], *refs...  23.1 us
    ppermute x8, starting transfers between devices, step(): lax.ppermute(left, 'gx', self.onward)  13.3 us
    pallas_call x1, Pallas kernels, project(): pl.pallas_call(lambda *refs: project_kernel(n, len(weights), *refs), out_...  11.2 us
    ppermute x8, waiting for transfers between devices, step(): lax.ppermute(right, 'gx', self.back)  9.52 us
    ppermute x4, waiting for transfers between devices, swap_pair(): return lax.ppermute(x, 'gy', [(0, 1), (1, 0)])  5.26 us
    pallas_call x1, Pallas kernels, output_project(): pl.pallas_call(lambda *refs: output_kernel(n, *refs), out_shape=[shape, s...  5.05 us
    pallas_call x2, Pallas kernels, load_cache(): pl.pallas_call(load_cache_kernel, out_shape=pltpu.VMEM(cache.shape, cache...  4.42 us
    ppermute x8, starting transfers between devices, step(): lax.ppermute(right, 'gx', self.back)  4.04 us
  transfers between devices with their start and end apart: 24, of which 19 were waited for; matrix products, arithmetic and copies ran while one was open for 0% of the time, Pallas kernels for 32%

profile of v15, /device:TPU:0, one launch (start us, length us, event | category | flops | bytes accessed | tf_op | source)
XLA Modules:
  0.0 89.0 jit_solution(14315899975732122977)
XLA Ops:
  0.0 3.0 %collective-permute-start = (bf16[8,9216]{1,0:T(8,128)(2,1)}, bf16[8,9216]{1,0:T(8,128)(2,1)S(1)}, u32[]{:S(2)}, u32[]{:S(2)}) collective-permute-start(bf16[8,9216]{1,0:T(8,128)(2,1)} %refs_3_.1), channel_id=1, source_target_pairs={{0,4},{4,8},{8,12},{12,14},{14,10},{10,6},{6,2},{2,0},{1,5},{5,9},... | collective-permute-start | bytes 442376 | tf_op jit(solution)/shard_map/ppermute | solution.py:55
  3.0 3.1 %load.9.refs_12_ = bf16[384,9216]{1,0:T(8,128)(2,1)S(1)} custom-call(bf16[1536,9216]{1,0:T(8,128)(2,1)} %refs_0_.14), custom_call_target="tpu_custom_call" | custom-call | tf_op jit(solution)/shard_map/load/pallas_call | solution.py:103
  6.1 1.0 %collective-permute-done.refs_1_.refs_4_ = bf16[8,9216]{1,0:T(8,128)(2,1)S(1)} collective-permute-done((bf16[8,9216]{1,0:T(8,128)(2,1)}, bf16[8,9216]{1,0:T(8,128)(2,1)S(1)}, u32[]{:S(2)}, u32[]{:S(2)}) %collective-permute-start) | collective-permute-done | bytes 147488 | tf_op jit(solution)/shard_map/ppermute | solution.py:55
  7.1 1.4 %collective-permute-done.1.refs_2_.refs_5_ = bf16[8,9216]{1,0:T(8,128)(2,1)S(1)} collective-permute-done((bf16[8,9216]{1,0:T(8,128)(2,1)}, bf16[8,9216]{1,0:T(8,128)(2,1)S(1)}, u32[]{:S(2)}, u32[]{:S(2)}) %collective-permute-start.1) | collective-permute-done | bytes 147488 | tf_op jit(solution)/shard_map/ppermute | solution.py:55
  8.5 1.6 %collective-permute-start.2 = (bf16[8,9216]{1,0:T(8,128)(2,1)S(1)}, bf16[8,9216]{1,0:T(8,128)(2,1)S(1)}, u32[]{:S(2)}, u32[]{:S(2)}) collective-permute-start(bf16[8,9216]{1,0:T(8,128)(2,1)S(1)} %collective-permute-done.refs_1_.refs_4_), channel_id=1, source_target_pairs={{0,4},{4,8},{8,12},{12,14},{14,10},{10,6},{6,2},{2,0},{1,5},{5,9},... | collective-permute-start | bytes 442376 | tf_op jit(solution)/shard_map/ppermute | solution.py:55
  10.1 0.4 collective-permute-start.3
  10.8 3.1 %load.10.refs_13_ = bf16[384,9216]{1,0:T(8,128)(2,1)S(1)} custom-call(bf16[1536,9216]{1,0:T(8,128)(2,1)} %refs_0_.14, bf16[8,9216]{1,0:T(8,128)(2,1)S(1)} %collective-permute-done.refs_1_.refs_4_, bf16[8,9216]{1,0:T(8,128)(2,1)S(1)} %collective-permute-done.1.refs_2_.refs_5_), custom_call_target="tpu_custom_call" | custom-call | tf_op jit(solution)/shard_map/load/pallas_call | solution.py:103
  13.9 1.3 %collective-permute-done.3.refs_2_.refs_7_ = bf16[8,9216]{1,0:T(8,128)(2,1)S(1)} collective-permute-done((bf16[8,9216]{1,0:T(8,128)(2,1)S(1)}, bf16[8,9216]{1,0:T(8,128)(2,1)S(1)}, u32[]{:S(2)}, u32[]{:S(2)}) %collective-permute-start.3) | collective-permute-done | bytes 147488 | tf_op jit(solution)/shard_map/ppermute | solution.py:55
  15.3 1.6 %collective-permute-start.4 = (bf16[8,9216]{1,0:T(8,128)(2,1)S(1)}, bf16[8,9216]{1,0:T(8,128)(2,1)S(1)}, u32[]{:S(2)}, u32[]{:S(2)}) collective-permute-start(bf16[8,9216]{1,0:T(8,128)(2,1)S(1)} %collective-permute-done.2.refs_1_.refs_6_), channel_id=1, source_target_pairs={{0,4},{4,8},{8,12},{12,14},{14,10},{10,6},{6,2},{2,0},{1,5},{5,9},... | collective-permute-start | bytes 442376 | tf_op jit(solution)/shard_map/ppermute | solution.py:55
  16.8 0.4 collective-permute-start.5
  17.3 3.1 %load.11.refs_14_ = bf16[384,9216]{1,0:T(8,128)(2,1)S(1)} custom-call(bf16[1536,9216]{1,0:T(8,128)(2,1)} %refs_0_.14, bf16[8,9216]{1,0:T(8,128)(2,1)S(1)} %collective-permute-done.2.refs_1_.refs_6_, bf16[8,9216]{1,0:T(8,128)(2,1)S(1)} %collective-permute-done.3.refs_2_.refs_7_), custom_call_target="tpu_custom_call" | custom-call | tf_op jit(solution)/shard_map/load/pallas_call | solution.py:103
  20.6 1.4 %collective-permute-done.5.refs_2_.refs_3_.refs_9_ = bf16[8,9216]{1,0:T(8,128)(2,1)S(1)} collective-permute-done((bf16[8,9216]{1,0:T(8,128)(2,1)S(1)}, bf16[8,9216]{1,0:T(8,128)(2,1)S(1)}, u32[]{:S(2)}, u32[]{:S(2)}) %collective-permute-start.5) | collective-permute-done | bytes 147488 | tf_op jit(solution)/shard_map/ppermute | solution.py:55
  22.0 1.9 %collective-permute-start.6 = (bf16[8,4608]{1,0:T(8,128)(2,1)S(1)}, bf16[8,4608]{1,0:T(8,128)(2,1)S(1)}, u32[]{:S(2)}, u32[]{:S(2)}) collective-permute-start(bf16[8,4608]{1,0:T(8,128)(2,1)S(1)} %slice.12), channel_id=1, source_target_pairs={{0,4},{4,8},{8,12},{12,14},{14,10},{10,6},{6,2},{2,0},{1,5},{5,9},... | collective-permute-start | bytes 221192 | tf_op jit(solution)/shard_map/ppermute | solution.py:55
  24.1 3.4 %load.12.refs_15_ = bf16[512,9216]{1,0:T(8,128)(2,1)S(1)} custom-call(bf16[1536,9216]{1,0:T(8,128)(2,1)} %refs_0_.14, bf16[64,9216]{1,0:T(8,128)(2,1)} %refs_1_.1, bf16[8,9216]{1,0:T(8,128)(2,1)S(1)} %collective-permute-done.4.refs_1_.refs_2_.refs_8_, bf16[8,9216]{1,0:T(8,128)(2,1)S(1)} %collective-permute-done.5.refs_2_.refs_3_.refs_9_), custom_call_target="tpu_custom_call" | custom-call | tf_op jit(solution)/shard_map/load/pallas_call | solution.py:103
  27.6 0.7 collective-permute-done.7.refs_2_.refs_11_
  28.5 1.2 %collective-permute-done.8.refs_1_ = f32[64,128]{1,0:T(8,128)S(1)} collective-permute-done((f32[64,128]{1,0:T(8,128)S(1)}, f32[64,128]{1,0:T(8,128)S(1)}, u32[]{:S(2)}, u32[]{:S(2)}) %collective-permute-start.8) | collective-permute-done | bytes 32800 | tf_op jit(solution)/shard_map/ppermute | solution.py:44
  29.7 11.2 %project.1 = (f32[8,4,1664]{2,1,0:T(4,128)S(1)}, f32[8,4,1664]{2,1,0:T(4,128)S(1)}, bf16[2048,2304]{1,0:T(8,128)(2,1)S(1)}) custom-call(f32[64,128]{1,0:T(8,128)S(1)} %row_sums.7.refs_0_, f32[64,128]{1,0:T(8,128)S(1)} %collective-permute-done.8.refs_1_, f32[1,9216]{1,0:T(1,128)S(1)} %bitcast.3, bf16[8,9216]{1,0:T(8,128)(2,1)S(1)} %copy-done, ...), custom_call_target="tpu_custom_call" | custom-call | tf_op jit(solution)/shard_map/project/pallas_call | solution.py:231
  41.1 1.3 %collective-permute-done.9.got = f32[8,4,1664]{2,1,0:T(4,128)S(1)} collective-permute-done((f32[8,4,1664]{2,1,0:T(4,128)S(1)}, f32[8,4,1664]{2,1,0:T(4,128)S(1)}, u32[]{:S(2)}, u32[]{:S(2)}) %collective-permute-start.9) | collective-permute-done | bytes 213024 | tf_op jit(solution)/shard_map/ppermute | solution.py:44
  42.6 1.2 %collective-permute-start.11 = (bf16[2,4,1664]{2,1,0:T(4,128)(2,1)S(1)}, bf16[2,4,1664]{2,1,0:T(4,128)(2,1)S(1)}, u32[]{:S(2)}, u32[]{:S(2)}) collective-permute-start(bf16[2,4,1664]{2,1,0:T(4,128)(2,1)S(1)} %get-tuple-element.69), channel_id=1, source_target_pairs={{0,4},{2,6},{4,0},{6,2},{8,12},{10,14},{12,8},{14,10},{1,5},{3,7},... | collective-permute-start | bytes 79880 | tf_op jit(solution)/shard_map/ppermute | solution.py:550
  43.8 2.2 %collective-permute-start.12 = (bf16[2,4,1664]{2,1,0:T(4,128)(2,1)S(1)}, bf16[2,4,1664]{2,1,0:T(4,128)(2,1)S(1)}, u32[]{:S(2)}, u32[]{:S(2)}) collective-permute-start(bf16[2,4,1664]{2,1,0:T(4,128)(2,1)S(1)} %get-tuple-element.70), channel_id=1, source_target_pairs={{0,6},{2,4},{4,2},{6,0},{8,14},{10,12},{12,10},{14,8},{1,7},{3,5},... | collective-permute-start | bytes 79880 | tf_op jit(solution)/shard_map/ppermute | solution.py:550
  46.0 2.2 %load_cache.2.refs_7_ = bf16[4,2048,256]{2,1,0:T(8,128)(2,1)S(1)} custom-call(bf16[4,2048,256]{2,1,0:T(8,128)(2,1)} %source.2, bf16[2,4,1664]{2,1,0:T(4,128)(2,1)S(1)} %get-tuple-element.67.refs_0_), custom_call_target="tpu_custom_call" | custom-call | tf_op jit(solution)/shard_map/load_cache/pallas_call | solution.py:125
  48.2 0.3 collective-permute-done.12.refs_3_
  48.6 0.5 collective-permute-start.13
  49.1 2.4 %load.13.refs_10_ = bf16[1024,2304]{1,0:T(8,128)(2,1)S(1)} custom-call(bf16[6144,2304]{1,0:T(8,128)(2,1)} %refs_0_.19, bf16[4,4,1664]{2,1,0:T(4,128)(2,1)S(1)} %pack.1.refs_1_.refs_0_), custom_call_target="tpu_custom_call" | custom-call | tf_op jit(solution)/shard_map/load/pallas_call | solution.py:103
  51.5 2.2 %load_cache.3.refs_8_ = bf16[4,2048,256]{2,1,0:T(8,128)(2,1)S(1)} custom-call(bf16[4,2048,256]{2,1,0:T(8,128)(2,1)} %source.3, bf16[4,4,1664]{2,1,0:T(4,128)(2,1)S(1)} %pack.1.refs_1_.refs_0_), custom_call_target="tpu_custom_call" | custom-call | tf_op jit(solution)/shard_map/load_cache/pallas_call | solution.py:125
  53.7 0.4 collective-permute-done.13.refs_4_
  54.2 2.7 %attend.1 = (bf16[4,6144]{1,0:T(4,128)(2,1)S(1)}, bf16[4,6144]{1,0:T(4,128)(2,1)S(1)}) custom-call(s32[4]{0:T(128)S(1)} %copy-done.1, bf16[2,4,1664]{2,1,0:T(4,128)(2,1)S(1)} %get-tuple-element.71.refs_0_, bf16[2,4,1664]{2,1,0:T(4,128)(2,1)S(1)} %collective-permute-done.10.refs_1_, bf16[2,4,1664]{2,1,0:T(4,128)(2,1)S(1)} %collective-permute-done.11.refs_2_, ...), custom_call_target="tpu_custom_call" | custom-call | tf_op jit(solution)/shard_map/attend/pallas_call | solution.py:353
  57.0 1.2 %collective-permute-done.14 = bf16[4,6144]{1,0:T(4,128)(2,1)S(1)} collective-permute-done((bf16[4,6144]{1,0:T(4,128)(2,1)S(1)}, bf16[4,6144]{1,0:T(4,128)(2,1)S(1)}, u32[]{:S(2)}, u32[]{:S(2)}) %collective-permute-start.14) | collective-permute-done | bytes 49184 | tf_op jit(solution)/shard_map/ppermute | solution.py:44
  58.3 0.7 collective-permute-start.15
  58.9 1.4 %collective-permute-start.16 = (bf16[8,6144]{1,0:T(8,128)(2,1)S(1)}, bf16[8,6144]{1,0:T(8,128)(2,1)S(1)}, u32[]{:S(2)}, u32[]{:S(2)}) collective-permute-start(bf16[8,6144]{1,0:T(8,128)(2,1)S(1)} %pad_maximum_fusion.refs_1_.refs_0_), channel_id=1, source_target_pairs={{0,2},{4,0},{8,4},{12,8},{14,12},{10,14},{6,10},{2,6},{1,3},{5,1},... | collective-permute-start | bytes 294920 | tf_op jit(solution)/shard_map/ppermute | solution.py:55
  60.4 2.0 %load.14.refs_11_ = bf16[768,2304]{1,0:T(8,128)(2,1)S(1)} custom-call(bf16[6144,2304]{1,0:T(8,128)(2,1)} %refs_0_.19, bf16[8,6144]{1,0:T(8,128)(2,1)S(1)} %pad_maximum_fusion.refs_1_.refs_0_), custom_call_target="tpu_custom_call" | custom-call | tf_op jit(solution)/shard_map/load/pallas_call | solution.py:103
  62.4 1.0 %collective-permute-done.15.refs_1_ = bf16[8,6144]{1,0:T(8,128)(2,1)S(1)} collective-permute-done((bf16[8,6144]{1,0:T(8,128)(2,1)S(1)}, bf16[8,6144]{1,0:T(8,128)(2,1)S(1)}, u32[]{:S(2)}, u32[]{:S(2)}) %collective-permute-start.15) | collective-permute-done | bytes 98336 | tf_op jit(solution)/shard_map/ppermute | solution.py:55
  63.4 0.4 collective-permute-done.16.refs_2_
  63.8 1.8 %collective-permute-start.17 = (bf16[8,6144]{1,0:T(8,128)(2,1)S(1)}, bf16[8,6144]{1,0:T(8,128)(2,1)S(1)}, u32[]{:S(2)}, u32[]{:S(2)}) collective-permute-start(bf16[8,6144]{1,0:T(8,128)(2,1)S(1)} %collective-permute-done.15.refs_1_), channel_id=1, source_target_pairs={{0,4},{4,8},{8,12},{12,14},{14,10},{10,6},{6,2},{2,0},{1,5},{5,9},... | collective-permute-start | bytes 294920 | tf_op jit(solution)/shard_map/ppermute | solution.py:55
  65.8 2.0 %load.15.refs_12_ = bf16[768,2304]{1,0:T(8,128)(2,1)S(1)} custom-call(bf16[6144,2304]{1,0:T(8,128)(2,1)} %refs_0_.19, bf16[8,6144]{1,0:T(8,128)(2,1)S(1)} %collective-permute-done.15.refs_1_, bf16[8,6144]{1,0:T(8,128)(2,1)S(1)} %collective-permute-done.16.refs_2_), custom_call_target="tpu_custom_call" | custom-call | tf_op jit(solution)/shard_map/load/pallas_call | solution.py:103
  67.8 0.6 collective-permute-done.17.refs_1_.refs_3_
  68.4 1.8 %collective-permute-done.18.refs_2_.refs_4_ = bf16[8,6144]{1,0:T(8,128)(2,1)S(1)} collective-permute-done((bf16[8,6144]{1,0:T(8,128)(2,1)S(1)}, bf16[8,6144]{1,0:T(8,128)(2,1)S(1)}, u32[]{:S(2)}, u32[]{:S(2)}) %collective-permute-start.18) | collective-permute-done | bytes 98336 | tf_op jit(solution)/shard_map/ppermute | solution.py:55
  70.2 1.0 %collective-permute-start.19 = (bf16[8,6144]{1,0:T(8,128)(2,1)S(1)}, bf16[8,6144]{1,0:T(8,128)(2,1)S(1)}, u32[]{:S(2)}, u32[]{:S(2)}) collective-permute-start(bf16[8,6144]{1,0:T(8,128)(2,1)S(1)} %collective-permute-done.17.refs_1_.refs_3_), channel_id=1, source_target_pairs={{0,4},{4,8},{8,12},{12,14},{14,10},{10,6},{6,2},{2,0},{1,5},{5,9},... | collective-permute-start | bytes 294920 | tf_op jit(solution)/shard_map/ppermute | solution.py:55
  71.2 1.0 %collective-permute-start.20 = (bf16[8,6144]{1,0:T(8,128)(2,1)S(1)}, bf16[8,6144]{1,0:T(8,128)(2,1)S(1)}, u32[]{:S(2)}, u32[]{:S(2)}) collective-permute-start(bf16[8,6144]{1,0:T(8,128)(2,1)S(1)} %collective-permute-done.18.refs_2_.refs_4_), channel_id=1, source_target_pairs={{0,2},{4,0},{8,4},{12,8},{14,12},{10,14},{6,10},{2,6},{1,3},{5,1},... | collective-permute-start | bytes 294920 | tf_op jit(solution)/shard_map/ppermute | solution.py:55
  72.2 2.0 %load.16.refs_13_ = bf16[768,2304]{1,0:T(8,128)(2,1)S(1)} custom-call(bf16[6144,2304]{1,0:T(8,128)(2,1)} %refs_0_.19, bf16[8,6144]{1,0:T(8,128)(2,1)S(1)} %collective-permute-done.17.refs_1_.refs_3_, bf16[8,6144]{1,0:T(8,128)(2,1)S(1)} %collective-permute-done.18.refs_2_.refs_4_), custom_call_target="tpu_custom_call" | custom-call | tf_op jit(solution)/shard_map/load/pallas_call | solution.py:103
  74.2 0.8 collective-permute-done.19.refs_1_.refs_5_
  75.0 0.8 collective-permute-done.20.refs_2_.refs_6_
  75.8 1.7 %collective-permute-start.21 = (bf16[8,3072]{1,0:T(8,128)(2,1)S(1)}, bf16[8,3072]{1,0:T(8,128)(2,1)S(1)}, u32[]{:S(2)}, u32[]{:S(2)}) collective-permute-start(bf16[8,3072]{1,0:T(8,128)(2,1)S(1)} %slice.14), channel_id=1, source_target_pairs={{0,4},{4,8},{8,12},{12,14},{14,10},{10,6},{6,2},{2,0},{1,5},{5,9},... | collective-permute-start | bytes 147464 | tf_op jit(solution)/shard_map/ppermute | solution.py:55
  77.8 2.0 %load.17.refs_14_ = bf16[768,2304]{1,0:T(8,128)(2,1)S(1)} custom-call(bf16[6144,2304]{1,0:T(8,128)(2,1)} %refs_0_.19, bf16[8,6144]{1,0:T(8,128)(2,1)S(1)} %collective-permute-done.19.refs_1_.refs_5_, bf16[8,6144]{1,0:T(8,128)(2,1)S(1)} %collective-permute-done.20.refs_2_.refs_6_), custom_call_target="tpu_custom_call" | custom-call | tf_op jit(solution)/shard_map/load/pallas_call | solution.py:103
  79.9 1.7 %collective-permute-done.22.refs_8_ = bf16[8,3072]{1,0:T(8,128)(2,1)S(1)} collective-permute-done((bf16[8,3072]{1,0:T(8,128)(2,1)S(1)}, bf16[8,3072]{1,0:T(8,128)(2,1)S(1)}, u32[]{:S(2)}, u32[]{:S(2)}) %collective-permute-start.22) | collective-permute-done | bytes 49184 | tf_op jit(solution)/shard_map/ppermute | solution.py:55
  81.6 5.0 %output_project.1 = (f32[4,8,2304]{2,1,0:T(8,128)S(1)}, f32[4,8,2304]{2,1,0:T(8,128)S(1)}) custom-call(bf16[8,6144]{1,0:T(8,128)(2,1)S(1)} %pad_maximum_fusion.refs_1_.refs_0_, bf16[8,6144]{1,0:T(8,128)(2,1)S(1)} %collective-permute-done.15.refs_1_, bf16[8,6144]{1,0:T(8,128)(2,1)S(1)} %collective-permute-done.16.refs_2_, ...), custom_call_target="tpu_custom_call" | custom-call | tf_op jit(solution)/shard_map/output_project/pallas_call | solution.py:408
  86.7 1.6 %collective-permute-done.23 = f32[4,8,2304]{2,1,0:T(8,128)S(1)} collective-permute-done((f32[4,8,2304]{2,1,0:T(8,128)S(1)}, f32[4,8,2304]{2,1,0:T(8,128)S(1)}, u32[]{:S(2)}, u32[]{:S(2)}) %collective-permute-start.23) | collective-permute-done | bytes 294944 | tf_op jit(solution)/shard_map/ppermute | solution.py:44
  88.3 0.7 fusion
  (36 shorter events, 2.3 us)
Async XLA Ops:
  0.0 10.6 %copy-start = (bf16[8,9216]{1,0:T(8,128)(2,1)S(1)}, bf16[8,9216]{1,0:T(8,128)(2,1)}, u32[]{:S(2)}) copy-start(bf16[8,9216]{1,0:T(8,128)(2,1)} %refs_3_.1) | copy-start | bytes 442372
  0.0 7.1 %collective-permute-start = (bf16[8,9216]{1,0:T(8,128)(2,1)}, bf16[8,9216]{1,0:T(8,128)(2,1)S(1)}, u32[]{:S(2)}, u32[]{:S(2)}) collective-permute-start(bf16[8,9216]{1,0:T(8,128)(2,1)} %refs_3_.1), channel_id=1, source_target_pairs={{0,4},{4,8},{8,12},{12,14},{14,10},{10,6},{6,2},{2,0},{1,5},{5,9},... | collective-permute-start | bytes 442376 | tf_op jit(solution)/shard_map/ppermute | solution.py:55
  3.0 5.5 %collective-permute-start.1 = (bf16[8,9216]{1,0:T(8,128)(2,1)}, bf16[8,9216]{1,0:T(8,128)(2,1)S(1)}, u32[]{:S(2)}, u32[]{:S(2)}) collective-permute-start(bf16[8,9216]{1,0:T(8,128)(2,1)} %refs_3_.1), channel_id=1, source_target_pairs={{0,2},{4,0},{8,4},{12,8},{14,12},{10,14},{6,10},{2,6},{1,3},{5,1},... | collective-permute-start | bytes 442376 | tf_op jit(solution)/shard_map/ppermute | solution.py:55
  8.5 5.4 %collective-permute-start.2 = (bf16[8,9216]{1,0:T(8,128)(2,1)S(1)}, bf16[8,9216]{1,0:T(8,128)(2,1)S(1)}, u32[]{:S(2)}, u32[]{:S(2)}) collective-permute-start(bf16[8,9216]{1,0:T(8,128)(2,1)S(1)} %collective-permute-done.refs_1_.refs_4_), channel_id=1, source_target_pairs={{0,4},{4,8},{8,12},{12,14},{14,10},{10,6},{6,2},{2,0},{1,5},{5,9},... | collective-permute-start | bytes 442376 | tf_op jit(solution)/shard_map/ppermute | solution.py:55
  10.1 5.1 %collective-permute-start.3 = (bf16[8,9216]{1,0:T(8,128)(2,1)S(1)}, bf16[8,9216]{1,0:T(8,128)(2,1)S(1)}, u32[]{:S(2)}, u32[]{:S(2)}) collective-permute-start(bf16[8,9216]{1,0:T(8,128)(2,1)S(1)} %collective-permute-done.1.refs_2_.refs_5_), channel_id=1, source_target_pairs={{0,2},{4,0},{8,4},{12,8},{14,12},{10,14},{6,10},{2,6},{1,3},{5,1},... | collective-permute-start | bytes 442376 | tf_op jit(solution)/shard_map/ppermute | solution.py:55
  15.3 5.3 %collective-permute-start.4 = (bf16[8,9216]{1,0:T(8,128)(2,1)S(1)}, bf16[8,9216]{1,0:T(8,128)(2,1)S(1)}, u32[]{:S(2)}, u32[]{:S(2)}) collective-permute-start(bf16[8,9216]{1,0:T(8,128)(2,1)S(1)} %collective-permute-done.2.refs_1_.refs_6_), channel_id=1, source_target_pairs={{0,4},{4,8},{8,12},{12,14},{14,10},{10,6},{6,2},{2,0},{1,5},{5,9},... | collective-permute-start | bytes 442376 | tf_op jit(solution)/shard_map/ppermute | solution.py:55
  16.8 5.1 %collective-permute-start.5 = (bf16[8,9216]{1,0:T(8,128)(2,1)S(1)}, bf16[8,9216]{1,0:T(8,128)(2,1)S(1)}, u32[]{:S(2)}, u32[]{:S(2)}) collective-permute-start(bf16[8,9216]{1,0:T(8,128)(2,1)S(1)} %collective-permute-done.3.refs_2_.refs_7_), channel_id=1, source_target_pairs={{0,2},{4,0},{8,4},{12,8},{14,12},{10,14},{6,10},{2,6},{1,3},{5,1},... | collective-permute-start | bytes 442376 | tf_op jit(solution)/shard_map/ppermute | solution.py:55
  22.0 5.7 %collective-permute-start.6 = (bf16[8,4608]{1,0:T(8,128)(2,1)S(1)}, bf16[8,4608]{1,0:T(8,128)(2,1)S(1)}, u32[]{:S(2)}, u32[]{:S(2)}) collective-permute-start(bf16[8,4608]{1,0:T(8,128)(2,1)S(1)} %slice.12), channel_id=1, source_target_pairs={{0,4},{4,8},{8,12},{12,14},{14,10},{10,6},{6,2},{2,0},{1,5},{5,9},... | collective-permute-start | bytes 221192 | tf_op jit(solution)/shard_map/ppermute | solution.py:55
  23.9 4.5 %copy-start.2 = (bf16[9216]{0:T(1024)(128)(2,1)S(1)}, bf16[9216]{0:T(1024)(128)(2,1)}, u32[]{:S(2)}) copy-start(bf16[9216]{0:T(1024)(128)(2,1)} %param.9) | copy-start | bytes 55300
  23.9 4.4 %collective-permute-start.7 = (bf16[8,4608]{1,0:T(8,128)(2,1)S(1)}, bf16[8,4608]{1,0:T(8,128)(2,1)S(1)}, u32[]{:S(2)}, u32[]{:S(2)}) collective-permute-start(bf16[8,4608]{1,0:T(8,128)(2,1)S(1)} %slice.13), channel_id=1, source_target_pairs={{0,2},{4,0},{8,4},{12,8},{14,12},{10,14},{6,10},{2,6},{1,3},{5,1},... | collective-permute-start | bytes 221192 | tf_op jit(solution)/shard_map/ppermute | solution.py:55
  28.5 1.2 %collective-permute-start.8 = (f32[64,128]{1,0:T(8,128)S(1)}, f32[64,128]{1,0:T(8,128)S(1)}, u32[]{:S(2)}, u32[]{:S(2)}) collective-permute-start(f32[64,128]{1,0:T(8,128)S(1)} %row_sums.7.refs_0_), channel_id=1, source_target_pairs={{0,1},{1,0},{2,3},{3,2},{4,5},{5,4},{6,7},{7,6},{8,9},{9,8},{10,11... | collective-permute-start | bytes 98312 | tf_op jit(solution)/shard_map/ppermute | solution.py:44
  29.7 16.3 %copy-start.1 = (s32[4]{0:T(128)S(1)}, s32[4]{0:T(128)}, u32[]{:S(2)}) copy-start(s32[4]{0:T(128)} %lengths.1) | copy-start | bytes 52
  40.8 1.5 %collective-permute-start.9 = (f32[8,4,1664]{2,1,0:T(4,128)S(1)}, f32[8,4,1664]{2,1,0:T(4,128)S(1)}, u32[]{:S(2)}, u32[]{:S(2)}) collective-permute-start(f32[8,4,1664]{2,1,0:T(4,128)S(1)} %get-tuple-element.66), channel_id=1, source_target_pairs={{0,1},{1,0},{2,3},{3,2},{4,5},{5,4},{6,7},{7,6},{8,9},{9,8},{10,11... | collective-permute-start | bytes 638984 | tf_op jit(solution)/shard_map/ppermute | solution.py:44
  42.4 5.8 %collective-permute-start.10 = (bf16[2,4,1664]{2,1,0:T(4,128)(2,1)S(1)}, bf16[2,4,1664]{2,1,0:T(4,128)(2,1)S(1)}, u32[]{:S(2)}, u32[]{:S(2)}) collective-permute-start(bf16[2,4,1664]{2,1,0:T(4,128)(2,1)S(1)} %get-tuple-element.67.refs_0_), channel_id=1, source_target_pairs={{0,2},{2,0},{4,6},{6,4},{8,10},{10,8},{12,14},{14,12},{1,3},{3,1},... | collective-permute-start | bytes 79880 | tf_op jit(solution)/shard_map/ppermute | solution.py:550
  42.6 5.6 %collective-permute-start.11 = (bf16[2,4,1664]{2,1,0:T(4,128)(2,1)S(1)}, bf16[2,4,1664]{2,1,0:T(4,128)(2,1)S(1)}, u32[]{:S(2)}, u32[]{:S(2)}) collective-permute-start(bf16[2,4,1664]{2,1,0:T(4,128)(2,1)S(1)} %get-tuple-element.69), channel_id=1, source_target_pairs={{0,4},{2,6},{4,0},{6,2},{8,12},{10,14},{12,8},{14,10},{1,5},{3,7},... | collective-permute-start | bytes 79880 | tf_op jit(solution)/shard_map/ppermute | solution.py:550
  43.8 4.7 %collective-permute-start.12 = (bf16[2,4,1664]{2,1,0:T(4,128)(2,1)S(1)}, bf16[2,4,1664]{2,1,0:T(4,128)(2,1)S(1)}, u32[]{:S(2)}, u32[]{:S(2)}) collective-permute-start(bf16[2,4,1664]{2,1,0:T(4,128)(2,1)S(1)} %get-tuple-element.70), channel_id=1, source_target_pairs={{0,6},{2,4},{4,2},{6,0},{8,14},{10,12},{12,10},{14,8},{1,7},{3,5},... | collective-permute-start | bytes 79880 | tf_op jit(solution)/shard_map/ppermute | solution.py:550
  48.6 5.6 %collective-permute-start.13 = (bf16[4,4,1664]{2,1,0:T(4,128)(2,1)S(1)}, bf16[4,4,1664]{2,1,0:T(4,128)(2,1)S(1)}, u32[]{:S(2)}, u32[]{:S(2)}) collective-permute-start(bf16[4,4,1664]{2,1,0:T(4,128)(2,1)S(1)} %pack.1.refs_1_.refs_0_), channel_id=1, source_target_pairs={{0,8},{2,10},{4,12},{6,14},{8,0},{10,2},{12,4},{14,6},{1,9},{3,11}... | collective-permute-start | bytes 159752 | tf_op jit(solution)/shard_map/ppermute | solution.py:550
  56.9 1.3 %collective-permute-start.14 = (bf16[4,6144]{1,0:T(4,128)(2,1)S(1)}, bf16[4,6144]{1,0:T(4,128)(2,1)S(1)}, u32[]{:S(2)}, u32[]{:S(2)}) collective-permute-start(bf16[4,6144]{1,0:T(4,128)(2,1)S(1)} %get-tuple-element.80), channel_id=1, source_target_pairs={{0,1},{1,0},{2,3},{3,2},{4,5},{5,4},{6,7},{7,6},{8,9},{9,8},{10,11... | collective-permute-start | bytes 147464 | tf_op jit(solution)/shard_map/ppermute | solution.py:44
  58.3 5.1 %collective-permute-start.15 = (bf16[8,6144]{1,0:T(8,128)(2,1)S(1)}, bf16[8,6144]{1,0:T(8,128)(2,1)S(1)}, u32[]{:S(2)}, u32[]{:S(2)}) collective-permute-start(bf16[8,6144]{1,0:T(8,128)(2,1)S(1)} %pad_maximum_fusion.refs_1_.refs_0_), channel_id=1, source_target_pairs={{0,4},{4,8},{8,12},{12,14},{14,10},{10,6},{6,2},{2,0},{1,5},{5,9},... | collective-permute-start | bytes 294920 | tf_op jit(solution)/shard_map/ppermute | solution.py:55
  58.9 4.8 %collective-permute-start.16 = (bf16[8,6144]{1,0:T(8,128)(2,1)S(1)}, bf16[8,6144]{1,0:T(8,128)(2,1)S(1)}, u32[]{:S(2)}, u32[]{:S(2)}) collective-permute-start(bf16[8,6144]{1,0:T(8,128)(2,1)S(1)} %pad_maximum_fusion.refs_1_.refs_0_), channel_id=1, source_target_pairs={{0,2},{4,0},{8,4},{12,8},{14,12},{10,14},{6,10},{2,6},{1,3},{5,1},... | collective-permute-start | bytes 294920 | tf_op jit(solution)/shard_map/ppermute | solution.py:55
  63.8 4.6 %collective-permute-start.17 = (bf16[8,6144]{1,0:T(8,128)(2,1)S(1)}, bf16[8,6144]{1,0:T(8,128)(2,1)S(1)}, u32[]{:S(2)}, u32[]{:S(2)}) collective-permute-start(bf16[8,6144]{1,0:T(8,128)(2,1)S(1)} %collective-permute-done.15.refs_1_), channel_id=1, source_target_pairs={{0,4},{4,8},{8,12},{12,14},{14,10},{10,6},{6,2},{2,0},{1,5},{5,9},... | collective-permute-start | bytes 294920 | tf_op jit(solution)/shard_map/ppermute | solution.py:55
  65.5 4.6 %collective-permute-start.18 = (bf16[8,6144]{1,0:T(8,128)(2,1)S(1)}, bf16[8,6144]{1,0:T(8,128)(2,1)S(1)}, u32[]{:S(2)}, u32[]{:S(2)}) collective-permute-start(bf16[8,6144]{1,0:T(8,128)(2,1)S(1)} %collective-permute-done.16.refs_2_), channel_id=1, source_target_pairs={{0,2},{4,0},{8,4},{12,8},{14,12},{10,14},{6,10},{2,6},{1,3},{5,1},... | collective-permute-start | bytes 294920 | tf_op jit(solution)/shard_map/ppermute | solution.py:55
  70.2 4.9 %collective-permute-start.19 = (bf16[8,6144]{1,0:T(8,128)(2,1)S(1)}, bf16[8,6144]{1,0:T(8,128)(2,1)S(1)}, u32[]{:S(2)}, u32[]{:S(2)}) collective-permute-start(bf16[8,6144]{1,0:T(8,128)(2,1)S(1)} %collective-permute-done.17.refs_1_.refs_3_), channel_id=1, source_target_pairs={{0,4},{4,8},{8,12},{12,14},{14,10},{10,6},{6,2},{2,0},{1,5},{5,9},... | collective-permute-start | bytes 294920 | tf_op jit(solution)/shard_map/ppermute | solution.py:55
  71.2 4.6 %collective-permute-start.20 = (bf16[8,6144]{1,0:T(8,128)(2,1)S(1)}, bf16[8,6144]{1,0:T(8,128)(2,1)S(1)}, u32[]{:S(2)}, u32[]{:S(2)}) collective-permute-start(bf16[8,6144]{1,0:T(8,128)(2,1)S(1)} %collective-permute-done.18.refs_2_.refs_4_), channel_id=1, source_target_pairs={{0,2},{4,0},{8,4},{12,8},{14,12},{10,14},{6,10},{2,6},{1,3},{5,1},... | collective-permute-start | bytes 294920 | tf_op jit(solution)/shard_map/ppermute | solution.py:55
  75.8 4.1 %collective-permute-start.21 = (bf16[8,3072]{1,0:T(8,128)(2,1)S(1)}, bf16[8,3072]{1,0:T(8,128)(2,1)S(1)}, u32[]{:S(2)}, u32[]{:S(2)}) collective-permute-start(bf16[8,3072]{1,0:T(8,128)(2,1)S(1)} %slice.14), channel_id=1, source_target_pairs={{0,4},{4,8},{8,12},{12,14},{14,10},{10,6},{6,2},{2,0},{1,5},{5,9},... | collective-permute-start | bytes 147464 | tf_op jit(solution)/shard_map/ppermute | solution.py:55
  77.5 4.1 %collective-permute-start.22 = (bf16[8,3072]{1,0:T(8,128)(2,1)S(1)}, bf16[8,3072]{1,0:T(8,128)(2,1)S(1)}, u32[]{:S(2)}, u32[]{:S(2)}) collective-permute-start(bf16[8,3072]{1,0:T(8,128)(2,1)S(1)} %slice.15), channel_id=1, source_target_pairs={{0,2},{4,0},{8,4},{12,8},{14,12},{10,14},{6,10},{2,6},{1,3},{5,1},... | collective-permute-start | bytes 147464 | tf_op jit(solution)/shard_map/ppermute | solution.py:55
  86.7 1.6 %collective-permute-start.23 = (f32[4,8,2304]{2,1,0:T(8,128)S(1)}, f32[4,8,2304]{2,1,0:T(8,128)S(1)}, u32[]{:S(2)}, u32[]{:S(2)}) collective-permute-start(f32[4,8,2304]{2,1,0:T(8,128)S(1)} %get-tuple-element.96), channel_id=1, source_target_pairs={{0,1},{1,0},{2,3},{3,2},{4,5},{5,4},{6,7},{7,6},{8,9},{9,8},{10,11... | collective-permute-start | bytes 884744 | tf_op jit(solution)/shard_map/ppermute | solution.py:44

commit v16 on v14

--- a/solution.py
+++ b/solution.py
@@ -86,12 +86,6 @@
     sources, target, sems = refs[: len(jobs)], refs[-2], refs[-1]
     copies = []
     for i, (first, size, at) in enumerate(jobs):
-        if at is None:
-            at = target.shape[0] - 2 * size
-            odd = lax.rem(lax.axis_index("gx"), 2)
-            unused = pl.ds(pl.multiple_of(at + (1 - odd) * size, size), size)
-            at = pl.multiple_of(at + odd * size, size)
-            target[unused, :] = jnp.zeros((size, target.shape[1]), target.dtype)
         part = sources[i].at[pl.ds(first, size)]
         copies += start_copies(part, target.at[pl.ds(at, size)], sems.at[i], 4)
     for copy in copies:
@@ -152,32 +146,27 @@
     for ref in refs[:ready]:
         out[start : start + ref.shape[0], :] = ref[...]
         start += ref.shape[0]
-
-    def both_sums(ref):
+    rows = refs[ready].shape[0]
+    lane = lax.broadcasted_iota(jnp.int32, (rows, 128), 1)
+    for ref in refs[ready : ready + count]:
         x = ref[...].astype(jnp.float32)
         total = jnp.sum(x, axis=1, keepdims=True)
         square = jnp.sum(x * x, axis=1, keepdims=True)
-        lane = lax.broadcasted_iota(jnp.int32, (x.shape[0], 128), 1)
-        return jnp.where(lane == 0, total, jnp.where(lane == 1, square, 0.0))
-
-    for ref in refs[ready : ready + count]:
-        out[start : start + ref.shape[0], :] = both_sums(ref)
-        start += ref.shape[0]
-    halves = refs[ready + count : -1]
-    if halves:
-        out[start:, :] = both_sums(halves[0]) + both_sums(halves[1])
-
-
-def row_sums(shards, ready=(), halves=()):
-    rows = sum(a.shape[0] for a in (*ready, *shards, *halves[:1]))
+        both = jnp.where(lane == 0, total, jnp.where(lane == 1, square, 0.0))
+        out[start : start + rows, :] = both
+        start += rows
+
+
+def row_sums(shards, ready=(), after=()):
+    rows = shards[0].shape[0] * len(shards) + sum(r.shape[0] for r in ready)
     return pl.pallas_call(
         lambda *refs: sums_kernel(len(ready), len(shards), *refs),
         out_shape=jax.ShapeDtypeStruct((rows, 128), jnp.float32),
-        in_specs=[IN_VMEM] * (len(ready) + len(shards) + len(halves)),
+        in_specs=[IN_VMEM] * (len(ready) + len(shards)) + [ANY] * len(after),
         out_specs=IN_VMEM,
         compiler_params=pltpu.CompilerParams(vmem_limit_bytes=8 * MIB),
         name="row_sums",
-    )(*ready, *shards, *halves)
+    )(*ready, *shards, *after)
 
 
 def project_kernel(n, parts, *refs):
@@ -211,6 +200,11 @@
             else:
                 total[:, stripe] += term
             start = stripe.stop
+    last = slice(total.shape[1] - 128, total.shape[1])
+    lane = lax.broadcasted_iota(jnp.int32, (total.shape[0], 128), 1)
+    new = jnp.where(lane < 64, total[:, last], 0.0)
+    odd = lax.rem(lax.axis_index("gx"), 2)
+    total[:, last] = jnp.where(odd == 0, new, pltpu.roll(new, 64, 1))
     side = lax.axis_index("gy")
     local = rows // 2
     for i, owner in enumerate(owners(n)):
@@ -223,7 +217,7 @@
 def project(sums, gain, shards, far, weights):
     n = len(shards) + 1
     rows, width = shards[0].shape
-    stripe = sum(w.shape[0] for w in weights)
+    stripe = sum(w.shape[0] for w in weights) + 64
     shape = jax.ShapeDtypeStruct((n, rows // 2, stripe), jnp.float32)
     return pl.pallas_call(
         lambda *refs: project_kernel(n, len(weights), *refs),
@@ -294,6 +288,8 @@
         block = arrived[i][j].astype(jnp.float32)
         for r in range(rows):
             spread[r, pl.ds(jnp.bitwise_xor(me, d), 1), :] = block[r : r + 1, :]
+    starts = range(0, query_cols, DH)
+    ready = []
     for r in range(rows):
         given = spread[r]
         cos, sin = cosine[r : r + 1, :], sine[r : r + 1, :]
@@ -302,11 +298,11 @@
             turned = jnp.concatenate([a * cos - b * sin, b * cos + a * sin], axis=1)
             return turned.astype(jnp.bfloat16)
 
-        starts = range(0, query_cols, DH)
         q = turn(
             jnp.concatenate([given[:, c : c + DH // 2] for c in starts], axis=0),
             jnp.concatenate([given[:, c + DH // 2 : c + DH] for c in starts], axis=0),
         )
+        q = (q.astype(jnp.float32) * score_scale).astype(jnp.bfloat16)
         new = [
             given[i : i + 1, query_cols:] + given[i + 1 : i + 2, query_cols:]
             for i in range(0, n, 2)
@@ -314,10 +310,11 @@
         new_key = turn(new[0], new[1]).astype(jnp.float32)
         new_value = jnp.concatenate(new[2:], axis=1)
         scores = lax.dot_general(q, keys[r], contract, preferred_element_type=jnp.float32)
-        scores = scores * score_scale
+        own_score = jnp.sum(q.astype(jnp.float32) * new_key, axis=1, keepdims=True)
+        ready.append((scores, own_score, new_value))
+    for r, (scores, own_score, new_value) in enumerate(ready):
         place = lax.broadcasted_iota(jnp.int32, scores.shape, 1)
         scores = jnp.where(place < lengths[r], scores, -1e30)
-        own_score = jnp.sum(q.astype(jnp.float32) * new_key, axis=1, keepdims=True) * score_scale
         highest = jnp.maximum(jnp.max(scores, axis=1, keepdims=True), own_score)
         weights = jnp.exp(scores - highest)
         own_weight = jnp.exp(own_score - highest)
@@ -519,17 +516,22 @@
         left, right = ring.step(left, right)
         if step > 1:
             sums = [row_sums([activations, *arrived] if step == 2 else arrived, sums)]
+        if step == 3:
+            far_sums = lax.ppermute(sums[0][: activations.shape[0]], "gx", ring.across)
         weight = piece_of(query_weight, (step - 1) * piece, piece, arrived)
         weight, (left, right, *sums) = before(weight, left, right, *sums)
         weights.append(weight)
         shards += [left, right]
-    far = ring.step(left[:, : width // 2], right[:, width // 2 :])
+    cut, (cut_right, left, right) = before(
+        left[:, : width // 2], right[:, width // 2 :], left, right
+    )
+    far = ring.step(cut, cut_right)
     sums = row_sums([left, right], sums)
-    jobs = [(query_weight, 3 * piece, piece, 0), (keyval_weight, 0, new_cols, None)]
-    weight = load(piece + 2 * new_cols, jobs, [left, right])
-    weight, far = before(weight, *far)
-    sums = row_sums([], [sums], far)
+    jobs = [(query_weight, 3 * piece, piece, 0), (keyval_weight, 0, new_cols, piece)]
+    weight = load(piece + new_cols, jobs, [sums])
+    sums = jnp.concatenate([sums, far_sums], axis=0)
     other_sums = swap_pair(sums)
+    weight, (other_sums, *far) = before(weight, other_sums, *far)
     weights.append(weight)
     gain = norm_gain.astype(jnp.float32)[None, :]
     keep, give = project((sums, other_sums), gain, shards, far, weights)

time: 88.4 us -> 86.7 us (0.981)
  waiting for transfers between devices: 16 us -> 12.1 us
  starting transfers between devices: 21.7 us -> 25.3 us
  Pallas kernels: 49.3 us -> 48 us
    ppermute x8, waiting for transfers between devices: 8.73 us -> 5.9 us  [step(): lax.ppermute(right, 'gx', self.back)]
    ppermute x0 -> x1, starting transfers between devices: none -> 2.34 us  [on_device(): far_sums = lax.ppermute(sums[0][:activations.shape[0]], 'gx', ring.across)]
    ppermute x8, starting transfers between devices: 13.3 us -> 11.1 us  [step(): lax.ppermute(left, 'gx', self.onward)]
    ppermute x8, starting transfers between devices: 4.03 us -> 6.2 us  [step(): lax.ppermute(right, 'gx', self.back)]
    ppermute x4, waiting for transfers between devices: 5.26 us -> 3.88 us  [swap_pair(): return lax.ppermute(x, 'gy', [(0, 1), (1, 0)])]
  transfers between devices with their start and end apart: 24 -> 25, of which waited for: 16 -> 11; matrix products, arithmetic and copies ran while one was open for 0% -> 0% of each run, Pallas kernels for 35% -> 36%
where the time goes in v16:
time: 86.7 us; the launch traced here: 86.5 us
  Pallas kernels  48 us (55%)
  starting transfers between devices  25.3 us (29%)
  waiting for transfers between devices  12.1 us (14%)
  other arithmetic  0.89 us (1%)
    pallas_call x9, Pallas kernels, load(): pl.pallas_call(lambda *refs: load_kernel([job[1:] for job in jobs], *refs...  26 us
    ppermute x8, starting transfers between devices, step(): lax.ppermute(left, 'gx', self.onward)  11.1 us
    pallas_call x1, Pallas kernels, project(): pl.pallas_call(lambda *refs: project_kernel(n, len(weights), *refs), out_...  9.08 us
    ppermute x8, starting transfers between devices, step(): lax.ppermute(right, 'gx', self.back)  6.2 us
    ppermute x8, waiting for transfers between devices, step(): lax.ppermute(right, 'gx', self.back)  5.9 us
    pallas_call x1, Pallas kernels, output_project(): pl.pallas_call(lambda *refs: output_kernel(n, *refs), out_shape=[shape, s...  5.05 us
    ppermute x4, starting transfers between devices, exchange(): return lax.ppermute(blocks, 'gx', [(i, i ^ d) for i in range(n)])  4.86 us
    pallas_call x2, Pallas kernels, load_cache(): pl.pallas_call(load_cache_kernel, out_shape=pltpu.VMEM(cache.shape, cache...  4.42 us
  transfers between devices with their start and end apart: 25, of which 11 were waited for; matrix products, arithmetic and copies ran while one was open for 0% of the time, Pallas kernels for 36%

profile of v16, /device:TPU:0, one launch (start us, length us, event | category | flops | bytes accessed | tf_op | source)
XLA Modules:
  0.0 86.5 jit_solution(14527707170070069793)
XLA Ops:
  0.0 3.0 %collective-permute-start = (bf16[8,9216]{1,0:T(8,128)(2,1)}, bf16[8,9216]{1,0:T(8,128)(2,1)S(1)}, u32[]{:S(2)}, u32[]{:S(2)}) collective-permute-start(bf16[8,9216]{1,0:T(8,128)(2,1)} %refs_3_.1), channel_id=1, source_target_pairs={{0,4},{4,8},{8,12},{12,14},{14,10},{10,6},{6,2},{2,0},{1,5},{5,9},... | collective-permute-start | bytes 442376 | tf_op jit(solution)/shard_map/ppermute | solution.py:55
  3.0 3.1 %load.9.refs_12_ = bf16[384,9216]{1,0:T(8,128)(2,1)S(1)} custom-call(bf16[1536,9216]{1,0:T(8,128)(2,1)} %refs_0_.14), custom_call_target="tpu_custom_call" | custom-call | tf_op jit(solution)/shard_map/load/pallas_call | solution.py:97
  6.1 1.0 %collective-permute-done.refs_1_.refs_4_ = bf16[8,9216]{1,0:T(8,128)(2,1)S(1)} collective-permute-done((bf16[8,9216]{1,0:T(8,128)(2,1)}, bf16[8,9216]{1,0:T(8,128)(2,1)S(1)}, u32[]{:S(2)}, u32[]{:S(2)}) %collective-permute-start) | collective-permute-done | bytes 147488 | tf_op jit(solution)/shard_map/ppermute | solution.py:55
  7.1 1.4 %collective-permute-done.1.refs_2_.refs_5_ = bf16[8,9216]{1,0:T(8,128)(2,1)S(1)} collective-permute-done((bf16[8,9216]{1,0:T(8,128)(2,1)}, bf16[8,9216]{1,0:T(8,128)(2,1)S(1)}, u32[]{:S(2)}, u32[]{:S(2)}) %collective-permute-start.1) | collective-permute-done | bytes 147488 | tf_op jit(solution)/shard_map/ppermute | solution.py:55
  8.5 1.6 %collective-permute-start.2 = (bf16[8,9216]{1,0:T(8,128)(2,1)S(1)}, bf16[8,9216]{1,0:T(8,128)(2,1)S(1)}, u32[]{:S(2)}, u32[]{:S(2)}) collective-permute-start(bf16[8,9216]{1,0:T(8,128)(2,1)S(1)} %collective-permute-done.refs_1_.refs_4_), channel_id=1, source_target_pairs={{0,4},{4,8},{8,12},{12,14},{14,10},{10,6},{6,2},{2,0},{1,5},{5,9},... | collective-permute-start | bytes 442376 | tf_op jit(solution)/shard_map/ppermute | solution.py:55
  10.1 0.4 collective-permute-start.3
  10.6 0.2 row_sums.3.refs_0_
  10.8 3.1 %load.10.refs_13_ = bf16[384,9216]{1,0:T(8,128)(2,1)S(1)} custom-call(bf16[1536,9216]{1,0:T(8,128)(2,1)} %refs_0_.14, bf16[8,9216]{1,0:T(8,128)(2,1)S(1)} %collective-permute-done.refs_1_.refs_4_, bf16[8,9216]{1,0:T(8,128)(2,1)S(1)} %collective-permute-done.1.refs_2_.refs_5_), custom_call_target="tpu_custom_call" | custom-call | tf_op jit(solution)/shard_map/load/pallas_call | solution.py:97
  13.9 1.3 %collective-permute-done.3.refs_2_.refs_7_ = bf16[8,9216]{1,0:T(8,128)(2,1)S(1)} collective-permute-done((bf16[8,9216]{1,0:T(8,128)(2,1)S(1)}, bf16[8,9216]{1,0:T(8,128)(2,1)S(1)}, u32[]{:S(2)}, u32[]{:S(2)}) %collective-permute-start.3) | collective-permute-done | bytes 147488 | tf_op jit(solution)/shard_map/ppermute | solution.py:55
  15.3 1.6 %collective-permute-start.4 = (bf16[8,9216]{1,0:T(8,128)(2,1)S(1)}, bf16[8,9216]{1,0:T(8,128)(2,1)S(1)}, u32[]{:S(2)}, u32[]{:S(2)}) collective-permute-start(bf16[8,9216]{1,0:T(8,128)(2,1)S(1)} %collective-permute-done.2.refs_1_.refs_6_), channel_id=1, source_target_pairs={{0,4},{4,8},{8,12},{12,14},{14,10},{10,6},{6,2},{2,0},{1,5},{5,9},... | collective-permute-start | bytes 442376 | tf_op jit(solution)/shard_map/ppermute | solution.py:55
  16.8 0.4 collective-permute-start.5
  17.3 0.2 row_sums.4.refs_0_
  17.5 2.3 %collective-permute-start.6 = (f32[8,128]{1,0:T(8,128)S(1)}, f32[8,128]{1,0:T(8,128)S(1)}, u32[]{:S(2)}, u32[]{:S(2)}) collective-permute-start(f32[8,128]{1,0:T(8,128)S(1)} %slice.20), channel_id=1, source_target_pairs={{0,14},{4,10},{8,6},{12,2},{14,0},{10,4},{6,8},{2,12},{1,15},{5,11... | collective-permute-start | bytes 12296 | tf_op jit(solution)/shard_map/ppermute | solution.py:520
  19.8 3.1 %load.11.refs_14_ = bf16[384,9216]{1,0:T(8,128)(2,1)S(1)} custom-call(bf16[1536,9216]{1,0:T(8,128)(2,1)} %refs_0_.14, bf16[8,9216]{1,0:T(8,128)(2,1)S(1)} %collective-permute-done.2.refs_1_.refs_6_, bf16[8,9216]{1,0:T(8,128)(2,1)S(1)} %collective-permute-done.3.refs_2_.refs_7_), custom_call_target="tpu_custom_call" | custom-call | tf_op jit(solution)/shard_map/load/pallas_call | solution.py:97
  23.0 1.0 %collective-permute-start.8 = (bf16[8,4608]{1,0:T(8,128)(2,1)S(1)}, bf16[8,4608]{1,0:T(8,128)(2,1)S(1)}, u32[]{:S(2)}, u32[]{:S(2)}) collective-permute-start(bf16[8,4608]{1,0:T(8,128)(2,1)S(1)} %slice.15), channel_id=1, source_target_pairs={{0,4},{4,8},{8,12},{12,14},{14,10},{10,6},{6,2},{2,0},{1,5},{5,9},... | collective-permute-start | bytes 221192 | tf_op jit(solution)/shard_map/ppermute | solution.py:55
  24.0 1.1 %collective-permute-start.9 = (bf16[8,4608]{1,0:T(8,128)(2,1)S(1)}, bf16[8,4608]{1,0:T(8,128)(2,1)S(1)}, u32[]{:S(2)}, u32[]{:S(2)}) collective-permute-start(bf16[8,4608]{1,0:T(8,128)(2,1)S(1)} %slice.16), channel_id=1, source_target_pairs={{0,2},{4,0},{8,4},{12,8},{14,12},{10,14},{6,10},{2,6},{1,3},{5,1},... | collective-permute-start | bytes 221192 | tf_op jit(solution)/shard_map/ppermute | solution.py:55
  25.3 3.4 %load.12.refs_15_ = bf16[448,9216]{1,0:T(8,128)(2,1)S(1)} custom-call(bf16[1536,9216]{1,0:T(8,128)(2,1)} %refs_0_.14, bf16[64,9216]{1,0:T(8,128)(2,1)} %refs_1_.1, f32[56,128]{1,0:T(8,128)S(1)} %row_sums.5.refs_2_), custom_call_target="tpu_custom_call" | custom-call | tf_op jit(solution)/shard_map/load/pallas_call | solution.py:97
  28.8 9.1 %project.1 = (f32[8,4,1664]{2,1,0:T(4,128)S(1)}, f32[8,4,1664]{2,1,0:T(4,128)S(1)}) custom-call(f32[64,128]{1,0:T(8,128)S(1)} %pad_maximum_fusion.1.refs_0_, f32[64,128]{1,0:T(8,128)S(1)} %collective-permute-done.7.refs_1_, f32[1,9216]{1,0:T(1,128)S(1)} %bitcast.3, bf16[8,9216]{1,0:T(8,128)(2,1)S(1)} %copy-done, ...), custom_call_target="tpu_custom_call" | custom-call | tf_op jit(solution)/shard_map/project/pallas_call | solution.py:222
  37.8 0.5 collective-permute-start.10
  38.4 1.1 %collective-permute-done.10.got = f32[8,4,1664]{2,1,0:T(4,128)S(1)} collective-permute-done((f32[8,4,1664]{2,1,0:T(4,128)S(1)}, f32[8,4,1664]{2,1,0:T(4,128)S(1)}, u32[]{:S(2)}, u32[]{:S(2)}) %collective-permute-start.10) | collective-permute-done | bytes 213024 | tf_op jit(solution)/shard_map/ppermute | solution.py:44
  39.5 1.7 %collective-permute-start.11 = (bf16[2,4,1664]{2,1,0:T(4,128)(2,1)S(1)}, bf16[2,4,1664]{2,1,0:T(4,128)(2,1)S(1)}, u32[]{:S(2)}, u32[]{:S(2)}) collective-permute-start(bf16[2,4,1664]{2,1,0:T(4,128)(2,1)S(1)} %get-tuple-element.76.refs_0_), channel_id=1, source_target_pairs={{0,2},{2,0},{4,6},{6,4},{8,10},{10,8},{12,14},{14,12},{1,3},{3,1},... | collective-permute-start | bytes 79880 | tf_op jit(solution)/shard_map/ppermute | solution.py:540
  41.2 0.7 collective-permute-start.12
  41.9 1.2 %collective-permute-start.13 = (bf16[2,4,1664]{2,1,0:T(4,128)(2,1)S(1)}, bf16[2,4,1664]{2,1,0:T(4,128)(2,1)S(1)}, u32[]{:S(2)}, u32[]{:S(2)}) collective-permute-start(bf16[2,4,1664]{2,1,0:T(4,128)(2,1)S(1)} %get-tuple-element.79), channel_id=1, source_target_pairs={{0,6},{2,4},{4,2},{6,0},{8,14},{10,12},{12,10},{14,8},{1,7},{3,5},... | collective-permute-start | bytes 79880 | tf_op jit(solution)/shard_map/ppermute | solution.py:540
  43.1 2.2 %load_cache.2.refs_7_ = bf16[4,2048,256]{2,1,0:T(8,128)(2,1)S(1)} custom-call(bf16[4,2048,256]{2,1,0:T(8,128)(2,1)} %source.2, bf16[2,4,1664]{2,1,0:T(4,128)(2,1)S(1)} %get-tuple-element.76.refs_0_), custom_call_target="tpu_custom_call" | custom-call | tf_op jit(solution)/shard_map/load_cache/pallas_call | solution.py:119
  45.4 1.3 %collective-permute-done.13.refs_3_ = bf16[2,4,1664]{2,1,0:T(4,128)(2,1)S(1)} collective-permute-done((bf16[2,4,1664]{2,1,0:T(4,128)(2,1)S(1)}, bf16[2,4,1664]{2,1,0:T(4,128)(2,1)S(1)}, u32[]{:S(2)}, u32[]{:S(2)}) %collective-permute-start.13) | collective-permute-done | bytes 26656 | tf_op jit(solution)/shard_map/ppermute | solution.py:540
  46.6 1.3 %collective-permute-start.14 = (bf16[4,4,1664]{2,1,0:T(4,128)(2,1)S(1)}, bf16[4,4,1664]{2,1,0:T(4,128)(2,1)S(1)}, u32[]{:S(2)}, u32[]{:S(2)}) collective-permute-start(bf16[4,4,1664]{2,1,0:T(4,128)(2,1)S(1)} %pack.1.refs_1_.refs_0_), channel_id=1, source_target_pairs={{0,8},{2,10},{4,12},{6,14},{8,0},{10,2},{12,4},{14,6},{1,9},{3,11}... | collective-permute-start | bytes 159752 | tf_op jit(solution)/shard_map/ppermute | solution.py:540
  48.0 2.2 %load_cache.3.refs_8_ = bf16[4,2048,256]{2,1,0:T(8,128)(2,1)S(1)} custom-call(bf16[4,2048,256]{2,1,0:T(8,128)(2,1)} %source.3, bf16[4,4,1664]{2,1,0:T(4,128)(2,1)S(1)} %pack.1.refs_1_.refs_0_), custom_call_target="tpu_custom_call" | custom-call | tf_op jit(solution)/shard_map/load_cache/pallas_call | solution.py:119
  50.2 2.4 %load.13.refs_9_ = bf16[1024,2304]{1,0:T(8,128)(2,1)S(1)} custom-call(bf16[6144,2304]{1,0:T(8,128)(2,1)} %refs_0_.19, bf16[4,4,1664]{2,1,0:T(4,128)(2,1)S(1)} %pack.1.refs_1_.refs_0_), custom_call_target="tpu_custom_call" | custom-call | tf_op jit(solution)/shard_map/load/pallas_call | solution.py:97
  52.6 2.8 %attend.1 = (bf16[4,6144]{1,0:T(4,128)(2,1)S(1)}, bf16[4,6144]{1,0:T(4,128)(2,1)S(1)}) custom-call(s32[4]{0:T(128)S(1)} %copy-done.1, bf16[2,4,1664]{2,1,0:T(4,128)(2,1)S(1)} %get-tuple-element.80.refs_0_, bf16[2,4,1664]{2,1,0:T(4,128)(2,1)S(1)} %collective-permute-done.11.refs_1_, bf16[2,4,1664]{2,1,0:T(4,128)(2,1)S(1)} %collective-permute-done.12.refs_2_, ...), custom_call_target="tpu_custom_call" | custom-call | tf_op jit(solution)/shard_map/attend/pallas_call | solution.py:342
  55.5 1.2 %collective-permute-done.15 = bf16[4,6144]{1,0:T(4,128)(2,1)S(1)} collective-permute-done((bf16[4,6144]{1,0:T(4,128)(2,1)S(1)}, bf16[4,6144]{1,0:T(4,128)(2,1)S(1)}, u32[]{:S(2)}, u32[]{:S(2)}) %collective-permute-start.15) | collective-permute-done | bytes 49184 | tf_op jit(solution)/shard_map/ppermute | solution.py:44
  56.7 0.7 collective-permute-start.16
  57.5 1.3 %collective-permute-start.17 = (bf16[8,6144]{1,0:T(8,128)(2,1)S(1)}, bf16[8,6144]{1,0:T(8,128)(2,1)S(1)}, u32[]{:S(2)}, u32[]{:S(2)}) collective-permute-start(bf16[8,6144]{1,0:T(8,128)(2,1)S(1)} %pad_maximum_fusion.refs_1_.refs_0_), channel_id=1, source_target_pairs={{0,2},{4,0},{8,4},{12,8},{14,12},{10,14},{6,10},{2,6},{1,3},{5,1},... | collective-permute-start | bytes 294920 | tf_op jit(solution)/shard_map/ppermute | solution.py:55
  58.8 2.7 %load.14.refs_10_ = bf16[1280,2304]{1,0:T(8,128)(2,1)S(1)} custom-call(bf16[6144,2304]{1,0:T(8,128)(2,1)} %refs_0_.19, bf16[8,6144]{1,0:T(8,128)(2,1)S(1)} %pad_maximum_fusion.refs_1_.refs_0_), custom_call_target="tpu_custom_call" | custom-call | tf_op jit(solution)/shard_map/load/pallas_call | solution.py:97
  61.7 0.4 collective-permute-done.17.refs_2_
  62.1 1.5 %collective-permute-start.18 = (bf16[8,6144]{1,0:T(8,128)(2,1)S(1)}, bf16[8,6144]{1,0:T(8,128)(2,1)S(1)}, u32[]{:S(2)}, u32[]{:S(2)}) collective-permute-start(bf16[8,6144]{1,0:T(8,128)(2,1)S(1)} %collective-permute-done.16.refs_1_), channel_id=1, source_target_pairs={{0,4},{4,8},{8,12},{12,14},{14,10},{10,6},{6,2},{2,0},{1,5},{5,9},... | collective-permute-start | bytes 294920 | tf_op jit(solution)/shard_map/ppermute | solution.py:55
  63.6 0.5 collective-permute-start.19
  64.1 2.7 %load.15.refs_11_ = bf16[1280,2304]{1,0:T(8,128)(2,1)S(1)} custom-call(bf16[6144,2304]{1,0:T(8,128)(2,1)} %refs_0_.19, bf16[8,6144]{1,0:T(8,128)(2,1)S(1)} %collective-permute-done.16.refs_1_, bf16[8,6144]{1,0:T(8,128)(2,1)S(1)} %collective-permute-done.17.refs_2_), custom_call_target="tpu_custom_call" | custom-call | tf_op jit(solution)/shard_map/load/pallas_call | solution.py:97
  66.9 1.3 %collective-permute-done.19.refs_2_.refs_4_ = bf16[8,6144]{1,0:T(8,128)(2,1)S(1)} collective-permute-done((bf16[8,6144]{1,0:T(8,128)(2,1)S(1)}, bf16[8,6144]{1,0:T(8,128)(2,1)S(1)}, u32[]{:S(2)}, u32[]{:S(2)}) %collective-permute-start.19) | collective-permute-done | bytes 98336 | tf_op jit(solution)/shard_map/ppermute | solution.py:55
  68.2 1.4 %collective-permute-start.20 = (bf16[8,6144]{1,0:T(8,128)(2,1)S(1)}, bf16[8,6144]{1,0:T(8,128)(2,1)S(1)}, u32[]{:S(2)}, u32[]{:S(2)}) collective-permute-start(bf16[8,6144]{1,0:T(8,128)(2,1)S(1)} %collective-permute-done.18.refs_1_.refs_3_), channel_id=1, source_target_pairs={{0,4},{4,8},{8,12},{12,14},{14,10},{10,6},{6,2},{2,0},{1,5},{5,9},... | collective-permute-start | bytes 294920 | tf_op jit(solution)/shard_map/ppermute | solution.py:55
  69.6 0.7 collective-permute-start.21
  70.2 2.7 %load.16.refs_12_ = bf16[1280,2304]{1,0:T(8,128)(2,1)S(1)} custom-call(bf16[6144,2304]{1,0:T(8,128)(2,1)} %refs_0_.19, bf16[8,6144]{1,0:T(8,128)(2,1)S(1)} %collective-permute-done.18.refs_1_.refs_3_, bf16[8,6144]{1,0:T(8,128)(2,1)S(1)} %collective-permute-done.19.refs_2_.refs_4_), custom_call_target="tpu_custom_call" | custom-call | tf_op jit(solution)/shard_map/load/pallas_call | solution.py:97
  73.0 1.3 %collective-permute-done.21.refs_2_.refs_6_ = bf16[8,6144]{1,0:T(8,128)(2,1)S(1)} collective-permute-done((bf16[8,6144]{1,0:T(8,128)(2,1)S(1)}, bf16[8,6144]{1,0:T(8,128)(2,1)S(1)}, u32[]{:S(2)}, u32[]{:S(2)}) %collective-permute-start.21) | collective-permute-done | bytes 98336 | tf_op jit(solution)/shard_map/ppermute | solution.py:55
  74.3 0.3 collective-permute-start.22
  74.6 1.7 %collective-permute-start.23 = (bf16[8,3072]{1,0:T(8,128)(2,1)S(1)}, bf16[8,3072]{1,0:T(8,128)(2,1)S(1)}, u32[]{:S(2)}, u32[]{:S(2)}) collective-permute-start(bf16[8,3072]{1,0:T(8,128)(2,1)S(1)} %slice.19), channel_id=1, source_target_pairs={{0,2},{4,0},{8,4},{12,8},{14,12},{10,14},{6,10},{2,6},{1,3},{5,1},... | collective-permute-start | bytes 147464 | tf_op jit(solution)/shard_map/ppermute | solution.py:55
  76.4 2.7 %load.17.refs_13_ = bf16[1280,2304]{1,0:T(8,128)(2,1)S(1)} custom-call(bf16[6144,2304]{1,0:T(8,128)(2,1)} %refs_0_.19, bf16[8,6144]{1,0:T(8,128)(2,1)S(1)} %collective-permute-done.20.refs_1_.refs_5_, bf16[8,6144]{1,0:T(8,128)(2,1)S(1)} %collective-permute-done.21.refs_2_.refs_6_), custom_call_target="tpu_custom_call" | custom-call | tf_op jit(solution)/shard_map/load/pallas_call | solution.py:97
  79.1 5.1 %output_project.1 = (f32[4,8,2304]{2,1,0:T(8,128)S(1)}, f32[4,8,2304]{2,1,0:T(8,128)S(1)}) custom-call(bf16[8,6144]{1,0:T(8,128)(2,1)S(1)} %pad_maximum_fusion.refs_1_.refs_0_, bf16[8,6144]{1,0:T(8,128)(2,1)S(1)} %collective-permute-done.16.refs_1_, bf16[8,6144]{1,0:T(8,128)(2,1)S(1)} %collective-permute-done.17.refs_2_, ...), custom_call_target="tpu_custom_call" | custom-call | tf_op jit(solution)/shard_map/output_project/pallas_call | solution.py:397
  84.3 1.6 %collective-permute-done.24 = f32[4,8,2304]{2,1,0:T(8,128)S(1)} collective-permute-done((f32[4,8,2304]{2,1,0:T(8,128)S(1)}, f32[4,8,2304]{2,1,0:T(8,128)S(1)}, u32[]{:S(2)}, u32[]{:S(2)}) %collective-permute-start.24) | collective-permute-done | bytes 294944 | tf_op jit(solution)/shard_map/ppermute | solution.py:44
  85.8 0.7 fusion
  (39 shorter events, 0.8 us)
Async XLA Ops:
  0.0 10.6 %copy-start = (bf16[8,9216]{1,0:T(8,128)(2,1)S(1)}, bf16[8,9216]{1,0:T(8,128)(2,1)}, u32[]{:S(2)}) copy-start(bf16[8,9216]{1,0:T(8,128)(2,1)} %refs_3_.1) | copy-start | bytes 442372
  0.0 7.1 %collective-permute-start = (bf16[8,9216]{1,0:T(8,128)(2,1)}, bf16[8,9216]{1,0:T(8,128)(2,1)S(1)}, u32[]{:S(2)}, u32[]{:S(2)}) collective-permute-start(bf16[8,9216]{1,0:T(8,128)(2,1)} %refs_3_.1), channel_id=1, source_target_pairs={{0,4},{4,8},{8,12},{12,14},{14,10},{10,6},{6,2},{2,0},{1,5},{5,9},... | collective-permute-start | bytes 442376 | tf_op jit(solution)/shard_map/ppermute | solution.py:55
  3.0 5.5 %collective-permute-start.1 = (bf16[8,9216]{1,0:T(8,128)(2,1)}, bf16[8,9216]{1,0:T(8,128)(2,1)S(1)}, u32[]{:S(2)}, u32[]{:S(2)}) collective-permute-start(bf16[8,9216]{1,0:T(8,128)(2,1)} %refs_3_.1), channel_id=1, source_target_pairs={{0,2},{4,0},{8,4},{12,8},{14,12},{10,14},{6,10},{2,6},{1,3},{5,1},... | collective-permute-start | bytes 442376 | tf_op jit(solution)/shard_map/ppermute | solution.py:55
  8.5 5.4 %collective-permute-start.2 = (bf16[8,9216]{1,0:T(8,128)(2,1)S(1)}, bf16[8,9216]{1,0:T(8,128)(2,1)S(1)}, u32[]{:S(2)}, u32[]{:S(2)}) collective-permute-start(bf16[8,9216]{1,0:T(8,128)(2,1)S(1)} %collective-permute-done.refs_1_.refs_4_), channel_id=1, source_target_pairs={{0,4},{4,8},{8,12},{12,14},{14,10},{10,6},{6,2},{2,0},{1,5},{5,9},... | collective-permute-start | bytes 442376 | tf_op jit(solution)/shard_map/ppermute | solution.py:55
  10.1 5.1 %collective-permute-start.3 = (bf16[8,9216]{1,0:T(8,128)(2,1)S(1)}, bf16[8,9216]{1,0:T(8,128)(2,1)S(1)}, u32[]{:S(2)}, u32[]{:S(2)}) collective-permute-start(bf16[8,9216]{1,0:T(8,128)(2,1)S(1)} %collective-permute-done.1.refs_2_.refs_5_), channel_id=1, source_target_pairs={{0,2},{4,0},{8,4},{12,8},{14,12},{10,14},{6,10},{2,6},{1,3},{5,1},... | collective-permute-start | bytes 442376 | tf_op jit(solution)/shard_map/ppermute | solution.py:55
  15.3 7.7 %collective-permute-start.4 = (bf16[8,9216]{1,0:T(8,128)(2,1)S(1)}, bf16[8,9216]{1,0:T(8,128)(2,1)S(1)}, u32[]{:S(2)}, u32[]{:S(2)}) collective-permute-start(bf16[8,9216]{1,0:T(8,128)(2,1)S(1)} %collective-permute-done.2.refs_1_.refs_6_), channel_id=1, source_target_pairs={{0,4},{4,8},{8,12},{12,14},{14,10},{10,6},{6,2},{2,0},{1,5},{5,9},... | collective-permute-start | bytes 442376 | tf_op jit(solution)/shard_map/ppermute | solution.py:55
  16.8 6.1 %collective-permute-start.5 = (bf16[8,9216]{1,0:T(8,128)(2,1)S(1)}, bf16[8,9216]{1,0:T(8,128)(2,1)S(1)}, u32[]{:S(2)}, u32[]{:S(2)}) collective-permute-start(bf16[8,9216]{1,0:T(8,128)(2,1)S(1)} %collective-permute-done.3.refs_2_.refs_7_), channel_id=1, source_target_pairs={{0,2},{4,0},{8,4},{12,8},{14,12},{10,14},{6,10},{2,6},{1,3},{5,1},... | collective-permute-start | bytes 442376 | tf_op jit(solution)/shard_map/ppermute | solution.py:55
  17.5 7.8 %copy-start.2 = (bf16[9216]{0:T(1024)(128)(2,1)S(1)}, bf16[9216]{0:T(1024)(128)(2,1)}, u32[]{:S(2)}) copy-start(bf16[9216]{0:T(1024)(128)(2,1)} %param.9) | copy-start | bytes 55300
  17.5 7.8 %collective-permute-start.6 = (f32[8,128]{1,0:T(8,128)S(1)}, f32[8,128]{1,0:T(8,128)S(1)}, u32[]{:S(2)}, u32[]{:S(2)}) collective-permute-start(f32[8,128]{1,0:T(8,128)S(1)} %slice.20), channel_id=1, source_target_pairs={{0,14},{4,10},{8,6},{12,2},{14,0},{10,4},{6,8},{2,12},{1,15},{5,11... | collective-permute-start | bytes 12296 | tf_op jit(solution)/shard_map/ppermute | solution.py:520
  23.0 5.8 %collective-permute-start.8 = (bf16[8,4608]{1,0:T(8,128)(2,1)S(1)}, bf16[8,4608]{1,0:T(8,128)(2,1)S(1)}, u32[]{:S(2)}, u32[]{:S(2)}) collective-permute-start(bf16[8,4608]{1,0:T(8,128)(2,1)S(1)} %slice.15), channel_id=1, source_target_pairs={{0,4},{4,8},{8,12},{12,14},{14,10},{10,6},{6,2},{2,0},{1,5},{5,9},... | collective-permute-start | bytes 221192 | tf_op jit(solution)/shard_map/ppermute | solution.py:55
  24.0 4.7 %collective-permute-start.9 = (bf16[8,4608]{1,0:T(8,128)(2,1)S(1)}, bf16[8,4608]{1,0:T(8,128)(2,1)S(1)}, u32[]{:S(2)}, u32[]{:S(2)}) collective-permute-start(bf16[8,4608]{1,0:T(8,128)(2,1)S(1)} %slice.16), channel_id=1, source_target_pairs={{0,2},{4,0},{8,4},{12,8},{14,12},{10,14},{6,10},{2,6},{1,3},{5,1},... | collective-permute-start | bytes 221192 | tf_op jit(solution)/shard_map/ppermute | solution.py:55
  25.2 3.5 %collective-permute-start.7 = (f32[64,128]{1,0:T(8,128)S(1)}, f32[64,128]{1,0:T(8,128)S(1)}, u32[]{:S(2)}, u32[]{:S(2)}) collective-permute-start(f32[64,128]{1,0:T(8,128)S(1)} %pad_maximum_fusion.1.refs_0_), channel_id=1, source_target_pairs={{0,1},{1,0},{2,3},{3,2},{4,5},{5,4},{6,7},{7,6},{8,9},{9,8},{10,11... | collective-permute-start | bytes 98312 | tf_op jit(solution)/shard_map/ppermute | solution.py:44
  28.7 14.4 %copy-start.1 = (s32[4]{0:T(128)S(1)}, s32[4]{0:T(128)}, u32[]{:S(2)}) copy-start(s32[4]{0:T(128)} %lengths.1) | copy-start | bytes 52
  37.8 1.6 %collective-permute-start.10 = (f32[8,4,1664]{2,1,0:T(4,128)S(1)}, f32[8,4,1664]{2,1,0:T(4,128)S(1)}, u32[]{:S(2)}, u32[]{:S(2)}) collective-permute-start(f32[8,4,1664]{2,1,0:T(4,128)S(1)} %get-tuple-element.75), channel_id=1, source_target_pairs={{0,1},{1,0},{2,3},{3,2},{4,5},{5,4},{6,7},{7,6},{8,9},{9,8},{10,11... | collective-permute-start | bytes 638984 | tf_op jit(solution)/shard_map/ppermute | solution.py:44
  39.5 5.8 %collective-permute-start.11 = (bf16[2,4,1664]{2,1,0:T(4,128)(2,1)S(1)}, bf16[2,4,1664]{2,1,0:T(4,128)(2,1)S(1)}, u32[]{:S(2)}, u32[]{:S(2)}) collective-permute-start(bf16[2,4,1664]{2,1,0:T(4,128)(2,1)S(1)} %get-tuple-element.76.refs_0_), channel_id=1, source_target_pairs={{0,2},{2,0},{4,6},{6,4},{8,10},{10,8},{12,14},{14,12},{1,3},{3,1},... | collective-permute-start | bytes 79880 | tf_op jit(solution)/shard_map/ppermute | solution.py:540
  41.2 4.2 %collective-permute-start.12 = (bf16[2,4,1664]{2,1,0:T(4,128)(2,1)S(1)}, bf16[2,4,1664]{2,1,0:T(4,128)(2,1)S(1)}, u32[]{:S(2)}, u32[]{:S(2)}) collective-permute-start(bf16[2,4,1664]{2,1,0:T(4,128)(2,1)S(1)} %get-tuple-element.78), channel_id=1, source_target_pairs={{0,4},{2,6},{4,0},{6,2},{8,12},{10,14},{12,8},{14,10},{1,5},{3,7},... | collective-permute-start | bytes 79880 | tf_op jit(solution)/shard_map/ppermute | solution.py:540
  41.9 4.7 %collective-permute-start.13 = (bf16[2,4,1664]{2,1,0:T(4,128)(2,1)S(1)}, bf16[2,4,1664]{2,1,0:T(4,128)(2,1)S(1)}, u32[]{:S(2)}, u32[]{:S(2)}) collective-permute-start(bf16[2,4,1664]{2,1,0:T(4,128)(2,1)S(1)} %get-tuple-element.79), channel_id=1, source_target_pairs={{0,6},{2,4},{4,2},{6,0},{8,14},{10,12},{12,10},{14,8},{1,7},{3,5},... | collective-permute-start | bytes 79880 | tf_op jit(solution)/shard_map/ppermute | solution.py:540
  46.6 6.0 %collective-permute-start.14 = (bf16[4,4,1664]{2,1,0:T(4,128)(2,1)S(1)}, bf16[4,4,1664]{2,1,0:T(4,128)(2,1)S(1)}, u32[]{:S(2)}, u32[]{:S(2)}) collective-permute-start(bf16[4,4,1664]{2,1,0:T(4,128)(2,1)S(1)} %pack.1.refs_1_.refs_0_), channel_id=1, source_target_pairs={{0,8},{2,10},{4,12},{6,14},{8,0},{10,2},{12,4},{14,6},{1,9},{3,11}... | collective-permute-start | bytes 159752 | tf_op jit(solution)/shard_map/ppermute | solution.py:540
  55.4 1.3 %collective-permute-start.15 = (bf16[4,6144]{1,0:T(4,128)(2,1)S(1)}, bf16[4,6144]{1,0:T(4,128)(2,1)S(1)}, u32[]{:S(2)}, u32[]{:S(2)}) collective-permute-start(bf16[4,6144]{1,0:T(4,128)(2,1)S(1)} %get-tuple-element.89), channel_id=1, source_target_pairs={{0,1},{1,0},{2,3},{3,2},{4,5},{5,4},{6,7},{7,6},{8,9},{9,8},{10,11... | collective-permute-start | bytes 147464 | tf_op jit(solution)/shard_map/ppermute | solution.py:44
  56.7 4.9 %collective-permute-start.16 = (bf16[8,6144]{1,0:T(8,128)(2,1)S(1)}, bf16[8,6144]{1,0:T(8,128)(2,1)S(1)}, u32[]{:S(2)}, u32[]{:S(2)}) collective-permute-start(bf16[8,6144]{1,0:T(8,128)(2,1)S(1)} %pad_maximum_fusion.refs_1_.refs_0_), channel_id=1, source_target_pairs={{0,4},{4,8},{8,12},{12,14},{14,10},{10,6},{6,2},{2,0},{1,5},{5,9},... | collective-permute-start | bytes 294920 | tf_op jit(solution)/shard_map/ppermute | solution.py:55
  57.5 4.6 %collective-permute-start.17 = (bf16[8,6144]{1,0:T(8,128)(2,1)S(1)}, bf16[8,6144]{1,0:T(8,128)(2,1)S(1)}, u32[]{:S(2)}, u32[]{:S(2)}) collective-permute-start(bf16[8,6144]{1,0:T(8,128)(2,1)S(1)} %pad_maximum_fusion.refs_1_.refs_0_), channel_id=1, source_target_pairs={{0,2},{4,0},{8,4},{12,8},{14,12},{10,14},{6,10},{2,6},{1,3},{5,1},... | collective-permute-start | bytes 294920 | tf_op jit(solution)/shard_map/ppermute | solution.py:55
  62.1 4.8 %collective-permute-start.18 = (bf16[8,6144]{1,0:T(8,128)(2,1)S(1)}, bf16[8,6144]{1,0:T(8,128)(2,1)S(1)}, u32[]{:S(2)}, u32[]{:S(2)}) collective-permute-start(bf16[8,6144]{1,0:T(8,128)(2,1)S(1)} %collective-permute-done.16.refs_1_), channel_id=1, source_target_pairs={{0,4},{4,8},{8,12},{12,14},{14,10},{10,6},{6,2},{2,0},{1,5},{5,9},... | collective-permute-start | bytes 294920 | tf_op jit(solution)/shard_map/ppermute | solution.py:55
  63.6 4.6 %collective-permute-start.19 = (bf16[8,6144]{1,0:T(8,128)(2,1)S(1)}, bf16[8,6144]{1,0:T(8,128)(2,1)S(1)}, u32[]{:S(2)}, u32[]{:S(2)}) collective-permute-start(bf16[8,6144]{1,0:T(8,128)(2,1)S(1)} %collective-permute-done.17.refs_2_), channel_id=1, source_target_pairs={{0,2},{4,0},{8,4},{12,8},{14,12},{10,14},{6,10},{2,6},{1,3},{5,1},... | collective-permute-start | bytes 294920 | tf_op jit(solution)/shard_map/ppermute | solution.py:55
  68.2 4.8 %collective-permute-start.20 = (bf16[8,6144]{1,0:T(8,128)(2,1)S(1)}, bf16[8,6144]{1,0:T(8,128)(2,1)S(1)}, u32[]{:S(2)}, u32[]{:S(2)}) collective-permute-start(bf16[8,6144]{1,0:T(8,128)(2,1)S(1)} %collective-permute-done.18.refs_1_.refs_3_), channel_id=1, source_target_pairs={{0,4},{4,8},{8,12},{12,14},{14,10},{10,6},{6,2},{2,0},{1,5},{5,9},... | collective-permute-start | bytes 294920 | tf_op jit(solution)/shard_map/ppermute | solution.py:55
  69.6 4.7 %collective-permute-start.21 = (bf16[8,6144]{1,0:T(8,128)(2,1)S(1)}, bf16[8,6144]{1,0:T(8,128)(2,1)S(1)}, u32[]{:S(2)}, u32[]{:S(2)}) collective-permute-start(bf16[8,6144]{1,0:T(8,128)(2,1)S(1)} %collective-permute-done.19.refs_2_.refs_4_), channel_id=1, source_target_pairs={{0,2},{4,0},{8,4},{12,8},{14,12},{10,14},{6,10},{2,6},{1,3},{5,1},... | collective-permute-start | bytes 294920 | tf_op jit(solution)/shard_map/ppermute | solution.py:55
  74.3 4.8 %collective-permute-start.22 = (bf16[8,3072]{1,0:T(8,128)(2,1)S(1)}, bf16[8,3072]{1,0:T(8,128)(2,1)S(1)}, u32[]{:S(2)}, u32[]{:S(2)}) collective-permute-start(bf16[8,3072]{1,0:T(8,128)(2,1)S(1)} %slice.18), channel_id=1, source_target_pairs={{0,4},{4,8},{8,12},{12,14},{14,10},{10,6},{6,2},{2,0},{1,5},{5,9},... | collective-permute-start | bytes 147464 | tf_op jit(solution)/shard_map/ppermute | solution.py:55
  74.6 4.5 %collective-permute-start.23 = (bf16[8,3072]{1,0:T(8,128)(2,1)S(1)}, bf16[8,3072]{1,0:T(8,128)(2,1)S(1)}, u32[]{:S(2)}, u32[]{:S(2)}) collective-permute-start(bf16[8,3072]{1,0:T(8,128)(2,1)S(1)} %slice.19), channel_id=1, source_target_pairs={{0,2},{4,0},{8,4},{12,8},{14,12},{10,14},{6,10},{2,6},{1,3},{5,1},... | collective-permute-start | bytes 147464 | tf_op jit(solution)/shard_map/ppermute | solution.py:55
  84.2 1.6 %collective-permute-start.24 = (f32[4,8,2304]{2,1,0:T(8,128)S(1)}, f32[4,8,2304]{2,1,0:T(8,128)S(1)}, u32[]{:S(2)}, u32[]{:S(2)}) collective-permute-start(f32[4,8,2304]{2,1,0:T(8,128)S(1)} %get-tuple-element.104), channel_id=1, source_target_pairs={{0,1},{1,0},{2,3},{3,2},{4,5},{5,4},{6,7},{7,6},{8,9},{9,8},{10,11... | collective-permute-start | bytes 884744 | tf_op jit(solution)/shard_map/ppermute | solution.py:44

commit v17 on v16

--- a/solution.py
+++ b/solution.py
@@ -497,7 +497,8 @@
     ring = Ring(n)
     query_cols, width = query_weight.shape
     new_cols = keyval_weight.shape[0]
-    piece = query_cols // 4
+    unit = query_cols // 6
+    sizes = [2 * unit, 2 * unit, unit, unit]
     weights = []
 
     indices = jnp.arange(DH // 2, dtype=jnp.float32)
@@ -518,7 +519,7 @@
             sums = [row_sums([activations, *arrived] if step == 2 else arrived, sums)]
         if step == 3:
             far_sums = lax.ppermute(sums[0][: activations.shape[0]], "gx", ring.across)
-        weight = piece_of(query_weight, (step - 1) * piece, piece, arrived)
+        weight = piece_of(query_weight, sum(sizes[: step - 1]), sizes[step - 1], arrived)
         weight, (left, right, *sums) = before(weight, left, right, *sums)
         weights.append(weight)
         shards += [left, right]
@@ -527,8 +528,8 @@
     )
     far = ring.step(cut, cut_right)
     sums = row_sums([left, right], sums)
-    jobs = [(query_weight, 3 * piece, piece, 0), (keyval_weight, 0, new_cols, piece)]
-    weight = load(piece + new_cols, jobs, [sums])
+    jobs = [(query_weight, 5 * unit, unit, 0), (keyval_weight, 0, new_cols, unit)]
+    weight = load(unit + new_cols, jobs, [sums])
     sums = jnp.concatenate([sums, far_sums], axis=0)
     other_sums = swap_pair(sums)
     weight, (other_sums, *far) = before(weight, other_sums, *far)
@@ -546,8 +547,9 @@
     across = pack([(0, 1), (1, 1), (2, 1), (3, 1)], *arrived)
     last = exchange(across, 4)
     values = load_cache(cache_values, [across])
-    done = output_weight.shape[0] // 6
-    weight = load(done, [(output_weight, 0, done, 0)], [across])
+    unit = output_weight.shape[0] // 12
+    sizes = [unit, 3 * unit, 3 * unit, 3 * unit, 2 * unit]
+    weight = load(unit, [(output_weight, 0, unit, 0)], [across])
     values, (last,) = before(values, last)
     weight, (last,) = before(weight, last)
     weights = [weight]
@@ -557,18 +559,17 @@
 
     left = right = shard
     shards = [shard]
-    piece = (output_weight.shape[0] - done) // 4
 
     for step in range(1, n // 2):
         arrived = shards[-2:]
         left, right = ring.step(left, right)
-        weight = piece_of(output_weight, done + (step - 1) * piece, piece, arrived)
+        weight = piece_of(output_weight, sum(sizes[:step]), sizes[step], arrived)
         weight, (left, right) = before(weight, left, right)
         weights.append(weight)
         shards += [left, right]
     half = shard.shape[1] // 2
     far = ring.step(left[:, :half], right[:, half:])
-    weight = piece_of(output_weight, done + 3 * piece, piece, [left, right])
+    weight = piece_of(output_weight, sum(sizes[:4]), sizes[4], [left, right])
     weight, far = before(weight, *far)
     weights.append(weight)
     keep, give = output_project(shards, far, weights)

time: 86.7 us -> 84.6 us (0.976)
  waiting for transfers between devices: 12.1 us -> 10.8 us
    ppermute x8, waiting for transfers between devices: 5.9 us -> 3.48 us  [step(): lax.ppermute(right, 'gx', self.back)]
    ppermute x4, waiting for transfers between devices: 1.26 us -> 3.16 us  [exchange(): return lax.ppermute(blocks, 'gx', [(i, i ^ d) for i in range(n)])]
    ppermute x4, starting transfers between devices: 4.86 us -> 3.81 us  [exchange(): return lax.ppermute(blocks, 'gx', [(i, i ^ d) for i in range(n)])]
    ppermute x8, starting transfers between devices: 6.2 us -> 7.19 us  [step(): lax.ppermute(right, 'gx', self.back)]
    ppermute x8, starting transfers between devices: 11.1 us -> 10.2 us  [step(): lax.ppermute(left, 'gx', self.onward)]
  transfers between devices with their start and end apart: 25 -> 25, of which waited for: 11 -> 11; matrix products, arithmetic and copies ran while one was open for 0% -> 0% of each run, Pallas kernels for 36% -> 37%
where the time goes in v17:
time: 84.6 us; the launch traced here: 84.4 us
  Pallas kernels  47.7 us (56%)
  starting transfers between devices  24.8 us (29%)
  waiting for transfers between devices  10.8 us (13%)
  other arithmetic  0.89 us (1%)
    pallas_call x9, Pallas kernels, load(): pl.pallas_call(lambda *refs: load_kernel([job[1:] for job in jobs], *refs...  26 us
    ppermute x8, starting transfers between devices, step(): lax.ppermute(left, 'gx', self.onward)  10.2 us
    pallas_call x1, Pallas kernels, project(): pl.pallas_call(lambda *refs: project_kernel(n, len(weights), *refs), out_...  8.82 us
    ppermute x8, starting transfers between devices, step(): lax.ppermute(right, 'gx', self.back)  7.19 us
    pallas_call x1, Pallas kernels, output_project(): pl.pallas_call(lambda *refs: output_kernel(n, *refs), out_shape=[shape, s...  5.05 us
    pallas_call x2, Pallas kernels, load_cache(): pl.pallas_call(load_cache_kernel, out_shape=pltpu.VMEM(cache.shape, cache...  4.42 us
    ppermute x4, waiting for transfers between devices, swap_pair(): return lax.ppermute(x, 'gy', [(0, 1), (1, 0)])  3.88 us
    ppermute x4, starting transfers between devices, exchange(): return lax.ppermute(blocks, 'gx', [(i, i ^ d) for i in range(n)])  3.81 us
  transfers between devices with their start and end apart: 25, of which 11 were waited for; matrix products, arithmetic and copies ran while one was open for 0% of the time, Pallas kernels for 37%

profile of v17, /device:TPU:0, one launch (start us, length us, event | category | flops | bytes accessed | tf_op | source)
XLA Modules:
  0.0 84.4 jit_solution(10920822598660959927)
XLA Ops:
  0.0 3.0 %collective-permute-start = (bf16[8,9216]{1,0:T(8,128)(2,1)}, bf16[8,9216]{1,0:T(8,128)(2,1)S(1)}, u32[]{:S(2)}, u32[]{:S(2)}) collective-permute-start(bf16[8,9216]{1,0:T(8,128)(2,1)} %refs_3_.1), channel_id=1, source_target_pairs={{0,4},{4,8},{8,12},{12,14},{14,10},{10,6},{6,2},{2,0},{1,5},{5,9},... | collective-permute-start | bytes 442376 | tf_op jit(solution)/shard_map/ppermute | solution.py:55
  3.0 3.8 %load.9.refs_12_ = bf16[512,9216]{1,0:T(8,128)(2,1)S(1)} custom-call(bf16[1536,9216]{1,0:T(8,128)(2,1)} %refs_0_.14), custom_call_target="tpu_custom_call" | custom-call | tf_op jit(solution)/shard_map/load/pallas_call | solution.py:97
  6.8 0.3 collective-permute-done.refs_1_.refs_4_
  7.1 1.4 %collective-permute-done.1.refs_2_.refs_5_ = bf16[8,9216]{1,0:T(8,128)(2,1)S(1)} collective-permute-done((bf16[8,9216]{1,0:T(8,128)(2,1)}, bf16[8,9216]{1,0:T(8,128)(2,1)S(1)}, u32[]{:S(2)}, u32[]{:S(2)}) %collective-permute-start.1) | collective-permute-done | bytes 147488 | tf_op jit(solution)/shard_map/ppermute | solution.py:55
  8.5 1.6 %collective-permute-start.2 = (bf16[8,9216]{1,0:T(8,128)(2,1)S(1)}, bf16[8,9216]{1,0:T(8,128)(2,1)S(1)}, u32[]{:S(2)}, u32[]{:S(2)}) collective-permute-start(bf16[8,9216]{1,0:T(8,128)(2,1)S(1)} %collective-permute-done.refs_1_.refs_4_), channel_id=1, source_target_pairs={{0,4},{4,8},{8,12},{12,14},{14,10},{10,6},{6,2},{2,0},{1,5},{5,9},... | collective-permute-start | bytes 442376 | tf_op jit(solution)/shard_map/ppermute | solution.py:55
  10.1 0.4 collective-permute-start.3
  10.6 0.2 row_sums.3.refs_0_
  10.8 3.8 %load.10.refs_13_ = bf16[512,9216]{1,0:T(8,128)(2,1)S(1)} custom-call(bf16[1536,9216]{1,0:T(8,128)(2,1)} %refs_0_.14, bf16[8,9216]{1,0:T(8,128)(2,1)S(1)} %collective-permute-done.refs_1_.refs_4_, bf16[8,9216]{1,0:T(8,128)(2,1)S(1)} %collective-permute-done.1.refs_2_.refs_5_), custom_call_target="tpu_custom_call" | custom-call | tf_op jit(solution)/shard_map/load/pallas_call | solution.py:97
  14.6 0.6 collective-permute-done.3.refs_2_.refs_7_
  15.3 1.6 %collective-permute-start.4 = (bf16[8,9216]{1,0:T(8,128)(2,1)S(1)}, bf16[8,9216]{1,0:T(8,128)(2,1)S(1)}, u32[]{:S(2)}, u32[]{:S(2)}) collective-permute-start(bf16[8,9216]{1,0:T(8,128)(2,1)S(1)} %collective-permute-done.2.refs_1_.refs_6_), channel_id=1, source_target_pairs={{0,4},{4,8},{8,12},{12,14},{14,10},{10,6},{6,2},{2,0},{1,5},{5,9},... | collective-permute-start | bytes 442376 | tf_op jit(solution)/shard_map/ppermute | solution.py:55
  16.8 0.4 collective-permute-start.5
  17.5 2.9 %collective-permute-start.6 = (f32[8,128]{1,0:T(8,128)S(1)}, f32[8,128]{1,0:T(8,128)S(1)}, u32[]{:S(2)}, u32[]{:S(2)}) collective-permute-start(f32[8,128]{1,0:T(8,128)S(1)} %slice.20), channel_id=1, source_target_pairs={{0,14},{4,10},{8,6},{12,2},{14,0},{10,4},{6,8},{2,12},{1,15},{5,11... | collective-permute-start | bytes 12296 | tf_op jit(solution)/shard_map/ppermute | solution.py:521
  20.3 2.4 %load.11.refs_14_ = bf16[256,9216]{1,0:T(8,128)(2,1)S(1)} custom-call(bf16[1536,9216]{1,0:T(8,128)(2,1)} %refs_0_.14, bf16[8,9216]{1,0:T(8,128)(2,1)S(1)} %collective-permute-done.2.refs_1_.refs_6_, bf16[8,9216]{1,0:T(8,128)(2,1)S(1)} %collective-permute-done.3.refs_2_.refs_7_), custom_call_target="tpu_custom_call" | custom-call | tf_op jit(solution)/shard_map/load/pallas_call | solution.py:97
  22.8 0.8 collective-permute-start.8
  23.6 1.3 %collective-permute-start.9 = (bf16[8,4608]{1,0:T(8,128)(2,1)S(1)}, bf16[8,4608]{1,0:T(8,128)(2,1)S(1)}, u32[]{:S(2)}, u32[]{:S(2)}) collective-permute-start(bf16[8,4608]{1,0:T(8,128)(2,1)S(1)} %slice.16), channel_id=1, source_target_pairs={{0,2},{4,0},{8,4},{12,8},{14,12},{10,14},{6,10},{2,6},{1,3},{5,1},... | collective-permute-start | bytes 221192 | tf_op jit(solution)/shard_map/ppermute | solution.py:55
  25.1 2.7 %load.12.refs_15_ = bf16[320,9216]{1,0:T(8,128)(2,1)S(1)} custom-call(bf16[1536,9216]{1,0:T(8,128)(2,1)} %refs_0_.14, bf16[64,9216]{1,0:T(8,128)(2,1)} %refs_1_.1, f32[56,128]{1,0:T(8,128)S(1)} %row_sums.5.refs_2_), custom_call_target="tpu_custom_call" | custom-call | tf_op jit(solution)/shard_map/load/pallas_call | solution.py:97
  27.9 8.8 %project.1 = (f32[8,4,1664]{2,1,0:T(4,128)S(1)}, f32[8,4,1664]{2,1,0:T(4,128)S(1)}) custom-call(f32[64,128]{1,0:T(8,128)S(1)} %pad_maximum_fusion.1.refs_0_, f32[64,128]{1,0:T(8,128)S(1)} %collective-permute-done.7.refs_1_, f32[1,9216]{1,0:T(1,128)S(1)} %bitcast.3, bf16[8,9216]{1,0:T(8,128)(2,1)S(1)} %copy-done, ...), custom_call_target="tpu_custom_call" | custom-call | tf_op jit(solution)/shard_map/project/pallas_call | solution.py:222
  36.8 0.5 collective-permute-start.10
  37.3 1.1 %collective-permute-done.10.got = f32[8,4,1664]{2,1,0:T(4,128)S(1)} collective-permute-done((f32[8,4,1664]{2,1,0:T(4,128)S(1)}, f32[8,4,1664]{2,1,0:T(4,128)S(1)}, u32[]{:S(2)}, u32[]{:S(2)}) %collective-permute-start.10) | collective-permute-done | bytes 213024 | tf_op jit(solution)/shard_map/ppermute | solution.py:44
  38.4 1.7 %collective-permute-start.11 = (bf16[2,4,1664]{2,1,0:T(4,128)(2,1)S(1)}, bf16[2,4,1664]{2,1,0:T(4,128)(2,1)S(1)}, u32[]{:S(2)}, u32[]{:S(2)}) collective-permute-start(bf16[2,4,1664]{2,1,0:T(4,128)(2,1)S(1)} %get-tuple-element.76.refs_0_), channel_id=1, source_target_pairs={{0,2},{2,0},{4,6},{6,4},{8,10},{10,8},{12,14},{14,12},{1,3},{3,1},... | collective-permute-start | bytes 79880 | tf_op jit(solution)/shard_map/ppermute | solution.py:541
  40.1 1.2 %collective-permute-start.12 = (bf16[2,4,1664]{2,1,0:T(4,128)(2,1)S(1)}, bf16[2,4,1664]{2,1,0:T(4,128)(2,1)S(1)}, u32[]{:S(2)}, u32[]{:S(2)}) collective-permute-start(bf16[2,4,1664]{2,1,0:T(4,128)(2,1)S(1)} %get-tuple-element.78), channel_id=1, source_target_pairs={{0,4},{2,6},{4,0},{6,2},{8,12},{10,14},{12,8},{14,10},{1,5},{3,7},... | collective-permute-start | bytes 79880 | tf_op jit(solution)/shard_map/ppermute | solution.py:541
  41.2 0.7 collective-permute-start.13
  42.0 2.2 %load_cache.2.refs_7_ = bf16[4,2048,256]{2,1,0:T(8,128)(2,1)S(1)} custom-call(bf16[4,2048,256]{2,1,0:T(8,128)(2,1)} %source.2, bf16[2,4,1664]{2,1,0:T(4,128)(2,1)S(1)} %get-tuple-element.76.refs_0_), custom_call_target="tpu_custom_call" | custom-call | tf_op jit(solution)/shard_map/load_cache/pallas_call | solution.py:119
  44.2 1.8 %collective-permute-done.13.refs_3_ = bf16[2,4,1664]{2,1,0:T(4,128)(2,1)S(1)} collective-permute-done((bf16[2,4,1664]{2,1,0:T(4,128)(2,1)S(1)}, bf16[2,4,1664]{2,1,0:T(4,128)(2,1)S(1)}, u32[]{:S(2)}, u32[]{:S(2)}) %collective-permute-start.13) | collective-permute-done | bytes 26656 | tf_op jit(solution)/shard_map/ppermute | solution.py:541
  46.0 0.2 collective-permute-start.14
  46.4 2.2 %load_cache.3.refs_8_ = bf16[4,2048,256]{2,1,0:T(8,128)(2,1)S(1)} custom-call(bf16[4,2048,256]{2,1,0:T(8,128)(2,1)} %source.3, bf16[4,4,1664]{2,1,0:T(4,128)(2,1)S(1)} %pack.1.refs_1_.refs_0_), custom_call_target="tpu_custom_call" | custom-call | tf_op jit(solution)/shard_map/load_cache/pallas_call | solution.py:119
  48.6 1.6 %load.13.refs_9_ = bf16[512,2304]{1,0:T(8,128)(2,1)S(1)} custom-call(bf16[6144,2304]{1,0:T(8,128)(2,1)} %refs_0_.19, bf16[4,4,1664]{2,1,0:T(4,128)(2,1)S(1)} %pack.1.refs_1_.refs_0_), custom_call_target="tpu_custom_call" | custom-call | tf_op jit(solution)/shard_map/load/pallas_call | solution.py:97
  50.2 1.4 %collective-permute-done.14.refs_4_ = bf16[4,4,1664]{2,1,0:T(4,128)(2,1)S(1)} collective-permute-done((bf16[4,4,1664]{2,1,0:T(4,128)(2,1)S(1)}, bf16[4,4,1664]{2,1,0:T(4,128)(2,1)S(1)}, u32[]{:S(2)}, u32[]{:S(2)}) %collective-permute-start.14) | collective-permute-done | bytes 53280 | tf_op jit(solution)/shard_map/ppermute | solution.py:541
  51.6 2.7 %attend.1 = (bf16[4,6144]{1,0:T(4,128)(2,1)S(1)}, bf16[4,6144]{1,0:T(4,128)(2,1)S(1)}) custom-call(s32[4]{0:T(128)S(1)} %copy-done.1, bf16[2,4,1664]{2,1,0:T(4,128)(2,1)S(1)} %get-tuple-element.80.refs_0_, bf16[2,4,1664]{2,1,0:T(4,128)(2,1)S(1)} %collective-permute-done.11.refs_1_, bf16[2,4,1664]{2,1,0:T(4,128)(2,1)S(1)} %collective-permute-done.12.refs_2_, ...), custom_call_target="tpu_custom_call" | custom-call | tf_op jit(solution)/shard_map/attend/pallas_call | solution.py:342
  54.4 1.2 %collective-permute-done.15 = bf16[4,6144]{1,0:T(4,128)(2,1)S(1)} collective-permute-done((bf16[4,6144]{1,0:T(4,128)(2,1)S(1)}, bf16[4,6144]{1,0:T(4,128)(2,1)S(1)}, u32[]{:S(2)}, u32[]{:S(2)}) %collective-permute-start.15) | collective-permute-done | bytes 49184 | tf_op jit(solution)/shard_map/ppermute | solution.py:44
  55.7 0.4 collective-permute-start.16
  56.1 1.7 %collective-permute-start.17 = (bf16[8,6144]{1,0:T(8,128)(2,1)S(1)}, bf16[8,6144]{1,0:T(8,128)(2,1)S(1)}, u32[]{:S(2)}, u32[]{:S(2)}) collective-permute-start(bf16[8,6144]{1,0:T(8,128)(2,1)S(1)} %pad_maximum_fusion.refs_1_.refs_0_), channel_id=1, source_target_pairs={{0,2},{4,0},{8,4},{12,8},{14,12},{10,14},{6,10},{2,6},{1,3},{5,1},... | collective-permute-start | bytes 294920 | tf_op jit(solution)/shard_map/ppermute | solution.py:55
  57.8 3.1 %load.14.refs_10_ = bf16[1536,2304]{1,0:T(8,128)(2,1)S(1)} custom-call(bf16[6144,2304]{1,0:T(8,128)(2,1)} %refs_0_.19, bf16[8,6144]{1,0:T(8,128)(2,1)S(1)} %pad_maximum_fusion.refs_1_.refs_0_), custom_call_target="tpu_custom_call" | custom-call | tf_op jit(solution)/shard_map/load/pallas_call | solution.py:97
  60.9 1.3 %collective-permute-start.18 = (bf16[8,6144]{1,0:T(8,128)(2,1)S(1)}, bf16[8,6144]{1,0:T(8,128)(2,1)S(1)}, u32[]{:S(2)}, u32[]{:S(2)}) collective-permute-start(bf16[8,6144]{1,0:T(8,128)(2,1)S(1)} %collective-permute-done.16.refs_1_), channel_id=1, source_target_pairs={{0,4},{4,8},{8,12},{12,14},{14,10},{10,6},{6,2},{2,0},{1,5},{5,9},... | collective-permute-start | bytes 294920 | tf_op jit(solution)/shard_map/ppermute | solution.py:55
  62.3 0.8 collective-permute-start.19
  63.0 3.1 %load.15.refs_11_ = bf16[1536,2304]{1,0:T(8,128)(2,1)S(1)} custom-call(bf16[6144,2304]{1,0:T(8,128)(2,1)} %refs_0_.19, bf16[8,6144]{1,0:T(8,128)(2,1)S(1)} %collective-permute-done.16.refs_1_, bf16[8,6144]{1,0:T(8,128)(2,1)S(1)} %collective-permute-done.17.refs_2_), custom_call_target="tpu_custom_call" | custom-call | tf_op jit(solution)/shard_map/load/pallas_call | solution.py:97
  66.1 0.7 collective-permute-done.19.refs_2_.refs_4_
  66.9 0.8 collective-permute-start.20
  67.7 1.2 %collective-permute-start.21 = (bf16[8,6144]{1,0:T(8,128)(2,1)S(1)}, bf16[8,6144]{1,0:T(8,128)(2,1)S(1)}, u32[]{:S(2)}, u32[]{:S(2)}) collective-permute-start(bf16[8,6144]{1,0:T(8,128)(2,1)S(1)} %collective-permute-done.19.refs_2_.refs_4_), channel_id=1, source_target_pairs={{0,2},{4,0},{8,4},{12,8},{14,12},{10,14},{6,10},{2,6},{1,3},{5,1},... | collective-permute-start | bytes 294920 | tf_op jit(solution)/shard_map/ppermute | solution.py:55
  68.9 3.1 %load.16.refs_12_ = bf16[1536,2304]{1,0:T(8,128)(2,1)S(1)} custom-call(bf16[6144,2304]{1,0:T(8,128)(2,1)} %refs_0_.19, bf16[8,6144]{1,0:T(8,128)(2,1)S(1)} %collective-permute-done.18.refs_1_.refs_3_, bf16[8,6144]{1,0:T(8,128)(2,1)S(1)} %collective-permute-done.19.refs_2_.refs_4_), custom_call_target="tpu_custom_call" | custom-call | tf_op jit(solution)/shard_map/load/pallas_call | solution.py:97
  72.0 0.3 collective-permute-done.21.refs_2_.refs_6_
  72.3 0.6 collective-permute-start.22
  72.9 1.4 %collective-permute-start.23 = (bf16[8,3072]{1,0:T(8,128)(2,1)S(1)}, bf16[8,3072]{1,0:T(8,128)(2,1)S(1)}, u32[]{:S(2)}, u32[]{:S(2)}) collective-permute-start(bf16[8,3072]{1,0:T(8,128)(2,1)S(1)} %slice.19), channel_id=1, source_target_pairs={{0,2},{4,0},{8,4},{12,8},{14,12},{10,14},{6,10},{2,6},{1,3},{5,1},... | collective-permute-start | bytes 147464 | tf_op jit(solution)/shard_map/ppermute | solution.py:55
  74.4 2.4 %load.17.refs_13_ = bf16[1024,2304]{1,0:T(8,128)(2,1)S(1)} custom-call(bf16[6144,2304]{1,0:T(8,128)(2,1)} %refs_0_.19, bf16[8,6144]{1,0:T(8,128)(2,1)S(1)} %collective-permute-done.20.refs_1_.refs_5_, bf16[8,6144]{1,0:T(8,128)(2,1)S(1)} %collective-permute-done.21.refs_2_.refs_6_), custom_call_target="tpu_custom_call" | custom-call | tf_op jit(solution)/shard_map/load/pallas_call | solution.py:97
  76.8 0.3 collective-permute-done.23.refs_8_
  77.0 5.0 %output_project.1 = (f32[4,8,2304]{2,1,0:T(8,128)S(1)}, f32[4,8,2304]{2,1,0:T(8,128)S(1)}) custom-call(bf16[8,6144]{1,0:T(8,128)(2,1)S(1)} %pad_maximum_fusion.refs_1_.refs_0_, bf16[8,6144]{1,0:T(8,128)(2,1)S(1)} %collective-permute-done.16.refs_1_, bf16[8,6144]{1,0:T(8,128)(2,1)S(1)} %collective-permute-done.17.refs_2_, ...), custom_call_target="tpu_custom_call" | custom-call | tf_op jit(solution)/shard_map/output_project/pallas_call | solution.py:397
  82.2 1.6 %collective-permute-done.24 = f32[4,8,2304]{2,1,0:T(8,128)S(1)} collective-permute-done((f32[4,8,2304]{2,1,0:T(8,128)S(1)}, f32[4,8,2304]{2,1,0:T(8,128)S(1)}, u32[]{:S(2)}, u32[]{:S(2)}) %collective-permute-start.24) | collective-permute-done | bytes 294944 | tf_op jit(solution)/shard_map/ppermute | solution.py:44
  83.7 0.7 fusion
  (39 shorter events, 0.9 us)
Async XLA Ops:
  0.0 10.6 %copy-start = (bf16[8,9216]{1,0:T(8,128)(2,1)S(1)}, bf16[8,9216]{1,0:T(8,128)(2,1)}, u32[]{:S(2)}) copy-start(bf16[8,9216]{1,0:T(8,128)(2,1)} %refs_3_.1) | copy-start | bytes 442372
  0.0 7.1 %collective-permute-start = (bf16[8,9216]{1,0:T(8,128)(2,1)}, bf16[8,9216]{1,0:T(8,128)(2,1)S(1)}, u32[]{:S(2)}, u32[]{:S(2)}) collective-permute-start(bf16[8,9216]{1,0:T(8,128)(2,1)} %refs_3_.1), channel_id=1, source_target_pairs={{0,4},{4,8},{8,12},{12,14},{14,10},{10,6},{6,2},{2,0},{1,5},{5,9},... | collective-permute-start | bytes 442376 | tf_op jit(solution)/shard_map/ppermute | solution.py:55
  3.0 5.5 %collective-permute-start.1 = (bf16[8,9216]{1,0:T(8,128)(2,1)}, bf16[8,9216]{1,0:T(8,128)(2,1)S(1)}, u32[]{:S(2)}, u32[]{:S(2)}) collective-permute-start(bf16[8,9216]{1,0:T(8,128)(2,1)} %refs_3_.1), channel_id=1, source_target_pairs={{0,2},{4,0},{8,4},{12,8},{14,12},{10,14},{6,10},{2,6},{1,3},{5,1},... | collective-permute-start | bytes 442376 | tf_op jit(solution)/shard_map/ppermute | solution.py:55
  8.5 6.1 %collective-permute-start.2 = (bf16[8,9216]{1,0:T(8,128)(2,1)S(1)}, bf16[8,9216]{1,0:T(8,128)(2,1)S(1)}, u32[]{:S(2)}, u32[]{:S(2)}) collective-permute-start(bf16[8,9216]{1,0:T(8,128)(2,1)S(1)} %collective-permute-done.refs_1_.refs_4_), channel_id=1, source_target_pairs={{0,4},{4,8},{8,12},{12,14},{14,10},{10,6},{6,2},{2,0},{1,5},{5,9},... | collective-permute-start | bytes 442376 | tf_op jit(solution)/shard_map/ppermute | solution.py:55
  10.1 5.1 %collective-permute-start.3 = (bf16[8,9216]{1,0:T(8,128)(2,1)S(1)}, bf16[8,9216]{1,0:T(8,128)(2,1)S(1)}, u32[]{:S(2)}, u32[]{:S(2)}) collective-permute-start(bf16[8,9216]{1,0:T(8,128)(2,1)S(1)} %collective-permute-done.1.refs_2_.refs_5_), channel_id=1, source_target_pairs={{0,2},{4,0},{8,4},{12,8},{14,12},{10,14},{6,10},{2,6},{1,3},{5,1},... | collective-permute-start | bytes 442376 | tf_op jit(solution)/shard_map/ppermute | solution.py:55
  15.3 7.5 %collective-permute-start.4 = (bf16[8,9216]{1,0:T(8,128)(2,1)S(1)}, bf16[8,9216]{1,0:T(8,128)(2,1)S(1)}, u32[]{:S(2)}, u32[]{:S(2)}) collective-permute-start(bf16[8,9216]{1,0:T(8,128)(2,1)S(1)} %collective-permute-done.2.refs_1_.refs_6_), channel_id=1, source_target_pairs={{0,4},{4,8},{8,12},{12,14},{14,10},{10,6},{6,2},{2,0},{1,5},{5,9},... | collective-permute-start | bytes 442376 | tf_op jit(solution)/shard_map/ppermute | solution.py:55
  16.8 5.9 %collective-permute-start.5 = (bf16[8,9216]{1,0:T(8,128)(2,1)S(1)}, bf16[8,9216]{1,0:T(8,128)(2,1)S(1)}, u32[]{:S(2)}, u32[]{:S(2)}) collective-permute-start(bf16[8,9216]{1,0:T(8,128)(2,1)S(1)} %collective-permute-done.3.refs_2_.refs_7_), channel_id=1, source_target_pairs={{0,2},{4,0},{8,4},{12,8},{14,12},{10,14},{6,10},{2,6},{1,3},{5,1},... | collective-permute-start | bytes 442376 | tf_op jit(solution)/shard_map/ppermute | solution.py:55
  17.5 7.6 %copy-start.2 = (bf16[9216]{0:T(1024)(128)(2,1)S(1)}, bf16[9216]{0:T(1024)(128)(2,1)}, u32[]{:S(2)}) copy-start(bf16[9216]{0:T(1024)(128)(2,1)} %param.9) | copy-start | bytes 55300
  17.5 7.6 %collective-permute-start.6 = (f32[8,128]{1,0:T(8,128)S(1)}, f32[8,128]{1,0:T(8,128)S(1)}, u32[]{:S(2)}, u32[]{:S(2)}) collective-permute-start(f32[8,128]{1,0:T(8,128)S(1)} %slice.20), channel_id=1, source_target_pairs={{0,14},{4,10},{8,6},{12,2},{14,0},{10,4},{6,8},{2,12},{1,15},{5,11... | collective-permute-start | bytes 12296 | tf_op jit(solution)/shard_map/ppermute | solution.py:521
  22.8 5.1 %collective-permute-start.8 = (bf16[8,4608]{1,0:T(8,128)(2,1)S(1)}, bf16[8,4608]{1,0:T(8,128)(2,1)S(1)}, u32[]{:S(2)}, u32[]{:S(2)}) collective-permute-start(bf16[8,4608]{1,0:T(8,128)(2,1)S(1)} %slice.15), channel_id=1, source_target_pairs={{0,4},{4,8},{8,12},{12,14},{14,10},{10,6},{6,2},{2,0},{1,5},{5,9},... | collective-permute-start | bytes 221192 | tf_op jit(solution)/shard_map/ppermute | solution.py:55
  23.6 4.4 %collective-permute-start.9 = (bf16[8,4608]{1,0:T(8,128)(2,1)S(1)}, bf16[8,4608]{1,0:T(8,128)(2,1)S(1)}, u32[]{:S(2)}, u32[]{:S(2)}) collective-permute-start(bf16[8,4608]{1,0:T(8,128)(2,1)S(1)} %slice.16), channel_id=1, source_target_pairs={{0,2},{4,0},{8,4},{12,8},{14,12},{10,14},{6,10},{2,6},{1,3},{5,1},... | collective-permute-start | bytes 221192 | tf_op jit(solution)/shard_map/ppermute | solution.py:55
  25.0 2.8 %collective-permute-start.7 = (f32[64,128]{1,0:T(8,128)S(1)}, f32[64,128]{1,0:T(8,128)S(1)}, u32[]{:S(2)}, u32[]{:S(2)}) collective-permute-start(f32[64,128]{1,0:T(8,128)S(1)} %pad_maximum_fusion.1.refs_0_), channel_id=1, source_target_pairs={{0,1},{1,0},{2,3},{3,2},{4,5},{5,4},{6,7},{7,6},{8,9},{9,8},{10,11... | collective-permute-start | bytes 98312 | tf_op jit(solution)/shard_map/ppermute | solution.py:44
  27.9 14.1 %copy-start.1 = (s32[4]{0:T(128)S(1)}, s32[4]{0:T(128)}, u32[]{:S(2)}) copy-start(s32[4]{0:T(128)} %lengths.1) | copy-start | bytes 52
  36.8 1.6 %collective-permute-start.10 = (f32[8,4,1664]{2,1,0:T(4,128)S(1)}, f32[8,4,1664]{2,1,0:T(4,128)S(1)}, u32[]{:S(2)}, u32[]{:S(2)}) collective-permute-start(f32[8,4,1664]{2,1,0:T(4,128)S(1)} %get-tuple-element.75), channel_id=1, source_target_pairs={{0,1},{1,0},{2,3},{3,2},{4,5},{5,4},{6,7},{7,6},{8,9},{9,8},{10,11... | collective-permute-start | bytes 638984 | tf_op jit(solution)/shard_map/ppermute | solution.py:44
  38.4 5.8 %collective-permute-start.11 = (bf16[2,4,1664]{2,1,0:T(4,128)(2,1)S(1)}, bf16[2,4,1664]{2,1,0:T(4,128)(2,1)S(1)}, u32[]{:S(2)}, u32[]{:S(2)}) collective-permute-start(bf16[2,4,1664]{2,1,0:T(4,128)(2,1)S(1)} %get-tuple-element.76.refs_0_), channel_id=1, source_target_pairs={{0,2},{2,0},{4,6},{6,4},{8,10},{10,8},{12,14},{14,12},{1,3},{3,1},... | collective-permute-start | bytes 79880 | tf_op jit(solution)/shard_map/ppermute | solution.py:541
  40.1 4.2 %collective-permute-start.12 = (bf16[2,4,1664]{2,1,0:T(4,128)(2,1)S(1)}, bf16[2,4,1664]{2,1,0:T(4,128)(2,1)S(1)}, u32[]{:S(2)}, u32[]{:S(2)}) collective-permute-start(bf16[2,4,1664]{2,1,0:T(4,128)(2,1)S(1)} %get-tuple-element.78), channel_id=1, source_target_pairs={{0,4},{2,6},{4,0},{6,2},{8,12},{10,14},{12,8},{14,10},{1,5},{3,7},... | collective-permute-start | bytes 79880 | tf_op jit(solution)/shard_map/ppermute | solution.py:541
  41.2 4.7 %collective-permute-start.13 = (bf16[2,4,1664]{2,1,0:T(4,128)(2,1)S(1)}, bf16[2,4,1664]{2,1,0:T(4,128)(2,1)S(1)}, u32[]{:S(2)}, u32[]{:S(2)}) collective-permute-start(bf16[2,4,1664]{2,1,0:T(4,128)(2,1)S(1)} %get-tuple-element.79), channel_id=1, source_target_pairs={{0,6},{2,4},{4,2},{6,0},{8,14},{10,12},{12,10},{14,8},{1,7},{3,5},... | collective-permute-start | bytes 79880 | tf_op jit(solution)/shard_map/ppermute | solution.py:541
  46.0 5.6 %collective-permute-start.14 = (bf16[4,4,1664]{2,1,0:T(4,128)(2,1)S(1)}, bf16[4,4,1664]{2,1,0:T(4,128)(2,1)S(1)}, u32[]{:S(2)}, u32[]{:S(2)}) collective-permute-start(bf16[4,4,1664]{2,1,0:T(4,128)(2,1)S(1)} %pack.1.refs_1_.refs_0_), channel_id=1, source_target_pairs={{0,8},{2,10},{4,12},{6,14},{8,0},{10,2},{12,4},{14,6},{1,9},{3,11}... | collective-permute-start | bytes 159752 | tf_op jit(solution)/shard_map/ppermute | solution.py:541
  54.4 1.3 %collective-permute-start.15 = (bf16[4,6144]{1,0:T(4,128)(2,1)S(1)}, bf16[4,6144]{1,0:T(4,128)(2,1)S(1)}, u32[]{:S(2)}, u32[]{:S(2)}) collective-permute-start(bf16[4,6144]{1,0:T(4,128)(2,1)S(1)} %get-tuple-element.89), channel_id=1, source_target_pairs={{0,1},{1,0},{2,3},{3,2},{4,5},{5,4},{6,7},{7,6},{8,9},{9,8},{10,11... | collective-permute-start | bytes 147464 | tf_op jit(solution)/shard_map/ppermute | solution.py:44
  55.7 5.2 %collective-permute-start.16 = (bf16[8,6144]{1,0:T(8,128)(2,1)S(1)}, bf16[8,6144]{1,0:T(8,128)(2,1)S(1)}, u32[]{:S(2)}, u32[]{:S(2)}) collective-permute-start(bf16[8,6144]{1,0:T(8,128)(2,1)S(1)} %pad_maximum_fusion.refs_1_.refs_0_), channel_id=1, source_target_pairs={{0,4},{4,8},{8,12},{12,14},{14,10},{10,6},{6,2},{2,0},{1,5},{5,9},... | collective-permute-start | bytes 294920 | tf_op jit(solution)/shard_map/ppermute | solution.py:55
  56.1 4.8 %collective-permute-start.17 = (bf16[8,6144]{1,0:T(8,128)(2,1)S(1)}, bf16[8,6144]{1,0:T(8,128)(2,1)S(1)}, u32[]{:S(2)}, u32[]{:S(2)}) collective-permute-start(bf16[8,6144]{1,0:T(8,128)(2,1)S(1)} %pad_maximum_fusion.refs_1_.refs_0_), channel_id=1, source_target_pairs={{0,2},{4,0},{8,4},{12,8},{14,12},{10,14},{6,10},{2,6},{1,3},{5,1},... | collective-permute-start | bytes 294920 | tf_op jit(solution)/shard_map/ppermute | solution.py:55
  60.9 5.2 %collective-permute-start.18 = (bf16[8,6144]{1,0:T(8,128)(2,1)S(1)}, bf16[8,6144]{1,0:T(8,128)(2,1)S(1)}, u32[]{:S(2)}, u32[]{:S(2)}) collective-permute-start(bf16[8,6144]{1,0:T(8,128)(2,1)S(1)} %collective-permute-done.16.refs_1_), channel_id=1, source_target_pairs={{0,4},{4,8},{8,12},{12,14},{14,10},{10,6},{6,2},{2,0},{1,5},{5,9},... | collective-permute-start | bytes 294920 | tf_op jit(solution)/shard_map/ppermute | solution.py:55
  62.3 4.6 %collective-permute-start.19 = (bf16[8,6144]{1,0:T(8,128)(2,1)S(1)}, bf16[8,6144]{1,0:T(8,128)(2,1)S(1)}, u32[]{:S(2)}, u32[]{:S(2)}) collective-permute-start(bf16[8,6144]{1,0:T(8,128)(2,1)S(1)} %collective-permute-done.17.refs_2_), channel_id=1, source_target_pairs={{0,2},{4,0},{8,4},{12,8},{14,12},{10,14},{6,10},{2,6},{1,3},{5,1},... | collective-permute-start | bytes 294920 | tf_op jit(solution)/shard_map/ppermute | solution.py:55
  66.9 5.1 %collective-permute-start.20 = (bf16[8,6144]{1,0:T(8,128)(2,1)S(1)}, bf16[8,6144]{1,0:T(8,128)(2,1)S(1)}, u32[]{:S(2)}, u32[]{:S(2)}) collective-permute-start(bf16[8,6144]{1,0:T(8,128)(2,1)S(1)} %collective-permute-done.18.refs_1_.refs_3_), channel_id=1, source_target_pairs={{0,4},{4,8},{8,12},{12,14},{14,10},{10,6},{6,2},{2,0},{1,5},{5,9},... | collective-permute-start | bytes 294920 | tf_op jit(solution)/shard_map/ppermute | solution.py:55
  67.7 4.6 %collective-permute-start.21 = (bf16[8,6144]{1,0:T(8,128)(2,1)S(1)}, bf16[8,6144]{1,0:T(8,128)(2,1)S(1)}, u32[]{:S(2)}, u32[]{:S(2)}) collective-permute-start(bf16[8,6144]{1,0:T(8,128)(2,1)S(1)} %collective-permute-done.19.refs_2_.refs_4_), channel_id=1, source_target_pairs={{0,2},{4,0},{8,4},{12,8},{14,12},{10,14},{6,10},{2,6},{1,3},{5,1},... | collective-permute-start | bytes 294920 | tf_op jit(solution)/shard_map/ppermute | solution.py:55
  72.3 4.4 %collective-permute-start.22 = (bf16[8,3072]{1,0:T(8,128)(2,1)S(1)}, bf16[8,3072]{1,0:T(8,128)(2,1)S(1)}, u32[]{:S(2)}, u32[]{:S(2)}) collective-permute-start(bf16[8,3072]{1,0:T(8,128)(2,1)S(1)} %slice.18), channel_id=1, source_target_pairs={{0,4},{4,8},{8,12},{12,14},{14,10},{10,6},{6,2},{2,0},{1,5},{5,9},... | collective-permute-start | bytes 147464 | tf_op jit(solution)/shard_map/ppermute | solution.py:55
  72.9 4.1 %collective-permute-start.23 = (bf16[8,3072]{1,0:T(8,128)(2,1)S(1)}, bf16[8,3072]{1,0:T(8,128)(2,1)S(1)}, u32[]{:S(2)}, u32[]{:S(2)}) collective-permute-start(bf16[8,3072]{1,0:T(8,128)(2,1)S(1)} %slice.19), channel_id=1, source_target_pairs={{0,2},{4,0},{8,4},{12,8},{14,12},{10,14},{6,10},{2,6},{1,3},{5,1},... | collective-permute-start | bytes 147464 | tf_op jit(solution)/shard_map/ppermute | solution.py:55
  82.1 1.6 %collective-permute-start.24 = (f32[4,8,2304]{2,1,0:T(8,128)S(1)}, f32[4,8,2304]{2,1,0:T(8,128)S(1)}, u32[]{:S(2)}, u32[]{:S(2)}) collective-permute-start(f32[4,8,2304]{2,1,0:T(8,128)S(1)} %get-tuple-element.104), channel_id=1, source_target_pairs={{0,1},{1,0},{2,3},{3,2},{4,5},{5,4},{6,7},{7,6},{8,9},{9,8},{10,11... | collective-permute-start | bytes 884744 | tf_op jit(solution)/shard_map/ppermute | solution.py:44

commit v18 on v17

--- a/solution.py
+++ b/solution.py
@@ -356,31 +356,29 @@
 def output_kernel(n, *refs):
     shards = refs[: n - 1]
     far = refs[n - 1 : n + 1]
-    weights = refs[n + 1 : -4]
-    keep, give, total, placed = refs[-4:]
+    weights = refs[n + 1 : -5]
+    keep, give, rounded, total, placed = refs[-5:]
     rows = shards[0].shape[0]
     half = far[0].shape[1]
     for part in range(2):
-        start = part * half
-        cols = slice(start, start + half)
+        cols = slice(part * half, (part + 1) * half)
         x = [ref[:, cols] for ref in shards] + [far[part][...]]
         x = jnp.concatenate([piece.astype(jnp.float32) for piece in x], axis=0)
-        x = x.astype(jnp.bfloat16)
+        rounded[:, cols] = x.astype(jnp.bfloat16)
+    width = total.shape[1] // 3
+    for start in range(0, total.shape[1], width):
+        cols = slice(start, start + width)
         first = 0
+        terms = []
         for weight in weights:
             last = first + weight.shape[0]
-            low, high = max(first, start), min(last, start + half)
-            if low < high:
-                term = jnp.dot(
-                    x[:, low - start : high - start],
-                    weight[low - first : high - first, :],
-                    preferred_element_type=jnp.float32,
+            terms.append(
+                jnp.dot(
+                    rounded[:, first:last], weight[:, cols], preferred_element_type=jnp.float32
                 )
-                if low == 0:
-                    total[...] = term
-                else:
-                    total[...] += term
+            )
             first = last
+        total[:, cols] = sum(terms[1:], terms[0])
     side = lax.axis_index("gy")
     for i, owner in enumerate(owners(n)):
         block = total[i * rows : (i + 1) * rows, :]
@@ -400,6 +398,7 @@
         in_specs=[IN_VMEM] * (n + 1 + len(weights)),
         out_specs=[IN_VMEM] * 2,
         scratch_shapes=[
+            pltpu.VMEM((n * rows, 2 * far[0].shape[1]), jnp.bfloat16),
             pltpu.VMEM((n * rows, cols), jnp.float32),
             pltpu.VMEM((n, rows, cols), jnp.float32),
         ],
@@ -498,7 +497,7 @@
     query_cols, width = query_weight.shape
     new_cols = keyval_weight.shape[0]
     unit = query_cols // 6
-    sizes = [2 * unit, 2 * unit, unit, unit]
+    sizes = [5 * unit // 2, 2 * unit, unit // 2, unit]
     weights = []
 
     indices = jnp.arange(DH // 2, dtype=jnp.float32)

time: 84.6 us -> 84.9 us (level)
  starting transfers between devices: 24.8 us -> 26.2 us
  waiting for transfers between devices: 10.8 us -> 9.44 us
    ppermute x4, waiting for transfers between devices: 3.16 us -> 1.64 us  [exchange(): return lax.ppermute(blocks, 'gx', [(i, i ^ d) for i in range(n)])]
    ppermute x4, starting transfers between devices: 3.81 us -> 4.75 us  [exchange(): return lax.ppermute(blocks, 'gx', [(i, i ^ d) for i in range(n)])]
    ppermute x8, starting transfers between devices: 7.19 us -> 6.28 us  [step(): lax.ppermute(right, 'gx', self.back)]
    ppermute x8, starting transfers between devices: 10.2 us -> 11.1 us  [step(): lax.ppermute(left, 'gx', self.onward)]
where the time goes in v18:
time: 84.9 us; the launch traced here: 84.7 us
  Pallas kernels  47.8 us (56%)
  starting transfers between devices  26.2 us (31%)
  waiting for transfers between devices  9.44 us (11%)
  other arithmetic  0.89 us (1%)
    pallas_call x9, Pallas kernels, load(): pl.pallas_call(lambda *refs: load_kernel([job[1:] for job in jobs], *refs...  25.9 us
    ppermute x8, starting transfers between devices, step(): lax.ppermute(left, 'gx', self.onward)  11.1 us
    pallas_call x1, Pallas kernels, project(): pl.pallas_call(lambda *refs: project_kernel(n, len(weights), *refs), out_...  9.08 us
    ppermute x8, starting transfers between devices, step(): lax.ppermute(right, 'gx', self.back)  6.28 us
    pallas_call x1, Pallas kernels, output_project(): pl.pallas_call(lambda *refs: output_kernel(n, *refs), out_shape=[shape, s...  5.05 us
    ppermute x4, starting transfers between devices, exchange(): return lax.ppermute(blocks, 'gx', [(i, i ^ d) for i in range(n)])  4.75 us
    pallas_call x2, Pallas kernels, load_cache(): pl.pallas_call(load_cache_kernel, out_shape=pltpu.VMEM(cache.shape, cache...  4.42 us
    ppermute x4, waiting for transfers between devices, swap_pair(): return lax.ppermute(x, 'gy', [(0, 1), (1, 0)])  3.94 us
  transfers between devices with their start and end apart: 25, of which 11 were waited for; matrix products, arithmetic and copies ran while one was open for 0% of the time, Pallas kernels for 37%

profile of v18, /device:TPU:0, one launch (start us, length us, event | category | flops | bytes accessed | tf_op | source)
XLA Modules:
  0.0 84.7 jit_solution(3007908688802302194)
XLA Ops:
  0.0 3.0 %collective-permute-start = (bf16[8,9216]{1,0:T(8,128)(2,1)}, bf16[8,9216]{1,0:T(8,128)(2,1)S(1)}, u32[]{:S(2)}, u32[]{:S(2)}) collective-permute-start(bf16[8,9216]{1,0:T(8,128)(2,1)} %refs_3_.1), channel_id=1, source_target_pairs={{0,4},{4,8},{8,12},{12,14},{14,10},{10,6},{6,2},{2,0},{1,5},{5,9},... | collective-permute-start | bytes 442376 | tf_op jit(solution)/shard_map/ppermute | solution.py:55
  3.0 4.5 %load.9.refs_12_ = bf16[640,9216]{1,0:T(8,128)(2,1)S(1)} custom-call(bf16[1536,9216]{1,0:T(8,128)(2,1)} %refs_0_.14), custom_call_target="tpu_custom_call" | custom-call | tf_op jit(solution)/shard_map/load/pallas_call | solution.py:97
  7.5 1.0 %collective-permute-done.1.refs_2_.refs_5_ = bf16[8,9216]{1,0:T(8,128)(2,1)S(1)} collective-permute-done((bf16[8,9216]{1,0:T(8,128)(2,1)}, bf16[8,9216]{1,0:T(8,128)(2,1)S(1)}, u32[]{:S(2)}, u32[]{:S(2)}) %collective-permute-start.1) | collective-permute-done | bytes 147488 | tf_op jit(solution)/shard_map/ppermute | solution.py:55
  8.5 1.6 %collective-permute-start.2 = (bf16[8,9216]{1,0:T(8,128)(2,1)S(1)}, bf16[8,9216]{1,0:T(8,128)(2,1)S(1)}, u32[]{:S(2)}, u32[]{:S(2)}) collective-permute-start(bf16[8,9216]{1,0:T(8,128)(2,1)S(1)} %collective-permute-done.refs_1_.refs_4_), channel_id=1, source_target_pairs={{0,4},{4,8},{8,12},{12,14},{14,10},{10,6},{6,2},{2,0},{1,5},{5,9},... | collective-permute-start | bytes 442376 | tf_op jit(solution)/shard_map/ppermute | solution.py:55
  10.1 0.4 collective-permute-start.3
  10.6 0.2 row_sums.3.refs_0_
  10.8 3.8 %load.10.refs_13_ = bf16[512,9216]{1,0:T(8,128)(2,1)S(1)} custom-call(bf16[1536,9216]{1,0:T(8,128)(2,1)} %refs_0_.14, bf16[8,9216]{1,0:T(8,128)(2,1)S(1)} %collective-permute-done.refs_1_.refs_4_, bf16[8,9216]{1,0:T(8,128)(2,1)S(1)} %collective-permute-done.1.refs_2_.refs_5_), custom_call_target="tpu_custom_call" | custom-call | tf_op jit(solution)/shard_map/load/pallas_call | solution.py:97
  14.6 0.6 collective-permute-done.3.refs_2_.refs_7_
  15.3 1.6 %collective-permute-start.4 = (bf16[8,9216]{1,0:T(8,128)(2,1)S(1)}, bf16[8,9216]{1,0:T(8,128)(2,1)S(1)}, u32[]{:S(2)}, u32[]{:S(2)}) collective-permute-start(bf16[8,9216]{1,0:T(8,128)(2,1)S(1)} %collective-permute-done.2.refs_1_.refs_6_), channel_id=1, source_target_pairs={{0,4},{4,8},{8,12},{12,14},{14,10},{10,6},{6,2},{2,0},{1,5},{5,9},... | collective-permute-start | bytes 442376 | tf_op jit(solution)/shard_map/ppermute | solution.py:55
  16.8 0.4 collective-permute-start.5
  17.5 3.5 %collective-permute-start.6 = (f32[8,128]{1,0:T(8,128)S(1)}, f32[8,128]{1,0:T(8,128)S(1)}, u32[]{:S(2)}, u32[]{:S(2)}) collective-permute-start(f32[8,128]{1,0:T(8,128)S(1)} %slice.20), channel_id=1, source_target_pairs={{0,14},{4,10},{8,6},{12,2},{14,0},{10,4},{6,8},{2,12},{1,15},{5,11... | collective-permute-start | bytes 12296 | tf_op jit(solution)/shard_map/ppermute | solution.py:520
  21.0 1.6 %load.11.refs_14_ = bf16[128,9216]{1,0:T(8,128)(2,1)S(1)} custom-call(bf16[1536,9216]{1,0:T(8,128)(2,1)} %refs_0_.14, bf16[8,9216]{1,0:T(8,128)(2,1)S(1)} %collective-permute-done.2.refs_1_.refs_6_, bf16[8,9216]{1,0:T(8,128)(2,1)S(1)} %collective-permute-done.3.refs_2_.refs_7_), custom_call_target="tpu_custom_call" | custom-call | tf_op jit(solution)/shard_map/load/pallas_call | solution.py:97
  22.6 0.9 %collective-permute-start.8 = (bf16[8,4608]{1,0:T(8,128)(2,1)S(1)}, bf16[8,4608]{1,0:T(8,128)(2,1)S(1)}, u32[]{:S(2)}, u32[]{:S(2)}) collective-permute-start(bf16[8,4608]{1,0:T(8,128)(2,1)S(1)} %slice.15), channel_id=1, source_target_pairs={{0,4},{4,8},{8,12},{12,14},{14,10},{10,6},{6,2},{2,0},{1,5},{5,9},... | collective-permute-start | bytes 221192 | tf_op jit(solution)/shard_map/ppermute | solution.py:55
  23.6 1.1 %collective-permute-start.9 = (bf16[8,4608]{1,0:T(8,128)(2,1)S(1)}, bf16[8,4608]{1,0:T(8,128)(2,1)S(1)}, u32[]{:S(2)}, u32[]{:S(2)}) collective-permute-start(bf16[8,4608]{1,0:T(8,128)(2,1)S(1)} %slice.16), channel_id=1, source_target_pairs={{0,2},{4,0},{8,4},{12,8},{14,12},{10,14},{6,10},{2,6},{1,3},{5,1},... | collective-permute-start | bytes 221192 | tf_op jit(solution)/shard_map/ppermute | solution.py:55
  25.0 2.7 %load.12.refs_15_ = bf16[320,9216]{1,0:T(8,128)(2,1)S(1)} custom-call(bf16[1536,9216]{1,0:T(8,128)(2,1)} %refs_0_.14, bf16[64,9216]{1,0:T(8,128)(2,1)} %refs_1_.1, f32[56,128]{1,0:T(8,128)S(1)} %row_sums.5.refs_2_), custom_call_target="tpu_custom_call" | custom-call | tf_op jit(solution)/shard_map/load/pallas_call | solution.py:97
  27.7 0.2 collective-permute-done.9.refs_11_
  27.9 9.1 %project.1 = (f32[8,4,1664]{2,1,0:T(4,128)S(1)}, f32[8,4,1664]{2,1,0:T(4,128)S(1)}) custom-call(f32[64,128]{1,0:T(8,128)S(1)} %pad_maximum_fusion.1.refs_0_, f32[64,128]{1,0:T(8,128)S(1)} %collective-permute-done.7.refs_1_, f32[1,9216]{1,0:T(1,128)S(1)} %bitcast.3, bf16[8,9216]{1,0:T(8,128)(2,1)S(1)} %copy-done, ...), custom_call_target="tpu_custom_call" | custom-call | tf_op jit(solution)/shard_map/project/pallas_call | solution.py:222
  37.0 0.4 collective-permute-start.10
  37.4 1.1 %collective-permute-done.10.got = f32[8,4,1664]{2,1,0:T(4,128)S(1)} collective-permute-done((f32[8,4,1664]{2,1,0:T(4,128)S(1)}, f32[8,4,1664]{2,1,0:T(4,128)S(1)}, u32[]{:S(2)}, u32[]{:S(2)}) %collective-permute-start.10) | collective-permute-done | bytes 213024 | tf_op jit(solution)/shard_map/ppermute | solution.py:44
  38.6 1.2 %collective-permute-start.11 = (bf16[2,4,1664]{2,1,0:T(4,128)(2,1)S(1)}, bf16[2,4,1664]{2,1,0:T(4,128)(2,1)S(1)}, u32[]{:S(2)}, u32[]{:S(2)}) collective-permute-start(bf16[2,4,1664]{2,1,0:T(4,128)(2,1)S(1)} %get-tuple-element.76.refs_0_), channel_id=1, source_target_pairs={{0,2},{2,0},{4,6},{6,4},{8,10},{10,8},{12,14},{14,12},{1,3},{3,1},... | collective-permute-start | bytes 79880 | tf_op jit(solution)/shard_map/ppermute | solution.py:540
  39.8 1.0 %collective-permute-start.12 = (bf16[2,4,1664]{2,1,0:T(4,128)(2,1)S(1)}, bf16[2,4,1664]{2,1,0:T(4,128)(2,1)S(1)}, u32[]{:S(2)}, u32[]{:S(2)}) collective-permute-start(bf16[2,4,1664]{2,1,0:T(4,128)(2,1)S(1)} %get-tuple-element.78), channel_id=1, source_target_pairs={{0,4},{2,6},{4,0},{6,2},{8,12},{10,14},{12,8},{14,10},{1,5},{3,7},... | collective-permute-start | bytes 79880 | tf_op jit(solution)/shard_map/ppermute | solution.py:540
  40.9 1.3 %collective-permute-start.13 = (bf16[2,4,1664]{2,1,0:T(4,128)(2,1)S(1)}, bf16[2,4,1664]{2,1,0:T(4,128)(2,1)S(1)}, u32[]{:S(2)}, u32[]{:S(2)}) collective-permute-start(bf16[2,4,1664]{2,1,0:T(4,128)(2,1)S(1)} %get-tuple-element.79), channel_id=1, source_target_pairs={{0,6},{2,4},{4,2},{6,0},{8,14},{10,12},{12,10},{14,8},{1,7},{3,5},... | collective-permute-start | bytes 79880 | tf_op jit(solution)/shard_map/ppermute | solution.py:540
  42.2 2.2 %load_cache.2.refs_7_ = bf16[4,2048,256]{2,1,0:T(8,128)(2,1)S(1)} custom-call(bf16[4,2048,256]{2,1,0:T(8,128)(2,1)} %source.2, bf16[2,4,1664]{2,1,0:T(4,128)(2,1)S(1)} %get-tuple-element.76.refs_0_), custom_call_target="tpu_custom_call" | custom-call | tf_op jit(solution)/shard_map/load_cache/pallas_call | solution.py:119
  44.4 1.2 %collective-permute-done.13.refs_3_ = bf16[2,4,1664]{2,1,0:T(4,128)(2,1)S(1)} collective-permute-done((bf16[2,4,1664]{2,1,0:T(4,128)(2,1)S(1)}, bf16[2,4,1664]{2,1,0:T(4,128)(2,1)S(1)}, u32[]{:S(2)}, u32[]{:S(2)}) %collective-permute-start.13) | collective-permute-done | bytes 26656 | tf_op jit(solution)/shard_map/ppermute | solution.py:540
  45.6 1.2 %collective-permute-start.14 = (bf16[4,4,1664]{2,1,0:T(4,128)(2,1)S(1)}, bf16[4,4,1664]{2,1,0:T(4,128)(2,1)S(1)}, u32[]{:S(2)}, u32[]{:S(2)}) collective-permute-start(bf16[4,4,1664]{2,1,0:T(4,128)(2,1)S(1)} %pack.1.refs_1_.refs_0_), channel_id=1, source_target_pairs={{0,8},{2,10},{4,12},{6,14},{8,0},{10,2},{12,4},{14,6},{1,9},{3,11}... | collective-permute-start | bytes 159752 | tf_op jit(solution)/shard_map/ppermute | solution.py:540
  46.9 2.2 %load_cache.3.refs_8_ = bf16[4,2048,256]{2,1,0:T(8,128)(2,1)S(1)} custom-call(bf16[4,2048,256]{2,1,0:T(8,128)(2,1)} %source.3, bf16[4,4,1664]{2,1,0:T(4,128)(2,1)S(1)} %pack.1.refs_1_.refs_0_), custom_call_target="tpu_custom_call" | custom-call | tf_op jit(solution)/shard_map/load_cache/pallas_call | solution.py:119
  49.1 1.6 %load.13.refs_9_ = bf16[512,2304]{1,0:T(8,128)(2,1)S(1)} custom-call(bf16[6144,2304]{1,0:T(8,128)(2,1)} %refs_0_.19, bf16[4,4,1664]{2,1,0:T(4,128)(2,1)S(1)} %pack.1.refs_1_.refs_0_), custom_call_target="tpu_custom_call" | custom-call | tf_op jit(solution)/shard_map/load/pallas_call | solution.py:97
  50.8 0.4 collective-permute-done.14.refs_4_
  51.2 2.7 %attend.1 = (bf16[4,6144]{1,0:T(4,128)(2,1)S(1)}, bf16[4,6144]{1,0:T(4,128)(2,1)S(1)}) custom-call(s32[4]{0:T(128)S(1)} %copy-done.1, bf16[2,4,1664]{2,1,0:T(4,128)(2,1)S(1)} %get-tuple-element.80.refs_0_, bf16[2,4,1664]{2,1,0:T(4,128)(2,1)S(1)} %collective-permute-done.11.refs_1_, bf16[2,4,1664]{2,1,0:T(4,128)(2,1)S(1)} %collective-permute-done.12.refs_2_, ...), custom_call_target="tpu_custom_call" | custom-call | tf_op jit(solution)/shard_map/attend/pallas_call | solution.py:342
  54.0 1.2 %collective-permute-done.15 = bf16[4,6144]{1,0:T(4,128)(2,1)S(1)} collective-permute-done((bf16[4,6144]{1,0:T(4,128)(2,1)S(1)}, bf16[4,6144]{1,0:T(4,128)(2,1)S(1)}, u32[]{:S(2)}, u32[]{:S(2)}) %collective-permute-start.15) | collective-permute-done | bytes 49184 | tf_op jit(solution)/shard_map/ppermute | solution.py:44
  55.3 0.6 collective-permute-start.16
  55.9 1.5 %collective-permute-start.17 = (bf16[8,6144]{1,0:T(8,128)(2,1)S(1)}, bf16[8,6144]{1,0:T(8,128)(2,1)S(1)}, u32[]{:S(2)}, u32[]{:S(2)}) collective-permute-start(bf16[8,6144]{1,0:T(8,128)(2,1)S(1)} %pad_maximum_fusion.refs_1_.refs_0_), channel_id=1, source_target_pairs={{0,2},{4,0},{8,4},{12,8},{14,12},{10,14},{6,10},{2,6},{1,3},{5,1},... | collective-permute-start | bytes 294920 | tf_op jit(solution)/shard_map/ppermute | solution.py:55
  57.4 3.1 %load.14.refs_10_ = bf16[1536,2304]{1,0:T(8,128)(2,1)S(1)} custom-call(bf16[6144,2304]{1,0:T(8,128)(2,1)} %refs_0_.19, bf16[8,6144]{1,0:T(8,128)(2,1)S(1)} %pad_maximum_fusion.refs_1_.refs_0_), custom_call_target="tpu_custom_call" | custom-call | tf_op jit(solution)/shard_map/load/pallas_call | solution.py:97
  60.5 1.3 %collective-permute-start.18 = (bf16[8,6144]{1,0:T(8,128)(2,1)S(1)}, bf16[8,6144]{1,0:T(8,128)(2,1)S(1)}, u32[]{:S(2)}, u32[]{:S(2)}) collective-permute-start(bf16[8,6144]{1,0:T(8,128)(2,1)S(1)} %collective-permute-done.16.refs_1_), channel_id=1, source_target_pairs={{0,4},{4,8},{8,12},{12,14},{14,10},{10,6},{6,2},{2,0},{1,5},{5,9},... | collective-permute-start | bytes 294920 | tf_op jit(solution)/shard_map/ppermute | solution.py:55
  61.9 0.8 collective-permute-start.19
  62.6 3.1 %load.15.refs_11_ = bf16[1536,2304]{1,0:T(8,128)(2,1)S(1)} custom-call(bf16[6144,2304]{1,0:T(8,128)(2,1)} %refs_0_.19, bf16[8,6144]{1,0:T(8,128)(2,1)S(1)} %collective-permute-done.16.refs_1_, bf16[8,6144]{1,0:T(8,128)(2,1)S(1)} %collective-permute-done.17.refs_2_), custom_call_target="tpu_custom_call" | custom-call | tf_op jit(solution)/shard_map/load/pallas_call | solution.py:97
  65.7 0.7 collective-permute-done.19.refs_2_.refs_4_
  66.5 1.0 %collective-permute-start.20 = (bf16[8,6144]{1,0:T(8,128)(2,1)S(1)}, bf16[8,6144]{1,0:T(8,128)(2,1)S(1)}, u32[]{:S(2)}, u32[]{:S(2)}) collective-permute-start(bf16[8,6144]{1,0:T(8,128)(2,1)S(1)} %collective-permute-done.18.refs_1_.refs_3_), channel_id=1, source_target_pairs={{0,4},{4,8},{8,12},{12,14},{14,10},{10,6},{6,2},{2,0},{1,5},{5,9},... | collective-permute-start | bytes 294920 | tf_op jit(solution)/shard_map/ppermute | solution.py:55
  67.5 1.0 %collective-permute-start.21 = (bf16[8,6144]{1,0:T(8,128)(2,1)S(1)}, bf16[8,6144]{1,0:T(8,128)(2,1)S(1)}, u32[]{:S(2)}, u32[]{:S(2)}) collective-permute-start(bf16[8,6144]{1,0:T(8,128)(2,1)S(1)} %collective-permute-done.19.refs_2_.refs_4_), channel_id=1, source_target_pairs={{0,2},{4,0},{8,4},{12,8},{14,12},{10,14},{6,10},{2,6},{1,3},{5,1},... | collective-permute-start | bytes 294920 | tf_op jit(solution)/shard_map/ppermute | solution.py:55
  68.5 3.1 %load.16.refs_12_ = bf16[1536,2304]{1,0:T(8,128)(2,1)S(1)} custom-call(bf16[6144,2304]{1,0:T(8,128)(2,1)} %refs_0_.19, bf16[8,6144]{1,0:T(8,128)(2,1)S(1)} %collective-permute-done.18.refs_1_.refs_3_, bf16[8,6144]{1,0:T(8,128)(2,1)S(1)} %collective-permute-done.19.refs_2_.refs_4_), custom_call_target="tpu_custom_call" | custom-call | tf_op jit(solution)/shard_map/load/pallas_call | solution.py:97
  71.6 0.5 collective-permute-done.21.refs_2_.refs_6_
  72.1 1.1 %collective-permute-start.22 = (bf16[8,3072]{1,0:T(8,128)(2,1)S(1)}, bf16[8,3072]{1,0:T(8,128)(2,1)S(1)}, u32[]{:S(2)}, u32[]{:S(2)}) collective-permute-start(bf16[8,3072]{1,0:T(8,128)(2,1)S(1)} %slice.18), channel_id=1, source_target_pairs={{0,4},{4,8},{8,12},{12,14},{14,10},{10,6},{6,2},{2,0},{1,5},{5,9},... | collective-permute-start | bytes 147464 | tf_op jit(solution)/shard_map/ppermute | solution.py:55
  73.2 0.9 %collective-permute-start.23 = (bf16[8,3072]{1,0:T(8,128)(2,1)S(1)}, bf16[8,3072]{1,0:T(8,128)(2,1)S(1)}, u32[]{:S(2)}, u32[]{:S(2)}) collective-permute-start(bf16[8,3072]{1,0:T(8,128)(2,1)S(1)} %slice.19), channel_id=1, source_target_pairs={{0,2},{4,0},{8,4},{12,8},{14,12},{10,14},{6,10},{2,6},{1,3},{5,1},... | collective-permute-start | bytes 147464 | tf_op jit(solution)/shard_map/ppermute | solution.py:55
  74.1 2.4 %load.17.refs_13_ = bf16[1024,2304]{1,0:T(8,128)(2,1)S(1)} custom-call(bf16[6144,2304]{1,0:T(8,128)(2,1)} %refs_0_.19, bf16[8,6144]{1,0:T(8,128)(2,1)S(1)} %collective-permute-done.20.refs_1_.refs_5_, bf16[8,6144]{1,0:T(8,128)(2,1)S(1)} %collective-permute-done.21.refs_2_.refs_6_), custom_call_target="tpu_custom_call" | custom-call | tf_op jit(solution)/shard_map/load/pallas_call | solution.py:97
  76.5 0.8 collective-permute-done.23.refs_8_
  77.3 5.0 %output_project.1 = (f32[4,8,2304]{2,1,0:T(8,128)S(1)}, f32[4,8,2304]{2,1,0:T(8,128)S(1)}) custom-call(bf16[8,6144]{1,0:T(8,128)(2,1)S(1)} %pad_maximum_fusion.refs_1_.refs_0_, bf16[8,6144]{1,0:T(8,128)(2,1)S(1)} %collective-permute-done.16.refs_1_, bf16[8,6144]{1,0:T(8,128)(2,1)S(1)} %collective-permute-done.17.refs_2_, ...), custom_call_target="tpu_custom_call" | custom-call | tf_op jit(solution)/shard_map/output_project/pallas_call | solution.py:395
  82.4 1.6 %collective-permute-done.24 = f32[4,8,2304]{2,1,0:T(8,128)S(1)} collective-permute-done((f32[4,8,2304]{2,1,0:T(8,128)S(1)}, f32[4,8,2304]{2,1,0:T(8,128)S(1)}, u32[]{:S(2)}, u32[]{:S(2)}) %collective-permute-start.24) | collective-permute-done | bytes 294944 | tf_op jit(solution)/shard_map/ppermute | solution.py:44
  84.0 0.7 fusion
  (39 shorter events, 0.9 us)
Async XLA Ops:
  0.0 10.6 %copy-start = (bf16[8,9216]{1,0:T(8,128)(2,1)S(1)}, bf16[8,9216]{1,0:T(8,128)(2,1)}, u32[]{:S(2)}) copy-start(bf16[8,9216]{1,0:T(8,128)(2,1)} %refs_3_.1) | copy-start | bytes 442372
  0.0 7.5 %collective-permute-start = (bf16[8,9216]{1,0:T(8,128)(2,1)}, bf16[8,9216]{1,0:T(8,128)(2,1)S(1)}, u32[]{:S(2)}, u32[]{:S(2)}) collective-permute-start(bf16[8,9216]{1,0:T(8,128)(2,1)} %refs_3_.1), channel_id=1, source_target_pairs={{0,4},{4,8},{8,12},{12,14},{14,10},{10,6},{6,2},{2,0},{1,5},{5,9},... | collective-permute-start | bytes 442376 | tf_op jit(solution)/shard_map/ppermute | solution.py:55
  3.0 5.5 %collective-permute-start.1 = (bf16[8,9216]{1,0:T(8,128)(2,1)}, bf16[8,9216]{1,0:T(8,128)(2,1)S(1)}, u32[]{:S(2)}, u32[]{:S(2)}) collective-permute-start(bf16[8,9216]{1,0:T(8,128)(2,1)} %refs_3_.1), channel_id=1, source_target_pairs={{0,2},{4,0},{8,4},{12,8},{14,12},{10,14},{6,10},{2,6},{1,3},{5,1},... | collective-permute-start | bytes 442376 | tf_op jit(solution)/shard_map/ppermute | solution.py:55
  8.5 6.1 %collective-permute-start.2 = (bf16[8,9216]{1,0:T(8,128)(2,1)S(1)}, bf16[8,9216]{1,0:T(8,128)(2,1)S(1)}, u32[]{:S(2)}, u32[]{:S(2)}) collective-permute-start(bf16[8,9216]{1,0:T(8,128)(2,1)S(1)} %collective-permute-done.refs_1_.refs_4_), channel_id=1, source_target_pairs={{0,4},{4,8},{8,12},{12,14},{14,10},{10,6},{6,2},{2,0},{1,5},{5,9},... | collective-permute-start | bytes 442376 | tf_op jit(solution)/shard_map/ppermute | solution.py:55
  10.1 5.1 %collective-permute-start.3 = (bf16[8,9216]{1,0:T(8,128)(2,1)S(1)}, bf16[8,9216]{1,0:T(8,128)(2,1)S(1)}, u32[]{:S(2)}, u32[]{:S(2)}) collective-permute-start(bf16[8,9216]{1,0:T(8,128)(2,1)S(1)} %collective-permute-done.1.refs_2_.refs_5_), channel_id=1, source_target_pairs={{0,2},{4,0},{8,4},{12,8},{14,12},{10,14},{6,10},{2,6},{1,3},{5,1},... | collective-permute-start | bytes 442376 | tf_op jit(solution)/shard_map/ppermute | solution.py:55
  15.3 7.3 %collective-permute-start.4 = (bf16[8,9216]{1,0:T(8,128)(2,1)S(1)}, bf16[8,9216]{1,0:T(8,128)(2,1)S(1)}, u32[]{:S(2)}, u32[]{:S(2)}) collective-permute-start(bf16[8,9216]{1,0:T(8,128)(2,1)S(1)} %collective-permute-done.2.refs_1_.refs_6_), channel_id=1, source_target_pairs={{0,4},{4,8},{8,12},{12,14},{14,10},{10,6},{6,2},{2,0},{1,5},{5,9},... | collective-permute-start | bytes 442376 | tf_op jit(solution)/shard_map/ppermute | solution.py:55
  16.8 5.8 %collective-permute-start.5 = (bf16[8,9216]{1,0:T(8,128)(2,1)S(1)}, bf16[8,9216]{1,0:T(8,128)(2,1)S(1)}, u32[]{:S(2)}, u32[]{:S(2)}) collective-permute-start(bf16[8,9216]{1,0:T(8,128)(2,1)S(1)} %collective-permute-done.3.refs_2_.refs_7_), channel_id=1, source_target_pairs={{0,2},{4,0},{8,4},{12,8},{14,12},{10,14},{6,10},{2,6},{1,3},{5,1},... | collective-permute-start | bytes 442376 | tf_op jit(solution)/shard_map/ppermute | solution.py:55
  17.5 7.5 %copy-start.2 = (bf16[9216]{0:T(1024)(128)(2,1)S(1)}, bf16[9216]{0:T(1024)(128)(2,1)}, u32[]{:S(2)}) copy-start(bf16[9216]{0:T(1024)(128)(2,1)} %param.9) | copy-start | bytes 55300
  17.5 7.4 %collective-permute-start.6 = (f32[8,128]{1,0:T(8,128)S(1)}, f32[8,128]{1,0:T(8,128)S(1)}, u32[]{:S(2)}, u32[]{:S(2)}) collective-permute-start(f32[8,128]{1,0:T(8,128)S(1)} %slice.20), channel_id=1, source_target_pairs={{0,14},{4,10},{8,6},{12,2},{14,0},{10,4},{6,8},{2,12},{1,15},{5,11... | collective-permute-start | bytes 12296 | tf_op jit(solution)/shard_map/ppermute | solution.py:520
  22.6 5.1 %collective-permute-start.8 = (bf16[8,4608]{1,0:T(8,128)(2,1)S(1)}, bf16[8,4608]{1,0:T(8,128)(2,1)S(1)}, u32[]{:S(2)}, u32[]{:S(2)}) collective-permute-start(bf16[8,4608]{1,0:T(8,128)(2,1)S(1)} %slice.15), channel_id=1, source_target_pairs={{0,4},{4,8},{8,12},{12,14},{14,10},{10,6},{6,2},{2,0},{1,5},{5,9},... | collective-permute-start | bytes 221192 | tf_op jit(solution)/shard_map/ppermute | solution.py:55
  23.6 4.4 %collective-permute-start.9 = (bf16[8,4608]{1,0:T(8,128)(2,1)S(1)}, bf16[8,4608]{1,0:T(8,128)(2,1)S(1)}, u32[]{:S(2)}, u32[]{:S(2)}) collective-permute-start(bf16[8,4608]{1,0:T(8,128)(2,1)S(1)} %slice.16), channel_id=1, source_target_pairs={{0,2},{4,0},{8,4},{12,8},{14,12},{10,14},{6,10},{2,6},{1,3},{5,1},... | collective-permute-start | bytes 221192 | tf_op jit(solution)/shard_map/ppermute | solution.py:55
  24.9 2.8 %collective-permute-start.7 = (f32[64,128]{1,0:T(8,128)S(1)}, f32[64,128]{1,0:T(8,128)S(1)}, u32[]{:S(2)}, u32[]{:S(2)}) collective-permute-start(f32[64,128]{1,0:T(8,128)S(1)} %pad_maximum_fusion.1.refs_0_), channel_id=1, source_target_pairs={{0,1},{1,0},{2,3},{3,2},{4,5},{5,4},{6,7},{7,6},{8,9},{9,8},{10,11... | collective-permute-start | bytes 98312 | tf_op jit(solution)/shard_map/ppermute | solution.py:44
  27.9 14.2 %copy-start.1 = (s32[4]{0:T(128)S(1)}, s32[4]{0:T(128)}, u32[]{:S(2)}) copy-start(s32[4]{0:T(128)} %lengths.1) | copy-start | bytes 52
  37.0 1.5 %collective-permute-start.10 = (f32[8,4,1664]{2,1,0:T(4,128)S(1)}, f32[8,4,1664]{2,1,0:T(4,128)S(1)}, u32[]{:S(2)}, u32[]{:S(2)}) collective-permute-start(f32[8,4,1664]{2,1,0:T(4,128)S(1)} %get-tuple-element.75), channel_id=1, source_target_pairs={{0,1},{1,0},{2,3},{3,2},{4,5},{5,4},{6,7},{7,6},{8,9},{9,8},{10,11... | collective-permute-start | bytes 638984 | tf_op jit(solution)/shard_map/ppermute | solution.py:44
  38.6 5.8 %collective-permute-start.11 = (bf16[2,4,1664]{2,1,0:T(4,128)(2,1)S(1)}, bf16[2,4,1664]{2,1,0:T(4,128)(2,1)S(1)}, u32[]{:S(2)}, u32[]{:S(2)}) collective-permute-start(bf16[2,4,1664]{2,1,0:T(4,128)(2,1)S(1)} %get-tuple-element.76.refs_0_), channel_id=1, source_target_pairs={{0,2},{2,0},{4,6},{6,4},{8,10},{10,8},{12,14},{14,12},{1,3},{3,1},... | collective-permute-start | bytes 79880 | tf_op jit(solution)/shard_map/ppermute | solution.py:540
  39.8 4.6 %collective-permute-start.12 = (bf16[2,4,1664]{2,1,0:T(4,128)(2,1)S(1)}, bf16[2,4,1664]{2,1,0:T(4,128)(2,1)S(1)}, u32[]{:S(2)}, u32[]{:S(2)}) collective-permute-start(bf16[2,4,1664]{2,1,0:T(4,128)(2,1)S(1)} %get-tuple-element.78), channel_id=1, source_target_pairs={{0,4},{2,6},{4,0},{6,2},{8,12},{10,14},{12,8},{14,10},{1,5},{3,7},... | collective-permute-start | bytes 79880 | tf_op jit(solution)/shard_map/ppermute | solution.py:540
  40.9 4.7 %collective-permute-start.13 = (bf16[2,4,1664]{2,1,0:T(4,128)(2,1)S(1)}, bf16[2,4,1664]{2,1,0:T(4,128)(2,1)S(1)}, u32[]{:S(2)}, u32[]{:S(2)}) collective-permute-start(bf16[2,4,1664]{2,1,0:T(4,128)(2,1)S(1)} %get-tuple-element.79), channel_id=1, source_target_pairs={{0,6},{2,4},{4,2},{6,0},{8,14},{10,12},{12,10},{14,8},{1,7},{3,5},... | collective-permute-start | bytes 79880 | tf_op jit(solution)/shard_map/ppermute | solution.py:540
  45.6 5.6 %collective-permute-start.14 = (bf16[4,4,1664]{2,1,0:T(4,128)(2,1)S(1)}, bf16[4,4,1664]{2,1,0:T(4,128)(2,1)S(1)}, u32[]{:S(2)}, u32[]{:S(2)}) collective-permute-start(bf16[4,4,1664]{2,1,0:T(4,128)(2,1)S(1)} %pack.1.refs_1_.refs_0_), channel_id=1, source_target_pairs={{0,8},{2,10},{4,12},{6,14},{8,0},{10,2},{12,4},{14,6},{1,9},{3,11}... | collective-permute-start | bytes 159752 | tf_op jit(solution)/shard_map/ppermute | solution.py:540
  54.0 1.3 %collective-permute-start.15 = (bf16[4,6144]{1,0:T(4,128)(2,1)S(1)}, bf16[4,6144]{1,0:T(4,128)(2,1)S(1)}, u32[]{:S(2)}, u32[]{:S(2)}) collective-permute-start(bf16[4,6144]{1,0:T(4,128)(2,1)S(1)} %get-tuple-element.89), channel_id=1, source_target_pairs={{0,1},{1,0},{2,3},{3,2},{4,5},{5,4},{6,7},{7,6},{8,9},{9,8},{10,11... | collective-permute-start | bytes 147464 | tf_op jit(solution)/shard_map/ppermute | solution.py:44
  55.3 5.2 %collective-permute-start.16 = (bf16[8,6144]{1,0:T(8,128)(2,1)S(1)}, bf16[8,6144]{1,0:T(8,128)(2,1)S(1)}, u32[]{:S(2)}, u32[]{:S(2)}) collective-permute-start(bf16[8,6144]{1,0:T(8,128)(2,1)S(1)} %pad_maximum_fusion.refs_1_.refs_0_), channel_id=1, source_target_pairs={{0,4},{4,8},{8,12},{12,14},{14,10},{10,6},{6,2},{2,0},{1,5},{5,9},... | collective-permute-start | bytes 294920 | tf_op jit(solution)/shard_map/ppermute | solution.py:55
  55.9 4.6 %collective-permute-start.17 = (bf16[8,6144]{1,0:T(8,128)(2,1)S(1)}, bf16[8,6144]{1,0:T(8,128)(2,1)S(1)}, u32[]{:S(2)}, u32[]{:S(2)}) collective-permute-start(bf16[8,6144]{1,0:T(8,128)(2,1)S(1)} %pad_maximum_fusion.refs_1_.refs_0_), channel_id=1, source_target_pairs={{0,2},{4,0},{8,4},{12,8},{14,12},{10,14},{6,10},{2,6},{1,3},{5,1},... | collective-permute-start | bytes 294920 | tf_op jit(solution)/shard_map/ppermute | solution.py:55
  60.5 5.2 %collective-permute-start.18 = (bf16[8,6144]{1,0:T(8,128)(2,1)S(1)}, bf16[8,6144]{1,0:T(8,128)(2,1)S(1)}, u32[]{:S(2)}, u32[]{:S(2)}) collective-permute-start(bf16[8,6144]{1,0:T(8,128)(2,1)S(1)} %collective-permute-done.16.refs_1_), channel_id=1, source_target_pairs={{0,4},{4,8},{8,12},{12,14},{14,10},{10,6},{6,2},{2,0},{1,5},{5,9},... | collective-permute-start | bytes 294920 | tf_op jit(solution)/shard_map/ppermute | solution.py:55
  61.9 4.6 %collective-permute-start.19 = (bf16[8,6144]{1,0:T(8,128)(2,1)S(1)}, bf16[8,6144]{1,0:T(8,128)(2,1)S(1)}, u32[]{:S(2)}, u32[]{:S(2)}) collective-permute-start(bf16[8,6144]{1,0:T(8,128)(2,1)S(1)} %collective-permute-done.17.refs_2_), channel_id=1, source_target_pairs={{0,2},{4,0},{8,4},{12,8},{14,12},{10,14},{6,10},{2,6},{1,3},{5,1},... | collective-permute-start | bytes 294920 | tf_op jit(solution)/shard_map/ppermute | solution.py:55
  66.5 5.1 %collective-permute-start.20 = (bf16[8,6144]{1,0:T(8,128)(2,1)S(1)}, bf16[8,6144]{1,0:T(8,128)(2,1)S(1)}, u32[]{:S(2)}, u32[]{:S(2)}) collective-permute-start(bf16[8,6144]{1,0:T(8,128)(2,1)S(1)} %collective-permute-done.18.refs_1_.refs_3_), channel_id=1, source_target_pairs={{0,4},{4,8},{8,12},{12,14},{14,10},{10,6},{6,2},{2,0},{1,5},{5,9},... | collective-permute-start | bytes 294920 | tf_op jit(solution)/shard_map/ppermute | solution.py:55
  67.5 4.6 %collective-permute-start.21 = (bf16[8,6144]{1,0:T(8,128)(2,1)S(1)}, bf16[8,6144]{1,0:T(8,128)(2,1)S(1)}, u32[]{:S(2)}, u32[]{:S(2)}) collective-permute-start(bf16[8,6144]{1,0:T(8,128)(2,1)S(1)} %collective-permute-done.19.refs_2_.refs_4_), channel_id=1, source_target_pairs={{0,2},{4,0},{8,4},{12,8},{14,12},{10,14},{6,10},{2,6},{1,3},{5,1},... | collective-permute-start | bytes 294920 | tf_op jit(solution)/shard_map/ppermute | solution.py:55
  72.1 4.4 %collective-permute-start.22 = (bf16[8,3072]{1,0:T(8,128)(2,1)S(1)}, bf16[8,3072]{1,0:T(8,128)(2,1)S(1)}, u32[]{:S(2)}, u32[]{:S(2)}) collective-permute-start(bf16[8,3072]{1,0:T(8,128)(2,1)S(1)} %slice.18), channel_id=1, source_target_pairs={{0,4},{4,8},{8,12},{12,14},{14,10},{10,6},{6,2},{2,0},{1,5},{5,9},... | collective-permute-start | bytes 147464 | tf_op jit(solution)/shard_map/ppermute | solution.py:55
  73.2 4.1 %collective-permute-start.23 = (bf16[8,3072]{1,0:T(8,128)(2,1)S(1)}, bf16[8,3072]{1,0:T(8,128)(2,1)S(1)}, u32[]{:S(2)}, u32[]{:S(2)}) collective-permute-start(bf16[8,3072]{1,0:T(8,128)(2,1)S(1)} %slice.19), channel_id=1, source_target_pairs={{0,2},{4,0},{8,4},{12,8},{14,12},{10,14},{6,10},{2,6},{1,3},{5,1},... | collective-permute-start | bytes 147464 | tf_op jit(solution)/shard_map/ppermute | solution.py:55
  82.3 1.6 %collective-permute-start.24 = (f32[4,8,2304]{2,1,0:T(8,128)S(1)}, f32[4,8,2304]{2,1,0:T(8,128)S(1)}, u32[]{:S(2)}, u32[]{:S(2)}) collective-permute-start(f32[4,8,2304]{2,1,0:T(8,128)S(1)} %get-tuple-element.104), channel_id=1, source_target_pairs={{0,1},{1,0},{2,3},{3,2},{4,5},{5,4},{6,7},{7,6},{8,9},{9,8},{10,11... | collective-permute-start | bytes 884744 | tf_op jit(solution)/shard_map/ppermute | solution.py:44

commit v19 on v17

--- a/solution.py
+++ b/solution.py
@@ -188,18 +188,13 @@
             at = slice(i * rows, (i + 2) * rows)
             x = (x - row_mean[at]) * scale[at] * gain[:, cols]
             normed[at, cols] = x.astype(jnp.bfloat16)
-        x = normed[:, cols]
-        start = 0
-        for weight in weights:
-            term = lax.dot_general(
-                x, weight[:, cols], contract, preferred_element_type=jnp.float32
-            )
-            stripe = slice(start, start + weight.shape[0])
-            if part == 0:
-                total[:, stripe] = term
-            else:
-                total[:, stripe] += term
-            start = stripe.stop
+    start = 0
+    for weight in weights:
+        stripe = slice(start, start + weight.shape[0])
+        total[:, stripe] = lax.dot_general(
+            normed[...], weight[...], contract, preferred_element_type=jnp.float32
+        )
+        start = stripe.stop
     last = slice(total.shape[1] - 128, total.shape[1])
     lane = lax.broadcasted_iota(jnp.int32, (total.shape[0], 128), 1)
     new = jnp.where(lane < 64, total[:, last], 0.0)

time: 84.6 us -> 84.9 us (level)
  no operation moved by 1% of the time
where the time goes in v19:
time: 84.9 us; the launch traced here: 84.8 us
  Pallas kernels  48 us (57%)
  starting transfers between devices  24.8 us (29%)
  waiting for transfers between devices  10.8 us (13%)
  other arithmetic  0.89 us (1%)
    pallas_call x9, Pallas kernels, load(): pl.pallas_call(lambda *refs: load_kernel([job[1:] for job in jobs], *refs...  26 us
    ppermute x8, starting transfers between devices, step(): lax.ppermute(left, 'gx', self.onward)  10.2 us
    pallas_call x1, Pallas kernels, project(): pl.pallas_call(lambda *refs: project_kernel(n, len(weights), *refs), out_...  9.16 us
    ppermute x8, starting transfers between devices, step(): lax.ppermute(right, 'gx', self.back)  7.2 us
    pallas_call x1, Pallas kernels, output_project(): pl.pallas_call(lambda *refs: output_kernel(n, *refs), out_shape=[shape, s...  5.05 us
    pallas_call x2, Pallas kernels, load_cache(): pl.pallas_call(load_cache_kernel, out_shape=pltpu.VMEM(cache.shape, cache...  4.42 us
    ppermute x4, waiting for transfers between devices, swap_pair(): return lax.ppermute(x, 'gy', [(0, 1), (1, 0)])  3.88 us
    ppermute x4, starting transfers between devices, exchange(): return lax.ppermute(blocks, 'gx', [(i, i ^ d) for i in range(n)])  3.81 us
  transfers between devices with their start and end apart: 25, of which 11 were waited for; matrix products, arithmetic and copies ran while one was open for 0% of the time, Pallas kernels for 37%

profile of v19, /device:TPU:0, one launch (start us, length us, event | category | flops | bytes accessed | tf_op | source)
XLA Modules:
  0.0 84.8 jit_solution(14004474539511689452)
XLA Ops:
  0.0 3.0 %collective-permute-start = (bf16[8,9216]{1,0:T(8,128)(2,1)}, bf16[8,9216]{1,0:T(8,128)(2,1)S(1)}, u32[]{:S(2)}, u32[]{:S(2)}) collective-permute-start(bf16[8,9216]{1,0:T(8,128)(2,1)} %refs_3_.1), channel_id=1, source_target_pairs={{0,4},{4,8},{8,12},{12,14},{14,10},{10,6},{6,2},{2,0},{1,5},{5,9},... | collective-permute-start | bytes 442376 | tf_op jit(solution)/shard_map/ppermute | solution.py:55
  3.0 3.8 %load.9.refs_12_ = bf16[512,9216]{1,0:T(8,128)(2,1)S(1)} custom-call(bf16[1536,9216]{1,0:T(8,128)(2,1)} %refs_0_.14), custom_call_target="tpu_custom_call" | custom-call | tf_op jit(solution)/shard_map/load/pallas_call | solution.py:97
  6.8 0.3 collective-permute-done.refs_1_.refs_4_
  7.1 1.4 %collective-permute-done.1.refs_2_.refs_5_ = bf16[8,9216]{1,0:T(8,128)(2,1)S(1)} collective-permute-done((bf16[8,9216]{1,0:T(8,128)(2,1)}, bf16[8,9216]{1,0:T(8,128)(2,1)S(1)}, u32[]{:S(2)}, u32[]{:S(2)}) %collective-permute-start.1) | collective-permute-done | bytes 147488 | tf_op jit(solution)/shard_map/ppermute | solution.py:55
  8.5 1.6 %collective-permute-start.2 = (bf16[8,9216]{1,0:T(8,128)(2,1)S(1)}, bf16[8,9216]{1,0:T(8,128)(2,1)S(1)}, u32[]{:S(2)}, u32[]{:S(2)}) collective-permute-start(bf16[8,9216]{1,0:T(8,128)(2,1)S(1)} %collective-permute-done.refs_1_.refs_4_), channel_id=1, source_target_pairs={{0,4},{4,8},{8,12},{12,14},{14,10},{10,6},{6,2},{2,0},{1,5},{5,9},... | collective-permute-start | bytes 442376 | tf_op jit(solution)/shard_map/ppermute | solution.py:55
  10.1 0.4 collective-permute-start.3
  10.6 0.2 row_sums.3.refs_0_
  10.8 3.8 %load.10.refs_13_ = bf16[512,9216]{1,0:T(8,128)(2,1)S(1)} custom-call(bf16[1536,9216]{1,0:T(8,128)(2,1)} %refs_0_.14, bf16[8,9216]{1,0:T(8,128)(2,1)S(1)} %collective-permute-done.refs_1_.refs_4_, bf16[8,9216]{1,0:T(8,128)(2,1)S(1)} %collective-permute-done.1.refs_2_.refs_5_), custom_call_target="tpu_custom_call" | custom-call | tf_op jit(solution)/shard_map/load/pallas_call | solution.py:97
  14.6 0.6 collective-permute-done.3.refs_2_.refs_7_
  15.3 1.6 %collective-permute-start.4 = (bf16[8,9216]{1,0:T(8,128)(2,1)S(1)}, bf16[8,9216]{1,0:T(8,128)(2,1)S(1)}, u32[]{:S(2)}, u32[]{:S(2)}) collective-permute-start(bf16[8,9216]{1,0:T(8,128)(2,1)S(1)} %collective-permute-done.2.refs_1_.refs_6_), channel_id=1, source_target_pairs={{0,4},{4,8},{8,12},{12,14},{14,10},{10,6},{6,2},{2,0},{1,5},{5,9},... | collective-permute-start | bytes 442376 | tf_op jit(solution)/shard_map/ppermute | solution.py:55
  16.8 0.4 collective-permute-start.5
  17.5 2.9 %collective-permute-start.6 = (f32[8,128]{1,0:T(8,128)S(1)}, f32[8,128]{1,0:T(8,128)S(1)}, u32[]{:S(2)}, u32[]{:S(2)}) collective-permute-start(f32[8,128]{1,0:T(8,128)S(1)} %slice.20), channel_id=1, source_target_pairs={{0,14},{4,10},{8,6},{12,2},{14,0},{10,4},{6,8},{2,12},{1,15},{5,11... | collective-permute-start | bytes 12296 | tf_op jit(solution)/shard_map/ppermute | solution.py:516
  20.3 2.4 %load.11.refs_14_ = bf16[256,9216]{1,0:T(8,128)(2,1)S(1)} custom-call(bf16[1536,9216]{1,0:T(8,128)(2,1)} %refs_0_.14, bf16[8,9216]{1,0:T(8,128)(2,1)S(1)} %collective-permute-done.2.refs_1_.refs_6_, bf16[8,9216]{1,0:T(8,128)(2,1)S(1)} %collective-permute-done.3.refs_2_.refs_7_), custom_call_target="tpu_custom_call" | custom-call | tf_op jit(solution)/shard_map/load/pallas_call | solution.py:97
  22.8 0.8 collective-permute-start.8
  23.6 1.3 %collective-permute-start.9 = (bf16[8,4608]{1,0:T(8,128)(2,1)S(1)}, bf16[8,4608]{1,0:T(8,128)(2,1)S(1)}, u32[]{:S(2)}, u32[]{:S(2)}) collective-permute-start(bf16[8,4608]{1,0:T(8,128)(2,1)S(1)} %slice.16), channel_id=1, source_target_pairs={{0,2},{4,0},{8,4},{12,8},{14,12},{10,14},{6,10},{2,6},{1,3},{5,1},... | collective-permute-start | bytes 221192 | tf_op jit(solution)/shard_map/ppermute | solution.py:55
  25.1 2.7 %load.12.refs_15_ = bf16[320,9216]{1,0:T(8,128)(2,1)S(1)} custom-call(bf16[1536,9216]{1,0:T(8,128)(2,1)} %refs_0_.14, bf16[64,9216]{1,0:T(8,128)(2,1)} %refs_1_.1, f32[56,128]{1,0:T(8,128)S(1)} %row_sums.5.refs_2_), custom_call_target="tpu_custom_call" | custom-call | tf_op jit(solution)/shard_map/load/pallas_call | solution.py:97
  27.9 9.2 %project.1 = (f32[8,4,1664]{2,1,0:T(4,128)S(1)}, f32[8,4,1664]{2,1,0:T(4,128)S(1)}) custom-call(f32[64,128]{1,0:T(8,128)S(1)} %pad_maximum_fusion.1.refs_0_, f32[64,128]{1,0:T(8,128)S(1)} %collective-permute-done.7.refs_1_, f32[1,9216]{1,0:T(1,128)S(1)} %bitcast.3, bf16[8,9216]{1,0:T(8,128)(2,1)S(1)} %copy-done, ...), custom_call_target="tpu_custom_call" | custom-call | tf_op jit(solution)/shard_map/project/pallas_call | solution.py:217
  37.1 0.5 collective-permute-start.10
  37.6 1.1 %collective-permute-done.10.got = f32[8,4,1664]{2,1,0:T(4,128)S(1)} collective-permute-done((f32[8,4,1664]{2,1,0:T(4,128)S(1)}, f32[8,4,1664]{2,1,0:T(4,128)S(1)}, u32[]{:S(2)}, u32[]{:S(2)}) %collective-permute-start.10) | collective-permute-done | bytes 213024 | tf_op jit(solution)/shard_map/ppermute | solution.py:44
  38.7 1.7 %collective-permute-start.11 = (bf16[2,4,1664]{2,1,0:T(4,128)(2,1)S(1)}, bf16[2,4,1664]{2,1,0:T(4,128)(2,1)S(1)}, u32[]{:S(2)}, u32[]{:S(2)}) collective-permute-start(bf16[2,4,1664]{2,1,0:T(4,128)(2,1)S(1)} %get-tuple-element.76.refs_0_), channel_id=1, source_target_pairs={{0,2},{2,0},{4,6},{6,4},{8,10},{10,8},{12,14},{14,12},{1,3},{3,1},... | collective-permute-start | bytes 79880 | tf_op jit(solution)/shard_map/ppermute | solution.py:536
  40.4 1.2 %collective-permute-start.12 = (bf16[2,4,1664]{2,1,0:T(4,128)(2,1)S(1)}, bf16[2,4,1664]{2,1,0:T(4,128)(2,1)S(1)}, u32[]{:S(2)}, u32[]{:S(2)}) collective-permute-start(bf16[2,4,1664]{2,1,0:T(4,128)(2,1)S(1)} %get-tuple-element.78), channel_id=1, source_target_pairs={{0,4},{2,6},{4,0},{6,2},{8,12},{10,14},{12,8},{14,10},{1,5},{3,7},... | collective-permute-start | bytes 79880 | tf_op jit(solution)/shard_map/ppermute | solution.py:536
  41.6 0.7 collective-permute-start.13
  42.3 2.2 %load_cache.2.refs_7_ = bf16[4,2048,256]{2,1,0:T(8,128)(2,1)S(1)} custom-call(bf16[4,2048,256]{2,1,0:T(8,128)(2,1)} %source.2, bf16[2,4,1664]{2,1,0:T(4,128)(2,1)S(1)} %get-tuple-element.76.refs_0_), custom_call_target="tpu_custom_call" | custom-call | tf_op jit(solution)/shard_map/load_cache/pallas_call | solution.py:119
  44.6 1.8 %collective-permute-done.13.refs_3_ = bf16[2,4,1664]{2,1,0:T(4,128)(2,1)S(1)} collective-permute-done((bf16[2,4,1664]{2,1,0:T(4,128)(2,1)S(1)}, bf16[2,4,1664]{2,1,0:T(4,128)(2,1)S(1)}, u32[]{:S(2)}, u32[]{:S(2)}) %collective-permute-start.13) | collective-permute-done | bytes 26656 | tf_op jit(solution)/shard_map/ppermute | solution.py:536
  46.3 0.2 collective-permute-start.14
  46.7 2.2 %load_cache.3.refs_8_ = bf16[4,2048,256]{2,1,0:T(8,128)(2,1)S(1)} custom-call(bf16[4,2048,256]{2,1,0:T(8,128)(2,1)} %source.3, bf16[4,4,1664]{2,1,0:T(4,128)(2,1)S(1)} %pack.1.refs_1_.refs_0_), custom_call_target="tpu_custom_call" | custom-call | tf_op jit(solution)/shard_map/load_cache/pallas_call | solution.py:119
  48.9 1.6 %load.13.refs_9_ = bf16[512,2304]{1,0:T(8,128)(2,1)S(1)} custom-call(bf16[6144,2304]{1,0:T(8,128)(2,1)} %refs_0_.19, bf16[4,4,1664]{2,1,0:T(4,128)(2,1)S(1)} %pack.1.refs_1_.refs_0_), custom_call_target="tpu_custom_call" | custom-call | tf_op jit(solution)/shard_map/load/pallas_call | solution.py:97
  50.6 1.4 %collective-permute-done.14.refs_4_ = bf16[4,4,1664]{2,1,0:T(4,128)(2,1)S(1)} collective-permute-done((bf16[4,4,1664]{2,1,0:T(4,128)(2,1)S(1)}, bf16[4,4,1664]{2,1,0:T(4,128)(2,1)S(1)}, u32[]{:S(2)}, u32[]{:S(2)}) %collective-permute-start.14) | collective-permute-done | bytes 53280 | tf_op jit(solution)/shard_map/ppermute | solution.py:536
  52.0 2.7 %attend.1 = (bf16[4,6144]{1,0:T(4,128)(2,1)S(1)}, bf16[4,6144]{1,0:T(4,128)(2,1)S(1)}) custom-call(s32[4]{0:T(128)S(1)} %copy-done.1, bf16[2,4,1664]{2,1,0:T(4,128)(2,1)S(1)} %get-tuple-element.80.refs_0_, bf16[2,4,1664]{2,1,0:T(4,128)(2,1)S(1)} %collective-permute-done.11.refs_1_, bf16[2,4,1664]{2,1,0:T(4,128)(2,1)S(1)} %collective-permute-done.12.refs_2_, ...), custom_call_target="tpu_custom_call" | custom-call | tf_op jit(solution)/shard_map/attend/pallas_call | solution.py:337
  54.8 1.2 %collective-permute-done.15 = bf16[4,6144]{1,0:T(4,128)(2,1)S(1)} collective-permute-done((bf16[4,6144]{1,0:T(4,128)(2,1)S(1)}, bf16[4,6144]{1,0:T(4,128)(2,1)S(1)}, u32[]{:S(2)}, u32[]{:S(2)}) %collective-permute-start.15) | collective-permute-done | bytes 49184 | tf_op jit(solution)/shard_map/ppermute | solution.py:44
  56.1 0.4 collective-permute-start.16
  56.5 1.7 %collective-permute-start.17 = (bf16[8,6144]{1,0:T(8,128)(2,1)S(1)}, bf16[8,6144]{1,0:T(8,128)(2,1)S(1)}, u32[]{:S(2)}, u32[]{:S(2)}) collective-permute-start(bf16[8,6144]{1,0:T(8,128)(2,1)S(1)} %pad_maximum_fusion.refs_1_.refs_0_), channel_id=1, source_target_pairs={{0,2},{4,0},{8,4},{12,8},{14,12},{10,14},{6,10},{2,6},{1,3},{5,1},... | collective-permute-start | bytes 294920 | tf_op jit(solution)/shard_map/ppermute | solution.py:55
  58.1 3.1 %load.14.refs_10_ = bf16[1536,2304]{1,0:T(8,128)(2,1)S(1)} custom-call(bf16[6144,2304]{1,0:T(8,128)(2,1)} %refs_0_.19, bf16[8,6144]{1,0:T(8,128)(2,1)S(1)} %pad_maximum_fusion.refs_1_.refs_0_), custom_call_target="tpu_custom_call" | custom-call | tf_op jit(solution)/shard_map/load/pallas_call | solution.py:97
  61.3 1.3 %collective-permute-start.18 = (bf16[8,6144]{1,0:T(8,128)(2,1)S(1)}, bf16[8,6144]{1,0:T(8,128)(2,1)S(1)}, u32[]{:S(2)}, u32[]{:S(2)}) collective-permute-start(bf16[8,6144]{1,0:T(8,128)(2,1)S(1)} %collective-permute-done.16.refs_1_), channel_id=1, source_target_pairs={{0,4},{4,8},{8,12},{12,14},{14,10},{10,6},{6,2},{2,0},{1,5},{5,9},... | collective-permute-start | bytes 294920 | tf_op jit(solution)/shard_map/ppermute | solution.py:55
  62.6 0.7 collective-permute-start.19
  63.4 3.1 %load.15.refs_11_ = bf16[1536,2304]{1,0:T(8,128)(2,1)S(1)} custom-call(bf16[6144,2304]{1,0:T(8,128)(2,1)} %refs_0_.19, bf16[8,6144]{1,0:T(8,128)(2,1)S(1)} %collective-permute-done.16.refs_1_, bf16[8,6144]{1,0:T(8,128)(2,1)S(1)} %collective-permute-done.17.refs_2_), custom_call_target="tpu_custom_call" | custom-call | tf_op jit(solution)/shard_map/load/pallas_call | solution.py:97
  66.5 0.7 collective-permute-done.19.refs_2_.refs_4_
  67.2 0.8 collective-permute-start.20
  68.1 1.2 %collective-permute-start.21 = (bf16[8,6144]{1,0:T(8,128)(2,1)S(1)}, bf16[8,6144]{1,0:T(8,128)(2,1)S(1)}, u32[]{:S(2)}, u32[]{:S(2)}) collective-permute-start(bf16[8,6144]{1,0:T(8,128)(2,1)S(1)} %collective-permute-done.19.refs_2_.refs_4_), channel_id=1, source_target_pairs={{0,2},{4,0},{8,4},{12,8},{14,12},{10,14},{6,10},{2,6},{1,3},{5,1},... | collective-permute-start | bytes 294920 | tf_op jit(solution)/shard_map/ppermute | solution.py:55
  69.2 3.1 %load.16.refs_12_ = bf16[1536,2304]{1,0:T(8,128)(2,1)S(1)} custom-call(bf16[6144,2304]{1,0:T(8,128)(2,1)} %refs_0_.19, bf16[8,6144]{1,0:T(8,128)(2,1)S(1)} %collective-permute-done.18.refs_1_.refs_3_, bf16[8,6144]{1,0:T(8,128)(2,1)S(1)} %collective-permute-done.19.refs_2_.refs_4_), custom_call_target="tpu_custom_call" | custom-call | tf_op jit(solution)/shard_map/load/pallas_call | solution.py:97
  72.4 0.3 collective-permute-done.21.refs_2_.refs_6_
  72.7 0.6 collective-permute-start.22
  73.3 1.4 %collective-permute-start.23 = (bf16[8,3072]{1,0:T(8,128)(2,1)S(1)}, bf16[8,3072]{1,0:T(8,128)(2,1)S(1)}, u32[]{:S(2)}, u32[]{:S(2)}) collective-permute-start(bf16[8,3072]{1,0:T(8,128)(2,1)S(1)} %slice.19), channel_id=1, source_target_pairs={{0,2},{4,0},{8,4},{12,8},{14,12},{10,14},{6,10},{2,6},{1,3},{5,1},... | collective-permute-start | bytes 147464 | tf_op jit(solution)/shard_map/ppermute | solution.py:55
  74.7 2.4 %load.17.refs_13_ = bf16[1024,2304]{1,0:T(8,128)(2,1)S(1)} custom-call(bf16[6144,2304]{1,0:T(8,128)(2,1)} %refs_0_.19, bf16[8,6144]{1,0:T(8,128)(2,1)S(1)} %collective-permute-done.20.refs_1_.refs_5_, bf16[8,6144]{1,0:T(8,128)(2,1)S(1)} %collective-permute-done.21.refs_2_.refs_6_), custom_call_target="tpu_custom_call" | custom-call | tf_op jit(solution)/shard_map/load/pallas_call | solution.py:97
  77.1 0.3 collective-permute-done.23.refs_8_
  77.4 5.0 %output_project.1 = (f32[4,8,2304]{2,1,0:T(8,128)S(1)}, f32[4,8,2304]{2,1,0:T(8,128)S(1)}) custom-call(bf16[8,6144]{1,0:T(8,128)(2,1)S(1)} %pad_maximum_fusion.refs_1_.refs_0_, bf16[8,6144]{1,0:T(8,128)(2,1)S(1)} %collective-permute-done.16.refs_1_, bf16[8,6144]{1,0:T(8,128)(2,1)S(1)} %collective-permute-done.17.refs_2_, ...), custom_call_target="tpu_custom_call" | custom-call | tf_op jit(solution)/shard_map/output_project/pallas_call | solution.py:392
  82.5 1.6 %collective-permute-done.24 = f32[4,8,2304]{2,1,0:T(8,128)S(1)} collective-permute-done((f32[4,8,2304]{2,1,0:T(8,128)S(1)}, f32[4,8,2304]{2,1,0:T(8,128)S(1)}, u32[]{:S(2)}, u32[]{:S(2)}) %collective-permute-start.24) | collective-permute-done | bytes 294944 | tf_op jit(solution)/shard_map/ppermute | solution.py:44
  84.1 0.7 fusion
  (39 shorter events, 0.9 us)
Async XLA Ops:
  0.0 10.6 %copy-start = (bf16[8,9216]{1,0:T(8,128)(2,1)S(1)}, bf16[8,9216]{1,0:T(8,128)(2,1)}, u32[]{:S(2)}) copy-start(bf16[8,9216]{1,0:T(8,128)(2,1)} %refs_3_.1) | copy-start | bytes 442372
  0.0 7.1 %collective-permute-start = (bf16[8,9216]{1,0:T(8,128)(2,1)}, bf16[8,9216]{1,0:T(8,128)(2,1)S(1)}, u32[]{:S(2)}, u32[]{:S(2)}) collective-permute-start(bf16[8,9216]{1,0:T(8,128)(2,1)} %refs_3_.1), channel_id=1, source_target_pairs={{0,4},{4,8},{8,12},{12,14},{14,10},{10,6},{6,2},{2,0},{1,5},{5,9},... | collective-permute-start | bytes 442376 | tf_op jit(solution)/shard_map/ppermute | solution.py:55
  3.0 5.5 %collective-permute-start.1 = (bf16[8,9216]{1,0:T(8,128)(2,1)}, bf16[8,9216]{1,0:T(8,128)(2,1)S(1)}, u32[]{:S(2)}, u32[]{:S(2)}) collective-permute-start(bf16[8,9216]{1,0:T(8,128)(2,1)} %refs_3_.1), channel_id=1, source_target_pairs={{0,2},{4,0},{8,4},{12,8},{14,12},{10,14},{6,10},{2,6},{1,3},{5,1},... | collective-permute-start | bytes 442376 | tf_op jit(solution)/shard_map/ppermute | solution.py:55
  8.5 6.1 %collective-permute-start.2 = (bf16[8,9216]{1,0:T(8,128)(2,1)S(1)}, bf16[8,9216]{1,0:T(8,128)(2,1)S(1)}, u32[]{:S(2)}, u32[]{:S(2)}) collective-permute-start(bf16[8,9216]{1,0:T(8,128)(2,1)S(1)} %collective-permute-done.refs_1_.refs_4_), channel_id=1, source_target_pairs={{0,4},{4,8},{8,12},{12,14},{14,10},{10,6},{6,2},{2,0},{1,5},{5,9},... | collective-permute-start | bytes 442376 | tf_op jit(solution)/shard_map/ppermute | solution.py:55
  10.1 5.1 %collective-permute-start.3 = (bf16[8,9216]{1,0:T(8,128)(2,1)S(1)}, bf16[8,9216]{1,0:T(8,128)(2,1)S(1)}, u32[]{:S(2)}, u32[]{:S(2)}) collective-permute-start(bf16[8,9216]{1,0:T(8,128)(2,1)S(1)} %collective-permute-done.1.refs_2_.refs_5_), channel_id=1, source_target_pairs={{0,2},{4,0},{8,4},{12,8},{14,12},{10,14},{6,10},{2,6},{1,3},{5,1},... | collective-permute-start | bytes 442376 | tf_op jit(solution)/shard_map/ppermute | solution.py:55
  15.3 7.5 %collective-permute-start.4 = (bf16[8,9216]{1,0:T(8,128)(2,1)S(1)}, bf16[8,9216]{1,0:T(8,128)(2,1)S(1)}, u32[]{:S(2)}, u32[]{:S(2)}) collective-permute-start(bf16[8,9216]{1,0:T(8,128)(2,1)S(1)} %collective-permute-done.2.refs_1_.refs_6_), channel_id=1, source_target_pairs={{0,4},{4,8},{8,12},{12,14},{14,10},{10,6},{6,2},{2,0},{1,5},{5,9},... | collective-permute-start | bytes 442376 | tf_op jit(solution)/shard_map/ppermute | solution.py:55
  16.8 5.9 %collective-permute-start.5 = (bf16[8,9216]{1,0:T(8,128)(2,1)S(1)}, bf16[8,9216]{1,0:T(8,128)(2,1)S(1)}, u32[]{:S(2)}, u32[]{:S(2)}) collective-permute-start(bf16[8,9216]{1,0:T(8,128)(2,1)S(1)} %collective-permute-done.3.refs_2_.refs_7_), channel_id=1, source_target_pairs={{0,2},{4,0},{8,4},{12,8},{14,12},{10,14},{6,10},{2,6},{1,3},{5,1},... | collective-permute-start | bytes 442376 | tf_op jit(solution)/shard_map/ppermute | solution.py:55
  17.5 7.6 %copy-start.2 = (bf16[9216]{0:T(1024)(128)(2,1)S(1)}, bf16[9216]{0:T(1024)(128)(2,1)}, u32[]{:S(2)}) copy-start(bf16[9216]{0:T(1024)(128)(2,1)} %param.9) | copy-start | bytes 55300
  17.5 7.6 %collective-permute-start.6 = (f32[8,128]{1,0:T(8,128)S(1)}, f32[8,128]{1,0:T(8,128)S(1)}, u32[]{:S(2)}, u32[]{:S(2)}) collective-permute-start(f32[8,128]{1,0:T(8,128)S(1)} %slice.20), channel_id=1, source_target_pairs={{0,14},{4,10},{8,6},{12,2},{14,0},{10,4},{6,8},{2,12},{1,15},{5,11... | collective-permute-start | bytes 12296 | tf_op jit(solution)/shard_map/ppermute | solution.py:516
  22.8 5.1 %collective-permute-start.8 = (bf16[8,4608]{1,0:T(8,128)(2,1)S(1)}, bf16[8,4608]{1,0:T(8,128)(2,1)S(1)}, u32[]{:S(2)}, u32[]{:S(2)}) collective-permute-start(bf16[8,4608]{1,0:T(8,128)(2,1)S(1)} %slice.15), channel_id=1, source_target_pairs={{0,4},{4,8},{8,12},{12,14},{14,10},{10,6},{6,2},{2,0},{1,5},{5,9},... | collective-permute-start | bytes 221192 | tf_op jit(solution)/shard_map/ppermute | solution.py:55
  23.6 4.4 %collective-permute-start.9 = (bf16[8,4608]{1,0:T(8,128)(2,1)S(1)}, bf16[8,4608]{1,0:T(8,128)(2,1)S(1)}, u32[]{:S(2)}, u32[]{:S(2)}) collective-permute-start(bf16[8,4608]{1,0:T(8,128)(2,1)S(1)} %slice.16), channel_id=1, source_target_pairs={{0,2},{4,0},{8,4},{12,8},{14,12},{10,14},{6,10},{2,6},{1,3},{5,1},... | collective-permute-start | bytes 221192 | tf_op jit(solution)/shard_map/ppermute | solution.py:55
  25.0 2.8 %collective-permute-start.7 = (f32[64,128]{1,0:T(8,128)S(1)}, f32[64,128]{1,0:T(8,128)S(1)}, u32[]{:S(2)}, u32[]{:S(2)}) collective-permute-start(f32[64,128]{1,0:T(8,128)S(1)} %pad_maximum_fusion.1.refs_0_), channel_id=1, source_target_pairs={{0,1},{1,0},{2,3},{3,2},{4,5},{5,4},{6,7},{7,6},{8,9},{9,8},{10,11... | collective-permute-start | bytes 98312 | tf_op jit(solution)/shard_map/ppermute | solution.py:44
  27.9 14.4 %copy-start.1 = (s32[4]{0:T(128)S(1)}, s32[4]{0:T(128)}, u32[]{:S(2)}) copy-start(s32[4]{0:T(128)} %lengths.1) | copy-start | bytes 52
  37.1 1.6 %collective-permute-start.10 = (f32[8,4,1664]{2,1,0:T(4,128)S(1)}, f32[8,4,1664]{2,1,0:T(4,128)S(1)}, u32[]{:S(2)}, u32[]{:S(2)}) collective-permute-start(f32[8,4,1664]{2,1,0:T(4,128)S(1)} %get-tuple-element.75), channel_id=1, source_target_pairs={{0,1},{1,0},{2,3},{3,2},{4,5},{5,4},{6,7},{7,6},{8,9},{9,8},{10,11... | collective-permute-start | bytes 638984 | tf_op jit(solution)/shard_map/ppermute | solution.py:44
  38.7 5.8 %collective-permute-start.11 = (bf16[2,4,1664]{2,1,0:T(4,128)(2,1)S(1)}, bf16[2,4,1664]{2,1,0:T(4,128)(2,1)S(1)}, u32[]{:S(2)}, u32[]{:S(2)}) collective-permute-start(bf16[2,4,1664]{2,1,0:T(4,128)(2,1)S(1)} %get-tuple-element.76.refs_0_), channel_id=1, source_target_pairs={{0,2},{2,0},{4,6},{6,4},{8,10},{10,8},{12,14},{14,12},{1,3},{3,1},... | collective-permute-start | bytes 79880 | tf_op jit(solution)/shard_map/ppermute | solution.py:536
  40.4 4.2 %collective-permute-start.12 = (bf16[2,4,1664]{2,1,0:T(4,128)(2,1)S(1)}, bf16[2,4,1664]{2,1,0:T(4,128)(2,1)S(1)}, u32[]{:S(2)}, u32[]{:S(2)}) collective-permute-start(bf16[2,4,1664]{2,1,0:T(4,128)(2,1)S(1)} %get-tuple-element.78), channel_id=1, source_target_pairs={{0,4},{2,6},{4,0},{6,2},{8,12},{10,14},{12,8},{14,10},{1,5},{3,7},... | collective-permute-start | bytes 79880 | tf_op jit(solution)/shard_map/ppermute | solution.py:536
  41.6 4.7 %collective-permute-start.13 = (bf16[2,4,1664]{2,1,0:T(4,128)(2,1)S(1)}, bf16[2,4,1664]{2,1,0:T(4,128)(2,1)S(1)}, u32[]{:S(2)}, u32[]{:S(2)}) collective-permute-start(bf16[2,4,1664]{2,1,0:T(4,128)(2,1)S(1)} %get-tuple-element.79), channel_id=1, source_target_pairs={{0,6},{2,4},{4,2},{6,0},{8,14},{10,12},{12,10},{14,8},{1,7},{3,5},... | collective-permute-start | bytes 79880 | tf_op jit(solution)/shard_map/ppermute | solution.py:536
  46.3 5.6 %collective-permute-start.14 = (bf16[4,4,1664]{2,1,0:T(4,128)(2,1)S(1)}, bf16[4,4,1664]{2,1,0:T(4,128)(2,1)S(1)}, u32[]{:S(2)}, u32[]{:S(2)}) collective-permute-start(bf16[4,4,1664]{2,1,0:T(4,128)(2,1)S(1)} %pack.1.refs_1_.refs_0_), channel_id=1, source_target_pairs={{0,8},{2,10},{4,12},{6,14},{8,0},{10,2},{12,4},{14,6},{1,9},{3,11}... | collective-permute-start | bytes 159752 | tf_op jit(solution)/shard_map/ppermute | solution.py:536
  54.7 1.3 %collective-permute-start.15 = (bf16[4,6144]{1,0:T(4,128)(2,1)S(1)}, bf16[4,6144]{1,0:T(4,128)(2,1)S(1)}, u32[]{:S(2)}, u32[]{:S(2)}) collective-permute-start(bf16[4,6144]{1,0:T(4,128)(2,1)S(1)} %get-tuple-element.89), channel_id=1, source_target_pairs={{0,1},{1,0},{2,3},{3,2},{4,5},{5,4},{6,7},{7,6},{8,9},{9,8},{10,11... | collective-permute-start | bytes 147464 | tf_op jit(solution)/shard_map/ppermute | solution.py:44
  56.1 5.2 %collective-permute-start.16 = (bf16[8,6144]{1,0:T(8,128)(2,1)S(1)}, bf16[8,6144]{1,0:T(8,128)(2,1)S(1)}, u32[]{:S(2)}, u32[]{:S(2)}) collective-permute-start(bf16[8,6144]{1,0:T(8,128)(2,1)S(1)} %pad_maximum_fusion.refs_1_.refs_0_), channel_id=1, source_target_pairs={{0,4},{4,8},{8,12},{12,14},{14,10},{10,6},{6,2},{2,0},{1,5},{5,9},... | collective-permute-start | bytes 294920 | tf_op jit(solution)/shard_map/ppermute | solution.py:55
  56.5 4.8 %collective-permute-start.17 = (bf16[8,6144]{1,0:T(8,128)(2,1)S(1)}, bf16[8,6144]{1,0:T(8,128)(2,1)S(1)}, u32[]{:S(2)}, u32[]{:S(2)}) collective-permute-start(bf16[8,6144]{1,0:T(8,128)(2,1)S(1)} %pad_maximum_fusion.refs_1_.refs_0_), channel_id=1, source_target_pairs={{0,2},{4,0},{8,4},{12,8},{14,12},{10,14},{6,10},{2,6},{1,3},{5,1},... | collective-permute-start | bytes 294920 | tf_op jit(solution)/shard_map/ppermute | solution.py:55
  61.3 5.2 %collective-permute-start.18 = (bf16[8,6144]{1,0:T(8,128)(2,1)S(1)}, bf16[8,6144]{1,0:T(8,128)(2,1)S(1)}, u32[]{:S(2)}, u32[]{:S(2)}) collective-permute-start(bf16[8,6144]{1,0:T(8,128)(2,1)S(1)} %collective-permute-done.16.refs_1_), channel_id=1, source_target_pairs={{0,4},{4,8},{8,12},{12,14},{14,10},{10,6},{6,2},{2,0},{1,5},{5,9},... | collective-permute-start | bytes 294920 | tf_op jit(solution)/shard_map/ppermute | solution.py:55
  62.6 4.6 %collective-permute-start.19 = (bf16[8,6144]{1,0:T(8,128)(2,1)S(1)}, bf16[8,6144]{1,0:T(8,128)(2,1)S(1)}, u32[]{:S(2)}, u32[]{:S(2)}) collective-permute-start(bf16[8,6144]{1,0:T(8,128)(2,1)S(1)} %collective-permute-done.17.refs_2_), channel_id=1, source_target_pairs={{0,2},{4,0},{8,4},{12,8},{14,12},{10,14},{6,10},{2,6},{1,3},{5,1},... | collective-permute-start | bytes 294920 | tf_op jit(solution)/shard_map/ppermute | solution.py:55
  67.2 5.1 %collective-permute-start.20 = (bf16[8,6144]{1,0:T(8,128)(2,1)S(1)}, bf16[8,6144]{1,0:T(8,128)(2,1)S(1)}, u32[]{:S(2)}, u32[]{:S(2)}) collective-permute-start(bf16[8,6144]{1,0:T(8,128)(2,1)S(1)} %collective-permute-done.18.refs_1_.refs_3_), channel_id=1, source_target_pairs={{0,4},{4,8},{8,12},{12,14},{14,10},{10,6},{6,2},{2,0},{1,5},{5,9},... | collective-permute-start | bytes 294920 | tf_op jit(solution)/shard_map/ppermute | solution.py:55
  68.1 4.6 %collective-permute-start.21 = (bf16[8,6144]{1,0:T(8,128)(2,1)S(1)}, bf16[8,6144]{1,0:T(8,128)(2,1)S(1)}, u32[]{:S(2)}, u32[]{:S(2)}) collective-permute-start(bf16[8,6144]{1,0:T(8,128)(2,1)S(1)} %collective-permute-done.19.refs_2_.refs_4_), channel_id=1, source_target_pairs={{0,2},{4,0},{8,4},{12,8},{14,12},{10,14},{6,10},{2,6},{1,3},{5,1},... | collective-permute-start | bytes 294920 | tf_op jit(solution)/shard_map/ppermute | solution.py:55
  72.7 4.4 %collective-permute-start.22 = (bf16[8,3072]{1,0:T(8,128)(2,1)S(1)}, bf16[8,3072]{1,0:T(8,128)(2,1)S(1)}, u32[]{:S(2)}, u32[]{:S(2)}) collective-permute-start(bf16[8,3072]{1,0:T(8,128)(2,1)S(1)} %slice.18), channel_id=1, source_target_pairs={{0,4},{4,8},{8,12},{12,14},{14,10},{10,6},{6,2},{2,0},{1,5},{5,9},... | collective-permute-start | bytes 147464 | tf_op jit(solution)/shard_map/ppermute | solution.py:55
  73.3 4.1 %collective-permute-start.23 = (bf16[8,3072]{1,0:T(8,128)(2,1)S(1)}, bf16[8,3072]{1,0:T(8,128)(2,1)S(1)}, u32[]{:S(2)}, u32[]{:S(2)}) collective-permute-start(bf16[8,3072]{1,0:T(8,128)(2,1)S(1)} %slice.19), channel_id=1, source_target_pairs={{0,2},{4,0},{8,4},{12,8},{14,12},{10,14},{6,10},{2,6},{1,3},{5,1},... | collective-permute-start | bytes 147464 | tf_op jit(solution)/shard_map/ppermute | solution.py:55
  82.4 1.6 %collective-permute-start.24 = (f32[4,8,2304]{2,1,0:T(8,128)S(1)}, f32[4,8,2304]{2,1,0:T(8,128)S(1)}, u32[]{:S(2)}, u32[]{:S(2)}) collective-permute-start(f32[4,8,2304]{2,1,0:T(8,128)S(1)} %get-tuple-element.104), channel_id=1, source_target_pairs={{0,1},{1,0},{2,3},{3,2},{4,5},{5,4},{6,7},{7,6},{8,9},{9,8},{10,11... | collective-permute-start | bytes 884744 | tf_op jit(solution)/shard_map/ppermute | solution.py:44

commit v20 on v17

--- a/solution.py
+++ b/solution.py
@@ -180,10 +180,11 @@
     row_mean = sums[:, :1] / D
     row_square = sums[:, 1:2] / D
     scale = lax.rsqrt(row_square - row_mean * row_mean + epsilon)
-    for part in range(2):
-        cols = slice(part * width // 2, (part + 1) * width // 2)
+    for part in range(4):
+        cols = slice(part * width // 4, (part + 1) * width // 4)
+        end = slice(part % 2 * width // 4, (part % 2 + 1) * width // 4)
         for i in range(0, n, 2):
-            x = [ref[:, cols] if ref is not far[part] else ref[...] for ref in (*shards, far[part])]
+            x = [ref[:, cols] for ref in shards] + [far[part // 2][:, end]]
             x = jnp.concatenate([piece.astype(jnp.float32) for piece in x[i : i + 2]], axis=0)
             at = slice(i * rows, (i + 2) * rows)
             x = (x - row_mean[at]) * scale[at] * gain[:, cols]

time: 84.6 us -> 84.5 us (level)
  no operation moved by 1% of the time
where the time goes in v20:
time: 84.5 us; the launch traced here: 84.4 us
  Pallas kernels  47.6 us (56%)
  starting transfers between devices  24.8 us (29%)
  waiting for transfers between devices  10.8 us (13%)
  other arithmetic  0.89 us (1%)
    pallas_call x9, Pallas kernels, load(): pl.pallas_call(lambda *refs: load_kernel([job[1:] for job in jobs], *refs...  26 us
    ppermute x8, starting transfers between devices, step(): lax.ppermute(left, 'gx', self.onward)  10.2 us
    pallas_call x1, Pallas kernels, project(): pl.pallas_call(lambda *refs: project_kernel(n, len(weights), *refs), out_...  8.75 us
    ppermute x8, starting transfers between devices, step(): lax.ppermute(right, 'gx', self.back)  7.2 us
    pallas_call x1, Pallas kernels, output_project(): pl.pallas_call(lambda *refs: output_kernel(n, *refs), out_shape=[shape, s...  5.05 us
    pallas_call x2, Pallas kernels, load_cache(): pl.pallas_call(load_cache_kernel, out_shape=pltpu.VMEM(cache.shape, cache...  4.42 us
    ppermute x4, waiting for transfers between devices, swap_pair(): return lax.ppermute(x, 'gy', [(0, 1), (1, 0)])  3.88 us
    ppermute x4, starting transfers between devices, exchange(): return lax.ppermute(blocks, 'gx', [(i, i ^ d) for i in range(n)])  3.81 us
  transfers between devices with their start and end apart: 25, of which 11 were waited for; matrix products, arithmetic and copies ran while one was open for 0% of the time, Pallas kernels for 37%

profile of v20, /device:TPU:0, one launch (start us, length us, event | category | flops | bytes accessed | tf_op | source)
XLA Modules:
  0.0 84.4 jit_solution(18147200294919042555)
XLA Ops:
  0.0 3.0 %collective-permute-start = (bf16[8,9216]{1,0:T(8,128)(2,1)}, bf16[8,9216]{1,0:T(8,128)(2,1)S(1)}, u32[]{:S(2)}, u32[]{:S(2)}) collective-permute-start(bf16[8,9216]{1,0:T(8,128)(2,1)} %refs_3_.1), channel_id=1, source_target_pairs={{0,4},{4,8},{8,12},{12,14},{14,10},{10,6},{6,2},{2,0},{1,5},{5,9},... | collective-permute-start | bytes 442376 | tf_op jit(solution)/shard_map/ppermute | solution.py:55
  3.0 3.8 %load.9.refs_12_ = bf16[512,9216]{1,0:T(8,128)(2,1)S(1)} custom-call(bf16[1536,9216]{1,0:T(8,128)(2,1)} %refs_0_.14), custom_call_target="tpu_custom_call" | custom-call | tf_op jit(solution)/shard_map/load/pallas_call | solution.py:97
  6.8 0.3 collective-permute-done.refs_1_.refs_4_
  7.1 1.4 %collective-permute-done.1.refs_2_.refs_5_ = bf16[8,9216]{1,0:T(8,128)(2,1)S(1)} collective-permute-done((bf16[8,9216]{1,0:T(8,128)(2,1)}, bf16[8,9216]{1,0:T(8,128)(2,1)S(1)}, u32[]{:S(2)}, u32[]{:S(2)}) %collective-permute-start.1) | collective-permute-done | bytes 147488 | tf_op jit(solution)/shard_map/ppermute | solution.py:55
  8.5 1.6 %collective-permute-start.2 = (bf16[8,9216]{1,0:T(8,128)(2,1)S(1)}, bf16[8,9216]{1,0:T(8,128)(2,1)S(1)}, u32[]{:S(2)}, u32[]{:S(2)}) collective-permute-start(bf16[8,9216]{1,0:T(8,128)(2,1)S(1)} %collective-permute-done.refs_1_.refs_4_), channel_id=1, source_target_pairs={{0,4},{4,8},{8,12},{12,14},{14,10},{10,6},{6,2},{2,0},{1,5},{5,9},... | collective-permute-start | bytes 442376 | tf_op jit(solution)/shard_map/ppermute | solution.py:55
  10.1 0.4 collective-permute-start.3
  10.6 0.2 row_sums.3.refs_0_
  10.8 3.8 %load.10.refs_13_ = bf16[512,9216]{1,0:T(8,128)(2,1)S(1)} custom-call(bf16[1536,9216]{1,0:T(8,128)(2,1)} %refs_0_.14, bf16[8,9216]{1,0:T(8,128)(2,1)S(1)} %collective-permute-done.refs_1_.refs_4_, bf16[8,9216]{1,0:T(8,128)(2,1)S(1)} %collective-permute-done.1.refs_2_.refs_5_), custom_call_target="tpu_custom_call" | custom-call | tf_op jit(solution)/shard_map/load/pallas_call | solution.py:97
  14.6 0.6 collective-permute-done.3.refs_2_.refs_7_
  15.3 1.6 %collective-permute-start.4 = (bf16[8,9216]{1,0:T(8,128)(2,1)S(1)}, bf16[8,9216]{1,0:T(8,128)(2,1)S(1)}, u32[]{:S(2)}, u32[]{:S(2)}) collective-permute-start(bf16[8,9216]{1,0:T(8,128)(2,1)S(1)} %collective-permute-done.2.refs_1_.refs_6_), channel_id=1, source_target_pairs={{0,4},{4,8},{8,12},{12,14},{14,10},{10,6},{6,2},{2,0},{1,5},{5,9},... | collective-permute-start | bytes 442376 | tf_op jit(solution)/shard_map/ppermute | solution.py:55
  16.8 0.4 collective-permute-start.5
  17.5 2.9 %collective-permute-start.6 = (f32[8,128]{1,0:T(8,128)S(1)}, f32[8,128]{1,0:T(8,128)S(1)}, u32[]{:S(2)}, u32[]{:S(2)}) collective-permute-start(f32[8,128]{1,0:T(8,128)S(1)} %slice.20), channel_id=1, source_target_pairs={{0,14},{4,10},{8,6},{12,2},{14,0},{10,4},{6,8},{2,12},{1,15},{5,11... | collective-permute-start | bytes 12296 | tf_op jit(solution)/shard_map/ppermute | solution.py:522
  20.3 2.4 %load.11.refs_14_ = bf16[256,9216]{1,0:T(8,128)(2,1)S(1)} custom-call(bf16[1536,9216]{1,0:T(8,128)(2,1)} %refs_0_.14, bf16[8,9216]{1,0:T(8,128)(2,1)S(1)} %collective-permute-done.2.refs_1_.refs_6_, bf16[8,9216]{1,0:T(8,128)(2,1)S(1)} %collective-permute-done.3.refs_2_.refs_7_), custom_call_target="tpu_custom_call" | custom-call | tf_op jit(solution)/shard_map/load/pallas_call | solution.py:97
  22.8 0.8 collective-permute-start.8
  23.6 1.3 %collective-permute-start.9 = (bf16[8,4608]{1,0:T(8,128)(2,1)S(1)}, bf16[8,4608]{1,0:T(8,128)(2,1)S(1)}, u32[]{:S(2)}, u32[]{:S(2)}) collective-permute-start(bf16[8,4608]{1,0:T(8,128)(2,1)S(1)} %slice.16), channel_id=1, source_target_pairs={{0,2},{4,0},{8,4},{12,8},{14,12},{10,14},{6,10},{2,6},{1,3},{5,1},... | collective-permute-start | bytes 221192 | tf_op jit(solution)/shard_map/ppermute | solution.py:55
  25.1 2.7 %load.12.refs_15_ = bf16[320,9216]{1,0:T(8,128)(2,1)S(1)} custom-call(bf16[1536,9216]{1,0:T(8,128)(2,1)} %refs_0_.14, bf16[64,9216]{1,0:T(8,128)(2,1)} %refs_1_.1, f32[56,128]{1,0:T(8,128)S(1)} %row_sums.5.refs_2_), custom_call_target="tpu_custom_call" | custom-call | tf_op jit(solution)/shard_map/load/pallas_call | solution.py:97
  27.9 8.7 %project.1 = (f32[8,4,1664]{2,1,0:T(4,128)S(1)}, f32[8,4,1664]{2,1,0:T(4,128)S(1)}) custom-call(f32[64,128]{1,0:T(8,128)S(1)} %pad_maximum_fusion.1.refs_0_, f32[64,128]{1,0:T(8,128)S(1)} %collective-permute-done.7.refs_1_, f32[1,9216]{1,0:T(1,128)S(1)} %bitcast.3, bf16[8,9216]{1,0:T(8,128)(2,1)S(1)} %copy-done, ...), custom_call_target="tpu_custom_call" | custom-call | tf_op jit(solution)/shard_map/project/pallas_call | solution.py:223
  36.7 0.5 collective-permute-start.10
  37.2 1.1 %collective-permute-done.10.got = f32[8,4,1664]{2,1,0:T(4,128)S(1)} collective-permute-done((f32[8,4,1664]{2,1,0:T(4,128)S(1)}, f32[8,4,1664]{2,1,0:T(4,128)S(1)}, u32[]{:S(2)}, u32[]{:S(2)}) %collective-permute-start.10) | collective-permute-done | bytes 213024 | tf_op jit(solution)/shard_map/ppermute | solution.py:44
  38.3 1.7 %collective-permute-start.11 = (bf16[2,4,1664]{2,1,0:T(4,128)(2,1)S(1)}, bf16[2,4,1664]{2,1,0:T(4,128)(2,1)S(1)}, u32[]{:S(2)}, u32[]{:S(2)}) collective-permute-start(bf16[2,4,1664]{2,1,0:T(4,128)(2,1)S(1)} %get-tuple-element.76.refs_0_), channel_id=1, source_target_pairs={{0,2},{2,0},{4,6},{6,4},{8,10},{10,8},{12,14},{14,12},{1,3},{3,1},... | collective-permute-start | bytes 79880 | tf_op jit(solution)/shard_map/ppermute | solution.py:542
  40.0 1.2 %collective-permute-start.12 = (bf16[2,4,1664]{2,1,0:T(4,128)(2,1)S(1)}, bf16[2,4,1664]{2,1,0:T(4,128)(2,1)S(1)}, u32[]{:S(2)}, u32[]{:S(2)}) collective-permute-start(bf16[2,4,1664]{2,1,0:T(4,128)(2,1)S(1)} %get-tuple-element.78), channel_id=1, source_target_pairs={{0,4},{2,6},{4,0},{6,2},{8,12},{10,14},{12,8},{14,10},{1,5},{3,7},... | collective-permute-start | bytes 79880 | tf_op jit(solution)/shard_map/ppermute | solution.py:542
  41.2 0.7 collective-permute-start.13
  41.9 2.2 %load_cache.2.refs_7_ = bf16[4,2048,256]{2,1,0:T(8,128)(2,1)S(1)} custom-call(bf16[4,2048,256]{2,1,0:T(8,128)(2,1)} %source.2, bf16[2,4,1664]{2,1,0:T(4,128)(2,1)S(1)} %get-tuple-element.76.refs_0_), custom_call_target="tpu_custom_call" | custom-call | tf_op jit(solution)/shard_map/load_cache/pallas_call | solution.py:119
  44.2 1.8 %collective-permute-done.13.refs_3_ = bf16[2,4,1664]{2,1,0:T(4,128)(2,1)S(1)} collective-permute-done((bf16[2,4,1664]{2,1,0:T(4,128)(2,1)S(1)}, bf16[2,4,1664]{2,1,0:T(4,128)(2,1)S(1)}, u32[]{:S(2)}, u32[]{:S(2)}) %collective-permute-start.13) | collective-permute-done | bytes 26656 | tf_op jit(solution)/shard_map/ppermute | solution.py:542
  45.9 0.2 collective-permute-start.14
  46.3 2.2 %load_cache.3.refs_8_ = bf16[4,2048,256]{2,1,0:T(8,128)(2,1)S(1)} custom-call(bf16[4,2048,256]{2,1,0:T(8,128)(2,1)} %source.3, bf16[4,4,1664]{2,1,0:T(4,128)(2,1)S(1)} %pack.1.refs_1_.refs_0_), custom_call_target="tpu_custom_call" | custom-call | tf_op jit(solution)/shard_map/load_cache/pallas_call | solution.py:119
  48.5 1.6 %load.13.refs_9_ = bf16[512,2304]{1,0:T(8,128)(2,1)S(1)} custom-call(bf16[6144,2304]{1,0:T(8,128)(2,1)} %refs_0_.19, bf16[4,4,1664]{2,1,0:T(4,128)(2,1)S(1)} %pack.1.refs_1_.refs_0_), custom_call_target="tpu_custom_call" | custom-call | tf_op jit(solution)/shard_map/load/pallas_call | solution.py:97
  50.2 1.4 %collective-permute-done.14.refs_4_ = bf16[4,4,1664]{2,1,0:T(4,128)(2,1)S(1)} collective-permute-done((bf16[4,4,1664]{2,1,0:T(4,128)(2,1)S(1)}, bf16[4,4,1664]{2,1,0:T(4,128)(2,1)S(1)}, u32[]{:S(2)}, u32[]{:S(2)}) %collective-permute-start.14) | collective-permute-done | bytes 53280 | tf_op jit(solution)/shard_map/ppermute | solution.py:542
  51.5 2.7 %attend.1 = (bf16[4,6144]{1,0:T(4,128)(2,1)S(1)}, bf16[4,6144]{1,0:T(4,128)(2,1)S(1)}) custom-call(s32[4]{0:T(128)S(1)} %copy-done.1, bf16[2,4,1664]{2,1,0:T(4,128)(2,1)S(1)} %get-tuple-element.80.refs_0_, bf16[2,4,1664]{2,1,0:T(4,128)(2,1)S(1)} %collective-permute-done.11.refs_1_, bf16[2,4,1664]{2,1,0:T(4,128)(2,1)S(1)} %collective-permute-done.12.refs_2_, ...), custom_call_target="tpu_custom_call" | custom-call | tf_op jit(solution)/shard_map/attend/pallas_call | solution.py:343
  54.4 1.2 %collective-permute-done.15 = bf16[4,6144]{1,0:T(4,128)(2,1)S(1)} collective-permute-done((bf16[4,6144]{1,0:T(4,128)(2,1)S(1)}, bf16[4,6144]{1,0:T(4,128)(2,1)S(1)}, u32[]{:S(2)}, u32[]{:S(2)}) %collective-permute-start.15) | collective-permute-done | bytes 49184 | tf_op jit(solution)/shard_map/ppermute | solution.py:44
  55.6 0.4 collective-permute-start.16
  56.1 1.7 %collective-permute-start.17 = (bf16[8,6144]{1,0:T(8,128)(2,1)S(1)}, bf16[8,6144]{1,0:T(8,128)(2,1)S(1)}, u32[]{:S(2)}, u32[]{:S(2)}) collective-permute-start(bf16[8,6144]{1,0:T(8,128)(2,1)S(1)} %pad_maximum_fusion.refs_1_.refs_0_), channel_id=1, source_target_pairs={{0,2},{4,0},{8,4},{12,8},{14,12},{10,14},{6,10},{2,6},{1,3},{5,1},... | collective-permute-start | bytes 294920 | tf_op jit(solution)/shard_map/ppermute | solution.py:55
  57.7 3.1 %load.14.refs_10_ = bf16[1536,2304]{1,0:T(8,128)(2,1)S(1)} custom-call(bf16[6144,2304]{1,0:T(8,128)(2,1)} %refs_0_.19, bf16[8,6144]{1,0:T(8,128)(2,1)S(1)} %pad_maximum_fusion.refs_1_.refs_0_), custom_call_target="tpu_custom_call" | custom-call | tf_op jit(solution)/shard_map/load/pallas_call | solution.py:97
  60.9 1.3 %collective-permute-start.18 = (bf16[8,6144]{1,0:T(8,128)(2,1)S(1)}, bf16[8,6144]{1,0:T(8,128)(2,1)S(1)}, u32[]{:S(2)}, u32[]{:S(2)}) collective-permute-start(bf16[8,6144]{1,0:T(8,128)(2,1)S(1)} %collective-permute-done.16.refs_1_), channel_id=1, source_target_pairs={{0,4},{4,8},{8,12},{12,14},{14,10},{10,6},{6,2},{2,0},{1,5},{5,9},... | collective-permute-start | bytes 294920 | tf_op jit(solution)/shard_map/ppermute | solution.py:55
  62.2 0.8 collective-permute-start.19
  62.9 3.1 %load.15.refs_11_ = bf16[1536,2304]{1,0:T(8,128)(2,1)S(1)} custom-call(bf16[6144,2304]{1,0:T(8,128)(2,1)} %refs_0_.19, bf16[8,6144]{1,0:T(8,128)(2,1)S(1)} %collective-permute-done.16.refs_1_, bf16[8,6144]{1,0:T(8,128)(2,1)S(1)} %collective-permute-done.17.refs_2_), custom_call_target="tpu_custom_call" | custom-call | tf_op jit(solution)/shard_map/load/pallas_call | solution.py:97
  66.1 0.7 collective-permute-done.19.refs_2_.refs_4_
  66.8 0.8 collective-permute-start.20
  67.6 1.2 %collective-permute-start.21 = (bf16[8,6144]{1,0:T(8,128)(2,1)S(1)}, bf16[8,6144]{1,0:T(8,128)(2,1)S(1)}, u32[]{:S(2)}, u32[]{:S(2)}) collective-permute-start(bf16[8,6144]{1,0:T(8,128)(2,1)S(1)} %collective-permute-done.19.refs_2_.refs_4_), channel_id=1, source_target_pairs={{0,2},{4,0},{8,4},{12,8},{14,12},{10,14},{6,10},{2,6},{1,3},{5,1},... | collective-permute-start | bytes 294920 | tf_op jit(solution)/shard_map/ppermute | solution.py:55
  68.8 3.1 %load.16.refs_12_ = bf16[1536,2304]{1,0:T(8,128)(2,1)S(1)} custom-call(bf16[6144,2304]{1,0:T(8,128)(2,1)} %refs_0_.19, bf16[8,6144]{1,0:T(8,128)(2,1)S(1)} %collective-permute-done.18.refs_1_.refs_3_, bf16[8,6144]{1,0:T(8,128)(2,1)S(1)} %collective-permute-done.19.refs_2_.refs_4_), custom_call_target="tpu_custom_call" | custom-call | tf_op jit(solution)/shard_map/load/pallas_call | solution.py:97
  72.0 0.3 collective-permute-done.21.refs_2_.refs_6_
  72.3 0.6 collective-permute-start.22
  72.9 1.4 %collective-permute-start.23 = (bf16[8,3072]{1,0:T(8,128)(2,1)S(1)}, bf16[8,3072]{1,0:T(8,128)(2,1)S(1)}, u32[]{:S(2)}, u32[]{:S(2)}) collective-permute-start(bf16[8,3072]{1,0:T(8,128)(2,1)S(1)} %slice.19), channel_id=1, source_target_pairs={{0,2},{4,0},{8,4},{12,8},{14,12},{10,14},{6,10},{2,6},{1,3},{5,1},... | collective-permute-start | bytes 147464 | tf_op jit(solution)/shard_map/ppermute | solution.py:55
  74.3 2.4 %load.17.refs_13_ = bf16[1024,2304]{1,0:T(8,128)(2,1)S(1)} custom-call(bf16[6144,2304]{1,0:T(8,128)(2,1)} %refs_0_.19, bf16[8,6144]{1,0:T(8,128)(2,1)S(1)} %collective-permute-done.20.refs_1_.refs_5_, bf16[8,6144]{1,0:T(8,128)(2,1)S(1)} %collective-permute-done.21.refs_2_.refs_6_), custom_call_target="tpu_custom_call" | custom-call | tf_op jit(solution)/shard_map/load/pallas_call | solution.py:97
  76.7 0.3 collective-permute-done.23.refs_8_
  77.0 5.0 %output_project.1 = (f32[4,8,2304]{2,1,0:T(8,128)S(1)}, f32[4,8,2304]{2,1,0:T(8,128)S(1)}) custom-call(bf16[8,6144]{1,0:T(8,128)(2,1)S(1)} %pad_maximum_fusion.refs_1_.refs_0_, bf16[8,6144]{1,0:T(8,128)(2,1)S(1)} %collective-permute-done.16.refs_1_, bf16[8,6144]{1,0:T(8,128)(2,1)S(1)} %collective-permute-done.17.refs_2_, ...), custom_call_target="tpu_custom_call" | custom-call | tf_op jit(solution)/shard_map/output_project/pallas_call | solution.py:398
  82.1 1.6 %collective-permute-done.24 = f32[4,8,2304]{2,1,0:T(8,128)S(1)} collective-permute-done((f32[4,8,2304]{2,1,0:T(8,128)S(1)}, f32[4,8,2304]{2,1,0:T(8,128)S(1)}, u32[]{:S(2)}, u32[]{:S(2)}) %collective-permute-start.24) | collective-permute-done | bytes 294944 | tf_op jit(solution)/shard_map/ppermute | solution.py:44
  83.7 0.7 fusion
  (39 shorter events, 0.9 us)
Async XLA Ops:
  0.0 10.6 %copy-start = (bf16[8,9216]{1,0:T(8,128)(2,1)S(1)}, bf16[8,9216]{1,0:T(8,128)(2,1)}, u32[]{:S(2)}) copy-start(bf16[8,9216]{1,0:T(8,128)(2,1)} %refs_3_.1) | copy-start | bytes 442372
  0.0 7.1 %collective-permute-start = (bf16[8,9216]{1,0:T(8,128)(2,1)}, bf16[8,9216]{1,0:T(8,128)(2,1)S(1)}, u32[]{:S(2)}, u32[]{:S(2)}) collective-permute-start(bf16[8,9216]{1,0:T(8,128)(2,1)} %refs_3_.1), channel_id=1, source_target_pairs={{0,4},{4,8},{8,12},{12,14},{14,10},{10,6},{6,2},{2,0},{1,5},{5,9},... | collective-permute-start | bytes 442376 | tf_op jit(solution)/shard_map/ppermute | solution.py:55
  3.0 5.5 %collective-permute-start.1 = (bf16[8,9216]{1,0:T(8,128)(2,1)}, bf16[8,9216]{1,0:T(8,128)(2,1)S(1)}, u32[]{:S(2)}, u32[]{:S(2)}) collective-permute-start(bf16[8,9216]{1,0:T(8,128)(2,1)} %refs_3_.1), channel_id=1, source_target_pairs={{0,2},{4,0},{8,4},{12,8},{14,12},{10,14},{6,10},{2,6},{1,3},{5,1},... | collective-permute-start | bytes 442376 | tf_op jit(solution)/shard_map/ppermute | solution.py:55
  8.5 6.1 %collective-permute-start.2 = (bf16[8,9216]{1,0:T(8,128)(2,1)S(1)}, bf16[8,9216]{1,0:T(8,128)(2,1)S(1)}, u32[]{:S(2)}, u32[]{:S(2)}) collective-permute-start(bf16[8,9216]{1,0:T(8,128)(2,1)S(1)} %collective-permute-done.refs_1_.refs_4_), channel_id=1, source_target_pairs={{0,4},{4,8},{8,12},{12,14},{14,10},{10,6},{6,2},{2,0},{1,5},{5,9},... | collective-permute-start | bytes 442376 | tf_op jit(solution)/shard_map/ppermute | solution.py:55
  10.1 5.1 %collective-permute-start.3 = (bf16[8,9216]{1,0:T(8,128)(2,1)S(1)}, bf16[8,9216]{1,0:T(8,128)(2,1)S(1)}, u32[]{:S(2)}, u32[]{:S(2)}) collective-permute-start(bf16[8,9216]{1,0:T(8,128)(2,1)S(1)} %collective-permute-done.1.refs_2_.refs_5_), channel_id=1, source_target_pairs={{0,2},{4,0},{8,4},{12,8},{14,12},{10,14},{6,10},{2,6},{1,3},{5,1},... | collective-permute-start | bytes 442376 | tf_op jit(solution)/shard_map/ppermute | solution.py:55
  15.3 7.5 %collective-permute-start.4 = (bf16[8,9216]{1,0:T(8,128)(2,1)S(1)}, bf16[8,9216]{1,0:T(8,128)(2,1)S(1)}, u32[]{:S(2)}, u32[]{:S(2)}) collective-permute-start(bf16[8,9216]{1,0:T(8,128)(2,1)S(1)} %collective-permute-done.2.refs_1_.refs_6_), channel_id=1, source_target_pairs={{0,4},{4,8},{8,12},{12,14},{14,10},{10,6},{6,2},{2,0},{1,5},{5,9},... | collective-permute-start | bytes 442376 | tf_op jit(solution)/shard_map/ppermute | solution.py:55
  16.8 5.9 %collective-permute-start.5 = (bf16[8,9216]{1,0:T(8,128)(2,1)S(1)}, bf16[8,9216]{1,0:T(8,128)(2,1)S(1)}, u32[]{:S(2)}, u32[]{:S(2)}) collective-permute-start(bf16[8,9216]{1,0:T(8,128)(2,1)S(1)} %collective-permute-done.3.refs_2_.refs_7_), channel_id=1, source_target_pairs={{0,2},{4,0},{8,4},{12,8},{14,12},{10,14},{6,10},{2,6},{1,3},{5,1},... | collective-permute-start | bytes 442376 | tf_op jit(solution)/shard_map/ppermute | solution.py:55
  17.5 7.6 %copy-start.2 = (bf16[9216]{0:T(1024)(128)(2,1)S(1)}, bf16[9216]{0:T(1024)(128)(2,1)}, u32[]{:S(2)}) copy-start(bf16[9216]{0:T(1024)(128)(2,1)} %param.9) | copy-start | bytes 55300
  17.5 7.6 %collective-permute-start.6 = (f32[8,128]{1,0:T(8,128)S(1)}, f32[8,128]{1,0:T(8,128)S(1)}, u32[]{:S(2)}, u32[]{:S(2)}) collective-permute-start(f32[8,128]{1,0:T(8,128)S(1)} %slice.20), channel_id=1, source_target_pairs={{0,14},{4,10},{8,6},{12,2},{14,0},{10,4},{6,8},{2,12},{1,15},{5,11... | collective-permute-start | bytes 12296 | tf_op jit(solution)/shard_map/ppermute | solution.py:522
  22.8 5.1 %collective-permute-start.8 = (bf16[8,4608]{1,0:T(8,128)(2,1)S(1)}, bf16[8,4608]{1,0:T(8,128)(2,1)S(1)}, u32[]{:S(2)}, u32[]{:S(2)}) collective-permute-start(bf16[8,4608]{1,0:T(8,128)(2,1)S(1)} %slice.15), channel_id=1, source_target_pairs={{0,4},{4,8},{8,12},{12,14},{14,10},{10,6},{6,2},{2,0},{1,5},{5,9},... | collective-permute-start | bytes 221192 | tf_op jit(solution)/shard_map/ppermute | solution.py:55
  23.6 4.4 %collective-permute-start.9 = (bf16[8,4608]{1,0:T(8,128)(2,1)S(1)}, bf16[8,4608]{1,0:T(8,128)(2,1)S(1)}, u32[]{:S(2)}, u32[]{:S(2)}) collective-permute-start(bf16[8,4608]{1,0:T(8,128)(2,1)S(1)} %slice.16), channel_id=1, source_target_pairs={{0,2},{4,0},{8,4},{12,8},{14,12},{10,14},{6,10},{2,6},{1,3},{5,1},... | collective-permute-start | bytes 221192 | tf_op jit(solution)/shard_map/ppermute | solution.py:55
  25.0 2.8 %collective-permute-start.7 = (f32[64,128]{1,0:T(8,128)S(1)}, f32[64,128]{1,0:T(8,128)S(1)}, u32[]{:S(2)}, u32[]{:S(2)}) collective-permute-start(f32[64,128]{1,0:T(8,128)S(1)} %pad_maximum_fusion.1.refs_0_), channel_id=1, source_target_pairs={{0,1},{1,0},{2,3},{3,2},{4,5},{5,4},{6,7},{7,6},{8,9},{9,8},{10,11... | collective-permute-start | bytes 98312 | tf_op jit(solution)/shard_map/ppermute | solution.py:44
  27.9 14.0 %copy-start.1 = (s32[4]{0:T(128)S(1)}, s32[4]{0:T(128)}, u32[]{:S(2)}) copy-start(s32[4]{0:T(128)} %lengths.1) | copy-start | bytes 52
  36.7 1.6 %collective-permute-start.10 = (f32[8,4,1664]{2,1,0:T(4,128)S(1)}, f32[8,4,1664]{2,1,0:T(4,128)S(1)}, u32[]{:S(2)}, u32[]{:S(2)}) collective-permute-start(f32[8,4,1664]{2,1,0:T(4,128)S(1)} %get-tuple-element.75), channel_id=1, source_target_pairs={{0,1},{1,0},{2,3},{3,2},{4,5},{5,4},{6,7},{7,6},{8,9},{9,8},{10,11... | collective-permute-start | bytes 638984 | tf_op jit(solution)/shard_map/ppermute | solution.py:44
  38.3 5.8 %collective-permute-start.11 = (bf16[2,4,1664]{2,1,0:T(4,128)(2,1)S(1)}, bf16[2,4,1664]{2,1,0:T(4,128)(2,1)S(1)}, u32[]{:S(2)}, u32[]{:S(2)}) collective-permute-start(bf16[2,4,1664]{2,1,0:T(4,128)(2,1)S(1)} %get-tuple-element.76.refs_0_), channel_id=1, source_target_pairs={{0,2},{2,0},{4,6},{6,4},{8,10},{10,8},{12,14},{14,12},{1,3},{3,1},... | collective-permute-start | bytes 79880 | tf_op jit(solution)/shard_map/ppermute | solution.py:542
  40.0 4.2 %collective-permute-start.12 = (bf16[2,4,1664]{2,1,0:T(4,128)(2,1)S(1)}, bf16[2,4,1664]{2,1,0:T(4,128)(2,1)S(1)}, u32[]{:S(2)}, u32[]{:S(2)}) collective-permute-start(bf16[2,4,1664]{2,1,0:T(4,128)(2,1)S(1)} %get-tuple-element.78), channel_id=1, source_target_pairs={{0,4},{2,6},{4,0},{6,2},{8,12},{10,14},{12,8},{14,10},{1,5},{3,7},... | collective-permute-start | bytes 79880 | tf_op jit(solution)/shard_map/ppermute | solution.py:542
  41.2 4.7 %collective-permute-start.13 = (bf16[2,4,1664]{2,1,0:T(4,128)(2,1)S(1)}, bf16[2,4,1664]{2,1,0:T(4,128)(2,1)S(1)}, u32[]{:S(2)}, u32[]{:S(2)}) collective-permute-start(bf16[2,4,1664]{2,1,0:T(4,128)(2,1)S(1)} %get-tuple-element.79), channel_id=1, source_target_pairs={{0,6},{2,4},{4,2},{6,0},{8,14},{10,12},{12,10},{14,8},{1,7},{3,5},... | collective-permute-start | bytes 79880 | tf_op jit(solution)/shard_map/ppermute | solution.py:542
  45.9 5.6 %collective-permute-start.14 = (bf16[4,4,1664]{2,1,0:T(4,128)(2,1)S(1)}, bf16[4,4,1664]{2,1,0:T(4,128)(2,1)S(1)}, u32[]{:S(2)}, u32[]{:S(2)}) collective-permute-start(bf16[4,4,1664]{2,1,0:T(4,128)(2,1)S(1)} %pack.1.refs_1_.refs_0_), channel_id=1, source_target_pairs={{0,8},{2,10},{4,12},{6,14},{8,0},{10,2},{12,4},{14,6},{1,9},{3,11}... | collective-permute-start | bytes 159752 | tf_op jit(solution)/shard_map/ppermute | solution.py:542
  54.3 1.3 %collective-permute-start.15 = (bf16[4,6144]{1,0:T(4,128)(2,1)S(1)}, bf16[4,6144]{1,0:T(4,128)(2,1)S(1)}, u32[]{:S(2)}, u32[]{:S(2)}) collective-permute-start(bf16[4,6144]{1,0:T(4,128)(2,1)S(1)} %get-tuple-element.89), channel_id=1, source_target_pairs={{0,1},{1,0},{2,3},{3,2},{4,5},{5,4},{6,7},{7,6},{8,9},{9,8},{10,11... | collective-permute-start | bytes 147464 | tf_op jit(solution)/shard_map/ppermute | solution.py:44
  55.6 5.2 %collective-permute-start.16 = (bf16[8,6144]{1,0:T(8,128)(2,1)S(1)}, bf16[8,6144]{1,0:T(8,128)(2,1)S(1)}, u32[]{:S(2)}, u32[]{:S(2)}) collective-permute-start(bf16[8,6144]{1,0:T(8,128)(2,1)S(1)} %pad_maximum_fusion.refs_1_.refs_0_), channel_id=1, source_target_pairs={{0,4},{4,8},{8,12},{12,14},{14,10},{10,6},{6,2},{2,0},{1,5},{5,9},... | collective-permute-start | bytes 294920 | tf_op jit(solution)/shard_map/ppermute | solution.py:55
  56.1 4.8 %collective-permute-start.17 = (bf16[8,6144]{1,0:T(8,128)(2,1)S(1)}, bf16[8,6144]{1,0:T(8,128)(2,1)S(1)}, u32[]{:S(2)}, u32[]{:S(2)}) collective-permute-start(bf16[8,6144]{1,0:T(8,128)(2,1)S(1)} %pad_maximum_fusion.refs_1_.refs_0_), channel_id=1, source_target_pairs={{0,2},{4,0},{8,4},{12,8},{14,12},{10,14},{6,10},{2,6},{1,3},{5,1},... | collective-permute-start | bytes 294920 | tf_op jit(solution)/shard_map/ppermute | solution.py:55
  60.9 5.2 %collective-permute-start.18 = (bf16[8,6144]{1,0:T(8,128)(2,1)S(1)}, bf16[8,6144]{1,0:T(8,128)(2,1)S(1)}, u32[]{:S(2)}, u32[]{:S(2)}) collective-permute-start(bf16[8,6144]{1,0:T(8,128)(2,1)S(1)} %collective-permute-done.16.refs_1_), channel_id=1, source_target_pairs={{0,4},{4,8},{8,12},{12,14},{14,10},{10,6},{6,2},{2,0},{1,5},{5,9},... | collective-permute-start | bytes 294920 | tf_op jit(solution)/shard_map/ppermute | solution.py:55
  62.2 4.6 %collective-permute-start.19 = (bf16[8,6144]{1,0:T(8,128)(2,1)S(1)}, bf16[8,6144]{1,0:T(8,128)(2,1)S(1)}, u32[]{:S(2)}, u32[]{:S(2)}) collective-permute-start(bf16[8,6144]{1,0:T(8,128)(2,1)S(1)} %collective-permute-done.17.refs_2_), channel_id=1, source_target_pairs={{0,2},{4,0},{8,4},{12,8},{14,12},{10,14},{6,10},{2,6},{1,3},{5,1},... | collective-permute-start | bytes 294920 | tf_op jit(solution)/shard_map/ppermute | solution.py:55
  66.8 5.1 %collective-permute-start.20 = (bf16[8,6144]{1,0:T(8,128)(2,1)S(1)}, bf16[8,6144]{1,0:T(8,128)(2,1)S(1)}, u32[]{:S(2)}, u32[]{:S(2)}) collective-permute-start(bf16[8,6144]{1,0:T(8,128)(2,1)S(1)} %collective-permute-done.18.refs_1_.refs_3_), channel_id=1, source_target_pairs={{0,4},{4,8},{8,12},{12,14},{14,10},{10,6},{6,2},{2,0},{1,5},{5,9},... | collective-permute-start | bytes 294920 | tf_op jit(solution)/shard_map/ppermute | solution.py:55
  67.6 4.6 %collective-permute-start.21 = (bf16[8,6144]{1,0:T(8,128)(2,1)S(1)}, bf16[8,6144]{1,0:T(8,128)(2,1)S(1)}, u32[]{:S(2)}, u32[]{:S(2)}) collective-permute-start(bf16[8,6144]{1,0:T(8,128)(2,1)S(1)} %collective-permute-done.19.refs_2_.refs_4_), channel_id=1, source_target_pairs={{0,2},{4,0},{8,4},{12,8},{14,12},{10,14},{6,10},{2,6},{1,3},{5,1},... | collective-permute-start | bytes 294920 | tf_op jit(solution)/shard_map/ppermute | solution.py:55
  72.3 4.4 %collective-permute-start.22 = (bf16[8,3072]{1,0:T(8,128)(2,1)S(1)}, bf16[8,3072]{1,0:T(8,128)(2,1)S(1)}, u32[]{:S(2)}, u32[]{:S(2)}) collective-permute-start(bf16[8,3072]{1,0:T(8,128)(2,1)S(1)} %slice.18), channel_id=1, source_target_pairs={{0,4},{4,8},{8,12},{12,14},{14,10},{10,6},{6,2},{2,0},{1,5},{5,9},... | collective-permute-start | bytes 147464 | tf_op jit(solution)/shard_map/ppermute | solution.py:55
  72.9 4.1 %collective-permute-start.23 = (bf16[8,3072]{1,0:T(8,128)(2,1)S(1)}, bf16[8,3072]{1,0:T(8,128)(2,1)S(1)}, u32[]{:S(2)}, u32[]{:S(2)}) collective-permute-start(bf16[8,3072]{1,0:T(8,128)(2,1)S(1)} %slice.19), channel_id=1, source_target_pairs={{0,2},{4,0},{8,4},{12,8},{14,12},{10,14},{6,10},{2,6},{1,3},{5,1},... | collective-permute-start | bytes 147464 | tf_op jit(solution)/shard_map/ppermute | solution.py:55
  82.0 1.6 %collective-permute-start.24 = (f32[4,8,2304]{2,1,0:T(8,128)S(1)}, f32[4,8,2304]{2,1,0:T(8,128)S(1)}, u32[]{:S(2)}, u32[]{:S(2)}) collective-permute-start(f32[4,8,2304]{2,1,0:T(8,128)S(1)} %get-tuple-element.104), channel_id=1, source_target_pairs={{0,1},{1,0},{2,3},{3,2},{4,5},{5,4},{6,7},{7,6},{8,9},{9,8},{10,11... | collective-permute-start | bytes 884744 | tf_op jit(solution)/shard_map/ppermute | solution.py:44
